TPU v7x, 32 devices: a whole 2x2x4 slice. The times are simulated.
32 devices in a mesh: parts: 2 (over y), ctx: 4 (over z), ch: 2 (over x), sub: 2 (over core).
Axes of the slice: x: 2, y: 2, z: 4, core: 2. Of those that a mesh axis runs over, the one named last changes fastest.
Arguments:
- x_one: bfloat16 [1024, 8192], P(('parts', 'ctx'), ('ch', 'sub')), parts along dimension 0, may hold values from -6 to 6
- x_two: bfloat16 [1024, 8192], P(('parts', 'ctx'), ('ch', 'sub')), parts along dimension 0, may hold values from -6 to 6
- values: bfloat16 [1024, 8192], P(('parts', 'ctx'), ('ch', 'sub')), parts along dimension 0, may hold values from -6 to 6
- grad_out: bfloat16 [1024, 8192], P(('parts', 'ctx'), ('ch', 'sub')), parts along dimension 0, may hold values from -6 to 6
- first_weight: float32 [32, 64], replicated, may hold values from -3 to 3
- second_weight: float32 [64, 8192], P(None, ('ch', 'sub')), may hold values from -0.75 to 0.75
- skip_bias: float32 [8192], P(('ch', 'sub')), may hold values from 0.5 to 1.5
- decay_rate: float32 [8192], P(('ch', 'sub')), may hold values from 9.765625e-05 to 0.033
Outputs:
- grad_one: bfloat16 [1024, 8192], P(('parts', 'ctx'), ('ch', 'sub')), parts along dimension 0
- grad_two: bfloat16 [1024, 8192], P(('parts', 'ctx'), ('ch', 'sub')), parts along dimension 0
- grad_value: bfloat16 [1024, 8192], P(('parts', 'ctx'), ('ch', 'sub')), parts along dimension 0
- grad_first: float32 [64, 64], P('parts'), parts along dimension 0
- grad_second: float32 [128, 8192], P('parts', ('ch', 'sub')), parts along dimension 0
- grad_bias: float32 [16384], P(('parts', 'ch', 'sub')), parts along dimension 0
There are 2 independent parts, one for each index of `parts`. A program takes and returns all parts, laid end to end along the dimension named above; an argument that names none is the same for every part. Nothing has to cross between parts.
All inputs are finite; a program needn't handle non-finite values.
Results may differ from a plain program's by a relative error of at most 0.004.
Values may be sent and summed in bfloat16 or wider, within the bound.
No kernel may reach another device: no remote copies, remote signals or barrier semaphores. Data moves between devices by JAX's collectives and lax.ppermute only.
A program may use at most 128 MiB of HBM per device.

v0:
```python
import math

import jax
import jax.numpy as jnp
from jax import lax
from jax.sharding import PartitionSpec as P

band_steps = (1763, 1201, 811, 547, 367, 251, 167, 113, 79, 53, 37, 23, 17, 11, 7, 3)
highest = lax.Precision.HIGHEST


def features(positions):
    multiplier = jnp.array(band_steps, dtype=jnp.int32)
    phase = positions[:, None] * multiplier[None, :] % 4096
    angle = phase.astype(jnp.float32) * (2.0 * math.pi / 4096.0)
    return jnp.concatenate([jnp.cos(angle), jnp.sin(angle)], axis=1)


def tables(out_count, in_count, modulus, sign_value):
    row_index = lax.broadcasted_iota(jnp.int32, (out_count, in_count), 0)
    col_index = lax.broadcasted_iota(jnp.int32, (out_count, in_count), 1)
    angle = (row_index * col_index % modulus).astype(jnp.float32) * (2.0 * math.pi / modulus)
    return (jnp.cos(angle), sign_value * jnp.sin(angle))


def twiddle(spec_re, spec_im, freq_count, span, modulus, sign_value):
    freq_index = lax.broadcasted_iota(jnp.int32, (freq_count, span), 0)
    pos_index = lax.broadcasted_iota(jnp.int32, (freq_count, span), 1)
    angle = (freq_index * pos_index % modulus).astype(jnp.float32) * (2.0 * math.pi / modulus)
    factor_re = jnp.cos(angle)[None, None, :, :]
    factor_im = (sign_value * jnp.sin(angle))[None, None, :, :]
    return (spec_re * factor_re - spec_im * factor_im, spec_re * factor_im + spec_im * factor_re)


def contract(kernel, array):
    return jnp.einsum(
        "lj,mckj->mckl", kernel, array, precision=highest, preferred_element_type=jnp.float32
    )


def along_positions(spec_re, spec_im, kernel_re, kernel_im):
    return (
        contract(kernel_re, spec_re) - contract(kernel_im, spec_im),
        contract(kernel_re, spec_im) + contract(kernel_im, spec_re),
    )


def body(x_one, x_two, values, grad_out, first_weight, second_weight, skip_bias, decay_rate):
    row_count, chan_count = x_one.shape
    shards = lax.axis_size("ctx")
    rank = lax.axis_index("ctx")
    seq_len = row_count * shards
    total = 2 * seq_len
    narrow = chan_count // shards
    chan_weight = lax.dynamic_slice_in_dim(second_weight, rank * narrow, narrow, 1)
    chan_rate = lax.dynamic_slice_in_dim(decay_rate, rank * narrow, narrow, 0)
    source = x_one.astype(jnp.float32) * values.astype(jnp.float32)
    cotan = grad_out.astype(jnp.float32) * x_two.astype(jnp.float32)
    spread = lax.all_to_all(
        jnp.stack([source.T, cotan.T])[:, :, None, :],
        "ctx",
        split_axis=1,
        concat_axis=2,
        tiled=True,
    )
    far_source = spread[0]
    far_cotan = spread[1]
    positions = jnp.arange(seq_len, dtype=jnp.int32)
    feats = features(positions)
    pre_act = jnp.dot(feats, first_weight, precision=highest, preferred_element_type=jnp.float32)
    hidden = jnp.sin(pre_act)
    envelope = jnp.exp(-chan_rate[:, None] * positions.astype(jnp.float32)[None, :]) * float(
        seq_len
    ) ** (-0.5)
    filt = (
        jnp.einsum(
            "th,hc->ct", hidden, chan_weight, precision=highest, preferred_element_type=jnp.float32
        )
        * envelope
    )
    filt_blocks = filt.reshape(narrow, shards, row_count)
    fields = jnp.stack([far_source, far_cotan])

    def first_section(kernel):
        field_part = jnp.einsum(
            "kn,mcnj->mckj", kernel, fields, precision=highest, preferred_element_type=jnp.float32
        )
        filter_part = jnp.einsum(
            "kn,cnj->ckj",
            kernel,
            filt_blocks,
            precision=highest,
            preferred_element_type=jnp.float32,
        )
        return jnp.concatenate([field_part, filter_part[None]], axis=0)

    first_re, first_im = tables(2 * shards, shards, 2 * shards, -1.0)
    spec_re, spec_im = (first_section(first_re), first_section(first_im))
    spec_re, spec_im = twiddle(spec_re, spec_im, 2 * shards, row_count, total, -1.0)
    fwd_re, fwd_im = tables(row_count, row_count, row_count, -1.0)
    spec_re, spec_im = along_positions(spec_re, spec_im, fwd_re, fwd_im)
    source_re, source_im = (spec_re[0], spec_im[0])
    cotan_re, cotan_im = (spec_re[1], spec_im[1])
    filter_re, filter_im = (spec_re[2], spec_im[2])
    prod_re = jnp.stack(
        [
            source_re * filter_re - source_im * filter_im,
            cotan_re * filter_re + cotan_im * filter_im,
            cotan_re * source_re + cotan_im * source_im,
        ]
    )
    prod_im = jnp.stack(
        [
            source_re * filter_im + source_im * filter_re,
            cotan_im * filter_re - cotan_re * filter_im,
            cotan_im * source_re - cotan_re * source_im,
        ]
    )
    back_re, back_im = tables(row_count, row_count, row_count, 1.0)
    prod_re, prod_im = along_positions(prod_re, prod_im, back_re, back_im)
    prod_re, prod_im = twiddle(prod_re, prod_im, 2 * shards, row_count, total, 1.0)
    last_re, last_im = tables(shards, 2 * shards, 2 * shards, 1.0)
    field_out = jnp.einsum(
        "nk,mckj->mcnj", last_re, prod_re[:2], precision=highest, preferred_element_type=jnp.float32
    ) - jnp.einsum(
        "nk,mckj->mcnj", last_im, prod_im[:2], precision=highest, preferred_element_type=jnp.float32
    )
    field_out = field_out * (1.0 / total)
    filt_grad = jnp.einsum(
        "nk,ckj->cnj", last_re, prod_re[2], precision=highest, preferred_element_type=jnp.float32
    ) - jnp.einsum(
        "nk,ckj->cnj", last_im, prod_im[2], precision=highest, preferred_element_type=jnp.float32
    )
    filt_grad = (filt_grad * (1.0 / total)).reshape(narrow, seq_len)
    modulated = filt_grad * envelope
    weight_part = jnp.einsum(
        "th,ct->hc", hidden, modulated, precision=highest, preferred_element_type=jnp.float32
    )
    hidden_grad = jnp.einsum(
        "ct,hc->th", modulated, chan_weight, precision=highest, preferred_element_type=jnp.float32
    )
    first_part = jnp.dot(
        feats.T,
        hidden_grad * jnp.cos(pre_act),
        precision=highest,
        preferred_element_type=jnp.float32,
    )
    grad_first = lax.psum(first_part, ("ctx", "ch", "sub"))
    returned = lax.all_to_all(
        field_out.astype(jnp.bfloat16), "ctx", split_axis=2, concat_axis=1, tiled=True
    ).astype(field_out.dtype)
    conv_part = returned[0, :, 0, :].T
    corr_part = returned[1, :, 0, :].T
    grad_two = (grad_out.astype(jnp.float32) * (conv_part + skip_bias[None, :] * source)).astype(
        jnp.bfloat16
    )
    grad_mid = corr_part + skip_bias[None, :] * cotan
    grad_one = (grad_mid * values.astype(jnp.float32)).astype(jnp.bfloat16)
    grad_value = (grad_mid * x_one.astype(jnp.float32)).astype(jnp.bfloat16)
    grad_bias = lax.psum(jnp.sum(source * cotan, axis=0), "ctx")
    grad_second = lax.all_gather(weight_part, "ctx", axis=1, tiled=True)
    return (grad_one, grad_two, grad_value, grad_first, grad_second, grad_bias)


def solution(mesh):
    in_specs = (
        P(("parts", "ctx"), ("ch", "sub")),
        P(("parts", "ctx"), ("ch", "sub")),
        P(("parts", "ctx"), ("ch", "sub")),
        P(("parts", "ctx"), ("ch", "sub")),
        P(),
        P(None, ("ch", "sub")),
        P(("ch", "sub")),
        P(("ch", "sub")),
    )
    out_specs = (
        P(("parts", "ctx"), ("ch", "sub")),
        P(("parts", "ctx"), ("ch", "sub")),
        P(("parts", "ctx"), ("ch", "sub")),
        P("parts", None),
        P("parts", ("ch", "sub")),
        P(("parts", "ch", "sub")),
    )
    return jax.shard_map(body, mesh=mesh, in_specs=in_specs, out_specs=out_specs, check_vma=False)
```

profile of v0, /device:TPU:0, one launch (start us, length us, event | category | flops | bytes accessed | tf_op | source)
XLA Modules:
  0.0 307.1 jit_solution(12694146341535602598)
XLA Ops:
  0.6 0.0 copy-start
  0.6 1.4 copy.47
  2.0 1.3 copy.50
  3.3 1.3 copy.49
  4.7 0.0 copy-start.10
  4.7 1.5 copy.48
  6.2 0.0 copy-start.12
  6.2 0.2 fusion.31
  6.4 0.0 copy-start.16
  6.4 0.0 copy-start.14
  6.4 0.1 maximum_bitcast_fusion
  6.6 8.5 %copy.51 = f32[2,2048,1,128]{3,0,2,1:T(2,128)} copy(f32[2,2048,1,128]{3,1,0,2:T(8,128)S(1)} %maximum_bitcast_fusion) | data formatting | bytes 4194304 | tf_op jit(solution)/shard_map/broadcast_in_dim | solution.py:60
  15.1 6.5 %all-to-all-start = ((f32[2,2048,1,128]{3,0,2,1:T(2,128)}), f32[2,2048,1,128]{3,0,2,1:T(2,128)}, u32[]{:S(2)}, u32[]{:S(2)}) async-start(f32[2,2048,1,128]{3,0,2,1:T(2,128)} %copy.51), calls=%async_computation | async-start | bytes 4194304 | tf_op jit(solution)/shard_map/all_to_all | solution.py:59
  21.6 0.8 dynamic-slice_negate_fusion
  22.4 0.2 fusion.72
  22.6 0.7 fusion.184
  23.4 2.1 convolution_multiply_fusion
  25.5 1.6 copy.54
  27.1 0.1 fusion.94
  27.1 0.1 broadcast_multiply_fusion
  27.2 3.3 %convolution_bitcast_fusion.2 = f32[1,512,8,128]{3,2,1,0:T(8,128)} fusion(f32[512,4,128]{2,1,0:T(4,128)S(1)} %copy.54), kind=kOutput, calls=%fused_computation.43 | convolution fusion | flops 25166304 | bytes 3145728 | tf_op jit(solution)/shard_map/kn,cnj->ckj/dot_general | solution.py:88
  30.5 3.3 %convolution_bitcast_fusion.3 = f32[1,512,8,128]{3,2,1,0:T(8,128)} fusion(f32[512,4,128]{2,1,0:T(4,128)S(1)} %copy.54), kind=kOutput, calls=%fused_computation.44 | convolution fusion | flops 25166272 | bytes 3145728 | tf_op jit(solution)/shard_map/kn,cnj->ckj/dot_general | solution.py:88
  33.9 35.9 %all-to-all-done = f32[2,2048,1,128]{3,0,2,1:T(2,128)} async-done(((f32[2,2048,1,128]{3,0,2,1:T(2,128)}), f32[2,2048,1,128]{3,0,2,1:T(2,128)}, u32[]{:S(2)}, u32[]{:S(2)}) %all-to-all-start) | async-done | bytes 2097184 | tf_op jit(solution)/shard_map/all_to_all | solution.py:59
  69.8 2.9 copy.109
  72.7 0.1 slice_bitcast_fusion.11
  72.9 4.4 %convolution_bitcast_fusion = f32[2,512,8,128]{3,2,1,0:T(8,128)S(1)} fusion(f32[1,512,4,128]{3,2,1,0:T(4,128)S(1)} %get-tuple-element.34, f32[1,512,4,128]{3,2,1,0:T(4,128)S(1)} %get-tuple-element.33), kind=kOutput, calls=%fused_computation.26 | convolution fusion | flops 50856416 | bytes 6291456 | tf_op jit(solution)/shard_map/kn,mcnj->mckj/dot_general | solution.py:85
  77.3 4.8 %convolution_bitcast_fusion.1 = f32[2,512,8,128]{3,2,1,0:T(8,128)S(1)} fusion(f32[1,512,4,128]{3,2,1,0:T(4,128)S(1)} %get-tuple-element.34, f32[1,512,4,128]{3,2,1,0:T(4,128)S(1)} %get-tuple-element.33), kind=kOutput, calls=%fused_computation.27 | convolution fusion | flops 50856384 | bytes 6291456 | tf_op jit(solution)/shard_map/kn,mcnj->mckj/dot_general | solution.py:85
  82.1 1.4 multiply_subtract_fusion.1
  83.4 5.5 %fusion.8 = f32[3,512,8,128]{3,1,2,0:T(8,128)S(1)} fusion(f32[3,512,8,128]{3,2,1,0:T(8,128)S(1)} %get-tuple-element.21), kind=kOutput, calls=%fused_computation.16 | convolution fusion | flops 2416148480 | bytes 12582912 | tf_op jit(solution)/shard_map/lj,mckj->mckl/dot_general | solution.py:36
  89.0 7.7 %fusion.10 = f32[3,512,8,128]{3,1,2,0:T(8,128)} fusion(f32[3,512,8,128]{3,2,1,0:T(8,128)S(1)} %get-tuple-element.21), kind=kOutput, calls=%fused_computation.18 | convolution fusion | flops 2416164864 | bytes 12582912 | tf_op jit(solution)/shard_map/lj,mckj->mckl/dot_general | solution.py:36
  96.7 5.5 %fusion.19 = f32[3,512,8,128]{3,1,2,0:T(8,128)S(1)} fusion(f32[3,512,8,128]{3,1,2,0:T(8,128)S(1)} %fusion.8, f32[3,512,8,128]{3,2,1,0:T(8,128)S(1)} %get-tuple-element.20), kind=kOutput, calls=%fused_computation.25 | convolution fusion | flops 2417737728 | bytes 18874368 | tf_op jit(solution)/shard_map/lj,mckj->mckl/dot_general | solution.py:36
  102.2 5.7 %fusion.16 = f32[3,512,8,128]{3,1,2,0:T(8,128)S(1)} fusion(f32[3,512,8,128]{3,1,2,0:T(8,128)S(1)} %copy-done.3, f32[3,512,8,128]{3,2,1,0:T(8,128)S(1)} %get-tuple-element.20), kind=kOutput, calls=%fused_computation.24 | convolution fusion | flops 2417721344 | bytes 18874368 | tf_op jit(solution)/shard_map/lj,mckj->mckl/dot_general | solution.py:36
  108.0 4.3 %multiply_subtract_fusion.4 = (f32[1,512,8,128]{3,1,2,0:T(8,128)}, f32[1,512,8,128]{3,1,2,0:T(8,128)}, f32[1,512,8,128]{3,1,2,0:T(8,128)}, f32[1,512,8,128]{3,1,2,0:T(8,128)}) fusion(f32[3,512,8,128]{3,1,2,0:T(8,128)S(1)} %fusion.19, f32[3,512,8,128]{3,1,2,0:T(8,128)S(1)} %fusion.16), kind=kLoop, calls=%fused_computation.42 | loop fusion | flops 6291456 | bytes 20971520 | tf_op jit(solution)/shard_map/sub | solution.py:107
  112.3 2.0 multiply_add_fusion.4
  114.3 1.0 copy-done.9
  115.3 2.0 pad_maximum_fusion.2
  117.3 13.6 %fusion.4 = f32[3,512,8,128]{3,2,1,0:T(8,128)} fusion(f32[3,512,8,128]{3,1,2,0:T(8,128)S(1)} %pad_maximum_fusion.2), kind=kOutput, calls=%fused_computation.12 | convolution fusion | flops 2416148480 | bytes 12582912 | tf_op jit(solution)/shard_map/lj,mckj->mckl/dot_general | solution.py:36
  130.9 13.5 %fusion.6 = f32[3,512,8,128]{3,2,1,0:T(8,128)} fusion(f32[3,512,8,128]{3,1,2,0:T(8,128)S(1)} %pad_maximum_fusion.2), kind=kOutput, calls=%fused_computation.14 | convolution fusion | flops 2416148480 | bytes 12582912 | tf_op jit(solution)/shard_map/lj,mckj->mckl/dot_general | solution.py:36
  144.4 0.5 pad_maximum_fusion.3
  144.9 13.7 %fusion.2 = f32[3,512,8,128]{3,2,1,0:T(8,128)} fusion(f32[3,512,8,128]{3,1,2,0:T(8,128)S(1)} %pad_maximum_fusion.3), kind=kOutput, calls=%fused_computation.10 | convolution fusion | flops 2416148480 | bytes 12582912 | tf_op jit(solution)/shard_map/lj,mckj->mckl/dot_general | solution.py:36
  158.6 17.4 %multiply_add_fusion = (f32[3,512,8,128]{3,2,1,0:T(8,128)}, f32[3,512,8,128]{3,2,1,0:T(8,128)S(1)}) fusion(f32[8,128]{1,0:T(8,128)S(1)} %fusion.94, f32[8,128]{1,0:T(8,128)S(1)} %get-tuple-element.43, f32[3,512,8,128]{3,2,1,0:T(8,128)} %fusion.4, f32[3,512,8,128]{3,2,1,0:T(8,128)} %fusion.6, f32[3,512,8,128]{3,2,1,0:T(8,128)} %fusion.2, ...), kind=kOutput, calls=%fused_computation.4 | convolution fusion | flops 2428731392 | bytes 37756928 | tf_op jit(solution)/shard_map/lj,mckj->mckl/dot_general | solution.py:36
  176.0 3.9 %fusion.86 = f32[2,512,128,4]{2,3,1,0:T(4,128)S(1)} fusion(f32[3,512,8,128]{3,2,1,0:T(8,128)S(1)} %get-tuple-element.19), kind=kOutput, calls=%fused_computation.129 | convolution fusion | flops 50332096 | bytes 8388608 | tf_op jit(solution)/shard_map/nk,mckj->mcnj/dot_general | solution.py:123
  179.9 1.2 copy-done.2
  181.1 4.4 %fusion.24 = bf16[2,512,4,128]{3,2,1,0:T(4,128)(2,1)S(1)} fusion(f32[2,512,128,4]{2,3,1,0:T(4,128)S(1)} %fusion.86, f32[3,512,8,128]{3,2,1,0:T(8,128)S(1)} %copy-done.2), kind=kOutput, calls=%fused_computation.45 | convolution fusion | flops 51904960 | bytes 9437184 | tf_op jit(solution)/shard_map/nk,mckj->mcnj/dot_general | solution.py:125
  185.5 1.2 copy.64
  186.7 4.3 %all-to-all-start.1 = ((bf16[2,512,4,128]{3,1,0,2:T(8,128)(2,1)}), bf16[2,512,4,128]{3,1,0,2:T(8,128)(2,1)}, u32[]{:S(2)}, u32[]{:S(2)}) async-start(bf16[2,512,4,128]{3,1,0,2:T(8,128)(2,1)} %copy.64), calls=%async_computation.1 | async-start | bytes 2097152 | tf_op jit(solution)/shard_map/all_to_all | solution.py:149
  191.0 3.5 %fusion.22 = f32[512,128,4]{1,2,0:T(4,128)S(1)} fusion(f32[3,512,8,128]{3,2,1,0:T(8,128)} %get-tuple-element.18), kind=kOutput, calls=%fused_computation.29 | convolution fusion | flops 25166272 | bytes 3145728 | tf_op jit(solution)/shard_map/nk,ckj->cnj/dot_general | solution.py:131
  194.5 3.7 %fusion.27 = f32[512,4,128]{2,1,0:T(4,128)S(1)} fusion(f32[512,128,4]{1,2,0:T(4,128)S(1)} %fusion.22, f32[3,512,8,128]{3,2,1,0:T(8,128)} %copy-done.1), kind=kOutput, calls=%fused_computation.48 | convolution fusion | flops 25690560 | bytes 4194304 | tf_op jit(solution)/shard_map/nk,ckj->cnj/dot_general | solution.py:129
  198.2 1.4 copy.66
  199.5 1.6 bitcast_multiply_fusion
  201.1 0.8 fusion.185
  201.8 24.9 %all_gather.3 = f32[64,2048]{1,0:T(8,128)} all-gather(f32[64,512]{1,0:T(8,128)S(1)} %fusion.185), channel_id=1, replica_groups=mesh['parts'=2,'ctx'=4,'ch'=2,'sub'=2] {'ctx'}, dimensions={1}, use_global_device_ids=true | all-gather | bytes 655360 | tf_op jit(solution)/shard_map/all_gather | solution.py:161
  226.8 1.4 convolution_multiply_fusion.1
  228.2 0.2 fusion.51
  228.5 57.8 %psum.14 = f32[32,64]{1,0:T(8,128)} all-reduce(f32[32,64]{1,0:T(8,128)S(1)} %fusion.51), channel_id=1, replica_groups=mesh['parts'=2,'ctx'=4,'ch'=2,'sub'=2] {'ctx','ch','sub'}, use_global_device_ids=true, to_apply=%region_0.1 | all-reduce | flops 2048 | bytes 16384 | tf_op jit(solution)/shard_map/psum | solution.py:148
  286.3 0.0 all-to-all-done.1
  286.3 1.4 convert_bitcast_fusion
  287.7 0.1 fusion.183
  287.9 1.9 fusion.28
  289.8 2.0 copy.67
  291.8 2.0 copy.68
  293.9 2.0 copy.69
  295.9 9.1 %psum.15 = f32[2048]{0:T(1024)} all-reduce(f32[2048]{0:T(1024)S(1)} %get-tuple-element.30), channel_id=1, replica_groups=mesh['parts'=2,'ctx'=4,'ch'=2,'sub'=2] {'ctx'}, use_global_device_ids=true, to_apply=%region_2.3 | all-reduce | flops 2048 | bytes 16384 | tf_op jit(solution)/shard_map/psum | solution.py:160
  305.0 1.9 copy.111
  (28 shorter events, 0.1 us)
Async XLA Ops:
  0.6 22.7 %copy-start = (f32[64,2048]{1,0:T(8,128)S(1)}, f32[64,2048]{1,0:T(8,128)}, u32[]{:S(2)}) copy-start(f32[64,2048]{1,0:T(8,128)} %param.14) | copy-start | bytes 1572868
  4.7 10.5 %copy-start.10 = (bf16[128,2048]{0,1:T(8,128)(2,1)}, bf16[128,2048]{0,1:T(8,128)(2,1)S(1)}, u32[]{:S(2)}) copy-start(bf16[128,2048]{0,1:T(8,128)(2,1)S(1)} %copy.49) | copy-start | bytes 1572868
  6.2 8.9 %copy-start.12 = (bf16[128,2048]{0,1:T(8,128)(2,1)}, bf16[128,2048]{0,1:T(8,128)(2,1)S(1)}, u32[]{:S(2)}) copy-start(bf16[128,2048]{0,1:T(8,128)(2,1)S(1)} %copy.48) | copy-start | bytes 1572868
  6.4 16.0 %copy-start.16 = (s32[16]{0:T(128)S(1)}, s32[16]{0:T(128)}, u32[]{:S(2)}) copy-start(s32[16]{0:T(128)} %constant.103.clone) | copy-start | bytes 196
  6.4 16.2 %copy-start.14 = (f32[32,64]{1,0:T(8,128)S(1)}, f32[32,64]{1,0:T(8,128)}, u32[]{:S(2)}) copy-start(f32[32,64]{1,0:T(8,128)} %param.13) | copy-start | bytes 24580
  15.1 54.6 %all-to-all-start = ((f32[2,2048,1,128]{3,0,2,1:T(2,128)}), f32[2,2048,1,128]{3,0,2,1:T(2,128)}, u32[]{:S(2)}, u32[]{:S(2)}) async-start(f32[2,2048,1,128]{3,0,2,1:T(2,128)} %copy.51), calls=%async_computation | async-start | bytes 4194304 | tf_op jit(solution)/shard_map/all_to_all | solution.py:59
  72.8 9.2 %copy-start.4 = (f32[1,512,8,128]{3,2,1,0:T(8,128)S(1)}, f32[1,512,8,128]{3,2,1,0:T(8,128)}, u32[]{:S(2)}) copy-start(f32[1,512,8,128]{3,2,1,0:T(8,128)} %convolution_bitcast_fusion.2) | copy-start | bytes 6291460
  72.9 9.2 %copy-start.5 = (f32[1,512,8,128]{3,2,1,0:T(8,128)S(1)}, f32[1,512,8,128]{3,2,1,0:T(8,128)}, u32[]{:S(2)}) copy-start(f32[1,512,8,128]{3,2,1,0:T(8,128)} %convolution_bitcast_fusion.3) | copy-start | bytes 6291460
  96.7 5.6 %copy-start.3 = (f32[3,512,8,128]{3,1,2,0:T(8,128)S(1)}, f32[3,512,8,128]{3,1,2,0:T(8,128)}, u32[]{:S(2)}) copy-start(f32[3,512,8,128]{3,1,2,0:T(8,128)} %fusion.10) | copy-start | bytes 18874372
  112.3 2.0 copy-start.8
  112.3 3.0 copy-start.9
  130.9 13.5 %copy-start.6 = (f32[1,512,8,128]{3,1,2,0:T(8,128)S(1)}, f32[1,512,8,128]{3,1,2,0:T(8,128)}, u32[]{:S(2)}) copy-start(f32[1,512,8,128]{3,1,2,0:T(8,128)} %get-tuple-element.24) | copy-start | bytes 6291460
  130.9 13.5 %copy-start.7 = (f32[1,512,8,128]{3,1,2,0:T(8,128)S(1)}, f32[1,512,8,128]{3,1,2,0:T(8,128)}, u32[]{:S(2)}) copy-start(f32[1,512,8,128]{3,1,2,0:T(8,128)} %get-tuple-element.25) | copy-start | bytes 6291460
  176.0 9.5 %copy-start.1 = (f32[3,512,8,128]{3,2,1,0:T(8,128)}, f32[3,512,8,128]{3,2,1,0:T(8,128)S(1)}, u32[]{:S(2)}) copy-start(f32[3,512,8,128]{3,2,1,0:T(8,128)S(1)} %get-tuple-element.19) | copy-start | bytes 18874372
  176.0 5.1 %copy-start.2 = (f32[3,512,8,128]{3,2,1,0:T(8,128)S(1)}, f32[3,512,8,128]{3,2,1,0:T(8,128)}, u32[]{:S(2)}) copy-start(f32[3,512,8,128]{3,2,1,0:T(8,128)} %get-tuple-element.18) | copy-start | bytes 18874372
  186.7 99.6 %all-to-all-start.1 = ((bf16[2,512,4,128]{3,1,0,2:T(8,128)(2,1)}), bf16[2,512,4,128]{3,1,0,2:T(8,128)(2,1)}, u32[]{:S(2)}, u32[]{:S(2)}) async-start(bf16[2,512,4,128]{3,1,0,2:T(8,128)(2,1)} %copy.64), calls=%async_computation.1 | async-start | bytes 2097152 | tf_op jit(solution)/shard_map/all_to_all | solution.py:149
  199.5 88.3 %copy-start.11 = (bf16[128,2048]{0,1:T(8,128)(2,1)S(1)}, bf16[128,2048]{0,1:T(8,128)(2,1)}, u32[]{:S(2)}) copy-start(bf16[128,2048]{0,1:T(8,128)(2,1)} %copy-done.10) | copy-start | bytes 1572868
  199.5 88.3 %copy-start.13 = (bf16[128,2048]{0,1:T(8,128)(2,1)S(1)}, bf16[128,2048]{0,1:T(8,128)(2,1)}, u32[]{:S(2)}) copy-start(bf16[128,2048]{0,1:T(8,128)(2,1)} %copy-done.12) | copy-start | bytes 1572868
  199.5 88.3 %copy-start.15 = (f32[2048]{0:T(1024)S(1)}, f32[2048]{0:T(1024)}, u32[]{:S(2)}) copy-start(f32[2048]{0:T(1024)} %param.15) | copy-start | bytes 24580
where the time goes:
time: 312 us; the launch traced here: 307 us
  matrix products  119 us (38%)
  blocking collectives  91.8 us (29%)
  waiting for transfers between devices  35.9 us (12%)
  local copies, waits for them, and re-layouts  31.6 us (10%)
  other arithmetic  16.5 us (5%)
  starting transfers between devices  10.7 us (3%)
    dot_general x8, matrix products, contract(): jnp.einsum('lj,mckj->mckl', kernel, array, precision=highest, preferred_e...  82.7 us
    psum x1, blocking collectives, body(): grad_first = lax.psum(first_part, ('ctx', 'ch', 'sub'))  57.8 us
    all_to_all x1, waiting for transfers between devices, body(): lax.all_to_all(jnp.stack([source.T, cotan.T])[:, :, None, :], 'ctx', spli...  35.9 us
    all_gather x1, blocking collectives, body(): grad_second = lax.all_gather(weight_part, 'ctx', axis=1, tiled=True)  24.9 us
    unnamed x42, local copies, waits for them, and re-layouts  15.7 us
    dot_general x2, matrix products, first_section(): jnp.einsum('kn,mcnj->mckj', kernel, fields, precision=highest, preferred_...  9.18 us
    psum x1, blocking collectives, body(): grad_bias = lax.psum(jnp.sum(source * cotan, axis=0), 'ctx')  9.06 us
    broadcast_in_dim x1, local copies, waits for them, and re-layouts, body(): jnp.stack([source.T, cotan.T])[:, :, None, :]  8.55 us
  transfers between devices with their start and end apart: 2, of which 1 were waited for; matrix products, arithmetic and copies ran while one was open for 8% of the time, Pallas kernels for 0%

commit v1 on v0

--- a/solution.py
+++ b/solution.py
@@ -1,12 +1,18 @@
+import functools
 import math
 
 import jax
 import jax.numpy as jnp
+import numpy as np
 from jax import lax
+from jax.experimental import pallas as pl
+from jax.experimental.pallas import tpu as pltpu
 from jax.sharding import PartitionSpec as P
 
 band_steps = (1763, 1201, 811, 547, 367, 251, 167, 113, 79, 53, 37, 23, 17, 11, 7, 3)
 highest = lax.Precision.HIGHEST
+f32 = jnp.float32
+bf16 = jnp.bfloat16
 
 
 def features(positions):
@@ -45,7 +51,9 @@
     )
 
 
-def body(x_one, x_two, values, grad_out, first_weight, second_weight, skip_bias, decay_rate):
+def many_shards_body(
+    x_one, x_two, values, grad_out, first_weight, second_weight, skip_bias, decay_rate
+):
     row_count, chan_count = x_one.shape
     shards = lax.axis_size("ctx")
     rank = lax.axis_index("ctx")
@@ -162,6 +170,406 @@
     return (grad_one, grad_two, grad_value, grad_first, grad_second, grad_bias)
 
 
+def halves(array):
+    array = np.asarray(array, np.float32)
+    high = array.astype(bf16)
+    low = (array - high.astype(np.float32)).astype(bf16)
+    return high, low
+
+
+def block_tables(rows):
+    double = 2 * rows
+    freq = 2 * np.arange(rows)[:, None] + 1
+    place = np.arange(double)[None, :]
+    angle = (freq * place % (2 * double)) * (2.0 * np.pi / (2 * double))
+    full = np.concatenate([np.cos(angle), -np.sin(angle)], axis=0)
+    window = np.concatenate([-full[:, rows:], full[:, :rows]], axis=1)
+    front_high, front_low = halves(full[:, :rows])
+    return dict(
+        front=np.concatenate([front_high, front_low], axis=1),
+        window=halves(window),
+        back=halves(full[:, :rows].T / rows),
+        back_window=halves(window.T / rows),
+    )
+
+
+def feature_table(seq_len):
+    phase = np.arange(seq_len)[:, None] * np.array(band_steps)[None, :] % 4096
+    angle = phase * (2.0 * np.pi / 4096.0)
+    return np.concatenate([np.cos(angle), np.sin(angle)], axis=1).astype(np.float32)
+
+
+def split(array):
+    high = array.astype(bf16)
+    return high, (array - high.astype(f32)).astype(bf16)
+
+
+def dot(left, right):
+    return jnp.dot(left, right, preferred_element_type=f32)
+
+
+def dot_across(left, right):
+    return lax.dot_general(left, right, (((1,), (1,)), ((), ())), preferred_element_type=f32)
+
+
+def decay(rate, first, count, scale):
+    place = lax.broadcasted_iota(jnp.int32, (count, rate.shape[1]), 0) + first
+    return jnp.exp(-place.astype(f32) * rate) * scale
+
+
+def products_kernel(rank_ref, one_ref, two_ref, val_ref, out_ref, source_ref, cotan_ref, edge_ref, bias_ref):
+    source = one_ref[...].astype(f32) * val_ref[...].astype(f32)
+    cotan = out_ref[...].astype(f32) * two_ref[...].astype(f32)
+    source_ref[...] = source.astype(bf16)
+    cotan_ref[...] = cotan.astype(bf16)
+    edge_ref[...] = jnp.where(rank_ref[0] == 0, cotan, source).astype(bf16)
+    bias_ref[...] = jnp.sum(source * cotan, axis=0, keepdims=True)
+
+
+def filter_kernel(rows, shards, hidden_ref, weight_ref, rate_ref, front_ref, win_high_ref, win_low_ref, spec_ref):
+    seq_len = rows * shards
+    w_high, w_low = split(weight_ref[...])
+    stacked = jnp.concatenate([w_high, w_low, w_high], axis=0)
+    filt = dot(hidden_ref[...], stacked) * decay(rate_ref[...], 0, seq_len, float(seq_len) ** -0.5)
+    f_high, f_low = split(filt)
+    first = f_high[:rows]
+    spec_ref[0] = dot(front_ref[...], jnp.concatenate([first, first], axis=0)) + dot(
+        front_ref[:, :rows], f_low[:rows]
+    )
+    for lag in range(1, shards):
+        span = slice((lag - 1) * rows, (lag + 1) * rows)
+        spec_ref[lag] = (
+            dot(win_high_ref[...], f_high[span])
+            + dot(win_low_ref[...], f_high[span])
+            + dot(win_high_ref[...], f_low[span])
+        )
+
+
+def times(a, b):
+    return a[0] * b[0] - a[1] * b[1], a[0] * b[1] + a[1] * b[0]
+
+
+def conj_times(a, b):
+    return a[0] * b[0] + a[1] * b[1], a[0] * b[1] - a[1] * b[0]
+
+
+def plus(a, b):
+    return a[0] + b[0], a[1] + b[1]
+
+
+def main_kernel(
+    rows, shards, step_rows, rank_ref, x0_ref, c0_ref, x1_ref, c1_ref, x2_ref, c2_ref, edge_ref, spec_ref,
+    weight_ref, rate_ref, front_ref, back_high_ref, back_low_ref, bw_high_ref, bw_low_ref, ht_high_ref, ht_low_ref,
+    featt_ref, slope_ref, conv_ref, corr_ref, part_ref, second_ref, first_ref, fields, prod_high, prod_low, hid_acc,
+):
+    rank = rank_ref[0]
+    seq_len = rows * shards
+    lower = rank == 1
+    second = x2_ref[...] + c2_ref[...]
+    blocks = (x0_ref[...], c0_ref[...], x1_ref[...], c1_ref[...], second, edge_ref[...])
+    for index, block in enumerate(blocks):
+        fields[index] = dot(front_ref[...], jnp.concatenate([block, block], axis=0))
+    mask_up = jnp.where(rank == 2, 1.0, 0.0).astype(f32)
+    mask_down = jnp.where(rank == 1, 1.0, 0.0).astype(f32)
+    side = mask_up - mask_down
+
+    def one_step(step, carry):
+        low_rows = pl.ds(pl.multiple_of(step * step_rows, step_rows), step_rows)
+        high_rows = pl.ds(pl.multiple_of(rows + step * step_rows, step_rows), step_rows)
+
+        def get(ref, index):
+            return ref[index, low_rows, :], ref[index, high_rows, :]
+
+        def put(index, value):
+            for part, where in zip(value, (low_rows, high_rows)):
+                high, low = split(part)
+                prod_high[index, where, :] = high
+                prod_low[index, where, :] = low
+
+        x0, c0, x1, c1, far, edge = (get(fields, i) for i in range(6))
+        w0, w1, w2, w3 = (get(spec_ref, i) for i in range(4))
+        x2 = (far[0] * mask_up, far[1] * mask_up)
+        c2 = (far[0] * mask_down, far[1] * mask_down)
+        put(0, plus(plus(times(w0, x0), times(w1, x1)), times(w2, x2)))
+        put(1, plus(plus(conj_times(w0, c0), conj_times(w1, c1)), conj_times(w2, c2)))
+        near = (jnp.where(lower, c1[0], x1[0]), jnp.where(lower, c1[1], x1[1]))
+        w2s = (w2[0], w2[1] * side)
+        w3s = (w3[0], w3[1] * side)
+        put(2, plus(times(w2s, near), times(w3s, far)))
+        own_a = (jnp.where(lower, x1[0], edge[0]), jnp.where(lower, x1[1], edge[1]))
+        own_b = (jnp.where(lower, edge[0], c1[0]), jnp.where(lower, edge[1], c1[1]))
+        put(3, plus(conj_times(x0, c0), conj_times(own_a, own_b)))
+        up = conj_times(x0, c1)
+        put(4, plus(conj_times(x1, c0), (up[0] * mask_up, up[1] * mask_up)))
+        put(5, conj_times(x1, c1))
+        put(6, conj_times(x1, c2))
+        return carry
+
+    lax.fori_loop(0, rows // step_rows, one_step, 0)
+
+    def back(index):
+        return (
+            dot(back_high_ref[...], prod_high[index])
+            + dot(back_low_ref[...], prod_high[index])
+            + dot(back_high_ref[...], prod_low[index])
+        )
+
+    def back_window(index):
+        return (
+            dot(bw_high_ref[...], prod_high[index])
+            + dot(bw_low_ref[...], prod_high[index])
+            + dot(bw_high_ref[...], prod_low[index])
+        )
+
+    part_ref[...] = back(2).astype(bf16)
+    conv_ref[...] = back(0)
+    corr_ref[...] = back(1)
+    wide = [back_window(4 + lag) for lag in range(shards - 1)]
+    grads = [back(3) + wide[0][:rows]]
+    for lag in range(1, shards):
+        tail = wide[lag - 1][rows:]
+        grads.append(tail + wide[lag][:rows] if lag < shards - 1 else tail)
+    rate = rate_ref[...]
+    scale = float(seq_len) ** -0.5
+    grads = [g * decay(rate, lag * rows, rows, scale) for lag, g in enumerate(grads)]
+    m_high, m_low = split(jnp.concatenate(grads, axis=0))
+    second_ref[...] = (
+        dot(ht_high_ref[...], m_high) + dot(ht_low_ref[...], m_high) + dot(ht_high_ref[...], m_low)
+    )
+    w_high, w_low = split(weight_ref[...])
+    hid = dot_across(m_high, w_high) + dot_across(m_low, w_high) + dot_across(m_high, w_low)
+    block = pl.program_id(0)
+
+    @pl.when(block == 0)
+    def _():
+        hid_acc[...] = hid
+
+    @pl.when(block > 0)
+    def _():
+        hid_acc[...] += hid
+
+    @pl.when(block == pl.num_programs(0) - 1)
+    def _():
+        first_ref[...] = jnp.dot(
+            featt_ref[...], hid_acc[...] * slope_ref[...], precision=highest, preferred_element_type=f32
+        )
+
+
+def final_kernel(
+    shards, rank_ref, one_ref, two_ref, val_ref, out_ref, skip_ref, conv_ref, corr_ref, part_ref, *rest
+):
+    grad_one_ref, grad_two_ref, grad_value_ref = rest[-3:]
+    rank = rank_ref[0]
+    part = part_ref[...].astype(f32)
+    zero = jnp.zeros_like(part)
+    one = one_ref[...].astype(f32)
+    val = val_ref[...].astype(f32)
+    out = out_ref[...].astype(f32)
+    skip = skip_ref[...]
+    conv = conv_ref[...] + jnp.where(rank == shards - 1, part, zero)
+    corr = corr_ref[...] + jnp.where(rank == 0, part, zero)
+    grad_two_ref[...] = (out * (conv + skip * (one * val))).astype(bf16)
+    mid = corr + skip * (out * two_ref[...].astype(f32))
+    grad_one_ref[...] = (mid * val).astype(bf16)
+    grad_value_ref[...] = (mid * one).astype(bf16)
+
+
+def few_shards_body(
+    x_one, x_two, values, grad_out, first_weight, second_weight, skip_bias, decay_rate, pieces=2
+):
+    rows, chan_count = x_one.shape
+    shards = lax.axis_size("ctx")
+    hid_count = second_weight.shape[0]
+    feat_count = first_weight.shape[0]
+    seq_len = rows * shards
+    double = 2 * rows
+    narrow = chan_count // pieces
+    width = min(256, narrow)
+    blocks = narrow // width
+    rank = lax.axis_index("ctx")
+    rank_cell = rank.astype(jnp.int32).reshape(1)
+    table = block_tables(rows)
+    skip_row = skip_bias.reshape(1, chan_count)
+    rate_row = decay_rate.reshape(1, chan_count)
+    smem = pl.BlockSpec(memory_space=pltpu.SMEM)
+    params = pltpu.CompilerParams(vmem_limit_bytes=48 * 1024 * 1024)
+
+    def whole(shape):
+        return pl.BlockSpec(shape, lambda i: (0,) * len(shape))
+
+    def local(*lead):
+        return pl.BlockSpec(lead + (width,), lambda i: (0,) * len(lead) + (i,))
+
+    def strip(count, piece):
+        return pl.BlockSpec((count, width), lambda i: (0, piece * blocks + i))
+
+    def shape(*dims, dtype=f32):
+        return jax.ShapeDtypeStruct(dims, dtype)
+
+    def products(piece):
+        gate = strip(rows, piece)
+        return pl.pallas_call(
+            products_kernel,
+            grid=(blocks,),
+            in_specs=[smem, gate, gate, gate, gate],
+            out_specs=[local(rows), local(rows), local(rows), local(1)],
+            out_shape=[shape(rows, narrow, dtype=bf16)] * 3 + [shape(1, narrow)],
+            compiler_params=params,
+            cost_estimate=pl.CostEstimate(
+                flops=6 * rows * narrow, bytes_accessed=14 * rows * narrow, transcendentals=0
+            ),
+            name="products",
+        )(rank_cell, x_one, x_two, values, grad_out)
+
+    def filters(piece, stacked_hidden):
+        return pl.pallas_call(
+            functools.partial(filter_kernel, rows, shards),
+            grid=(blocks,),
+            in_specs=[
+                whole((seq_len, 3 * hid_count)),
+                strip(hid_count, piece),
+                strip(1, piece),
+                whole((double, double)),
+                whole((double, double)),
+                whole((double, double)),
+            ],
+            out_specs=local(shards, double),
+            out_shape=shape(shards, double, narrow),
+            compiler_params=params,
+            cost_estimate=pl.CostEstimate(
+                flops=2 * 14 * double * double * narrow,
+                bytes_accessed=4 * shards * double * narrow,
+                transcendentals=seq_len * narrow,
+            ),
+            name="filters",
+        )(stacked_hidden, second_weight, rate_row, table["front"], *table["window"])
+
+    def main(piece, fields, spec, ht_high, ht_low, featt, slope):
+        return pl.pallas_call(
+            functools.partial(main_kernel, rows, shards, 16),
+            grid=(blocks,),
+            in_specs=[smem]
+            + [local(rows)] * 7
+            + [
+                local(shards, double),
+                strip(hid_count, piece),
+                strip(1, piece),
+                whole((double, double)),
+                whole((rows, double)),
+                whole((rows, double)),
+                whole((double, double)),
+                whole((double, double)),
+                whole((hid_count, seq_len)),
+                whole((hid_count, seq_len)),
+                whole((feat_count, seq_len)),
+                whole((seq_len, hid_count)),
+            ],
+            out_specs=[
+                local(rows),
+                local(rows),
+                local(rows),
+                local(hid_count),
+                whole((feat_count, hid_count)),
+            ],
+            out_shape=[
+                shape(rows, narrow),
+                shape(rows, narrow),
+                shape(rows, narrow, dtype=bf16),
+                shape(hid_count, narrow),
+                shape(feat_count, hid_count),
+            ],
+            scratch_shapes=[
+                pltpu.VMEM((6, double, width), f32),
+                pltpu.VMEM((7, double, width), bf16),
+                pltpu.VMEM((7, double, width), bf16),
+                pltpu.VMEM((seq_len, hid_count), f32),
+            ],
+            compiler_params=params,
+            cost_estimate=pl.CostEstimate(
+                flops=2 * 25 * double * double * narrow,
+                bytes_accessed=6 * shards * double * narrow,
+                transcendentals=seq_len * narrow,
+            ),
+            name="block_products",
+        )(
+            rank_cell, *fields, spec, second_weight, rate_row, table["front"], *table["back"],
+            *table["back_window"], ht_high, ht_low, featt, slope,
+        )
+
+    def final(piece, conv, corr, part, before):
+        gate = strip(rows, piece)
+        held = [pl.BlockSpec(memory_space=pl.ANY)] * len(before)
+        return pl.pallas_call(
+            functools.partial(final_kernel, shards),
+            grid=(blocks,),
+            in_specs=[smem, gate, gate, gate, gate, strip(1, piece)] + [local(rows)] * 3 + held,
+            out_specs=[gate] * 3,
+            out_shape=[shape(rows, chan_count, dtype=bf16)] * 3,
+            input_output_aliases={9 + i: i for i in range(len(before))},
+            compiler_params=params,
+            cost_estimate=pl.CostEstimate(
+                flops=10 * rows * narrow, bytes_accessed=24 * rows * narrow, transcendentals=0
+            ),
+            name="gates",
+        )(rank_cell, x_one, x_two, values, grad_out, skip_row, conv, corr, part, *before)
+
+    def move(array, pairs):
+        return lax.ppermute(array, "ctx", pairs)
+
+    up = [(i, i + 1) for i in range(shards - 1)]
+    down = [(i + 1, i) for i in range(shards - 1)]
+    inward = [(0, 1), (shards - 1, shards - 2)]
+    outward = [(1, 0), (shards - 2, shards - 1)]
+    across = [(1, 2), (2, 1)]
+
+    starts = [products(p) for p in range(pieces)]
+    x1 = [move(s[0], up) for s in starts]
+    c1 = [move(s[1], down) for s in starts]
+    x2 = [move(a, [(1, 2)]) for a in x1]
+    c2 = [move(a, [(2, 1)]) for a in c1]
+    edge = [move(s[2], inward) for s in starts]
+
+    feats = feature_table(seq_len)
+    pre_act = jnp.dot(feats, first_weight, precision=highest, preferred_element_type=f32)
+    hidden = jnp.sin(pre_act)
+    slope = jnp.cos(pre_act)
+    h_high, h_low = split(hidden)
+    stacked_hidden = jnp.concatenate([h_high, h_high, h_low], axis=1)
+    specs = [filters(p, stacked_hidden) for p in range(pieces)]
+
+    bias = jnp.concatenate([s[3] for s in starts], axis=1)
+    bias = bias + move(bias, [(i, i ^ 1) for i in range(shards)])
+    bias = bias + move(bias, [(i, i ^ 2) for i in range(shards)])
+
+    inner = (rank == 1) | (rank == 2)
+    outs = ()
+    seconds = []
+    firsts = []
+    for p in range(pieces):
+        fields = (starts[p][0], starts[p][1], x1[p], c1[p], x2[p], c2[p], edge[p])
+        conv, corr, part, second, first = main(
+            p, fields, specs[p], h_high.T, h_low.T, jnp.asarray(feats.T), slope
+        )
+        outs = final(p, conv, corr, move(part, outward), outs)
+        total = second + move(second, across)
+        seconds.append(jnp.where(inner, total, move(total, outward)))
+        firsts.append(first)
+    first = sum(firsts)
+    group = lax.axis_size(("ch", "sub"))
+
+    def swap(array, bit):
+        return lax.ppermute(array, ("ch", "sub"), [(i, i ^ bit) for i in range(group)])
+
+    bit = 1
+    while bit < group:
+        first = first + swap(first, bit)
+        bit *= 2
+    total = first + move(first, across)
+    grad_first = jnp.where(inner, total, move(total, outward))
+    grad_second = jnp.concatenate(seconds, axis=1)
+    return (*outs, grad_first, grad_second, bias.reshape(chan_count))
+
+
 def solution(mesh):
     in_specs = (
         P(("parts", "ctx"), ("ch", "sub")),
@@ -181,4 +589,5 @@
         P("parts", ("ch", "sub")),
         P(("parts", "ch", "sub")),
     )
+    body = few_shards_body if mesh.shape["ctx"] == 4 else many_shards_body
     return jax.shard_map(body, mesh=mesh, in_specs=in_specs, out_specs=out_specs, check_vma=False)

time: 312 us -> 150 us (0.48)
  matrix products: 119 us -> 1.46 us
  blocking collectives: 91.8 us -> 0 us
  Pallas kernels: 0 us -> 44.5 us
  starting transfers between devices: 10.7 us -> 52.4 us
  waiting for transfers between devices: 35.9 us -> 15.1 us
  other arithmetic: 16.5 us -> 6.47 us
  local copies, waits for them, and re-layouts: 31.6 us -> 26.9 us
    dot_general x21 -> x1, matrix products: 119 us -> 1.46 us  [few_shards_body(): jnp.dot(feats, first_weight, precision=highest, preferred_element_type=f32)]
    psum x2 -> x0, blocking collectives: 66.9 us -> none  [the longest x1 57.8 us: body(): grad_first = lax.psum(first_part, ('ctx', 'ch', 'sub'))]
    ppermute x0 -> x22, starting transfers between devices: none -> 52.4 us  [the longest x20 50.9 us: move(): return lax.ppermute(array, 'ctx', pairs)]
    pallas_call x0 -> x8, Pallas kernels: none -> 44.5 us  [the longest x2 29.2 us: main(): pl.pallas_call(functools.partial(main_kernel, rows, shards, 16), grid=(bl...]
    all_to_all x2 -> x0, waiting for transfers between devices: 35.9 us -> none  [the longest x1 35.9 us: body(): lax.all_to_all(jnp.stack([source.T, cotan.T])[:, :, None, :], 'ctx', spli...]
    all_gather x1 -> x0, blocking collectives: 24.9 us -> none  [body(): grad_second = lax.all_gather(weight_part, 'ctx', axis=1, tiled=True)]
    ppermute x0 -> x22, waiting for transfers between devices: none -> 15.1 us  [the longest x20 14.9 us: move(): return lax.ppermute(array, 'ctx', pairs)]
    all_to_all x2 -> x0, starting transfers between devices: 10.7 us -> none  [the longest x1 6.47 us: body(): lax.all_to_all(jnp.stack([source.T, cotan.T])[:, :, None, :], 'ctx', spli...]
  transfers between devices with their start and end apart: 2 -> 22, of which waited for: 1 -> 4; matrix products, arithmetic and copies ran while one was open for 8% -> 7% of each run, Pallas kernels for 0% -> 30%
where the time goes in v1:
time: 150 us; the launch traced here: 148 us
  starting transfers between devices  52.4 us (35%)
  Pallas kernels  44.5 us (30%)
  local copies, waits for them, and re-layouts  26.9 us (18%)
  waiting for transfers between devices  15.1 us (10%)
  other arithmetic  6.47 us (4%)
    ppermute x20, starting transfers between devices, move(): return lax.ppermute(array, 'ctx', pairs)  50.9 us
    pallas_call x2, Pallas kernels, main(): pl.pallas_call(functools.partial(main_kernel, rows, shards, 16), grid=(bl...  29.2 us
    unnamed x93, local copies, waits for them, and re-layouts  24 us
    ppermute x20, waiting for transfers between devices, move(): return lax.ppermute(array, 'ctx', pairs)  14.9 us
    pallas_call x2, Pallas kernels, final(): pl.pallas_call(functools.partial(final_kernel, shards), grid=(blocks,), i...  6.65 us
    pallas_call x2, Pallas kernels, filters(): pl.pallas_call(functools.partial(filter_kernel, rows, shards), grid=(bloc...  6.51 us
  transfers between devices with their start and end apart: 22, of which 4 were waited for; matrix products, arithmetic and copies ran while one was open for 7% of the time, Pallas kernels for 30%

profile of v1, /device:TPU:0, one launch (start us, length us, event | category | flops | bytes accessed | tf_op | source)
XLA Modules:
  0.0 148.1 jit_solution(1374556509912895201)
XLA Ops:
  0.7 1.0 copy-done.1
  1.7 1.0 copy-done.3
  2.8 1.0 copy-done.5
  3.8 1.0 copy-done.7
  5.4 4.9 %collective-permute-start = (bf16[128,1024]{1,0:T(8,128)(2,1)S(1)}, bf16[128,1024]{1,0:T(8,128)(2,1)S(1)}, u32[]{:S(2)}, u32[]{:S(2)}) collective-permute-start(bf16[128,1024]{1,0:T(8,128)(2,1)S(1)} %get-tuple-element.30.x0_ref), channel_id=1, source_target_pairs={{0,4},{4,8},{8,12},{1,5},{5,9},{9,13},{2,6},{6,10},{10,14},{3,7},{... | collective-permute-start | bytes 786440 | tf_op jit(solution)/shard_map/ppermute | solution.py:517
  10.3 1.3 collective-permute-start.1
  11.6 4.6 %collective-permute-start.4 = (bf16[128,1024]{1,0:T(8,128)(2,1)S(1)}, bf16[128,1024]{1,0:T(8,128)(2,1)S(1)}, u32[]{:S(2)}, u32[]{:S(2)}) collective-permute-start(bf16[128,1024]{1,0:T(8,128)(2,1)S(1)} %get-tuple-element.32), channel_id=1, source_target_pairs={{0,4},{12,8},{1,5},{13,9},{2,6},{14,10},{3,7},{15,11},{16,20},{28,... | collective-permute-start | bytes 786440 | tf_op jit(solution)/shard_map/ppermute | solution.py:517
  16.2 1.6 %products.3 = (bf16[128,1024]{1,0:T(8,128)(2,1)S(1)}, bf16[128,1024]{1,0:T(8,128)(2,1)S(1)}, bf16[128,1024]{1,0:T(8,128)(2,1)}, f32[1,1024]{1,0:T(1,128)S(1)}) custom-call(s32[1]{0:T(128)} %bitcast.rank_ref, bf16[128,2048]{1,0:T(8,128)(2,1)S(1)} %copy-done.1, bf16[128,2048]{1,0:T(8,128)(2,1)S(1)} %copy-done.3, bf16[128,2048]{1,0:T(8,128)(2,1)S(1)} %copy-done.5, ...), custom_call_target="tpu_custom_call" | custom-call | flops 786432 | bytes 1835008 | tf_op jit(solution)/shard_map/products/pallas_call | solution.py:411
  17.9 1.3 collective-permute-start.6
  19.2 1.3 collective-permute-start.7
  20.5 1.5 fusion.1
  22.6 0.7 pad_maximum_fusion.1
  23.3 1.1 copy.27.hidden_ref
  24.4 0.9 copy-done.36
  25.3 3.3 %filters.2.spec_ref = f32[4,256,1024]{2,1,0:T(8,128)S(1)} custom-call(bf16[512,192]{1,0:T(8,128)(2,1)S(1)} %copy.27.hidden_ref, f32[64,2048]{1,0:T(8,128)S(1)} %copy-done.14, f32[1,2048]{1,0:T(1,128)S(1)} %bitcast.14, bf16[256,256]{1,0:T(8,128)(2,1)S(1)} %copy-done.29, bf16[256,256]{1,0:T(8,128)(2,1)S(1)} %copy-done.34, bf16[256,256]{1,0:T(8,128)(2,1)S(1)} %copy-done.36), custom_call_target="tpu_custom_call" | custom-call | flops 1879048192 | bytes 4194304 | tf_op jit(solution)/shard_map/filters/pallas_call | solution.py:425
  28.6 2.0 %copy-done.43 = f32[4,256,1024]{2,1,0:T(8,128)} copy-done((f32[4,256,1024]{2,1,0:T(8,128)}, f32[4,256,1024]{2,1,0:T(8,128)S(1)}, u32[]{:S(2)}) %copy-start.43) | copy-done | bytes 4194328
  30.7 0.7 collective-permute-start.2
  31.4 1.4 collective-permute-start.3
  32.7 0.9 copy-done.30
  33.6 3.2 %filters.3.spec_ref = f32[4,256,1024]{2,1,0:T(8,128)S(1)} custom-call(bf16[512,192]{1,0:T(8,128)(2,1)S(1)} %copy.27.hidden_ref, f32[64,2048]{1,0:T(8,128)S(1)} %copy-done.14, f32[1,2048]{1,0:T(1,128)S(1)} %bitcast.15, bf16[256,256]{1,0:T(8,128)(2,1)S(1)} %copy-done.30, bf16[256,256]{1,0:T(8,128)(2,1)S(1)} %copy-done.35, bf16[256,256]{1,0:T(8,128)(2,1)S(1)} %copy-done.37), custom_call_target="tpu_custom_call" | custom-call | flops 1879048192 | bytes 4194304 | tf_op jit(solution)/shard_map/filters/pallas_call | solution.py:425
  36.9 2.0 %copy-done.42 = f32[4,256,1024]{2,1,0:T(8,128)} copy-done((f32[4,256,1024]{2,1,0:T(8,128)}, f32[4,256,1024]{2,1,0:T(8,128)S(1)}, u32[]{:S(2)}) %copy-start.42) | copy-done | bytes 4194328
  38.9 1.0 copy.28
  39.9 0.8 cos.3.slope_ref
  40.8 0.9 fusion
  41.7 0.7 copy-done.24
  42.4 7.9 %collective-permute-start.10 = (bf16[128,1024]{1,0:T(8,128)(2,1)}, bf16[128,1024]{1,0:T(8,128)(2,1)S(1)}, u32[]{:S(2)}, u32[]{:S(2)}) collective-permute-start(bf16[128,1024]{1,0:T(8,128)(2,1)} %get-tuple-element.38), channel_id=1, source_target_pairs={{0,4},{12,8},{1,5},{13,9},{2,6},{14,10},{3,7},{15,11},{16,20},{28,... | collective-permute-start | bytes 786440 | tf_op jit(solution)/shard_map/ppermute | solution.py:517
  50.3 0.7 collective-permute-start.8
  51.0 0.7 collective-permute-start.9
  51.7 0.7 copy-done.26
  52.5 0.9 copy-done.23
  53.4 0.9 copy-done.25
  54.4 0.9 copy-done.27
  55.3 0.9 copy-done.31
  56.2 0.9 copy-done.32
  57.1 0.9 copy-done.33
  58.0 0.8 copy-done.39
  58.9 0.8 copy-done.41
  59.7 14.6 %block_products.2 = (f32[128,1024]{1,0:T(8,128)S(1)}, f32[128,1024]{1,0:T(8,128)S(1)}, bf16[128,1024]{1,0:T(8,128)(2,1)}, f32[64,1024]{1,0:T(8,128)S(1)}, f32[32,64]{1,0:T(8,128)S(1)}) custom-call(s32[1]{0:T(128)} %bitcast.rank_ref, bf16[128,1024]{1,0:T(8,128)(2,1)S(1)} %get-tuple-element.30.x0_ref, bf16[128,1024]{1,0:T(8,128)(2,1)S(1)} %get-tuple-element.31.c0_ref, ...), custom_call_target="tpu_custom_call" | custom-call | flops 3355443200 | bytes 6291456 | tf_op jit(solution)/shard_map/block_products/pallas_call | solution.py:448
  74.4 0.8 collective-permute-start.18
  75.3 0.9 copy-done.21
  76.2 14.5 %block_products.3 = (f32[128,1024]{1,0:T(8,128)S(1)}, f32[128,1024]{1,0:T(8,128)S(1)}, bf16[128,1024]{1,0:T(8,128)(2,1)}, f32[64,1024]{1,0:T(8,128)S(1)}, f32[32,64]{1,0:T(8,128)S(1)}) custom-call(s32[1]{0:T(128)} %bitcast.rank_ref, bf16[128,1024]{1,0:T(8,128)(2,1)S(1)} %copy-done.17, bf16[128,1024]{1,0:T(8,128)(2,1)S(1)} %copy-done.19, ...), custom_call_target="tpu_custom_call" | custom-call | flops 3355443200 | bytes 6291456 | tf_op jit(solution)/shard_map/block_products/pallas_call | solution.py:448
  90.8 0.8 copy-done.9
  91.6 0.8 copy-done.11
  92.3 1.4 collective-permute-start.16
  93.8 1.3 collective-permute-start.5
  95.1 1.3 collective-permute-start.11
  96.4 1.6 %collective-permute-start.13 = (f32[32,64]{1,0:T(8,128)S(1)}, f32[32,64]{1,0:T(8,128)S(1)}, u32[]{:S(2)}, u32[]{:S(2)}) collective-permute-start(f32[32,64]{1,0:T(8,128)S(1)} %add.25), channel_id=1, source_target_pairs={{0,2},{1,3},{2,0},{3,1},{4,6},{5,7},{6,4},{7,5},{8,10},{9,11},{10,... | collective-permute-start | bytes 24584 | tf_op jit(solution)/shard_map/ppermute | solution.py:561
  97.9 0.7 add.29
  98.7 1.3 collective-permute-start.19
  100.2 10.9 %collective-permute-start.20 = (f32[1,2048]{1,0:T(1,128)S(1)}, f32[1,2048]{1,0:T(1,128)S(1)}, u32[]{:S(2)}, u32[]{:S(2)}) collective-permute-start(f32[1,2048]{1,0:T(1,128)S(1)} %constant_dynamic-update-slice_fusion), channel_id=1, source_target_pairs={{0,4},{4,0},{8,12},{12,8},{1,5},{5,1},{9,13},{13,9},{2,6},{6,2},{1... | collective-permute-start | bytes 24584 | tf_op jit(solution)/shard_map/ppermute | solution.py:517
  111.1 11.6 %collective-permute-done.20 = f32[1,2048]{1,0:T(1,128)S(1)} collective-permute-done((f32[1,2048]{1,0:T(1,128)S(1)}, f32[1,2048]{1,0:T(1,128)S(1)}, u32[]{:S(2)}, u32[]{:S(2)}) %collective-permute-start.20) | collective-permute-done | bytes 8224 | tf_op jit(solution)/shard_map/ppermute | solution.py:517
  122.7 0.7 collective-permute-start.14
  123.4 6.0 %collective-permute-start.21 = (f32[1,2048]{1,0:T(1,128)S(1)}, f32[1,2048]{1,0:T(1,128)S(1)}, u32[]{:S(2)}, u32[]{:S(2)}) collective-permute-start(f32[1,2048]{1,0:T(1,128)S(1)} %add.30), channel_id=1, source_target_pairs={{0,8},{4,12},{8,0},{12,4},{1,9},{5,13},{9,1},{13,5},{2,10},{6,14},... | collective-permute-start | bytes 24584 | tf_op jit(solution)/shard_map/ppermute | solution.py:517
  129.4 1.6 %collective-permute-done.21 = f32[1,2048]{1,0:T(1,128)S(1)} collective-permute-done((f32[1,2048]{1,0:T(1,128)S(1)}, f32[1,2048]{1,0:T(1,128)S(1)}, u32[]{:S(2)}, u32[]{:S(2)}) %collective-permute-start.21) | collective-permute-done | bytes 8224 | tf_op jit(solution)/shard_map/ppermute | solution.py:517
  131.0 1.3 collective-permute-start.15
  132.9 1.0 add.28
  133.9 1.3 collective-permute-start.17
  135.2 1.6 %collective-permute-done.15 = f32[32,64]{1,0:T(8,128)S(1)} collective-permute-done((f32[32,64]{1,0:T(8,128)S(1)}, f32[32,64]{1,0:T(8,128)S(1)}, u32[]{:S(2)}, u32[]{:S(2)}) %collective-permute-start.15) | collective-permute-done | bytes 8224 | tf_op jit(solution)/shard_map/ppermute | solution.py:517
  137.5 1.0 copy-done.10
  138.5 1.0 copy-done.12
  139.5 3.3 %gates.2 = (bf16[128,2048]{1,0:T(8,128)(2,1)}, bf16[128,2048]{1,0:T(8,128)(2,1)}, bf16[128,2048]{1,0:T(8,128)(2,1)}) custom-call(s32[1]{0:T(128)} %bitcast.rank_ref, bf16[128,2048]{1,0:T(8,128)(2,1)S(1)} %copy-done.2, bf16[128,2048]{1,0:T(8,128)(2,1)S(1)} %copy-done.4, bf16[128,2048]{1,0:T(8,128)(2,1)S(1)} %copy-done.6, bf16[128,2048]{1,0:T(8,128)(2,1)S(1)} %copy-done.8, ...), custom_call_target="tpu_custom_call" | custom-call | flops 1310720 | bytes 3145728 | tf_op jit(solution)/shard_map/gates/pallas_call | solution.py:502
  142.9 3.3 %gates.3 = (bf16[128,2048]{1,0:T(8,128)(2,1)}, bf16[128,2048]{1,0:T(8,128)(2,1)}, bf16[128,2048]{1,0:T(8,128)(2,1)}) custom-call(s32[1]{0:T(128)} %bitcast.rank_ref, bf16[128,2048]{1,0:T(8,128)(2,1)S(1)} %copy-done.2, bf16[128,2048]{1,0:T(8,128)(2,1)S(1)} %copy-done.4, ...), custom_call_target="tpu_custom_call", output_to_operand_aliasing={{0}: (9, {}), {1}: (10, {}), {2}: (11, {})} | custom-call | flops 1310720 | bytes 3145728 | tf_op jit(solution)/shard_map/gates/pallas_call | solution.py:502
  146.2 1.0 broadcast_select_fusion
  147.2 0.8 pad_maximum_fusion
  (101 shorter events, 2.9 us)
Async XLA Ops:
  0.6 19.8 %copy-start = (f32[32,64]{1,0:T(8,128)S(1)}, f32[32,64]{1,0:T(8,128)}, u32[]{:S(2)}) copy-start(f32[32,64]{1,0:T(8,128)} %param.22) | copy-start | bytes 24580
  0.6 23.7 %copy-start.28 = (f32[2048]{0:T(1024)S(1)}, f32[2048]{0:T(1024)}, u32[]{:S(2)}) copy-start(f32[2048]{0:T(1024)} %param.25) | copy-start | bytes 24580
  0.7 1.0 copy-start.1
  1.7 1.0 copy-start.3
  2.8 1.0 copy-start.5
  3.8 1.0 copy-start.7
  4.8 15.6 %copy-start.45 = (f32[512,32]{1,0:T(8,128)S(1)}, f32[512,32]{1,0:T(8,128)}, u32[]{:S(2)}) copy-start(f32[512,32]{1,0:T(8,128)} %constant.27.clone) | copy-start | bytes 196612
  4.8 19.5 %copy-start.14 = (f32[64,2048]{1,0:T(8,128)S(1)}, f32[64,2048]{1,0:T(8,128)}, u32[]{:S(2)}) copy-start(f32[64,2048]{1,0:T(8,128)} %weight_ref.7) | copy-start | bytes 1572868
  4.8 19.5 %copy-start.29 = (bf16[256,256]{1,0:T(8,128)(2,1)S(1)}, bf16[256,256]{1,0:T(8,128)(2,1)}, u32[]{:S(2)}) copy-start(bf16[256,256]{1,0:T(8,128)(2,1)} %constant.28.clone.front_ref) | copy-start | bytes 393220
  4.8 19.5 %copy-start.34 = (bf16[256,256]{1,0:T(8,128)(2,1)S(1)}, bf16[256,256]{1,0:T(8,128)(2,1)}, u32[]{:S(2)}) copy-start(bf16[256,256]{1,0:T(8,128)(2,1)} %constant.29.clone.win_high_ref) | copy-start | bytes 393220
  5.4 25.3 %collective-permute-start = (bf16[128,1024]{1,0:T(8,128)(2,1)S(1)}, bf16[128,1024]{1,0:T(8,128)(2,1)S(1)}, u32[]{:S(2)}, u32[]{:S(2)}) collective-permute-start(bf16[128,1024]{1,0:T(8,128)(2,1)S(1)} %get-tuple-element.30.x0_ref), channel_id=1, source_target_pairs={{0,4},{4,8},{8,12},{1,5},{5,9},{9,13},{2,6},{6,10},{10,14},{3,7},{... | collective-permute-start | bytes 786440 | tf_op jit(solution)/shard_map/ppermute | solution.py:517
  10.3 21.0 %collective-permute-start.1 = (bf16[128,1024]{1,0:T(8,128)(2,1)S(1)}, bf16[128,1024]{1,0:T(8,128)(2,1)S(1)}, u32[]{:S(2)}, u32[]{:S(2)}) collective-permute-start(bf16[128,1024]{1,0:T(8,128)(2,1)S(1)} %get-tuple-element.31.c0_ref), channel_id=1, source_target_pairs={{4,0},{8,4},{12,8},{5,1},{9,5},{13,9},{6,2},{10,6},{14,10},{7,3},{... | collective-permute-start | bytes 786440 | tf_op jit(solution)/shard_map/ppermute | solution.py:517
  11.6 30.0 %collective-permute-start.4 = (bf16[128,1024]{1,0:T(8,128)(2,1)S(1)}, bf16[128,1024]{1,0:T(8,128)(2,1)S(1)}, u32[]{:S(2)}, u32[]{:S(2)}) collective-permute-start(bf16[128,1024]{1,0:T(8,128)(2,1)S(1)} %get-tuple-element.32), channel_id=1, source_target_pairs={{0,4},{12,8},{1,5},{13,9},{2,6},{14,10},{3,7},{15,11},{16,20},{28,... | collective-permute-start | bytes 786440 | tf_op jit(solution)/shard_map/ppermute | solution.py:517
  17.8 10.8 %copy-start.16 = (bf16[128,1024]{1,0:T(8,128)(2,1)}, bf16[128,1024]{1,0:T(8,128)(2,1)S(1)}, u32[]{:S(2)}) copy-start(bf16[128,1024]{1,0:T(8,128)(2,1)S(1)} %get-tuple-element.36.x0_ref) | copy-start | bytes 786436
  17.8 10.8 %copy-start.18 = (bf16[128,1024]{1,0:T(8,128)(2,1)}, bf16[128,1024]{1,0:T(8,128)(2,1)S(1)}, u32[]{:S(2)}) copy-start(bf16[128,1024]{1,0:T(8,128)(2,1)S(1)} %get-tuple-element.37.c0_ref) | copy-start | bytes 786436
  17.9 32.5 %collective-permute-start.6 = (bf16[128,1024]{1,0:T(8,128)(2,1)S(1)}, bf16[128,1024]{1,0:T(8,128)(2,1)S(1)}, u32[]{:S(2)}, u32[]{:S(2)}) collective-permute-start(bf16[128,1024]{1,0:T(8,128)(2,1)S(1)} %get-tuple-element.36.x0_ref), channel_id=1, source_target_pairs={{0,4},{4,8},{8,12},{1,5},{5,9},{9,13},{2,6},{6,10},{10,14},{3,7},{... | collective-permute-start | bytes 786440 | tf_op jit(solution)/shard_map/ppermute | solution.py:517
  19.2 31.9 %collective-permute-start.7 = (bf16[128,1024]{1,0:T(8,128)(2,1)S(1)}, bf16[128,1024]{1,0:T(8,128)(2,1)}, u32[]{:S(2)}, u32[]{:S(2)}) collective-permute-start(bf16[128,1024]{1,0:T(8,128)(2,1)S(1)} %get-tuple-element.37.c0_ref), channel_id=1, source_target_pairs={{4,0},{8,4},{12,8},{5,1},{9,5},{13,9},{6,2},{10,6},{14,10},{7,3},{... | collective-permute-start | bytes 786440 | tf_op jit(solution)/shard_map/ppermute | solution.py:517
  24.3 8.4 %copy-start.35 = (bf16[256,256]{1,0:T(8,128)(2,1)S(1)}, bf16[256,256]{1,0:T(8,128)(2,1)}, u32[]{:S(2)}) copy-start(bf16[256,256]{1,0:T(8,128)(2,1)} %constant.29.clone.win_high_ref) | copy-start | bytes 393220
  24.4 0.9 copy-start.36
  25.3 7.4 %copy-start.37 = (bf16[256,256]{1,0:T(8,128)(2,1)S(1)}, bf16[256,256]{1,0:T(8,128)(2,1)}, u32[]{:S(2)}) copy-start(bf16[256,256]{1,0:T(8,128)(2,1)} %constant.30.clone.win_low_ref) | copy-start | bytes 393220
  25.3 27.1 %copy-start.38 = (bf16[128,256]{1,0:T(8,128)(2,1)S(1)}, bf16[128,256]{1,0:T(8,128)(2,1)}, u32[]{:S(2)}) copy-start(bf16[128,256]{1,0:T(8,128)(2,1)} %constant.32.clone.back_high_ref) | copy-start | bytes 196612
  28.6 2.0 %copy-start.43 = (f32[4,256,1024]{2,1,0:T(8,128)}, f32[4,256,1024]{2,1,0:T(8,128)S(1)}, u32[]{:S(2)}) copy-start(f32[4,256,1024]{2,1,0:T(8,128)S(1)} %filters.2.spec_ref) | copy-start | bytes 12582916
  30.7 21.1 %collective-permute-start.2 = (bf16[128,1024]{1,0:T(8,128)(2,1)S(1)}, bf16[128,1024]{1,0:T(8,128)(2,1)S(1)}, u32[]{:S(2)}, u32[]{:S(2)}) collective-permute-start(bf16[128,1024]{1,0:T(8,128)(2,1)S(1)} %collective-permute-done.x1_ref), channel_id=1, source_target_pairs={{4,8},{5,9},{6,10},{7,11},{20,24},{21,25},{22,26},{23,27}} | collective-permute-start | bytes 786440 | tf_op jit(solution)/shard_map/ppermute | solution.py:517
  31.3 21.1 %copy-start.22 = (bf16[128,1024]{1,0:T(8,128)(2,1)}, bf16[128,1024]{1,0:T(8,128)(2,1)S(1)}, u32[]{:S(2)}) copy-start(bf16[128,1024]{1,0:T(8,128)(2,1)S(1)} %collective-permute-done.1.c1_ref) | copy-start | bytes 786436
  31.4 21.1 %collective-permute-start.3 = (bf16[128,1024]{1,0:T(8,128)(2,1)S(1)}, bf16[128,1024]{1,0:T(8,128)(2,1)}, u32[]{:S(2)}, u32[]{:S(2)}) collective-permute-start(bf16[128,1024]{1,0:T(8,128)(2,1)S(1)} %collective-permute-done.1.c1_ref), channel_id=1, source_target_pairs={{8,4},{9,5},{10,6},{11,7},{24,20},{25,21},{26,22},{27,23}} | collective-permute-start | bytes 786440 | tf_op jit(solution)/shard_map/ppermute | solution.py:517
  32.7 0.9 copy-start.30
  36.9 2.0 %copy-start.42 = (f32[4,256,1024]{2,1,0:T(8,128)}, f32[4,256,1024]{2,1,0:T(8,128)S(1)}, u32[]{:S(2)}) copy-start(f32[4,256,1024]{2,1,0:T(8,128)S(1)} %filters.3.spec_ref) | copy-start | bytes 12582916
  42.4 32.8 %collective-permute-start.10 = (bf16[128,1024]{1,0:T(8,128)(2,1)}, bf16[128,1024]{1,0:T(8,128)(2,1)S(1)}, u32[]{:S(2)}, u32[]{:S(2)}) collective-permute-start(bf16[128,1024]{1,0:T(8,128)(2,1)} %get-tuple-element.38), channel_id=1, source_target_pairs={{0,4},{12,8},{1,5},{13,9},{2,6},{14,10},{3,7},{15,11},{16,20},{28,... | collective-permute-start | bytes 786440 | tf_op jit(solution)/shard_map/ppermute | solution.py:517
  50.3 24.0 %copy-start.20 = (bf16[128,1024]{1,0:T(8,128)(2,1)}, bf16[128,1024]{1,0:T(8,128)(2,1)S(1)}, u32[]{:S(2)}) copy-start(bf16[128,1024]{1,0:T(8,128)(2,1)S(1)} %collective-permute-done.6.x1_ref) | copy-start | bytes 786436
  50.3 24.9 %collective-permute-start.8 = (bf16[128,1024]{1,0:T(8,128)(2,1)S(1)}, bf16[128,1024]{1,0:T(8,128)(2,1)S(1)}, u32[]{:S(2)}, u32[]{:S(2)}) collective-permute-start(bf16[128,1024]{1,0:T(8,128)(2,1)S(1)} %collective-permute-done.6.x1_ref), channel_id=1, source_target_pairs={{4,8},{5,9},{6,10},{7,11},{20,24},{21,25},{22,26},{23,27}} | collective-permute-start | bytes 786440 | tf_op jit(solution)/shard_map/ppermute | solution.py:517
  51.0 24.2 %collective-permute-start.9 = (bf16[128,1024]{1,0:T(8,128)(2,1)}, bf16[128,1024]{1,0:T(8,128)(2,1)S(1)}, u32[]{:S(2)}, u32[]{:S(2)}) collective-permute-start(bf16[128,1024]{1,0:T(8,128)(2,1)} %collective-permute-done.7.c1_ref), channel_id=1, source_target_pairs={{8,4},{9,5},{10,6},{11,7},{24,20},{25,21},{26,22},{27,23}} | collective-permute-start | bytes 786440 | tf_op jit(solution)/shard_map/ppermute | solution.py:517
  52.4 1.0 copy-start.23
  53.4 0.9 copy-start.25
  54.4 0.9 copy-start.27
  55.3 0.9 copy-start.31
  56.2 0.9 copy-start.32
  57.1 0.9 copy-start.33
  58.0 0.8 copy-start.39
  58.9 0.8 copy-start.41
  59.7 15.6 %copy-start.15 = (f32[64,2048]{1,0:T(8,128)S(1)}, f32[64,2048]{1,0:T(8,128)}, u32[]{:S(2)}) copy-start(f32[64,2048]{1,0:T(8,128)} %weight_ref.7) | copy-start | bytes 1572868
  59.7 15.6 %copy-start.17 = (bf16[128,1024]{1,0:T(8,128)(2,1)S(1)}, bf16[128,1024]{1,0:T(8,128)(2,1)}, u32[]{:S(2)}) copy-start(bf16[128,1024]{1,0:T(8,128)(2,1)} %copy-done.16) | copy-start | bytes 786436
  59.7 15.6 %copy-start.19 = (bf16[128,1024]{1,0:T(8,128)(2,1)S(1)}, bf16[128,1024]{1,0:T(8,128)(2,1)}, u32[]{:S(2)}) copy-start(bf16[128,1024]{1,0:T(8,128)(2,1)} %copy-done.18) | copy-start | bytes 786436
  59.7 15.6 %copy-start.40 = (bf16[128,256]{1,0:T(8,128)(2,1)S(1)}, bf16[128,256]{1,0:T(8,128)(2,1)}, u32[]{:S(2)}) copy-start(bf16[128,256]{1,0:T(8,128)(2,1)} %constant.33.clone.back_low_ref) | copy-start | bytes 196612
  74.3 63.1 %copy-start.2 = (bf16[128,2048]{1,0:T(8,128)(2,1)S(1)}, bf16[128,2048]{1,0:T(8,128)(2,1)}, u32[]{:S(2)}) copy-start(bf16[128,2048]{1,0:T(8,128)(2,1)} %one_ref.7) | copy-start | bytes 1572868
  74.4 63.1 %copy-start.4 = (bf16[128,2048]{1,0:T(8,128)(2,1)S(1)}, bf16[128,2048]{1,0:T(8,128)(2,1)}, u32[]{:S(2)}) copy-start(bf16[128,2048]{1,0:T(8,128)(2,1)} %two_ref.7) | copy-start | bytes 1572868
  74.4 63.1 %copy-start.6 = (bf16[128,2048]{1,0:T(8,128)(2,1)S(1)}, bf16[128,2048]{1,0:T(8,128)(2,1)}, u32[]{:S(2)}) copy-start(bf16[128,2048]{1,0:T(8,128)(2,1)} %val_ref.7) | copy-start | bytes 1572868
  74.4 63.1 %copy-start.8 = (bf16[128,2048]{1,0:T(8,128)(2,1)S(1)}, bf16[128,2048]{1,0:T(8,128)(2,1)}, u32[]{:S(2)}) copy-start(bf16[128,2048]{1,0:T(8,128)(2,1)} %out_ref.7) | copy-start | bytes 1572868
  74.4 63.1 %copy-start.13 = (f32[2048]{0:T(1024)S(1)}, f32[2048]{0:T(1024)}, u32[]{:S(2)}) copy-start(f32[2048]{0:T(1024)} %param.24) | copy-start | bytes 24580
  74.4 23.5 %collective-permute-start.18 = (f32[64,1024]{1,0:T(8,128)S(1)}, f32[64,1024]{1,0:T(8,128)S(1)}, u32[]{:S(2)}, u32[]{:S(2)}) collective-permute-start(f32[64,1024]{1,0:T(8,128)S(1)} %get-tuple-element.51), channel_id=1, source_target_pairs={{4,8},{8,4},{5,9},{9,5},{6,10},{10,6},{7,11},{11,7},{20,24},{24,20... | collective-permute-start | bytes 786440 | tf_op jit(solution)/shard_map/ppermute | solution.py:517
  75.3 1.0 copy-start.21
  90.8 0.8 copy-start.9
  92.3 40.6 %collective-permute-start.16 = (f32[64,1024]{1,0:T(8,128)S(1)}, f32[64,1024]{1,0:T(8,128)}, u32[]{:S(2)}, u32[]{:S(2)}) collective-permute-start(f32[64,1024]{1,0:T(8,128)S(1)} %get-tuple-element.50), channel_id=1, source_target_pairs={{4,8},{8,4},{5,9},{9,5},{6,10},{10,6},{7,11},{11,7},{20,24},{24,20... | collective-permute-start | bytes 786440 | tf_op jit(solution)/shard_map/ppermute | solution.py:517
  93.7 2.6 %collective-permute-start.12 = (f32[32,64]{1,0:T(8,128)S(1)}, f32[32,64]{1,0:T(8,128)S(1)}, u32[]{:S(2)}, u32[]{:S(2)}) collective-permute-start(f32[32,64]{1,0:T(8,128)S(1)} %add.24), channel_id=1, source_target_pairs={{0,1},{1,0},{2,3},{3,2},{4,5},{5,4},{6,7},{7,6},{8,9},{9,8},{10,11... | collective-permute-start | bytes 24584 | tf_op jit(solution)/shard_map/ppermute | solution.py:561
  93.8 49.1 %collective-permute-start.5 = (bf16[128,1024]{1,0:T(8,128)(2,1)}, bf16[128,1024]{1,0:T(8,128)(2,1)}, u32[]{:S(2)}, u32[]{:S(2)}) collective-permute-start(bf16[128,1024]{1,0:T(8,128)(2,1)} %get-tuple-element.35), channel_id=1, source_target_pairs={{4,0},{8,12},{5,1},{9,13},{6,2},{10,14},{7,3},{11,15},{20,16},{24,... | collective-permute-start | bytes 786440 | tf_op jit(solution)/shard_map/ppermute | solution.py:517
  95.1 42.4 %collective-permute-start.11 = (bf16[128,1024]{1,0:T(8,128)(2,1)}, bf16[128,1024]{1,0:T(8,128)(2,1)}, u32[]{:S(2)}, u32[]{:S(2)}) collective-permute-start(bf16[128,1024]{1,0:T(8,128)(2,1)} %get-tuple-element.41), channel_id=1, source_target_pairs={{4,0},{8,12},{5,1},{9,13},{6,2},{10,14},{7,3},{11,15},{20,16},{24,... | collective-permute-start | bytes 786440 | tf_op jit(solution)/shard_map/ppermute | solution.py:517
  96.4 3.8 %collective-permute-start.13 = (f32[32,64]{1,0:T(8,128)S(1)}, f32[32,64]{1,0:T(8,128)S(1)}, u32[]{:S(2)}, u32[]{:S(2)}) collective-permute-start(f32[32,64]{1,0:T(8,128)S(1)} %add.25), channel_id=1, source_target_pairs={{0,2},{1,3},{2,0},{3,1},{4,6},{5,7},{6,4},{7,5},{8,10},{9,11},{10,... | collective-permute-start | bytes 24584 | tf_op jit(solution)/shard_map/ppermute | solution.py:561
  98.7 47.5 %collective-permute-start.19 = (f32[64,1024]{1,0:T(8,128)}, f32[64,1024]{1,0:T(8,128)}, u32[]{:S(2)}, u32[]{:S(2)}) collective-permute-start(f32[64,1024]{1,0:T(8,128)} %add.29), channel_id=1, source_target_pairs={{4,0},{8,12},{5,1},{9,13},{6,2},{10,14},{7,3},{11,15},{20,16},{24,... | collective-permute-start | bytes 786440 | tf_op jit(solution)/shard_map/ppermute | solution.py:517
  100.2 22.5 %collective-permute-start.20 = (f32[1,2048]{1,0:T(1,128)S(1)}, f32[1,2048]{1,0:T(1,128)S(1)}, u32[]{:S(2)}, u32[]{:S(2)}) collective-permute-start(f32[1,2048]{1,0:T(1,128)S(1)} %constant_dynamic-update-slice_fusion), channel_id=1, source_target_pairs={{0,4},{4,0},{8,12},{12,8},{1,5},{5,1},{9,13},{13,9},{2,6},{6,2},{1... | collective-permute-start | bytes 24584 | tf_op jit(solution)/shard_map/ppermute | solution.py:517
  122.7 0.7 collective-permute-start.14
  123.4 7.6 %collective-permute-start.21 = (f32[1,2048]{1,0:T(1,128)S(1)}, f32[1,2048]{1,0:T(1,128)S(1)}, u32[]{:S(2)}, u32[]{:S(2)}) collective-permute-start(f32[1,2048]{1,0:T(1,128)S(1)} %add.30), channel_id=1, source_target_pairs={{0,8},{4,12},{8,0},{12,4},{1,9},{5,13},{9,1},{13,5},{2,10},{6,14},... | collective-permute-start | bytes 24584 | tf_op jit(solution)/shard_map/ppermute | solution.py:517
  131.0 5.8 %collective-permute-start.15 = (f32[32,64]{1,0:T(8,128)S(1)}, f32[32,64]{1,0:T(8,128)S(1)}, u32[]{:S(2)}, u32[]{:S(2)}) collective-permute-start(f32[32,64]{1,0:T(8,128)S(1)} %add.27), channel_id=1, source_target_pairs={{4,0},{8,12},{5,1},{9,13},{6,2},{10,14},{7,3},{11,15},{20,16},{24,... | collective-permute-start | bytes 24584 | tf_op jit(solution)/shard_map/ppermute | solution.py:517
  133.9 13.3 %collective-permute-start.17 = (f32[64,1024]{1,0:T(8,128)S(1)}, f32[64,1024]{1,0:T(8,128)S(1)}, u32[]{:S(2)}, u32[]{:S(2)}) collective-permute-start(f32[64,1024]{1,0:T(8,128)S(1)} %add.28), channel_id=1, source_target_pairs={{4,0},{8,12},{5,1},{9,13},{6,2},{10,14},{7,3},{11,15},{20,16},{24,... | collective-permute-start | bytes 786440 | tf_op jit(solution)/shard_map/ppermute | solution.py:517
  137.4 1.0 copy-start.10
  138.5 1.0 copy-start.12
  (4 other events, 2.9 us)

commit v2 on v0

--- a/solution.py
+++ b/solution.py
@@ -1,12 +1,18 @@
+import functools
 import math
 
 import jax
 import jax.numpy as jnp
+import numpy as np
 from jax import lax
+from jax.experimental import pallas as pl
+from jax.experimental.pallas import tpu as pltpu
 from jax.sharding import PartitionSpec as P
 
 band_steps = (1763, 1201, 811, 547, 367, 251, 167, 113, 79, 53, 37, 23, 17, 11, 7, 3)
 highest = lax.Precision.HIGHEST
+f32 = jnp.float32
+bf16 = jnp.bfloat16
 
 
 def features(positions):
@@ -45,7 +51,9 @@
     )
 
 
-def body(x_one, x_two, values, grad_out, first_weight, second_weight, skip_bias, decay_rate):
+def many_shards_body(
+    x_one, x_two, values, grad_out, first_weight, second_weight, skip_bias, decay_rate
+):
     row_count, chan_count = x_one.shape
     shards = lax.axis_size("ctx")
     rank = lax.axis_index("ctx")
@@ -162,6 +170,525 @@
     return (grad_one, grad_two, grad_value, grad_first, grad_second, grad_bias)
 
 
+STEP = 16
+SIDE = 256
+
+
+def halves(array):
+    array = np.asarray(array, np.float32)
+    high = array.astype(bf16)
+    low = (array - high.astype(np.float32)).astype(bf16)
+    return high, low
+
+
+def block_tables(rows):
+    freq = np.concatenate([np.arange(0, rows, 2), np.arange(1, rows, 2)])
+    phase = (2 * freq + 1)[:, None] * np.arange(rows)[None, :] % (4 * rows)
+    angle = phase * (2.0 * np.pi / (4 * rows))
+    forward = np.concatenate([np.cos(angle), -np.sin(angle)], axis=0)
+    front = np.ascontiguousarray(np.concatenate(halves(forward), axis=1))
+    back = np.ascontiguousarray(np.concatenate(halves(forward.T / rows), axis=0))
+    return front, back
+
+
+def feature_table(seq_len):
+    phase = np.arange(seq_len)[:, None] * np.array(band_steps)[None, :] % 4096
+    angle = phase * (2.0 * np.pi / 4096.0)
+    return np.concatenate([np.cos(angle), np.sin(angle)], axis=1).astype(np.float32)
+
+
+def split(array):
+    high = array.astype(bf16)
+    return high, (array - high.astype(f32)).astype(bf16)
+
+
+def dot(left, right):
+    return jnp.dot(left, right, preferred_element_type=f32)
+
+
+def exact_dot(left, right):
+    return jnp.dot(left, right, precision=highest, preferred_element_type=f32)
+
+
+def dot_across(left, right):
+    return lax.dot_general(left, right, (((1,), (1,)), ((), ())), preferred_element_type=f32)
+
+
+def decay(rate, rows, scale):
+    place = lax.broadcasted_iota(jnp.int32, (rows, rate.shape[1]), 0)
+    return jnp.exp(-place.astype(f32) * rate) * scale
+
+
+def times(a, b):
+    return a[0] * b[0] - a[1] * b[1], a[0] * b[1] + a[1] * b[0]
+
+
+def conj_times(a, b):
+    return a[0] * b[0] + a[1] * b[1], a[0] * b[1] - a[1] * b[0]
+
+
+def plus(a, b):
+    return a[0] + b[0], a[1] + b[1]
+
+
+def scaled(a, factor):
+    return a[0] * factor, a[1] * factor
+
+
+def choose(condition, a, b):
+    return jnp.where(condition, a[0], b[0]), jnp.where(condition, a[1], b[1])
+
+
+def turned(a, sign):
+    return (a[1], -a[0]) if sign > 0 else (-a[1], a[0])
+
+
+def forward(front_ref, block):
+    return dot(front_ref[...], jnp.concatenate([block, block], axis=0))
+
+
+def backward(back_ref, high, low=None):
+    both = dot(back_ref[...], high)
+    rows = both.shape[0] // 2
+    out = both[:rows] + both[rows:]
+    return out if low is None else out + dot(back_ref[:rows], low)
+
+
+def row_groups(rows):
+    for step in range(rows // STEP):
+        sign = 1 if step * STEP < rows // 2 else -1
+        yield slice(step * STEP, (step + 1) * STEP), slice(rows + step * STEP, rows + (step + 1) * STEP), sign
+
+
+def weight_sums(trans, m_high, m_low):
+    both = dot(trans, m_high)
+    count = both.shape[0] // 2
+    return both[:count] + both[count:] + dot(trans[:count], m_low)
+
+
+def hidden_sums(m_high, m_low, w_high, w_low):
+    left = jnp.concatenate([m_high, m_high, m_low], axis=1)
+    right = jnp.concatenate([w_high, w_low, w_high], axis=1)
+    return dot_across(left, right)
+
+
+def add_up(ref, value, block):
+    @pl.when(block == 0)
+    def _():
+        ref[...] = value
+
+    @pl.when(block > 0)
+    def _():
+        ref[...] += value
+
+
+def products_kernel(one_ref, two_ref, val_ref, out_ref, source_ref, cotan_ref, bias_ref):
+    source = one_ref[...].astype(f32) * val_ref[...].astype(f32)
+    cotan = out_ref[...].astype(f32) * two_ref[...].astype(f32)
+    source_ref[...] = source.astype(bf16)
+    cotan_ref[...] = cotan.astype(bf16)
+    bias_ref[...] = jnp.sum(source * cotan, axis=0, keepdims=True)
+
+
+def filters_kernel(
+    rows, shards, feats_ref, featt_ref, first_ref, weight_ref, rate_ref, front_ref, back_ref, source_ref, cotan_ref,
+    bias_ref, spec_ref, sums_ref, trans_ref, slope_ref, hid_ref, acc_ref,
+):
+    block = pl.program_id(0)
+    last = pl.num_programs(0) - 1
+    hid_count, width = weight_ref.shape
+    channels = bias_ref.shape[1]
+    scale = float(rows * shards) ** -0.5
+
+    @pl.when(block == 0)
+    def _():
+        pre_act = exact_dot(feats_ref[...], first_ref[...])
+        hidden = jnp.sin(pre_act)
+        slope = jnp.cos(pre_act)
+        slope_ref[...] = slope
+        high, low = split(hidden)
+        hid_ref[...] = jnp.concatenate([high, high, low], axis=1)
+        turned_over = jnp.concatenate([hidden, slope], axis=1).T[:hid_count]
+        trans_ref[...] = jnp.concatenate(split(turned_over), axis=0)
+
+    w_high, w_low = split(weight_ref[...])
+    stacked = jnp.concatenate([w_high, w_low, w_high], axis=0)
+    rate = rate_ref[...]
+    env = decay(rate, rows, scale)
+    before = None
+    for lag in range(shards):
+        part = dot(hid_ref[lag * rows : (lag + 1) * rows, :], stacked)
+        part = part * (env * jnp.exp(rate * (-float(lag * rows))))
+        f_high, f_low = split(part)
+        now = forward(front_ref, f_high) + dot(front_ref[:, :rows], f_low)
+        for re, im, sign in row_groups(rows):
+            here = (now[re], now[im])
+            if before is not None:
+                here = plus(here, turned((before[re], before[im]), -sign))
+            spec_ref[lag, re, :] = here[0]
+            spec_ref[lag, im, :] = here[1]
+        before = now
+
+    x0 = forward(front_ref, source_ref[...])
+    c0 = forward(front_ref, cotan_ref[...])
+    pair = conj_times((x0[:rows], x0[rows:]), (c0[:rows], c0[rows:]))
+    high, low = split(jnp.concatenate(pair, axis=0))
+    m_high, m_low = split(backward(back_ref, high, low) * env)
+    sums_ref[:, pl.ds(pl.multiple_of(block * width, width), width)] = weight_sums(
+        trans_ref[:, :rows], m_high, m_low
+    )
+    add_up(acc_ref, hidden_sums(m_high, m_low, w_high, w_low), block)
+
+    @pl.when(block == last)
+    def _():
+        bias = bias_ref[...]
+        lanes = channels // 128
+        sums_ref[:, channels:] = jnp.zeros((hid_count, SIDE), f32)
+        sums_ref[:lanes, channels : channels + 128] = jnp.concatenate(
+            [bias[:, i * 128 : (i + 1) * 128] for i in range(lanes)], axis=0
+        )
+        first = exact_dot(featt_ref[:, :rows], acc_ref[...] * slope_ref[:rows, :])
+        sums_ref[hid_count // 2 :, channels : channels + hid_count] = first
+
+
+def near_kernel(
+    rows, shards, rank_ref, x0_ref, c0_ref, x1_ref, c1_ref, spec_ref, weight_ref, rate_ref, front_ref, back_ref,
+    trans_ref, featt_ref, slope_ref, own_ref, conv_ref, corr_ref, ahead_ref, sums_ref, first_ref, fields, fast, high_ref,
+    low_ref, acc_ref,
+):
+    block = pl.program_id(0)
+    last = pl.num_programs(0) - 1
+    rank = rank_ref[0]
+    count = shards - 1
+    lower = rank == 1
+    upper = jnp.where(rank == 2, 1.0, 0.0).astype(f32)
+    below_top = jnp.where(rank == shards - 1, 0.0, 1.0).astype(f32)
+    side = jnp.where(rank == 2, 1.0, -1.0).astype(f32)
+    for index, ref in enumerate((x0_ref, c0_ref, x1_ref, c1_ref)):
+        fields[index] = forward(front_ref, ref[...])
+    for re, im, sign in row_groups(rows):
+        x0, c0, x1, c1 = ((fields[i, re, :], fields[i, im, :]) for i in range(4))
+        w0, w1, w2 = ((spec_ref[i, re, :], spec_ref[i, im, :]) for i in range(3))
+        ahead = times((w2[0], w2[1] * side), choose(lower, c1, x1))
+        for index, value in enumerate(
+            (plus(times(w0, x0), times(w1, x1)), plus(conj_times(w0, c0), conj_times(w1, c1)), ahead)
+        ):
+            fast[index, re, :] = value[0].astype(bf16)
+            fast[index, im, :] = value[1].astype(bf16)
+        one = plus(scaled(conj_times(x1, c0), below_top), scaled(conj_times(x0, c1), upper))
+        two = conj_times(x1, c1)
+        for index, value in enumerate((turned(one, sign), plus(one, turned(two, sign)), two)):
+            for part, where in zip(value, (re, im)):
+                high_ref[index, where, :], low_ref[index, where, :] = split(part)
+    conv_ref[...] = backward(back_ref, fast[0])
+    corr_ref[...] = backward(back_ref, fast[1])
+    ahead_ref[...] = backward(back_ref, fast[2])
+    rate = rate_ref[...]
+    env = decay(rate, rows, float(rows * shards) ** -0.5)
+    parts = []
+    for lag in range(count):
+        grad = backward(back_ref, high_ref[lag], low_ref[lag])
+        parts.append(split(grad * (env * jnp.exp(rate * (-float(lag * rows))))))
+    m_high = jnp.concatenate([p[0] for p in parts], axis=0)
+    m_low = jnp.concatenate([p[1] for p in parts], axis=0)
+    sums_ref[...] = own_ref[...] + weight_sums(trans_ref[:, : count * rows], m_high, m_low)
+    w_high, w_low = split(weight_ref[...])
+    add_up(acc_ref, hidden_sums(m_high, m_low, w_high, w_low), block)
+
+    @pl.when(block == last)
+    def _():
+        first_ref[...] = exact_dot(
+            featt_ref[:, : count * rows], acc_ref[...] * slope_ref[: count * rows, :]
+        )
+
+
+def far_kernel(rows, rank_ref, x2_ref, c2_ref, spec_ref, front_ref, back_ref, ahead_ref, part_ref, late_ref):
+    side = jnp.where(rank_ref[0] == 2, 1.0, -1.0).astype(f32)
+    far = forward(front_ref, x2_ref[...] + c2_ref[...])
+    far = (far[:rows], far[rows:])
+    w2, w3 = ((spec_ref[i, :rows, :], spec_ref[i, rows:, :] * side) for i in range(2))
+    ahead = jnp.concatenate(times(w3, far), axis=0).astype(bf16)
+    part_ref[...] = (ahead_ref[...] + backward(back_ref, ahead)).astype(bf16)
+    late = jnp.concatenate(times(w2, far), axis=0).astype(bf16)
+    late_ref[...] = backward(back_ref, late)
+
+
+def last_kernel(
+    rows, shards, channels, rank_ref, x1_ref, c1_ref, x2_ref, c2_ref, weight_ref, rate_ref, front_ref, back_ref,
+    trans_ref, featt_ref, slope_ref, sums_ref, first_ref, own_ref, in_ref, after_ref, pay_ref, total_ref, acc_ref,
+):
+    del after_ref
+    block = pl.program_id(0)
+    blocks = pl.num_programs(0)
+    hid_count, width = weight_ref.shape
+    rank = rank_ref[0]
+    lower = rank == 1
+    start = pl.multiple_of(block * width, width)
+    here = sums_ref[...] + in_ref[:, pl.ds(start, width)]
+    mine = (block < blocks // 2) == lower
+
+    @pl.when(block == 0)
+    def _():
+        acc_ref[...] = jnp.zeros_like(acc_ref)
+
+    @pl.when(mine)
+    def _():
+        sign = jnp.where(lower, 1.0, -1.0).astype(f32)
+        near = forward(front_ref, jnp.where(lower, x1_ref[...], c1_ref[...]))
+        far = forward(front_ref, x2_ref[...] + c2_ref[...])
+        three = conj_times((near[:rows], near[rows:]), (far[:rows], far[rows:]))
+        three = (three[0], three[1] * sign)
+        half = rows // 2
+        two = jnp.concatenate([three[1][:half], -three[1][half:], -three[0][:half], three[0][half:]], axis=0)
+        rate = rate_ref[...]
+        env = decay(rate, rows, float(rows * shards) ** -0.5)
+        parts = []
+        for lag, value in ((shards - 2, two), (shards - 1, jnp.concatenate(three, axis=0))):
+            grad = backward(back_ref, *split(value))
+            parts.append(split(grad * (env * jnp.exp(rate * (-float(lag * rows))))))
+        m_high = jnp.concatenate([p[0] for p in parts], axis=0)
+        m_low = jnp.concatenate([p[1] for p in parts], axis=0)
+        trans = trans_ref[:, (shards - 2) * rows :]
+        pay_ref[:, pl.ds(start, width)] = (here + weight_sums(trans, m_high, m_low)).astype(bf16)
+        w_high, w_low = split(weight_ref[...])
+        acc_ref[...] += hidden_sums(m_high, m_low, w_high, w_low)
+
+    @pl.when(jnp.logical_not(mine))
+    def _():
+        pay_ref[:, pl.ds(start, width)] = here.astype(bf16)
+
+    @pl.when(block == blocks - 1)
+    def _():
+        lanes = channels // 128
+        half = hid_count // 2
+        pay_ref[:, channels:] = jnp.zeros((hid_count, SIDE), bf16)
+        bias = own_ref[:half, :128] + in_ref[:half, channels : channels + 128]
+        high, low = split(bias)
+        pay_ref[:half, channels : channels + 128] = high
+        pay_ref[:half, channels + 128 : channels + SIDE] = low
+        first = exact_dot(
+            featt_ref[:, (shards - 2) * rows :], acc_ref[...] * slope_ref[(shards - 2) * rows :, :]
+        )
+        total_ref[...] = (
+            first
+            + first_ref[...]
+            + own_ref[half:, :hid_count]
+            + in_ref[half:, channels : channels + hid_count]
+        )
+
+
+def total_kernel(channels, own_ref, come_ref, first_ref, far_first_ref, pay_ref):
+    half = own_ref.shape[0] // 2
+    hid_count = first_ref.shape[1]
+    pay_ref[:, :channels] = (own_ref[:, :channels].astype(f32) + come_ref[:, :channels].astype(f32)).astype(bf16)
+    high = own_ref[:half, channels : channels + 128].astype(f32) + come_ref[:half, channels : channels + 128].astype(f32)
+    low = own_ref[:half, channels + 128 :].astype(f32) + come_ref[:half, channels + 128 :].astype(f32)
+    pay_ref[:, channels:] = jnp.zeros((2 * half, SIDE), bf16)
+    high, low = split(high + low)
+    pay_ref[:half, channels : channels + 128] = high
+    pay_ref[:half, channels + 128 :] = low
+    high, low = split(first_ref[...] + far_first_ref[...])
+    pay_ref[half:, channels : channels + hid_count] = high
+    pay_ref[half:, channels + 128 : channels + 128 + hid_count] = low
+
+
+def gates_kernel(
+    shards, rank_ref, one_ref, two_ref, val_ref, out_ref, skip_ref, conv_ref, corr_ref, late_ref, part_ref,
+    grad_one_ref, grad_two_ref, grad_value_ref,
+):
+    rank = rank_ref[0]
+
+    def mask(wanted):
+        return jnp.where(rank == wanted, 1.0, 0.0).astype(f32)
+
+    part = part_ref[...].astype(f32)
+    late = late_ref[...]
+    one = one_ref[...].astype(f32)
+    val = val_ref[...].astype(f32)
+    out = out_ref[...].astype(f32)
+    skip = skip_ref[...]
+    conv = conv_ref[...] + late * mask(2) + part * mask(shards - 1)
+    corr = corr_ref[...] + late * mask(1) + part * mask(0)
+    grad_two_ref[...] = (out * (conv + skip * (one * val))).astype(bf16)
+    mid = corr + skip * (out * two_ref[...].astype(f32))
+    grad_one_ref[...] = (mid * val).astype(bf16)
+    grad_value_ref[...] = (mid * one).astype(bf16)
+
+
+def finish_kernel(channels, shards, rank_ref, own_ref, come_ref, second_ref, first_ref, bias_ref):
+    rank = rank_ref[0]
+    inner = jnp.logical_and(rank > 0, rank < shards - 1)
+    hid_count = second_ref.shape[0]
+    half = hid_count // 2
+    lanes = channels // 128
+
+    def pick(rows, cols):
+        return jnp.where(inner, own_ref[rows, cols].astype(f32), come_ref[rows, cols].astype(f32))
+
+    second_ref[...] = pick(slice(None), slice(0, channels))
+    top = pick(slice(0, half), slice(channels, channels + SIDE))
+    bias = top[:, :128] + top[:, 128:]
+    for i in range(lanes):
+        bias_ref[:, i * 128 : (i + 1) * 128] = bias[i : i + 1]
+    low = pick(slice(half, hid_count), slice(channels, channels + SIDE))
+    first_ref[...] = (low[:, :128] + low[:, 128:])[:, :hid_count]
+
+
+def few_shards_body(
+    x_one, x_two, values, grad_out, first_weight, second_weight, skip_bias, decay_rate
+):
+    rows, channels = x_one.shape
+    shards = lax.axis_size("ctx")
+    feat_count, hid_count = first_weight.shape
+    seq_len = rows * shards
+    double = 2 * rows
+    width = min(512, channels)
+    blocks = channels // width
+    rank = lax.axis_index("ctx").astype(jnp.int32).reshape(1)
+    front, back = block_tables(rows)
+    feats = feature_table(seq_len)
+    featt = np.ascontiguousarray(feats.T)
+    skip_row = skip_bias.reshape(1, channels)
+    rate_row = decay_rate.reshape(1, channels)
+    smem = pl.BlockSpec(memory_space=pltpu.SMEM)
+
+    def whole(*dims):
+        return pl.BlockSpec(dims, lambda i: (0,) * len(dims))
+
+    def strip(*lead):
+        return pl.BlockSpec(lead + (width,), lambda i: (0,) * len(lead) + (i,))
+
+    def shape(*dims, dtype=f32):
+        return jax.ShapeDtypeStruct(dims, dtype)
+
+    def call(kernel, name, units, size, **how):
+        how.setdefault("grid", (blocks,))
+        return pl.pallas_call(
+            kernel,
+            compiler_params=pltpu.CompilerParams(vmem_limit_bytes=64 * 1024 * 1024),
+            cost_estimate=pl.CostEstimate(
+                flops=2 * units * double * double * channels, bytes_accessed=size * rows * channels, transcendentals=0
+            ),
+            name=name,
+            **how,
+        )
+
+    def move(array, pairs):
+        return lax.ppermute(array, "ctx", pairs)
+
+    up = [(i, i + 1) for i in range(shards - 1)]
+    down = [(i + 1, i) for i in range(shards - 1)]
+    inward = [(0, 1), (shards - 1, shards - 2)]
+    outward = [(1, 0), (shards - 2, shards - 1)]
+    across = [(1, 2), (2, 1)]
+    block_like = strip(rows)
+    pay_shape = (hid_count, channels + SIDE)
+
+    x0, c0, bias = call(
+        products_kernel, "products", 0, 12,
+        in_specs=[block_like] * 4,
+        out_specs=[block_like, block_like, strip(1)],
+        out_shape=[shape(rows, channels, dtype=bf16)] * 2 + [shape(1, channels)],
+    )(x_one, x_two, values, grad_out)
+    x1 = move(x0, up)
+    c1 = move(c0, down)
+
+    spec, own, trans, slope = call(
+        functools.partial(filters_kernel, rows, shards), "filters", 16, 40,
+        in_specs=[
+            whole(seq_len, feat_count), whole(feat_count, seq_len), whole(feat_count, hid_count), strip(hid_count),
+            strip(1), whole(double, double), whole(double, double), block_like, block_like, whole(1, channels),
+        ],
+        out_specs=[
+            strip(shards, double), whole(*pay_shape), whole(2 * hid_count, seq_len), whole(seq_len, hid_count),
+        ],
+        out_shape=[
+            shape(shards, double, channels), shape(*pay_shape), shape(2 * hid_count, seq_len, dtype=bf16),
+            shape(seq_len, hid_count),
+        ],
+        scratch_shapes=[pltpu.VMEM((seq_len, 3 * hid_count), bf16), pltpu.VMEM((rows, hid_count), f32)],
+    )(feats, featt, first_weight, second_weight, rate_row, front, back, x0, c0, bias)
+    come = move(own, inward)
+
+    x2 = move(x1, [(1, 2)])
+    c2 = move(c1, [(2, 1)])
+    conv, corr, ahead, sums, first = call(
+        functools.partial(near_kernel, rows, shards), "near_blocks", 20, 50,
+        in_specs=[smem] + [block_like] * 4 + [
+            strip(shards - 1, double), strip(hid_count), strip(1), whole(double, double), whole(double, double),
+            whole(2 * hid_count, seq_len), whole(feat_count, seq_len), whole(seq_len, hid_count), strip(hid_count),
+        ],
+        out_specs=[block_like] * 3 + [strip(hid_count), whole(feat_count, hid_count)],
+        out_shape=[shape(rows, channels)] * 3 + [shape(hid_count, channels), shape(feat_count, hid_count)],
+        scratch_shapes=[
+            pltpu.VMEM((4, double, width), f32),
+            pltpu.VMEM((3, double, width), bf16),
+            pltpu.VMEM((shards - 1, double, width), bf16),
+            pltpu.VMEM((shards - 1, double, width), bf16),
+            pltpu.VMEM(((shards - 1) * rows, hid_count), f32),
+        ],
+    )(rank, x0, c0, x1, c1, spec, second_weight, rate_row, front, back, trans, featt, slope, own)
+
+    part, late = call(
+        functools.partial(far_kernel, rows), "far_block", 4, 30,
+        in_specs=[smem, block_like, block_like, pl.BlockSpec((2, double, width), lambda i: (1, 0, i)),
+                  whole(double, double), whole(double, double), block_like],
+        out_specs=[block_like] * 2,
+        out_shape=[shape(rows, channels, dtype=bf16), shape(rows, channels)],
+    )(rank, x2, c2, spec, front, back, ahead)
+    part_come = move(part, outward)
+
+    side_block = (channels // SIDE) if channels % SIDE == 0 else 0
+    pay, first = call(
+        functools.partial(last_kernel, rows, shards, channels), "last_pair", 5, 10,
+        in_specs=[smem] + [block_like] * 4 + [
+            strip(hid_count), strip(1), whole(double, double), whole(double, double), whole(2 * hid_count, seq_len),
+            whole(feat_count, seq_len), whole(seq_len, hid_count), strip(hid_count), whole(feat_count, hid_count),
+            pl.BlockSpec((hid_count, SIDE), lambda i: (0, side_block)), whole(*pay_shape),
+            pl.BlockSpec(memory_space=pl.ANY),
+        ],
+        out_specs=[whole(*pay_shape), whole(feat_count, hid_count)],
+        out_shape=[shape(*pay_shape, dtype=bf16), shape(feat_count, hid_count)],
+        scratch_shapes=[pltpu.VMEM((2 * rows, hid_count), f32)],
+    )(
+        rank, x1, c1, x2, c2, second_weight, rate_row, front, back, trans, featt, slope, sums, first, own, come,
+        late,
+    )
+    pay_come = move(pay, across)
+    group = lax.axis_size(("ch", "sub"))
+    bit = 1
+    while bit < group:
+        first = first + lax.ppermute(first, ("ch", "sub"), [(i, i ^ bit) for i in range(group)])
+        bit *= 2
+    first_come = move(first, across)
+
+    vmem = pl.BlockSpec(memory_space=pltpu.VMEM)
+    total = call(
+        functools.partial(total_kernel, channels), "total", 0, 4,
+        grid=(),
+        in_specs=[vmem] * 4,
+        out_specs=vmem,
+        out_shape=shape(*pay_shape, dtype=bf16),
+    )(pay, pay_come, first, first_come)
+    total_come = move(total, outward)
+
+    grad_one, grad_two, grad_value = call(
+        functools.partial(gates_kernel, shards), "gates", 0, 30,
+        in_specs=[smem] + [block_like] * 4 + [strip(1)] + [block_like] * 4,
+        out_specs=[block_like] * 3,
+        out_shape=[shape(rows, channels, dtype=bf16)] * 3,
+    )(rank, x_one, x_two, values, grad_out, skip_row, conv, corr, late, part_come)
+
+    grad_second, grad_first, grad_bias = call(
+        functools.partial(finish_kernel, channels, shards), "finish", 0, 4,
+        grid=(),
+        in_specs=[smem, vmem, vmem],
+        out_specs=[vmem] * 3,
+        out_shape=[shape(hid_count, channels), shape(feat_count, hid_count), shape(1, channels)],
+    )(rank, total, total_come)
+    return (grad_one, grad_two, grad_value, grad_first, grad_second, grad_bias.reshape(channels))
+
+
 def solution(mesh):
     in_specs = (
         P(("parts", "ctx"), ("ch", "sub")),
@@ -181,4 +708,5 @@
         P("parts", ("ch", "sub")),
         P(("parts", "ch", "sub")),
     )
+    body = few_shards_body if mesh.shape["ctx"] == 4 else many_shards_body
     return jax.shard_map(body, mesh=mesh, in_specs=in_specs, out_specs=out_specs, check_vma=False)

time: 312 us -> 100 us (0.32); the launches traced: 307 us -> 99.7 us
  matrix products: 119 us -> 0 us
  blocking collectives: 91.8 us -> 0 us
  Pallas kernels: 0 us -> 49.4 us
  local copies, waits for them, and re-layouts: 31.6 us -> 1.2 us
  other arithmetic: 16.5 us -> 0.73 us
  starting transfers between devices: 10.7 us -> 20.5 us
  waiting for transfers between devices: 35.9 us -> 27.1 us
    dot_general x21 -> x0, matrix products: 119 us -> none  [the longest x8 82.7 us: contract(): jnp.einsum('lj,mckj->mckl', kernel, array, precision=highest, preferred_e...]
    psum x2 -> x0, blocking collectives: 66.9 us -> none  [the longest x1 57.8 us: body(): grad_first = lax.psum(first_part, ('ctx', 'ch', 'sub'))]
    pallas_call x0 -> x8, Pallas kernels: none -> 49.4 us  [the longest x1 13 us: few_shards_body(): call(functools.partial(filters_kernel, rows, shards), 'filters', 16, 40,...]
    all_to_all x2 -> x0, waiting for transfers between devices: 35.9 us -> none  [the longest x1 35.9 us: body(): lax.all_to_all(jnp.stack([source.T, cotan.T])[:, :, None, :], 'ctx', spli...]
    ppermute x0 -> x11, waiting for transfers between devices: none -> 27.1 us  [the longest x9 23.5 us: move(): return lax.ppermute(array, 'ctx', pairs)]
    all_gather x1 -> x0, blocking collectives: 24.9 us -> none  [body(): grad_second = lax.all_gather(weight_part, 'ctx', axis=1, tiled=True)]
    ppermute x0 -> x11, starting transfers between devices: none -> 20.5 us  [the longest x9 19 us: move(): return lax.ppermute(array, 'ctx', pairs)]
    unnamed x42 -> x4, local copies, waits for them, and re-layouts: 15.7 us -> 1.2 us
  transfers between devices with their start and end apart: 2 -> 11, of which waited for: 1 -> 6; matrix products, arithmetic and copies ran while one was open for 8% -> 1% of each run, Pallas kernels for 0% -> 38%
where the time goes in v2:
time: 100 us; the launch traced here: 99.7 us
  Pallas kernels  49.4 us (49%)
  waiting for transfers between devices  27.1 us (27%)
  starting transfers between devices  20.5 us (20%)
  local copies, waits for them, and re-layouts  1.2 us (1%)
    ppermute x9, waiting for transfers between devices, move(): return lax.ppermute(array, 'ctx', pairs)  23.5 us
    ppermute x9, starting transfers between devices, move(): return lax.ppermute(array, 'ctx', pairs)  19 us
    pallas_call x1, Pallas kernels, few_shards_body(): call(functools.partial(filters_kernel, rows, shards), 'filters', 16, 40,...  13 us
    pallas_call x1, Pallas kernels, few_shards_body(): call(functools.partial(near_kernel, rows, shards), 'near_blocks', 20, 50,...  12.2 us
    pallas_call x1, Pallas kernels, few_shards_body(): call(functools.partial(last_kernel, rows, shards, channels), 'last_pair',...  6.29 us
    pallas_call x1, Pallas kernels, few_shards_body(): call(functools.partial(far_kernel, rows), 'far_block', 4, 30, in_specs=[s...  5.8 us
    pallas_call x1, Pallas kernels, few_shards_body(): call(functools.partial(gates_kernel, shards), 'gates', 0, 30, in_specs=[s...  4.64 us
    pallas_call x1, Pallas kernels, few_shards_body(): call(products_kernel, 'products', 0, 12, in_specs=[block_like] * 4, out_s...  3.66 us
  transfers between devices with their start and end apart: 11, of which 6 were waited for; matrix products, arithmetic and copies ran while one was open for 1% of the time, Pallas kernels for 38%

profile of v2, /device:TPU:0, one launch (start us, length us, event | category | flops | bytes accessed | tf_op | source)
XLA Modules:
  0.0 99.7 jit_solution(14873708051432739731)
XLA Ops:
  0.6 3.7 %products.1 = (bf16[128,2048]{1,0:T(8,128)(2,1)}, bf16[128,2048]{1,0:T(8,128)(2,1)}, f32[1,2048]{1,0:T(1,128)}) custom-call(bf16[128,2048]{1,0:T(8,128)(2,1)} %one_ref.3, bf16[128,2048]{1,0:T(8,128)(2,1)} %two_ref.3, bf16[128,2048]{1,0:T(8,128)(2,1)} %val_ref.3, bf16[128,2048]{1,0:T(8,128)(2,1)} %out_ref.3), custom_call_target="tpu_custom_call" | custom-call | bytes 3145728 | tf_op jit(solution)/shard_map/products/pallas_call | solution.py:587
  4.3 5.7 %collective-permute-start = (bf16[128,2048]{1,0:T(8,128)(2,1)}, bf16[128,2048]{1,0:T(8,128)(2,1)}, u32[]{:S(2)}, u32[]{:S(2)}) collective-permute-start(bf16[128,2048]{1,0:T(8,128)(2,1)} %get-tuple-element.28.source_ref.x0_ref), channel_id=1, source_target_pairs={{0,4},{4,8},{8,12},{1,5},{5,9},{9,13},{2,6},{6,10},{10,14},{3,7},{... | collective-permute-start | bytes 1572872 | tf_op jit(solution)/shard_map/ppermute | solution.py:577
  10.0 1.3 %collective-permute-start.1 = (bf16[128,2048]{1,0:T(8,128)(2,1)}, bf16[128,2048]{1,0:T(8,128)(2,1)}, u32[]{:S(2)}, u32[]{:S(2)}) collective-permute-start(bf16[128,2048]{1,0:T(8,128)(2,1)} %get-tuple-element.29.cotan_ref.c0_ref), channel_id=1, source_target_pairs={{4,0},{8,4},{12,8},{5,1},{9,5},{13,9},{6,2},{10,6},{14,10},{7,3},{... | collective-permute-start | bytes 1572872 | tf_op jit(solution)/shard_map/ppermute | solution.py:577
  11.3 9.4 %collective-permute-done.x1_ref = bf16[128,2048]{1,0:T(8,128)(2,1)} collective-permute-done((bf16[128,2048]{1,0:T(8,128)(2,1)}, bf16[128,2048]{1,0:T(8,128)(2,1)}, u32[]{:S(2)}, u32[]{:S(2)}) %collective-permute-start) | collective-permute-done | bytes 524320 | tf_op jit(solution)/shard_map/ppermute | solution.py:577
  20.7 1.5 %collective-permute-start.2 = (bf16[128,2048]{1,0:T(8,128)(2,1)}, bf16[128,2048]{1,0:T(8,128)(2,1)}, u32[]{:S(2)}, u32[]{:S(2)}) collective-permute-start(bf16[128,2048]{1,0:T(8,128)(2,1)} %collective-permute-done.x1_ref), channel_id=1, source_target_pairs={{4,8},{5,9},{6,10},{7,11},{20,24},{21,25},{22,26},{23,27}} | collective-permute-start | bytes 1572872 | tf_op jit(solution)/shard_map/ppermute | solution.py:577
  22.1 3.5 %collective-permute-done.1.c1_ref = bf16[128,2048]{1,0:T(8,128)(2,1)} collective-permute-done((bf16[128,2048]{1,0:T(8,128)(2,1)}, bf16[128,2048]{1,0:T(8,128)(2,1)}, u32[]{:S(2)}, u32[]{:S(2)}) %collective-permute-start.1) | collective-permute-done | bytes 524320 | tf_op jit(solution)/shard_map/ppermute | solution.py:577
  25.6 1.5 %collective-permute-start.3 = (bf16[128,2048]{1,0:T(8,128)(2,1)}, bf16[128,2048]{1,0:T(8,128)(2,1)}, u32[]{:S(2)}, u32[]{:S(2)}) collective-permute-start(bf16[128,2048]{1,0:T(8,128)(2,1)} %collective-permute-done.1.c1_ref), channel_id=1, source_target_pairs={{8,4},{9,5},{10,6},{11,7},{24,20},{25,21},{26,22},{27,23}} | collective-permute-start | bytes 1572872 | tf_op jit(solution)/shard_map/ppermute | solution.py:577
  27.1 13.0 %filters.1 = (f32[4,256,2048]{2,1,0:T(8,128)}, f32[64,2304]{1,0:T(8,128)}, bf16[128,512]{1,0:T(8,128)(2,1)}, f32[512,64]{1,0:T(8,128)}) custom-call(f32[512,32]{1,0:T(8,128)} %constant.13.clone.feats_ref, f32[32,512]{1,0:T(8,128)} %constant.14.clone.featt_ref, f32[32,64]{1,0:T(8,128)} %first_ref.1, f32[64,2048]{1,0:T(8,128)} %weight_ref.5, ...), custom_call_target="tpu_custom_call" | custom-call | flops 4294967296 | bytes 10485760 | tf_op jit(solution)/shard_map/filters/pallas_call | solution.py:596
  40.1 4.5 %collective-permute-start.5 = (f32[64,2304]{1,0:T(8,128)}, f32[64,2304]{1,0:T(8,128)}, u32[]{:S(2)}, u32[]{:S(2)}) collective-permute-start(f32[64,2304]{1,0:T(8,128)} %get-tuple-element.34.own_ref), channel_id=1, source_target_pairs={{0,4},{12,8},{1,5},{13,9},{2,6},{14,10},{3,7},{15,11},{16,20},{28,... | collective-permute-start | bytes 1769480 | tf_op jit(solution)/shard_map/ppermute | solution.py:577
  44.6 12.2 %near_blocks.1 = (f32[128,2048]{1,0:T(8,128)}, f32[128,2048]{1,0:T(8,128)}, f32[128,2048]{1,0:T(8,128)}, f32[64,2048]{1,0:T(8,128)}, f32[32,64]{1,0:T(8,128)}) custom-call(s32[1]{0:T(128)} %bitcast.rank_ref, bf16[128,2048]{1,0:T(8,128)(2,1)} %get-tuple-element.28.source_ref.x0_ref, bf16[128,2048]{1,0:T(8,128)(2,1)} %get-tuple-element.29.cotan_ref.c0_ref, ...), custom_call_target="tpu_custom_call" | custom-call | flops 5368709120 | bytes 13107200 | tf_op jit(solution)/shard_map/near_blocks/pallas_call | solution.py:615
  56.7 0.0 collective-permute-done.2.x2_ref
  56.8 0.0 collective-permute-done.3.c2_ref
  56.8 5.8 %far_block.1 = (bf16[128,2048]{1,0:T(8,128)(2,1)}, f32[128,2048]{1,0:T(8,128)}) custom-call(s32[1]{0:T(128)} %bitcast.rank_ref, bf16[128,2048]{1,0:T(8,128)(2,1)} %collective-permute-done.2.x2_ref, bf16[128,2048]{1,0:T(8,128)(2,1)} %collective-permute-done.3.c2_ref, f32[4,256,2048]{2,1,0:T(8,128)} %get-tuple-element.31.spec_ref, ...), custom_call_target="tpu_custom_call" | custom-call | flops 1073741824 | bytes 7864320 | tf_op jit(solution)/shard_map/far_block/pallas_call | solution.py:632
  62.6 0.0 collective-permute-done.5.in_ref
  62.6 6.3 %last_pair.1 = (bf16[64,2304]{1,0:T(8,128)(2,1)}, f32[32,64]{1,0:T(8,128)}) custom-call(s32[1]{0:T(128)} %bitcast.rank_ref, bf16[128,2048]{1,0:T(8,128)(2,1)} %collective-permute-done.x1_ref, bf16[128,2048]{1,0:T(8,128)(2,1)} %collective-permute-done.1.c1_ref, bf16[128,2048]{1,0:T(8,128)(2,1)} %collective-permute-done.2.x2_ref, ...), custom_call_target="tpu_custom_call" | custom-call | flops 1342177280 | bytes 2621440 | tf_op jit(solution)/shard_map/last_pair/pallas_call | solution.py:642
  68.9 1.4 %collective-permute-start.6 = (bf16[64,2304]{1,0:T(8,128)(2,1)}, bf16[64,2304]{1,0:T(8,128)(2,1)}, u32[]{:S(2)}, u32[]{:S(2)}) collective-permute-start(bf16[64,2304]{1,0:T(8,128)(2,1)} %get-tuple-element.45.own_ref), channel_id=1, source_target_pairs={{4,8},{8,4},{5,9},{9,5},{6,10},{10,6},{7,11},{11,7},{20,24},{24,20... | collective-permute-start | bytes 884744 | tf_op jit(solution)/shard_map/ppermute | solution.py:577
  70.2 1.3 %collective-permute-start.4 = (bf16[128,2048]{1,0:T(8,128)(2,1)}, bf16[128,2048]{1,0:T(8,128)(2,1)}, u32[]{:S(2)}, u32[]{:S(2)}) collective-permute-start(bf16[128,2048]{1,0:T(8,128)(2,1)} %get-tuple-element.39), channel_id=1, source_target_pairs={{4,0},{8,12},{5,1},{9,13},{6,2},{10,14},{7,3},{11,15},{20,16},{24,... | collective-permute-start | bytes 1572872 | tf_op jit(solution)/shard_map/ppermute | solution.py:577
  71.5 0.1 collective-permute-start.7
  71.6 1.4 %collective-permute-done.7 = f32[32,64]{1,0:T(8,128)S(1)} collective-permute-done((f32[32,64]{1,0:T(8,128)}, f32[32,64]{1,0:T(8,128)S(1)}, u32[]{:S(2)}, u32[]{:S(2)}) %collective-permute-start.7) | collective-permute-done | bytes 8224 | tf_op jit(solution)/shard_map/ppermute | solution.py:661
  73.0 0.7 add.6
  73.7 1.5 %collective-permute-start.8 = (f32[32,64]{1,0:T(8,128)S(1)}, f32[32,64]{1,0:T(8,128)S(1)}, u32[]{:S(2)}, u32[]{:S(2)}) collective-permute-start(f32[32,64]{1,0:T(8,128)S(1)} %add.6), channel_id=1, source_target_pairs={{0,2},{1,3},{2,0},{3,1},{4,6},{5,7},{6,4},{7,5},{8,10},{9,11},{10,... | collective-permute-start | bytes 24584 | tf_op jit(solution)/shard_map/ppermute | solution.py:661
  75.2 2.2 %collective-permute-done.8 = f32[32,64]{1,0:T(8,128)S(1)} collective-permute-done((f32[32,64]{1,0:T(8,128)S(1)}, f32[32,64]{1,0:T(8,128)S(1)}, u32[]{:S(2)}, u32[]{:S(2)}) %collective-permute-start.8) | collective-permute-done | bytes 8224 | tf_op jit(solution)/shard_map/ppermute | solution.py:661
  77.5 0.0 copy-start
  77.5 0.6 copy-done
  78.1 0.7 collective-permute-start.9
  78.7 0.0 collective-permute-done.9.far_first_ref
  78.7 0.0 copy-start.1
  78.8 0.6 copy-done.1
  79.3 0.0 collective-permute-done.6.come_ref
  79.3 1.8 %total.1.own_ref = bf16[64,2304]{1,0:T(8,128)(2,1)} custom-call(bf16[64,2304]{1,0:T(8,128)(2,1)} %get-tuple-element.45.own_ref, bf16[64,2304]{1,0:T(8,128)(2,1)} %collective-permute-done.6.come_ref, f32[32,64]{1,0:T(8,128)} %copy-done, f32[32,64]{1,0:T(8,128)} %copy-done.1), custom_call_target="tpu_custom_call" | custom-call | bytes 1048576 | tf_op jit(solution)/shard_map/total/pallas_call | solution.py:666
  81.2 1.3 %collective-permute-start.10 = (bf16[64,2304]{1,0:T(8,128)(2,1)}, bf16[64,2304]{1,0:T(8,128)(2,1)}, u32[]{:S(2)}, u32[]{:S(2)}) collective-permute-start(bf16[64,2304]{1,0:T(8,128)(2,1)} %total.1.own_ref), channel_id=1, source_target_pairs={{4,0},{8,12},{5,1},{9,13},{6,2},{10,14},{7,3},{11,15},{20,16},{24,... | collective-permute-start | bytes 884744 | tf_op jit(solution)/shard_map/ppermute | solution.py:577
  82.5 2.2 %collective-permute-done.4.part_ref = bf16[128,2048]{1,0:T(8,128)(2,1)} collective-permute-done((bf16[128,2048]{1,0:T(8,128)(2,1)}, bf16[128,2048]{1,0:T(8,128)(2,1)}, u32[]{:S(2)}, u32[]{:S(2)}) %collective-permute-start.4) | collective-permute-done | bytes 524320 | tf_op jit(solution)/shard_map/ppermute | solution.py:577
  84.7 4.6 %gates.1 = (bf16[128,2048]{1,0:T(8,128)(2,1)}, bf16[128,2048]{1,0:T(8,128)(2,1)}, bf16[128,2048]{1,0:T(8,128)(2,1)}) custom-call(s32[1]{0:T(128)} %bitcast.rank_ref, bf16[128,2048]{1,0:T(8,128)(2,1)} %one_ref.3, bf16[128,2048]{1,0:T(8,128)(2,1)} %two_ref.3, bf16[128,2048]{1,0:T(8,128)(2,1)} %val_ref.3, bf16[128,2048]{1,0:T(8,128)(2,1)} %out_ref.3, ...), custom_call_target="tpu_custom_call" | custom-call | bytes 7864320 | tf_op jit(solution)/shard_map/gates/pallas_call | solution.py:675
  89.4 8.4 %collective-permute-done.10.come_ref = bf16[64,2304]{1,0:T(8,128)(2,1)} collective-permute-done((bf16[64,2304]{1,0:T(8,128)(2,1)}, bf16[64,2304]{1,0:T(8,128)(2,1)}, u32[]{:S(2)}, u32[]{:S(2)}) %collective-permute-start.10) | collective-permute-done | bytes 294944 | tf_op jit(solution)/shard_map/ppermute | solution.py:577
  97.8 1.9 %finish.1 = (f32[64,2048]{1,0:T(8,128)}, f32[32,64]{1,0:T(8,128)}, f32[1,2048]{1,0:T(1,128)}) custom-call(s32[1]{0:T(128)} %bitcast.rank_ref, bf16[64,2304]{1,0:T(8,128)(2,1)} %total.1.own_ref, bf16[64,2304]{1,0:T(8,128)(2,1)} %collective-permute-done.10.come_ref), custom_call_target="tpu_custom_call" | custom-call | bytes 1048576 | tf_op jit(solution)/shard_map/finish/pallas_call | solution.py:682
  (1 shorter events, 0.0 us)
Async XLA Ops:
  4.3 16.4 %collective-permute-start = (bf16[128,2048]{1,0:T(8,128)(2,1)}, bf16[128,2048]{1,0:T(8,128)(2,1)}, u32[]{:S(2)}, u32[]{:S(2)}) collective-permute-start(bf16[128,2048]{1,0:T(8,128)(2,1)} %get-tuple-element.28.source_ref.x0_ref), channel_id=1, source_target_pairs={{0,4},{4,8},{8,12},{1,5},{5,9},{9,13},{2,6},{6,10},{10,14},{3,7},{... | collective-permute-start | bytes 1572872 | tf_op jit(solution)/shard_map/ppermute | solution.py:577
  10.0 15.6 %collective-permute-start.1 = (bf16[128,2048]{1,0:T(8,128)(2,1)}, bf16[128,2048]{1,0:T(8,128)(2,1)}, u32[]{:S(2)}, u32[]{:S(2)}) collective-permute-start(bf16[128,2048]{1,0:T(8,128)(2,1)} %get-tuple-element.29.cotan_ref.c0_ref), channel_id=1, source_target_pairs={{4,0},{8,4},{12,8},{5,1},{9,5},{13,9},{6,2},{10,6},{14,10},{7,3},{... | collective-permute-start | bytes 1572872 | tf_op jit(solution)/shard_map/ppermute | solution.py:577
  20.7 36.1 %collective-permute-start.2 = (bf16[128,2048]{1,0:T(8,128)(2,1)}, bf16[128,2048]{1,0:T(8,128)(2,1)}, u32[]{:S(2)}, u32[]{:S(2)}) collective-permute-start(bf16[128,2048]{1,0:T(8,128)(2,1)} %collective-permute-done.x1_ref), channel_id=1, source_target_pairs={{4,8},{5,9},{6,10},{7,11},{20,24},{21,25},{22,26},{23,27}} | collective-permute-start | bytes 1572872 | tf_op jit(solution)/shard_map/ppermute | solution.py:577
  25.6 31.2 %collective-permute-start.3 = (bf16[128,2048]{1,0:T(8,128)(2,1)}, bf16[128,2048]{1,0:T(8,128)(2,1)}, u32[]{:S(2)}, u32[]{:S(2)}) collective-permute-start(bf16[128,2048]{1,0:T(8,128)(2,1)} %collective-permute-done.1.c1_ref), channel_id=1, source_target_pairs={{8,4},{9,5},{10,6},{11,7},{24,20},{25,21},{26,22},{27,23}} | collective-permute-start | bytes 1572872 | tf_op jit(solution)/shard_map/ppermute | solution.py:577
  40.1 22.5 %collective-permute-start.5 = (f32[64,2304]{1,0:T(8,128)}, f32[64,2304]{1,0:T(8,128)}, u32[]{:S(2)}, u32[]{:S(2)}) collective-permute-start(f32[64,2304]{1,0:T(8,128)} %get-tuple-element.34.own_ref), channel_id=1, source_target_pairs={{0,4},{12,8},{1,5},{13,9},{2,6},{14,10},{3,7},{15,11},{16,20},{28,... | collective-permute-start | bytes 1769480 | tf_op jit(solution)/shard_map/ppermute | solution.py:577
  68.9 10.5 %collective-permute-start.6 = (bf16[64,2304]{1,0:T(8,128)(2,1)}, bf16[64,2304]{1,0:T(8,128)(2,1)}, u32[]{:S(2)}, u32[]{:S(2)}) collective-permute-start(bf16[64,2304]{1,0:T(8,128)(2,1)} %get-tuple-element.45.own_ref), channel_id=1, source_target_pairs={{4,8},{8,4},{5,9},{9,5},{6,10},{10,6},{7,11},{11,7},{20,24},{24,20... | collective-permute-start | bytes 884744 | tf_op jit(solution)/shard_map/ppermute | solution.py:577
  70.2 14.5 %collective-permute-start.4 = (bf16[128,2048]{1,0:T(8,128)(2,1)}, bf16[128,2048]{1,0:T(8,128)(2,1)}, u32[]{:S(2)}, u32[]{:S(2)}) collective-permute-start(bf16[128,2048]{1,0:T(8,128)(2,1)} %get-tuple-element.39), channel_id=1, source_target_pairs={{4,0},{8,12},{5,1},{9,13},{6,2},{10,14},{7,3},{11,15},{20,16},{24,... | collective-permute-start | bytes 1572872 | tf_op jit(solution)/shard_map/ppermute | solution.py:577
  71.5 1.5 %collective-permute-start.7 = (f32[32,64]{1,0:T(8,128)}, f32[32,64]{1,0:T(8,128)S(1)}, u32[]{:S(2)}, u32[]{:S(2)}) collective-permute-start(f32[32,64]{1,0:T(8,128)} %get-tuple-element.46), channel_id=1, source_target_pairs={{0,1},{1,0},{2,3},{3,2},{4,5},{5,4},{6,7},{7,6},{8,9},{9,8},{10,11... | collective-permute-start | bytes 24584 | tf_op jit(solution)/shard_map/ppermute | solution.py:661
  73.7 3.7 %collective-permute-start.8 = (f32[32,64]{1,0:T(8,128)S(1)}, f32[32,64]{1,0:T(8,128)S(1)}, u32[]{:S(2)}, u32[]{:S(2)}) collective-permute-start(f32[32,64]{1,0:T(8,128)S(1)} %add.6), channel_id=1, source_target_pairs={{0,2},{1,3},{2,0},{3,1},{4,6},{5,7},{6,4},{7,5},{8,10},{9,11},{10,... | collective-permute-start | bytes 24584 | tf_op jit(solution)/shard_map/ppermute | solution.py:661
  77.5 0.6 copy-start
  78.1 0.7 collective-permute-start.9
  78.7 0.6 copy-start.1
  81.2 16.6 %collective-permute-start.10 = (bf16[64,2304]{1,0:T(8,128)(2,1)}, bf16[64,2304]{1,0:T(8,128)(2,1)}, u32[]{:S(2)}, u32[]{:S(2)}) collective-permute-start(bf16[64,2304]{1,0:T(8,128)(2,1)} %total.1.own_ref), channel_id=1, source_target_pairs={{4,0},{8,12},{5,1},{9,13},{6,2},{10,14},{7,3},{11,15},{20,16},{24,... | collective-permute-start | bytes 884744 | tf_op jit(solution)/shard_map/ppermute | solution.py:577

commit v3 on v2

--- a/solution.py
+++ b/solution.py
@@ -282,17 +282,35 @@
         ref[...] += value
 
 
-def products_kernel(one_ref, two_ref, val_ref, out_ref, source_ref, cotan_ref, bias_ref):
+def products_kernel(rank_ref, one_ref, two_ref, val_ref, out_ref, source_ref, cotan_ref, far_ref, bias_ref):
     source = one_ref[...].astype(f32) * val_ref[...].astype(f32)
     cotan = out_ref[...].astype(f32) * two_ref[...].astype(f32)
     source_ref[...] = source.astype(bf16)
     cotan_ref[...] = cotan.astype(bf16)
-    bias_ref[...] = jnp.sum(source * cotan, axis=0, keepdims=True)
+    far_ref[...] = jnp.where(rank_ref[0] == 0, source, cotan).astype(bf16)
+    add_up(bias_ref, jnp.sum(source * cotan, axis=0, keepdims=True), pl.program_id(0))
+
+
+def sin_cos(angle):
+    turns = jnp.floor(angle * (2.0 / math.pi) + 0.5)
+    rest = ((angle - turns * 1.5703125) - turns * 4.837512969970703e-4) - turns * 7.54978995489188e-8
+    square = rest * rest
+    sine = rest + rest * square * (
+        -1.6666654611e-1 + square * (8.3321608736e-3 + square * -1.9515295891e-4)
+    )
+    cosine = 1.0 - 0.5 * square + square * square * (
+        4.166664568298827e-2 + square * (-1.388731625493765e-3 + square * 2.443315711809948e-5)
+    )
+    quarter = turns.astype(jnp.int32)
+    odd = (quarter & 1) == 1
+    sin_sign = jnp.where((quarter & 2) == 2, -1.0, 1.0).astype(f32)
+    cos_sign = jnp.where(((quarter + 1) & 2) == 2, -1.0, 1.0).astype(f32)
+    return jnp.where(odd, cosine, sine) * sin_sign, jnp.where(odd, sine, cosine) * cos_sign
 
 
 def filters_kernel(
     rows, shards, feats_ref, featt_ref, first_ref, weight_ref, rate_ref, front_ref, back_ref, source_ref, cotan_ref,
-    bias_ref, spec_ref, sums_ref, trans_ref, slope_ref, hid_ref, acc_ref,
+    bias_ref, spec_ref, sums_ref, send_ref, trans_ref, slope_ref, hid_ref, acc_ref,
 ):
     block = pl.program_id(0)
     last = pl.num_programs(0) - 1
@@ -303,8 +321,7 @@
     @pl.when(block == 0)
     def _():
         pre_act = exact_dot(feats_ref[...], first_ref[...])
-        hidden = jnp.sin(pre_act)
-        slope = jnp.cos(pre_act)
+        hidden, slope = sin_cos(pre_act)
         slope_ref[...] = slope
         high, low = split(hidden)
         hid_ref[...] = jnp.concatenate([high, high, low], axis=1)
@@ -325,8 +342,8 @@
             here = (now[re], now[im])
             if before is not None:
                 here = plus(here, turned((before[re], before[im]), -sign))
-            spec_ref[lag, re, :] = here[0]
-            spec_ref[lag, im, :] = here[1]
+            spec_ref[lag, re, :] = here[0].astype(bf16)
+            spec_ref[lag, im, :] = here[1].astype(bf16)
         before = now
 
     x0 = forward(front_ref, source_ref[...])
@@ -334,21 +351,34 @@
     pair = conj_times((x0[:rows], x0[rows:]), (c0[:rows], c0[rows:]))
     high, low = split(jnp.concatenate(pair, axis=0))
     m_high, m_low = split(backward(back_ref, high, low) * env)
-    sums_ref[:, pl.ds(pl.multiple_of(block * width, width), width)] = weight_sums(
-        trans_ref[:, :rows], m_high, m_low
-    )
+    sums = weight_sums(trans_ref[:, :rows], m_high, m_low)
+    sums_ref[...] = sums
+    send_ref[:, pl.ds(pl.multiple_of(block * width, width), width)] = sums.astype(bf16)
     add_up(acc_ref, hidden_sums(m_high, m_low, w_high, w_low), block)
 
     @pl.when(block == last)
     def _():
-        bias = bias_ref[...]
-        lanes = channels // 128
-        sums_ref[:, channels:] = jnp.zeros((hid_count, SIDE), f32)
-        sums_ref[:lanes, channels : channels + 128] = jnp.concatenate(
-            [bias[:, i * 128 : (i + 1) * 128] for i in range(lanes)], axis=0
-        )
         first = exact_dot(featt_ref[:, :rows], acc_ref[...] * slope_ref[:rows, :])
-        sums_ref[hid_count // 2 :, channels : channels + hid_count] = first
+        put_side(send_ref, channels, fold(bias_ref[...]), first)
+
+
+def fold(bias):
+    return jnp.concatenate([bias[:, i * 128 : (i + 1) * 128] for i in range(bias.shape[1] // 128)], axis=0)
+
+
+def put_side(pay_ref, channels, bias, first):
+    half = pay_ref.shape[0] // 2
+    pay_ref[:, channels:] = jnp.zeros((2 * half, SIDE), bf16)
+    for start, bias_part, first_part in zip((0, 128), split(bias), split(first)):
+        at = channels + start
+        pay_ref[: bias.shape[0], at : at + 128] = bias_part
+        pay_ref[half:, at : at + first.shape[1]] = first_part
+
+
+def get_side(pay, channels, lanes, hid_count):
+    half = pay.shape[0] // 2
+    side = pay[:, channels : channels + 128].astype(f32) + pay[:, channels + 128 :].astype(f32)
+    return side[:lanes], side[half:, :hid_count]
 
 
 def near_kernel(
@@ -368,7 +398,7 @@
         fields[index] = forward(front_ref, ref[...])
     for re, im, sign in row_groups(rows):
         x0, c0, x1, c1 = ((fields[i, re, :], fields[i, im, :]) for i in range(4))
-        w0, w1, w2 = ((spec_ref[i, re, :], spec_ref[i, im, :]) for i in range(3))
+        w0, w1, w2 = ((spec_ref[i, re, :].astype(f32), spec_ref[i, im, :].astype(f32)) for i in range(3))
         ahead = times((w2[0], w2[1] * side), choose(lower, c1, x1))
         for index, value in enumerate(
             (plus(times(w0, x0), times(w1, x1)), plus(conj_times(w0, c0), conj_times(w1, c1)), ahead)
@@ -402,11 +432,11 @@
         )
 
 
-def far_kernel(rows, rank_ref, x2_ref, c2_ref, spec_ref, front_ref, back_ref, ahead_ref, part_ref, late_ref):
+def far_kernel(rows, rank_ref, far_ref, spec_ref, front_ref, back_ref, ahead_ref, part_ref, late_ref):
     side = jnp.where(rank_ref[0] == 2, 1.0, -1.0).astype(f32)
-    far = forward(front_ref, x2_ref[...] + c2_ref[...])
+    far = forward(front_ref, far_ref[...])
     far = (far[:rows], far[rows:])
-    w2, w3 = ((spec_ref[i, :rows, :], spec_ref[i, rows:, :] * side) for i in range(2))
+    w2, w3 = ((spec_ref[i, :rows, :].astype(f32), spec_ref[i, rows:, :].astype(f32) * side) for i in range(2))
     ahead = jnp.concatenate(times(w3, far), axis=0).astype(bf16)
     part_ref[...] = (ahead_ref[...] + backward(back_ref, ahead)).astype(bf16)
     late = jnp.concatenate(times(w2, far), axis=0).astype(bf16)
@@ -414,17 +444,17 @@
 
 
 def last_kernel(
-    rows, shards, channels, rank_ref, x1_ref, c1_ref, x2_ref, c2_ref, weight_ref, rate_ref, front_ref, back_ref,
-    trans_ref, featt_ref, slope_ref, sums_ref, first_ref, own_ref, in_ref, after_ref, pay_ref, total_ref, acc_ref,
+    rows, shards, channels, rank_ref, x1_ref, c1_ref, far_ref, weight_ref, rate_ref, front_ref, back_ref,
+    trans_ref, featt_ref, slope_ref, sums_ref, first_ref, own_ref, bias_ref, in_ref, after_ref, pay_ref, total_ref,
+    acc_ref,
 ):
     del after_ref
     block = pl.program_id(0)
     blocks = pl.num_programs(0)
     hid_count, width = weight_ref.shape
-    rank = rank_ref[0]
-    lower = rank == 1
+    lower = rank_ref[0] == 1
     start = pl.multiple_of(block * width, width)
-    here = sums_ref[...] + in_ref[:, pl.ds(start, width)]
+    here = sums_ref[...] + in_ref[:, pl.ds(start, width)].astype(f32)
     mine = (block < blocks // 2) == lower
 
     @pl.when(block == 0)
@@ -435,7 +465,7 @@
     def _():
         sign = jnp.where(lower, 1.0, -1.0).astype(f32)
         near = forward(front_ref, jnp.where(lower, x1_ref[...], c1_ref[...]))
-        far = forward(front_ref, x2_ref[...] + c2_ref[...])
+        far = forward(front_ref, far_ref[...])
         three = conj_times((near[:rows], near[rows:]), (far[:rows], far[rows:]))
         three = (three[0], three[1] * sign)
         half = rows // 2
@@ -459,37 +489,23 @@
 
     @pl.when(block == blocks - 1)
     def _():
-        lanes = channels // 128
-        half = hid_count // 2
-        pay_ref[:, channels:] = jnp.zeros((hid_count, SIDE), bf16)
-        bias = own_ref[:half, :128] + in_ref[:half, channels : channels + 128]
-        high, low = split(bias)
-        pay_ref[:half, channels : channels + 128] = high
-        pay_ref[:half, channels + 128 : channels + SIDE] = low
         first = exact_dot(
             featt_ref[:, (shards - 2) * rows :], acc_ref[...] * slope_ref[(shards - 2) * rows :, :]
         )
-        total_ref[...] = (
-            first
-            + first_ref[...]
-            + own_ref[half:, :hid_count]
-            + in_ref[half:, channels : channels + hid_count]
-        )
+        lanes = channels // 128
+        own_first = get_side(own_ref[...], 0, lanes, hid_count)[1]
+        in_bias, in_first = get_side(in_ref[...], channels, lanes, hid_count)
+        first = first + first_ref[...] + own_first + in_first
+        put_side(pay_ref, channels, fold(bias_ref[...]) + in_bias, first)
+        total_ref[...] = first
 
 
 def total_kernel(channels, own_ref, come_ref, first_ref, far_first_ref, pay_ref):
-    half = own_ref.shape[0] // 2
     hid_count = first_ref.shape[1]
+    lanes = channels // 128
     pay_ref[:, :channels] = (own_ref[:, :channels].astype(f32) + come_ref[:, :channels].astype(f32)).astype(bf16)
-    high = own_ref[:half, channels : channels + 128].astype(f32) + come_ref[:half, channels : channels + 128].astype(f32)
-    low = own_ref[:half, channels + 128 :].astype(f32) + come_ref[:half, channels + 128 :].astype(f32)
-    pay_ref[:, channels:] = jnp.zeros((2 * half, SIDE), bf16)
-    high, low = split(high + low)
-    pay_ref[:half, channels : channels + 128] = high
-    pay_ref[:half, channels + 128 :] = low
-    high, low = split(first_ref[...] + far_first_ref[...])
-    pay_ref[half:, channels : channels + hid_count] = high
-    pay_ref[half:, channels + 128 : channels + 128 + hid_count] = low
+    bias = get_side(own_ref[...], channels, lanes, hid_count)[0] + get_side(come_ref[...], channels, lanes, hid_count)[0]
+    put_side(pay_ref, channels, bias, first_ref[...] + far_first_ref[...])
 
 
 def gates_kernel(
@@ -519,19 +535,13 @@
     rank = rank_ref[0]
     inner = jnp.logical_and(rank > 0, rank < shards - 1)
     hid_count = second_ref.shape[0]
-    half = hid_count // 2
     lanes = channels // 128
-
-    def pick(rows, cols):
-        return jnp.where(inner, own_ref[rows, cols].astype(f32), come_ref[rows, cols].astype(f32))
-
-    second_ref[...] = pick(slice(None), slice(0, channels))
-    top = pick(slice(0, half), slice(channels, channels + SIDE))
-    bias = top[:, :128] + top[:, 128:]
+    picked = jnp.where(inner, own_ref[...], come_ref[...])
+    second_ref[...] = picked[:, :channels].astype(f32)
+    bias, first = get_side(picked, channels, lanes, hid_count)
     for i in range(lanes):
         bias_ref[:, i * 128 : (i + 1) * 128] = bias[i : i + 1]
-    low = pick(slice(half, hid_count), slice(channels, channels + SIDE))
-    first_ref[...] = (low[:, :128] + low[:, 128:])[:, :hid_count]
+    first_ref[...] = first
 
 
 def few_shards_body(
@@ -584,34 +594,37 @@
     block_like = strip(rows)
     pay_shape = (hid_count, channels + SIDE)
 
-    x0, c0, bias = call(
+    row_step = max(rows // 4, 16)
+    gate_rows = pl.BlockSpec((row_step, channels), lambda i: (i, 0))
+    x0, c0, edge, bias = call(
         products_kernel, "products", 0, 12,
-        in_specs=[block_like] * 4,
-        out_specs=[block_like, block_like, strip(1)],
-        out_shape=[shape(rows, channels, dtype=bf16)] * 2 + [shape(1, channels)],
-    )(x_one, x_two, values, grad_out)
+        grid=(rows // row_step,),
+        in_specs=[smem] + [gate_rows] * 4,
+        out_specs=[gate_rows] * 3 + [whole(1, channels)],
+        out_shape=[shape(rows, channels, dtype=bf16)] * 3 + [shape(1, channels)],
+    )(rank, x_one, x_two, values, grad_out)
     x1 = move(x0, up)
     c1 = move(c0, down)
-
-    spec, own, trans, slope = call(
+    far = move(edge, [(0, 2), (shards - 1, shards - 3)])
+
+    spec, own, send, trans, slope = call(
         functools.partial(filters_kernel, rows, shards), "filters", 16, 40,
         in_specs=[
             whole(seq_len, feat_count), whole(feat_count, seq_len), whole(feat_count, hid_count), strip(hid_count),
             strip(1), whole(double, double), whole(double, double), block_like, block_like, whole(1, channels),
         ],
         out_specs=[
-            strip(shards, double), whole(*pay_shape), whole(2 * hid_count, seq_len), whole(seq_len, hid_count),
+            strip(shards, double), strip(hid_count), whole(*pay_shape), whole(2 * hid_count, seq_len),
+            whole(seq_len, hid_count),
         ],
         out_shape=[
-            shape(shards, double, channels), shape(*pay_shape), shape(2 * hid_count, seq_len, dtype=bf16),
-            shape(seq_len, hid_count),
+            shape(shards, double, channels, dtype=bf16), shape(hid_count, channels), shape(*pay_shape, dtype=bf16),
+            shape(2 * hid_count, seq_len, dtype=bf16), shape(seq_len, hid_count),
         ],
         scratch_shapes=[pltpu.VMEM((seq_len, 3 * hid_count), bf16), pltpu.VMEM((rows, hid_count), f32)],
     )(feats, featt, first_weight, second_weight, rate_row, front, back, x0, c0, bias)
-    come = move(own, inward)
-
-    x2 = move(x1, [(1, 2)])
-    c2 = move(c1, [(2, 1)])
+    come = move(send, inward)
+
     conv, corr, ahead, sums, first = call(
         functools.partial(near_kernel, rows, shards), "near_blocks", 20, 50,
         in_specs=[smem] + [block_like] * 4 + [
@@ -631,27 +644,26 @@
 
     part, late = call(
         functools.partial(far_kernel, rows), "far_block", 4, 30,
-        in_specs=[smem, block_like, block_like, pl.BlockSpec((2, double, width), lambda i: (1, 0, i)),
+        in_specs=[smem, block_like, pl.BlockSpec((2, double, width), lambda i: (1, 0, i)),
                   whole(double, double), whole(double, double), block_like],
         out_specs=[block_like] * 2,
         out_shape=[shape(rows, channels, dtype=bf16), shape(rows, channels)],
-    )(rank, x2, c2, spec, front, back, ahead)
+    )(rank, far, spec, front, back, ahead)
     part_come = move(part, outward)
 
-    side_block = (channels // SIDE) if channels % SIDE == 0 else 0
     pay, first = call(
-        functools.partial(last_kernel, rows, shards, channels), "last_pair", 5, 10,
-        in_specs=[smem] + [block_like] * 4 + [
+        functools.partial(last_kernel, rows, shards, channels), "last_pair", 0, 1,
+        in_specs=[smem] + [block_like] * 3 + [
             strip(hid_count), strip(1), whole(double, double), whole(double, double), whole(2 * hid_count, seq_len),
             whole(feat_count, seq_len), whole(seq_len, hid_count), strip(hid_count), whole(feat_count, hid_count),
-            pl.BlockSpec((hid_count, SIDE), lambda i: (0, side_block)), whole(*pay_shape),
+            pl.BlockSpec((hid_count, SIDE), lambda i: (0, channels // SIDE)), whole(1, channels), whole(*pay_shape),
             pl.BlockSpec(memory_space=pl.ANY),
         ],
         out_specs=[whole(*pay_shape), whole(feat_count, hid_count)],
         out_shape=[shape(*pay_shape, dtype=bf16), shape(feat_count, hid_count)],
         scratch_shapes=[pltpu.VMEM((2 * rows, hid_count), f32)],
     )(
-        rank, x1, c1, x2, c2, second_weight, rate_row, front, back, trans, featt, slope, sums, first, own, come,
+        rank, x1, c1, far, second_weight, rate_row, front, back, trans, featt, slope, sums, first, send, bias, come,
         late,
     )
     pay_come = move(pay, across)
@@ -664,7 +676,7 @@
 
     vmem = pl.BlockSpec(memory_space=pltpu.VMEM)
     total = call(
-        functools.partial(total_kernel, channels), "total", 0, 4,
+        functools.partial(total_kernel, channels), "total", 0, 1,
         grid=(),
         in_specs=[vmem] * 4,
         out_specs=vmem,
@@ -673,14 +685,14 @@
     total_come = move(total, outward)
 
     grad_one, grad_two, grad_value = call(
-        functools.partial(gates_kernel, shards), "gates", 0, 30,
+        functools.partial(gates_kernel, shards), "gates", 0, 1,
         in_specs=[smem] + [block_like] * 4 + [strip(1)] + [block_like] * 4,
         out_specs=[block_like] * 3,
         out_shape=[shape(rows, channels, dtype=bf16)] * 3,
     )(rank, x_one, x_two, values, grad_out, skip_row, conv, corr, late, part_come)
 
     grad_second, grad_first, grad_bias = call(
-        functools.partial(finish_kernel, channels, shards), "finish", 0, 4,
+        functools.partial(finish_kernel, channels, shards), "finish", 0, 1,
         grid=(),
         in_specs=[smem, vmem, vmem],
         out_specs=[vmem] * 3,

time: 100 us -> 86.6 us (0.87)
  waiting for transfers between devices: 27.1 us -> 14.4 us
  Pallas kernels: 49.4 us -> 48.1 us
    ppermute x9 -> x8, waiting for transfers between devices: 23.5 us -> 10.8 us  [move(): return lax.ppermute(array, 'ctx', pairs)]
    ppermute x9 -> x8, starting transfers between devices: 19 us -> 19.2 us  [move(): return lax.ppermute(array, 'ctx', pairs)]
  transfers between devices with their start and end apart: 11 -> 10, of which waited for: 6 -> 4; matrix products, arithmetic and copies ran while one was open for 1% -> 1% of each run, Pallas kernels for 38% -> 42%
where the time goes in v3:
time: 86.6 us; the launch traced here: 85.9 us
  Pallas kernels  48.1 us (56%)
  starting transfers between devices  20.8 us (24%)
  waiting for transfers between devices  14.4 us (17%)
  local copies, waits for them, and re-layouts  1.2 us (1%)
    ppermute x8, starting transfers between devices, move(): return lax.ppermute(array, 'ctx', pairs)  19.2 us
    pallas_call x1, Pallas kernels, few_shards_body(): call(functools.partial(filters_kernel, rows, shards), 'filters', 16, 40,...  12.1 us
    pallas_call x1, Pallas kernels, few_shards_body(): call(functools.partial(near_kernel, rows, shards), 'near_blocks', 20, 50,...  12.1 us
    ppermute x8, waiting for transfers between devices, move(): return lax.ppermute(array, 'ctx', pairs)  10.8 us
    pallas_call x1, Pallas kernels, few_shards_body(): call(functools.partial(last_kernel, rows, shards, channels), 'last_pair',...  6.12 us
    pallas_call x1, Pallas kernels, few_shards_body(): call(functools.partial(far_kernel, rows), 'far_block', 4, 30, in_specs=[s...  5.46 us
    pallas_call x1, Pallas kernels, few_shards_body(): call(functools.partial(gates_kernel, shards), 'gates', 0, 1, in_specs=[sm...  4.64 us
    pallas_call x1, Pallas kernels, few_shards_body(): call(products_kernel, 'products', 0, 12, grid=(rows // row_step,), in_spe...  3.89 us
  transfers between devices with their start and end apart: 10, of which 4 were waited for; matrix products, arithmetic and copies ran while one was open for 1% of the time, Pallas kernels for 42%

profile of v3, /device:TPU:0, one launch (start us, length us, event | category | flops | bytes accessed | tf_op | source)
XLA Modules:
  0.0 85.9 jit_solution(1561947949020602490)
XLA Ops:
  0.6 3.9 %products.1 = (bf16[128,2048]{1,0:T(8,128)(2,1)}, bf16[128,2048]{1,0:T(8,128)(2,1)}, bf16[128,2048]{1,0:T(8,128)(2,1)}, f32[1,2048]{1,0:T(1,128)}) custom-call(s32[1]{0:T(128)} %bitcast.rank_ref, bf16[128,2048]{1,0:T(8,128)(2,1)} %one_ref.3, bf16[128,2048]{1,0:T(8,128)(2,1)} %two_ref.3, bf16[128,2048]{1,0:T(8,128)(2,1)} %val_ref.3, bf16[128,2048]{1,0:T(8,128)(2,1)} %out_ref.3), custom_call_target="tpu_custom_call" | custom-call | bytes 3145728 | tf_op jit(solution)/shard_map/products/pallas_call | solution.py:599
  4.5 5.8 %collective-permute-start = (bf16[128,2048]{1,0:T(8,128)(2,1)}, bf16[128,2048]{1,0:T(8,128)(2,1)}, u32[]{:S(2)}, u32[]{:S(2)}) collective-permute-start(bf16[128,2048]{1,0:T(8,128)(2,1)} %get-tuple-element.30.source_ref.x0_ref), channel_id=1, source_target_pairs={{0,4},{4,8},{8,12},{1,5},{5,9},{9,13},{2,6},{6,10},{10,14},{3,7},{... | collective-permute-start | bytes 1572872 | tf_op jit(solution)/shard_map/ppermute | solution.py:587
  10.3 1.3 %collective-permute-start.1 = (bf16[128,2048]{1,0:T(8,128)(2,1)}, bf16[128,2048]{1,0:T(8,128)(2,1)}, u32[]{:S(2)}, u32[]{:S(2)}) collective-permute-start(bf16[128,2048]{1,0:T(8,128)(2,1)} %get-tuple-element.31.cotan_ref.c0_ref), channel_id=1, source_target_pairs={{4,0},{8,4},{12,8},{5,1},{9,5},{13,9},{6,2},{10,6},{14,10},{7,3},{... | collective-permute-start | bytes 1572872 | tf_op jit(solution)/shard_map/ppermute | solution.py:587
  11.6 5.6 %collective-permute-start.2 = (bf16[128,2048]{1,0:T(8,128)(2,1)}, bf16[128,2048]{1,0:T(8,128)(2,1)}, u32[]{:S(2)}, u32[]{:S(2)}) collective-permute-start(bf16[128,2048]{1,0:T(8,128)(2,1)} %get-tuple-element.39), channel_id=1, source_target_pairs={{0,8},{12,4},{1,9},{13,5},{2,10},{14,6},{3,11},{15,7},{16,24},{28,... | collective-permute-start | bytes 1572872 | tf_op jit(solution)/shard_map/ppermute | solution.py:587
  17.1 12.1 %filters.1 = (bf16[4,256,2048]{2,1,0:T(8,128)(2,1)}, f32[64,2048]{1,0:T(8,128)}, bf16[64,2304]{1,0:T(8,128)(2,1)}, bf16[128,512]{1,0:T(8,128)(2,1)}, f32[512,64]{1,0:T(8,128)}) custom-call(f32[512,32]{1,0:T(8,128)} %constant.13.clone.feats_ref, f32[32,512]{1,0:T(8,128)} %constant.14.clone.featt_ref, f32[32,64]{1,0:T(8,128)} %first_ref.1, ...), custom_call_target="tpu_custom_call" | custom-call | flops 4294967296 | bytes 10485760 | tf_op jit(solution)/shard_map/filters/pallas_call | solution.py:610
  29.3 2.0 %collective-permute-start.4 = (bf16[64,2304]{1,0:T(8,128)(2,1)}, bf16[64,2304]{1,0:T(8,128)(2,1)}, u32[]{:S(2)}, u32[]{:S(2)}) collective-permute-start(bf16[64,2304]{1,0:T(8,128)(2,1)} %get-tuple-element.48.own_ref), channel_id=1, source_target_pairs={{0,4},{12,8},{1,5},{13,9},{2,6},{14,10},{3,7},{15,11},{16,20},{28,... | collective-permute-start | bytes 884744 | tf_op jit(solution)/shard_map/ppermute | solution.py:587
  31.3 0.0 collective-permute-done.x1_ref
  31.3 0.0 collective-permute-done.1.c1_ref
  31.3 12.1 %near_blocks.1 = (f32[128,2048]{1,0:T(8,128)}, f32[128,2048]{1,0:T(8,128)}, f32[128,2048]{1,0:T(8,128)}, f32[64,2048]{1,0:T(8,128)}, f32[32,64]{1,0:T(8,128)}) custom-call(s32[1]{0:T(128)} %bitcast.rank_ref, bf16[128,2048]{1,0:T(8,128)(2,1)} %get-tuple-element.30.source_ref.x0_ref, bf16[128,2048]{1,0:T(8,128)(2,1)} %get-tuple-element.31.cotan_ref.c0_ref, ...), custom_call_target="tpu_custom_call" | custom-call | flops 5368709120 | bytes 13107200 | tf_op jit(solution)/shard_map/near_blocks/pallas_call | solution.py:628
  43.4 0.0 collective-permute-done.2.far_ref
  43.4 5.5 %far_block.1 = (bf16[128,2048]{1,0:T(8,128)(2,1)}, f32[128,2048]{1,0:T(8,128)}) custom-call(s32[1]{0:T(128)} %bitcast.rank_ref, bf16[128,2048]{1,0:T(8,128)(2,1)} %collective-permute-done.2.far_ref, bf16[4,256,2048]{2,1,0:T(8,128)(2,1)} %get-tuple-element.33.spec_ref, bf16[256,256]{1,0:T(8,128)(2,1)} %constant.15.clone.front_ref, ...), custom_call_target="tpu_custom_call" | custom-call | flops 1073741824 | bytes 7864320 | tf_op jit(solution)/shard_map/far_block/pallas_call | solution.py:645
  48.9 0.0 collective-permute-done.4.in_ref
  48.9 6.1 %last_pair.1 = (bf16[64,2304]{1,0:T(8,128)(2,1)}, f32[32,64]{1,0:T(8,128)}) custom-call(s32[1]{0:T(128)} %bitcast.rank_ref, bf16[128,2048]{1,0:T(8,128)(2,1)} %collective-permute-done.x1_ref, bf16[128,2048]{1,0:T(8,128)(2,1)} %collective-permute-done.1.c1_ref, bf16[128,2048]{1,0:T(8,128)(2,1)} %collective-permute-done.2.far_ref, f32[64,2048]{1,0:T(8,128)} %weight_ref.5, ...), custom_call_target="tpu_custom_call" | custom-call | bytes 262144 | tf_op jit(solution)/shard_map/last_pair/pallas_call | solution.py:654
  55.0 1.4 %collective-permute-start.5 = (bf16[64,2304]{1,0:T(8,128)(2,1)}, bf16[64,2304]{1,0:T(8,128)(2,1)}, u32[]{:S(2)}, u32[]{:S(2)}) collective-permute-start(bf16[64,2304]{1,0:T(8,128)(2,1)} %get-tuple-element.49.own_ref), channel_id=1, source_target_pairs={{4,8},{8,4},{5,9},{9,5},{6,10},{10,6},{7,11},{11,7},{20,24},{24,20... | collective-permute-start | bytes 884744 | tf_op jit(solution)/shard_map/ppermute | solution.py:587
  56.4 1.3 %collective-permute-start.3 = (bf16[128,2048]{1,0:T(8,128)(2,1)}, bf16[128,2048]{1,0:T(8,128)(2,1)}, u32[]{:S(2)}, u32[]{:S(2)}) collective-permute-start(bf16[128,2048]{1,0:T(8,128)(2,1)} %get-tuple-element.42), channel_id=1, source_target_pairs={{4,0},{8,12},{5,1},{9,13},{6,2},{10,14},{7,3},{11,15},{20,16},{24,... | collective-permute-start | bytes 1572872 | tf_op jit(solution)/shard_map/ppermute | solution.py:587
  57.7 0.1 collective-permute-start.6
  57.8 1.4 %collective-permute-done.6 = f32[32,64]{1,0:T(8,128)S(1)} collective-permute-done((f32[32,64]{1,0:T(8,128)}, f32[32,64]{1,0:T(8,128)S(1)}, u32[]{:S(2)}, u32[]{:S(2)}) %collective-permute-start.6) | collective-permute-done | bytes 8224 | tf_op jit(solution)/shard_map/ppermute | solution.py:673
  59.1 0.7 add.6
  59.9 1.5 %collective-permute-start.7 = (f32[32,64]{1,0:T(8,128)S(1)}, f32[32,64]{1,0:T(8,128)S(1)}, u32[]{:S(2)}, u32[]{:S(2)}) collective-permute-start(f32[32,64]{1,0:T(8,128)S(1)} %add.6), channel_id=1, source_target_pairs={{0,2},{1,3},{2,0},{3,1},{4,6},{5,7},{6,4},{7,5},{8,10},{9,11},{10,... | collective-permute-start | bytes 24584 | tf_op jit(solution)/shard_map/ppermute | solution.py:673
  61.3 2.3 %collective-permute-done.7 = f32[32,64]{1,0:T(8,128)S(1)} collective-permute-done((f32[32,64]{1,0:T(8,128)S(1)}, f32[32,64]{1,0:T(8,128)S(1)}, u32[]{:S(2)}, u32[]{:S(2)}) %collective-permute-start.7) | collective-permute-done | bytes 8224 | tf_op jit(solution)/shard_map/ppermute | solution.py:673
  63.6 0.0 copy-start
  63.6 0.6 copy-done
  64.2 0.7 collective-permute-start.8
  64.9 0.0 collective-permute-done.8.far_first_ref
  64.9 0.0 copy-start.1
  64.9 0.6 copy-done.1
  65.5 0.0 collective-permute-done.5.come_ref
  65.5 1.8 %total.1.own_ref = bf16[64,2304]{1,0:T(8,128)(2,1)} custom-call(bf16[64,2304]{1,0:T(8,128)(2,1)} %get-tuple-element.49.own_ref, bf16[64,2304]{1,0:T(8,128)(2,1)} %collective-permute-done.5.come_ref, f32[32,64]{1,0:T(8,128)} %copy-done, f32[32,64]{1,0:T(8,128)} %copy-done.1), custom_call_target="tpu_custom_call" | custom-call | bytes 262144 | tf_op jit(solution)/shard_map/total/pallas_call | solution.py:678
  67.3 1.3 %collective-permute-start.9 = (bf16[64,2304]{1,0:T(8,128)(2,1)}, bf16[64,2304]{1,0:T(8,128)(2,1)}, u32[]{:S(2)}, u32[]{:S(2)}) collective-permute-start(bf16[64,2304]{1,0:T(8,128)(2,1)} %total.1.own_ref), channel_id=1, source_target_pairs={{4,0},{8,12},{5,1},{9,13},{6,2},{10,14},{7,3},{11,15},{20,16},{24,... | collective-permute-start | bytes 884744 | tf_op jit(solution)/shard_map/ppermute | solution.py:587
  68.6 2.8 %collective-permute-done.3.part_ref = bf16[128,2048]{1,0:T(8,128)(2,1)} collective-permute-done((bf16[128,2048]{1,0:T(8,128)(2,1)}, bf16[128,2048]{1,0:T(8,128)(2,1)}, u32[]{:S(2)}, u32[]{:S(2)}) %collective-permute-start.3) | collective-permute-done | bytes 524320 | tf_op jit(solution)/shard_map/ppermute | solution.py:587
  71.4 4.6 %gates.1 = (bf16[128,2048]{1,0:T(8,128)(2,1)}, bf16[128,2048]{1,0:T(8,128)(2,1)}, bf16[128,2048]{1,0:T(8,128)(2,1)}) custom-call(s32[1]{0:T(128)} %bitcast.rank_ref, bf16[128,2048]{1,0:T(8,128)(2,1)} %one_ref.3, bf16[128,2048]{1,0:T(8,128)(2,1)} %two_ref.3, bf16[128,2048]{1,0:T(8,128)(2,1)} %val_ref.3, bf16[128,2048]{1,0:T(8,128)(2,1)} %out_ref.3, ...), custom_call_target="tpu_custom_call" | custom-call | bytes 262144 | tf_op jit(solution)/shard_map/gates/pallas_call | solution.py:687
  76.1 8.0 %collective-permute-done.9.come_ref = bf16[64,2304]{1,0:T(8,128)(2,1)} collective-permute-done((bf16[64,2304]{1,0:T(8,128)(2,1)}, bf16[64,2304]{1,0:T(8,128)(2,1)}, u32[]{:S(2)}, u32[]{:S(2)}) %collective-permute-start.9) | collective-permute-done | bytes 294944 | tf_op jit(solution)/shard_map/ppermute | solution.py:587
  84.0 1.9 %finish.1 = (f32[64,2048]{1,0:T(8,128)}, f32[32,64]{1,0:T(8,128)}, f32[1,2048]{1,0:T(1,128)}) custom-call(s32[1]{0:T(128)} %bitcast.rank_ref, bf16[64,2304]{1,0:T(8,128)(2,1)} %total.1.own_ref, bf16[64,2304]{1,0:T(8,128)(2,1)} %collective-permute-done.9.come_ref), custom_call_target="tpu_custom_call" | custom-call | bytes 262144 | tf_op jit(solution)/shard_map/finish/pallas_call | solution.py:694
  (1 shorter events, 0.0 us)
Async XLA Ops:
  4.5 26.8 %collective-permute-start = (bf16[128,2048]{1,0:T(8,128)(2,1)}, bf16[128,2048]{1,0:T(8,128)(2,1)}, u32[]{:S(2)}, u32[]{:S(2)}) collective-permute-start(bf16[128,2048]{1,0:T(8,128)(2,1)} %get-tuple-element.30.source_ref.x0_ref), channel_id=1, source_target_pairs={{0,4},{4,8},{8,12},{1,5},{5,9},{9,13},{2,6},{6,10},{10,14},{3,7},{... | collective-permute-start | bytes 1572872 | tf_op jit(solution)/shard_map/ppermute | solution.py:587
  10.3 21.0 %collective-permute-start.1 = (bf16[128,2048]{1,0:T(8,128)(2,1)}, bf16[128,2048]{1,0:T(8,128)(2,1)}, u32[]{:S(2)}, u32[]{:S(2)}) collective-permute-start(bf16[128,2048]{1,0:T(8,128)(2,1)} %get-tuple-element.31.cotan_ref.c0_ref), channel_id=1, source_target_pairs={{4,0},{8,4},{12,8},{5,1},{9,5},{13,9},{6,2},{10,6},{14,10},{7,3},{... | collective-permute-start | bytes 1572872 | tf_op jit(solution)/shard_map/ppermute | solution.py:587
  11.6 31.8 %collective-permute-start.2 = (bf16[128,2048]{1,0:T(8,128)(2,1)}, bf16[128,2048]{1,0:T(8,128)(2,1)}, u32[]{:S(2)}, u32[]{:S(2)}) collective-permute-start(bf16[128,2048]{1,0:T(8,128)(2,1)} %get-tuple-element.39), channel_id=1, source_target_pairs={{0,8},{12,4},{1,9},{13,5},{2,10},{14,6},{3,11},{15,7},{16,24},{28,... | collective-permute-start | bytes 1572872 | tf_op jit(solution)/shard_map/ppermute | solution.py:587
  29.3 19.6 %collective-permute-start.4 = (bf16[64,2304]{1,0:T(8,128)(2,1)}, bf16[64,2304]{1,0:T(8,128)(2,1)}, u32[]{:S(2)}, u32[]{:S(2)}) collective-permute-start(bf16[64,2304]{1,0:T(8,128)(2,1)} %get-tuple-element.48.own_ref), channel_id=1, source_target_pairs={{0,4},{12,8},{1,5},{13,9},{2,6},{14,10},{3,7},{15,11},{16,20},{28,... | collective-permute-start | bytes 884744 | tf_op jit(solution)/shard_map/ppermute | solution.py:587
  55.0 10.5 %collective-permute-start.5 = (bf16[64,2304]{1,0:T(8,128)(2,1)}, bf16[64,2304]{1,0:T(8,128)(2,1)}, u32[]{:S(2)}, u32[]{:S(2)}) collective-permute-start(bf16[64,2304]{1,0:T(8,128)(2,1)} %get-tuple-element.49.own_ref), channel_id=1, source_target_pairs={{4,8},{8,4},{5,9},{9,5},{6,10},{10,6},{7,11},{11,7},{20,24},{24,20... | collective-permute-start | bytes 884744 | tf_op jit(solution)/shard_map/ppermute | solution.py:587
  56.4 15.0 %collective-permute-start.3 = (bf16[128,2048]{1,0:T(8,128)(2,1)}, bf16[128,2048]{1,0:T(8,128)(2,1)}, u32[]{:S(2)}, u32[]{:S(2)}) collective-permute-start(bf16[128,2048]{1,0:T(8,128)(2,1)} %get-tuple-element.42), channel_id=1, source_target_pairs={{4,0},{8,12},{5,1},{9,13},{6,2},{10,14},{7,3},{11,15},{20,16},{24,... | collective-permute-start | bytes 1572872 | tf_op jit(solution)/shard_map/ppermute | solution.py:587
  57.7 1.5 %collective-permute-start.6 = (f32[32,64]{1,0:T(8,128)}, f32[32,64]{1,0:T(8,128)S(1)}, u32[]{:S(2)}, u32[]{:S(2)}) collective-permute-start(f32[32,64]{1,0:T(8,128)} %get-tuple-element.50), channel_id=1, source_target_pairs={{0,1},{1,0},{2,3},{3,2},{4,5},{5,4},{6,7},{7,6},{8,9},{9,8},{10,11... | collective-permute-start | bytes 24584 | tf_op jit(solution)/shard_map/ppermute | solution.py:673
  59.9 3.7 %collective-permute-start.7 = (f32[32,64]{1,0:T(8,128)S(1)}, f32[32,64]{1,0:T(8,128)S(1)}, u32[]{:S(2)}, u32[]{:S(2)}) collective-permute-start(f32[32,64]{1,0:T(8,128)S(1)} %add.6), channel_id=1, source_target_pairs={{0,2},{1,3},{2,0},{3,1},{4,6},{5,7},{6,4},{7,5},{8,10},{9,11},{10,... | collective-permute-start | bytes 24584 | tf_op jit(solution)/shard_map/ppermute | solution.py:673
  63.6 0.6 copy-start
  64.2 0.7 collective-permute-start.8
  64.9 0.6 copy-start.1
  67.3 16.7 %collective-permute-start.9 = (bf16[64,2304]{1,0:T(8,128)(2,1)}, bf16[64,2304]{1,0:T(8,128)(2,1)}, u32[]{:S(2)}, u32[]{:S(2)}) collective-permute-start(bf16[64,2304]{1,0:T(8,128)(2,1)} %total.1.own_ref), channel_id=1, source_target_pairs={{4,0},{8,12},{5,1},{9,13},{6,2},{10,14},{7,3},{11,15},{20,16},{24,... | collective-permute-start | bytes 884744 | tf_op jit(solution)/shard_map/ppermute | solution.py:587

commit v4 on v3

--- a/solution.py
+++ b/solution.py
@@ -272,23 +272,40 @@
     return dot_across(left, right)
 
 
-def add_up(ref, value, block):
-    @pl.when(block == 0)
-    def _():
-        ref[...] = value
-
-    @pl.when(block > 0)
-    def _():
-        ref[...] += value
-
-
-def products_kernel(rank_ref, one_ref, two_ref, val_ref, out_ref, source_ref, cotan_ref, far_ref, bias_ref):
+def looped(kernel, kinds, blocks, width):
+    def over_strips(*refs):
+        def step(block, carry):
+            cols = pl.ds(pl.multiple_of(block * width, width), width)
+            views = [
+                ref if kind is None else ref.at[(*kind, cols)]
+                for ref, kind in zip(refs, kinds + (None,) * (len(refs) - len(kinds)))
+            ]
+            kernel(block, blocks, *views)
+            return carry
+
+        lax.fori_loop(0, blocks, step, 0)
+
+    return over_strips
+
+
+ROWS = (slice(None),)
+CUBE = (slice(None), slice(None))
+
+
+def products_kernel(one_ref, two_ref, val_ref, out_ref, source_ref, cotan_ref, bias_ref):
     source = one_ref[...].astype(f32) * val_ref[...].astype(f32)
     cotan = out_ref[...].astype(f32) * two_ref[...].astype(f32)
     source_ref[...] = source.astype(bf16)
     cotan_ref[...] = cotan.astype(bf16)
-    far_ref[...] = jnp.where(rank_ref[0] == 0, source, cotan).astype(bf16)
-    add_up(bias_ref, jnp.sum(source * cotan, axis=0, keepdims=True), pl.program_id(0))
+    part = jnp.sum(source * cotan, axis=0, keepdims=True)
+
+    @pl.when(pl.program_id(0) == 0)
+    def _():
+        bias_ref[...] = part
+
+    @pl.when(pl.program_id(0) > 0)
+    def _():
+        bias_ref[...] += part
 
 
 def sin_cos(angle):
@@ -309,13 +326,10 @@
 
 
 def filters_kernel(
-    rows, shards, feats_ref, featt_ref, first_ref, weight_ref, rate_ref, front_ref, back_ref, source_ref, cotan_ref,
-    bias_ref, spec_ref, sums_ref, send_ref, trans_ref, slope_ref, hid_ref, acc_ref,
+    rows, shards, block, blocks, rank_ref, feats_ref, first_ref, weight_ref, rate_ref, front_ref, source_ref, cotan_ref,
+    spec_ref, trans_ref, slope_ref, edge_ref, hid_ref,
 ):
-    block = pl.program_id(0)
-    last = pl.num_programs(0) - 1
-    hid_count, width = weight_ref.shape
-    channels = bias_ref.shape[1]
+    hid_count = first_ref.shape[1]
     scale = float(rows * shards) ** -0.5
 
     @pl.when(block == 0)
@@ -328,6 +342,7 @@
         turned_over = jnp.concatenate([hidden, slope], axis=1).T[:hid_count]
         trans_ref[...] = jnp.concatenate(split(turned_over), axis=0)
 
+    edge_ref[...] = jnp.where(rank_ref[0] == 0, source_ref[...], cotan_ref[...])
     w_high, w_low = split(weight_ref[...])
     stacked = jnp.concatenate([w_high, w_low, w_high], axis=0)
     rate = rate_ref[...]
@@ -346,17 +361,29 @@
             spec_ref[lag, im, :] = here[1].astype(bf16)
         before = now
 
+
+def own_kernel(
+    rows, shards, channels, block, blocks, source_ref, cotan_ref, weight_ref, rate_ref, front_ref, back_ref, trans_ref,
+    slope_ref, featt_ref, bias_ref, sums_ref, send_ref, acc_ref,
+):
+    width = weight_ref.shape[1]
+
+    @pl.when(block == 0)
+    def _():
+        acc_ref[...] = jnp.zeros_like(acc_ref)
+
     x0 = forward(front_ref, source_ref[...])
     c0 = forward(front_ref, cotan_ref[...])
     pair = conj_times((x0[:rows], x0[rows:]), (c0[:rows], c0[rows:]))
     high, low = split(jnp.concatenate(pair, axis=0))
+    env = decay(rate_ref[...], rows, float(rows * shards) ** -0.5)
     m_high, m_low = split(backward(back_ref, high, low) * env)
     sums = weight_sums(trans_ref[:, :rows], m_high, m_low)
     sums_ref[...] = sums
     send_ref[:, pl.ds(pl.multiple_of(block * width, width), width)] = sums.astype(bf16)
-    add_up(acc_ref, hidden_sums(m_high, m_low, w_high, w_low), block)
-
-    @pl.when(block == last)
+    acc_ref[...] += hidden_sums(m_high, m_low, *split(weight_ref[...]))
+
+    @pl.when(block == blocks - 1)
     def _():
         first = exact_dot(featt_ref[:, :rows], acc_ref[...] * slope_ref[:rows, :])
         put_side(send_ref, channels, fold(bias_ref[...]), first)
@@ -366,13 +393,14 @@
     return jnp.concatenate([bias[:, i * 128 : (i + 1) * 128] for i in range(bias.shape[1] // 128)], axis=0)
 
 
-def put_side(pay_ref, channels, bias, first):
+def put_side(pay_ref, channels, bias, first=None):
     half = pay_ref.shape[0] // 2
     pay_ref[:, channels:] = jnp.zeros((2 * half, SIDE), bf16)
-    for start, bias_part, first_part in zip((0, 128), split(bias), split(first)):
-        at = channels + start
-        pay_ref[: bias.shape[0], at : at + 128] = bias_part
-        pay_ref[half:, at : at + first.shape[1]] = first_part
+    for start, part in zip((0, 128), split(bias)):
+        pay_ref[: bias.shape[0], channels + start : channels + start + 128] = part
+    if first is not None:
+        for start, part in zip((0, 128), split(first)):
+            pay_ref[half:, channels + start : channels + start + first.shape[1]] = part
 
 
 def get_side(pay, channels, lanes, hid_count):
@@ -382,14 +410,17 @@
 
 
 def near_kernel(
-    rows, shards, rank_ref, x0_ref, c0_ref, x1_ref, c1_ref, spec_ref, weight_ref, rate_ref, front_ref, back_ref,
+    rows, shards, block, blocks, rank_ref, x0_ref, c0_ref, x1_ref, c1_ref, spec_ref, weight_ref, rate_ref, front_ref, back_ref,
     trans_ref, featt_ref, slope_ref, own_ref, conv_ref, corr_ref, ahead_ref, sums_ref, first_ref, fields, fast, high_ref,
     low_ref, acc_ref,
 ):
-    block = pl.program_id(0)
-    last = pl.num_programs(0) - 1
     rank = rank_ref[0]
     count = shards - 1
+
+    @pl.when(block == 0)
+    def _():
+        acc_ref[...] = jnp.zeros_like(acc_ref)
+
     lower = rank == 1
     upper = jnp.where(rank == 2, 1.0, 0.0).astype(f32)
     below_top = jnp.where(rank == shards - 1, 0.0, 1.0).astype(f32)
@@ -423,16 +454,16 @@
     m_low = jnp.concatenate([p[1] for p in parts], axis=0)
     sums_ref[...] = own_ref[...] + weight_sums(trans_ref[:, : count * rows], m_high, m_low)
     w_high, w_low = split(weight_ref[...])
-    add_up(acc_ref, hidden_sums(m_high, m_low, w_high, w_low), block)
-
-    @pl.when(block == last)
+    acc_ref[...] += hidden_sums(m_high, m_low, w_high, w_low)
+
+    @pl.when(block == blocks - 1)
     def _():
         first_ref[...] = exact_dot(
             featt_ref[:, : count * rows], acc_ref[...] * slope_ref[: count * rows, :]
         )
 
 
-def far_kernel(rows, rank_ref, far_ref, spec_ref, front_ref, back_ref, ahead_ref, part_ref, late_ref):
+def far_kernel(rows, block, blocks, rank_ref, far_ref, spec_ref, front_ref, back_ref, ahead_ref, part_ref, late_ref):
     side = jnp.where(rank_ref[0] == 2, 1.0, -1.0).astype(f32)
     far = forward(front_ref, far_ref[...])
     far = (far[:rows], far[rows:])
@@ -444,13 +475,9 @@
 
 
 def last_kernel(
-    rows, shards, channels, rank_ref, x1_ref, c1_ref, far_ref, weight_ref, rate_ref, front_ref, back_ref,
-    trans_ref, featt_ref, slope_ref, sums_ref, first_ref, own_ref, bias_ref, in_ref, after_ref, pay_ref, total_ref,
-    acc_ref,
+    rows, shards, channels, block, blocks, rank_ref, x1_ref, c1_ref, far_ref, weight_ref, rate_ref, front_ref, back_ref,
+    trans_ref, featt_ref, slope_ref, sums_ref, first_ref, own_ref, bias_ref, in_ref, pay_ref, total_ref, acc_ref,
 ):
-    del after_ref
-    block = pl.program_id(0)
-    blocks = pl.num_programs(0)
     hid_count, width = weight_ref.shape
     lower = rank_ref[0] == 1
     start = pl.multiple_of(block * width, width)
@@ -493,23 +520,22 @@
             featt_ref[:, (shards - 2) * rows :], acc_ref[...] * slope_ref[(shards - 2) * rows :, :]
         )
         lanes = channels // 128
-        own_first = get_side(own_ref[...], 0, lanes, hid_count)[1]
+        own_first = get_side(own_ref[...], channels, lanes, hid_count)[1]
         in_bias, in_first = get_side(in_ref[...], channels, lanes, hid_count)
         first = first + first_ref[...] + own_first + in_first
-        put_side(pay_ref, channels, fold(bias_ref[...]) + in_bias, first)
+        put_side(pay_ref, channels, fold(bias_ref[...]) + in_bias)
         total_ref[...] = first
 
 
-def total_kernel(channels, own_ref, come_ref, first_ref, far_first_ref, pay_ref):
-    hid_count = first_ref.shape[1]
+def total_kernel(channels, hid_count, own_ref, come_ref, pay_ref):
     lanes = channels // 128
     pay_ref[:, :channels] = (own_ref[:, :channels].astype(f32) + come_ref[:, :channels].astype(f32)).astype(bf16)
-    bias = get_side(own_ref[...], channels, lanes, hid_count)[0] + get_side(come_ref[...], channels, lanes, hid_count)[0]
-    put_side(pay_ref, channels, bias, first_ref[...] + far_first_ref[...])
+    own, come = (get_side(ref[...], channels, lanes, hid_count)[0] for ref in (own_ref, come_ref))
+    put_side(pay_ref, channels, own + come)
 
 
 def gates_kernel(
-    shards, rank_ref, one_ref, two_ref, val_ref, out_ref, skip_ref, conv_ref, corr_ref, late_ref, part_ref,
+    shards, block, blocks, rank_ref, one_ref, two_ref, val_ref, out_ref, skip_ref, conv_ref, corr_ref, late_ref, part_ref,
     grad_one_ref, grad_two_ref, grad_value_ref,
 ):
     rank = rank_ref[0]
@@ -531,17 +557,28 @@
     grad_value_ref[...] = (mid * one).astype(bf16)
 
 
-def finish_kernel(channels, shards, rank_ref, own_ref, come_ref, second_ref, first_ref, bias_ref):
+def finish_kernel(
+    channels, shards, rank_ref, own_ref, come_ref, first_ref, first_come_ref, second_out, first_out, bias_out, second,
+    first, bias, sems,
+):
     rank = rank_ref[0]
     inner = jnp.logical_and(rank > 0, rank < shards - 1)
-    hid_count = second_ref.shape[0]
     lanes = channels // 128
+    copies = [
+        pltpu.make_async_copy(held, out, sems.at[i])
+        for i, (held, out) in enumerate(((second, second_out), (first, first_out), (bias, bias_out)))
+    ]
     picked = jnp.where(inner, own_ref[...], come_ref[...])
-    second_ref[...] = picked[:, :channels].astype(f32)
-    bias, first = get_side(picked, channels, lanes, hid_count)
+    second[...] = picked[:, :channels].astype(f32)
+    copies[0].start()
+    first[...] = jnp.where(inner, first_ref[...], first_come_ref[...])
+    copies[1].start()
+    rows = get_side(picked, channels, lanes, first.shape[1])[0]
     for i in range(lanes):
-        bias_ref[:, i * 128 : (i + 1) * 128] = bias[i : i + 1]
-    first_ref[...] = first
+        bias[:, i * 128 : (i + 1) * 128] = rows[i : i + 1]
+    copies[2].start()
+    for copy in copies:
+        copy.wait()
 
 
 def few_shards_body(
@@ -561,26 +598,25 @@
     skip_row = skip_bias.reshape(1, channels)
     rate_row = decay_rate.reshape(1, channels)
     smem = pl.BlockSpec(memory_space=pltpu.SMEM)
-
-    def whole(*dims):
-        return pl.BlockSpec(dims, lambda i: (0,) * len(dims))
-
-    def strip(*lead):
-        return pl.BlockSpec(lead + (width,), lambda i: (0,) * len(lead) + (i,))
+    vmem = pl.BlockSpec(memory_space=pltpu.VMEM)
+    anywhere = pl.BlockSpec(memory_space=pl.ANY)
+    mebi = 1024 * 1024
 
     def shape(*dims, dtype=f32):
         return jax.ShapeDtypeStruct(dims, dtype)
 
-    def call(kernel, name, units, size, **how):
-        how.setdefault("grid", (blocks,))
+    def call(kernel, name, units, out_shape, in_specs, out_specs=None, scratch=(), limit=16):
         return pl.pallas_call(
             kernel,
-            compiler_params=pltpu.CompilerParams(vmem_limit_bytes=64 * 1024 * 1024),
+            in_specs=in_specs,
+            out_specs=out_specs if out_specs is not None else [vmem] * len(out_shape),
+            out_shape=out_shape,
+            scratch_shapes=scratch,
+            compiler_params=pltpu.CompilerParams(vmem_limit_bytes=limit * mebi),
             cost_estimate=pl.CostEstimate(
-                flops=2 * units * double * double * channels, bytes_accessed=size * rows * channels, transcendentals=0
+                flops=2 * units * double * double * channels, bytes_accessed=rows * channels, transcendentals=0
             ),
             name=name,
-            **how,
         )
 
     def move(array, pairs):
@@ -591,49 +627,63 @@
     inward = [(0, 1), (shards - 1, shards - 2)]
     outward = [(1, 0), (shards - 2, shards - 1)]
     across = [(1, 2), (2, 1)]
-    block_like = strip(rows)
     pay_shape = (hid_count, channels + SIDE)
-
-    row_step = max(rows // 4, 16)
+    block_bf16 = shape(rows, channels, dtype=bf16)
+    block_f32 = shape(rows, channels)
+
+    row_step = max(rows // 2, 16)
     gate_rows = pl.BlockSpec((row_step, channels), lambda i: (i, 0))
-    x0, c0, edge, bias = call(
-        products_kernel, "products", 0, 12,
+    x0, c0, bias = pl.pallas_call(
+        products_kernel,
         grid=(rows // row_step,),
-        in_specs=[smem] + [gate_rows] * 4,
-        out_specs=[gate_rows] * 3 + [whole(1, channels)],
-        out_shape=[shape(rows, channels, dtype=bf16)] * 3 + [shape(1, channels)],
-    )(rank, x_one, x_two, values, grad_out)
+        in_specs=[gate_rows] * 4,
+        out_specs=[gate_rows] * 2 + [pl.BlockSpec((1, channels), lambda i: (0, 0))],
+        out_shape=[block_bf16] * 2 + [shape(1, channels)],
+        compiler_params=pltpu.CompilerParams(vmem_limit_bytes=64 * mebi),
+        name="products",
+    )(x_one, x_two, values, grad_out)
     x1 = move(x0, up)
     c1 = move(c0, down)
+
+    spec, trans, slope, edge = call(
+        looped(
+            functools.partial(filters_kernel, rows, shards),
+            (None, None, None, ROWS, ROWS, None, ROWS, ROWS, CUBE, None, None, ROWS),
+            blocks, width,
+        ),
+        "filters", 8,
+        [
+            shape(shards, double, channels, dtype=bf16), shape(2 * hid_count, seq_len, dtype=bf16),
+            shape(seq_len, hid_count), block_bf16,
+        ],
+        [smem] + [vmem] * 7,
+        scratch=[pltpu.VMEM((seq_len, 3 * hid_count), bf16)],
+    )(rank, feats, first_weight, second_weight, rate_row, front, x0, c0)
     far = move(edge, [(0, 2), (shards - 1, shards - 3)])
 
-    spec, own, send, trans, slope = call(
-        functools.partial(filters_kernel, rows, shards), "filters", 16, 40,
-        in_specs=[
-            whole(seq_len, feat_count), whole(feat_count, seq_len), whole(feat_count, hid_count), strip(hid_count),
-            strip(1), whole(double, double), whole(double, double), block_like, block_like, whole(1, channels),
-        ],
-        out_specs=[
-            strip(shards, double), strip(hid_count), whole(*pay_shape), whole(2 * hid_count, seq_len),
-            whole(seq_len, hid_count),
-        ],
-        out_shape=[
-            shape(shards, double, channels, dtype=bf16), shape(hid_count, channels), shape(*pay_shape, dtype=bf16),
-            shape(2 * hid_count, seq_len, dtype=bf16), shape(seq_len, hid_count),
-        ],
-        scratch_shapes=[pltpu.VMEM((seq_len, 3 * hid_count), bf16), pltpu.VMEM((rows, hid_count), f32)],
-    )(feats, featt, first_weight, second_weight, rate_row, front, back, x0, c0, bias)
+    own, send = call(
+        looped(
+            functools.partial(own_kernel, rows, shards, channels),
+            (ROWS, ROWS, ROWS, ROWS, None, None, None, None, None, None, ROWS),
+            blocks, width,
+        ),
+        "own_pair", 8,
+        [shape(hid_count, channels), shape(*pay_shape, dtype=bf16)],
+        [vmem] * 10,
+        scratch=[pltpu.VMEM((rows, hid_count), f32)],
+    )(x0, c0, second_weight, rate_row, front, back, trans, slope, featt, bias)
     come = move(send, inward)
 
     conv, corr, ahead, sums, first = call(
-        functools.partial(near_kernel, rows, shards), "near_blocks", 20, 50,
-        in_specs=[smem] + [block_like] * 4 + [
-            strip(shards - 1, double), strip(hid_count), strip(1), whole(double, double), whole(double, double),
-            whole(2 * hid_count, seq_len), whole(feat_count, seq_len), whole(seq_len, hid_count), strip(hid_count),
-        ],
-        out_specs=[block_like] * 3 + [strip(hid_count), whole(feat_count, hid_count)],
-        out_shape=[shape(rows, channels)] * 3 + [shape(hid_count, channels), shape(feat_count, hid_count)],
-        scratch_shapes=[
+        looped(
+            functools.partial(near_kernel, rows, shards),
+            (None, ROWS, ROWS, ROWS, ROWS, CUBE, ROWS, ROWS, None, None, None, None, None, ROWS, ROWS, ROWS, ROWS, ROWS),
+            blocks, width,
+        ),
+        "near_blocks", 20,
+        [block_f32] * 3 + [shape(hid_count, channels), shape(feat_count, hid_count)],
+        [smem] + [vmem] * 13,
+        scratch=[
             pltpu.VMEM((4, double, width), f32),
             pltpu.VMEM((3, double, width), bf16),
             pltpu.VMEM((shards - 1, double, width), bf16),
@@ -643,61 +693,61 @@
     )(rank, x0, c0, x1, c1, spec, second_weight, rate_row, front, back, trans, featt, slope, own)
 
     part, late = call(
-        functools.partial(far_kernel, rows), "far_block", 4, 30,
-        in_specs=[smem, block_like, pl.BlockSpec((2, double, width), lambda i: (1, 0, i)),
-                  whole(double, double), whole(double, double), block_like],
-        out_specs=[block_like] * 2,
-        out_shape=[shape(rows, channels, dtype=bf16), shape(rows, channels)],
+        looped(
+            functools.partial(far_kernel, rows),
+            (None, ROWS, (slice(2, 4), slice(None)), None, None, ROWS, ROWS, ROWS),
+            blocks, width,
+        ),
+        "far_block", 1,
+        [block_bf16, block_f32],
+        [smem] + [vmem] * 5,
     )(rank, far, spec, front, back, ahead)
     part_come = move(part, outward)
 
     pay, first = call(
-        functools.partial(last_kernel, rows, shards, channels), "last_pair", 0, 1,
-        in_specs=[smem] + [block_like] * 3 + [
-            strip(hid_count), strip(1), whole(double, double), whole(double, double), whole(2 * hid_count, seq_len),
-            whole(feat_count, seq_len), whole(seq_len, hid_count), strip(hid_count), whole(feat_count, hid_count),
-            pl.BlockSpec((hid_count, SIDE), lambda i: (0, channels // SIDE)), whole(1, channels), whole(*pay_shape),
-            pl.BlockSpec(memory_space=pl.ANY),
-        ],
-        out_specs=[whole(*pay_shape), whole(feat_count, hid_count)],
-        out_shape=[shape(*pay_shape, dtype=bf16), shape(feat_count, hid_count)],
-        scratch_shapes=[pltpu.VMEM((2 * rows, hid_count), f32)],
-    )(
-        rank, x1, c1, far, second_weight, rate_row, front, back, trans, featt, slope, sums, first, send, bias, come,
-        late,
-    )
+        looped(
+            functools.partial(last_kernel, rows, shards, channels),
+            (None, ROWS, ROWS, ROWS, ROWS, ROWS, None, None, None, None, None, ROWS),
+            blocks, width,
+        ),
+        "last_pair", 1,
+        [shape(*pay_shape, dtype=bf16), shape(feat_count, hid_count)],
+        [smem] + [vmem] * 15,
+        scratch=[pltpu.VMEM((2 * rows, hid_count), f32)],
+    )(rank, x1, c1, far, second_weight, rate_row, front, back, trans, featt, slope, sums, first, send, bias, come)
     pay_come = move(pay, across)
     group = lax.axis_size(("ch", "sub"))
     bit = 1
     while bit < group:
         first = first + lax.ppermute(first, ("ch", "sub"), [(i, i ^ bit) for i in range(group)])
         bit *= 2
-    first_come = move(first, across)
-
-    vmem = pl.BlockSpec(memory_space=pltpu.VMEM)
-    total = call(
-        functools.partial(total_kernel, channels), "total", 0, 1,
-        grid=(),
-        in_specs=[vmem] * 4,
-        out_specs=vmem,
-        out_shape=shape(*pay_shape, dtype=bf16),
-    )(pay, pay_come, first, first_come)
+    first = first + move(first, across)
+    first_come = move(first, outward)
+
+    (total,) = call(
+        functools.partial(total_kernel, channels, hid_count), "total", 0,
+        [shape(*pay_shape, dtype=bf16)],
+        [vmem] * 2,
+    )(pay, pay_come)
     total_come = move(total, outward)
 
     grad_one, grad_two, grad_value = call(
-        functools.partial(gates_kernel, shards), "gates", 0, 1,
-        in_specs=[smem] + [block_like] * 4 + [strip(1)] + [block_like] * 4,
-        out_specs=[block_like] * 3,
-        out_shape=[shape(rows, channels, dtype=bf16)] * 3,
+        looped(
+            functools.partial(gates_kernel, shards), (None,) + (ROWS,) * 12, blocks, width
+        ),
+        "gates", 0,
+        [block_bf16] * 3,
+        [smem] + [vmem] * 9,
     )(rank, x_one, x_two, values, grad_out, skip_row, conv, corr, late, part_come)
 
+    outs = [shape(hid_count, channels), shape(feat_count, hid_count), shape(1, channels)]
     grad_second, grad_first, grad_bias = call(
-        functools.partial(finish_kernel, channels, shards), "finish", 0, 1,
-        grid=(),
-        in_specs=[smem, vmem, vmem],
-        out_specs=[vmem] * 3,
-        out_shape=[shape(hid_count, channels), shape(feat_count, hid_count), shape(1, channels)],
-    )(rank, total, total_come)
+        functools.partial(finish_kernel, channels, shards), "finish", 0,
+        outs,
+        [smem] + [vmem] * 4,
+        out_specs=[anywhere] * 3,
+        scratch=[pltpu.VMEM(o.shape, f32) for o in outs] + [pltpu.SemaphoreType.DMA((3,))],
+    )(rank, total, total_come, first, first_come)
     return (grad_one, grad_two, grad_value, grad_first, grad_second, grad_bias.reshape(channels))
 
 

time: 86.6 us -> 76.1 us (0.88)
  Pallas kernels: 48.1 us -> 30.5 us
  local copies, waits for them, and re-layouts: 1.2 us -> 6.45 us
  waiting for transfers between devices: 14.4 us -> 17.2 us
    pallas_call x8 -> x9, Pallas kernels: 48.1 us -> 30.5 us  [the longest x1 9.47 us: few_shards_body(): call(looped(functools.partial(near_kernel, rows, shards), (None, ROWS, RO...]
    unnamed x4 -> x40, local copies, waits for them, and re-layouts: 1.2 us -> 6.45 us
    ppermute x8 -> x9, waiting for transfers between devices: 10.8 us -> 13.8 us  [move(): return lax.ppermute(array, 'ctx', pairs)]
    ppermute x8 -> x9, starting transfers between devices: 19.2 us -> 18.7 us  [move(): return lax.ppermute(array, 'ctx', pairs)]
  transfers between devices with their start and end apart: 10 -> 11, of which waited for: 4 -> 5; matrix products, arithmetic and copies ran while one was open for 1% -> 0% of each run, Pallas kernels for 42% -> 33%
where the time goes in v4:
time: 76.1 us; the launch traced here: 75.5 us
  Pallas kernels  30.5 us (40%)
  starting transfers between devices  20.3 us (27%)
  waiting for transfers between devices  17.2 us (23%)
  local copies, waits for them, and re-layouts  6.45 us (8%)
  between operations  0.96 us (1%)
    ppermute x9, starting transfers between devices, move(): return lax.ppermute(array, 'ctx', pairs)  18.7 us
    ppermute x9, waiting for transfers between devices, move(): return lax.ppermute(array, 'ctx', pairs)  13.8 us
    pallas_call x1, Pallas kernels, few_shards_body(): call(looped(functools.partial(near_kernel, rows, shards), (None, ROWS, RO...  9.47 us
    pallas_call x1, Pallas kernels, few_shards_body(): call(looped(functools.partial(filters_kernel, rows, shards), (None, None,...  6.62 us
    unnamed x40, local copies, waits for them, and re-layouts  6.45 us
    pallas_call x1, Pallas kernels, few_shards_body(): call(looped(functools.partial(own_kernel, rows, shards, channels), (ROWS,...  3.77 us
    ppermute x2, waiting for transfers between devices, few_shards_body(): lax.ppermute(first, ('ch', 'sub'), [(i, i ^ bit) for i in range(group)])  3.42 us
    pallas_call x1, Pallas kernels, few_shards_body(): call(looped(functools.partial(far_kernel, rows), (None, ROWS, (slice(2, 4...  2.59 us
  transfers between devices with their start and end apart: 11, of which 5 were waited for; matrix products, arithmetic and copies ran while one was open for 0% of the time, Pallas kernels for 33%

profile of v4, /device:TPU:0, one launch (start us, length us, event | category | flops | bytes accessed | tf_op | source)
XLA Modules:
  0.0 75.5 jit_solution(14606395568530774197)
XLA Ops:
  0.6 2.5 %products.1 = (bf16[128,2048]{1,0:T(8,128)(2,1)}, bf16[128,2048]{1,0:T(8,128)(2,1)}, f32[1,2048]{1,0:T(1,128)}) custom-call(bf16[128,2048]{1,0:T(8,128)(2,1)} %refs_1_.2, bf16[128,2048]{1,0:T(8,128)(2,1)} %refs_2_.5, bf16[128,2048]{1,0:T(8,128)(2,1)} %refs_3_.4, bf16[128,2048]{1,0:T(8,128)(2,1)} %refs_4_.4), custom_call_target="tpu_custom_call" | custom-call | tf_op jit(solution)/shard_map/products/pallas_call | solution.py:636
  3.1 5.1 %collective-permute-start = (bf16[128,2048]{1,0:T(8,128)(2,1)}, bf16[128,2048]{1,0:T(8,128)(2,1)S(1)}, u32[]{:S(2)}, u32[]{:S(2)}) collective-permute-start(bf16[128,2048]{1,0:T(8,128)(2,1)} %get-tuple-element.30.refs_6_.refs_0_.refs_1_), channel_id=1, source_target_pairs={{0,4},{4,8},{8,12},{1,5},{5,9},{9,13},{2,6},{6,10},{10,14},{3,7},{... | collective-permute-start | bytes 1572872 | tf_op jit(solution)/shard_map/ppermute | solution.py:623
  8.2 1.3 %collective-permute-start.1 = (bf16[128,2048]{1,0:T(8,128)(2,1)}, bf16[128,2048]{1,0:T(8,128)(2,1)S(1)}, u32[]{:S(2)}, u32[]{:S(2)}) collective-permute-start(bf16[128,2048]{1,0:T(8,128)(2,1)} %get-tuple-element.31.refs_7_.refs_1_.refs_2_), channel_id=1, source_target_pairs={{4,0},{8,4},{12,8},{5,1},{9,5},{13,9},{6,2},{10,6},{14,10},{7,3},{... | collective-permute-start | bytes 1572872 | tf_op jit(solution)/shard_map/ppermute | solution.py:623
  9.5 0.0 copy-start.4
  9.5 1.0 %copy-done.4 = f32[64,2048]{1,0:T(8,128)S(1)} copy-done((f32[64,2048]{1,0:T(8,128)S(1)}, f32[64,2048]{1,0:T(8,128)}, u32[]{:S(2)}) %copy-start.4) | copy-done | bytes 524312
  10.6 0.0 copy-start.6
  10.6 0.9 %copy-done.6 = bf16[256,256]{1,0:T(8,128)(2,1)S(1)} copy-done((bf16[256,256]{1,0:T(8,128)(2,1)S(1)}, bf16[256,256]{1,0:T(8,128)(2,1)}, u32[]{:S(2)}) %copy-start.6) | copy-done | bytes 131096
  11.5 0.0 copy-start.10
  11.5 0.7 copy-done.10
  12.2 0.0 copy-start.14
  12.2 1.0 %copy-done.14 = bf16[128,2048]{1,0:T(8,128)(2,1)S(1)} copy-done((bf16[128,2048]{1,0:T(8,128)(2,1)S(1)}, bf16[128,2048]{1,0:T(8,128)(2,1)}, u32[]{:S(2)}) %copy-start.14) | copy-done | bytes 524312
  13.2 0.0 copy-start.16
  13.2 1.0 %copy-done.16 = bf16[128,2048]{1,0:T(8,128)(2,1)S(1)} copy-done((bf16[128,2048]{1,0:T(8,128)(2,1)S(1)}, bf16[128,2048]{1,0:T(8,128)(2,1)}, u32[]{:S(2)}) %copy-start.16) | copy-done | bytes 524312
  14.3 0.7 copy-done.18
  15.0 0.9 %copy-done.19 = f32[512,32]{1,0:T(8,128)S(1)} copy-done((f32[512,32]{1,0:T(8,128)S(1)}, f32[512,32]{1,0:T(8,128)}, u32[]{:S(2)}) %copy-start.19) | copy-done | bytes 65560
  15.9 6.6 %filters.1 = (bf16[4,256,2048]{2,1,0:T(8,128)(2,1)S(1)}, bf16[128,512]{1,0:T(8,128)(2,1)S(1)}, f32[512,64]{1,0:T(8,128)S(1)}, bf16[128,2048]{1,0:T(8,128)(2,1)S(1)}) custom-call(s32[1]{0:T(128)} %bitcast.refs_0_.rank_ref, f32[512,32]{1,0:T(8,128)S(1)} %copy-done.19, f32[32,64]{1,0:T(8,128)S(1)} %copy-done.18, f32[64,2048]{1,0:T(8,128)S(1)} %copy-done.4, ...), custom_call_target="tpu_custom_call" | custom-call | flops 2147483648 | bytes 262144 | tf_op jit(solution)/shard_map/filters/pallas_call | solution.py:648
  22.6 0.0 copy-start.11
  22.6 0.0 copy-start.15
  22.6 0.0 copy-start.17
  22.6 5.7 %collective-permute-start.2 = (bf16[128,2048]{1,0:T(8,128)(2,1)S(1)}, bf16[128,2048]{1,0:T(8,128)(2,1)S(1)}, u32[]{:S(2)}, u32[]{:S(2)}) collective-permute-start(bf16[128,2048]{1,0:T(8,128)(2,1)S(1)} %get-tuple-element.39), channel_id=1, source_target_pairs={{0,8},{12,4},{1,9},{13,5},{2,10},{14,6},{3,11},{15,7},{16,24},{28,... | collective-permute-start | bytes 1572872 | tf_op jit(solution)/shard_map/ppermute | solution.py:623
  28.3 0.0 copy-done.13
  28.3 0.0 copy-done.5
  28.3 0.0 copy-done.7
  28.3 0.0 copy-done.8
  28.3 0.0 copy-done.9
  28.3 3.8 %own_pair.1 = (f32[64,2048]{1,0:T(8,128)S(1)}, bf16[64,2304]{1,0:T(8,128)(2,1)S(1)}) custom-call(bf16[128,2048]{1,0:T(8,128)(2,1)S(1)} %copy-done.14, bf16[128,2048]{1,0:T(8,128)(2,1)S(1)} %copy-done.16, f32[64,2048]{1,0:T(8,128)S(1)} %copy-done.5, f32[1,2048]{1,0:T(1,128)S(1)} %bitcast.5, bf16[256,256]{1,0:T(8,128)(2,1)S(1)} %copy-done.7, ...), custom_call_target="tpu_custom_call" | custom-call | flops 2147483648 | bytes 262144 | tf_op jit(solution)/shard_map/own_pair/pallas_call | solution.py:664
  32.1 1.3 %collective-permute-start.4 = (bf16[64,2304]{1,0:T(8,128)(2,1)S(1)}, bf16[64,2304]{1,0:T(8,128)(2,1)S(1)}, u32[]{:S(2)}, u32[]{:S(2)}) collective-permute-start(bf16[64,2304]{1,0:T(8,128)(2,1)S(1)} %get-tuple-element.48.refs_13_), channel_id=1, source_target_pairs={{0,4},{12,8},{1,5},{13,9},{2,6},{14,10},{3,7},{15,11},{16,20},{28,... | collective-permute-start | bytes 884744 | tf_op jit(solution)/shard_map/ppermute | solution.py:623
  33.4 0.0 collective-permute-done.refs_3_.refs_1_
  33.4 0.0 collective-permute-done.1.refs_4_.refs_2_
  33.4 0.0 copy-done.11
  33.5 0.0 copy-done.15
  33.5 0.0 copy-done.17
  33.5 9.5 %near_blocks.1 = (f32[128,2048]{1,0:T(8,128)S(1)}, f32[128,2048]{1,0:T(8,128)S(1)}, f32[128,2048]{1,0:T(8,128)S(1)}, f32[64,2048]{1,0:T(8,128)S(1)}, f32[32,64]{1,0:T(8,128)S(1)}) custom-call(s32[1]{0:T(128)} %bitcast.refs_0_.rank_ref, bf16[128,2048]{1,0:T(8,128)(2,1)S(1)} %copy-done.15, bf16[128,2048]{1,0:T(8,128)(2,1)S(1)} %copy-done.17, ...), custom_call_target="tpu_custom_call" | custom-call | flops 5368709120 | bytes 262144 | tf_op jit(solution)/shard_map/near_blocks/pallas_call | solution.py:677
  43.0 2.3 %collective-permute-done.4.refs_15_ = bf16[64,2304]{1,0:T(8,128)(2,1)S(1)} collective-permute-done((bf16[64,2304]{1,0:T(8,128)(2,1)S(1)}, bf16[64,2304]{1,0:T(8,128)(2,1)S(1)}, u32[]{:S(2)}, u32[]{:S(2)}) %collective-permute-start.4) | collective-permute-done | bytes 294944 | tf_op jit(solution)/shard_map/ppermute | solution.py:623
  45.2 0.0 collective-permute-done.2.refs_1_.refs_3_
  45.2 2.5 %last_pair.1 = (bf16[64,2304]{1,0:T(8,128)(2,1)S(1)}, f32[32,64]{1,0:T(8,128)S(1)}) custom-call(s32[1]{0:T(128)} %bitcast.refs_0_.rank_ref, bf16[128,2048]{1,0:T(8,128)(2,1)S(1)} %collective-permute-done.refs_3_.refs_1_, bf16[128,2048]{1,0:T(8,128)(2,1)S(1)} %collective-permute-done.1.refs_4_.refs_2_, ...), custom_call_target="tpu_custom_call" | custom-call | flops 268435456 | bytes 262144 | tf_op jit(solution)/shard_map/last_pair/pallas_call | solution.py:707
  47.8 0.0 copy-start
  47.8 0.0 copy-start.1
  47.8 0.0 copy-start.2
  47.8 0.0 copy-start.3
  47.8 0.0 copy-start.12
  47.8 0.8 %collective-permute-start.5 = (bf16[64,2304]{1,0:T(8,128)(2,1)S(1)}, bf16[64,2304]{1,0:T(8,128)(2,1)S(1)}, u32[]{:S(2)}, u32[]{:S(2)}) collective-permute-start(bf16[64,2304]{1,0:T(8,128)(2,1)S(1)} %get-tuple-element.49.own_ref), channel_id=1, source_target_pairs={{4,8},{8,4},{5,9},{9,5},{6,10},{10,6},{7,11},{11,7},{20,24},{24,20... | collective-permute-start | bytes 884744 | tf_op jit(solution)/shard_map/ppermute | solution.py:623
  48.6 2.6 %far_block.1 = (bf16[128,2048]{1,0:T(8,128)(2,1)S(1)}, f32[128,2048]{1,0:T(8,128)S(1)}) custom-call(s32[1]{0:T(128)} %bitcast.refs_0_.rank_ref, bf16[128,2048]{1,0:T(8,128)(2,1)S(1)} %collective-permute-done.2.refs_1_.refs_3_, bf16[4,256,2048]{2,1,0:T(8,128)(2,1)S(1)} %get-tuple-element.32.refs_5_.refs_2_, bf16[256,256]{1,0:T(8,128)(2,1)S(1)} %copy-done.7, ...), custom_call_target="tpu_custom_call" | custom-call | flops 268435456 | bytes 262144 | tf_op jit(solution)/shard_map/far_block/pallas_call | solution.py:695
  51.2 1.3 %collective-permute-start.3 = (bf16[128,2048]{1,0:T(8,128)(2,1)S(1)}, bf16[128,2048]{1,0:T(8,128)(2,1)S(1)}, u32[]{:S(2)}, u32[]{:S(2)}) collective-permute-start(bf16[128,2048]{1,0:T(8,128)(2,1)S(1)} %get-tuple-element.42), channel_id=1, source_target_pairs={{4,0},{8,12},{5,1},{9,13},{6,2},{10,14},{7,3},{11,15},{20,16},{24,... | collective-permute-start | bytes 1572872 | tf_op jit(solution)/shard_map/ppermute | solution.py:623
  52.5 0.0 collective-permute-done.5.come_ref
  52.5 0.1 total.1.own_ref
  52.6 1.3 %collective-permute-start.6 = (bf16[64,2304]{1,0:T(8,128)(2,1)S(1)}, bf16[64,2304]{1,0:T(8,128)(2,1)S(1)}, u32[]{:S(2)}, u32[]{:S(2)}) collective-permute-start(bf16[64,2304]{1,0:T(8,128)(2,1)S(1)} %total.1.own_ref), channel_id=1, source_target_pairs={{4,0},{8,12},{5,1},{9,13},{6,2},{10,14},{7,3},{11,15},{20,16},{24,... | collective-permute-start | bytes 884744 | tf_op jit(solution)/shard_map/ppermute | solution.py:623
  53.9 0.1 collective-permute-start.7
  54.0 1.2 %collective-permute-done.7 = f32[32,64]{1,0:T(8,128)S(1)} collective-permute-done((f32[32,64]{1,0:T(8,128)S(1)}, f32[32,64]{1,0:T(8,128)S(1)}, u32[]{:S(2)}, u32[]{:S(2)}) %collective-permute-start.7) | collective-permute-done | bytes 8224 | tf_op jit(solution)/shard_map/ppermute | solution.py:722
  55.2 1.5 %collective-permute-start.8 = (f32[32,64]{1,0:T(8,128)S(1)}, f32[32,64]{1,0:T(8,128)S(1)}, u32[]{:S(2)}, u32[]{:S(2)}) collective-permute-start(f32[32,64]{1,0:T(8,128)S(1)} %add.9), channel_id=1, source_target_pairs={{0,2},{1,3},{2,0},{3,1},{4,6},{5,7},{6,4},{7,5},{8,10},{9,11},{10,... | collective-permute-start | bytes 24584 | tf_op jit(solution)/shard_map/ppermute | solution.py:722
  56.7 2.2 %collective-permute-done.8 = f32[32,64]{1,0:T(8,128)S(1)} collective-permute-done((f32[32,64]{1,0:T(8,128)S(1)}, f32[32,64]{1,0:T(8,128)S(1)}, u32[]{:S(2)}, u32[]{:S(2)}) %collective-permute-start.8) | collective-permute-done | bytes 8224 | tf_op jit(solution)/shard_map/ppermute | solution.py:722
  58.9 0.7 collective-permute-start.9
  59.6 0.0 collective-permute-done.9
  59.6 1.3 %collective-permute-start.10 = (f32[32,64]{1,0:T(8,128)S(1)}, f32[32,64]{1,0:T(8,128)S(1)}, u32[]{:S(2)}, u32[]{:S(2)}) collective-permute-start(f32[32,64]{1,0:T(8,128)S(1)} %add.11.first_ref), channel_id=1, source_target_pairs={{4,0},{8,12},{5,1},{9,13},{6,2},{10,14},{7,3},{11,15},{20,16},{24,... | collective-permute-start | bytes 24584 | tf_op jit(solution)/shard_map/ppermute | solution.py:623
  60.9 8.6 %collective-permute-done.3.refs_9_ = bf16[128,2048]{1,0:T(8,128)(2,1)S(1)} collective-permute-done((bf16[128,2048]{1,0:T(8,128)(2,1)S(1)}, bf16[128,2048]{1,0:T(8,128)(2,1)S(1)}, u32[]{:S(2)}, u32[]{:S(2)}) %collective-permute-start.3) | collective-permute-done | bytes 524320 | tf_op jit(solution)/shard_map/ppermute | solution.py:623
  69.5 0.0 copy-done
  69.5 0.0 copy-done.1
  69.5 0.0 copy-done.2
  69.6 0.0 copy-done.3
  69.6 0.0 copy-done.12
  69.6 2.1 %gates.1 = (bf16[128,2048]{1,0:T(8,128)(2,1)}, bf16[128,2048]{1,0:T(8,128)(2,1)}, bf16[128,2048]{1,0:T(8,128)(2,1)}) custom-call(s32[1]{0:T(128)} %bitcast.refs_0_.rank_ref, bf16[128,2048]{1,0:T(8,128)(2,1)S(1)} %copy-done, bf16[128,2048]{1,0:T(8,128)(2,1)S(1)} %copy-done.1, bf16[128,2048]{1,0:T(8,128)(2,1)S(1)} %copy-done.2, ...), custom_call_target="tpu_custom_call" | custom-call | bytes 262144 | tf_op jit(solution)/shard_map/gates/pallas_call | solution.py:734
  71.7 2.9 %collective-permute-done.10.first_come_ref = f32[32,64]{1,0:T(8,128)S(1)} collective-permute-done((f32[32,64]{1,0:T(8,128)S(1)}, f32[32,64]{1,0:T(8,128)S(1)}, u32[]{:S(2)}, u32[]{:S(2)}) %collective-permute-start.10) | collective-permute-done | bytes 8224 | tf_op jit(solution)/shard_map/ppermute | solution.py:623
  74.6 0.0 collective-permute-done.6.come_ref
  74.6 0.9 %finish.1 = (f32[64,2048]{1,0:T(8,128)}, f32[32,64]{1,0:T(8,128)}, f32[1,2048]{1,0:T(1,128)}) custom-call(s32[1]{0:T(128)} %bitcast.refs_0_.rank_ref, bf16[64,2304]{1,0:T(8,128)(2,1)S(1)} %total.1.own_ref, bf16[64,2304]{1,0:T(8,128)(2,1)S(1)} %collective-permute-done.6.come_ref, f32[32,64]{1,0:T(8,128)S(1)} %add.11.first_ref, ...), custom_call_target="tpu_custom_call" | custom-call | bytes 262144 | tf_op jit(solution)/shard_map/finish/pallas_call | solution.py:744
  (10 shorter events, 0.0 us)
Async XLA Ops:
  3.1 25.2 %copy-start.13 = (f32[1,2048]{1,0:T(1,128)S(1)}, f32[1,2048]{1,0:T(1,128)}, u32[]{:S(2)}) copy-start(f32[1,2048]{1,0:T(1,128)} %get-tuple-element.35.refs_9_.refs_14_) | copy-start | bytes 24580
  3.1 30.3 %collective-permute-start = (bf16[128,2048]{1,0:T(8,128)(2,1)}, bf16[128,2048]{1,0:T(8,128)(2,1)S(1)}, u32[]{:S(2)}, u32[]{:S(2)}) collective-permute-start(bf16[128,2048]{1,0:T(8,128)(2,1)} %get-tuple-element.30.refs_6_.refs_0_.refs_1_), channel_id=1, source_target_pairs={{0,4},{4,8},{8,12},{1,5},{5,9},{9,13},{2,6},{6,10},{10,14},{3,7},{... | collective-permute-start | bytes 1572872 | tf_op jit(solution)/shard_map/ppermute | solution.py:623
  8.2 25.2 %collective-permute-start.1 = (bf16[128,2048]{1,0:T(8,128)(2,1)}, bf16[128,2048]{1,0:T(8,128)(2,1)S(1)}, u32[]{:S(2)}, u32[]{:S(2)}) collective-permute-start(bf16[128,2048]{1,0:T(8,128)(2,1)} %get-tuple-element.31.refs_7_.refs_1_.refs_2_), channel_id=1, source_target_pairs={{4,0},{8,4},{12,8},{5,1},{9,5},{13,9},{6,2},{10,6},{14,10},{7,3},{... | collective-permute-start | bytes 1572872 | tf_op jit(solution)/shard_map/ppermute | solution.py:623
  9.5 1.0 %copy-start.4 = (f32[64,2048]{1,0:T(8,128)S(1)}, f32[64,2048]{1,0:T(8,128)}, u32[]{:S(2)}) copy-start(f32[64,2048]{1,0:T(8,128)} %refs_4_.5) | copy-start | bytes 1572868
  10.6 0.9 %copy-start.6 = (bf16[256,256]{1,0:T(8,128)(2,1)S(1)}, bf16[256,256]{1,0:T(8,128)(2,1)}, u32[]{:S(2)}) copy-start(bf16[256,256]{1,0:T(8,128)(2,1)} %constant.14.clone.refs_5_.refs_4_.refs_8_.refs_3_.refs_6_) | copy-start | bytes 393220
  11.5 0.7 copy-start.10
  12.2 1.0 %copy-start.14 = (bf16[128,2048]{1,0:T(8,128)(2,1)S(1)}, bf16[128,2048]{1,0:T(8,128)(2,1)}, u32[]{:S(2)}) copy-start(bf16[128,2048]{1,0:T(8,128)(2,1)} %get-tuple-element.30.refs_6_.refs_0_.refs_1_) | copy-start | bytes 1572868
  13.2 1.0 %copy-start.16 = (bf16[128,2048]{1,0:T(8,128)(2,1)S(1)}, bf16[128,2048]{1,0:T(8,128)(2,1)}, u32[]{:S(2)}) copy-start(bf16[128,2048]{1,0:T(8,128)(2,1)} %get-tuple-element.31.refs_7_.refs_1_.refs_2_) | copy-start | bytes 1572868
  14.3 0.7 copy-start.18
  15.0 0.9 %copy-start.19 = (f32[512,32]{1,0:T(8,128)S(1)}, f32[512,32]{1,0:T(8,128)}, u32[]{:S(2)}) copy-start(f32[512,32]{1,0:T(8,128)} %constant.13.clone.refs_1_) | copy-start | bytes 196612
  15.9 12.4 %copy-start.5 = (f32[64,2048]{1,0:T(8,128)S(1)}, f32[64,2048]{1,0:T(8,128)}, u32[]{:S(2)}) copy-start(f32[64,2048]{1,0:T(8,128)} %refs_4_.5) | copy-start | bytes 1572868
  15.9 12.4 %copy-start.7 = (bf16[256,256]{1,0:T(8,128)(2,1)S(1)}, bf16[256,256]{1,0:T(8,128)(2,1)}, u32[]{:S(2)}) copy-start(bf16[256,256]{1,0:T(8,128)(2,1)} %constant.14.clone.refs_5_.refs_4_.refs_8_.refs_3_.refs_6_) | copy-start | bytes 393220
  15.9 12.4 %copy-start.8 = (bf16[256,256]{1,0:T(8,128)(2,1)S(1)}, bf16[256,256]{1,0:T(8,128)(2,1)}, u32[]{:S(2)}) copy-start(bf16[256,256]{1,0:T(8,128)(2,1)} %constant.15.clone.refs_5_.refs_9_.refs_4_.refs_7_) | copy-start | bytes 393220
  15.9 12.4 %copy-start.9 = (f32[32,512]{1,0:T(8,128)S(1)}, f32[32,512]{1,0:T(8,128)}, u32[]{:S(2)}) copy-start(f32[32,512]{1,0:T(8,128)} %constant.16.clone.refs_8_.refs_11_.refs_9_) | copy-start | bytes 196612
  22.6 10.9 %copy-start.11 = (f32[2048]{0:T(1024)S(1)}, f32[2048]{0:T(1024)}, u32[]{:S(2)}) copy-start(f32[2048]{0:T(1024)} %param.19) | copy-start | bytes 24580
  22.6 10.9 %copy-start.15 = (bf16[128,2048]{1,0:T(8,128)(2,1)S(1)}, bf16[128,2048]{1,0:T(8,128)(2,1)}, u32[]{:S(2)}) copy-start(bf16[128,2048]{1,0:T(8,128)(2,1)} %get-tuple-element.30.refs_6_.refs_0_.refs_1_) | copy-start | bytes 1572868
  22.6 10.9 %copy-start.17 = (bf16[128,2048]{1,0:T(8,128)(2,1)S(1)}, bf16[128,2048]{1,0:T(8,128)(2,1)}, u32[]{:S(2)}) copy-start(bf16[128,2048]{1,0:T(8,128)(2,1)} %get-tuple-element.31.refs_7_.refs_1_.refs_2_) | copy-start | bytes 1572868
  22.6 22.6 %collective-permute-start.2 = (bf16[128,2048]{1,0:T(8,128)(2,1)S(1)}, bf16[128,2048]{1,0:T(8,128)(2,1)S(1)}, u32[]{:S(2)}, u32[]{:S(2)}) collective-permute-start(bf16[128,2048]{1,0:T(8,128)(2,1)S(1)} %get-tuple-element.39), channel_id=1, source_target_pairs={{0,8},{12,4},{1,9},{13,5},{2,10},{14,6},{3,11},{15,7},{16,24},{28,... | collective-permute-start | bytes 1572872 | tf_op jit(solution)/shard_map/ppermute | solution.py:623
  32.1 13.1 %collective-permute-start.4 = (bf16[64,2304]{1,0:T(8,128)(2,1)S(1)}, bf16[64,2304]{1,0:T(8,128)(2,1)S(1)}, u32[]{:S(2)}, u32[]{:S(2)}) collective-permute-start(bf16[64,2304]{1,0:T(8,128)(2,1)S(1)} %get-tuple-element.48.refs_13_), channel_id=1, source_target_pairs={{0,4},{12,8},{1,5},{13,9},{2,6},{14,10},{3,7},{15,11},{16,20},{28,... | collective-permute-start | bytes 884744 | tf_op jit(solution)/shard_map/ppermute | solution.py:623
  47.8 21.8 %copy-start = (bf16[128,2048]{1,0:T(8,128)(2,1)S(1)}, bf16[128,2048]{1,0:T(8,128)(2,1)}, u32[]{:S(2)}) copy-start(bf16[128,2048]{1,0:T(8,128)(2,1)} %refs_1_.2) | copy-start | bytes 1572868
  47.8 21.8 %copy-start.1 = (bf16[128,2048]{1,0:T(8,128)(2,1)S(1)}, bf16[128,2048]{1,0:T(8,128)(2,1)}, u32[]{:S(2)}) copy-start(bf16[128,2048]{1,0:T(8,128)(2,1)} %refs_2_.5) | copy-start | bytes 1572868
  47.8 21.8 %copy-start.2 = (bf16[128,2048]{1,0:T(8,128)(2,1)S(1)}, bf16[128,2048]{1,0:T(8,128)(2,1)}, u32[]{:S(2)}) copy-start(bf16[128,2048]{1,0:T(8,128)(2,1)} %refs_3_.4) | copy-start | bytes 1572868
  47.8 21.8 %copy-start.3 = (bf16[128,2048]{1,0:T(8,128)(2,1)S(1)}, bf16[128,2048]{1,0:T(8,128)(2,1)}, u32[]{:S(2)}) copy-start(bf16[128,2048]{1,0:T(8,128)(2,1)} %refs_4_.4) | copy-start | bytes 1572868
  47.8 21.8 %copy-start.12 = (f32[2048]{0:T(1024)S(1)}, f32[2048]{0:T(1024)}, u32[]{:S(2)}) copy-start(f32[2048]{0:T(1024)} %param.18) | copy-start | bytes 24580
  47.8 4.7 %collective-permute-start.5 = (bf16[64,2304]{1,0:T(8,128)(2,1)S(1)}, bf16[64,2304]{1,0:T(8,128)(2,1)S(1)}, u32[]{:S(2)}, u32[]{:S(2)}) collective-permute-start(bf16[64,2304]{1,0:T(8,128)(2,1)S(1)} %get-tuple-element.49.own_ref), channel_id=1, source_target_pairs={{4,8},{8,4},{5,9},{9,5},{6,10},{10,6},{7,11},{11,7},{20,24},{24,20... | collective-permute-start | bytes 884744 | tf_op jit(solution)/shard_map/ppermute | solution.py:623
  51.2 18.3 %collective-permute-start.3 = (bf16[128,2048]{1,0:T(8,128)(2,1)S(1)}, bf16[128,2048]{1,0:T(8,128)(2,1)S(1)}, u32[]{:S(2)}, u32[]{:S(2)}) collective-permute-start(bf16[128,2048]{1,0:T(8,128)(2,1)S(1)} %get-tuple-element.42), channel_id=1, source_target_pairs={{4,0},{8,12},{5,1},{9,13},{6,2},{10,14},{7,3},{11,15},{20,16},{24,... | collective-permute-start | bytes 1572872 | tf_op jit(solution)/shard_map/ppermute | solution.py:623
  52.6 22.0 %collective-permute-start.6 = (bf16[64,2304]{1,0:T(8,128)(2,1)S(1)}, bf16[64,2304]{1,0:T(8,128)(2,1)S(1)}, u32[]{:S(2)}, u32[]{:S(2)}) collective-permute-start(bf16[64,2304]{1,0:T(8,128)(2,1)S(1)} %total.1.own_ref), channel_id=1, source_target_pairs={{4,0},{8,12},{5,1},{9,13},{6,2},{10,14},{7,3},{11,15},{20,16},{24,... | collective-permute-start | bytes 884744 | tf_op jit(solution)/shard_map/ppermute | solution.py:623
  53.9 1.2 %collective-permute-start.7 = (f32[32,64]{1,0:T(8,128)S(1)}, f32[32,64]{1,0:T(8,128)S(1)}, u32[]{:S(2)}, u32[]{:S(2)}) collective-permute-start(f32[32,64]{1,0:T(8,128)S(1)} %get-tuple-element.50), channel_id=1, source_target_pairs={{0,1},{1,0},{2,3},{3,2},{4,5},{5,4},{6,7},{7,6},{8,9},{9,8},{10,11... | collective-permute-start | bytes 24584 | tf_op jit(solution)/shard_map/ppermute | solution.py:722
  55.2 3.7 %collective-permute-start.8 = (f32[32,64]{1,0:T(8,128)S(1)}, f32[32,64]{1,0:T(8,128)S(1)}, u32[]{:S(2)}, u32[]{:S(2)}) collective-permute-start(f32[32,64]{1,0:T(8,128)S(1)} %add.9), channel_id=1, source_target_pairs={{0,2},{1,3},{2,0},{3,1},{4,6},{5,7},{6,4},{7,5},{8,10},{9,11},{10,... | collective-permute-start | bytes 24584 | tf_op jit(solution)/shard_map/ppermute | solution.py:722
  58.9 0.7 collective-permute-start.9
  59.6 15.0 %collective-permute-start.10 = (f32[32,64]{1,0:T(8,128)S(1)}, f32[32,64]{1,0:T(8,128)S(1)}, u32[]{:S(2)}, u32[]{:S(2)}) collective-permute-start(f32[32,64]{1,0:T(8,128)S(1)} %add.11.first_ref), channel_id=1, source_target_pairs={{4,0},{8,12},{5,1},{9,13},{6,2},{10,14},{7,3},{11,15},{20,16},{24,... | collective-permute-start | bytes 24584 | tf_op jit(solution)/shard_map/ppermute | solution.py:623

commit v5 on v4

--- a/solution.py
+++ b/solution.py
@@ -292,11 +292,12 @@
 CUBE = (slice(None), slice(None))
 
 
-def products_kernel(one_ref, two_ref, val_ref, out_ref, source_ref, cotan_ref, bias_ref):
+def products_kernel(rank_ref, one_ref, two_ref, val_ref, out_ref, source_ref, cotan_ref, edge_ref, bias_ref):
     source = one_ref[...].astype(f32) * val_ref[...].astype(f32)
     cotan = out_ref[...].astype(f32) * two_ref[...].astype(f32)
     source_ref[...] = source.astype(bf16)
     cotan_ref[...] = cotan.astype(bf16)
+    edge_ref[...] = jnp.where(rank_ref[0] == 0, source, cotan).astype(bf16)
     part = jnp.sum(source * cotan, axis=0, keepdims=True)
 
     @pl.when(pl.program_id(0) == 0)
@@ -325,24 +326,33 @@
     return jnp.where(odd, cosine, sine) * sin_sign, jnp.where(odd, sine, cosine) * cos_sign
 
 
-def filters_kernel(
-    rows, shards, block, blocks, rank_ref, feats_ref, first_ref, weight_ref, rate_ref, front_ref, source_ref, cotan_ref,
-    spec_ref, trans_ref, slope_ref, edge_ref, hid_ref,
-):
+def filters_kernel(rows, shards, blocks, width, *refs):
+    inputs, passed, outputs, held, (hid_ref, sems) = refs[:5], refs[5:6], refs[6:10], refs[10:15], refs[15:]
+    del passed
+    feats_ref, first_ref, weight_ref, rate_ref, front_ref = held
+    spec_ref, trans_ref, slope_ref, _ = outputs
+    copies = [pltpu.make_async_copy(far, near, sems.at[i]) for i, (far, near) in enumerate(zip(inputs, held))]
+    for copy in copies:
+        copy.start()
     hid_count = first_ref.shape[1]
+    copies[0].wait()
+    copies[1].wait()
+    hidden, slope = sin_cos(exact_dot(feats_ref[...], first_ref[...]))
+    slope_ref[...] = slope
+    high, low = split(hidden)
+    hid_ref[...] = jnp.concatenate([high, high, low], axis=1)
+    turned_over = jnp.concatenate([hidden, slope], axis=1).T[:hid_count]
+    trans_ref[...] = jnp.concatenate(split(turned_over), axis=0)
+    for copy in copies[2:]:
+        copy.wait()
+    strips = looped(
+        functools.partial(filter_strip, rows, shards), (None, ROWS, ROWS, None, CUBE), blocks, width
+    )
+    strips(hid_ref, weight_ref, rate_ref, front_ref, spec_ref)
+
+
+def filter_strip(rows, shards, block, blocks, hid_ref, weight_ref, rate_ref, front_ref, spec_ref):
     scale = float(rows * shards) ** -0.5
-
-    @pl.when(block == 0)
-    def _():
-        pre_act = exact_dot(feats_ref[...], first_ref[...])
-        hidden, slope = sin_cos(pre_act)
-        slope_ref[...] = slope
-        high, low = split(hidden)
-        hid_ref[...] = jnp.concatenate([high, high, low], axis=1)
-        turned_over = jnp.concatenate([hidden, slope], axis=1).T[:hid_count]
-        trans_ref[...] = jnp.concatenate(split(turned_over), axis=0)
-
-    edge_ref[...] = jnp.where(rank_ref[0] == 0, source_ref[...], cotan_ref[...])
     w_high, w_low = split(weight_ref[...])
     stacked = jnp.concatenate([w_high, w_low, w_high], axis=0)
     rate = rate_ref[...]
@@ -475,9 +485,10 @@
 
 
 def last_kernel(
-    rows, shards, channels, block, blocks, rank_ref, x1_ref, c1_ref, far_ref, weight_ref, rate_ref, front_ref, back_ref,
+    rows, shards, channels, block, blocks, after_ref, rank_ref, x1_ref, c1_ref, far_ref, weight_ref, rate_ref, front_ref, back_ref,
     trans_ref, featt_ref, slope_ref, sums_ref, first_ref, own_ref, bias_ref, in_ref, pay_ref, total_ref, acc_ref,
 ):
+    del after_ref
     hid_count, width = weight_ref.shape
     lower = rank_ref[0] == 1
     start = pl.multiple_of(block * width, width)
@@ -527,7 +538,8 @@
         total_ref[...] = first
 
 
-def total_kernel(channels, hid_count, own_ref, come_ref, pay_ref):
+def total_kernel(channels, hid_count, part_ref, first_ref, own_ref, come_ref, pay_ref):
+    del part_ref, first_ref
     lanes = channels // 128
     pay_ref[:, :channels] = (own_ref[:, :channels].astype(f32) + come_ref[:, :channels].astype(f32)).astype(bf16)
     own, come = (get_side(ref[...], channels, lanes, hid_count)[0] for ref in (own_ref, come_ref))
@@ -605,13 +617,14 @@
     def shape(*dims, dtype=f32):
         return jax.ShapeDtypeStruct(dims, dtype)
 
-    def call(kernel, name, units, out_shape, in_specs, out_specs=None, scratch=(), limit=16):
+    def call(kernel, name, units, out_shape, in_specs, out_specs=None, scratch=(), limit=16, aliases={}):
         return pl.pallas_call(
             kernel,
             in_specs=in_specs,
             out_specs=out_specs if out_specs is not None else [vmem] * len(out_shape),
             out_shape=out_shape,
             scratch_shapes=scratch,
+            input_output_aliases=aliases,
             compiler_params=pltpu.CompilerParams(vmem_limit_bytes=limit * mebi),
             cost_estimate=pl.CostEstimate(
                 flops=2 * units * double * double * channels, bytes_accessed=rows * channels, transcendentals=0
@@ -633,32 +646,33 @@
 
     row_step = max(rows // 2, 16)
     gate_rows = pl.BlockSpec((row_step, channels), lambda i: (i, 0))
-    x0, c0, bias = pl.pallas_call(
+    x0, c0, edge, bias = pl.pallas_call(
         products_kernel,
         grid=(rows // row_step,),
-        in_specs=[gate_rows] * 4,
-        out_specs=[gate_rows] * 2 + [pl.BlockSpec((1, channels), lambda i: (0, 0))],
-        out_shape=[block_bf16] * 2 + [shape(1, channels)],
+        in_specs=[smem] + [gate_rows] * 4,
+        out_specs=[gate_rows] * 3 + [pl.BlockSpec((1, channels), lambda i: (0, 0))],
+        out_shape=[block_bf16] * 3 + [shape(1, channels)],
         compiler_params=pltpu.CompilerParams(vmem_limit_bytes=64 * mebi),
         name="products",
-    )(x_one, x_two, values, grad_out)
+    )(rank, x_one, x_two, values, grad_out)
     x1 = move(x0, up)
     c1 = move(c0, down)
 
     spec, trans, slope, edge = call(
-        looped(
-            functools.partial(filters_kernel, rows, shards),
-            (None, None, None, ROWS, ROWS, None, ROWS, ROWS, CUBE, None, None, ROWS),
-            blocks, width,
-        ),
-        "filters", 8,
+        functools.partial(filters_kernel, rows, shards, blocks, width), "filters", 8,
         [
             shape(shards, double, channels, dtype=bf16), shape(2 * hid_count, seq_len, dtype=bf16),
             shape(seq_len, hid_count), block_bf16,
         ],
-        [smem] + [vmem] * 7,
-        scratch=[pltpu.VMEM((seq_len, 3 * hid_count), bf16)],
-    )(rank, feats, first_weight, second_weight, rate_row, front, x0, c0)
+        [pl.BlockSpec(memory_space=pltpu.HBM)] * 6,
+        out_specs=[vmem] * 3 + [pl.BlockSpec(memory_space=pltpu.HBM)],
+        scratch=[
+            pltpu.VMEM((seq_len, feat_count), f32), pltpu.VMEM((feat_count, hid_count), f32),
+            pltpu.VMEM((hid_count, channels), f32), pltpu.VMEM((1, channels), f32), pltpu.VMEM((double, double), bf16),
+            pltpu.VMEM((seq_len, 3 * hid_count), bf16), pltpu.SemaphoreType.DMA((5,)),
+        ],
+        aliases={5: 3},
+    )(feats, first_weight, second_weight, rate_row, front, edge)
     far = move(edge, [(0, 2), (shards - 1, shards - 3)])
 
     own, send = call(
@@ -707,29 +721,29 @@
     pay, first = call(
         looped(
             functools.partial(last_kernel, rows, shards, channels),
-            (None, ROWS, ROWS, ROWS, ROWS, ROWS, None, None, None, None, None, ROWS),
+            (None, None, ROWS, ROWS, ROWS, ROWS, ROWS, None, None, None, None, None, ROWS),
             blocks, width,
         ),
         "last_pair", 1,
         [shape(*pay_shape, dtype=bf16), shape(feat_count, hid_count)],
-        [smem] + [vmem] * 15,
+        [anywhere, smem] + [vmem] * 15,
         scratch=[pltpu.VMEM((2 * rows, hid_count), f32)],
-    )(rank, x1, c1, far, second_weight, rate_row, front, back, trans, featt, slope, sums, first, send, bias, come)
+    )(late, rank, x1, c1, far, second_weight, rate_row, front, back, trans, featt, slope, sums, first, send, bias, come)
     pay_come = move(pay, across)
     group = lax.axis_size(("ch", "sub"))
     bit = 1
     while bit < group:
         first = first + lax.ppermute(first, ("ch", "sub"), [(i, i ^ bit) for i in range(group)])
         bit *= 2
-    first = first + move(first, across)
-    first_come = move(first, outward)
 
     (total,) = call(
         functools.partial(total_kernel, channels, hid_count), "total", 0,
         [shape(*pay_shape, dtype=bf16)],
-        [vmem] * 2,
-    )(pay, pay_come)
+        [anywhere] * 2 + [vmem] * 2,
+    )(part_come, first, pay, pay_come)
     total_come = move(total, outward)
+    first = first + move(first, across)
+    first_come = move(first, outward)
 
     grad_one, grad_two, grad_value = call(
         looped(

time: 76.1 us -> 72.4 us (0.951)
  local copies, waits for them, and re-layouts: 6.45 us -> 4.37 us
  waiting for transfers between devices: 17.2 us -> 15.6 us
    unnamed x40 -> x34, local copies, waits for them, and re-layouts: 6.45 us -> 4.37 us
    ppermute x9, waiting for transfers between devices: 13.8 us -> 12.2 us  [move(): return lax.ppermute(array, 'ctx', pairs)]
  transfers between devices with their start and end apart: 11 -> 11, of which waited for: 5 -> 4; matrix products, arithmetic and copies ran while one was open for 0% -> 0% of each run, Pallas kernels for 33% -> 38%
where the time goes in v5:
time: 72.4 us; the launch traced here: 71.9 us
  Pallas kernels  30.8 us (43%)
  starting transfers between devices  20.1 us (28%)
  waiting for transfers between devices  15.6 us (22%)
  local copies, waits for them, and re-layouts  4.37 us (6%)
  between operations  0.98 us (1%)
    ppermute x9, starting transfers between devices, move(): return lax.ppermute(array, 'ctx', pairs)  18.5 us
    ppermute x9, waiting for transfers between devices, move(): return lax.ppermute(array, 'ctx', pairs)  12.2 us
    pallas_call x1, Pallas kernels, few_shards_body(): call(looped(functools.partial(near_kernel, rows, shards), (None, ROWS, RO...  9.38 us
    pallas_call x1, Pallas kernels, few_shards_body(): call(functools.partial(filters_kernel, rows, shards, blocks, width), 'fil...  6.84 us
    unnamed x34, local copies, waits for them, and re-layouts  4.37 us
    pallas_call x1, Pallas kernels, few_shards_body(): call(looped(functools.partial(own_kernel, rows, shards, channels), (ROWS,...  3.77 us
    ppermute x2, waiting for transfers between devices, few_shards_body(): lax.ppermute(first, ('ch', 'sub'), [(i, i ^ bit) for i in range(group)])  3.39 us
    pallas_call x1, Pallas kernels, few_shards_body(): pl.pallas_call(products_kernel, grid=(rows // row_step,), in_specs=[smem]...  2.62 us
  transfers between devices with their start and end apart: 11, of which 4 were waited for; matrix products, arithmetic and copies ran while one was open for 0% of the time, Pallas kernels for 38%

profile of v5, /device:TPU:0, one launch (start us, length us, event | category | flops | bytes accessed | tf_op | source)
XLA Modules:
  0.0 71.9 jit_solution(12856649275802409062)
XLA Ops:
  0.6 2.6 %products.1 = (bf16[128,2048]{1,0:T(8,128)(2,1)}, bf16[128,2048]{1,0:T(8,128)(2,1)}, bf16[128,2048]{1,0:T(8,128)(2,1)}, f32[1,2048]{1,0:T(1,128)}) custom-call(s32[1]{0:T(128)} %bitcast.rank_ref.refs_0_.refs_1_, bf16[128,2048]{1,0:T(8,128)(2,1)} %refs_1_.3, bf16[128,2048]{1,0:T(8,128)(2,1)} %refs_2_.5, bf16[128,2048]{1,0:T(8,128)(2,1)} %refs_3_.2, ...), custom_call_target="tpu_custom_call" | custom-call | tf_op jit(solution)/shard_map/products/pallas_call | solution.py:649
  3.3 5.0 %collective-permute-start = (bf16[128,2048]{1,0:T(8,128)(2,1)}, bf16[128,2048]{1,0:T(8,128)(2,1)S(1)}, u32[]{:S(2)}, u32[]{:S(2)}) collective-permute-start(bf16[128,2048]{1,0:T(8,128)(2,1)} %get-tuple-element.31.refs_0_.refs_1_), channel_id=1, source_target_pairs={{0,4},{4,8},{8,12},{1,5},{5,9},{9,13},{2,6},{6,10},{10,14},{3,7},{... | collective-permute-start | bytes 1572872 | tf_op jit(solution)/shard_map/ppermute | solution.py:636
  8.2 1.3 %collective-permute-start.1 = (bf16[128,2048]{1,0:T(8,128)(2,1)}, bf16[128,2048]{1,0:T(8,128)(2,1)S(1)}, u32[]{:S(2)}, u32[]{:S(2)}) collective-permute-start(bf16[128,2048]{1,0:T(8,128)(2,1)} %get-tuple-element.32.refs_1_.refs_2_), channel_id=1, source_target_pairs={{4,0},{8,4},{12,8},{5,1},{9,5},{13,9},{6,2},{10,6},{14,10},{7,3},{... | collective-permute-start | bytes 1572872 | tf_op jit(solution)/shard_map/ppermute | solution.py:636
  9.5 0.0 copy-start.4
  9.5 1.0 %copy-done.4 = f32[64,2048]{1,0:T(8,128)S(1)} copy-done((f32[64,2048]{1,0:T(8,128)S(1)}, f32[64,2048]{1,0:T(8,128)}, u32[]{:S(2)}) %copy-start.4) | copy-done | bytes 524312
  10.6 0.0 copy-start.6
  10.6 0.9 %copy-done.6 = bf16[256,256]{1,0:T(8,128)(2,1)S(1)} copy-done((bf16[256,256]{1,0:T(8,128)(2,1)S(1)}, bf16[256,256]{1,0:T(8,128)(2,1)}, u32[]{:S(2)}) %copy-start.6) | copy-done | bytes 131096
  11.5 0.0 copy-start.10
  11.5 0.7 copy-done.10
  12.2 0.0 copy-start.15
  12.2 0.7 copy-done.15
  12.9 0.0 copy-start.16
  12.9 0.9 %copy-done.16 = f32[512,32]{1,0:T(8,128)S(1)} copy-done((f32[512,32]{1,0:T(8,128)S(1)}, f32[512,32]{1,0:T(8,128)}, u32[]{:S(2)}) %copy-start.16) | copy-done | bytes 65560
  13.8 0.0 copy-start.5
  13.8 0.0 copy-start.7
  13.8 0.0 copy-start.8
  13.8 0.0 copy-start.12
  13.9 0.0 copy-start.13
  13.9 0.0 copy-start.14
  13.9 6.8 %filters.1 = (bf16[4,256,2048]{2,1,0:T(8,128)(2,1)S(1)}, bf16[128,512]{1,0:T(8,128)(2,1)S(1)}, f32[512,64]{1,0:T(8,128)S(1)}, bf16[128,2048]{1,0:T(8,128)(2,1)}) custom-call(f32[512,32]{1,0:T(8,128)S(1)} %copy-done.16, f32[32,64]{1,0:T(8,128)S(1)} %copy-done.15, f32[64,2048]{1,0:T(8,128)S(1)} %copy-done.4, ...), custom_call_target="tpu_custom_call", output_to_operand_aliasing={{3}: (5, {})} | custom-call | flops 2147483648 | bytes 262144 | tf_op jit(solution)/shard_map/filters/pallas_call | solution.py:661
  20.7 5.6 %collective-permute-start.2 = (bf16[128,2048]{1,0:T(8,128)(2,1)}, bf16[128,2048]{1,0:T(8,128)(2,1)S(1)}, u32[]{:S(2)}, u32[]{:S(2)}) collective-permute-start(bf16[128,2048]{1,0:T(8,128)(2,1)} %get-tuple-element.41), channel_id=1, source_target_pairs={{0,8},{12,4},{1,9},{13,5},{2,10},{14,6},{3,11},{15,7},{16,24},{28,... | collective-permute-start | bytes 1572872 | tf_op jit(solution)/shard_map/ppermute | solution.py:636
  26.3 0.0 copy-done.5
  26.3 0.0 copy-done.7
  26.3 0.0 copy-done.8
  26.3 0.0 copy-done.11
  26.3 0.0 copy-done.12
  26.3 0.0 copy-done.13
  26.4 0.0 copy-done.14
  26.4 3.8 %own_pair.1 = (f32[64,2048]{1,0:T(8,128)S(1)}, bf16[64,2304]{1,0:T(8,128)(2,1)S(1)}) custom-call(bf16[128,2048]{1,0:T(8,128)(2,1)S(1)} %copy-done.13, bf16[128,2048]{1,0:T(8,128)(2,1)S(1)} %copy-done.14, f32[64,2048]{1,0:T(8,128)S(1)} %copy-done.5, f32[1,2048]{1,0:T(1,128)S(1)} %bitcast.6, bf16[256,256]{1,0:T(8,128)(2,1)S(1)} %copy-done.6, ...), custom_call_target="tpu_custom_call" | custom-call | flops 2147483648 | bytes 262144 | tf_op jit(solution)/shard_map/own_pair/pallas_call | solution.py:678
  30.1 1.3 %collective-permute-start.4 = (bf16[64,2304]{1,0:T(8,128)(2,1)S(1)}, bf16[64,2304]{1,0:T(8,128)(2,1)S(1)}, u32[]{:S(2)}, u32[]{:S(2)}) collective-permute-start(bf16[64,2304]{1,0:T(8,128)(2,1)S(1)} %get-tuple-element.50.refs_14_), channel_id=1, source_target_pairs={{0,4},{12,8},{1,5},{13,9},{2,6},{14,10},{3,7},{15,11},{16,20},{28,... | collective-permute-start | bytes 884744 | tf_op jit(solution)/shard_map/ppermute | solution.py:636
  31.5 0.0 collective-permute-done.refs_3_.refs_2_
  31.5 0.0 collective-permute-done.1.refs_4_.refs_3_
  31.5 9.4 %near_blocks.1 = (f32[128,2048]{1,0:T(8,128)S(1)}, f32[128,2048]{1,0:T(8,128)S(1)}, f32[128,2048]{1,0:T(8,128)S(1)}, f32[64,2048]{1,0:T(8,128)S(1)}, f32[32,64]{1,0:T(8,128)S(1)}) custom-call(s32[1]{0:T(128)} %bitcast.rank_ref.refs_0_.refs_1_, bf16[128,2048]{1,0:T(8,128)(2,1)S(1)} %copy-done.13, bf16[128,2048]{1,0:T(8,128)(2,1)S(1)} %copy-done.14, ...), custom_call_target="tpu_custom_call" | custom-call | flops 5368709120 | bytes 262144 | tf_op jit(solution)/shard_map/near_blocks/pallas_call | solution.py:691
  40.9 0.0 collective-permute-done.2.refs_1_.refs_4_
  40.9 2.6 %far_block.1 = (bf16[128,2048]{1,0:T(8,128)(2,1)S(1)}, f32[128,2048]{1,0:T(8,128)S(1)}) custom-call(s32[1]{0:T(128)} %bitcast.rank_ref.refs_0_.refs_1_, bf16[128,2048]{1,0:T(8,128)(2,1)S(1)} %collective-permute-done.2.refs_1_.refs_4_, bf16[4,256,2048]{2,1,0:T(8,128)(2,1)S(1)} %get-tuple-element.34.refs_5_.refs_2_, bf16[256,256]{1,0:T(8,128)(2,1)S(1)} %copy-done.6, ...), custom_call_target="tpu_custom_call" | custom-call | flops 268435456 | bytes 262144 | tf_op jit(solution)/shard_map/far_block/pallas_call | solution.py:709
  43.5 0.0 copy-start
  43.5 0.0 copy-start.1
  43.5 0.0 copy-start.2
  43.5 0.0 copy-start.3
  43.5 0.0 copy-start.9
  43.5 1.4 %collective-permute-start.3 = (bf16[128,2048]{1,0:T(8,128)(2,1)S(1)}, bf16[128,2048]{1,0:T(8,128)(2,1)S(1)}, u32[]{:S(2)}, u32[]{:S(2)}) collective-permute-start(bf16[128,2048]{1,0:T(8,128)(2,1)S(1)} %get-tuple-element.44), channel_id=1, source_target_pairs={{4,0},{8,12},{5,1},{9,13},{6,2},{10,14},{7,3},{11,15},{20,16},{24,... | collective-permute-start | bytes 1572872 | tf_op jit(solution)/shard_map/ppermute | solution.py:636
  45.0 0.0 collective-permute-done.4.refs_16_
  45.0 2.6 %last_pair.1 = (bf16[64,2304]{1,0:T(8,128)(2,1)S(1)}, f32[32,64]{1,0:T(8,128)S(1)}) custom-call(f32[128,2048]{1,0:T(8,128)S(1)} %get-tuple-element.43.refs_8_.refs_0_, s32[1]{0:T(128)} %bitcast.rank_ref.refs_0_.refs_1_, bf16[128,2048]{1,0:T(8,128)(2,1)S(1)} %collective-permute-done.refs_3_.refs_2_, ...), custom_call_target="tpu_custom_call" | custom-call | flops 268435456 | bytes 262144 | tf_op jit(solution)/shard_map/last_pair/pallas_call | solution.py:721
  47.6 0.7 collective-permute-start.7
  48.2 0.1 collective-permute-start.5
  48.3 1.2 %collective-permute-done.5 = f32[32,64]{1,0:T(8,128)S(1)} collective-permute-done((f32[32,64]{1,0:T(8,128)S(1)}, f32[32,64]{1,0:T(8,128)S(1)}, u32[]{:S(2)}, u32[]{:S(2)}) %collective-permute-start.5) | collective-permute-done | bytes 8224 | tf_op jit(solution)/shard_map/ppermute | solution.py:736
  49.5 1.5 %collective-permute-start.6 = (f32[32,64]{1,0:T(8,128)S(1)}, f32[32,64]{1,0:T(8,128)S(1)}, u32[]{:S(2)}, u32[]{:S(2)}) collective-permute-start(f32[32,64]{1,0:T(8,128)S(1)} %add.9), channel_id=1, source_target_pairs={{0,2},{1,3},{2,0},{3,1},{4,6},{5,7},{6,4},{7,5},{8,10},{9,11},{10,... | collective-permute-start | bytes 24584 | tf_op jit(solution)/shard_map/ppermute | solution.py:736
  51.0 2.2 %collective-permute-done.6 = f32[32,64]{1,0:T(8,128)S(1)} collective-permute-done((f32[32,64]{1,0:T(8,128)S(1)}, f32[32,64]{1,0:T(8,128)S(1)}, u32[]{:S(2)}, u32[]{:S(2)}) %collective-permute-start.6) | collective-permute-done | bytes 8224 | tf_op jit(solution)/shard_map/ppermute | solution.py:736
  53.2 0.0 collective-permute-done.7.come_ref
  53.2 5.1 %collective-permute-done.3.refs_9_.part_ref = bf16[128,2048]{1,0:T(8,128)(2,1)S(1)} collective-permute-done((bf16[128,2048]{1,0:T(8,128)(2,1)S(1)}, bf16[128,2048]{1,0:T(8,128)(2,1)S(1)}, u32[]{:S(2)}, u32[]{:S(2)}) %collective-permute-start.3) | collective-permute-done | bytes 524320 | tf_op jit(solution)/shard_map/ppermute | solution.py:636
  58.4 0.1 total.1.own_ref
  58.4 1.3 %collective-permute-start.8 = (bf16[64,2304]{1,0:T(8,128)(2,1)S(1)}, bf16[64,2304]{1,0:T(8,128)(2,1)S(1)}, u32[]{:S(2)}, u32[]{:S(2)}) collective-permute-start(bf16[64,2304]{1,0:T(8,128)(2,1)S(1)} %total.1.own_ref), channel_id=1, source_target_pairs={{4,0},{8,12},{5,1},{9,13},{6,2},{10,14},{7,3},{11,15},{20,16},{24,... | collective-permute-start | bytes 884744 | tf_op jit(solution)/shard_map/ppermute | solution.py:636
  59.7 0.7 collective-permute-start.9
  60.4 0.0 collective-permute-done.9
  60.4 1.3 %collective-permute-start.10 = (f32[32,64]{1,0:T(8,128)S(1)}, f32[32,64]{1,0:T(8,128)S(1)}, u32[]{:S(2)}, u32[]{:S(2)}) collective-permute-start(f32[32,64]{1,0:T(8,128)S(1)} %add.11.first_ref), channel_id=1, source_target_pairs={{4,0},{8,12},{5,1},{9,13},{6,2},{10,14},{7,3},{11,15},{20,16},{24,... | collective-permute-start | bytes 24584 | tf_op jit(solution)/shard_map/ppermute | solution.py:636
  61.7 0.0 copy-done
  61.7 0.0 copy-done.1
  61.7 0.0 copy-done.2
  61.8 0.0 copy-done.3
  61.8 0.0 copy-done.9
  61.8 2.1 %gates.1 = (bf16[128,2048]{1,0:T(8,128)(2,1)}, bf16[128,2048]{1,0:T(8,128)(2,1)}, bf16[128,2048]{1,0:T(8,128)(2,1)}) custom-call(s32[1]{0:T(128)} %bitcast.rank_ref.refs_0_.refs_1_, bf16[128,2048]{1,0:T(8,128)(2,1)S(1)} %copy-done, bf16[128,2048]{1,0:T(8,128)(2,1)S(1)} %copy-done.1, bf16[128,2048]{1,0:T(8,128)(2,1)S(1)} %copy-done.2, ...), custom_call_target="tpu_custom_call" | custom-call | bytes 262144 | tf_op jit(solution)/shard_map/gates/pallas_call | solution.py:748
  63.9 7.1 %collective-permute-done.10.first_come_ref = f32[32,64]{1,0:T(8,128)S(1)} collective-permute-done((f32[32,64]{1,0:T(8,128)S(1)}, f32[32,64]{1,0:T(8,128)S(1)}, u32[]{:S(2)}, u32[]{:S(2)}) %collective-permute-start.10) | collective-permute-done | bytes 8224 | tf_op jit(solution)/shard_map/ppermute | solution.py:636
  71.0 0.0 collective-permute-done.8.come_ref
  71.0 0.9 %finish.1 = (f32[64,2048]{1,0:T(8,128)}, f32[32,64]{1,0:T(8,128)}, f32[1,2048]{1,0:T(1,128)}) custom-call(s32[1]{0:T(128)} %bitcast.rank_ref.refs_0_.refs_1_, bf16[64,2304]{1,0:T(8,128)(2,1)S(1)} %total.1.own_ref, bf16[64,2304]{1,0:T(8,128)(2,1)S(1)} %collective-permute-done.8.come_ref, f32[32,64]{1,0:T(8,128)S(1)} %add.11.first_ref, ...), custom_call_target="tpu_custom_call" | custom-call | bytes 262144 | tf_op jit(solution)/shard_map/finish/pallas_call | solution.py:758
  (4 shorter events, 0.0 us)
Async XLA Ops:
  3.3 28.2 %collective-permute-start = (bf16[128,2048]{1,0:T(8,128)(2,1)}, bf16[128,2048]{1,0:T(8,128)(2,1)S(1)}, u32[]{:S(2)}, u32[]{:S(2)}) collective-permute-start(bf16[128,2048]{1,0:T(8,128)(2,1)} %get-tuple-element.31.refs_0_.refs_1_), channel_id=1, source_target_pairs={{0,4},{4,8},{8,12},{1,5},{5,9},{9,13},{2,6},{6,10},{10,14},{3,7},{... | collective-permute-start | bytes 1572872 | tf_op jit(solution)/shard_map/ppermute | solution.py:636
  8.2 23.2 %collective-permute-start.1 = (bf16[128,2048]{1,0:T(8,128)(2,1)}, bf16[128,2048]{1,0:T(8,128)(2,1)S(1)}, u32[]{:S(2)}, u32[]{:S(2)}) collective-permute-start(bf16[128,2048]{1,0:T(8,128)(2,1)} %get-tuple-element.32.refs_1_.refs_2_), channel_id=1, source_target_pairs={{4,0},{8,4},{12,8},{5,1},{9,5},{13,9},{6,2},{10,6},{14,10},{7,3},{... | collective-permute-start | bytes 1572872 | tf_op jit(solution)/shard_map/ppermute | solution.py:636
  9.5 1.0 %copy-start.4 = (f32[64,2048]{1,0:T(8,128)S(1)}, f32[64,2048]{1,0:T(8,128)}, u32[]{:S(2)}) copy-start(f32[64,2048]{1,0:T(8,128)} %refs_5_.2) | copy-start | bytes 1572868
  10.6 0.9 %copy-start.6 = (bf16[256,256]{1,0:T(8,128)(2,1)S(1)}, bf16[256,256]{1,0:T(8,128)(2,1)}, u32[]{:S(2)}) copy-start(bf16[256,256]{1,0:T(8,128)(2,1)} %constant.14.clone.refs_4_.refs_8_.refs_3_.refs_7_) | copy-start | bytes 393220
  11.5 0.7 copy-start.10
  12.2 0.7 copy-start.15
  12.9 0.9 %copy-start.16 = (f32[512,32]{1,0:T(8,128)S(1)}, f32[512,32]{1,0:T(8,128)}, u32[]{:S(2)}) copy-start(f32[512,32]{1,0:T(8,128)} %constant.13.clone.refs_0_) | copy-start | bytes 196612
  13.8 12.5 %copy-start.5 = (f32[64,2048]{1,0:T(8,128)S(1)}, f32[64,2048]{1,0:T(8,128)}, u32[]{:S(2)}) copy-start(f32[64,2048]{1,0:T(8,128)} %refs_5_.2) | copy-start | bytes 1572868
  13.8 12.5 %copy-start.7 = (bf16[256,256]{1,0:T(8,128)(2,1)S(1)}, bf16[256,256]{1,0:T(8,128)(2,1)}, u32[]{:S(2)}) copy-start(bf16[256,256]{1,0:T(8,128)(2,1)} %constant.15.clone.refs_5_.refs_9_.refs_4_.refs_8_) | copy-start | bytes 393220
  13.8 12.5 %copy-start.8 = (f32[32,512]{1,0:T(8,128)S(1)}, f32[32,512]{1,0:T(8,128)}, u32[]{:S(2)}) copy-start(f32[32,512]{1,0:T(8,128)} %constant.16.clone.refs_8_.refs_11_.refs_10_) | copy-start | bytes 196612
  13.8 12.5 %copy-start.11 = (f32[2048]{0:T(1024)S(1)}, f32[2048]{0:T(1024)}, u32[]{:S(2)}) copy-start(f32[2048]{0:T(1024)} %param.19) | copy-start | bytes 24580
  13.8 12.5 %copy-start.12 = (f32[1,2048]{1,0:T(1,128)S(1)}, f32[1,2048]{1,0:T(1,128)}, u32[]{:S(2)}) copy-start(f32[1,2048]{1,0:T(1,128)} %get-tuple-element.37.refs_9_.refs_15_) | copy-start | bytes 24580
  13.9 12.5 %copy-start.13 = (bf16[128,2048]{1,0:T(8,128)(2,1)S(1)}, bf16[128,2048]{1,0:T(8,128)(2,1)}, u32[]{:S(2)}) copy-start(bf16[128,2048]{1,0:T(8,128)(2,1)} %get-tuple-element.31.refs_0_.refs_1_) | copy-start | bytes 1572868
  13.9 12.5 %copy-start.14 = (bf16[128,2048]{1,0:T(8,128)(2,1)S(1)}, bf16[128,2048]{1,0:T(8,128)(2,1)}, u32[]{:S(2)}) copy-start(bf16[128,2048]{1,0:T(8,128)(2,1)} %get-tuple-element.32.refs_1_.refs_2_) | copy-start | bytes 1572868
  20.7 20.1 %collective-permute-start.2 = (bf16[128,2048]{1,0:T(8,128)(2,1)}, bf16[128,2048]{1,0:T(8,128)(2,1)S(1)}, u32[]{:S(2)}, u32[]{:S(2)}) collective-permute-start(bf16[128,2048]{1,0:T(8,128)(2,1)} %get-tuple-element.41), channel_id=1, source_target_pairs={{0,8},{12,4},{1,9},{13,5},{2,10},{14,6},{3,11},{15,7},{16,24},{28,... | collective-permute-start | bytes 1572872 | tf_op jit(solution)/shard_map/ppermute | solution.py:636
  30.1 14.8 %collective-permute-start.4 = (bf16[64,2304]{1,0:T(8,128)(2,1)S(1)}, bf16[64,2304]{1,0:T(8,128)(2,1)S(1)}, u32[]{:S(2)}, u32[]{:S(2)}) collective-permute-start(bf16[64,2304]{1,0:T(8,128)(2,1)S(1)} %get-tuple-element.50.refs_14_), channel_id=1, source_target_pairs={{0,4},{12,8},{1,5},{13,9},{2,6},{14,10},{3,7},{15,11},{16,20},{28,... | collective-permute-start | bytes 884744 | tf_op jit(solution)/shard_map/ppermute | solution.py:636
  43.5 18.2 %copy-start = (bf16[128,2048]{1,0:T(8,128)(2,1)S(1)}, bf16[128,2048]{1,0:T(8,128)(2,1)}, u32[]{:S(2)}) copy-start(bf16[128,2048]{1,0:T(8,128)(2,1)} %refs_1_.3) | copy-start | bytes 1572868
  43.5 18.2 %copy-start.1 = (bf16[128,2048]{1,0:T(8,128)(2,1)S(1)}, bf16[128,2048]{1,0:T(8,128)(2,1)}, u32[]{:S(2)}) copy-start(bf16[128,2048]{1,0:T(8,128)(2,1)} %refs_2_.5) | copy-start | bytes 1572868
  43.5 18.2 %copy-start.2 = (bf16[128,2048]{1,0:T(8,128)(2,1)S(1)}, bf16[128,2048]{1,0:T(8,128)(2,1)}, u32[]{:S(2)}) copy-start(bf16[128,2048]{1,0:T(8,128)(2,1)} %refs_3_.2) | copy-start | bytes 1572868
  43.5 18.2 %copy-start.3 = (bf16[128,2048]{1,0:T(8,128)(2,1)S(1)}, bf16[128,2048]{1,0:T(8,128)(2,1)}, u32[]{:S(2)}) copy-start(bf16[128,2048]{1,0:T(8,128)(2,1)} %refs_4_.4) | copy-start | bytes 1572868
  43.5 18.2 %copy-start.9 = (f32[2048]{0:T(1024)S(1)}, f32[2048]{0:T(1024)}, u32[]{:S(2)}) copy-start(f32[2048]{0:T(1024)} %param.18) | copy-start | bytes 24580
  43.5 14.8 %collective-permute-start.3 = (bf16[128,2048]{1,0:T(8,128)(2,1)S(1)}, bf16[128,2048]{1,0:T(8,128)(2,1)S(1)}, u32[]{:S(2)}, u32[]{:S(2)}) collective-permute-start(bf16[128,2048]{1,0:T(8,128)(2,1)S(1)} %get-tuple-element.44), channel_id=1, source_target_pairs={{4,0},{8,12},{5,1},{9,13},{6,2},{10,14},{7,3},{11,15},{20,16},{24,... | collective-permute-start | bytes 1572872 | tf_op jit(solution)/shard_map/ppermute | solution.py:636
  47.6 5.7 %collective-permute-start.7 = (bf16[64,2304]{1,0:T(8,128)(2,1)S(1)}, bf16[64,2304]{1,0:T(8,128)(2,1)S(1)}, u32[]{:S(2)}, u32[]{:S(2)}) collective-permute-start(bf16[64,2304]{1,0:T(8,128)(2,1)S(1)} %get-tuple-element.52.own_ref), channel_id=1, source_target_pairs={{4,8},{8,4},{5,9},{9,5},{6,10},{10,6},{7,11},{11,7},{20,24},{24,20... | collective-permute-start | bytes 884744 | tf_op jit(solution)/shard_map/ppermute | solution.py:636
  48.2 1.2 %collective-permute-start.5 = (f32[32,64]{1,0:T(8,128)S(1)}, f32[32,64]{1,0:T(8,128)S(1)}, u32[]{:S(2)}, u32[]{:S(2)}) collective-permute-start(f32[32,64]{1,0:T(8,128)S(1)} %get-tuple-element.51), channel_id=1, source_target_pairs={{0,1},{1,0},{2,3},{3,2},{4,5},{5,4},{6,7},{7,6},{8,9},{9,8},{10,11... | collective-permute-start | bytes 24584 | tf_op jit(solution)/shard_map/ppermute | solution.py:736
  49.5 3.7 %collective-permute-start.6 = (f32[32,64]{1,0:T(8,128)S(1)}, f32[32,64]{1,0:T(8,128)S(1)}, u32[]{:S(2)}, u32[]{:S(2)}) collective-permute-start(f32[32,64]{1,0:T(8,128)S(1)} %add.9), channel_id=1, source_target_pairs={{0,2},{1,3},{2,0},{3,1},{4,6},{5,7},{6,4},{7,5},{8,10},{9,11},{10,... | collective-permute-start | bytes 24584 | tf_op jit(solution)/shard_map/ppermute | solution.py:736
  58.4 12.6 %collective-permute-start.8 = (bf16[64,2304]{1,0:T(8,128)(2,1)S(1)}, bf16[64,2304]{1,0:T(8,128)(2,1)S(1)}, u32[]{:S(2)}, u32[]{:S(2)}) collective-permute-start(bf16[64,2304]{1,0:T(8,128)(2,1)S(1)} %total.1.own_ref), channel_id=1, source_target_pairs={{4,0},{8,12},{5,1},{9,13},{6,2},{10,14},{7,3},{11,15},{20,16},{24,... | collective-permute-start | bytes 884744 | tf_op jit(solution)/shard_map/ppermute | solution.py:636
  59.7 0.7 collective-permute-start.9
  60.4 10.6 %collective-permute-start.10 = (f32[32,64]{1,0:T(8,128)S(1)}, f32[32,64]{1,0:T(8,128)S(1)}, u32[]{:S(2)}, u32[]{:S(2)}) collective-permute-start(f32[32,64]{1,0:T(8,128)S(1)} %add.11.first_ref), channel_id=1, source_target_pairs={{4,0},{8,12},{5,1},{9,13},{6,2},{10,14},{7,3},{11,15},{20,16},{24,... | collective-permute-start | bytes 24584 | tf_op jit(solution)/shard_map/ppermute | solution.py:636

commit v6 on v5

--- a/solution.py
+++ b/solution.py
@@ -373,15 +373,33 @@
 
 
 def own_kernel(
-    rows, shards, channels, block, blocks, source_ref, cotan_ref, weight_ref, rate_ref, front_ref, back_ref, trans_ref,
-    slope_ref, featt_ref, bias_ref, sums_ref, send_ref, acc_ref,
+    rows, shards, channels, blocks, width, trans_out, slope_out, source_ref, cotan_ref, weight_ref, rate_ref, front_ref,
+    back_ref, featt_ref, bias_ref, sums_ref, send_ref, trans_ref, slope_ref, acc_ref, sems,
 ):
-    width = weight_ref.shape[1]
-
-    @pl.when(block == 0)
-    def _():
-        acc_ref[...] = jnp.zeros_like(acc_ref)
-
+    copies = [
+        pltpu.make_async_copy(trans_out, trans_ref, sems.at[0]),
+        pltpu.make_async_copy(slope_out, slope_ref, sems.at[1]),
+    ]
+    for copy in copies:
+        copy.start()
+    acc_ref[...] = jnp.zeros_like(acc_ref)
+    copies[0].wait()
+    strips = looped(
+        functools.partial(own_strip, rows, shards),
+        (ROWS, ROWS, ROWS, ROWS, None, None, None, ROWS, ROWS, None), blocks, width,
+    )
+    strips(
+        source_ref, cotan_ref, weight_ref, rate_ref, front_ref, back_ref, trans_ref, sums_ref, send_ref, acc_ref
+    )
+    copies[1].wait()
+    first = exact_dot(featt_ref[:, :rows], acc_ref[...] * slope_ref[:rows, :])
+    put_side(send_ref, channels, fold(bias_ref[...]), first)
+
+
+def own_strip(
+    rows, shards, block, blocks, source_ref, cotan_ref, weight_ref, rate_ref, front_ref, back_ref, trans_ref, sums_ref,
+    send_ref, acc_ref,
+):
     x0 = forward(front_ref, source_ref[...])
     c0 = forward(front_ref, cotan_ref[...])
     pair = conj_times((x0[:rows], x0[rows:]), (c0[:rows], c0[rows:]))
@@ -390,13 +408,8 @@
     m_high, m_low = split(backward(back_ref, high, low) * env)
     sums = weight_sums(trans_ref[:, :rows], m_high, m_low)
     sums_ref[...] = sums
-    send_ref[:, pl.ds(pl.multiple_of(block * width, width), width)] = sums.astype(bf16)
+    send_ref[...] = sums.astype(bf16)
     acc_ref[...] += hidden_sums(m_high, m_low, *split(weight_ref[...]))
-
-    @pl.when(block == blocks - 1)
-    def _():
-        first = exact_dot(featt_ref[:, :rows], acc_ref[...] * slope_ref[:rows, :])
-        put_side(send_ref, channels, fold(bias_ref[...]), first)
 
 
 def fold(bias):
@@ -538,12 +551,12 @@
         total_ref[...] = first
 
 
-def total_kernel(channels, hid_count, part_ref, first_ref, own_ref, come_ref, pay_ref):
-    del part_ref, first_ref
+def total_kernel(channels, hid_count, part_ref, own_ref, come_ref, first_ref, first_come_ref, pay_ref):
+    del part_ref
     lanes = channels // 128
     pay_ref[:, :channels] = (own_ref[:, :channels].astype(f32) + come_ref[:, :channels].astype(f32)).astype(bf16)
     own, come = (get_side(ref[...], channels, lanes, hid_count)[0] for ref in (own_ref, come_ref))
-    put_side(pay_ref, channels, own + come)
+    put_side(pay_ref, channels, own + come, first_ref[...] + first_come_ref[...])
 
 
 def gates_kernel(
@@ -570,8 +583,7 @@
 
 
 def finish_kernel(
-    channels, shards, rank_ref, own_ref, come_ref, first_ref, first_come_ref, second_out, first_out, bias_out, second,
-    first, bias, sems,
+    channels, shards, rank_ref, own_ref, come_ref, second_out, first_out, bias_out, second, first, bias, sems
 ):
     rank = rank_ref[0]
     inner = jnp.logical_and(rank > 0, rank < shards - 1)
@@ -583,9 +595,8 @@
     picked = jnp.where(inner, own_ref[...], come_ref[...])
     second[...] = picked[:, :channels].astype(f32)
     copies[0].start()
-    first[...] = jnp.where(inner, first_ref[...], first_come_ref[...])
+    rows, first[...] = get_side(picked, channels, lanes, first.shape[1])
     copies[1].start()
-    rows = get_side(picked, channels, lanes, first.shape[1])[0]
     for i in range(lanes):
         bias[:, i * 128 : (i + 1) * 128] = rows[i : i + 1]
     copies[2].start()
@@ -671,21 +682,19 @@
             pltpu.VMEM((hid_count, channels), f32), pltpu.VMEM((1, channels), f32), pltpu.VMEM((double, double), bf16),
             pltpu.VMEM((seq_len, 3 * hid_count), bf16), pltpu.SemaphoreType.DMA((5,)),
         ],
-        aliases={5: 3},
+        aliases={5: 3}, limit=57,
     )(feats, first_weight, second_weight, rate_row, front, edge)
     far = move(edge, [(0, 2), (shards - 1, shards - 3)])
 
     own, send = call(
-        looped(
-            functools.partial(own_kernel, rows, shards, channels),
-            (ROWS, ROWS, ROWS, ROWS, None, None, None, None, None, None, ROWS),
-            blocks, width,
-        ),
-        "own_pair", 8,
+        functools.partial(own_kernel, rows, shards, channels, blocks, width), "own_pair", 8,
         [shape(hid_count, channels), shape(*pay_shape, dtype=bf16)],
-        [vmem] * 10,
-        scratch=[pltpu.VMEM((rows, hid_count), f32)],
-    )(x0, c0, second_weight, rate_row, front, back, trans, slope, featt, bias)
+        [anywhere] * 2 + [vmem] * 8,
+        scratch=[
+            pltpu.VMEM((2 * hid_count, seq_len), bf16), pltpu.VMEM((seq_len, hid_count), f32),
+            pltpu.VMEM((rows, hid_count), f32), pltpu.SemaphoreType.DMA((2,)),
+        ],
+    )(trans, slope, x0, c0, second_weight, rate_row, front, back, featt, bias)
     come = move(send, inward)
 
     conv, corr, ahead, sums, first = call(
@@ -739,11 +748,9 @@
     (total,) = call(
         functools.partial(total_kernel, channels, hid_count), "total", 0,
         [shape(*pay_shape, dtype=bf16)],
-        [anywhere] * 2 + [vmem] * 2,
-    )(part_come, first, pay, pay_come)
+        [anywhere] + [vmem] * 4,
+    )(part_come, pay, pay_come, first, move(first, across))
     total_come = move(total, outward)
-    first = first + move(first, across)
-    first_come = move(first, outward)
 
     grad_one, grad_two, grad_value = call(
         looped(
@@ -758,10 +765,10 @@
     grad_second, grad_first, grad_bias = call(
         functools.partial(finish_kernel, channels, shards), "finish", 0,
         outs,
-        [smem] + [vmem] * 4,
+        [smem] + [vmem] * 2,
         out_specs=[anywhere] * 3,
         scratch=[pltpu.VMEM(o.shape, f32) for o in outs] + [pltpu.SemaphoreType.DMA((3,))],
-    )(rank, total, total_come, first, first_come)
+    )(rank, total, total_come)
     return (grad_one, grad_two, grad_value, grad_first, grad_second, grad_bias.reshape(channels))
 
 

time: 72.4 us -> 71.8 us (level)
  Pallas kernels: 30.8 us -> 33.4 us
  local copies, waits for them, and re-layouts: 4.37 us -> 1.93 us
  starting transfers between devices: 20.1 us -> 19.1 us
    pallas_call x1, Pallas kernels: 6.84 us -> 9.49 us  [few_shards_body(): call(functools.partial(filters_kernel, rows, shards, blocks, width), 'fil...]
    unnamed x34 -> x32, local copies, waits for them, and re-layouts: 4.37 us -> 1.93 us
    ppermute x9 -> x8, starting transfers between devices: 18.5 us -> 17.6 us  [move(): return lax.ppermute(array, 'ctx', pairs)]
    ppermute x9 -> x8, waiting for transfers between devices: 12.2 us -> 12.6 us  [move(): return lax.ppermute(array, 'ctx', pairs)]
  transfers between devices with their start and end apart: 11 -> 10, of which waited for: 4 -> 4; matrix products, arithmetic and copies ran while one was open for 0% -> 0% of each run, Pallas kernels for 38% -> 42%
where the time goes in v6:
time: 71.8 us; the launch traced here: 71.5 us
  Pallas kernels  33.4 us (47%)
  starting transfers between devices  19.1 us (27%)
  waiting for transfers between devices  16 us (22%)
  local copies, waits for them, and re-layouts  1.93 us (3%)
  between operations  1.02 us (1%)
    ppermute x8, starting transfers between devices, move(): return lax.ppermute(array, 'ctx', pairs)  17.6 us
    ppermute x8, waiting for transfers between devices, move(): return lax.ppermute(array, 'ctx', pairs)  12.6 us
    pallas_call x1, Pallas kernels, few_shards_body(): call(functools.partial(filters_kernel, rows, shards, blocks, width), 'fil...  9.49 us
    pallas_call x1, Pallas kernels, few_shards_body(): call(looped(functools.partial(near_kernel, rows, shards), (None, ROWS, RO...  9.19 us
    pallas_call x1, Pallas kernels, few_shards_body(): call(functools.partial(own_kernel, rows, shards, channels, blocks, width)...  3.96 us
    ppermute x2, waiting for transfers between devices, few_shards_body(): lax.ppermute(first, ('ch', 'sub'), [(i, i ^ bit) for i in range(group)])  3.45 us
    pallas_call x1, Pallas kernels, few_shards_body(): pl.pallas_call(products_kernel, grid=(rows // row_step,), in_specs=[smem]...  2.62 us
    pallas_call x1, Pallas kernels, few_shards_body(): call(looped(functools.partial(far_kernel, rows), (None, ROWS, (slice(2, 4...  2.59 us
  transfers between devices with their start and end apart: 10, of which 4 were waited for; matrix products, arithmetic and copies ran while one was open for 0% of the time, Pallas kernels for 42%

profile of v6, /device:TPU:0, one launch (start us, length us, event | category | flops | bytes accessed | tf_op | source)
XLA Modules:
  0.0 71.5 jit_solution(16686806743647650923)
XLA Ops:
  0.6 2.6 %products.1 = (bf16[128,2048]{1,0:T(8,128)(2,1)}, bf16[128,2048]{1,0:T(8,128)(2,1)}, bf16[128,2048]{1,0:T(8,128)(2,1)}, f32[1,2048]{1,0:T(1,128)}) custom-call(s32[1]{0:T(128)} %bitcast.rank_ref.refs_0_.refs_1_, bf16[128,2048]{1,0:T(8,128)(2,1)} %refs_1_.3, bf16[128,2048]{1,0:T(8,128)(2,1)} %refs_2_.3, bf16[128,2048]{1,0:T(8,128)(2,1)} %refs_3_.2, ...), custom_call_target="tpu_custom_call" | custom-call | tf_op jit(solution)/shard_map/products/pallas_call | solution.py:660
  3.3 0.0 copy-start.5
  3.3 0.0 copy-start.6
  3.3 0.0 copy-start.7
  3.3 0.0 copy-start.10
  3.3 0.0 copy-start.12
  3.3 0.0 copy-start.13
  3.3 0.0 copy-start.14
  3.3 0.0 copy-start.15
  3.3 5.1 %collective-permute-start = (bf16[128,2048]{1,0:T(8,128)(2,1)}, bf16[128,2048]{1,0:T(8,128)(2,1)S(1)}, u32[]{:S(2)}, u32[]{:S(2)}) collective-permute-start(bf16[128,2048]{1,0:T(8,128)(2,1)} %get-tuple-element.31.source_ref.refs_1_), channel_id=1, source_target_pairs={{0,4},{4,8},{8,12},{1,5},{5,9},{9,13},{2,6},{6,10},{10,14},{3,7},{... | collective-permute-start | bytes 1572872 | tf_op jit(solution)/shard_map/ppermute | solution.py:647
  8.4 1.3 %collective-permute-start.1 = (bf16[128,2048]{1,0:T(8,128)(2,1)}, bf16[128,2048]{1,0:T(8,128)(2,1)S(1)}, u32[]{:S(2)}, u32[]{:S(2)}) collective-permute-start(bf16[128,2048]{1,0:T(8,128)(2,1)} %get-tuple-element.32.cotan_ref.refs_2_), channel_id=1, source_target_pairs={{4,0},{8,4},{12,8},{5,1},{9,5},{13,9},{6,2},{10,6},{14,10},{7,3},{... | collective-permute-start | bytes 1572872 | tf_op jit(solution)/shard_map/ppermute | solution.py:647
  9.7 9.5 %filters.1 = (bf16[4,256,2048]{2,1,0:T(8,128)(2,1)}, bf16[128,512]{1,0:T(8,128)(2,1)}, f32[512,64]{1,0:T(8,128)}, bf16[128,2048]{1,0:T(8,128)(2,1)}) custom-call(f32[512,32]{1,0:T(8,128)} %constant.13.clone.refs_0_, f32[32,64]{1,0:T(8,128)} %refs_1_.2, f32[64,2048]{1,0:T(8,128)} %refs_5_.1, f32[1,2048]{1,0:T(1,128)} %bitcast.5, ...), custom_call_target="tpu_custom_call", output_to_operand_aliasing={{3}: (5, {})} | custom-call | flops 2147483648 | bytes 262144 | tf_op jit(solution)/shard_map/filters/pallas_call | solution.py:672
  19.2 0.0 copy-start
  19.3 5.8 %collective-permute-start.2 = (bf16[128,2048]{1,0:T(8,128)(2,1)}, bf16[128,2048]{1,0:T(8,128)(2,1)S(1)}, u32[]{:S(2)}, u32[]{:S(2)}) collective-permute-start(bf16[128,2048]{1,0:T(8,128)(2,1)} %get-tuple-element.41), channel_id=1, source_target_pairs={{0,8},{12,4},{1,9},{13,5},{2,10},{14,6},{3,11},{15,7},{16,24},{28,... | collective-permute-start | bytes 1572872 | tf_op jit(solution)/shard_map/ppermute | solution.py:647
  25.1 0.0 copy-done.5
  25.1 0.0 copy-done.6
  25.1 0.0 copy-done.7
  25.1 0.0 copy-done.10
  25.1 0.0 copy-done.12
  25.1 0.0 copy-done.13
  25.2 0.0 copy-done.14
  25.2 0.0 copy-done.15
  25.2 0.0 copy-start.8
  25.2 0.9 %copy-done.8 = f32[512,64]{1,0:T(8,128)S(1)} copy-done((f32[512,64]{1,0:T(8,128)S(1)}, f32[512,64]{1,0:T(8,128)}, u32[]{:S(2)}) %copy-start.8) | copy-done | bytes 131096
  26.1 0.0 copy-start.9
  26.1 0.9 %copy-done.9 = bf16[128,512]{1,0:T(8,128)(2,1)S(1)} copy-done((bf16[128,512]{1,0:T(8,128)(2,1)S(1)}, bf16[128,512]{1,0:T(8,128)(2,1)}, u32[]{:S(2)}) %copy-start.9) | copy-done | bytes 131096
  27.0 4.0 %own_pair.1 = (f32[64,2048]{1,0:T(8,128)S(1)}, bf16[64,2304]{1,0:T(8,128)(2,1)S(1)}) custom-call(bf16[128,512]{1,0:T(8,128)(2,1)S(1)} %copy-done.9, f32[512,64]{1,0:T(8,128)S(1)} %copy-done.8, bf16[128,2048]{1,0:T(8,128)(2,1)S(1)} %copy-done.14, bf16[128,2048]{1,0:T(8,128)(2,1)S(1)} %copy-done.15, f32[64,2048]{1,0:T(8,128)S(1)} %copy-done.5, ...), custom_call_target="tpu_custom_call" | custom-call | flops 2147483648 | bytes 262144 | tf_op jit(solution)/shard_map/own_pair/pallas_call | solution.py:689
  31.0 1.3 %collective-permute-start.4 = (bf16[64,2304]{1,0:T(8,128)(2,1)S(1)}, bf16[64,2304]{1,0:T(8,128)(2,1)S(1)}, u32[]{:S(2)}, u32[]{:S(2)}) collective-permute-start(bf16[64,2304]{1,0:T(8,128)(2,1)S(1)} %get-tuple-element.50.refs_14_), channel_id=1, source_target_pairs={{0,4},{12,8},{1,5},{13,9},{2,6},{14,10},{3,7},{15,11},{16,20},{28,... | collective-permute-start | bytes 884744 | tf_op jit(solution)/shard_map/ppermute | solution.py:647
  32.3 0.0 collective-permute-done.refs_3_.refs_2_
  32.3 0.0 collective-permute-done.1.refs_4_.refs_3_
  32.3 0.0 copy-done
  32.3 9.2 %near_blocks.1 = (f32[128,2048]{1,0:T(8,128)S(1)}, f32[128,2048]{1,0:T(8,128)S(1)}, f32[128,2048]{1,0:T(8,128)S(1)}, f32[64,2048]{1,0:T(8,128)S(1)}, f32[32,64]{1,0:T(8,128)S(1)}) custom-call(s32[1]{0:T(128)} %bitcast.rank_ref.refs_0_.refs_1_, bf16[128,2048]{1,0:T(8,128)(2,1)S(1)} %copy-done.14, bf16[128,2048]{1,0:T(8,128)(2,1)S(1)} %copy-done.15, ...), custom_call_target="tpu_custom_call" | custom-call | flops 5368709120 | bytes 262144 | tf_op jit(solution)/shard_map/near_blocks/pallas_call | solution.py:700
  41.5 0.0 collective-permute-done.2.refs_1_.refs_4_
  41.6 2.6 %far_block.1 = (bf16[128,2048]{1,0:T(8,128)(2,1)S(1)}, f32[128,2048]{1,0:T(8,128)S(1)}) custom-call(s32[1]{0:T(128)} %bitcast.rank_ref.refs_0_.refs_1_, bf16[128,2048]{1,0:T(8,128)(2,1)S(1)} %collective-permute-done.2.refs_1_.refs_4_, bf16[4,256,2048]{2,1,0:T(8,128)(2,1)S(1)} %copy-done, bf16[256,256]{1,0:T(8,128)(2,1)S(1)} %copy-done.6, ...), custom_call_target="tpu_custom_call" | custom-call | flops 268435456 | bytes 262144 | tf_op jit(solution)/shard_map/far_block/pallas_call | solution.py:718
  44.1 0.0 copy-start.1
  44.2 0.0 copy-start.2
  44.2 0.0 copy-start.3
  44.2 0.0 copy-start.4
  44.2 0.0 copy-start.11
  44.2 1.4 %collective-permute-start.3 = (bf16[128,2048]{1,0:T(8,128)(2,1)S(1)}, bf16[128,2048]{1,0:T(8,128)(2,1)S(1)}, u32[]{:S(2)}, u32[]{:S(2)}) collective-permute-start(bf16[128,2048]{1,0:T(8,128)(2,1)S(1)} %get-tuple-element.44), channel_id=1, source_target_pairs={{4,0},{8,12},{5,1},{9,13},{6,2},{10,14},{7,3},{11,15},{20,16},{24,... | collective-permute-start | bytes 1572872 | tf_op jit(solution)/shard_map/ppermute | solution.py:647
  45.6 0.0 collective-permute-done.4.refs_16_
  45.6 2.6 %last_pair.1 = (bf16[64,2304]{1,0:T(8,128)(2,1)S(1)}, f32[32,64]{1,0:T(8,128)S(1)}) custom-call(f32[128,2048]{1,0:T(8,128)S(1)} %get-tuple-element.43.refs_8_.refs_0_, s32[1]{0:T(128)} %bitcast.rank_ref.refs_0_.refs_1_, bf16[128,2048]{1,0:T(8,128)(2,1)S(1)} %collective-permute-done.refs_3_.refs_2_, ...), custom_call_target="tpu_custom_call" | custom-call | flops 268435456 | bytes 262144 | tf_op jit(solution)/shard_map/last_pair/pallas_call | solution.py:730
  48.2 0.7 collective-permute-start.5
  48.9 0.1 collective-permute-start.6
  49.0 1.2 %collective-permute-done.6 = f32[32,64]{1,0:T(8,128)S(1)} collective-permute-done((f32[32,64]{1,0:T(8,128)S(1)}, f32[32,64]{1,0:T(8,128)S(1)}, u32[]{:S(2)}, u32[]{:S(2)}) %collective-permute-start.6) | collective-permute-done | bytes 8224 | tf_op jit(solution)/shard_map/ppermute | solution.py:745
  50.1 1.5 %collective-permute-start.7 = (f32[32,64]{1,0:T(8,128)S(1)}, f32[32,64]{1,0:T(8,128)S(1)}, u32[]{:S(2)}, u32[]{:S(2)}) collective-permute-start(f32[32,64]{1,0:T(8,128)S(1)} %add.6), channel_id=1, source_target_pairs={{0,2},{1,3},{2,0},{3,1},{4,6},{5,7},{6,4},{7,5},{8,10},{9,11},{10,... | collective-permute-start | bytes 24584 | tf_op jit(solution)/shard_map/ppermute | solution.py:745
  51.6 2.3 %collective-permute-done.7 = f32[32,64]{1,0:T(8,128)S(1)} collective-permute-done((f32[32,64]{1,0:T(8,128)S(1)}, f32[32,64]{1,0:T(8,128)S(1)}, u32[]{:S(2)}, u32[]{:S(2)}) %collective-permute-start.7) | collective-permute-done | bytes 8224 | tf_op jit(solution)/shard_map/ppermute | solution.py:745
  53.9 0.7 collective-permute-start.8
  54.5 0.0 collective-permute-done.8.first_come_ref
  54.6 0.0 collective-permute-done.5.come_ref
  54.6 4.5 %collective-permute-done.3.refs_9_.part_ref = bf16[128,2048]{1,0:T(8,128)(2,1)S(1)} collective-permute-done((bf16[128,2048]{1,0:T(8,128)(2,1)S(1)}, bf16[128,2048]{1,0:T(8,128)(2,1)S(1)}, u32[]{:S(2)}, u32[]{:S(2)}) %collective-permute-start.3) | collective-permute-done | bytes 524320 | tf_op jit(solution)/shard_map/ppermute | solution.py:647
  59.0 0.1 total.1.own_ref
  59.1 1.3 %collective-permute-start.9 = (bf16[64,2304]{1,0:T(8,128)(2,1)S(1)}, bf16[64,2304]{1,0:T(8,128)(2,1)S(1)}, u32[]{:S(2)}, u32[]{:S(2)}) collective-permute-start(bf16[64,2304]{1,0:T(8,128)(2,1)S(1)} %total.1.own_ref), channel_id=1, source_target_pairs={{4,0},{8,12},{5,1},{9,13},{6,2},{10,14},{7,3},{11,15},{20,16},{24,... | collective-permute-start | bytes 884744 | tf_op jit(solution)/shard_map/ppermute | solution.py:647
  60.4 0.0 copy-done.1
  60.4 0.0 copy-done.2
  60.4 0.0 copy-done.3
  60.4 0.0 copy-done.4
  60.4 0.0 copy-done.11
  60.5 2.1 %gates.1 = (bf16[128,2048]{1,0:T(8,128)(2,1)}, bf16[128,2048]{1,0:T(8,128)(2,1)}, bf16[128,2048]{1,0:T(8,128)(2,1)}) custom-call(s32[1]{0:T(128)} %bitcast.rank_ref.refs_0_.refs_1_, bf16[128,2048]{1,0:T(8,128)(2,1)S(1)} %copy-done.1, bf16[128,2048]{1,0:T(8,128)(2,1)S(1)} %copy-done.2, bf16[128,2048]{1,0:T(8,128)(2,1)S(1)} %copy-done.3, ...), custom_call_target="tpu_custom_call" | custom-call | bytes 262144 | tf_op jit(solution)/shard_map/gates/pallas_call | solution.py:755
  62.5 8.1 %collective-permute-done.9.come_ref = bf16[64,2304]{1,0:T(8,128)(2,1)S(1)} collective-permute-done((bf16[64,2304]{1,0:T(8,128)(2,1)S(1)}, bf16[64,2304]{1,0:T(8,128)(2,1)S(1)}, u32[]{:S(2)}, u32[]{:S(2)}) %collective-permute-start.9) | collective-permute-done | bytes 294944 | tf_op jit(solution)/shard_map/ppermute | solution.py:647
  70.6 0.9 %finish.1 = (f32[64,2048]{1,0:T(8,128)}, f32[32,64]{1,0:T(8,128)}, f32[1,2048]{1,0:T(1,128)}) custom-call(s32[1]{0:T(128)} %bitcast.rank_ref.refs_0_.refs_1_, bf16[64,2304]{1,0:T(8,128)(2,1)S(1)} %total.1.own_ref, bf16[64,2304]{1,0:T(8,128)(2,1)S(1)} %collective-permute-done.9.come_ref), custom_call_target="tpu_custom_call" | custom-call | bytes 262144 | tf_op jit(solution)/shard_map/finish/pallas_call | solution.py:765
  (2 shorter events, 0.0 us)
Async XLA Ops:
  3.3 21.8 %copy-start.5 = (f32[64,2048]{1,0:T(8,128)S(1)}, f32[64,2048]{1,0:T(8,128)}, u32[]{:S(2)}) copy-start(f32[64,2048]{1,0:T(8,128)} %refs_5_.1) | copy-start | bytes 1572868
  3.3 21.8 %copy-start.6 = (bf16[256,256]{1,0:T(8,128)(2,1)S(1)}, bf16[256,256]{1,0:T(8,128)(2,1)}, u32[]{:S(2)}) copy-start(bf16[256,256]{1,0:T(8,128)(2,1)} %constant.14.clone.refs_4_.front_ref.refs_8_.refs_3_.refs_7_) | copy-start | bytes 393220
  3.3 21.8 %copy-start.7 = (bf16[256,256]{1,0:T(8,128)(2,1)S(1)}, bf16[256,256]{1,0:T(8,128)(2,1)}, u32[]{:S(2)}) copy-start(bf16[256,256]{1,0:T(8,128)(2,1)} %constant.15.clone.back_ref.refs_9_.refs_4_.refs_8_) | copy-start | bytes 393220
  3.3 21.8 %copy-start.10 = (f32[32,512]{1,0:T(8,128)S(1)}, f32[32,512]{1,0:T(8,128)}, u32[]{:S(2)}) copy-start(f32[32,512]{1,0:T(8,128)} %constant.16.clone.featt_ref.refs_11_.refs_10_) | copy-start | bytes 196612
  3.3 21.8 %copy-start.12 = (f32[2048]{0:T(1024)S(1)}, f32[2048]{0:T(1024)}, u32[]{:S(2)}) copy-start(f32[2048]{0:T(1024)} %param.19) | copy-start | bytes 24580
  3.3 21.8 %copy-start.13 = (f32[1,2048]{1,0:T(1,128)S(1)}, f32[1,2048]{1,0:T(1,128)}, u32[]{:S(2)}) copy-start(f32[1,2048]{1,0:T(1,128)} %get-tuple-element.37.bias_ref.refs_15_) | copy-start | bytes 24580
  3.3 21.8 %copy-start.14 = (bf16[128,2048]{1,0:T(8,128)(2,1)S(1)}, bf16[128,2048]{1,0:T(8,128)(2,1)}, u32[]{:S(2)}) copy-start(bf16[128,2048]{1,0:T(8,128)(2,1)} %get-tuple-element.31.source_ref.refs_1_) | copy-start | bytes 1572868
  3.3 21.8 %copy-start.15 = (bf16[128,2048]{1,0:T(8,128)(2,1)S(1)}, bf16[128,2048]{1,0:T(8,128)(2,1)}, u32[]{:S(2)}) copy-start(bf16[128,2048]{1,0:T(8,128)(2,1)} %get-tuple-element.32.cotan_ref.refs_2_) | copy-start | bytes 1572868
  3.3 29.0 %collective-permute-start = (bf16[128,2048]{1,0:T(8,128)(2,1)}, bf16[128,2048]{1,0:T(8,128)(2,1)S(1)}, u32[]{:S(2)}, u32[]{:S(2)}) collective-permute-start(bf16[128,2048]{1,0:T(8,128)(2,1)} %get-tuple-element.31.source_ref.refs_1_), channel_id=1, source_target_pairs={{0,4},{4,8},{8,12},{1,5},{5,9},{9,13},{2,6},{6,10},{10,14},{3,7},{... | collective-permute-start | bytes 1572872 | tf_op jit(solution)/shard_map/ppermute | solution.py:647
  8.4 23.9 %collective-permute-start.1 = (bf16[128,2048]{1,0:T(8,128)(2,1)}, bf16[128,2048]{1,0:T(8,128)(2,1)S(1)}, u32[]{:S(2)}, u32[]{:S(2)}) collective-permute-start(bf16[128,2048]{1,0:T(8,128)(2,1)} %get-tuple-element.32.cotan_ref.refs_2_), channel_id=1, source_target_pairs={{4,0},{8,4},{12,8},{5,1},{9,5},{13,9},{6,2},{10,6},{14,10},{7,3},{... | collective-permute-start | bytes 1572872 | tf_op jit(solution)/shard_map/ppermute | solution.py:647
  19.2 13.1 %copy-start = (bf16[4,256,2048]{2,1,0:T(8,128)(2,1)S(1)}, bf16[4,256,2048]{2,1,0:T(8,128)(2,1)}, u32[]{:S(2)}) copy-start(bf16[4,256,2048]{2,1,0:T(8,128)(2,1)} %get-tuple-element.34.refs_5_.refs_2_) | copy-start | bytes 12582916
  19.3 22.3 %collective-permute-start.2 = (bf16[128,2048]{1,0:T(8,128)(2,1)}, bf16[128,2048]{1,0:T(8,128)(2,1)S(1)}, u32[]{:S(2)}, u32[]{:S(2)}) collective-permute-start(bf16[128,2048]{1,0:T(8,128)(2,1)} %get-tuple-element.41), channel_id=1, source_target_pairs={{0,8},{12,4},{1,9},{13,5},{2,10},{14,6},{3,11},{15,7},{16,24},{28,... | collective-permute-start | bytes 1572872 | tf_op jit(solution)/shard_map/ppermute | solution.py:647
  25.2 1.0 %copy-start.8 = (f32[512,64]{1,0:T(8,128)S(1)}, f32[512,64]{1,0:T(8,128)}, u32[]{:S(2)}) copy-start(f32[512,64]{1,0:T(8,128)} %get-tuple-element.36.slope_out.refs_12_.refs_11_) | copy-start | bytes 393220
  26.1 0.9 %copy-start.9 = (bf16[128,512]{1,0:T(8,128)(2,1)S(1)}, bf16[128,512]{1,0:T(8,128)(2,1)}, u32[]{:S(2)}) copy-start(bf16[128,512]{1,0:T(8,128)(2,1)} %get-tuple-element.35.trans_out.refs_10_.refs_9_) | copy-start | bytes 393220
  31.0 14.6 %collective-permute-start.4 = (bf16[64,2304]{1,0:T(8,128)(2,1)S(1)}, bf16[64,2304]{1,0:T(8,128)(2,1)S(1)}, u32[]{:S(2)}, u32[]{:S(2)}) collective-permute-start(bf16[64,2304]{1,0:T(8,128)(2,1)S(1)} %get-tuple-element.50.refs_14_), channel_id=1, source_target_pairs={{0,4},{12,8},{1,5},{13,9},{2,6},{14,10},{3,7},{15,11},{16,20},{28,... | collective-permute-start | bytes 884744 | tf_op jit(solution)/shard_map/ppermute | solution.py:647
  44.1 16.3 %copy-start.1 = (bf16[128,2048]{1,0:T(8,128)(2,1)S(1)}, bf16[128,2048]{1,0:T(8,128)(2,1)}, u32[]{:S(2)}) copy-start(bf16[128,2048]{1,0:T(8,128)(2,1)} %refs_1_.3) | copy-start | bytes 1572868
  44.2 16.3 %copy-start.2 = (bf16[128,2048]{1,0:T(8,128)(2,1)S(1)}, bf16[128,2048]{1,0:T(8,128)(2,1)}, u32[]{:S(2)}) copy-start(bf16[128,2048]{1,0:T(8,128)(2,1)} %refs_2_.3) | copy-start | bytes 1572868
  44.2 16.3 %copy-start.3 = (bf16[128,2048]{1,0:T(8,128)(2,1)S(1)}, bf16[128,2048]{1,0:T(8,128)(2,1)}, u32[]{:S(2)}) copy-start(bf16[128,2048]{1,0:T(8,128)(2,1)} %refs_3_.2) | copy-start | bytes 1572868
  44.2 16.3 %copy-start.4 = (bf16[128,2048]{1,0:T(8,128)(2,1)S(1)}, bf16[128,2048]{1,0:T(8,128)(2,1)}, u32[]{:S(2)}) copy-start(bf16[128,2048]{1,0:T(8,128)(2,1)} %refs_4_.3) | copy-start | bytes 1572868
  44.2 16.3 %copy-start.11 = (f32[2048]{0:T(1024)S(1)}, f32[2048]{0:T(1024)}, u32[]{:S(2)}) copy-start(f32[2048]{0:T(1024)} %param.18) | copy-start | bytes 24580
  44.2 14.8 %collective-permute-start.3 = (bf16[128,2048]{1,0:T(8,128)(2,1)S(1)}, bf16[128,2048]{1,0:T(8,128)(2,1)S(1)}, u32[]{:S(2)}, u32[]{:S(2)}) collective-permute-start(bf16[128,2048]{1,0:T(8,128)(2,1)S(1)} %get-tuple-element.44), channel_id=1, source_target_pairs={{4,0},{8,12},{5,1},{9,13},{6,2},{10,14},{7,3},{11,15},{20,16},{24,... | collective-permute-start | bytes 1572872 | tf_op jit(solution)/shard_map/ppermute | solution.py:647
  48.2 6.4 %collective-permute-start.5 = (bf16[64,2304]{1,0:T(8,128)(2,1)S(1)}, bf16[64,2304]{1,0:T(8,128)(2,1)S(1)}, u32[]{:S(2)}, u32[]{:S(2)}) collective-permute-start(bf16[64,2304]{1,0:T(8,128)(2,1)S(1)} %get-tuple-element.51.own_ref), channel_id=1, source_target_pairs={{4,8},{8,4},{5,9},{9,5},{6,10},{10,6},{7,11},{11,7},{20,24},{24,20... | collective-permute-start | bytes 884744 | tf_op jit(solution)/shard_map/ppermute | solution.py:647
  48.9 1.2 %collective-permute-start.6 = (f32[32,64]{1,0:T(8,128)S(1)}, f32[32,64]{1,0:T(8,128)S(1)}, u32[]{:S(2)}, u32[]{:S(2)}) collective-permute-start(f32[32,64]{1,0:T(8,128)S(1)} %get-tuple-element.52), channel_id=1, source_target_pairs={{0,1},{1,0},{2,3},{3,2},{4,5},{5,4},{6,7},{7,6},{8,9},{9,8},{10,11... | collective-permute-start | bytes 24584 | tf_op jit(solution)/shard_map/ppermute | solution.py:745
  50.1 3.7 %collective-permute-start.7 = (f32[32,64]{1,0:T(8,128)S(1)}, f32[32,64]{1,0:T(8,128)S(1)}, u32[]{:S(2)}, u32[]{:S(2)}) collective-permute-start(f32[32,64]{1,0:T(8,128)S(1)} %add.6), channel_id=1, source_target_pairs={{0,2},{1,3},{2,0},{3,1},{4,6},{5,7},{6,4},{7,5},{8,10},{9,11},{10,... | collective-permute-start | bytes 24584 | tf_op jit(solution)/shard_map/ppermute | solution.py:745
  53.9 0.7 collective-permute-start.8
  59.1 11.5 %collective-permute-start.9 = (bf16[64,2304]{1,0:T(8,128)(2,1)S(1)}, bf16[64,2304]{1,0:T(8,128)(2,1)S(1)}, u32[]{:S(2)}, u32[]{:S(2)}) collective-permute-start(bf16[64,2304]{1,0:T(8,128)(2,1)S(1)} %total.1.own_ref), channel_id=1, source_target_pairs={{4,0},{8,12},{5,1},{9,13},{6,2},{10,14},{7,3},{11,15},{20,16},{24,... | collective-permute-start | bytes 884744 | tf_op jit(solution)/shard_map/ppermute | solution.py:647

commit v7 on v6

--- a/solution.py
+++ b/solution.py
@@ -326,32 +326,43 @@
     return jnp.where(odd, cosine, sine) * sin_sign, jnp.where(odd, sine, cosine) * cos_sign
 
 
+def turned_over(hidden, slope):
+    both = jnp.concatenate([hidden, slope], axis=1).T
+    return jnp.concatenate(split(both[: hidden.shape[1]]), axis=0)
+
+
 def filters_kernel(rows, shards, blocks, width, *refs):
-    inputs, passed, outputs, held, (hid_ref, sems) = refs[:5], refs[5:6], refs[6:10], refs[10:15], refs[15:]
-    del passed
+    inputs, (spec_out, trans_ref, slope_ref), held, (spec_ref, hid_ref, sems, out_sems) = (
+        refs[:5], refs[6:9], refs[10:15], refs[15:]
+    )
     feats_ref, first_ref, weight_ref, rate_ref, front_ref = held
-    spec_ref, trans_ref, slope_ref, _ = outputs
     copies = [pltpu.make_async_copy(far, near, sems.at[i]) for i, (far, near) in enumerate(zip(inputs, held))]
     for copy in copies:
         copy.start()
-    hid_count = first_ref.shape[1]
     copies[0].wait()
     copies[1].wait()
     hidden, slope = sin_cos(exact_dot(feats_ref[...], first_ref[...]))
     slope_ref[...] = slope
     high, low = split(hidden)
     hid_ref[...] = jnp.concatenate([high, high, low], axis=1)
-    turned_over = jnp.concatenate([hidden, slope], axis=1).T[:hid_count]
-    trans_ref[...] = jnp.concatenate(split(turned_over), axis=0)
+    trans_ref[...] = turned_over(hidden, slope)
     for copy in copies[2:]:
         copy.wait()
-    strips = looped(
-        functools.partial(filter_strip, rows, shards), (None, ROWS, ROWS, None, CUBE), blocks, width
-    )
-    strips(hid_ref, weight_ref, rate_ref, front_ref, spec_ref)
-
-
-def filter_strip(rows, shards, block, blocks, hid_ref, weight_ref, rate_ref, front_ref, spec_ref):
+
+    def leaving(block):
+        cols = pl.ds(pl.multiple_of(block * width, width), width)
+        return pltpu.make_async_copy(spec_ref.at[:, :, cols], spec_out.at[:, :, cols], out_sems.at[block])
+
+    def strip(block, blocks, *views):
+        filter_strip(rows, shards, *views)
+        leaving(block).start()
+
+    looped(strip, (None, ROWS, ROWS, None, CUBE), blocks, width)(hid_ref, weight_ref, rate_ref, front_ref, spec_ref)
+    for block in range(blocks):
+        leaving(block).wait()
+
+
+def filter_strip(rows, shards, hid_ref, weight_ref, rate_ref, front_ref, spec_ref):
     scale = float(rows * shards) ** -0.5
     w_high, w_low = split(weight_ref[...])
     stacked = jnp.concatenate([w_high, w_low, w_high], axis=0)
@@ -373,17 +384,13 @@
 
 
 def own_kernel(
-    rows, shards, channels, blocks, width, trans_out, slope_out, source_ref, cotan_ref, weight_ref, rate_ref, front_ref,
-    back_ref, featt_ref, bias_ref, sums_ref, send_ref, trans_ref, slope_ref, acc_ref, sems,
+    rows, shards, channels, blocks, width, passed, feats_ref, first_ref, source_ref, cotan_ref, weight_ref, rate_ref,
+    front_ref, back_ref, featt_ref, bias_ref, sums_ref, send_ref, passing, trans_ref, acc_ref,
 ):
-    copies = [
-        pltpu.make_async_copy(trans_out, trans_ref, sems.at[0]),
-        pltpu.make_async_copy(slope_out, slope_ref, sems.at[1]),
-    ]
-    for copy in copies:
-        copy.start()
+    del passed, passing
+    hidden, slope = sin_cos(exact_dot(feats_ref[...], first_ref[...]))
+    trans_ref[...] = turned_over(hidden, slope)
     acc_ref[...] = jnp.zeros_like(acc_ref)
-    copies[0].wait()
     strips = looped(
         functools.partial(own_strip, rows, shards),
         (ROWS, ROWS, ROWS, ROWS, None, None, None, ROWS, ROWS, None), blocks, width,
@@ -391,8 +398,7 @@
     strips(
         source_ref, cotan_ref, weight_ref, rate_ref, front_ref, back_ref, trans_ref, sums_ref, send_ref, acc_ref
     )
-    copies[1].wait()
-    first = exact_dot(featt_ref[:, :rows], acc_ref[...] * slope_ref[:rows, :])
+    first = exact_dot(featt_ref[:, :rows], acc_ref[...] * slope)
     put_side(send_ref, channels, fold(bias_ref[...]), first)
 
 
@@ -406,7 +412,7 @@
     high, low = split(jnp.concatenate(pair, axis=0))
     env = decay(rate_ref[...], rows, float(rows * shards) ** -0.5)
     m_high, m_low = split(backward(back_ref, high, low) * env)
-    sums = weight_sums(trans_ref[:, :rows], m_high, m_low)
+    sums = weight_sums(trans_ref[...], m_high, m_low)
     sums_ref[...] = sums
     send_ref[...] = sums.astype(bf16)
     acc_ref[...] += hidden_sums(m_high, m_low, *split(weight_ref[...]))
@@ -433,10 +439,11 @@
 
 
 def near_kernel(
-    rows, shards, block, blocks, rank_ref, x0_ref, c0_ref, x1_ref, c1_ref, spec_ref, weight_ref, rate_ref, front_ref, back_ref,
-    trans_ref, featt_ref, slope_ref, own_ref, conv_ref, corr_ref, ahead_ref, sums_ref, first_ref, fields, fast, high_ref,
-    low_ref, acc_ref,
+    rows, shards, block, blocks, passed, rank_ref, x0_ref, c0_ref, x1_ref, c1_ref, spec_ref, weight_ref, rate_ref, front_ref, back_ref,
+    trans_ref, featt_ref, slope_ref, own_ref, conv_ref, corr_ref, ahead_ref, sums_ref, first_ref, passing, fields, fast,
+    high_ref, low_ref, acc_ref,
 ):
+    del passed, passing
     rank = rank_ref[0]
     count = shards - 1
 
@@ -675,37 +682,39 @@
             shape(shards, double, channels, dtype=bf16), shape(2 * hid_count, seq_len, dtype=bf16),
             shape(seq_len, hid_count), block_bf16,
         ],
-        [pl.BlockSpec(memory_space=pltpu.HBM)] * 6,
-        out_specs=[vmem] * 3 + [pl.BlockSpec(memory_space=pltpu.HBM)],
+        [anywhere] * 6,
+        out_specs=[anywhere] + [vmem] * 2 + [anywhere],
         scratch=[
             pltpu.VMEM((seq_len, feat_count), f32), pltpu.VMEM((feat_count, hid_count), f32),
             pltpu.VMEM((hid_count, channels), f32), pltpu.VMEM((1, channels), f32), pltpu.VMEM((double, double), bf16),
-            pltpu.VMEM((seq_len, 3 * hid_count), bf16), pltpu.SemaphoreType.DMA((5,)),
+            pltpu.VMEM((shards, double, channels), bf16), pltpu.VMEM((seq_len, 3 * hid_count), bf16),
+            pltpu.SemaphoreType.DMA((5,)), pltpu.SemaphoreType.DMA((blocks,)),
         ],
-        aliases={5: 3}, limit=57,
+        aliases={5: 3},
+        limit=60,
     )(feats, first_weight, second_weight, rate_row, front, edge)
+
+    own, send, edge = call(
+        functools.partial(own_kernel, rows, shards, channels, blocks, width), "own_pair", 8,
+        [shape(hid_count, channels), shape(*pay_shape, dtype=bf16), block_bf16],
+        [anywhere] + [vmem] * 10,
+        out_specs=[vmem] * 2 + [anywhere],
+        scratch=[pltpu.VMEM((2 * hid_count, rows), bf16), pltpu.VMEM((rows, hid_count), f32)],
+        aliases={0: 2},
+    )(edge, feats[:rows], first_weight, x0, c0, second_weight, rate_row, front, back, featt, bias)
     far = move(edge, [(0, 2), (shards - 1, shards - 3)])
 
-    own, send = call(
-        functools.partial(own_kernel, rows, shards, channels, blocks, width), "own_pair", 8,
-        [shape(hid_count, channels), shape(*pay_shape, dtype=bf16)],
-        [anywhere] * 2 + [vmem] * 8,
-        scratch=[
-            pltpu.VMEM((2 * hid_count, seq_len), bf16), pltpu.VMEM((seq_len, hid_count), f32),
-            pltpu.VMEM((rows, hid_count), f32), pltpu.SemaphoreType.DMA((2,)),
-        ],
-    )(trans, slope, x0, c0, second_weight, rate_row, front, back, featt, bias)
-    come = move(send, inward)
-
-    conv, corr, ahead, sums, first = call(
+    conv, corr, ahead, sums, first, send = call(
         looped(
             functools.partial(near_kernel, rows, shards),
-            (None, ROWS, ROWS, ROWS, ROWS, CUBE, ROWS, ROWS, None, None, None, None, None, ROWS, ROWS, ROWS, ROWS, ROWS),
+            (None, None) + (ROWS,) * 4 + (CUBE, ROWS, ROWS) + (None,) * 5 + (ROWS,) * 5,
             blocks, width,
         ),
         "near_blocks", 20,
-        [block_f32] * 3 + [shape(hid_count, channels), shape(feat_count, hid_count)],
-        [smem] + [vmem] * 13,
+        [block_f32] * 3
+        + [shape(hid_count, channels), shape(feat_count, hid_count), shape(*pay_shape, dtype=bf16)],
+        [anywhere, smem] + [vmem] * 13,
+        out_specs=[vmem] * 5 + [anywhere],
         scratch=[
             pltpu.VMEM((4, double, width), f32),
             pltpu.VMEM((3, double, width), bf16),
@@ -713,7 +722,10 @@
             pltpu.VMEM((shards - 1, double, width), bf16),
             pltpu.VMEM(((shards - 1) * rows, hid_count), f32),
         ],
-    )(rank, x0, c0, x1, c1, spec, second_weight, rate_row, front, back, trans, featt, slope, own)
+        aliases={0: 5},
+    )(send, rank, x0, c0, x1, c1, spec, second_weight, rate_row, front, back, trans, featt, slope, own)
+
+    come = move(send, inward)
 
     part, late = call(
         looped(

time: 71.8 us -> 72 us (level)
  waiting for transfers between devices: 16 us -> 18.2 us
  local copies, waits for them, and re-layouts: 1.93 us -> 0.11 us
    ppermute x8, waiting for transfers between devices: 12.6 us -> 14.8 us  [move(): return lax.ppermute(array, 'ctx', pairs)]
    unnamed x32 -> x36, local copies, waits for them, and re-layouts: 1.93 us -> 0.11 us
  transfers between devices with their start and end apart: 10 -> 10, of which waited for: 4 -> 6; matrix products, arithmetic and copies ran while one was open for 0% -> 0% of each run, Pallas kernels for 42% -> 42%
where the time goes in v7:
time: 72 us; the launch traced here: 71.6 us
  Pallas kernels  33.4 us (46%)
  starting transfers between devices  18.9 us (26%)
  waiting for transfers between devices  18.2 us (25%)
  between operations  1.05 us (1%)
    ppermute x8, starting transfers between devices, move(): return lax.ppermute(array, 'ctx', pairs)  17.3 us
    ppermute x8, waiting for transfers between devices, move(): return lax.ppermute(array, 'ctx', pairs)  14.8 us
    pallas_call x1, Pallas kernels, few_shards_body(): call(functools.partial(filters_kernel, rows, shards, blocks, width), 'fil...  9.32 us
    pallas_call x1, Pallas kernels, few_shards_body(): call(looped(functools.partial(near_kernel, rows, shards), (None, None) +...  9.19 us
    pallas_call x1, Pallas kernels, few_shards_body(): call(functools.partial(own_kernel, rows, shards, channels, blocks, width)...  4.15 us
    ppermute x2, waiting for transfers between devices, few_shards_body(): lax.ppermute(first, ('ch', 'sub'), [(i, i ^ bit) for i in range(group)])  3.4 us
    pallas_call x1, Pallas kernels, few_shards_body(): pl.pallas_call(products_kernel, grid=(rows // row_step,), in_specs=[smem]...  2.62 us
    pallas_call x1, Pallas kernels, few_shards_body(): call(looped(functools.partial(far_kernel, rows), (None, ROWS, (slice(2, 4...  2.58 us
  transfers between devices with their start and end apart: 10, of which 6 were waited for; matrix products, arithmetic and copies ran while one was open for 0% of the time, Pallas kernels for 42%

profile of v7, /device:TPU:0, one launch (start us, length us, event | category | flops | bytes accessed | tf_op | source)
XLA Modules:
  0.0 71.6 jit_solution(4678402579382711377)
XLA Ops:
  0.6 2.6 %products.1 = (bf16[128,2048]{1,0:T(8,128)(2,1)}, bf16[128,2048]{1,0:T(8,128)(2,1)}, bf16[128,2048]{1,0:T(8,128)(2,1)}, f32[1,2048]{1,0:T(1,128)}) custom-call(s32[1]{0:T(128)} %bitcast.rank_ref.refs_1_.refs_0_, bf16[128,2048]{1,0:T(8,128)(2,1)} %refs_1_.3, bf16[128,2048]{1,0:T(8,128)(2,1)} %refs_2_.3, bf16[128,2048]{1,0:T(8,128)(2,1)} %refs_3_.2, ...), custom_call_target="tpu_custom_call" | custom-call | tf_op jit(solution)/shard_map/products/pallas_call | solution.py:667
  3.3 0.0 copy-start.6
  3.3 0.0 copy-start.7
  3.3 0.0 copy-start.10
  3.3 0.0 copy-start.12
  3.3 0.0 copy-start.13
  3.3 0.0 copy-start.14
  3.3 0.0 copy-start.15
  3.3 0.0 copy-start.16
  3.4 0.0 copy-start.17
  3.4 5.1 %collective-permute-start = (bf16[128,2048]{1,0:T(8,128)(2,1)}, bf16[128,2048]{1,0:T(8,128)(2,1)S(1)}, u32[]{:S(2)}, u32[]{:S(2)}) collective-permute-start(bf16[128,2048]{1,0:T(8,128)(2,1)} %get-tuple-element.35.source_ref.refs_2_), channel_id=1, source_target_pairs={{0,4},{4,8},{8,12},{1,5},{5,9},{9,13},{2,6},{6,10},{10,14},{3,7},{... | collective-permute-start | bytes 1572872 | tf_op jit(solution)/shard_map/ppermute | solution.py:654
  8.5 1.3 %collective-permute-start.1 = (bf16[128,2048]{1,0:T(8,128)(2,1)}, bf16[128,2048]{1,0:T(8,128)(2,1)S(1)}, u32[]{:S(2)}, u32[]{:S(2)}) collective-permute-start(bf16[128,2048]{1,0:T(8,128)(2,1)} %get-tuple-element.36.cotan_ref.refs_3_), channel_id=1, source_target_pairs={{4,0},{8,4},{12,8},{5,1},{9,5},{13,9},{6,2},{10,6},{14,10},{7,3},{... | collective-permute-start | bytes 1572872 | tf_op jit(solution)/shard_map/ppermute | solution.py:654
  9.8 9.3 %filters.1 = (bf16[4,256,2048]{2,1,0:T(8,128)(2,1)}, bf16[128,512]{1,0:T(8,128)(2,1)}, f32[512,64]{1,0:T(8,128)}, bf16[128,2048]{1,0:T(8,128)(2,1)}) custom-call(f32[512,32]{1,0:T(8,128)} %constant.15.clone.refs_0_, f32[32,64]{1,0:T(8,128)} %first_ref.1, f32[64,2048]{1,0:T(8,128)} %refs_5_.1, f32[1,2048]{1,0:T(1,128)} %bitcast.5, ...), custom_call_target="tpu_custom_call", output_to_operand_aliasing={{3}: (5, {})} | custom-call | flops 2147483648 | bytes 262144 | tf_op jit(solution)/shard_map/filters/pallas_call | solution.py:679
  19.1 0.0 copy-start
  19.1 0.0 copy-start.8
  19.1 0.0 copy-start.9
  19.1 0.0 copy-done.5
  19.1 0.0 copy-done.6
  19.2 0.0 copy-done.7
  19.2 0.0 copy-done.10
  19.2 0.0 copy-done.12
  19.2 0.0 copy-done.13
  19.2 0.0 copy-done.14
  19.2 0.0 copy-done.15
  19.2 0.0 copy-done.16
  19.2 0.0 copy-done.17
  19.2 4.2 %own_pair.1 = (f32[64,2048]{1,0:T(8,128)S(1)}, bf16[64,2304]{1,0:T(8,128)(2,1)S(1)}, bf16[128,2048]{1,0:T(8,128)(2,1)}) custom-call(bf16[128,2048]{1,0:T(8,128)(2,1)} %get-tuple-element.34.passed, f32[128,32]{1,0:T(8,128)S(1)} %copy-done.17, f32[32,64]{1,0:T(8,128)S(1)} %copy-done.16, ...), custom_call_target="tpu_custom_call", output_to_operand_aliasing={{2}: (0, {})} | custom-call | flops 2147483648 | bytes 262144 | tf_op jit(solution)/shard_map/own_pair/pallas_call | solution.py:697
  23.4 5.6 %collective-permute-start.2 = (bf16[128,2048]{1,0:T(8,128)(2,1)}, bf16[128,2048]{1,0:T(8,128)(2,1)S(1)}, u32[]{:S(2)}, u32[]{:S(2)}) collective-permute-start(bf16[128,2048]{1,0:T(8,128)(2,1)} %get-tuple-element.45), channel_id=1, source_target_pairs={{0,8},{12,4},{1,9},{13,5},{2,10},{14,6},{3,11},{15,7},{16,24},{28,... | collective-permute-start | bytes 1572872 | tf_op jit(solution)/shard_map/ppermute | solution.py:654
  28.9 0.0 collective-permute-done.refs_4_.refs_2_
  29.0 0.0 collective-permute-done.1.refs_5_.refs_3_
  29.0 0.0 copy-done
  29.0 0.0 copy-done.8
  29.0 0.0 copy-done.9
  29.0 9.2 %near_blocks.1 = (f32[128,2048]{1,0:T(8,128)S(1)}, f32[128,2048]{1,0:T(8,128)S(1)}, f32[128,2048]{1,0:T(8,128)S(1)}, f32[64,2048]{1,0:T(8,128)S(1)}, f32[32,64]{1,0:T(8,128)S(1)}, /*index=5*/bf16[64,2304]{1,0:T(8,128)(2,1)S(1)}) custom-call(bf16[64,2304]{1,0:T(8,128)(2,1)S(1)} %get-tuple-element.38.refs_0_, ...), custom_call_target="tpu_custom_call", output_to_operand_aliasing={{5}: (0, {})} | custom-call | flops 5368709120 | bytes 262144 | tf_op jit(solution)/shard_map/near_blocks/pallas_call | solution.py:707
  38.2 1.3 %collective-permute-start.4 = (bf16[64,2304]{1,0:T(8,128)(2,1)S(1)}, bf16[64,2304]{1,0:T(8,128)(2,1)S(1)}, u32[]{:S(2)}, u32[]{:S(2)}) collective-permute-start(bf16[64,2304]{1,0:T(8,128)(2,1)S(1)} %get-tuple-element.54.refs_14_), channel_id=1, source_target_pairs={{0,4},{12,8},{1,5},{13,9},{2,6},{14,10},{3,7},{15,11},{16,20},{28,... | collective-permute-start | bytes 884744 | tf_op jit(solution)/shard_map/ppermute | solution.py:654
  39.5 1.1 %collective-permute-done.2.refs_1_.refs_4_ = bf16[128,2048]{1,0:T(8,128)(2,1)S(1)} collective-permute-done((bf16[128,2048]{1,0:T(8,128)(2,1)}, bf16[128,2048]{1,0:T(8,128)(2,1)S(1)}, u32[]{:S(2)}, u32[]{:S(2)}) %collective-permute-start.2) | collective-permute-done | bytes 524320 | tf_op jit(solution)/shard_map/ppermute | solution.py:654
  40.6 2.6 %far_block.1 = (bf16[128,2048]{1,0:T(8,128)(2,1)S(1)}, f32[128,2048]{1,0:T(8,128)S(1)}) custom-call(s32[1]{0:T(128)} %bitcast.rank_ref.refs_1_.refs_0_, bf16[128,2048]{1,0:T(8,128)(2,1)S(1)} %collective-permute-done.2.refs_1_.refs_4_, bf16[4,256,2048]{2,1,0:T(8,128)(2,1)S(1)} %copy-done, bf16[256,256]{1,0:T(8,128)(2,1)S(1)} %copy-done.6, ...), custom_call_target="tpu_custom_call" | custom-call | flops 268435456 | bytes 262144 | tf_op jit(solution)/shard_map/far_block/pallas_call | solution.py:730
  43.2 0.0 copy-start.1
  43.2 0.0 copy-start.2
  43.2 0.0 copy-start.3
  43.2 0.0 copy-start.4
  43.3 0.0 copy-start.11
  43.3 1.4 %collective-permute-start.3 = (bf16[128,2048]{1,0:T(8,128)(2,1)S(1)}, bf16[128,2048]{1,0:T(8,128)(2,1)S(1)}, u32[]{:S(2)}, u32[]{:S(2)}) collective-permute-start(bf16[128,2048]{1,0:T(8,128)(2,1)S(1)} %get-tuple-element.48), channel_id=1, source_target_pairs={{4,0},{8,12},{5,1},{9,13},{6,2},{10,14},{7,3},{11,15},{20,16},{24,... | collective-permute-start | bytes 1572872 | tf_op jit(solution)/shard_map/ppermute | solution.py:654
  44.7 1.3 %collective-permute-done.4.refs_16_ = bf16[64,2304]{1,0:T(8,128)(2,1)S(1)} collective-permute-done((bf16[64,2304]{1,0:T(8,128)(2,1)S(1)}, bf16[64,2304]{1,0:T(8,128)(2,1)S(1)}, u32[]{:S(2)}, u32[]{:S(2)}) %collective-permute-start.4) | collective-permute-done | bytes 294944 | tf_op jit(solution)/shard_map/ppermute | solution.py:654
  46.0 2.5 %last_pair.1 = (bf16[64,2304]{1,0:T(8,128)(2,1)S(1)}, f32[32,64]{1,0:T(8,128)S(1)}) custom-call(f32[128,2048]{1,0:T(8,128)S(1)} %get-tuple-element.47.refs_8_.refs_0_, s32[1]{0:T(128)} %bitcast.rank_ref.refs_1_.refs_0_, bf16[128,2048]{1,0:T(8,128)(2,1)S(1)} %collective-permute-done.refs_4_.refs_2_, ...), custom_call_target="tpu_custom_call" | custom-call | flops 268435456 | bytes 262144 | tf_op jit(solution)/shard_map/last_pair/pallas_call | solution.py:742
  48.6 0.7 collective-permute-start.5
  49.3 0.1 collective-permute-start.6
  49.3 1.2 %collective-permute-done.6 = f32[32,64]{1,0:T(8,128)S(1)} collective-permute-done((f32[32,64]{1,0:T(8,128)S(1)}, f32[32,64]{1,0:T(8,128)S(1)}, u32[]{:S(2)}, u32[]{:S(2)}) %collective-permute-start.6) | collective-permute-done | bytes 8224 | tf_op jit(solution)/shard_map/ppermute | solution.py:757
  50.5 1.5 %collective-permute-start.7 = (f32[32,64]{1,0:T(8,128)S(1)}, f32[32,64]{1,0:T(8,128)S(1)}, u32[]{:S(2)}, u32[]{:S(2)}) collective-permute-start(f32[32,64]{1,0:T(8,128)S(1)} %add.6), channel_id=1, source_target_pairs={{0,2},{1,3},{2,0},{3,1},{4,6},{5,7},{6,4},{7,5},{8,10},{9,11},{10,... | collective-permute-start | bytes 24584 | tf_op jit(solution)/shard_map/ppermute | solution.py:757
  52.0 2.2 %collective-permute-done.7 = f32[32,64]{1,0:T(8,128)S(1)} collective-permute-done((f32[32,64]{1,0:T(8,128)S(1)}, f32[32,64]{1,0:T(8,128)S(1)}, u32[]{:S(2)}, u32[]{:S(2)}) %collective-permute-start.7) | collective-permute-done | bytes 8224 | tf_op jit(solution)/shard_map/ppermute | solution.py:757
  54.3 0.7 collective-permute-start.8
  54.9 0.0 collective-permute-done.8.first_come_ref
  54.9 2.1 %collective-permute-done.3.refs_9_.part_ref = bf16[128,2048]{1,0:T(8,128)(2,1)S(1)} collective-permute-done((bf16[128,2048]{1,0:T(8,128)(2,1)S(1)}, bf16[128,2048]{1,0:T(8,128)(2,1)S(1)}, u32[]{:S(2)}, u32[]{:S(2)}) %collective-permute-start.3) | collective-permute-done | bytes 524320 | tf_op jit(solution)/shard_map/ppermute | solution.py:654
  57.0 0.0 collective-permute-done.5.come_ref
  57.0 0.1 total.1.own_ref
  57.1 1.3 %collective-permute-start.9 = (bf16[64,2304]{1,0:T(8,128)(2,1)S(1)}, bf16[64,2304]{1,0:T(8,128)(2,1)S(1)}, u32[]{:S(2)}, u32[]{:S(2)}) collective-permute-start(bf16[64,2304]{1,0:T(8,128)(2,1)S(1)} %total.1.own_ref), channel_id=1, source_target_pairs={{4,0},{8,12},{5,1},{9,13},{6,2},{10,14},{7,3},{11,15},{20,16},{24,... | collective-permute-start | bytes 884744 | tf_op jit(solution)/shard_map/ppermute | solution.py:654
  58.4 0.0 copy-done.1
  58.4 0.0 copy-done.2
  58.4 0.0 copy-done.3
  58.4 0.0 copy-done.4
  58.4 0.0 copy-done.11
  58.4 2.1 %gates.1 = (bf16[128,2048]{1,0:T(8,128)(2,1)}, bf16[128,2048]{1,0:T(8,128)(2,1)}, bf16[128,2048]{1,0:T(8,128)(2,1)}) custom-call(s32[1]{0:T(128)} %bitcast.rank_ref.refs_1_.refs_0_, bf16[128,2048]{1,0:T(8,128)(2,1)S(1)} %copy-done.1, bf16[128,2048]{1,0:T(8,128)(2,1)S(1)} %copy-done.2, bf16[128,2048]{1,0:T(8,128)(2,1)S(1)} %copy-done.3, ...), custom_call_target="tpu_custom_call" | custom-call | bytes 262144 | tf_op jit(solution)/shard_map/gates/pallas_call | solution.py:767
  60.5 10.3 %collective-permute-done.9.come_ref = bf16[64,2304]{1,0:T(8,128)(2,1)S(1)} collective-permute-done((bf16[64,2304]{1,0:T(8,128)(2,1)S(1)}, bf16[64,2304]{1,0:T(8,128)(2,1)S(1)}, u32[]{:S(2)}, u32[]{:S(2)}) %collective-permute-start.9) | collective-permute-done | bytes 294944 | tf_op jit(solution)/shard_map/ppermute | solution.py:654
  70.8 0.9 %finish.1 = (f32[64,2048]{1,0:T(8,128)}, f32[32,64]{1,0:T(8,128)}, f32[1,2048]{1,0:T(1,128)}) custom-call(s32[1]{0:T(128)} %bitcast.rank_ref.refs_1_.refs_0_, bf16[64,2304]{1,0:T(8,128)(2,1)S(1)} %total.1.own_ref, bf16[64,2304]{1,0:T(8,128)(2,1)S(1)} %collective-permute-done.9.come_ref), custom_call_target="tpu_custom_call" | custom-call | bytes 262144 | tf_op jit(solution)/shard_map/finish/pallas_call | solution.py:777
  (3 shorter events, 0.0 us)
Async XLA Ops:
  3.3 15.9 %copy-start.5 = (f32[64,2048]{1,0:T(8,128)S(1)}, f32[64,2048]{1,0:T(8,128)}, u32[]{:S(2)}) copy-start(f32[64,2048]{1,0:T(8,128)} %refs_5_.1) | copy-start | bytes 1572868
  3.3 15.9 %copy-start.6 = (bf16[256,256]{1,0:T(8,128)(2,1)S(1)}, bf16[256,256]{1,0:T(8,128)(2,1)}, u32[]{:S(2)}) copy-start(bf16[256,256]{1,0:T(8,128)(2,1)} %constant.16.clone.refs_4_.front_ref.refs_9_.refs_3_.refs_7_) | copy-start | bytes 393220
  3.3 15.9 %copy-start.7 = (bf16[256,256]{1,0:T(8,128)(2,1)S(1)}, bf16[256,256]{1,0:T(8,128)(2,1)}, u32[]{:S(2)}) copy-start(bf16[256,256]{1,0:T(8,128)(2,1)} %constant.18.clone.back_ref.refs_10_.refs_4_.refs_8_) | copy-start | bytes 393220
  3.3 15.9 %copy-start.10 = (f32[32,512]{1,0:T(8,128)S(1)}, f32[32,512]{1,0:T(8,128)}, u32[]{:S(2)}) copy-start(f32[32,512]{1,0:T(8,128)} %constant.19.clone.featt_ref.refs_12_.refs_10_) | copy-start | bytes 196612
  3.3 15.9 %copy-start.12 = (f32[2048]{0:T(1024)S(1)}, f32[2048]{0:T(1024)}, u32[]{:S(2)}) copy-start(f32[2048]{0:T(1024)} %param.20) | copy-start | bytes 24580
  3.3 15.9 %copy-start.13 = (f32[1,2048]{1,0:T(1,128)S(1)}, f32[1,2048]{1,0:T(1,128)}, u32[]{:S(2)}) copy-start(f32[1,2048]{1,0:T(1,128)} %get-tuple-element.37.bias_ref.refs_15_) | copy-start | bytes 24580
  3.3 15.9 %copy-start.14 = (bf16[128,2048]{1,0:T(8,128)(2,1)S(1)}, bf16[128,2048]{1,0:T(8,128)(2,1)}, u32[]{:S(2)}) copy-start(bf16[128,2048]{1,0:T(8,128)(2,1)} %get-tuple-element.35.source_ref.refs_2_) | copy-start | bytes 1572868
  3.3 15.9 %copy-start.15 = (bf16[128,2048]{1,0:T(8,128)(2,1)S(1)}, bf16[128,2048]{1,0:T(8,128)(2,1)}, u32[]{:S(2)}) copy-start(bf16[128,2048]{1,0:T(8,128)(2,1)} %get-tuple-element.36.cotan_ref.refs_3_) | copy-start | bytes 1572868
  3.3 15.9 %copy-start.16 = (f32[32,64]{1,0:T(8,128)S(1)}, f32[32,64]{1,0:T(8,128)}, u32[]{:S(2)}) copy-start(f32[32,64]{1,0:T(8,128)} %first_ref.1) | copy-start | bytes 24580
  3.4 15.9 %copy-start.17 = (f32[128,32]{1,0:T(8,128)S(1)}, f32[128,32]{1,0:T(8,128)}, u32[]{:S(2)}) copy-start(f32[128,32]{1,0:T(8,128)} %constant.17.clone.feats_ref) | copy-start | bytes 49156
  3.4 25.6 %collective-permute-start = (bf16[128,2048]{1,0:T(8,128)(2,1)}, bf16[128,2048]{1,0:T(8,128)(2,1)S(1)}, u32[]{:S(2)}, u32[]{:S(2)}) collective-permute-start(bf16[128,2048]{1,0:T(8,128)(2,1)} %get-tuple-element.35.source_ref.refs_2_), channel_id=1, source_target_pairs={{0,4},{4,8},{8,12},{1,5},{5,9},{9,13},{2,6},{6,10},{10,14},{3,7},{... | collective-permute-start | bytes 1572872 | tf_op jit(solution)/shard_map/ppermute | solution.py:654
  8.5 20.5 %collective-permute-start.1 = (bf16[128,2048]{1,0:T(8,128)(2,1)}, bf16[128,2048]{1,0:T(8,128)(2,1)S(1)}, u32[]{:S(2)}, u32[]{:S(2)}) collective-permute-start(bf16[128,2048]{1,0:T(8,128)(2,1)} %get-tuple-element.36.cotan_ref.refs_3_), channel_id=1, source_target_pairs={{4,0},{8,4},{12,8},{5,1},{9,5},{13,9},{6,2},{10,6},{14,10},{7,3},{... | collective-permute-start | bytes 1572872 | tf_op jit(solution)/shard_map/ppermute | solution.py:654
  19.1 9.9 %copy-start = (bf16[4,256,2048]{2,1,0:T(8,128)(2,1)S(1)}, bf16[4,256,2048]{2,1,0:T(8,128)(2,1)}, u32[]{:S(2)}) copy-start(bf16[4,256,2048]{2,1,0:T(8,128)(2,1)} %get-tuple-element.39.refs_6_.refs_2_) | copy-start | bytes 12582916
  19.1 9.9 %copy-start.8 = (f32[512,64]{1,0:T(8,128)S(1)}, f32[512,64]{1,0:T(8,128)}, u32[]{:S(2)}) copy-start(f32[512,64]{1,0:T(8,128)} %get-tuple-element.41.refs_13_.refs_11_) | copy-start | bytes 393220
  19.1 9.9 %copy-start.9 = (bf16[128,512]{1,0:T(8,128)(2,1)S(1)}, bf16[128,512]{1,0:T(8,128)(2,1)}, u32[]{:S(2)}) copy-start(bf16[128,512]{1,0:T(8,128)(2,1)} %get-tuple-element.40.refs_11_.refs_9_) | copy-start | bytes 393220
  23.4 17.2 %collective-permute-start.2 = (bf16[128,2048]{1,0:T(8,128)(2,1)}, bf16[128,2048]{1,0:T(8,128)(2,1)S(1)}, u32[]{:S(2)}, u32[]{:S(2)}) collective-permute-start(bf16[128,2048]{1,0:T(8,128)(2,1)} %get-tuple-element.45), channel_id=1, source_target_pairs={{0,8},{12,4},{1,9},{13,5},{2,10},{14,6},{3,11},{15,7},{16,24},{28,... | collective-permute-start | bytes 1572872 | tf_op jit(solution)/shard_map/ppermute | solution.py:654
  38.2 7.8 %collective-permute-start.4 = (bf16[64,2304]{1,0:T(8,128)(2,1)S(1)}, bf16[64,2304]{1,0:T(8,128)(2,1)S(1)}, u32[]{:S(2)}, u32[]{:S(2)}) collective-permute-start(bf16[64,2304]{1,0:T(8,128)(2,1)S(1)} %get-tuple-element.54.refs_14_), channel_id=1, source_target_pairs={{0,4},{12,8},{1,5},{13,9},{2,6},{14,10},{3,7},{15,11},{16,20},{28,... | collective-permute-start | bytes 884744 | tf_op jit(solution)/shard_map/ppermute | solution.py:654
  43.2 15.2 %copy-start.1 = (bf16[128,2048]{1,0:T(8,128)(2,1)S(1)}, bf16[128,2048]{1,0:T(8,128)(2,1)}, u32[]{:S(2)}) copy-start(bf16[128,2048]{1,0:T(8,128)(2,1)} %refs_1_.3) | copy-start | bytes 1572868
  43.2 15.2 %copy-start.2 = (bf16[128,2048]{1,0:T(8,128)(2,1)S(1)}, bf16[128,2048]{1,0:T(8,128)(2,1)}, u32[]{:S(2)}) copy-start(bf16[128,2048]{1,0:T(8,128)(2,1)} %refs_2_.3) | copy-start | bytes 1572868
  43.2 15.2 %copy-start.3 = (bf16[128,2048]{1,0:T(8,128)(2,1)S(1)}, bf16[128,2048]{1,0:T(8,128)(2,1)}, u32[]{:S(2)}) copy-start(bf16[128,2048]{1,0:T(8,128)(2,1)} %refs_3_.2) | copy-start | bytes 1572868
  43.2 15.2 %copy-start.4 = (bf16[128,2048]{1,0:T(8,128)(2,1)S(1)}, bf16[128,2048]{1,0:T(8,128)(2,1)}, u32[]{:S(2)}) copy-start(bf16[128,2048]{1,0:T(8,128)(2,1)} %refs_4_.3) | copy-start | bytes 1572868
  43.3 15.2 %copy-start.11 = (f32[2048]{0:T(1024)S(1)}, f32[2048]{0:T(1024)}, u32[]{:S(2)}) copy-start(f32[2048]{0:T(1024)} %param.19) | copy-start | bytes 24580
  43.3 13.7 %collective-permute-start.3 = (bf16[128,2048]{1,0:T(8,128)(2,1)S(1)}, bf16[128,2048]{1,0:T(8,128)(2,1)S(1)}, u32[]{:S(2)}, u32[]{:S(2)}) collective-permute-start(bf16[128,2048]{1,0:T(8,128)(2,1)S(1)} %get-tuple-element.48), channel_id=1, source_target_pairs={{4,0},{8,12},{5,1},{9,13},{6,2},{10,14},{7,3},{11,15},{20,16},{24,... | collective-permute-start | bytes 1572872 | tf_op jit(solution)/shard_map/ppermute | solution.py:654
  48.6 8.4 %collective-permute-start.5 = (bf16[64,2304]{1,0:T(8,128)(2,1)S(1)}, bf16[64,2304]{1,0:T(8,128)(2,1)S(1)}, u32[]{:S(2)}, u32[]{:S(2)}) collective-permute-start(bf16[64,2304]{1,0:T(8,128)(2,1)S(1)} %get-tuple-element.55.own_ref), channel_id=1, source_target_pairs={{4,8},{8,4},{5,9},{9,5},{6,10},{10,6},{7,11},{11,7},{20,24},{24,20... | collective-permute-start | bytes 884744 | tf_op jit(solution)/shard_map/ppermute | solution.py:654
  49.3 1.2 %collective-permute-start.6 = (f32[32,64]{1,0:T(8,128)S(1)}, f32[32,64]{1,0:T(8,128)S(1)}, u32[]{:S(2)}, u32[]{:S(2)}) collective-permute-start(f32[32,64]{1,0:T(8,128)S(1)} %get-tuple-element.56), channel_id=1, source_target_pairs={{0,1},{1,0},{2,3},{3,2},{4,5},{5,4},{6,7},{7,6},{8,9},{9,8},{10,11... | collective-permute-start | bytes 24584 | tf_op jit(solution)/shard_map/ppermute | solution.py:757
  50.5 3.7 %collective-permute-start.7 = (f32[32,64]{1,0:T(8,128)S(1)}, f32[32,64]{1,0:T(8,128)S(1)}, u32[]{:S(2)}, u32[]{:S(2)}) collective-permute-start(f32[32,64]{1,0:T(8,128)S(1)} %add.6), channel_id=1, source_target_pairs={{0,2},{1,3},{2,0},{3,1},{4,6},{5,7},{6,4},{7,5},{8,10},{9,11},{10,... | collective-permute-start | bytes 24584 | tf_op jit(solution)/shard_map/ppermute | solution.py:757
  54.3 0.7 collective-permute-start.8
  57.1 13.7 %collective-permute-start.9 = (bf16[64,2304]{1,0:T(8,128)(2,1)S(1)}, bf16[64,2304]{1,0:T(8,128)(2,1)S(1)}, u32[]{:S(2)}, u32[]{:S(2)}) collective-permute-start(bf16[64,2304]{1,0:T(8,128)(2,1)S(1)} %total.1.own_ref), channel_id=1, source_target_pairs={{4,0},{8,12},{5,1},{9,13},{6,2},{10,14},{7,3},{11,15},{20,16},{24,... | collective-permute-start | bytes 884744 | tf_op jit(solution)/shard_map/ppermute | solution.py:654

commit v8 on v7

--- a/solution.py
+++ b/solution.py
@@ -331,38 +331,23 @@
     return jnp.concatenate(split(both[: hidden.shape[1]]), axis=0)
 
 
-def filters_kernel(rows, shards, blocks, width, *refs):
-    inputs, (spec_out, trans_ref, slope_ref), held, (spec_ref, hid_ref, sems, out_sems) = (
-        refs[:5], refs[6:9], refs[10:15], refs[15:]
-    )
-    feats_ref, first_ref, weight_ref, rate_ref, front_ref = held
-    copies = [pltpu.make_async_copy(far, near, sems.at[i]) for i, (far, near) in enumerate(zip(inputs, held))]
-    for copy in copies:
-        copy.start()
-    copies[0].wait()
-    copies[1].wait()
+def filters_kernel(
+    rows, shards, blocks, width, passed, feats_ref, first_ref, weight_ref, rate_ref, front_ref, spec_ref, trans_ref,
+    slope_ref, passing, hid_ref,
+):
+    del passed, passing
     hidden, slope = sin_cos(exact_dot(feats_ref[...], first_ref[...]))
     slope_ref[...] = slope
     high, low = split(hidden)
     hid_ref[...] = jnp.concatenate([high, high, low], axis=1)
     trans_ref[...] = turned_over(hidden, slope)
-    for copy in copies[2:]:
-        copy.wait()
-
-    def leaving(block):
-        cols = pl.ds(pl.multiple_of(block * width, width), width)
-        return pltpu.make_async_copy(spec_ref.at[:, :, cols], spec_out.at[:, :, cols], out_sems.at[block])
-
-    def strip(block, blocks, *views):
-        filter_strip(rows, shards, *views)
-        leaving(block).start()
-
-    looped(strip, (None, ROWS, ROWS, None, CUBE), blocks, width)(hid_ref, weight_ref, rate_ref, front_ref, spec_ref)
-    for block in range(blocks):
-        leaving(block).wait()
-
-
-def filter_strip(rows, shards, hid_ref, weight_ref, rate_ref, front_ref, spec_ref):
+    strips = looped(
+        functools.partial(filter_strip, rows, shards), (None, ROWS, ROWS, None, CUBE), blocks, width
+    )
+    strips(hid_ref, weight_ref, rate_ref, front_ref, spec_ref)
+
+
+def filter_strip(rows, shards, block, blocks, hid_ref, weight_ref, rate_ref, front_ref, spec_ref):
     scale = float(rows * shards) ** -0.5
     w_high, w_low = split(weight_ref[...])
     stacked = jnp.concatenate([w_high, w_low, w_high], axis=0)
@@ -383,27 +368,46 @@
         before = now
 
 
-def own_kernel(
-    rows, shards, channels, blocks, width, passed, feats_ref, first_ref, source_ref, cotan_ref, weight_ref, rate_ref,
-    front_ref, back_ref, featt_ref, bias_ref, sums_ref, send_ref, passing, trans_ref, acc_ref,
-):
-    del passed, passing
+def own_kernel(rows, shards, channels, blocks, width, *refs):
+    inputs, (sums_out, send_out), held = refs[:10], refs[11:13], refs[14:24]
+    sums_ref, send_ref, trans_ref, acc_ref, sems, out_sems = refs[24:]
+    (
+        feats_ref, first_ref, source_ref, cotan_ref, weight_ref, rate_ref, front_ref, back_ref, featt_ref, bias_ref
+    ) = held
+    copies = [pltpu.make_async_copy(far, near, sems.at[i]) for i, (far, near) in enumerate(zip(inputs, held))]
+    for copy in copies:
+        copy.start()
+    acc_ref[...] = jnp.zeros_like(acc_ref)
+    copies[0].wait()
+    copies[1].wait()
     hidden, slope = sin_cos(exact_dot(feats_ref[...], first_ref[...]))
     trans_ref[...] = turned_over(hidden, slope)
-    acc_ref[...] = jnp.zeros_like(acc_ref)
-    strips = looped(
-        functools.partial(own_strip, rows, shards),
-        (ROWS, ROWS, ROWS, ROWS, None, None, None, ROWS, ROWS, None), blocks, width,
-    )
-    strips(
+    for copy in copies[2:]:
+        copy.wait()
+
+    def leaving(block):
+        cols = pl.ds(pl.multiple_of(block * width, width), width)
+        return pltpu.make_async_copy(sums_ref.at[:, cols], sums_out.at[:, cols], out_sems.at[block])
+
+    def strip(block, blocks, *views):
+        own_strip(rows, shards, *views)
+        leaving(block).start()
+
+    kinds = (ROWS, ROWS, ROWS, ROWS, None, None, None, ROWS, ROWS, None)
+    looped(strip, kinds, blocks, width)(
         source_ref, cotan_ref, weight_ref, rate_ref, front_ref, back_ref, trans_ref, sums_ref, send_ref, acc_ref
     )
     first = exact_dot(featt_ref[:, :rows], acc_ref[...] * slope)
     put_side(send_ref, channels, fold(bias_ref[...]), first)
+    last = pltpu.make_async_copy(send_ref, send_out, out_sems.at[blocks])
+    last.start()
+    for block in range(blocks):
+        leaving(block).wait()
+    last.wait()
 
 
 def own_strip(
-    rows, shards, block, blocks, source_ref, cotan_ref, weight_ref, rate_ref, front_ref, back_ref, trans_ref, sums_ref,
+    rows, shards, source_ref, cotan_ref, weight_ref, rate_ref, front_ref, back_ref, trans_ref, sums_ref,
     send_ref, acc_ref,
 ):
     x0 = forward(front_ref, source_ref[...])
@@ -439,52 +443,65 @@
 
 
 def near_kernel(
-    rows, shards, block, blocks, passed, rank_ref, x0_ref, c0_ref, x1_ref, c1_ref, spec_ref, weight_ref, rate_ref, front_ref, back_ref,
-    trans_ref, featt_ref, slope_ref, own_ref, conv_ref, corr_ref, ahead_ref, sums_ref, first_ref, passing, fields, fast,
-    high_ref, low_ref, acc_ref,
+    rows, shards, block, blocks, passed, rank_ref, x0_ref, c0_ref, x1_ref, c1_ref, spec_ref, weight_ref, rate_ref,
+    front_ref, back_ref, trans_ref, featt_ref, slope_ref, own_ref, conv_ref, corr_ref, ahead_ref, sums_ref, first_ref,
+    passing, fields, fast, high_ref, low_ref, acc_ref,
 ):
     del passed, passing
     rank = rank_ref[0]
     count = shards - 1
+    lower = rank == 1
+    inner = jnp.logical_and(rank > 0, rank < shards - 1)
+    upper = jnp.where(rank == 2, 1.0, 0.0).astype(f32)
+    side = jnp.where(rank == 2, 1.0, -1.0).astype(f32)
 
     @pl.when(block == 0)
     def _():
         acc_ref[...] = jnp.zeros_like(acc_ref)
 
-    lower = rank == 1
-    upper = jnp.where(rank == 2, 1.0, 0.0).astype(f32)
-    below_top = jnp.where(rank == shards - 1, 0.0, 1.0).astype(f32)
-    side = jnp.where(rank == 2, 1.0, -1.0).astype(f32)
     for index, ref in enumerate((x0_ref, c0_ref, x1_ref, c1_ref)):
         fields[index] = forward(front_ref, ref[...])
     for re, im, sign in row_groups(rows):
         x0, c0, x1, c1 = ((fields[i, re, :], fields[i, im, :]) for i in range(4))
-        w0, w1, w2 = ((spec_ref[i, re, :].astype(f32), spec_ref[i, im, :].astype(f32)) for i in range(3))
-        ahead = times((w2[0], w2[1] * side), choose(lower, c1, x1))
+        w0, w1 = ((spec_ref[i, re, :].astype(f32), spec_ref[i, im, :].astype(f32)) for i in range(2))
         for index, value in enumerate(
-            (plus(times(w0, x0), times(w1, x1)), plus(conj_times(w0, c0), conj_times(w1, c1)), ahead)
+            (plus(times(w0, x0), times(w1, x1)), plus(conj_times(w0, c0), conj_times(w1, c1)))
         ):
             fast[index, re, :] = value[0].astype(bf16)
             fast[index, im, :] = value[1].astype(bf16)
-        one = plus(scaled(conj_times(x1, c0), below_top), scaled(conj_times(x0, c1), upper))
-        two = conj_times(x1, c1)
-        for index, value in enumerate((turned(one, sign), plus(one, turned(two, sign)), two)):
-            for part, where in zip(value, (re, im)):
-                high_ref[index, where, :], low_ref[index, where, :] = split(part)
     conv_ref[...] = backward(back_ref, fast[0])
     corr_ref[...] = backward(back_ref, fast[1])
-    ahead_ref[...] = backward(back_ref, fast[2])
-    rate = rate_ref[...]
-    env = decay(rate, rows, float(rows * shards) ** -0.5)
-    parts = []
-    for lag in range(count):
-        grad = backward(back_ref, high_ref[lag], low_ref[lag])
-        parts.append(split(grad * (env * jnp.exp(rate * (-float(lag * rows))))))
-    m_high = jnp.concatenate([p[0] for p in parts], axis=0)
-    m_low = jnp.concatenate([p[1] for p in parts], axis=0)
-    sums_ref[...] = own_ref[...] + weight_sums(trans_ref[:, : count * rows], m_high, m_low)
-    w_high, w_low = split(weight_ref[...])
-    acc_ref[...] += hidden_sums(m_high, m_low, w_high, w_low)
+
+    @pl.when(jnp.logical_not(inner))
+    def _():
+        sums_ref[...] = own_ref[...]
+        ahead_ref[...] = jnp.zeros_like(ahead_ref)
+
+    @pl.when(inner)
+    def _():
+        for re, im, sign in row_groups(rows):
+            x0, c0, x1, c1 = ((fields[i, re, :], fields[i, im, :]) for i in range(4))
+            w2 = (spec_ref[2, re, :].astype(f32), spec_ref[2, im, :].astype(f32) * side)
+            ahead = times(w2, choose(lower, c1, x1))
+            fast[2, re, :] = ahead[0].astype(bf16)
+            fast[2, im, :] = ahead[1].astype(bf16)
+            one = plus(conj_times(x1, c0), scaled(conj_times(x0, c1), upper))
+            two = conj_times(x1, c1)
+            for index, value in enumerate((turned(one, sign), plus(one, turned(two, sign)), two)):
+                for part, where in zip(value, (re, im)):
+                    high_ref[index, where, :], low_ref[index, where, :] = split(part)
+        ahead_ref[...] = backward(back_ref, fast[2])
+        rate = rate_ref[...]
+        env = decay(rate, rows, float(rows * shards) ** -0.5)
+        parts = []
+        for lag in range(count):
+            grad = backward(back_ref, high_ref[lag], low_ref[lag])
+            parts.append(split(grad * (env * jnp.exp(rate * (-float(lag * rows))))))
+        m_high = jnp.concatenate([p[0] for p in parts], axis=0)
+        m_low = jnp.concatenate([p[1] for p in parts], axis=0)
+        sums_ref[...] = own_ref[...] + weight_sums(trans_ref[:, : count * rows], m_high, m_low)
+        w_high, w_low = split(weight_ref[...])
+        acc_ref[...] += hidden_sums(m_high, m_low, w_high, w_low)
 
     @pl.when(block == blocks - 1)
     def _():
@@ -676,33 +693,37 @@
     x1 = move(x0, up)
     c1 = move(c0, down)
 
-    spec, trans, slope, edge = call(
+    own_shapes = [
+        shape(rows, feat_count), shape(feat_count, hid_count), block_bf16, block_bf16, shape(hid_count, channels),
+        shape(1, channels), shape(double, double, dtype=bf16), shape(double, double, dtype=bf16),
+        shape(feat_count, seq_len), shape(1, channels), shape(hid_count, channels), shape(*pay_shape, dtype=bf16),
+    ]
+    own, send, edge = call(
+        functools.partial(own_kernel, rows, shards, channels, blocks, width), "own_pair", 8,
+        [shape(hid_count, channels), shape(*pay_shape, dtype=bf16), block_bf16],
+        [anywhere] * 11,
+        out_specs=[anywhere] * 3,
+        scratch=[pltpu.VMEM(s.shape, s.dtype) for s in own_shapes]
+        + [
+            pltpu.VMEM((2 * hid_count, rows), bf16), pltpu.VMEM((rows, hid_count), f32),
+            pltpu.SemaphoreType.DMA((10,)), pltpu.SemaphoreType.DMA((blocks + 1,)),
+        ],
+        aliases={10: 2},
+        limit=60,
+    )(feats[:rows], first_weight, x0, c0, second_weight, rate_row, front, back, featt, bias, edge)
+    far = move(edge, [(0, 2), (shards - 1, shards - 3)])
+
+    spec, trans, slope, send = call(
         functools.partial(filters_kernel, rows, shards, blocks, width), "filters", 8,
         [
             shape(shards, double, channels, dtype=bf16), shape(2 * hid_count, seq_len, dtype=bf16),
-            shape(seq_len, hid_count), block_bf16,
+            shape(seq_len, hid_count), shape(*pay_shape, dtype=bf16),
         ],
-        [anywhere] * 6,
-        out_specs=[anywhere] + [vmem] * 2 + [anywhere],
-        scratch=[
-            pltpu.VMEM((seq_len, feat_count), f32), pltpu.VMEM((feat_count, hid_count), f32),
-            pltpu.VMEM((hid_count, channels), f32), pltpu.VMEM((1, channels), f32), pltpu.VMEM((double, double), bf16),
-            pltpu.VMEM((shards, double, channels), bf16), pltpu.VMEM((seq_len, 3 * hid_count), bf16),
-            pltpu.SemaphoreType.DMA((5,)), pltpu.SemaphoreType.DMA((blocks,)),
-        ],
-        aliases={5: 3},
-        limit=60,
-    )(feats, first_weight, second_weight, rate_row, front, edge)
-
-    own, send, edge = call(
-        functools.partial(own_kernel, rows, shards, channels, blocks, width), "own_pair", 8,
-        [shape(hid_count, channels), shape(*pay_shape, dtype=bf16), block_bf16],
-        [anywhere] + [vmem] * 10,
-        out_specs=[vmem] * 2 + [anywhere],
-        scratch=[pltpu.VMEM((2 * hid_count, rows), bf16), pltpu.VMEM((rows, hid_count), f32)],
-        aliases={0: 2},
-    )(edge, feats[:rows], first_weight, x0, c0, second_weight, rate_row, front, back, featt, bias)
-    far = move(edge, [(0, 2), (shards - 1, shards - 3)])
+        [anywhere] + [vmem] * 5,
+        out_specs=[vmem] * 3 + [anywhere],
+        scratch=[pltpu.VMEM((seq_len, 3 * hid_count), bf16)],
+        aliases={0: 3},
+    )(send, feats, first_weight, second_weight, rate_row, front)
 
     conv, corr, ahead, sums, first, send = call(
         looped(

time: 72 us -> 74.1 us (1.029)
  Pallas kernels: 33.4 us -> 27.9 us
  starting transfers between devices: 18.9 us -> 24.3 us
  local copies, waits for them, and re-layouts: 0.11 us -> 2.02 us
    ppermute x8, starting transfers between devices: 17.3 us -> 22.7 us  [move(): return lax.ppermute(array, 'ctx', pairs)]
    pallas_call x1, Pallas kernels: 9.19 us -> 4.45 us  [few_shards_body(): call(looped(functools.partial(near_kernel, rows, shards), (None, None) +...]
    pallas_call x1, Pallas kernels: 9.32 us -> 6.51 us  [few_shards_body(): call(functools.partial(filters_kernel, rows, shards, blocks, width), 'fil...]
    pallas_call x1, Pallas kernels: 4.15 us -> 6.2 us  [few_shards_body(): call(functools.partial(own_kernel, rows, shards, channels, blocks, width)...]
    unnamed x36 -> x38, local copies, waits for them, and re-layouts: 0.11 us -> 2.02 us
  transfers between devices with their start and end apart: 10 -> 10, of which waited for: 6 -> 5; matrix products, arithmetic and copies ran while one was open for 0% -> 0% of each run, Pallas kernels for 42% -> 33%
where the time goes in v8:
time: 74.1 us; the launch traced here: 73.6 us
  Pallas kernels  27.9 us (38%)
  starting transfers between devices  24.3 us (33%)
  waiting for transfers between devices  18.4 us (25%)
  local copies, waits for them, and re-layouts  2.02 us (3%)
  between operations  1.04 us (1%)
    ppermute x8, starting transfers between devices, move(): return lax.ppermute(array, 'ctx', pairs)  22.7 us
    ppermute x8, waiting for transfers between devices, move(): return lax.ppermute(array, 'ctx', pairs)  15 us
    pallas_call x1, Pallas kernels, few_shards_body(): call(functools.partial(filters_kernel, rows, shards, blocks, width), 'fil...  6.51 us
    pallas_call x1, Pallas kernels, few_shards_body(): call(functools.partial(own_kernel, rows, shards, channels, blocks, width)...  6.2 us
    pallas_call x1, Pallas kernels, few_shards_body(): call(looped(functools.partial(near_kernel, rows, shards), (None, None) +...  4.45 us
    ppermute x2, waiting for transfers between devices, few_shards_body(): lax.ppermute(first, ('ch', 'sub'), [(i, i ^ bit) for i in range(group)])  3.41 us
    pallas_call x1, Pallas kernels, few_shards_body(): pl.pallas_call(products_kernel, grid=(rows // row_step,), in_specs=[smem]...  2.62 us
    pallas_call x1, Pallas kernels, few_shards_body(): call(looped(functools.partial(far_kernel, rows), (None, ROWS, (slice(2, 4...  2.62 us
  transfers between devices with their start and end apart: 10, of which 5 were waited for; matrix products, arithmetic and copies ran while one was open for 0% of the time, Pallas kernels for 33%

profile of v8, /device:TPU:0, one launch (start us, length us, event | category | flops | bytes accessed | tf_op | source)
XLA Modules:
  0.0 73.6 jit_solution(3937535250445948299)
XLA Ops:
  0.6 2.6 %products.1 = (bf16[128,2048]{1,0:T(8,128)(2,1)}, bf16[128,2048]{1,0:T(8,128)(2,1)}, bf16[128,2048]{1,0:T(8,128)(2,1)}, f32[1,2048]{1,0:T(1,128)}) custom-call(s32[1]{0:T(128)} %bitcast.rank_ref.refs_1_.refs_0_, bf16[128,2048]{1,0:T(8,128)(2,1)} %refs_1_.3, bf16[128,2048]{1,0:T(8,128)(2,1)} %refs_2_.1, bf16[128,2048]{1,0:T(8,128)(2,1)} %refs_3_.2, ...), custom_call_target="tpu_custom_call" | custom-call | tf_op jit(solution)/shard_map/products/pallas_call | solution.py:684
  3.3 0.0 copy-start.5
  3.3 0.0 copy-start.12
  3.3 0.0 copy-start.16
  3.3 0.0 copy-start.17
  3.3 5.1 %collective-permute-start = (bf16[128,2048]{1,0:T(8,128)(2,1)}, bf16[128,2048]{1,0:T(8,128)(2,1)S(1)}, u32[]{:S(2)}, u32[]{:S(2)}) collective-permute-start(bf16[128,2048]{1,0:T(8,128)(2,1)} %get-tuple-element.33.refs_2_), channel_id=1, source_target_pairs={{0,4},{4,8},{8,12},{1,5},{5,9},{9,13},{2,6},{6,10},{10,14},{3,7},{... | collective-permute-start | bytes 1572872 | tf_op jit(solution)/shard_map/ppermute | solution.py:671
  8.4 1.3 %collective-permute-start.1 = (bf16[128,2048]{1,0:T(8,128)(2,1)}, bf16[128,2048]{1,0:T(8,128)(2,1)S(1)}, u32[]{:S(2)}, u32[]{:S(2)}) collective-permute-start(bf16[128,2048]{1,0:T(8,128)(2,1)} %get-tuple-element.34.refs_3_), channel_id=1, source_target_pairs={{4,0},{8,4},{12,8},{5,1},{9,5},{13,9},{6,2},{10,6},{14,10},{7,3},{... | collective-permute-start | bytes 1572872 | tf_op jit(solution)/shard_map/ppermute | solution.py:671
  9.7 0.0 copy-start.10
  9.7 0.0 copy-start.14
  9.7 0.0 copy-start.15
  9.7 6.2 %own_pair.1 = (f32[64,2048]{1,0:T(8,128)}, bf16[64,2304]{1,0:T(8,128)(2,1)}, bf16[128,2048]{1,0:T(8,128)(2,1)}) custom-call(f32[128,32]{1,0:T(8,128)} %constant.15.clone.refs_0_, f32[32,64]{1,0:T(8,128)} %first_ref.1, bf16[128,2048]{1,0:T(8,128)(2,1)} %get-tuple-element.33.refs_2_, ...), custom_call_target="tpu_custom_call", output_to_operand_aliasing={{2}: (10, {})} | custom-call | flops 2147483648 | bytes 262144 | tf_op jit(solution)/shard_map/own_pair/pallas_call | solution.py:701
  16.0 0.0 copy-start.6
  16.0 5.7 %collective-permute-start.2 = (bf16[128,2048]{1,0:T(8,128)(2,1)}, bf16[128,2048]{1,0:T(8,128)(2,1)S(1)}, u32[]{:S(2)}, u32[]{:S(2)}) collective-permute-start(bf16[128,2048]{1,0:T(8,128)(2,1)} %get-tuple-element.45), channel_id=1, source_target_pairs={{0,8},{12,4},{1,9},{13,5},{2,10},{14,6},{3,11},{15,7},{16,24},{28,... | collective-permute-start | bytes 1572872 | tf_op jit(solution)/shard_map/ppermute | solution.py:671
  21.7 0.0 copy-done.4
  21.7 0.0 copy-done.5
  21.7 0.0 copy-done.12
  21.7 0.0 copy-done.16
  21.7 0.0 copy-done.17
  21.7 0.0 copy-start.7
  21.7 1.0 %copy-done.7 = bf16[64,2304]{1,0:T(8,128)(2,1)S(1)} copy-done((bf16[64,2304]{1,0:T(8,128)(2,1)S(1)}, bf16[64,2304]{1,0:T(8,128)(2,1)}, u32[]{:S(2)}) %copy-start.7) | copy-done | bytes 294936
  22.7 6.5 %filters.1 = (bf16[4,256,2048]{2,1,0:T(8,128)(2,1)S(1)}, bf16[128,512]{1,0:T(8,128)(2,1)S(1)}, f32[512,64]{1,0:T(8,128)S(1)}, bf16[64,2304]{1,0:T(8,128)(2,1)S(1)}) custom-call(bf16[64,2304]{1,0:T(8,128)(2,1)S(1)} %copy-done.7, f32[512,32]{1,0:T(8,128)S(1)} %copy-done.17, f32[32,64]{1,0:T(8,128)S(1)} %copy-done.16, ...), custom_call_target="tpu_custom_call", output_to_operand_aliasing={{3}: (0, {})} | custom-call | flops 2147483648 | bytes 262144 | tf_op jit(solution)/shard_map/filters/pallas_call | solution.py:716
  29.2 0.0 collective-permute-done.refs_4_.refs_2_
  29.2 0.0 collective-permute-done.1.refs_5_.refs_3_
  29.2 0.0 copy-done.10
  29.2 0.0 copy-done.14
  29.2 0.0 copy-done.15
  29.3 0.0 copy-done.6
  29.3 0.0 copy-done.18
  29.3 4.4 %near_blocks.1 = (f32[128,2048]{1,0:T(8,128)S(1)}, f32[128,2048]{1,0:T(8,128)S(1)}, f32[128,2048]{1,0:T(8,128)S(1)}, f32[64,2048]{1,0:T(8,128)S(1)}, f32[32,64]{1,0:T(8,128)S(1)}, /*index=5*/bf16[64,2304]{1,0:T(8,128)(2,1)S(1)}) custom-call(bf16[64,2304]{1,0:T(8,128)(2,1)S(1)} %get-tuple-element.38.refs_0_, ...), custom_call_target="tpu_custom_call", output_to_operand_aliasing={{5}: (0, {})} | custom-call | flops 5368709120 | bytes 262144 | tf_op jit(solution)/shard_map/near_blocks/pallas_call | solution.py:728
  33.7 0.0 copy-start.8
  33.7 0.0 copy-start.13
  33.8 6.6 %collective-permute-start.4 = (bf16[64,2304]{1,0:T(8,128)(2,1)S(1)}, bf16[64,2304]{1,0:T(8,128)(2,1)S(1)}, u32[]{:S(2)}, u32[]{:S(2)}) collective-permute-start(bf16[64,2304]{1,0:T(8,128)(2,1)S(1)} %get-tuple-element.54.refs_14_), channel_id=1, source_target_pairs={{0,4},{12,8},{1,5},{13,9},{2,6},{14,10},{3,7},{15,11},{16,20},{28,... | collective-permute-start | bytes 884744 | tf_op jit(solution)/shard_map/ppermute | solution.py:671
  40.3 0.0 collective-permute-done.2.refs_1_.refs_4_
  40.3 0.0 copy-start.11
  40.4 2.6 %far_block.1 = (bf16[128,2048]{1,0:T(8,128)(2,1)S(1)}, f32[128,2048]{1,0:T(8,128)S(1)}) custom-call(s32[1]{0:T(128)} %bitcast.rank_ref.refs_1_.refs_0_, bf16[128,2048]{1,0:T(8,128)(2,1)S(1)} %collective-permute-done.2.refs_1_.refs_4_, bf16[4,256,2048]{2,1,0:T(8,128)(2,1)S(1)} %get-tuple-element.39.refs_6_.refs_2_, bf16[256,256]{1,0:T(8,128)(2,1)S(1)} %copy-done.5, ...), custom_call_target="tpu_custom_call" | custom-call | flops 268435456 | bytes 262144 | tf_op jit(solution)/shard_map/far_block/pallas_call | solution.py:751
  43.0 0.0 copy-start
  43.0 0.0 copy-start.1
  43.0 0.0 copy-start.2
  43.0 0.0 copy-start.3
  43.0 1.4 %collective-permute-start.3 = (bf16[128,2048]{1,0:T(8,128)(2,1)S(1)}, bf16[128,2048]{1,0:T(8,128)(2,1)S(1)}, u32[]{:S(2)}, u32[]{:S(2)}) collective-permute-start(bf16[128,2048]{1,0:T(8,128)(2,1)S(1)} %get-tuple-element.48), channel_id=1, source_target_pairs={{4,0},{8,12},{5,1},{9,13},{6,2},{10,14},{7,3},{11,15},{20,16},{24,... | collective-permute-start | bytes 1572872 | tf_op jit(solution)/shard_map/ppermute | solution.py:671
  44.5 1.5 %collective-permute-done.4.refs_16_ = bf16[64,2304]{1,0:T(8,128)(2,1)S(1)} collective-permute-done((bf16[64,2304]{1,0:T(8,128)(2,1)S(1)}, bf16[64,2304]{1,0:T(8,128)(2,1)S(1)}, u32[]{:S(2)}, u32[]{:S(2)}) %collective-permute-start.4) | collective-permute-done | bytes 294944 | tf_op jit(solution)/shard_map/ppermute | solution.py:671
  46.0 0.0 copy-done.8
  46.0 0.0 copy-done.13
  46.0 1.0 %copy-done.9 = bf16[64,2304]{1,0:T(8,128)(2,1)S(1)} copy-done((bf16[64,2304]{1,0:T(8,128)(2,1)S(1)}, bf16[64,2304]{1,0:T(8,128)(2,1)}, u32[]{:S(2)}) %copy-start.9) | copy-done | bytes 294936
  47.0 2.5 %last_pair.1 = (bf16[64,2304]{1,0:T(8,128)(2,1)S(1)}, f32[32,64]{1,0:T(8,128)S(1)}) custom-call(f32[128,2048]{1,0:T(8,128)S(1)} %get-tuple-element.47.refs_8_.refs_0_, s32[1]{0:T(128)} %bitcast.rank_ref.refs_1_.refs_0_, bf16[128,2048]{1,0:T(8,128)(2,1)S(1)} %collective-permute-done.refs_4_.refs_2_, ...), custom_call_target="tpu_custom_call" | custom-call | flops 268435456 | bytes 262144 | tf_op jit(solution)/shard_map/last_pair/pallas_call | solution.py:763
  49.5 0.7 collective-permute-start.5
  50.2 0.1 collective-permute-start.6
  50.3 1.2 %collective-permute-done.6 = f32[32,64]{1,0:T(8,128)S(1)} collective-permute-done((f32[32,64]{1,0:T(8,128)S(1)}, f32[32,64]{1,0:T(8,128)S(1)}, u32[]{:S(2)}, u32[]{:S(2)}) %collective-permute-start.6) | collective-permute-done | bytes 8224 | tf_op jit(solution)/shard_map/ppermute | solution.py:778
  51.5 1.5 %collective-permute-start.7 = (f32[32,64]{1,0:T(8,128)S(1)}, f32[32,64]{1,0:T(8,128)S(1)}, u32[]{:S(2)}, u32[]{:S(2)}) collective-permute-start(f32[32,64]{1,0:T(8,128)S(1)} %add.6), channel_id=1, source_target_pairs={{0,2},{1,3},{2,0},{3,1},{4,6},{5,7},{6,4},{7,5},{8,10},{9,11},{10,... | collective-permute-start | bytes 24584 | tf_op jit(solution)/shard_map/ppermute | solution.py:778
  53.0 2.2 %collective-permute-done.7 = f32[32,64]{1,0:T(8,128)S(1)} collective-permute-done((f32[32,64]{1,0:T(8,128)S(1)}, f32[32,64]{1,0:T(8,128)S(1)}, u32[]{:S(2)}, u32[]{:S(2)}) %collective-permute-start.7) | collective-permute-done | bytes 8224 | tf_op jit(solution)/shard_map/ppermute | solution.py:778
  55.2 0.7 collective-permute-start.8
  55.9 0.0 collective-permute-done.8.first_come_ref
  55.9 2.0 %collective-permute-done.3.refs_9_.part_ref = bf16[128,2048]{1,0:T(8,128)(2,1)S(1)} collective-permute-done((bf16[128,2048]{1,0:T(8,128)(2,1)S(1)}, bf16[128,2048]{1,0:T(8,128)(2,1)S(1)}, u32[]{:S(2)}, u32[]{:S(2)}) %collective-permute-start.3) | collective-permute-done | bytes 524320 | tf_op jit(solution)/shard_map/ppermute | solution.py:671
  57.9 0.0 collective-permute-done.5.come_ref
  57.9 0.1 total.1.own_ref
  58.0 1.3 %collective-permute-start.9 = (bf16[64,2304]{1,0:T(8,128)(2,1)S(1)}, bf16[64,2304]{1,0:T(8,128)(2,1)S(1)}, u32[]{:S(2)}, u32[]{:S(2)}) collective-permute-start(bf16[64,2304]{1,0:T(8,128)(2,1)S(1)} %total.1.own_ref), channel_id=1, source_target_pairs={{4,0},{8,12},{5,1},{9,13},{6,2},{10,14},{7,3},{11,15},{20,16},{24,... | collective-permute-start | bytes 884744 | tf_op jit(solution)/shard_map/ppermute | solution.py:671
  59.3 0.0 copy-done.11
  59.3 0.0 copy-done
  59.3 0.0 copy-done.1
  59.3 0.0 copy-done.2
  59.3 0.0 copy-done.3
  59.3 2.1 %gates.1 = (bf16[128,2048]{1,0:T(8,128)(2,1)}, bf16[128,2048]{1,0:T(8,128)(2,1)}, bf16[128,2048]{1,0:T(8,128)(2,1)}) custom-call(s32[1]{0:T(128)} %bitcast.rank_ref.refs_1_.refs_0_, bf16[128,2048]{1,0:T(8,128)(2,1)S(1)} %copy-done, bf16[128,2048]{1,0:T(8,128)(2,1)S(1)} %copy-done.1, bf16[128,2048]{1,0:T(8,128)(2,1)S(1)} %copy-done.2, ...), custom_call_target="tpu_custom_call" | custom-call | bytes 262144 | tf_op jit(solution)/shard_map/gates/pallas_call | solution.py:788
  61.4 11.4 %collective-permute-done.9.come_ref = bf16[64,2304]{1,0:T(8,128)(2,1)S(1)} collective-permute-done((bf16[64,2304]{1,0:T(8,128)(2,1)S(1)}, bf16[64,2304]{1,0:T(8,128)(2,1)S(1)}, u32[]{:S(2)}, u32[]{:S(2)}) %collective-permute-start.9) | collective-permute-done | bytes 294944 | tf_op jit(solution)/shard_map/ppermute | solution.py:671
  72.8 0.9 %finish.1 = (f32[64,2048]{1,0:T(8,128)}, f32[32,64]{1,0:T(8,128)}, f32[1,2048]{1,0:T(1,128)}) custom-call(s32[1]{0:T(128)} %bitcast.rank_ref.refs_1_.refs_0_, bf16[64,2304]{1,0:T(8,128)(2,1)S(1)} %total.1.own_ref, bf16[64,2304]{1,0:T(8,128)(2,1)S(1)} %collective-permute-done.9.come_ref), custom_call_target="tpu_custom_call" | custom-call | bytes 262144 | tf_op jit(solution)/shard_map/finish/pallas_call | solution.py:798
  (5 shorter events, 0.0 us)
Async XLA Ops:
  3.3 18.4 %copy-start.4 = (f32[64,2048]{1,0:T(8,128)S(1)}, f32[64,2048]{1,0:T(8,128)}, u32[]{:S(2)}) copy-start(f32[64,2048]{1,0:T(8,128)} %refs_5_.1) | copy-start | bytes 1572868
  3.3 18.4 %copy-start.5 = (bf16[256,256]{1,0:T(8,128)(2,1)S(1)}, bf16[256,256]{1,0:T(8,128)(2,1)}, u32[]{:S(2)}) copy-start(bf16[256,256]{1,0:T(8,128)(2,1)} %constant.16.clone.refs_6_.front_ref.refs_9_.refs_3_.refs_7_) | copy-start | bytes 393220
  3.3 18.4 %copy-start.12 = (f32[2048]{0:T(1024)S(1)}, f32[2048]{0:T(1024)}, u32[]{:S(2)}) copy-start(f32[2048]{0:T(1024)} %param.20) | copy-start | bytes 24580
  3.3 18.4 %copy-start.16 = (f32[32,64]{1,0:T(8,128)S(1)}, f32[32,64]{1,0:T(8,128)}, u32[]{:S(2)}) copy-start(f32[32,64]{1,0:T(8,128)} %first_ref.1) | copy-start | bytes 24580
  3.3 18.4 %copy-start.17 = (f32[512,32]{1,0:T(8,128)S(1)}, f32[512,32]{1,0:T(8,128)}, u32[]{:S(2)}) copy-start(f32[512,32]{1,0:T(8,128)} %constant.19.clone.feats_ref) | copy-start | bytes 196612
  3.3 25.9 %collective-permute-start = (bf16[128,2048]{1,0:T(8,128)(2,1)}, bf16[128,2048]{1,0:T(8,128)(2,1)S(1)}, u32[]{:S(2)}, u32[]{:S(2)}) collective-permute-start(bf16[128,2048]{1,0:T(8,128)(2,1)} %get-tuple-element.33.refs_2_), channel_id=1, source_target_pairs={{0,4},{4,8},{8,12},{1,5},{5,9},{9,13},{2,6},{6,10},{10,14},{3,7},{... | collective-permute-start | bytes 1572872 | tf_op jit(solution)/shard_map/ppermute | solution.py:671
  8.4 20.8 %collective-permute-start.1 = (bf16[128,2048]{1,0:T(8,128)(2,1)}, bf16[128,2048]{1,0:T(8,128)(2,1)S(1)}, u32[]{:S(2)}, u32[]{:S(2)}) collective-permute-start(bf16[128,2048]{1,0:T(8,128)(2,1)} %get-tuple-element.34.refs_3_), channel_id=1, source_target_pairs={{4,0},{8,4},{12,8},{5,1},{9,5},{13,9},{6,2},{10,6},{14,10},{7,3},{... | collective-permute-start | bytes 1572872 | tf_op jit(solution)/shard_map/ppermute | solution.py:671
  9.7 19.5 %copy-start.10 = (f32[32,512]{1,0:T(8,128)S(1)}, f32[32,512]{1,0:T(8,128)}, u32[]{:S(2)}) copy-start(f32[32,512]{1,0:T(8,128)} %constant.18.clone.refs_8_.refs_12_.refs_10_) | copy-start | bytes 196612
  9.7 19.5 %copy-start.14 = (bf16[128,2048]{1,0:T(8,128)(2,1)S(1)}, bf16[128,2048]{1,0:T(8,128)(2,1)}, u32[]{:S(2)}) copy-start(bf16[128,2048]{1,0:T(8,128)(2,1)} %get-tuple-element.33.refs_2_) | copy-start | bytes 1572868
  9.7 19.5 %copy-start.15 = (bf16[128,2048]{1,0:T(8,128)(2,1)S(1)}, bf16[128,2048]{1,0:T(8,128)(2,1)}, u32[]{:S(2)}) copy-start(bf16[128,2048]{1,0:T(8,128)(2,1)} %get-tuple-element.34.refs_3_) | copy-start | bytes 1572868
  16.0 13.3 %copy-start.6 = (bf16[256,256]{1,0:T(8,128)(2,1)S(1)}, bf16[256,256]{1,0:T(8,128)(2,1)}, u32[]{:S(2)}) copy-start(bf16[256,256]{1,0:T(8,128)(2,1)} %constant.17.clone.refs_7_.refs_10_.refs_4_.refs_8_) | copy-start | bytes 393220
  16.0 24.4 %collective-permute-start.2 = (bf16[128,2048]{1,0:T(8,128)(2,1)}, bf16[128,2048]{1,0:T(8,128)(2,1)S(1)}, u32[]{:S(2)}, u32[]{:S(2)}) collective-permute-start(bf16[128,2048]{1,0:T(8,128)(2,1)} %get-tuple-element.45), channel_id=1, source_target_pairs={{0,8},{12,4},{1,9},{13,5},{2,10},{14,6},{3,11},{15,7},{16,24},{28,... | collective-permute-start | bytes 1572872 | tf_op jit(solution)/shard_map/ppermute | solution.py:671
  21.7 1.0 %copy-start.7 = (bf16[64,2304]{1,0:T(8,128)(2,1)S(1)}, bf16[64,2304]{1,0:T(8,128)(2,1)}, u32[]{:S(2)}) copy-start(bf16[64,2304]{1,0:T(8,128)(2,1)} %get-tuple-element.37.passed) | copy-start | bytes 884740
  22.7 6.6 %copy-start.18 = (f32[64,2048]{1,0:T(8,128)S(1)}, f32[64,2048]{1,0:T(8,128)}, u32[]{:S(2)}) copy-start(f32[64,2048]{1,0:T(8,128)} %get-tuple-element.42.refs_14_) | copy-start | bytes 1572868
  33.7 12.3 %copy-start.8 = (bf16[64,2304]{1,0:T(8,128)(2,1)}, bf16[64,2304]{1,0:T(8,128)(2,1)S(1)}, u32[]{:S(2)}) copy-start(bf16[64,2304]{1,0:T(8,128)(2,1)S(1)} %get-tuple-element.54.refs_14_) | copy-start | bytes 884740
  33.7 12.3 %copy-start.13 = (f32[1,2048]{1,0:T(1,128)S(1)}, f32[1,2048]{1,0:T(1,128)}, u32[]{:S(2)}) copy-start(f32[1,2048]{1,0:T(1,128)} %get-tuple-element.35.refs_9_.refs_15_) | copy-start | bytes 24580
  33.8 12.3 %collective-permute-start.4 = (bf16[64,2304]{1,0:T(8,128)(2,1)S(1)}, bf16[64,2304]{1,0:T(8,128)(2,1)S(1)}, u32[]{:S(2)}, u32[]{:S(2)}) collective-permute-start(bf16[64,2304]{1,0:T(8,128)(2,1)S(1)} %get-tuple-element.54.refs_14_), channel_id=1, source_target_pairs={{0,4},{12,8},{1,5},{13,9},{2,6},{14,10},{3,7},{15,11},{16,20},{28,... | collective-permute-start | bytes 884744 | tf_op jit(solution)/shard_map/ppermute | solution.py:671
  40.3 18.9 %copy-start.11 = (f32[2048]{0:T(1024)S(1)}, f32[2048]{0:T(1024)}, u32[]{:S(2)}) copy-start(f32[2048]{0:T(1024)} %param.19) | copy-start | bytes 24580
  43.0 16.3 %copy-start = (bf16[128,2048]{1,0:T(8,128)(2,1)S(1)}, bf16[128,2048]{1,0:T(8,128)(2,1)}, u32[]{:S(2)}) copy-start(bf16[128,2048]{1,0:T(8,128)(2,1)} %refs_1_.3) | copy-start | bytes 1572868
  43.0 16.3 %copy-start.1 = (bf16[128,2048]{1,0:T(8,128)(2,1)S(1)}, bf16[128,2048]{1,0:T(8,128)(2,1)}, u32[]{:S(2)}) copy-start(bf16[128,2048]{1,0:T(8,128)(2,1)} %refs_2_.1) | copy-start | bytes 1572868
  43.0 16.3 %copy-start.2 = (bf16[128,2048]{1,0:T(8,128)(2,1)S(1)}, bf16[128,2048]{1,0:T(8,128)(2,1)}, u32[]{:S(2)}) copy-start(bf16[128,2048]{1,0:T(8,128)(2,1)} %refs_3_.2) | copy-start | bytes 1572868
  43.0 16.3 %copy-start.3 = (bf16[128,2048]{1,0:T(8,128)(2,1)S(1)}, bf16[128,2048]{1,0:T(8,128)(2,1)}, u32[]{:S(2)}) copy-start(bf16[128,2048]{1,0:T(8,128)(2,1)} %refs_4_.4) | copy-start | bytes 1572868
  43.0 14.8 %collective-permute-start.3 = (bf16[128,2048]{1,0:T(8,128)(2,1)S(1)}, bf16[128,2048]{1,0:T(8,128)(2,1)S(1)}, u32[]{:S(2)}, u32[]{:S(2)}) collective-permute-start(bf16[128,2048]{1,0:T(8,128)(2,1)S(1)} %get-tuple-element.48), channel_id=1, source_target_pairs={{4,0},{8,12},{5,1},{9,13},{6,2},{10,14},{7,3},{11,15},{20,16},{24,... | collective-permute-start | bytes 1572872 | tf_op jit(solution)/shard_map/ppermute | solution.py:671
  46.0 1.0 %copy-start.9 = (bf16[64,2304]{1,0:T(8,128)(2,1)S(1)}, bf16[64,2304]{1,0:T(8,128)(2,1)}, u32[]{:S(2)}) copy-start(bf16[64,2304]{1,0:T(8,128)(2,1)} %copy-done.8) | copy-start | bytes 884740
  49.5 8.4 %collective-permute-start.5 = (bf16[64,2304]{1,0:T(8,128)(2,1)S(1)}, bf16[64,2304]{1,0:T(8,128)(2,1)S(1)}, u32[]{:S(2)}, u32[]{:S(2)}) collective-permute-start(bf16[64,2304]{1,0:T(8,128)(2,1)S(1)} %get-tuple-element.55.own_ref), channel_id=1, source_target_pairs={{4,8},{8,4},{5,9},{9,5},{6,10},{10,6},{7,11},{11,7},{20,24},{24,20... | collective-permute-start | bytes 884744 | tf_op jit(solution)/shard_map/ppermute | solution.py:671
  50.2 1.2 %collective-permute-start.6 = (f32[32,64]{1,0:T(8,128)S(1)}, f32[32,64]{1,0:T(8,128)S(1)}, u32[]{:S(2)}, u32[]{:S(2)}) collective-permute-start(f32[32,64]{1,0:T(8,128)S(1)} %get-tuple-element.56), channel_id=1, source_target_pairs={{0,1},{1,0},{2,3},{3,2},{4,5},{5,4},{6,7},{7,6},{8,9},{9,8},{10,11... | collective-permute-start | bytes 24584 | tf_op jit(solution)/shard_map/ppermute | solution.py:778
  51.5 3.7 %collective-permute-start.7 = (f32[32,64]{1,0:T(8,128)S(1)}, f32[32,64]{1,0:T(8,128)S(1)}, u32[]{:S(2)}, u32[]{:S(2)}) collective-permute-start(f32[32,64]{1,0:T(8,128)S(1)} %add.6), channel_id=1, source_target_pairs={{0,2},{1,3},{2,0},{3,1},{4,6},{5,7},{6,4},{7,5},{8,10},{9,11},{10,... | collective-permute-start | bytes 24584 | tf_op jit(solution)/shard_map/ppermute | solution.py:778
  55.2 0.7 collective-permute-start.8
  58.0 14.8 %collective-permute-start.9 = (bf16[64,2304]{1,0:T(8,128)(2,1)S(1)}, bf16[64,2304]{1,0:T(8,128)(2,1)S(1)}, u32[]{:S(2)}, u32[]{:S(2)}) collective-permute-start(bf16[64,2304]{1,0:T(8,128)(2,1)S(1)} %total.1.own_ref), channel_id=1, source_target_pairs={{4,0},{8,12},{5,1},{9,13},{6,2},{10,14},{7,3},{11,15},{20,16},{24,... | collective-permute-start | bytes 884744 | tf_op jit(solution)/shard_map/ppermute | solution.py:671

commit v9 on v8

--- a/solution.py
+++ b/solution.py
@@ -332,10 +332,9 @@
 
 
 def filters_kernel(
-    rows, shards, blocks, width, passed, feats_ref, first_ref, weight_ref, rate_ref, front_ref, spec_ref, trans_ref,
-    slope_ref, passing, hid_ref,
+    rows, shards, blocks, width, feats_ref, first_ref, weight_ref, rate_ref, front_ref, spec_ref, trans_ref, slope_ref,
+    hid_ref,
 ):
-    del passed, passing
     hidden, slope = sin_cos(exact_dot(feats_ref[...], first_ref[...]))
     slope_ref[...] = slope
     high, low = split(hidden)
@@ -369,8 +368,8 @@
 
 
 def own_kernel(rows, shards, channels, blocks, width, *refs):
-    inputs, (sums_out, send_out), held = refs[:10], refs[11:13], refs[14:24]
-    sums_ref, send_ref, trans_ref, acc_ref, sems, out_sems = refs[24:]
+    inputs, (sums_out, send_out, first_out), held = refs[:10], refs[11:14], refs[15:25]
+    sums_ref, send_ref, own_first_ref, trans_ref, acc_ref, sems, out_sems = refs[25:]
     (
         feats_ref, first_ref, source_ref, cotan_ref, weight_ref, rate_ref, front_ref, back_ref, featt_ref, bias_ref
     ) = held
@@ -398,12 +397,18 @@
         source_ref, cotan_ref, weight_ref, rate_ref, front_ref, back_ref, trans_ref, sums_ref, send_ref, acc_ref
     )
     first = exact_dot(featt_ref[:, :rows], acc_ref[...] * slope)
+    own_first_ref[...] = first
     put_side(send_ref, channels, fold(bias_ref[...]), first)
-    last = pltpu.make_async_copy(send_ref, send_out, out_sems.at[blocks])
-    last.start()
+    ends = [
+        pltpu.make_async_copy(own_first_ref, first_out, out_sems.at[blocks]),
+        pltpu.make_async_copy(send_ref, send_out, out_sems.at[blocks + 1]),
+    ]
+    for end in ends:
+        end.start()
     for block in range(blocks):
         leaving(block).wait()
-    last.wait()
+    for end in ends:
+        end.wait()
 
 
 def own_strip(
@@ -443,71 +448,92 @@
 
 
 def near_kernel(
-    rows, shards, block, blocks, passed, rank_ref, x0_ref, c0_ref, x1_ref, c1_ref, spec_ref, weight_ref, rate_ref,
-    front_ref, back_ref, trans_ref, featt_ref, slope_ref, own_ref, conv_ref, corr_ref, ahead_ref, sums_ref, first_ref,
-    passing, fields, fast, high_ref, low_ref, acc_ref,
+    rows, shards, blocks, width, rank_ref, x0_ref, c0_ref, x1_ref, c1_ref, spec_ref, weight_ref, rate_ref, front_ref,
+    back_ref, trans_ref, featt_ref, slope_ref, own_ref, own_first_ref, conv_ref, corr_ref, ahead_ref, sums_ref,
+    first_ref, fields, fast, high_ref, low_ref, acc_ref,
 ):
-    del passed, passing
+    rank = rank_ref[0]
+    inner = jnp.logical_and(rank > 0, rank < shards - 1)
+    count = shards - 1
+    tables = (front_ref, back_ref)
+    blocks_in = (x0_ref, c0_ref, x1_ref, c1_ref)
+
+    @pl.when(jnp.logical_not(inner))
+    def _():
+        looped(
+            functools.partial(near_strip, rows, shards, False),
+            (None, None, None) + (ROWS,) * 4 + (CUBE, ROWS, ROWS), blocks, width,
+        )(rank_ref, *tables, *blocks_in, spec_ref, conv_ref, corr_ref, fields, fast)
+
+    @pl.when(inner)
+    def _():
+        acc_ref[...] = jnp.zeros_like(acc_ref)
+        looped(
+            functools.partial(near_strip, rows, shards, True),
+            (None, None, None) + (ROWS,) * 4 + (CUBE, ROWS, ROWS) + (None, None, None) + (ROWS,) * 5, blocks, width,
+        )(
+            rank_ref, *tables, *blocks_in, spec_ref, conv_ref, corr_ref, fields, fast, trans_ref, weight_ref, rate_ref,
+            own_ref, ahead_ref, sums_ref, high_ref, low_ref, acc_ref,
+        )
+        first_ref[...] = own_first_ref[...] + exact_dot(
+            featt_ref[:, : count * rows], acc_ref[...] * slope_ref[: count * rows, :]
+        )
+
+
+def near_strip(
+    rows, shards, inner, block, blocks, rank_ref, front_ref, back_ref, x0_ref, c0_ref, x1_ref, c1_ref, spec_ref,
+    conv_ref, corr_ref, fields, fast, *rest
+):
     rank = rank_ref[0]
     count = shards - 1
-    lower = rank == 1
-    inner = jnp.logical_and(rank > 0, rank < shards - 1)
-    upper = jnp.where(rank == 2, 1.0, 0.0).astype(f32)
-    side = jnp.where(rank == 2, 1.0, -1.0).astype(f32)
-
-    @pl.when(block == 0)
-    def _():
-        acc_ref[...] = jnp.zeros_like(acc_ref)
-
+    if inner:
+        trans_ref, weight_ref, rate_ref, own_ref, ahead_ref, sums_ref, high_ref, low_ref, acc_ref = rest
+        lower = rank == 1
+        upper = jnp.where(rank == 2, 1.0, 0.0).astype(f32)
+        side = jnp.where(rank == 2, 1.0, -1.0).astype(f32)
     for index, ref in enumerate((x0_ref, c0_ref, x1_ref, c1_ref)):
         fields[index] = forward(front_ref, ref[...])
     for re, im, sign in row_groups(rows):
         x0, c0, x1, c1 = ((fields[i, re, :], fields[i, im, :]) for i in range(4))
-        w0, w1 = ((spec_ref[i, re, :].astype(f32), spec_ref[i, im, :].astype(f32)) for i in range(2))
-        for index, value in enumerate(
-            (plus(times(w0, x0), times(w1, x1)), plus(conj_times(w0, c0), conj_times(w1, c1)))
-        ):
+        w0, w1, w2 = ((spec_ref[i, re, :].astype(f32), spec_ref[i, im, :].astype(f32)) for i in range(3))
+        values = [plus(times(w0, x0), times(w1, x1)), plus(conj_times(w0, c0), conj_times(w1, c1))]
+        if inner:
+            values.append(times((w2[0], w2[1] * side), choose(lower, c1, x1)))
+        for index, value in enumerate(values):
             fast[index, re, :] = value[0].astype(bf16)
             fast[index, im, :] = value[1].astype(bf16)
-    conv_ref[...] = backward(back_ref, fast[0])
-    corr_ref[...] = backward(back_ref, fast[1])
-
-    @pl.when(jnp.logical_not(inner))
-    def _():
-        sums_ref[...] = own_ref[...]
-        ahead_ref[...] = jnp.zeros_like(ahead_ref)
-
-    @pl.when(inner)
-    def _():
-        for re, im, sign in row_groups(rows):
-            x0, c0, x1, c1 = ((fields[i, re, :], fields[i, im, :]) for i in range(4))
-            w2 = (spec_ref[2, re, :].astype(f32), spec_ref[2, im, :].astype(f32) * side)
-            ahead = times(w2, choose(lower, c1, x1))
-            fast[2, re, :] = ahead[0].astype(bf16)
-            fast[2, im, :] = ahead[1].astype(bf16)
+        if inner:
             one = plus(conj_times(x1, c0), scaled(conj_times(x0, c1), upper))
             two = conj_times(x1, c1)
             for index, value in enumerate((turned(one, sign), plus(one, turned(two, sign)), two)):
                 for part, where in zip(value, (re, im)):
                     high_ref[index, where, :], low_ref[index, where, :] = split(part)
-        ahead_ref[...] = backward(back_ref, fast[2])
-        rate = rate_ref[...]
-        env = decay(rate, rows, float(rows * shards) ** -0.5)
-        parts = []
-        for lag in range(count):
-            grad = backward(back_ref, high_ref[lag], low_ref[lag])
-            parts.append(split(grad * (env * jnp.exp(rate * (-float(lag * rows))))))
-        m_high = jnp.concatenate([p[0] for p in parts], axis=0)
-        m_low = jnp.concatenate([p[1] for p in parts], axis=0)
-        sums_ref[...] = own_ref[...] + weight_sums(trans_ref[:, : count * rows], m_high, m_low)
-        w_high, w_low = split(weight_ref[...])
-        acc_ref[...] += hidden_sums(m_high, m_low, w_high, w_low)
-
-    @pl.when(block == blocks - 1)
-    def _():
-        first_ref[...] = exact_dot(
-            featt_ref[:, : count * rows], acc_ref[...] * slope_ref[: count * rows, :]
-        )
+    conv_ref[...] = backward(back_ref, fast[0])
+    corr_ref[...] = backward(back_ref, fast[1])
+    if not inner:
+        return
+    ahead_ref[...] = backward(back_ref, fast[2])
+    rate = rate_ref[...]
+    env = decay(rate, rows, float(rows * shards) ** -0.5)
+    parts = []
+    for lag in range(count):
+        grad = backward(back_ref, high_ref[lag], low_ref[lag])
+        parts.append(split(grad * (env * jnp.exp(rate * (-float(lag * rows))))))
+    m_high = jnp.concatenate([p[0] for p in parts], axis=0)
+    m_low = jnp.concatenate([p[1] for p in parts], axis=0)
+    sums_ref[...] = own_ref[...] + weight_sums(trans_ref[:, : count * rows], m_high, m_low)
+    acc_ref[...] += hidden_sums(m_high, m_low, *split(weight_ref[...]))
+
+
+def on_inner(shards, rank_at, kernel):
+    def run(*refs):
+        rank = refs[rank_at][0]
+
+        @pl.when(jnp.logical_and(rank > 0, rank < shards - 1))
+        def _():
+            kernel(*refs)
+
+    return run
 
 
 def far_kernel(rows, block, blocks, rank_ref, far_ref, spec_ref, front_ref, back_ref, ahead_ref, part_ref, late_ref):
@@ -523,7 +549,7 @@
 
 def last_kernel(
     rows, shards, channels, block, blocks, after_ref, rank_ref, x1_ref, c1_ref, far_ref, weight_ref, rate_ref, front_ref, back_ref,
-    trans_ref, featt_ref, slope_ref, sums_ref, first_ref, own_ref, bias_ref, in_ref, pay_ref, total_ref, acc_ref,
+    trans_ref, featt_ref, slope_ref, sums_ref, first_ref, bias_ref, in_ref, pay_ref, total_ref, acc_ref,
 ):
     del after_ref
     hid_count, width = weight_ref.shape
@@ -568,19 +594,18 @@
             featt_ref[:, (shards - 2) * rows :], acc_ref[...] * slope_ref[(shards - 2) * rows :, :]
         )
         lanes = channels // 128
-        own_first = get_side(own_ref[...], channels, lanes, hid_count)[1]
         in_bias, in_first = get_side(in_ref[...], channels, lanes, hid_count)
-        first = first + first_ref[...] + own_first + in_first
+        first = first + first_ref[...] + in_first
         put_side(pay_ref, channels, fold(bias_ref[...]) + in_bias)
         total_ref[...] = first
 
 
-def total_kernel(channels, hid_count, part_ref, own_ref, come_ref, first_ref, first_come_ref, pay_ref):
+def total_kernel(channels, hid_count, part_ref, own_ref, come_ref, first_ref, pay_ref):
     del part_ref
     lanes = channels // 128
     pay_ref[:, :channels] = (own_ref[:, :channels].astype(f32) + come_ref[:, :channels].astype(f32)).astype(bf16)
     own, come = (get_side(ref[...], channels, lanes, hid_count)[0] for ref in (own_ref, come_ref))
-    put_side(pay_ref, channels, own + come, first_ref[...] + first_come_ref[...])
+    put_side(pay_ref, channels, own + come, first_ref[...])
 
 
 def gates_kernel(
@@ -589,8 +614,8 @@
 ):
     rank = rank_ref[0]
 
-    def mask(wanted):
-        return jnp.where(rank == wanted, 1.0, 0.0).astype(f32)
+    def on(wanted, value):
+        return jnp.where(rank == wanted, value, jnp.zeros_like(value))
 
     part = part_ref[...].astype(f32)
     late = late_ref[...]
@@ -598,8 +623,8 @@
     val = val_ref[...].astype(f32)
     out = out_ref[...].astype(f32)
     skip = skip_ref[...]
-    conv = conv_ref[...] + late * mask(2) + part * mask(shards - 1)
-    corr = corr_ref[...] + late * mask(1) + part * mask(0)
+    conv = conv_ref[...] + on(2, late) + on(shards - 1, part)
+    corr = corr_ref[...] + on(1, late) + on(0, part)
     grad_two_ref[...] = (out * (conv + skip * (one * val))).astype(bf16)
     mid = corr + skip * (out * two_ref[...].astype(f32))
     grad_one_ref[...] = (mid * val).astype(bf16)
@@ -697,45 +722,37 @@
         shape(rows, feat_count), shape(feat_count, hid_count), block_bf16, block_bf16, shape(hid_count, channels),
         shape(1, channels), shape(double, double, dtype=bf16), shape(double, double, dtype=bf16),
         shape(feat_count, seq_len), shape(1, channels), shape(hid_count, channels), shape(*pay_shape, dtype=bf16),
+        shape(feat_count, hid_count),
     ]
-    own, send, edge = call(
+    own, send, own_first, edge = call(
         functools.partial(own_kernel, rows, shards, channels, blocks, width), "own_pair", 8,
-        [shape(hid_count, channels), shape(*pay_shape, dtype=bf16), block_bf16],
+        [shape(hid_count, channels), shape(*pay_shape, dtype=bf16), shape(feat_count, hid_count), block_bf16],
         [anywhere] * 11,
-        out_specs=[anywhere] * 3,
+        out_specs=[anywhere] * 4,
         scratch=[pltpu.VMEM(s.shape, s.dtype) for s in own_shapes]
         + [
             pltpu.VMEM((2 * hid_count, rows), bf16), pltpu.VMEM((rows, hid_count), f32),
-            pltpu.SemaphoreType.DMA((10,)), pltpu.SemaphoreType.DMA((blocks + 1,)),
+            pltpu.SemaphoreType.DMA((10,)), pltpu.SemaphoreType.DMA((blocks + 2,)),
         ],
-        aliases={10: 2},
+        aliases={10: 3},
         limit=60,
     )(feats[:rows], first_weight, x0, c0, second_weight, rate_row, front, back, featt, bias, edge)
     far = move(edge, [(0, 2), (shards - 1, shards - 3)])
 
-    spec, trans, slope, send = call(
+    spec, trans, slope = call(
         functools.partial(filters_kernel, rows, shards, blocks, width), "filters", 8,
         [
             shape(shards, double, channels, dtype=bf16), shape(2 * hid_count, seq_len, dtype=bf16),
-            shape(seq_len, hid_count), shape(*pay_shape, dtype=bf16),
+            shape(seq_len, hid_count),
         ],
-        [anywhere] + [vmem] * 5,
-        out_specs=[vmem] * 3 + [anywhere],
+        [vmem] * 5,
         scratch=[pltpu.VMEM((seq_len, 3 * hid_count), bf16)],
-        aliases={0: 3},
-    )(send, feats, first_weight, second_weight, rate_row, front)
-
-    conv, corr, ahead, sums, first, send = call(
-        looped(
-            functools.partial(near_kernel, rows, shards),
-            (None, None) + (ROWS,) * 4 + (CUBE, ROWS, ROWS) + (None,) * 5 + (ROWS,) * 5,
-            blocks, width,
-        ),
-        "near_blocks", 20,
-        [block_f32] * 3
-        + [shape(hid_count, channels), shape(feat_count, hid_count), shape(*pay_shape, dtype=bf16)],
-        [anywhere, smem] + [vmem] * 13,
-        out_specs=[vmem] * 5 + [anywhere],
+    )(feats, first_weight, second_weight, rate_row, front)
+
+    conv, corr, ahead, sums, first = call(
+        functools.partial(near_kernel, rows, shards, blocks, width), "near_blocks", 20,
+        [block_f32] * 3 + [shape(hid_count, channels), shape(feat_count, hid_count)],
+        [smem] + [vmem] * 14,
         scratch=[
             pltpu.VMEM((4, double, width), f32),
             pltpu.VMEM((3, double, width), bf16),
@@ -743,16 +760,17 @@
             pltpu.VMEM((shards - 1, double, width), bf16),
             pltpu.VMEM(((shards - 1) * rows, hid_count), f32),
         ],
-        aliases={0: 5},
-    )(send, rank, x0, c0, x1, c1, spec, second_weight, rate_row, front, back, trans, featt, slope, own)
-
+    )(rank, x0, c0, x1, c1, spec, second_weight, rate_row, front, back, trans, featt, slope, own, own_first)
     come = move(send, inward)
 
     part, late = call(
-        looped(
-            functools.partial(far_kernel, rows),
-            (None, ROWS, (slice(2, 4), slice(None)), None, None, ROWS, ROWS, ROWS),
-            blocks, width,
+        on_inner(
+            shards, 0,
+            looped(
+                functools.partial(far_kernel, rows),
+                (None, ROWS, (slice(2, 4), slice(None)), None, None, ROWS, ROWS, ROWS),
+                blocks, width,
+            ),
         ),
         "far_block", 1,
         [block_bf16, block_f32],
@@ -761,16 +779,20 @@
     part_come = move(part, outward)
 
     pay, first = call(
-        looped(
-            functools.partial(last_kernel, rows, shards, channels),
-            (None, None, ROWS, ROWS, ROWS, ROWS, ROWS, None, None, None, None, None, ROWS),
-            blocks, width,
+        on_inner(
+            shards, 1,
+            looped(
+                functools.partial(last_kernel, rows, shards, channels),
+                (None, None, ROWS, ROWS, ROWS, ROWS, ROWS, None, None, None, None, None, ROWS),
+                blocks, width,
+            ),
         ),
         "last_pair", 1,
         [shape(*pay_shape, dtype=bf16), shape(feat_count, hid_count)],
-        [anywhere, smem] + [vmem] * 15,
+        [anywhere, smem] + [vmem] * 14,
         scratch=[pltpu.VMEM((2 * rows, hid_count), f32)],
-    )(late, rank, x1, c1, far, second_weight, rate_row, front, back, trans, featt, slope, sums, first, send, bias, come)
+    )(late, rank, x1, c1, far, second_weight, rate_row, front, back, trans, featt, slope, sums, first, bias, come)
+    first = first + move(first, across)
     pay_come = move(pay, across)
     group = lax.axis_size(("ch", "sub"))
     bit = 1
@@ -781,8 +803,8 @@
     (total,) = call(
         functools.partial(total_kernel, channels, hid_count), "total", 0,
         [shape(*pay_shape, dtype=bf16)],
-        [anywhere] + [vmem] * 4,
-    )(part_come, pay, pay_come, first, move(first, across))
+        [anywhere] + [vmem] * 3,
+    )(part_come, pay, pay_come, first)
     total_come = move(total, outward)
 
     grad_one, grad_two, grad_value = call(

time: 74.1 us -> 74.2 us (level)
  waiting for transfers between devices: 18.4 us -> 31.4 us
  Pallas kernels: 27.9 us -> 22.3 us
  starting transfers between devices: 24.3 us -> 19 us
  local copies, waits for them, and re-layouts: 2.02 us -> 0.1 us
    ppermute x8, waiting for transfers between devices: 15 us -> 28 us  [move(): return lax.ppermute(array, 'ctx', pairs)]
    pallas_call x3, Pallas kernels: 9.6 us -> 4.07 us  [the longest x1 4.05 us: few_shards_body(): call(functools.partial(near_kernel, rows, shards, blocks, width), 'near_b...]
    ppermute x8, starting transfers between devices: 22.7 us -> 17.4 us  [move(): return lax.ppermute(array, 'ctx', pairs)]
    unnamed x38 -> x34, local copies, waits for them, and re-layouts: 2.02 us -> 0.1 us
  transfers between devices with their start and end apart: 10 -> 10, of which waited for: 5 -> 5; matrix products, arithmetic and copies ran while one was open for 0% -> 0% of each run, Pallas kernels for 33% -> 25%
where the time goes in v9:
time: 74.2 us; the launch traced here: 73.9 us
  waiting for transfers between devices  31.4 us (42%)
  Pallas kernels  22.3 us (30%)
  starting transfers between devices  19 us (26%)
  between operations  1.02 us (1%)
    ppermute x8, waiting for transfers between devices, move(): return lax.ppermute(array, 'ctx', pairs)  28 us
    ppermute x8, starting transfers between devices, move(): return lax.ppermute(array, 'ctx', pairs)  17.4 us
    pallas_call x1, Pallas kernels, few_shards_body(): call(functools.partial(filters_kernel, rows, shards, blocks, width), 'fil...  6.51 us
    pallas_call x1, Pallas kernels, few_shards_body(): call(functools.partial(own_kernel, rows, shards, channels, blocks, width)...  6.11 us
    pallas_call x1, Pallas kernels, few_shards_body(): call(functools.partial(near_kernel, rows, shards, blocks, width), 'near_b...  4.05 us
    ppermute x2, waiting for transfers between devices, few_shards_body(): lax.ppermute(first, ('ch', 'sub'), [(i, i ^ bit) for i in range(group)])  3.42 us
    pallas_call x1, Pallas kernels, few_shards_body(): pl.pallas_call(products_kernel, grid=(rows // row_step,), in_specs=[smem]...  2.62 us
    pallas_call x1, Pallas kernels, few_shards_body(): call(looped(functools.partial(gates_kernel, shards), (None,) + (ROWS,) *...  2.08 us
  transfers between devices with their start and end apart: 10, of which 5 were waited for; matrix products, arithmetic and copies ran while one was open for 0% of the time, Pallas kernels for 25%

profile of v9, /device:TPU:0, one launch (start us, length us, event | category | flops | bytes accessed | tf_op | source)
XLA Modules:
  0.0 73.9 jit_solution(1857657879008629165)
XLA Ops:
  0.6 2.6 %products.1 = (bf16[128,2048]{1,0:T(8,128)(2,1)}, bf16[128,2048]{1,0:T(8,128)(2,1)}, bf16[128,2048]{1,0:T(8,128)(2,1)}, f32[1,2048]{1,0:T(1,128)}) custom-call(s32[1]{0:T(128)} %bitcast.rank_ref.refs_0_.refs_1_, bf16[128,2048]{1,0:T(8,128)(2,1)} %refs_1_.3, bf16[128,2048]{1,0:T(8,128)(2,1)} %refs_2_.1, bf16[128,2048]{1,0:T(8,128)(2,1)} %refs_3_.2, ...), custom_call_target="tpu_custom_call" | custom-call | tf_op jit(solution)/shard_map/products/pallas_call | solution.py:709
  3.3 0.0 copy-start.4
  3.3 0.0 copy-start.5
  3.3 0.0 copy-start.8
  3.3 0.0 copy-start.13
  3.3 0.0 copy-start.14
  3.3 5.1 %collective-permute-start = (bf16[128,2048]{1,0:T(8,128)(2,1)}, bf16[128,2048]{1,0:T(8,128)(2,1)S(1)}, u32[]{:S(2)}, u32[]{:S(2)}) collective-permute-start(bf16[128,2048]{1,0:T(8,128)(2,1)} %get-tuple-element.32.refs_2_.x0_ref), channel_id=1, source_target_pairs={{0,4},{4,8},{8,12},{1,5},{5,9},{9,13},{2,6},{6,10},{10,14},{3,7},{... | collective-permute-start | bytes 1572872 | tf_op jit(solution)/shard_map/ppermute | solution.py:696
  8.4 1.3 %collective-permute-start.1 = (bf16[128,2048]{1,0:T(8,128)(2,1)}, bf16[128,2048]{1,0:T(8,128)(2,1)S(1)}, u32[]{:S(2)}, u32[]{:S(2)}) collective-permute-start(bf16[128,2048]{1,0:T(8,128)(2,1)} %get-tuple-element.33.refs_3_.c0_ref), channel_id=1, source_target_pairs={{4,0},{8,4},{12,8},{5,1},{9,5},{13,9},{6,2},{10,6},{14,10},{7,3},{... | collective-permute-start | bytes 1572872 | tf_op jit(solution)/shard_map/ppermute | solution.py:696
  9.7 6.1 %own_pair.1 = (f32[64,2048]{1,0:T(8,128)}, bf16[64,2304]{1,0:T(8,128)(2,1)}, f32[32,64]{1,0:T(8,128)}, bf16[128,2048]{1,0:T(8,128)(2,1)}) custom-call(f32[128,32]{1,0:T(8,128)} %constant.15.clone.refs_0_, f32[32,64]{1,0:T(8,128)} %refs_1_.2, bf16[128,2048]{1,0:T(8,128)(2,1)} %get-tuple-element.32.refs_2_.x0_ref, ...), custom_call_target="tpu_custom_call", output_to_operand_aliasing={{3}: (10, {})} | custom-call | flops 2147483648 | bytes 262144 | tf_op jit(solution)/shard_map/own_pair/pallas_call | solution.py:727
  15.8 0.0 copy-start.6
  15.8 0.0 copy-start.7
  15.9 0.0 copy-start.11
  15.9 0.0 copy-start.12
  15.9 0.0 copy-start.15
  15.9 0.0 copy-start.16
  15.9 4.7 %collective-permute-start.4 = (bf16[64,2304]{1,0:T(8,128)(2,1)}, bf16[64,2304]{1,0:T(8,128)(2,1)S(1)}, u32[]{:S(2)}, u32[]{:S(2)}) collective-permute-start(bf16[64,2304]{1,0:T(8,128)(2,1)} %get-tuple-element.52), channel_id=1, source_target_pairs={{0,4},{12,8},{1,5},{13,9},{2,6},{14,10},{3,7},{15,11},{16,20},{28,... | collective-permute-start | bytes 884744 | tf_op jit(solution)/shard_map/ppermute | solution.py:696
  20.6 2.3 %collective-permute-start.2 = (bf16[128,2048]{1,0:T(8,128)(2,1)}, bf16[128,2048]{1,0:T(8,128)(2,1)S(1)}, u32[]{:S(2)}, u32[]{:S(2)}) collective-permute-start(bf16[128,2048]{1,0:T(8,128)(2,1)} %get-tuple-element.43), channel_id=1, source_target_pairs={{0,8},{12,4},{1,9},{13,5},{2,10},{14,6},{3,11},{15,7},{16,24},{28,... | collective-permute-start | bytes 1572872 | tf_op jit(solution)/shard_map/ppermute | solution.py:696
  22.9 0.0 copy-done.4
  22.9 0.0 copy-done.5
  22.9 0.0 copy-done.8
  22.9 0.0 copy-done.13
  22.9 0.0 copy-done.14
  22.9 6.5 %filters.1 = (bf16[4,256,2048]{2,1,0:T(8,128)(2,1)S(1)}, bf16[128,512]{1,0:T(8,128)(2,1)S(1)}, f32[512,64]{1,0:T(8,128)S(1)}) custom-call(f32[512,32]{1,0:T(8,128)S(1)} %copy-done.14, f32[32,64]{1,0:T(8,128)S(1)} %copy-done.13, f32[64,2048]{1,0:T(8,128)S(1)} %copy-done.4, f32[1,2048]{1,0:T(1,128)S(1)} %bitcast.5, bf16[256,256]{1,0:T(8,128)(2,1)S(1)} %copy-done.5), custom_call_target="tpu_custom_call" | custom-call | flops 2147483648 | bytes 262144 | tf_op jit(solution)/shard_map/filters/pallas_call | solution.py:742
  29.5 0.0 collective-permute-done.x1_ref.refs_2_
  29.5 0.0 collective-permute-done.1.c1_ref.refs_3_
  29.5 0.0 copy-done.6
  29.5 0.0 copy-done.7
  29.5 0.0 copy-done.11
  29.5 0.0 copy-done.12
  29.5 0.0 copy-done.15
  29.5 0.0 copy-done.16
  29.5 4.0 %near_blocks.1 = (f32[128,2048]{1,0:T(8,128)S(1)}, f32[128,2048]{1,0:T(8,128)S(1)}, f32[128,2048]{1,0:T(8,128)S(1)}, f32[64,2048]{1,0:T(8,128)S(1)}, f32[32,64]{1,0:T(8,128)S(1)}) custom-call(s32[1]{0:T(128)} %bitcast.rank_ref.refs_0_.refs_1_, bf16[128,2048]{1,0:T(8,128)(2,1)S(1)} %copy-done.11, bf16[128,2048]{1,0:T(8,128)(2,1)S(1)} %copy-done.12, ...), custom_call_target="tpu_custom_call" | custom-call | flops 5368709120 | bytes 262144 | tf_op jit(solution)/shard_map/near_blocks/pallas_call | solution.py:752
  33.6 0.0 copy-start.10
  33.6 4.2 %collective-permute-done.2.refs_1_.refs_4_ = bf16[128,2048]{1,0:T(8,128)(2,1)S(1)} collective-permute-done((bf16[128,2048]{1,0:T(8,128)(2,1)}, bf16[128,2048]{1,0:T(8,128)(2,1)S(1)}, u32[]{:S(2)}, u32[]{:S(2)}) %collective-permute-start.2) | collective-permute-done | bytes 524320 | tf_op jit(solution)/shard_map/ppermute | solution.py:696
  37.8 0.0 copy-start
  37.8 0.0 copy-start.1
  37.8 0.0 copy-start.2
  37.8 0.0 copy-start.3
  37.8 0.0 copy-start.9
  37.8 1.4 %collective-permute-start.3 = (bf16[128,2048]{1,0:T(8,128)(2,1)S(1)}, bf16[128,2048]{1,0:T(8,128)(2,1)S(1)}, u32[]{:S(2)}, u32[]{:S(2)}) collective-permute-start(bf16[128,2048]{1,0:T(8,128)(2,1)S(1)} %get-tuple-element.46), channel_id=1, source_target_pairs={{4,0},{8,12},{5,1},{9,13},{6,2},{10,14},{7,3},{11,15},{20,16},{24,... | collective-permute-start | bytes 1572872 | tf_op jit(solution)/shard_map/ppermute | solution.py:696
  39.3 0.0 collective-permute-done.4.refs_15_
  39.3 0.0 copy-done.10
  39.3 0.7 collective-permute-start.5
  40.0 0.7 collective-permute-start.6
  40.7 0.0 collective-permute-done.6
  40.7 0.1 collective-permute-start.7
  40.8 1.2 %collective-permute-done.7 = f32[32,64]{1,0:T(8,128)S(1)} collective-permute-done((f32[32,64]{1,0:T(8,128)S(1)}, f32[32,64]{1,0:T(8,128)S(1)}, u32[]{:S(2)}, u32[]{:S(2)}) %collective-permute-start.7) | collective-permute-done | bytes 8224 | tf_op jit(solution)/shard_map/ppermute | solution.py:800
  42.0 1.5 %collective-permute-start.8 = (f32[32,64]{1,0:T(8,128)S(1)}, f32[32,64]{1,0:T(8,128)S(1)}, u32[]{:S(2)}, u32[]{:S(2)}) collective-permute-start(f32[32,64]{1,0:T(8,128)S(1)} %add.10), channel_id=1, source_target_pairs={{0,2},{1,3},{2,0},{3,1},{4,6},{5,7},{6,4},{7,5},{8,10},{9,11},{10,... | collective-permute-start | bytes 24584 | tf_op jit(solution)/shard_map/ppermute | solution.py:800
  43.5 2.2 %collective-permute-done.8 = f32[32,64]{1,0:T(8,128)S(1)} collective-permute-done((f32[32,64]{1,0:T(8,128)S(1)}, f32[32,64]{1,0:T(8,128)S(1)}, u32[]{:S(2)}, u32[]{:S(2)}) %collective-permute-start.8) | collective-permute-done | bytes 8224 | tf_op jit(solution)/shard_map/ppermute | solution.py:800
  45.7 0.0 collective-permute-done.5.come_ref
  45.7 13.1 %collective-permute-done.3.refs_9_.part_ref = bf16[128,2048]{1,0:T(8,128)(2,1)S(1)} collective-permute-done((bf16[128,2048]{1,0:T(8,128)(2,1)S(1)}, bf16[128,2048]{1,0:T(8,128)(2,1)S(1)}, u32[]{:S(2)}, u32[]{:S(2)}) %collective-permute-start.3) | collective-permute-done | bytes 524320 | tf_op jit(solution)/shard_map/ppermute | solution.py:696
  58.8 0.1 total.1.own_ref
  58.9 1.3 %collective-permute-start.9 = (bf16[64,2304]{1,0:T(8,128)(2,1)S(1)}, bf16[64,2304]{1,0:T(8,128)(2,1)S(1)}, u32[]{:S(2)}, u32[]{:S(2)}) collective-permute-start(bf16[64,2304]{1,0:T(8,128)(2,1)S(1)} %total.1.own_ref), channel_id=1, source_target_pairs={{4,0},{8,12},{5,1},{9,13},{6,2},{10,14},{7,3},{11,15},{20,16},{24,... | collective-permute-start | bytes 884744 | tf_op jit(solution)/shard_map/ppermute | solution.py:696
  60.2 0.0 copy-done
  60.2 0.0 copy-done.1
  60.2 0.0 copy-done.2
  60.2 0.0 copy-done.3
  60.2 0.0 copy-done.9
  60.2 2.1 %gates.1 = (bf16[128,2048]{1,0:T(8,128)(2,1)}, bf16[128,2048]{1,0:T(8,128)(2,1)}, bf16[128,2048]{1,0:T(8,128)(2,1)}) custom-call(s32[1]{0:T(128)} %bitcast.rank_ref.refs_0_.refs_1_, bf16[128,2048]{1,0:T(8,128)(2,1)S(1)} %copy-done, bf16[128,2048]{1,0:T(8,128)(2,1)S(1)} %copy-done.1, bf16[128,2048]{1,0:T(8,128)(2,1)S(1)} %copy-done.2, ...), custom_call_target="tpu_custom_call" | custom-call | bytes 262144 | tf_op jit(solution)/shard_map/gates/pallas_call | solution.py:810
  62.3 10.7 %collective-permute-done.9.come_ref = bf16[64,2304]{1,0:T(8,128)(2,1)S(1)} collective-permute-done((bf16[64,2304]{1,0:T(8,128)(2,1)S(1)}, bf16[64,2304]{1,0:T(8,128)(2,1)S(1)}, u32[]{:S(2)}, u32[]{:S(2)}) %collective-permute-start.9) | collective-permute-done | bytes 294944 | tf_op jit(solution)/shard_map/ppermute | solution.py:696
  73.0 0.9 %finish.1 = (f32[64,2048]{1,0:T(8,128)}, f32[32,64]{1,0:T(8,128)}, f32[1,2048]{1,0:T(1,128)}) custom-call(s32[1]{0:T(128)} %bitcast.rank_ref.refs_0_.refs_1_, bf16[64,2304]{1,0:T(8,128)(2,1)S(1)} %total.1.own_ref, bf16[64,2304]{1,0:T(8,128)(2,1)S(1)} %collective-permute-done.9.come_ref), custom_call_target="tpu_custom_call" | custom-call | bytes 262144 | tf_op jit(solution)/shard_map/finish/pallas_call | solution.py:820
  (5 shorter events, 0.0 us)
Async XLA Ops:
  3.3 19.6 %copy-start.4 = (f32[64,2048]{1,0:T(8,128)S(1)}, f32[64,2048]{1,0:T(8,128)}, u32[]{:S(2)}) copy-start(f32[64,2048]{1,0:T(8,128)} %refs_5_.1) | copy-start | bytes 1572868
  3.3 19.6 %copy-start.5 = (bf16[256,256]{1,0:T(8,128)(2,1)S(1)}, bf16[256,256]{1,0:T(8,128)(2,1)}, u32[]{:S(2)}) copy-start(bf16[256,256]{1,0:T(8,128)(2,1)} %constant.16.clone.front_ref.refs_6_.refs_3_.refs_7_) | copy-start | bytes 393220
  3.3 19.6 %copy-start.8 = (f32[2048]{0:T(1024)S(1)}, f32[2048]{0:T(1024)}, u32[]{:S(2)}) copy-start(f32[2048]{0:T(1024)} %param.20) | copy-start | bytes 24580
  3.3 19.6 %copy-start.13 = (f32[32,64]{1,0:T(8,128)S(1)}, f32[32,64]{1,0:T(8,128)}, u32[]{:S(2)}) copy-start(f32[32,64]{1,0:T(8,128)} %refs_1_.2) | copy-start | bytes 24580
  3.3 19.6 %copy-start.14 = (f32[512,32]{1,0:T(8,128)S(1)}, f32[512,32]{1,0:T(8,128)}, u32[]{:S(2)}) copy-start(f32[512,32]{1,0:T(8,128)} %constant.19.clone.feats_ref) | copy-start | bytes 196612
  3.3 26.2 %collective-permute-start = (bf16[128,2048]{1,0:T(8,128)(2,1)}, bf16[128,2048]{1,0:T(8,128)(2,1)S(1)}, u32[]{:S(2)}, u32[]{:S(2)}) collective-permute-start(bf16[128,2048]{1,0:T(8,128)(2,1)} %get-tuple-element.32.refs_2_.x0_ref), channel_id=1, source_target_pairs={{0,4},{4,8},{8,12},{1,5},{5,9},{9,13},{2,6},{6,10},{10,14},{3,7},{... | collective-permute-start | bytes 1572872 | tf_op jit(solution)/shard_map/ppermute | solution.py:696
  8.4 21.1 %collective-permute-start.1 = (bf16[128,2048]{1,0:T(8,128)(2,1)}, bf16[128,2048]{1,0:T(8,128)(2,1)S(1)}, u32[]{:S(2)}, u32[]{:S(2)}) collective-permute-start(bf16[128,2048]{1,0:T(8,128)(2,1)} %get-tuple-element.33.refs_3_.c0_ref), channel_id=1, source_target_pairs={{4,0},{8,4},{12,8},{5,1},{9,5},{13,9},{6,2},{10,6},{14,10},{7,3},{... | collective-permute-start | bytes 1572872 | tf_op jit(solution)/shard_map/ppermute | solution.py:696
  15.8 13.7 %copy-start.6 = (bf16[256,256]{1,0:T(8,128)(2,1)S(1)}, bf16[256,256]{1,0:T(8,128)(2,1)}, u32[]{:S(2)}) copy-start(bf16[256,256]{1,0:T(8,128)(2,1)} %constant.17.clone.refs_7_.back_ref.refs_4_.refs_8_) | copy-start | bytes 393220
  15.8 13.7 %copy-start.7 = (f32[32,512]{1,0:T(8,128)S(1)}, f32[32,512]{1,0:T(8,128)}, u32[]{:S(2)}) copy-start(f32[32,512]{1,0:T(8,128)} %constant.18.clone.refs_8_.featt_ref.refs_10_) | copy-start | bytes 196612
  15.9 13.7 %copy-start.11 = (bf16[128,2048]{1,0:T(8,128)(2,1)S(1)}, bf16[128,2048]{1,0:T(8,128)(2,1)}, u32[]{:S(2)}) copy-start(bf16[128,2048]{1,0:T(8,128)(2,1)} %get-tuple-element.32.refs_2_.x0_ref) | copy-start | bytes 1572868
  15.9 13.7 %copy-start.12 = (bf16[128,2048]{1,0:T(8,128)(2,1)S(1)}, bf16[128,2048]{1,0:T(8,128)(2,1)}, u32[]{:S(2)}) copy-start(bf16[128,2048]{1,0:T(8,128)(2,1)} %get-tuple-element.33.refs_3_.c0_ref) | copy-start | bytes 1572868
  15.9 13.7 %copy-start.15 = (f32[64,2048]{1,0:T(8,128)S(1)}, f32[64,2048]{1,0:T(8,128)}, u32[]{:S(2)}) copy-start(f32[64,2048]{1,0:T(8,128)} %get-tuple-element.39.own_ref) | copy-start | bytes 1572868
  15.9 13.7 %copy-start.16 = (f32[32,64]{1,0:T(8,128)S(1)}, f32[32,64]{1,0:T(8,128)}, u32[]{:S(2)}) copy-start(f32[32,64]{1,0:T(8,128)} %get-tuple-element.40.own_first_ref) | copy-start | bytes 24580
  15.9 23.4 %collective-permute-start.4 = (bf16[64,2304]{1,0:T(8,128)(2,1)}, bf16[64,2304]{1,0:T(8,128)(2,1)S(1)}, u32[]{:S(2)}, u32[]{:S(2)}) collective-permute-start(bf16[64,2304]{1,0:T(8,128)(2,1)} %get-tuple-element.52), channel_id=1, source_target_pairs={{0,4},{12,8},{1,5},{13,9},{2,6},{14,10},{3,7},{15,11},{16,20},{28,... | collective-permute-start | bytes 884744 | tf_op jit(solution)/shard_map/ppermute | solution.py:696
  20.6 17.2 %collective-permute-start.2 = (bf16[128,2048]{1,0:T(8,128)(2,1)}, bf16[128,2048]{1,0:T(8,128)(2,1)S(1)}, u32[]{:S(2)}, u32[]{:S(2)}) collective-permute-start(bf16[128,2048]{1,0:T(8,128)(2,1)} %get-tuple-element.43), channel_id=1, source_target_pairs={{0,8},{12,4},{1,9},{13,5},{2,10},{14,6},{3,11},{15,7},{16,24},{28,... | collective-permute-start | bytes 1572872 | tf_op jit(solution)/shard_map/ppermute | solution.py:696
  33.6 5.7 %copy-start.10 = (f32[1,2048]{1,0:T(1,128)S(1)}, f32[1,2048]{1,0:T(1,128)}, u32[]{:S(2)}) copy-start(f32[1,2048]{1,0:T(1,128)} %get-tuple-element.37.refs_9_.refs_14_) | copy-start | bytes 24580
  37.8 22.4 %copy-start = (bf16[128,2048]{1,0:T(8,128)(2,1)S(1)}, bf16[128,2048]{1,0:T(8,128)(2,1)}, u32[]{:S(2)}) copy-start(bf16[128,2048]{1,0:T(8,128)(2,1)} %refs_1_.3) | copy-start | bytes 1572868
  37.8 22.4 %copy-start.1 = (bf16[128,2048]{1,0:T(8,128)(2,1)S(1)}, bf16[128,2048]{1,0:T(8,128)(2,1)}, u32[]{:S(2)}) copy-start(bf16[128,2048]{1,0:T(8,128)(2,1)} %refs_2_.1) | copy-start | bytes 1572868
  37.8 22.4 %copy-start.2 = (bf16[128,2048]{1,0:T(8,128)(2,1)S(1)}, bf16[128,2048]{1,0:T(8,128)(2,1)}, u32[]{:S(2)}) copy-start(bf16[128,2048]{1,0:T(8,128)(2,1)} %refs_3_.2) | copy-start | bytes 1572868
  37.8 22.4 %copy-start.3 = (bf16[128,2048]{1,0:T(8,128)(2,1)S(1)}, bf16[128,2048]{1,0:T(8,128)(2,1)}, u32[]{:S(2)}) copy-start(bf16[128,2048]{1,0:T(8,128)(2,1)} %refs_4_.4) | copy-start | bytes 1572868
  37.8 22.4 %copy-start.9 = (f32[2048]{0:T(1024)S(1)}, f32[2048]{0:T(1024)}, u32[]{:S(2)}) copy-start(f32[2048]{0:T(1024)} %param.19) | copy-start | bytes 24580
  37.8 21.0 %collective-permute-start.3 = (bf16[128,2048]{1,0:T(8,128)(2,1)S(1)}, bf16[128,2048]{1,0:T(8,128)(2,1)S(1)}, u32[]{:S(2)}, u32[]{:S(2)}) collective-permute-start(bf16[128,2048]{1,0:T(8,128)(2,1)S(1)} %get-tuple-element.46), channel_id=1, source_target_pairs={{4,0},{8,12},{5,1},{9,13},{6,2},{10,14},{7,3},{11,15},{20,16},{24,... | collective-permute-start | bytes 1572872 | tf_op jit(solution)/shard_map/ppermute | solution.py:696
  39.3 6.4 %collective-permute-start.5 = (bf16[64,2304]{1,0:T(8,128)(2,1)S(1)}, bf16[64,2304]{1,0:T(8,128)(2,1)S(1)}, u32[]{:S(2)}, u32[]{:S(2)}) collective-permute-start(bf16[64,2304]{1,0:T(8,128)(2,1)S(1)} %get-tuple-element.53.own_ref), channel_id=1, source_target_pairs={{4,8},{8,4},{5,9},{9,5},{6,10},{10,6},{7,11},{11,7},{20,24},{24,20... | collective-permute-start | bytes 884744 | tf_op jit(solution)/shard_map/ppermute | solution.py:696
  40.0 0.7 collective-permute-start.6
  40.7 1.2 %collective-permute-start.7 = (f32[32,64]{1,0:T(8,128)S(1)}, f32[32,64]{1,0:T(8,128)S(1)}, u32[]{:S(2)}, u32[]{:S(2)}) collective-permute-start(f32[32,64]{1,0:T(8,128)S(1)} %add.9), channel_id=1, source_target_pairs={{0,1},{1,0},{2,3},{3,2},{4,5},{5,4},{6,7},{7,6},{8,9},{9,8},{10,11... | collective-permute-start | bytes 24584 | tf_op jit(solution)/shard_map/ppermute | solution.py:800
  42.0 3.7 %collective-permute-start.8 = (f32[32,64]{1,0:T(8,128)S(1)}, f32[32,64]{1,0:T(8,128)S(1)}, u32[]{:S(2)}, u32[]{:S(2)}) collective-permute-start(f32[32,64]{1,0:T(8,128)S(1)} %add.10), channel_id=1, source_target_pairs={{0,2},{1,3},{2,0},{3,1},{4,6},{5,7},{6,4},{7,5},{8,10},{9,11},{10,... | collective-permute-start | bytes 24584 | tf_op jit(solution)/shard_map/ppermute | solution.py:800
  58.9 14.1 %collective-permute-start.9 = (bf16[64,2304]{1,0:T(8,128)(2,1)S(1)}, bf16[64,2304]{1,0:T(8,128)(2,1)S(1)}, u32[]{:S(2)}, u32[]{:S(2)}) collective-permute-start(bf16[64,2304]{1,0:T(8,128)(2,1)S(1)} %total.1.own_ref), channel_id=1, source_target_pairs={{4,0},{8,12},{5,1},{9,13},{6,2},{10,14},{7,3},{11,15},{20,16},{24,... | collective-permute-start | bytes 884744 | tf_op jit(solution)/shard_map/ppermute | solution.py:696

commit v10 on v9

--- a/solution.py
+++ b/solution.py
@@ -600,12 +600,12 @@
         total_ref[...] = first
 
 
-def total_kernel(channels, hid_count, part_ref, own_ref, come_ref, first_ref, pay_ref):
-    del part_ref
+def total_kernel(channels, hid_count, part_ref, first_ref, own_ref, come_ref, pay_ref):
+    del part_ref, first_ref
     lanes = channels // 128
     pay_ref[:, :channels] = (own_ref[:, :channels].astype(f32) + come_ref[:, :channels].astype(f32)).astype(bf16)
     own, come = (get_side(ref[...], channels, lanes, hid_count)[0] for ref in (own_ref, come_ref))
-    put_side(pay_ref, channels, own + come, first_ref[...])
+    put_side(pay_ref, channels, own + come)
 
 
 def gates_kernel(
@@ -632,7 +632,8 @@
 
 
 def finish_kernel(
-    channels, shards, rank_ref, own_ref, come_ref, second_out, first_out, bias_out, second, first, bias, sems
+    channels, shards, rank_ref, own_ref, come_ref, first_ref, first_come_ref, second_out, first_out, bias_out, second,
+    first, bias, sems,
 ):
     rank = rank_ref[0]
     inner = jnp.logical_and(rank > 0, rank < shards - 1)
@@ -644,8 +645,9 @@
     picked = jnp.where(inner, own_ref[...], come_ref[...])
     second[...] = picked[:, :channels].astype(f32)
     copies[0].start()
-    rows, first[...] = get_side(picked, channels, lanes, first.shape[1])
+    first[...] = jnp.where(inner, first_ref[...], first_come_ref[...])
     copies[1].start()
+    rows = get_side(picked, channels, lanes, first.shape[1])[0]
     for i in range(lanes):
         bias[:, i * 128 : (i + 1) * 128] = rows[i : i + 1]
     copies[2].start()
@@ -749,6 +751,9 @@
         scratch=[pltpu.VMEM((seq_len, 3 * hid_count), bf16)],
     )(feats, first_weight, second_weight, rate_row, front)
 
+    send, _ = lax.optimization_barrier((send, slope))
+    come = move(send, inward)
+
     conv, corr, ahead, sums, first = call(
         functools.partial(near_kernel, rows, shards, blocks, width), "near_blocks", 20,
         [block_f32] * 3 + [shape(hid_count, channels), shape(feat_count, hid_count)],
@@ -761,8 +766,6 @@
             pltpu.VMEM(((shards - 1) * rows, hid_count), f32),
         ],
     )(rank, x0, c0, x1, c1, spec, second_weight, rate_row, front, back, trans, featt, slope, own, own_first)
-    come = move(send, inward)
-
     part, late = call(
         on_inner(
             shards, 0,
@@ -792,7 +795,6 @@
         [anywhere, smem] + [vmem] * 14,
         scratch=[pltpu.VMEM((2 * rows, hid_count), f32)],
     )(late, rank, x1, c1, far, second_weight, rate_row, front, back, trans, featt, slope, sums, first, bias, come)
-    first = first + move(first, across)
     pay_come = move(pay, across)
     group = lax.axis_size(("ch", "sub"))
     bit = 1
@@ -803,9 +805,11 @@
     (total,) = call(
         functools.partial(total_kernel, channels, hid_count), "total", 0,
         [shape(*pay_shape, dtype=bf16)],
-        [anywhere] + [vmem] * 3,
-    )(part_come, pay, pay_come, first)
+        [anywhere] * 2 + [vmem] * 2,
+    )(part_come, first, pay, pay_come)
     total_come = move(total, outward)
+    first = first + move(first, across)
+    first_come = move(first, outward)
 
     grad_one, grad_two, grad_value = call(
         looped(
@@ -820,10 +824,10 @@
     grad_second, grad_first, grad_bias = call(
         functools.partial(finish_kernel, channels, shards), "finish", 0,
         outs,
-        [smem] + [vmem] * 2,
+        [smem] + [vmem] * 4,
         out_specs=[anywhere] * 3,
         scratch=[pltpu.VMEM(o.shape, f32) for o in outs] + [pltpu.SemaphoreType.DMA((3,))],
-    )(rank, total, total_come)
+    )(rank, total, total_come, first, first_come)
     return (grad_one, grad_two, grad_value, grad_first, grad_second, grad_bias.reshape(channels))
 
 

time: 74.2 us -> 67.1 us (0.904)
  waiting for transfers between devices: 31.4 us -> 23 us
  starting transfers between devices: 19 us -> 20.3 us
    ppermute x8 -> x9, waiting for transfers between devices: 28 us -> 19.6 us  [move(): return lax.ppermute(array, 'ctx', pairs)]
    ppermute x8 -> x9, starting transfers between devices: 17.4 us -> 18.7 us  [move(): return lax.ppermute(array, 'ctx', pairs)]
  transfers between devices with their start and end apart: 10 -> 11, of which waited for: 5 -> 6; matrix products, arithmetic and copies ran while one was open for 0% -> 0% of each run, Pallas kernels for 25% -> 28%
where the time goes in v10:
time: 67.1 us; the launch traced here: 66.8 us
  waiting for transfers between devices  23 us (34%)
  Pallas kernels  22.3 us (33%)
  starting transfers between devices  20.3 us (30%)
  between operations  1.02 us (2%)
    ppermute x9, waiting for transfers between devices, move(): return lax.ppermute(array, 'ctx', pairs)  19.6 us
    ppermute x9, starting transfers between devices, move(): return lax.ppermute(array, 'ctx', pairs)  18.7 us
    pallas_call x1, Pallas kernels, few_shards_body(): call(functools.partial(filters_kernel, rows, shards, blocks, width), 'fil...  6.52 us
    pallas_call x1, Pallas kernels, few_shards_body(): call(functools.partial(own_kernel, rows, shards, channels, blocks, width)...  6.13 us
    pallas_call x1, Pallas kernels, few_shards_body(): call(functools.partial(near_kernel, rows, shards, blocks, width), 'near_b...  4.05 us
    ppermute x2, waiting for transfers between devices, few_shards_body(): lax.ppermute(first, ('ch', 'sub'), [(i, i ^ bit) for i in range(group)])  3.43 us
    pallas_call x1, Pallas kernels, few_shards_body(): pl.pallas_call(products_kernel, grid=(rows // row_step,), in_specs=[smem]...  2.62 us
    pallas_call x1, Pallas kernels, few_shards_body(): call(looped(functools.partial(gates_kernel, shards), (None,) + (ROWS,) *...  2.08 us
  transfers between devices with their start and end apart: 11, of which 6 were waited for; matrix products, arithmetic and copies ran while one was open for 0% of the time, Pallas kernels for 28%

profile of v10, /device:TPU:0, one launch (start us, length us, event | category | flops | bytes accessed | tf_op | source)
XLA Modules:
  0.0 66.8 jit_solution(4972996334689932660)
XLA Ops:
  0.6 2.6 %products.1 = (bf16[128,2048]{1,0:T(8,128)(2,1)}, bf16[128,2048]{1,0:T(8,128)(2,1)}, bf16[128,2048]{1,0:T(8,128)(2,1)}, f32[1,2048]{1,0:T(1,128)}) custom-call(s32[1]{0:T(128)} %bitcast.rank_ref.refs_0_.refs_1_, bf16[128,2048]{1,0:T(8,128)(2,1)} %refs_1_.3, bf16[128,2048]{1,0:T(8,128)(2,1)} %refs_2_.1, bf16[128,2048]{1,0:T(8,128)(2,1)} %refs_3_.2, ...), custom_call_target="tpu_custom_call" | custom-call | tf_op jit(solution)/shard_map/products/pallas_call | solution.py:711
  3.3 0.0 copy-start.4
  3.3 0.0 copy-start.5
  3.3 0.0 copy-start.8
  3.3 0.0 copy-start.13
  3.3 0.0 copy-start.14
  3.3 5.1 %collective-permute-start = (bf16[128,2048]{1,0:T(8,128)(2,1)}, bf16[128,2048]{1,0:T(8,128)(2,1)S(1)}, u32[]{:S(2)}, u32[]{:S(2)}) collective-permute-start(bf16[128,2048]{1,0:T(8,128)(2,1)} %get-tuple-element.33.refs_2_.x0_ref), channel_id=1, source_target_pairs={{0,4},{4,8},{8,12},{1,5},{5,9},{9,13},{2,6},{6,10},{10,14},{3,7},{... | collective-permute-start | bytes 1572872 | tf_op jit(solution)/shard_map/ppermute | solution.py:698
  8.4 1.3 %collective-permute-start.1 = (bf16[128,2048]{1,0:T(8,128)(2,1)}, bf16[128,2048]{1,0:T(8,128)(2,1)S(1)}, u32[]{:S(2)}, u32[]{:S(2)}) collective-permute-start(bf16[128,2048]{1,0:T(8,128)(2,1)} %get-tuple-element.34.refs_3_.c0_ref), channel_id=1, source_target_pairs={{4,0},{8,4},{12,8},{5,1},{9,5},{13,9},{6,2},{10,6},{14,10},{7,3},{... | collective-permute-start | bytes 1572872 | tf_op jit(solution)/shard_map/ppermute | solution.py:698
  9.7 6.1 %own_pair.1 = (f32[64,2048]{1,0:T(8,128)}, bf16[64,2304]{1,0:T(8,128)(2,1)}, f32[32,64]{1,0:T(8,128)}, bf16[128,2048]{1,0:T(8,128)(2,1)}) custom-call(f32[128,32]{1,0:T(8,128)} %constant.15.clone.refs_0_, f32[32,64]{1,0:T(8,128)} %refs_1_.2, bf16[128,2048]{1,0:T(8,128)(2,1)} %get-tuple-element.33.refs_2_.x0_ref, ...), custom_call_target="tpu_custom_call", output_to_operand_aliasing={{3}: (10, {})} | custom-call | flops 2147483648 | bytes 262144 | tf_op jit(solution)/shard_map/own_pair/pallas_call | solution.py:729
  15.9 0.0 copy-start.17
  15.9 0.0 copy-start.6
  15.9 0.0 copy-start.7
  15.9 0.0 copy-start.11
  15.9 0.0 copy-start.12
  15.9 0.0 copy-start.15
  15.9 0.0 copy-start.16
  15.9 5.7 %collective-permute-start.2 = (bf16[128,2048]{1,0:T(8,128)(2,1)}, bf16[128,2048]{1,0:T(8,128)(2,1)S(1)}, u32[]{:S(2)}, u32[]{:S(2)}) collective-permute-start(bf16[128,2048]{1,0:T(8,128)(2,1)} %get-tuple-element.44), channel_id=1, source_target_pairs={{0,8},{12,4},{1,9},{13,5},{2,10},{14,6},{3,11},{15,7},{16,24},{28,... | collective-permute-start | bytes 1572872 | tf_op jit(solution)/shard_map/ppermute | solution.py:698
  21.6 0.0 copy-done.4
  21.6 0.0 copy-done.5
  21.7 0.0 copy-done.8
  21.7 0.0 copy-done.13
  21.7 0.0 copy-done.14
  21.7 6.5 %filters.1 = (bf16[4,256,2048]{2,1,0:T(8,128)(2,1)S(1)}, bf16[128,512]{1,0:T(8,128)(2,1)S(1)}, f32[512,64]{1,0:T(8,128)S(1)}) custom-call(f32[512,32]{1,0:T(8,128)S(1)} %copy-done.14, f32[32,64]{1,0:T(8,128)S(1)} %copy-done.13, f32[64,2048]{1,0:T(8,128)S(1)} %copy-done.4, f32[1,2048]{1,0:T(1,128)S(1)} %bitcast.5, bf16[256,256]{1,0:T(8,128)(2,1)S(1)} %copy-done.5), custom_call_target="tpu_custom_call" | custom-call | flops 2147483648 | bytes 262144 | tf_op jit(solution)/shard_map/filters/pallas_call | solution.py:744
  28.2 0.0 copy-done.17
  28.2 1.3 %collective-permute-start.4 = (bf16[64,2304]{1,0:T(8,128)(2,1)S(1)}, bf16[64,2304]{1,0:T(8,128)(2,1)S(1)}, u32[]{:S(2)}, u32[]{:S(2)}) collective-permute-start(bf16[64,2304]{1,0:T(8,128)(2,1)S(1)} %copy-done.17), channel_id=1, source_target_pairs={{0,4},{12,8},{1,5},{13,9},{2,6},{14,10},{3,7},{15,11},{16,20},{28,... | collective-permute-start | bytes 884744 | tf_op jit(solution)/shard_map/ppermute | solution.py:698
  29.5 0.0 collective-permute-done.x1_ref.refs_2_
  29.5 0.0 collective-permute-done.1.c1_ref.refs_3_
  29.6 0.0 copy-done.6
  29.6 0.0 copy-done.7
  29.6 0.0 copy-done.11
  29.6 0.0 copy-done.12
  29.6 0.0 copy-done.15
  29.6 0.0 copy-done.16
  29.6 4.0 %near_blocks.1 = (f32[128,2048]{1,0:T(8,128)S(1)}, f32[128,2048]{1,0:T(8,128)S(1)}, f32[128,2048]{1,0:T(8,128)S(1)}, f32[64,2048]{1,0:T(8,128)S(1)}, f32[32,64]{1,0:T(8,128)S(1)}) custom-call(s32[1]{0:T(128)} %bitcast.rank_ref.refs_0_.refs_1_, bf16[128,2048]{1,0:T(8,128)(2,1)S(1)} %copy-done.11, bf16[128,2048]{1,0:T(8,128)(2,1)S(1)} %copy-done.12, ...), custom_call_target="tpu_custom_call" | custom-call | flops 5368709120 | bytes 262144 | tf_op jit(solution)/shard_map/near_blocks/pallas_call | solution.py:757
  33.7 0.0 copy-start.10
  33.7 0.6 collective-permute-done.2.refs_1_.refs_4_
  34.3 0.0 copy-start.1
  34.3 0.0 copy-start.2
  34.3 0.0 copy-start.3
  34.3 0.0 copy-start.9
  34.3 1.4 %collective-permute-start.3 = (bf16[128,2048]{1,0:T(8,128)(2,1)S(1)}, bf16[128,2048]{1,0:T(8,128)(2,1)S(1)}, u32[]{:S(2)}, u32[]{:S(2)}) collective-permute-start(bf16[128,2048]{1,0:T(8,128)(2,1)S(1)} %get-tuple-element.47), channel_id=1, source_target_pairs={{4,0},{8,12},{5,1},{9,13},{6,2},{10,14},{7,3},{11,15},{20,16},{24,... | collective-permute-start | bytes 1572872 | tf_op jit(solution)/shard_map/ppermute | solution.py:698
  35.7 3.0 %collective-permute-done.4.refs_15_ = bf16[64,2304]{1,0:T(8,128)(2,1)S(1)} collective-permute-done((bf16[64,2304]{1,0:T(8,128)(2,1)S(1)}, bf16[64,2304]{1,0:T(8,128)(2,1)S(1)}, u32[]{:S(2)}, u32[]{:S(2)}) %collective-permute-start.4) | collective-permute-done | bytes 294944 | tf_op jit(solution)/shard_map/ppermute | solution.py:698
  38.7 0.0 copy-done.10
  38.7 0.7 %collective-permute-start.7 = (bf16[64,2304]{1,0:T(8,128)(2,1)S(1)}, bf16[64,2304]{1,0:T(8,128)(2,1)S(1)}, u32[]{:S(2)}, u32[]{:S(2)}) collective-permute-start(bf16[64,2304]{1,0:T(8,128)(2,1)S(1)} %get-tuple-element.56.own_ref), channel_id=1, source_target_pairs={{4,8},{8,4},{5,9},{9,5},{6,10},{10,6},{7,11},{11,7},{20,24},{24,20... | collective-permute-start | bytes 884744 | tf_op jit(solution)/shard_map/ppermute | solution.py:698
  39.4 0.1 collective-permute-start.5
  39.5 1.2 %collective-permute-done.5 = f32[32,64]{1,0:T(8,128)S(1)} collective-permute-done((f32[32,64]{1,0:T(8,128)S(1)}, f32[32,64]{1,0:T(8,128)S(1)}, u32[]{:S(2)}, u32[]{:S(2)}) %collective-permute-start.5) | collective-permute-done | bytes 8224 | tf_op jit(solution)/shard_map/ppermute | solution.py:802
  40.7 1.5 %collective-permute-start.6 = (f32[32,64]{1,0:T(8,128)S(1)}, f32[32,64]{1,0:T(8,128)S(1)}, u32[]{:S(2)}, u32[]{:S(2)}) collective-permute-start(f32[32,64]{1,0:T(8,128)S(1)} %add.9), channel_id=1, source_target_pairs={{0,2},{1,3},{2,0},{3,1},{4,6},{5,7},{6,4},{7,5},{8,10},{9,11},{10,... | collective-permute-start | bytes 24584 | tf_op jit(solution)/shard_map/ppermute | solution.py:802
  42.2 2.3 %collective-permute-done.6 = f32[32,64]{1,0:T(8,128)S(1)} collective-permute-done((f32[32,64]{1,0:T(8,128)S(1)}, f32[32,64]{1,0:T(8,128)S(1)}, u32[]{:S(2)}, u32[]{:S(2)}) %collective-permute-start.6) | collective-permute-done | bytes 8224 | tf_op jit(solution)/shard_map/ppermute | solution.py:802
  44.4 0.0 collective-permute-done.7.come_ref
  44.4 8.8 %collective-permute-done.3.refs_9_.part_ref = bf16[128,2048]{1,0:T(8,128)(2,1)S(1)} collective-permute-done((bf16[128,2048]{1,0:T(8,128)(2,1)S(1)}, bf16[128,2048]{1,0:T(8,128)(2,1)S(1)}, u32[]{:S(2)}, u32[]{:S(2)}) %collective-permute-start.3) | collective-permute-done | bytes 524320 | tf_op jit(solution)/shard_map/ppermute | solution.py:698
  53.2 0.1 total.1.own_ref
  53.3 1.3 %collective-permute-start.8 = (bf16[64,2304]{1,0:T(8,128)(2,1)S(1)}, bf16[64,2304]{1,0:T(8,128)(2,1)S(1)}, u32[]{:S(2)}, u32[]{:S(2)}) collective-permute-start(bf16[64,2304]{1,0:T(8,128)(2,1)S(1)} %total.1.own_ref), channel_id=1, source_target_pairs={{4,0},{8,12},{5,1},{9,13},{6,2},{10,14},{7,3},{11,15},{20,16},{24,... | collective-permute-start | bytes 884744 | tf_op jit(solution)/shard_map/ppermute | solution.py:698
  54.6 0.7 collective-permute-start.9
  55.3 0.0 collective-permute-done.9
  55.3 1.3 %collective-permute-start.10 = (f32[32,64]{1,0:T(8,128)S(1)}, f32[32,64]{1,0:T(8,128)S(1)}, u32[]{:S(2)}, u32[]{:S(2)}) collective-permute-start(f32[32,64]{1,0:T(8,128)S(1)} %add.11.first_ref), channel_id=1, source_target_pairs={{4,0},{8,12},{5,1},{9,13},{6,2},{10,14},{7,3},{11,15},{20,16},{24,... | collective-permute-start | bytes 24584 | tf_op jit(solution)/shard_map/ppermute | solution.py:698
  56.6 0.0 copy-done
  56.6 0.0 copy-done.1
  56.6 0.0 copy-done.2
  56.6 0.0 copy-done.3
  56.6 0.0 copy-done.9
  56.7 2.1 %gates.1 = (bf16[128,2048]{1,0:T(8,128)(2,1)}, bf16[128,2048]{1,0:T(8,128)(2,1)}, bf16[128,2048]{1,0:T(8,128)(2,1)}) custom-call(s32[1]{0:T(128)} %bitcast.rank_ref.refs_0_.refs_1_, bf16[128,2048]{1,0:T(8,128)(2,1)S(1)} %copy-done, bf16[128,2048]{1,0:T(8,128)(2,1)S(1)} %copy-done.1, bf16[128,2048]{1,0:T(8,128)(2,1)S(1)} %copy-done.2, ...), custom_call_target="tpu_custom_call" | custom-call | bytes 262144 | tf_op jit(solution)/shard_map/gates/pallas_call | solution.py:814
  58.7 7.2 %collective-permute-done.10.first_come_ref = f32[32,64]{1,0:T(8,128)S(1)} collective-permute-done((f32[32,64]{1,0:T(8,128)S(1)}, f32[32,64]{1,0:T(8,128)S(1)}, u32[]{:S(2)}, u32[]{:S(2)}) %collective-permute-start.10) | collective-permute-done | bytes 8224 | tf_op jit(solution)/shard_map/ppermute | solution.py:698
  65.9 0.0 collective-permute-done.8.come_ref
  65.9 0.9 %finish.1 = (f32[64,2048]{1,0:T(8,128)}, f32[32,64]{1,0:T(8,128)}, f32[1,2048]{1,0:T(1,128)}) custom-call(s32[1]{0:T(128)} %bitcast.rank_ref.refs_0_.refs_1_, bf16[64,2304]{1,0:T(8,128)(2,1)S(1)} %total.1.own_ref, bf16[64,2304]{1,0:T(8,128)(2,1)S(1)} %collective-permute-done.8.come_ref, f32[32,64]{1,0:T(8,128)S(1)} %add.11.first_ref, ...), custom_call_target="tpu_custom_call" | custom-call | bytes 262144 | tf_op jit(solution)/shard_map/finish/pallas_call | solution.py:824
  (6 shorter events, 0.0 us)
Async XLA Ops:
  3.3 18.4 %copy-start.4 = (f32[64,2048]{1,0:T(8,128)S(1)}, f32[64,2048]{1,0:T(8,128)}, u32[]{:S(2)}) copy-start(f32[64,2048]{1,0:T(8,128)} %refs_5_.1) | copy-start | bytes 1572868
  3.3 18.4 %copy-start.5 = (bf16[256,256]{1,0:T(8,128)(2,1)S(1)}, bf16[256,256]{1,0:T(8,128)(2,1)}, u32[]{:S(2)}) copy-start(bf16[256,256]{1,0:T(8,128)(2,1)} %constant.16.clone.front_ref.refs_6_.refs_3_.refs_7_) | copy-start | bytes 393220
  3.3 18.4 %copy-start.8 = (f32[2048]{0:T(1024)S(1)}, f32[2048]{0:T(1024)}, u32[]{:S(2)}) copy-start(f32[2048]{0:T(1024)} %param.20) | copy-start | bytes 24580
  3.3 18.4 %copy-start.13 = (f32[32,64]{1,0:T(8,128)S(1)}, f32[32,64]{1,0:T(8,128)}, u32[]{:S(2)}) copy-start(f32[32,64]{1,0:T(8,128)} %refs_1_.2) | copy-start | bytes 24580
  3.3 18.4 %copy-start.14 = (f32[512,32]{1,0:T(8,128)S(1)}, f32[512,32]{1,0:T(8,128)}, u32[]{:S(2)}) copy-start(f32[512,32]{1,0:T(8,128)} %constant.19.clone.feats_ref) | copy-start | bytes 196612
  3.3 26.2 %collective-permute-start = (bf16[128,2048]{1,0:T(8,128)(2,1)}, bf16[128,2048]{1,0:T(8,128)(2,1)S(1)}, u32[]{:S(2)}, u32[]{:S(2)}) collective-permute-start(bf16[128,2048]{1,0:T(8,128)(2,1)} %get-tuple-element.33.refs_2_.x0_ref), channel_id=1, source_target_pairs={{0,4},{4,8},{8,12},{1,5},{5,9},{9,13},{2,6},{6,10},{10,14},{3,7},{... | collective-permute-start | bytes 1572872 | tf_op jit(solution)/shard_map/ppermute | solution.py:698
  8.4 21.1 %collective-permute-start.1 = (bf16[128,2048]{1,0:T(8,128)(2,1)}, bf16[128,2048]{1,0:T(8,128)(2,1)S(1)}, u32[]{:S(2)}, u32[]{:S(2)}) collective-permute-start(bf16[128,2048]{1,0:T(8,128)(2,1)} %get-tuple-element.34.refs_3_.c0_ref), channel_id=1, source_target_pairs={{4,0},{8,4},{12,8},{5,1},{9,5},{13,9},{6,2},{10,6},{14,10},{7,3},{... | collective-permute-start | bytes 1572872 | tf_op jit(solution)/shard_map/ppermute | solution.py:698
  15.9 12.4 %copy-start.17 = (bf16[64,2304]{1,0:T(8,128)(2,1)S(1)}, bf16[64,2304]{1,0:T(8,128)(2,1)}, u32[]{:S(2)}) copy-start(bf16[64,2304]{1,0:T(8,128)(2,1)} %get-tuple-element.54) | copy-start | bytes 884740
  15.9 13.7 %copy-start.6 = (bf16[256,256]{1,0:T(8,128)(2,1)S(1)}, bf16[256,256]{1,0:T(8,128)(2,1)}, u32[]{:S(2)}) copy-start(bf16[256,256]{1,0:T(8,128)(2,1)} %constant.17.clone.refs_7_.back_ref.refs_4_.refs_8_) | copy-start | bytes 393220
  15.9 13.7 %copy-start.7 = (f32[32,512]{1,0:T(8,128)S(1)}, f32[32,512]{1,0:T(8,128)}, u32[]{:S(2)}) copy-start(f32[32,512]{1,0:T(8,128)} %constant.18.clone.refs_8_.featt_ref.refs_10_) | copy-start | bytes 196612
  15.9 13.7 %copy-start.11 = (bf16[128,2048]{1,0:T(8,128)(2,1)S(1)}, bf16[128,2048]{1,0:T(8,128)(2,1)}, u32[]{:S(2)}) copy-start(bf16[128,2048]{1,0:T(8,128)(2,1)} %get-tuple-element.33.refs_2_.x0_ref) | copy-start | bytes 1572868
  15.9 13.7 %copy-start.12 = (bf16[128,2048]{1,0:T(8,128)(2,1)S(1)}, bf16[128,2048]{1,0:T(8,128)(2,1)}, u32[]{:S(2)}) copy-start(bf16[128,2048]{1,0:T(8,128)(2,1)} %get-tuple-element.34.refs_3_.c0_ref) | copy-start | bytes 1572868
  15.9 13.7 %copy-start.15 = (f32[64,2048]{1,0:T(8,128)S(1)}, f32[64,2048]{1,0:T(8,128)}, u32[]{:S(2)}) copy-start(f32[64,2048]{1,0:T(8,128)} %get-tuple-element.40.own_ref) | copy-start | bytes 1572868
  15.9 13.7 %copy-start.16 = (f32[32,64]{1,0:T(8,128)S(1)}, f32[32,64]{1,0:T(8,128)}, u32[]{:S(2)}) copy-start(f32[32,64]{1,0:T(8,128)} %get-tuple-element.41.own_first_ref) | copy-start | bytes 24580
  15.9 18.3 %collective-permute-start.2 = (bf16[128,2048]{1,0:T(8,128)(2,1)}, bf16[128,2048]{1,0:T(8,128)(2,1)S(1)}, u32[]{:S(2)}, u32[]{:S(2)}) collective-permute-start(bf16[128,2048]{1,0:T(8,128)(2,1)} %get-tuple-element.44), channel_id=1, source_target_pairs={{0,8},{12,4},{1,9},{13,5},{2,10},{14,6},{3,11},{15,7},{16,24},{28,... | collective-permute-start | bytes 1572872 | tf_op jit(solution)/shard_map/ppermute | solution.py:698
  28.2 10.5 %collective-permute-start.4 = (bf16[64,2304]{1,0:T(8,128)(2,1)S(1)}, bf16[64,2304]{1,0:T(8,128)(2,1)S(1)}, u32[]{:S(2)}, u32[]{:S(2)}) collective-permute-start(bf16[64,2304]{1,0:T(8,128)(2,1)S(1)} %copy-done.17), channel_id=1, source_target_pairs={{0,4},{12,8},{1,5},{13,9},{2,6},{14,10},{3,7},{15,11},{16,20},{28,... | collective-permute-start | bytes 884744 | tf_op jit(solution)/shard_map/ppermute | solution.py:698
  33.7 5.1 %copy-start.10 = (f32[1,2048]{1,0:T(1,128)S(1)}, f32[1,2048]{1,0:T(1,128)}, u32[]{:S(2)}) copy-start(f32[1,2048]{1,0:T(1,128)} %get-tuple-element.38.refs_9_.refs_14_) | copy-start | bytes 24580
  34.3 22.3 %copy-start = (bf16[128,2048]{1,0:T(8,128)(2,1)S(1)}, bf16[128,2048]{1,0:T(8,128)(2,1)}, u32[]{:S(2)}) copy-start(bf16[128,2048]{1,0:T(8,128)(2,1)} %refs_1_.3) | copy-start | bytes 1572868
  34.3 22.3 %copy-start.1 = (bf16[128,2048]{1,0:T(8,128)(2,1)S(1)}, bf16[128,2048]{1,0:T(8,128)(2,1)}, u32[]{:S(2)}) copy-start(bf16[128,2048]{1,0:T(8,128)(2,1)} %refs_2_.1) | copy-start | bytes 1572868
  34.3 22.3 %copy-start.2 = (bf16[128,2048]{1,0:T(8,128)(2,1)S(1)}, bf16[128,2048]{1,0:T(8,128)(2,1)}, u32[]{:S(2)}) copy-start(bf16[128,2048]{1,0:T(8,128)(2,1)} %refs_3_.2) | copy-start | bytes 1572868
  34.3 22.4 %copy-start.3 = (bf16[128,2048]{1,0:T(8,128)(2,1)S(1)}, bf16[128,2048]{1,0:T(8,128)(2,1)}, u32[]{:S(2)}) copy-start(bf16[128,2048]{1,0:T(8,128)(2,1)} %refs_4_.4) | copy-start | bytes 1572868
  34.3 22.4 %copy-start.9 = (f32[2048]{0:T(1024)S(1)}, f32[2048]{0:T(1024)}, u32[]{:S(2)}) copy-start(f32[2048]{0:T(1024)} %param.19) | copy-start | bytes 24580
  34.3 18.9 %collective-permute-start.3 = (bf16[128,2048]{1,0:T(8,128)(2,1)S(1)}, bf16[128,2048]{1,0:T(8,128)(2,1)S(1)}, u32[]{:S(2)}, u32[]{:S(2)}) collective-permute-start(bf16[128,2048]{1,0:T(8,128)(2,1)S(1)} %get-tuple-element.47), channel_id=1, source_target_pairs={{4,0},{8,12},{5,1},{9,13},{6,2},{10,14},{7,3},{11,15},{20,16},{24,... | collective-permute-start | bytes 1572872 | tf_op jit(solution)/shard_map/ppermute | solution.py:698
  38.7 5.7 %collective-permute-start.7 = (bf16[64,2304]{1,0:T(8,128)(2,1)S(1)}, bf16[64,2304]{1,0:T(8,128)(2,1)S(1)}, u32[]{:S(2)}, u32[]{:S(2)}) collective-permute-start(bf16[64,2304]{1,0:T(8,128)(2,1)S(1)} %get-tuple-element.56.own_ref), channel_id=1, source_target_pairs={{4,8},{8,4},{5,9},{9,5},{6,10},{10,6},{7,11},{11,7},{20,24},{24,20... | collective-permute-start | bytes 884744 | tf_op jit(solution)/shard_map/ppermute | solution.py:698
  39.4 1.2 %collective-permute-start.5 = (f32[32,64]{1,0:T(8,128)S(1)}, f32[32,64]{1,0:T(8,128)S(1)}, u32[]{:S(2)}, u32[]{:S(2)}) collective-permute-start(f32[32,64]{1,0:T(8,128)S(1)} %get-tuple-element.55), channel_id=1, source_target_pairs={{0,1},{1,0},{2,3},{3,2},{4,5},{5,4},{6,7},{7,6},{8,9},{9,8},{10,11... | collective-permute-start | bytes 24584 | tf_op jit(solution)/shard_map/ppermute | solution.py:802
  40.7 3.7 %collective-permute-start.6 = (f32[32,64]{1,0:T(8,128)S(1)}, f32[32,64]{1,0:T(8,128)S(1)}, u32[]{:S(2)}, u32[]{:S(2)}) collective-permute-start(f32[32,64]{1,0:T(8,128)S(1)} %add.9), channel_id=1, source_target_pairs={{0,2},{1,3},{2,0},{3,1},{4,6},{5,7},{6,4},{7,5},{8,10},{9,11},{10,... | collective-permute-start | bytes 24584 | tf_op jit(solution)/shard_map/ppermute | solution.py:802
  53.3 12.6 %collective-permute-start.8 = (bf16[64,2304]{1,0:T(8,128)(2,1)S(1)}, bf16[64,2304]{1,0:T(8,128)(2,1)S(1)}, u32[]{:S(2)}, u32[]{:S(2)}) collective-permute-start(bf16[64,2304]{1,0:T(8,128)(2,1)S(1)} %total.1.own_ref), channel_id=1, source_target_pairs={{4,0},{8,12},{5,1},{9,13},{6,2},{10,14},{7,3},{11,15},{20,16},{24,... | collective-permute-start | bytes 884744 | tf_op jit(solution)/shard_map/ppermute | solution.py:698
  54.6 0.7 %collective-permute-start.9 = (f32[32,64]{1,0:T(8,128)S(1)}, f32[32,64]{1,0:T(8,128)S(1)}, u32[]{:S(2)}, u32[]{:S(2)}) collective-permute-start(f32[32,64]{1,0:T(8,128)S(1)} %add.10.first_ref), channel_id=1, source_target_pairs={{4,8},{8,4},{5,9},{9,5},{6,10},{10,6},{7,11},{11,7},{20,24},{24,20... | collective-permute-start | bytes 24584 | tf_op jit(solution)/shard_map/ppermute | solution.py:698
  55.3 10.6 %collective-permute-start.10 = (f32[32,64]{1,0:T(8,128)S(1)}, f32[32,64]{1,0:T(8,128)S(1)}, u32[]{:S(2)}, u32[]{:S(2)}) collective-permute-start(f32[32,64]{1,0:T(8,128)S(1)} %add.11.first_ref), channel_id=1, source_target_pairs={{4,0},{8,12},{5,1},{9,13},{6,2},{10,14},{7,3},{11,15},{20,16},{24,... | collective-permute-start | bytes 24584 | tf_op jit(solution)/shard_map/ppermute | solution.py:698

commit v11 on v10

--- a/solution.py
+++ b/solution.py
@@ -292,12 +292,13 @@
 CUBE = (slice(None), slice(None))
 
 
-def products_kernel(rank_ref, one_ref, two_ref, val_ref, out_ref, source_ref, cotan_ref, edge_ref, bias_ref):
+def products_kernel(rank_ref, one_ref, two_ref, val_ref, out_ref, pair_ref, other_ref, edge_ref, bias_ref):
     source = one_ref[...].astype(f32) * val_ref[...].astype(f32)
     cotan = out_ref[...].astype(f32) * two_ref[...].astype(f32)
-    source_ref[...] = source.astype(bf16)
-    cotan_ref[...] = cotan.astype(bf16)
-    edge_ref[...] = jnp.where(rank_ref[0] == 0, source, cotan).astype(bf16)
+    even = rank_ref[0] % 2 == 0
+    pair_ref[...] = jnp.where(even, source, cotan).astype(bf16)
+    edge_ref[...] = pair_ref[...]
+    other_ref[...] = jnp.where(even, cotan, source).astype(bf16)
     part = jnp.sum(source * cotan, axis=0, keepdims=True)
 
     @pl.when(pl.program_id(0) == 0)
@@ -307,6 +308,10 @@
     @pl.when(pl.program_id(0) > 0)
     def _():
         bias_ref[...] += part
+
+
+def ordered(first, a, b):
+    return (jnp.where(first, a, b), jnp.where(first, b, a))
 
 
 def sin_cos(angle):
@@ -367,11 +372,11 @@
         before = now
 
 
-def own_kernel(rows, shards, channels, blocks, width, *refs):
-    inputs, (sums_out, send_out, first_out), held = refs[:10], refs[11:14], refs[15:25]
-    sums_ref, send_ref, own_first_ref, trans_ref, acc_ref, sems, out_sems = refs[25:]
+def own_kernel(rows, shards, channels, blocks, width, rank_ref, *refs):
+    inputs, send_out, held = refs[:10], refs[10], refs[11:21]
+    send_ref, trans_ref, acc_ref, sems, out_sem = refs[21:]
     (
-        feats_ref, first_ref, source_ref, cotan_ref, weight_ref, rate_ref, front_ref, back_ref, featt_ref, bias_ref
+        feats_ref, first_ref, pair_ref, other_ref, weight_ref, rate_ref, front_ref, back_ref, featt_ref, bias_ref
     ) = held
     copies = [pltpu.make_async_copy(far, near, sems.at[i]) for i, (far, near) in enumerate(zip(inputs, held))]
     for copy in copies:
@@ -383,47 +388,29 @@
     trans_ref[...] = turned_over(hidden, slope)
     for copy in copies[2:]:
         copy.wait()
-
-    def leaving(block):
-        cols = pl.ds(pl.multiple_of(block * width, width), width)
-        return pltpu.make_async_copy(sums_ref.at[:, cols], sums_out.at[:, cols], out_sems.at[block])
-
-    def strip(block, blocks, *views):
-        own_strip(rows, shards, *views)
-        leaving(block).start()
-
-    kinds = (ROWS, ROWS, ROWS, ROWS, None, None, None, ROWS, ROWS, None)
-    looped(strip, kinds, blocks, width)(
-        source_ref, cotan_ref, weight_ref, rate_ref, front_ref, back_ref, trans_ref, sums_ref, send_ref, acc_ref
+    kinds = (None, ROWS, ROWS, ROWS, ROWS, None, None, None, ROWS, None)
+    looped(functools.partial(own_strip, rows, shards), kinds, blocks, width)(
+        rank_ref, pair_ref, other_ref, weight_ref, rate_ref, front_ref, back_ref, trans_ref, send_ref, acc_ref
     )
     first = exact_dot(featt_ref[:, :rows], acc_ref[...] * slope)
-    own_first_ref[...] = first
     put_side(send_ref, channels, fold(bias_ref[...]), first)
-    ends = [
-        pltpu.make_async_copy(own_first_ref, first_out, out_sems.at[blocks]),
-        pltpu.make_async_copy(send_ref, send_out, out_sems.at[blocks + 1]),
-    ]
-    for end in ends:
-        end.start()
-    for block in range(blocks):
-        leaving(block).wait()
-    for end in ends:
-        end.wait()
+    last = pltpu.make_async_copy(send_ref, send_out, out_sem)
+    last.start()
+    last.wait()
 
 
 def own_strip(
-    rows, shards, source_ref, cotan_ref, weight_ref, rate_ref, front_ref, back_ref, trans_ref, sums_ref,
+    rows, shards, block, blocks, rank_ref, pair_ref, other_ref, weight_ref, rate_ref, front_ref, back_ref, trans_ref,
     send_ref, acc_ref,
 ):
-    x0 = forward(front_ref, source_ref[...])
-    c0 = forward(front_ref, cotan_ref[...])
+    source, cotan = ordered(rank_ref[0] % 2 == 0, pair_ref[...], other_ref[...])
+    x0 = forward(front_ref, source)
+    c0 = forward(front_ref, cotan)
     pair = conj_times((x0[:rows], x0[rows:]), (c0[:rows], c0[rows:]))
     high, low = split(jnp.concatenate(pair, axis=0))
     env = decay(rate_ref[...], rows, float(rows * shards) ** -0.5)
     m_high, m_low = split(backward(back_ref, high, low) * env)
-    sums = weight_sums(trans_ref[...], m_high, m_low)
-    sums_ref[...] = sums
-    send_ref[...] = sums.astype(bf16)
+    send_ref[...] = weight_sums(trans_ref[...], m_high, m_low).astype(bf16)
     acc_ref[...] += hidden_sums(m_high, m_low, *split(weight_ref[...]))
 
 
@@ -448,70 +435,92 @@
 
 
 def near_kernel(
-    rows, shards, blocks, width, rank_ref, x0_ref, c0_ref, x1_ref, c1_ref, spec_ref, weight_ref, rate_ref, front_ref,
-    back_ref, trans_ref, featt_ref, slope_ref, own_ref, own_first_ref, conv_ref, corr_ref, ahead_ref, sums_ref,
-    first_ref, fields, fast, high_ref, low_ref, acc_ref,
+    rows, shards, blocks, width, rank_ref, pair_ref, other_ref, pair_in_ref, middle_in_ref, spec_ref, weight_ref,
+    rate_ref, front_ref, back_ref, trans_ref, featt_ref, slope_ref, conv_ref, corr_ref, ahead_ref, sums_ref, first_ref,
+    fields, fast, high_ref, low_ref, acc_ref,
 ):
     rank = rank_ref[0]
     inner = jnp.logical_and(rank > 0, rank < shards - 1)
     count = shards - 1
-    tables = (front_ref, back_ref)
-    blocks_in = (x0_ref, c0_ref, x1_ref, c1_ref)
+    kinds = (None, None, None) + (ROWS,) * 4 + (CUBE, ROWS, ROWS)
+    common = (
+        rank_ref, front_ref, back_ref, pair_ref, other_ref, pair_in_ref, middle_in_ref, spec_ref, conv_ref, corr_ref,
+        fields, fast,
+    )
 
     @pl.when(jnp.logical_not(inner))
     def _():
-        looped(
-            functools.partial(near_strip, rows, shards, False),
-            (None, None, None) + (ROWS,) * 4 + (CUBE, ROWS, ROWS), blocks, width,
-        )(rank_ref, *tables, *blocks_in, spec_ref, conv_ref, corr_ref, fields, fast)
+        looped(functools.partial(edge_strip, rows, shards), kinds, blocks, width)(*common)
 
     @pl.when(inner)
     def _():
         acc_ref[...] = jnp.zeros_like(acc_ref)
         looped(
-            functools.partial(near_strip, rows, shards, True),
-            (None, None, None) + (ROWS,) * 4 + (CUBE, ROWS, ROWS) + (None, None, None) + (ROWS,) * 5, blocks, width,
-        )(
-            rank_ref, *tables, *blocks_in, spec_ref, conv_ref, corr_ref, fields, fast, trans_ref, weight_ref, rate_ref,
-            own_ref, ahead_ref, sums_ref, high_ref, low_ref, acc_ref,
-        )
-        first_ref[...] = own_first_ref[...] + exact_dot(
+            functools.partial(inner_strip, rows, shards), kinds + (None, None, None) + (ROWS,) * 4, blocks, width
+        )(*common, trans_ref, weight_ref, rate_ref, ahead_ref, sums_ref, high_ref, low_ref, acc_ref)
+        first_ref[...] = exact_dot(
             featt_ref[:, : count * rows], acc_ref[...] * slope_ref[: count * rows, :]
         )
 
 
-def near_strip(
-    rows, shards, inner, block, blocks, rank_ref, front_ref, back_ref, x0_ref, c0_ref, x1_ref, c1_ref, spec_ref,
-    conv_ref, corr_ref, fields, fast, *rest
-):
-    rank = rank_ref[0]
+def edge_strip(
+    rows, shards, block, blocks, rank_ref, front_ref, back_ref, pair_ref, other_ref, pair_in_ref, middle_in_ref,
+    spec_ref, conv_ref, corr_ref, fields, fast,
+):
+    del middle_in_ref
+    top = rank_ref[0] == shards - 1
+    source, cotan = ordered(rank_ref[0] % 2 == 0, pair_ref[...], other_ref[...])
+    for index, block_in in enumerate((source, cotan, pair_in_ref[...])):
+        fields[index] = forward(front_ref, block_in)
+    on_conv = jnp.where(top, 1.0, 0.0).astype(f32)
+    on_corr = jnp.where(top, 0.0, 1.0).astype(f32)
+    for re, im, sign in row_groups(rows):
+        x0, c0, near = ((fields[i, re, :], fields[i, im, :]) for i in range(3))
+        w0, w1 = ((spec_ref[i, re, :].astype(f32), spec_ref[i, im, :].astype(f32)) for i in range(2))
+        values = (
+            plus(times(w0, x0), scaled(times(w1, near), on_conv)),
+            plus(conj_times(w0, c0), scaled(conj_times(w1, near), on_corr)),
+        )
+        for index, value in enumerate(values):
+            fast[index, re, :] = value[0].astype(bf16)
+            fast[index, im, :] = value[1].astype(bf16)
+    conv_ref[...] = backward(back_ref, fast[0])
+    corr_ref[...] = backward(back_ref, fast[1])
+
+
+def inner_strip(
+    rows, shards, block, blocks, rank_ref, front_ref, back_ref, pair_ref, other_ref, pair_in_ref, middle_in_ref,
+    spec_ref, conv_ref, corr_ref, fields, fast, trans_ref, weight_ref, rate_ref, ahead_ref, sums_ref, high_ref, low_ref,
+    acc_ref,
+):
+    lower = rank_ref[0] == 1
+    upper = jnp.where(lower, 0.0, 1.0).astype(f32)
+    side = jnp.where(lower, -1.0, 1.0).astype(f32)
     count = shards - 1
-    if inner:
-        trans_ref, weight_ref, rate_ref, own_ref, ahead_ref, sums_ref, high_ref, low_ref, acc_ref = rest
-        lower = rank == 1
-        upper = jnp.where(rank == 2, 1.0, 0.0).astype(f32)
-        side = jnp.where(rank == 2, 1.0, -1.0).astype(f32)
-    for index, ref in enumerate((x0_ref, c0_ref, x1_ref, c1_ref)):
-        fields[index] = forward(front_ref, ref[...])
+    blocks_in = (
+        *ordered(lower, other_ref[...], pair_ref[...]), *ordered(lower, pair_in_ref[...], middle_in_ref[...])
+    )
+    for index, block_in in enumerate(blocks_in):
+        fields[index] = forward(front_ref, block_in)
     for re, im, sign in row_groups(rows):
         x0, c0, x1, c1 = ((fields[i, re, :], fields[i, im, :]) for i in range(4))
         w0, w1, w2 = ((spec_ref[i, re, :].astype(f32), spec_ref[i, im, :].astype(f32)) for i in range(3))
-        values = [plus(times(w0, x0), times(w1, x1)), plus(conj_times(w0, c0), conj_times(w1, c1))]
-        if inner:
-            values.append(times((w2[0], w2[1] * side), choose(lower, c1, x1)))
+        values = (
+            plus(times(w0, x0), times(w1, x1)),
+            plus(conj_times(w0, c0), conj_times(w1, c1)),
+            times((w2[0], w2[1] * side), choose(lower, c1, x1)),
+        )
         for index, value in enumerate(values):
             fast[index, re, :] = value[0].astype(bf16)
             fast[index, im, :] = value[1].astype(bf16)
-        if inner:
-            one = plus(conj_times(x1, c0), scaled(conj_times(x0, c1), upper))
-            two = conj_times(x1, c1)
-            for index, value in enumerate((turned(one, sign), plus(one, turned(two, sign)), two)):
-                for part, where in zip(value, (re, im)):
-                    high_ref[index, where, :], low_ref[index, where, :] = split(part)
+        zero = conj_times(x0, c0)
+        one = plus(conj_times(x1, c0), scaled(conj_times(x0, c1), upper))
+        two = conj_times(x1, c1)
+        for index, value in enumerate((plus(zero, turned(one, sign)), plus(one, turned(two, sign)), two)):
+            for part, where in zip(value, (re, im)):
+                high_ref[index, where, :], low_ref[index, where, :] = split(part)
     conv_ref[...] = backward(back_ref, fast[0])
     corr_ref[...] = backward(back_ref, fast[1])
-    if not inner:
-        return
     ahead_ref[...] = backward(back_ref, fast[2])
     rate = rate_ref[...]
     env = decay(rate, rows, float(rows * shards) ** -0.5)
@@ -521,15 +530,15 @@
         parts.append(split(grad * (env * jnp.exp(rate * (-float(lag * rows))))))
     m_high = jnp.concatenate([p[0] for p in parts], axis=0)
     m_low = jnp.concatenate([p[1] for p in parts], axis=0)
-    sums_ref[...] = own_ref[...] + weight_sums(trans_ref[:, : count * rows], m_high, m_low)
+    sums_ref[...] = weight_sums(trans_ref[:, : count * rows], m_high, m_low)
     acc_ref[...] += hidden_sums(m_high, m_low, *split(weight_ref[...]))
 
 
-def on_inner(shards, rank_at, kernel):
+def only(inner, shards, rank_at, kernel):
     def run(*refs):
         rank = refs[rank_at][0]
 
-        @pl.when(jnp.logical_and(rank > 0, rank < shards - 1))
+        @pl.when(jnp.logical_and(rank > 0, rank < shards - 1) == inner)
         def _():
             kernel(*refs)
 
@@ -548,7 +557,7 @@
 
 
 def last_kernel(
-    rows, shards, channels, block, blocks, after_ref, rank_ref, x1_ref, c1_ref, far_ref, weight_ref, rate_ref, front_ref, back_ref,
+    rows, shards, channels, block, blocks, after_ref, rank_ref, near_ref, far_ref, weight_ref, rate_ref, front_ref, back_ref,
     trans_ref, featt_ref, slope_ref, sums_ref, first_ref, bias_ref, in_ref, pay_ref, total_ref, acc_ref,
 ):
     del after_ref
@@ -565,7 +574,7 @@
     @pl.when(mine)
     def _():
         sign = jnp.where(lower, 1.0, -1.0).astype(f32)
-        near = forward(front_ref, jnp.where(lower, x1_ref[...], c1_ref[...]))
+        near = forward(front_ref, near_ref[...])
         far = forward(front_ref, far_ref[...])
         three = conj_times((near[:rows], near[rows:]), (far[:rows], far[rows:]))
         three = (three[0], three[1] * sign)
@@ -697,8 +706,6 @@
     def move(array, pairs):
         return lax.ppermute(array, "ctx", pairs)
 
-    up = [(i, i + 1) for i in range(shards - 1)]
-    down = [(i + 1, i) for i in range(shards - 1)]
     inward = [(0, 1), (shards - 1, shards - 2)]
     outward = [(1, 0), (shards - 2, shards - 1)]
     across = [(1, 2), (2, 1)]
@@ -708,7 +715,7 @@
 
     row_step = max(rows // 2, 16)
     gate_rows = pl.BlockSpec((row_step, channels), lambda i: (i, 0))
-    x0, c0, edge, bias = pl.pallas_call(
+    pair, other, edge, bias = pl.pallas_call(
         products_kernel,
         grid=(rows // row_step,),
         in_specs=[smem] + [gate_rows] * 4,
@@ -717,28 +724,27 @@
         compiler_params=pltpu.CompilerParams(vmem_limit_bytes=64 * mebi),
         name="products",
     )(rank, x_one, x_two, values, grad_out)
-    x1 = move(x0, up)
-    c1 = move(c0, down)
+    pair_in = move(pair, inward + outward)
+    middle_in = move(other, across)
 
     own_shapes = [
         shape(rows, feat_count), shape(feat_count, hid_count), block_bf16, block_bf16, shape(hid_count, channels),
         shape(1, channels), shape(double, double, dtype=bf16), shape(double, double, dtype=bf16),
-        shape(feat_count, seq_len), shape(1, channels), shape(hid_count, channels), shape(*pay_shape, dtype=bf16),
-        shape(feat_count, hid_count),
+        shape(feat_count, seq_len), shape(1, channels), shape(*pay_shape, dtype=bf16),
     ]
-    own, send, own_first, edge = call(
-        functools.partial(own_kernel, rows, shards, channels, blocks, width), "own_pair", 8,
-        [shape(hid_count, channels), shape(*pay_shape, dtype=bf16), shape(feat_count, hid_count), block_bf16],
-        [anywhere] * 11,
-        out_specs=[anywhere] * 4,
+    (send,) = call(
+        only(False, shards, 0, functools.partial(own_kernel, rows, shards, channels, blocks, width)), "own_pair", 8,
+        [shape(*pay_shape, dtype=bf16)],
+        [smem] + [anywhere] * 10,
+        out_specs=[anywhere],
         scratch=[pltpu.VMEM(s.shape, s.dtype) for s in own_shapes]
         + [
             pltpu.VMEM((2 * hid_count, rows), bf16), pltpu.VMEM((rows, hid_count), f32),
-            pltpu.SemaphoreType.DMA((10,)), pltpu.SemaphoreType.DMA((blocks + 2,)),
+            pltpu.SemaphoreType.DMA((10,)), pltpu.SemaphoreType.DMA,
         ],
-        aliases={10: 3},
         limit=60,
-    )(feats[:rows], first_weight, x0, c0, second_weight, rate_row, front, back, featt, bias, edge)
+    )(rank, feats[:rows], first_weight, pair, other, second_weight, rate_row, front, back, featt, bias)
+    edge, _ = lax.optimization_barrier((edge, send))
     far = move(edge, [(0, 2), (shards - 1, shards - 3)])
 
     spec, trans, slope = call(
@@ -757,7 +763,7 @@
     conv, corr, ahead, sums, first = call(
         functools.partial(near_kernel, rows, shards, blocks, width), "near_blocks", 20,
         [block_f32] * 3 + [shape(hid_count, channels), shape(feat_count, hid_count)],
-        [smem] + [vmem] * 14,
+        [smem] + [vmem] * 12,
         scratch=[
             pltpu.VMEM((4, double, width), f32),
             pltpu.VMEM((3, double, width), bf16),
@@ -765,10 +771,11 @@
             pltpu.VMEM((shards - 1, double, width), bf16),
             pltpu.VMEM(((shards - 1) * rows, hid_count), f32),
         ],
-    )(rank, x0, c0, x1, c1, spec, second_weight, rate_row, front, back, trans, featt, slope, own, own_first)
+    )(rank, pair, other, pair_in, middle_in, spec, second_weight, rate_row, front, back, trans, featt, slope)
+
     part, late = call(
-        on_inner(
-            shards, 0,
+        only(
+            True, shards, 0,
             looped(
                 functools.partial(far_kernel, rows),
                 (None, ROWS, (slice(2, 4), slice(None)), None, None, ROWS, ROWS, ROWS),
@@ -782,19 +789,19 @@
     part_come = move(part, outward)
 
     pay, first = call(
-        on_inner(
-            shards, 1,
+        only(
+            True, shards, 1,
             looped(
                 functools.partial(last_kernel, rows, shards, channels),
-                (None, None, ROWS, ROWS, ROWS, ROWS, ROWS, None, None, None, None, None, ROWS),
+                (None, None, ROWS, ROWS, ROWS, ROWS, None, None, None, None, None, ROWS),
                 blocks, width,
             ),
         ),
         "last_pair", 1,
         [shape(*pay_shape, dtype=bf16), shape(feat_count, hid_count)],
-        [anywhere, smem] + [vmem] * 14,
+        [anywhere, smem] + [vmem] * 13,
         scratch=[pltpu.VMEM((2 * rows, hid_count), f32)],
-    )(late, rank, x1, c1, far, second_weight, rate_row, front, back, trans, featt, slope, sums, first, bias, come)
+    )(late, rank, pair_in, far, second_weight, rate_row, front, back, trans, featt, slope, sums, first, bias, come)
     pay_come = move(pay, across)
     group = lax.axis_size(("ch", "sub"))
     bit = 1

time: 67.1 us -> 73.4 us (1.094)
  waiting for transfers between devices: 23 us -> 36.3 us
  starting transfers between devices: 20.3 us -> 13.4 us
    ppermute x9, waiting for transfers between devices: 19.6 us -> 32.9 us  [move(): return lax.ppermute(array, 'ctx', pairs)]
    ppermute x9, starting transfers between devices: 18.7 us -> 11.9 us  [move(): return lax.ppermute(array, 'ctx', pairs)]
  transfers between devices with their start and end apart: 11 -> 11, of which waited for: 6 -> 6; matrix products, arithmetic and copies ran while one was open for 0% -> 0% of each run, Pallas kernels for 28% -> 25%
where the time goes in v11:
time: 73.4 us; the launch traced here: 73.1 us
  waiting for transfers between devices  36.3 us (49%)
  Pallas kernels  22.2 us (30%)
  starting transfers between devices  13.4 us (18%)
  between operations  1 us (1%)
    ppermute x9, waiting for transfers between devices, move(): return lax.ppermute(array, 'ctx', pairs)  32.9 us
    ppermute x9, starting transfers between devices, move(): return lax.ppermute(array, 'ctx', pairs)  11.9 us
    pallas_call x1, Pallas kernels, few_shards_body(): call(functools.partial(filters_kernel, rows, shards, blocks, width), 'fil...  6.5 us
    pallas_call x1, Pallas kernels, few_shards_body(): call(only(False, shards, 0, functools.partial(own_kernel, rows, shards, c...  6.09 us
    pallas_call x1, Pallas kernels, few_shards_body(): call(functools.partial(near_kernel, rows, shards, blocks, width), 'near_b...  3.8 us
    ppermute x2, waiting for transfers between devices, few_shards_body(): lax.ppermute(first, ('ch', 'sub'), [(i, i ^ bit) for i in range(group)])  3.42 us
    pallas_call x1, Pallas kernels, few_shards_body(): pl.pallas_call(products_kernel, grid=(rows // row_step,), in_specs=[smem]...  2.79 us
    pallas_call x1, Pallas kernels, few_shards_body(): call(looped(functools.partial(gates_kernel, shards), (None,) + (ROWS,) *...  2.08 us
  transfers between devices with their start and end apart: 11, of which 6 were waited for; matrix products, arithmetic and copies ran while one was open for 0% of the time, Pallas kernels for 25%

profile of v11, /device:TPU:0, one launch (start us, length us, event | category | flops | bytes accessed | tf_op | source)
XLA Modules:
  0.0 73.1 jit_solution(16821966087972279362)
XLA Ops:
  0.6 2.8 %products.1 = (bf16[128,2048]{1,0:T(8,128)(2,1)}, bf16[128,2048]{1,0:T(8,128)(2,1)}, bf16[128,2048]{1,0:T(8,128)(2,1)}, f32[1,2048]{1,0:T(1,128)}) custom-call(s32[1]{0:T(128)} %bitcast.rank_ref.refs_0_.refs_1_, bf16[128,2048]{1,0:T(8,128)(2,1)} %refs_1_.2, bf16[128,2048]{1,0:T(8,128)(2,1)} %refs_2_.3, bf16[128,2048]{1,0:T(8,128)(2,1)} %refs_3_.2, ...), custom_call_target="tpu_custom_call" | custom-call | tf_op jit(solution)/shard_map/products/pallas_call | solution.py:718
  3.4 0.0 copy-start.15
  3.4 0.0 copy-start.4
  3.4 0.0 copy-start.5
  3.5 0.0 copy-start.8
  3.5 0.0 copy-start.13
  3.5 0.0 copy-start.14
  3.5 3.1 %collective-permute-start = (bf16[128,2048]{1,0:T(8,128)(2,1)}, bf16[128,2048]{1,0:T(8,128)(2,1)S(1)}, u32[]{:S(2)}, u32[]{:S(2)}) collective-permute-start(bf16[128,2048]{1,0:T(8,128)(2,1)} %get-tuple-element.30.pair_ref.refs_3_), channel_id=1, source_target_pairs={{0,4},{12,8},{4,0},{8,12},{1,5},{13,9},{5,1},{9,13},{2,6},{14,10},... | collective-permute-start | bytes 1572872 | tf_op jit(solution)/shard_map/ppermute | solution.py:707
  6.6 0.7 collective-permute-start.1
  7.3 6.1 %own_pair.1 = bf16[64,2304]{1,0:T(8,128)(2,1)} custom-call(s32[1]{0:T(128)} %bitcast.rank_ref.refs_0_.refs_1_, f32[128,32]{1,0:T(8,128)} %constant.15.clone.refs_1_, f32[32,64]{1,0:T(8,128)} %refs_2_.2, bf16[128,2048]{1,0:T(8,128)(2,1)} %get-tuple-element.30.pair_ref.refs_3_, bf16[128,2048]{1,0:T(8,128)(2,1)} %get-tuple-element.31.other_ref.refs_4_, ...), custom_call_target="tpu_custom_call" | custom-call | flops 2147483648 | bytes 262144 | tf_op jit(solution)/shard_map/own_pair/pallas_call | solution.py:735
  13.4 0.0 copy-start.16
  13.4 0.0 copy-start.6
  13.4 0.0 copy-start.7
  13.4 0.0 copy-start.11
  13.4 0.0 copy-start.12
  13.4 0.0 copy-done.15
  13.4 1.5 %collective-permute-start.2 = (bf16[128,2048]{1,0:T(8,128)(2,1)S(1)}, bf16[128,2048]{1,0:T(8,128)(2,1)S(1)}, u32[]{:S(2)}, u32[]{:S(2)}) collective-permute-start(bf16[128,2048]{1,0:T(8,128)(2,1)S(1)} %copy-done.15), channel_id=1, source_target_pairs={{0,8},{12,4},{1,9},{13,5},{2,10},{14,6},{3,11},{15,7},{16,24},{28,... | collective-permute-start | bytes 1572872 | tf_op jit(solution)/shard_map/ppermute | solution.py:707
  14.9 0.0 copy-done.4
  14.9 0.0 copy-done.5
  14.9 0.0 copy-done.8
  14.9 0.0 copy-done.13
  14.9 0.0 copy-done.14
  15.0 6.5 %filters.1 = (bf16[4,256,2048]{2,1,0:T(8,128)(2,1)S(1)}, bf16[128,512]{1,0:T(8,128)(2,1)S(1)}, f32[512,64]{1,0:T(8,128)S(1)}) custom-call(f32[512,32]{1,0:T(8,128)S(1)} %copy-done.14, f32[32,64]{1,0:T(8,128)S(1)} %copy-done.13, f32[64,2048]{1,0:T(8,128)S(1)} %copy-done.4, f32[1,2048]{1,0:T(1,128)S(1)} %bitcast.5, bf16[256,256]{1,0:T(8,128)(2,1)S(1)} %copy-done.5), custom_call_target="tpu_custom_call" | custom-call | flops 2147483648 | bytes 262144 | tf_op jit(solution)/shard_map/filters/pallas_call | solution.py:750
  21.5 0.0 copy-done.16
  21.5 1.3 %collective-permute-start.4 = (bf16[64,2304]{1,0:T(8,128)(2,1)S(1)}, bf16[64,2304]{1,0:T(8,128)(2,1)S(1)}, u32[]{:S(2)}, u32[]{:S(2)}) collective-permute-start(bf16[64,2304]{1,0:T(8,128)(2,1)S(1)} %copy-done.16), channel_id=1, source_target_pairs={{0,4},{12,8},{1,5},{13,9},{2,6},{14,10},{3,7},{15,11},{16,20},{28,... | collective-permute-start | bytes 884744 | tf_op jit(solution)/shard_map/ppermute | solution.py:707
  22.8 0.0 collective-permute-done.pair_in_ref.refs_2_
  22.8 0.0 collective-permute-done.1.middle_in_ref
  22.8 0.0 copy-done.6
  22.8 0.0 copy-done.7
  22.8 0.0 copy-done.11
  22.8 0.0 copy-done.12
  22.8 3.8 %near_blocks.1 = (f32[128,2048]{1,0:T(8,128)S(1)}, f32[128,2048]{1,0:T(8,128)S(1)}, f32[128,2048]{1,0:T(8,128)S(1)}, f32[64,2048]{1,0:T(8,128)S(1)}, f32[32,64]{1,0:T(8,128)S(1)}) custom-call(s32[1]{0:T(128)} %bitcast.rank_ref.refs_0_.refs_1_, bf16[128,2048]{1,0:T(8,128)(2,1)S(1)} %copy-done.11, bf16[128,2048]{1,0:T(8,128)(2,1)S(1)} %copy-done.12, ...), custom_call_target="tpu_custom_call" | custom-call | flops 5368709120 | bytes 262144 | tf_op jit(solution)/shard_map/near_blocks/pallas_call | solution.py:763
  26.7 0.0 copy-start.10
  26.7 3.7 %collective-permute-done.2.refs_1_.refs_3_ = bf16[128,2048]{1,0:T(8,128)(2,1)S(1)} collective-permute-done((bf16[128,2048]{1,0:T(8,128)(2,1)S(1)}, bf16[128,2048]{1,0:T(8,128)(2,1)S(1)}, u32[]{:S(2)}, u32[]{:S(2)}) %collective-permute-start.2) | collective-permute-done | bytes 524320 | tf_op jit(solution)/shard_map/ppermute | solution.py:707
  30.4 0.0 copy-start
  30.4 0.0 copy-start.1
  30.4 0.0 copy-start.2
  30.4 0.0 copy-start.3
  30.4 0.0 copy-start.9
  30.4 1.4 %collective-permute-start.3 = (bf16[128,2048]{1,0:T(8,128)(2,1)S(1)}, bf16[128,2048]{1,0:T(8,128)(2,1)S(1)}, u32[]{:S(2)}, u32[]{:S(2)}) collective-permute-start(bf16[128,2048]{1,0:T(8,128)(2,1)S(1)} %get-tuple-element.42), channel_id=1, source_target_pairs={{4,0},{8,12},{5,1},{9,13},{6,2},{10,14},{7,3},{11,15},{20,16},{24,... | collective-permute-start | bytes 1572872 | tf_op jit(solution)/shard_map/ppermute | solution.py:707
  31.9 3.7 %collective-permute-done.4.refs_14_ = bf16[64,2304]{1,0:T(8,128)(2,1)S(1)} collective-permute-done((bf16[64,2304]{1,0:T(8,128)(2,1)S(1)}, bf16[64,2304]{1,0:T(8,128)(2,1)S(1)}, u32[]{:S(2)}, u32[]{:S(2)}) %collective-permute-start.4) | collective-permute-done | bytes 294944 | tf_op jit(solution)/shard_map/ppermute | solution.py:707
  35.6 0.0 copy-done.10
  35.6 0.7 collective-permute-start.7
  36.3 0.1 collective-permute-start.5
  36.3 1.2 %collective-permute-done.5 = f32[32,64]{1,0:T(8,128)S(1)} collective-permute-done((f32[32,64]{1,0:T(8,128)S(1)}, f32[32,64]{1,0:T(8,128)S(1)}, u32[]{:S(2)}, u32[]{:S(2)}) %collective-permute-start.5) | collective-permute-done | bytes 8224 | tf_op jit(solution)/shard_map/ppermute | solution.py:809
  37.5 1.5 %collective-permute-start.6 = (f32[32,64]{1,0:T(8,128)S(1)}, f32[32,64]{1,0:T(8,128)S(1)}, u32[]{:S(2)}, u32[]{:S(2)}) collective-permute-start(f32[32,64]{1,0:T(8,128)S(1)} %add.9), channel_id=1, source_target_pairs={{0,2},{1,3},{2,0},{3,1},{4,6},{5,7},{6,4},{7,5},{8,10},{9,11},{10,... | collective-permute-start | bytes 24584 | tf_op jit(solution)/shard_map/ppermute | solution.py:809
  39.0 2.2 %collective-permute-done.6 = f32[32,64]{1,0:T(8,128)S(1)} collective-permute-done((f32[32,64]{1,0:T(8,128)S(1)}, f32[32,64]{1,0:T(8,128)S(1)}, u32[]{:S(2)}, u32[]{:S(2)}) %collective-permute-start.6) | collective-permute-done | bytes 8224 | tf_op jit(solution)/shard_map/ppermute | solution.py:809
  41.3 0.0 collective-permute-done.7.come_ref
  41.3 18.3 %collective-permute-done.3.refs_9_.part_ref = bf16[128,2048]{1,0:T(8,128)(2,1)S(1)} collective-permute-done((bf16[128,2048]{1,0:T(8,128)(2,1)S(1)}, bf16[128,2048]{1,0:T(8,128)(2,1)S(1)}, u32[]{:S(2)}, u32[]{:S(2)}) %collective-permute-start.3) | collective-permute-done | bytes 524320 | tf_op jit(solution)/shard_map/ppermute | solution.py:707
  59.6 0.1 total.1.own_ref
  59.6 1.3 %collective-permute-start.8 = (bf16[64,2304]{1,0:T(8,128)(2,1)S(1)}, bf16[64,2304]{1,0:T(8,128)(2,1)S(1)}, u32[]{:S(2)}, u32[]{:S(2)}) collective-permute-start(bf16[64,2304]{1,0:T(8,128)(2,1)S(1)} %total.1.own_ref), channel_id=1, source_target_pairs={{4,0},{8,12},{5,1},{9,13},{6,2},{10,14},{7,3},{11,15},{20,16},{24,... | collective-permute-start | bytes 884744 | tf_op jit(solution)/shard_map/ppermute | solution.py:707
  60.9 0.7 collective-permute-start.9
  61.6 0.0 collective-permute-done.9
  61.6 1.3 %collective-permute-start.10 = (f32[32,64]{1,0:T(8,128)S(1)}, f32[32,64]{1,0:T(8,128)S(1)}, u32[]{:S(2)}, u32[]{:S(2)}) collective-permute-start(f32[32,64]{1,0:T(8,128)S(1)} %add.11.first_ref), channel_id=1, source_target_pairs={{4,0},{8,12},{5,1},{9,13},{6,2},{10,14},{7,3},{11,15},{20,16},{24,... | collective-permute-start | bytes 24584 | tf_op jit(solution)/shard_map/ppermute | solution.py:707
  62.9 0.0 copy-done
  62.9 0.0 copy-done.1
  63.0 0.0 copy-done.2
  63.0 0.0 copy-done.3
  63.0 0.0 copy-done.9
  63.0 2.1 %gates.1 = (bf16[128,2048]{1,0:T(8,128)(2,1)}, bf16[128,2048]{1,0:T(8,128)(2,1)}, bf16[128,2048]{1,0:T(8,128)(2,1)}) custom-call(s32[1]{0:T(128)} %bitcast.rank_ref.refs_0_.refs_1_, bf16[128,2048]{1,0:T(8,128)(2,1)S(1)} %copy-done, bf16[128,2048]{1,0:T(8,128)(2,1)S(1)} %copy-done.1, bf16[128,2048]{1,0:T(8,128)(2,1)S(1)} %copy-done.2, ...), custom_call_target="tpu_custom_call" | custom-call | bytes 262144 | tf_op jit(solution)/shard_map/gates/pallas_call | solution.py:821
  65.1 7.2 %collective-permute-done.10.first_come_ref = f32[32,64]{1,0:T(8,128)S(1)} collective-permute-done((f32[32,64]{1,0:T(8,128)S(1)}, f32[32,64]{1,0:T(8,128)S(1)}, u32[]{:S(2)}, u32[]{:S(2)}) %collective-permute-start.10) | collective-permute-done | bytes 8224 | tf_op jit(solution)/shard_map/ppermute | solution.py:707
  72.2 0.0 collective-permute-done.8.come_ref
  72.2 0.9 %finish.1 = (f32[64,2048]{1,0:T(8,128)}, f32[32,64]{1,0:T(8,128)}, f32[1,2048]{1,0:T(1,128)}) custom-call(s32[1]{0:T(128)} %bitcast.rank_ref.refs_0_.refs_1_, bf16[64,2304]{1,0:T(8,128)(2,1)S(1)} %total.1.own_ref, bf16[64,2304]{1,0:T(8,128)(2,1)S(1)} %collective-permute-done.8.come_ref, f32[32,64]{1,0:T(8,128)S(1)} %add.11.first_ref, ...), custom_call_target="tpu_custom_call" | custom-call | bytes 262144 | tf_op jit(solution)/shard_map/finish/pallas_call | solution.py:831
  (5 shorter events, 0.0 us)
Async XLA Ops:
  3.4 10.0 %copy-start.15 = (bf16[128,2048]{1,0:T(8,128)(2,1)S(1)}, bf16[128,2048]{1,0:T(8,128)(2,1)}, u32[]{:S(2)}) copy-start(bf16[128,2048]{1,0:T(8,128)(2,1)} %get-tuple-element.39) | copy-start | bytes 1572868
  3.4 11.5 %copy-start.4 = (f32[64,2048]{1,0:T(8,128)S(1)}, f32[64,2048]{1,0:T(8,128)}, u32[]{:S(2)}) copy-start(f32[64,2048]{1,0:T(8,128)} %refs_4_.4) | copy-start | bytes 1572868
  3.4 11.5 %copy-start.5 = (bf16[256,256]{1,0:T(8,128)(2,1)S(1)}, bf16[256,256]{1,0:T(8,128)(2,1)}, u32[]{:S(2)}) copy-start(bf16[256,256]{1,0:T(8,128)(2,1)} %constant.16.clone.front_ref.refs_7_.refs_3_.refs_6_) | copy-start | bytes 393220
  3.5 11.5 %copy-start.8 = (f32[2048]{0:T(1024)S(1)}, f32[2048]{0:T(1024)}, u32[]{:S(2)}) copy-start(f32[2048]{0:T(1024)} %param.20) | copy-start | bytes 24580
  3.5 11.5 %copy-start.13 = (f32[32,64]{1,0:T(8,128)S(1)}, f32[32,64]{1,0:T(8,128)}, u32[]{:S(2)}) copy-start(f32[32,64]{1,0:T(8,128)} %refs_2_.2) | copy-start | bytes 24580
  3.5 11.5 %copy-start.14 = (f32[512,32]{1,0:T(8,128)S(1)}, f32[512,32]{1,0:T(8,128)}, u32[]{:S(2)}) copy-start(f32[512,32]{1,0:T(8,128)} %constant.19.clone.feats_ref) | copy-start | bytes 196612
  3.5 19.3 %collective-permute-start = (bf16[128,2048]{1,0:T(8,128)(2,1)}, bf16[128,2048]{1,0:T(8,128)(2,1)S(1)}, u32[]{:S(2)}, u32[]{:S(2)}) collective-permute-start(bf16[128,2048]{1,0:T(8,128)(2,1)} %get-tuple-element.30.pair_ref.refs_3_), channel_id=1, source_target_pairs={{0,4},{12,8},{4,0},{8,12},{1,5},{13,9},{5,1},{9,13},{2,6},{14,10},... | collective-permute-start | bytes 1572872 | tf_op jit(solution)/shard_map/ppermute | solution.py:707
  6.6 16.2 %collective-permute-start.1 = (bf16[128,2048]{1,0:T(8,128)(2,1)}, bf16[128,2048]{1,0:T(8,128)(2,1)S(1)}, u32[]{:S(2)}, u32[]{:S(2)}) collective-permute-start(bf16[128,2048]{1,0:T(8,128)(2,1)} %get-tuple-element.31.other_ref.refs_4_), channel_id=1, source_target_pairs={{4,8},{8,4},{5,9},{9,5},{6,10},{10,6},{7,11},{11,7},{20,24},{24,20... | collective-permute-start | bytes 1572872 | tf_op jit(solution)/shard_map/ppermute | solution.py:707
  13.4 8.1 %copy-start.16 = (bf16[64,2304]{1,0:T(8,128)(2,1)S(1)}, bf16[64,2304]{1,0:T(8,128)(2,1)}, u32[]{:S(2)}) copy-start(bf16[64,2304]{1,0:T(8,128)(2,1)} %own_pair.1) | copy-start | bytes 884740
  13.4 9.4 %copy-start.6 = (bf16[256,256]{1,0:T(8,128)(2,1)S(1)}, bf16[256,256]{1,0:T(8,128)(2,1)}, u32[]{:S(2)}) copy-start(bf16[256,256]{1,0:T(8,128)(2,1)} %constant.17.clone.back_ref.refs_8_.refs_4_.refs_7_) | copy-start | bytes 393220
  13.4 9.4 %copy-start.7 = (f32[32,512]{1,0:T(8,128)S(1)}, f32[32,512]{1,0:T(8,128)}, u32[]{:S(2)}) copy-start(f32[32,512]{1,0:T(8,128)} %constant.18.clone.featt_ref.refs_9_) | copy-start | bytes 196612
  13.4 9.4 %copy-start.11 = (bf16[128,2048]{1,0:T(8,128)(2,1)S(1)}, bf16[128,2048]{1,0:T(8,128)(2,1)}, u32[]{:S(2)}) copy-start(bf16[128,2048]{1,0:T(8,128)(2,1)} %get-tuple-element.30.pair_ref.refs_3_) | copy-start | bytes 1572868
  13.4 9.4 %copy-start.12 = (bf16[128,2048]{1,0:T(8,128)(2,1)S(1)}, bf16[128,2048]{1,0:T(8,128)(2,1)}, u32[]{:S(2)}) copy-start(bf16[128,2048]{1,0:T(8,128)(2,1)} %get-tuple-element.31.other_ref.refs_4_) | copy-start | bytes 1572868
  13.4 17.0 %collective-permute-start.2 = (bf16[128,2048]{1,0:T(8,128)(2,1)S(1)}, bf16[128,2048]{1,0:T(8,128)(2,1)S(1)}, u32[]{:S(2)}, u32[]{:S(2)}) collective-permute-start(bf16[128,2048]{1,0:T(8,128)(2,1)S(1)} %copy-done.15), channel_id=1, source_target_pairs={{0,8},{12,4},{1,9},{13,5},{2,10},{14,6},{3,11},{15,7},{16,24},{28,... | collective-permute-start | bytes 1572872 | tf_op jit(solution)/shard_map/ppermute | solution.py:707
  21.5 14.1 %collective-permute-start.4 = (bf16[64,2304]{1,0:T(8,128)(2,1)S(1)}, bf16[64,2304]{1,0:T(8,128)(2,1)S(1)}, u32[]{:S(2)}, u32[]{:S(2)}) collective-permute-start(bf16[64,2304]{1,0:T(8,128)(2,1)S(1)} %copy-done.16), channel_id=1, source_target_pairs={{0,4},{12,8},{1,5},{13,9},{2,6},{14,10},{3,7},{15,11},{16,20},{28,... | collective-permute-start | bytes 884744 | tf_op jit(solution)/shard_map/ppermute | solution.py:707
  26.7 8.9 %copy-start.10 = (f32[1,2048]{1,0:T(1,128)S(1)}, f32[1,2048]{1,0:T(1,128)}, u32[]{:S(2)}) copy-start(f32[1,2048]{1,0:T(1,128)} %get-tuple-element.38.refs_10_.refs_13_) | copy-start | bytes 24580
  30.4 32.5 %copy-start = (bf16[128,2048]{1,0:T(8,128)(2,1)S(1)}, bf16[128,2048]{1,0:T(8,128)(2,1)}, u32[]{:S(2)}) copy-start(bf16[128,2048]{1,0:T(8,128)(2,1)} %refs_1_.2) | copy-start | bytes 1572868
  30.4 32.5 %copy-start.1 = (bf16[128,2048]{1,0:T(8,128)(2,1)S(1)}, bf16[128,2048]{1,0:T(8,128)(2,1)}, u32[]{:S(2)}) copy-start(bf16[128,2048]{1,0:T(8,128)(2,1)} %refs_2_.3) | copy-start | bytes 1572868
  30.4 32.5 %copy-start.2 = (bf16[128,2048]{1,0:T(8,128)(2,1)S(1)}, bf16[128,2048]{1,0:T(8,128)(2,1)}, u32[]{:S(2)}) copy-start(bf16[128,2048]{1,0:T(8,128)(2,1)} %refs_3_.2) | copy-start | bytes 1572868
  30.4 32.5 %copy-start.3 = (bf16[128,2048]{1,0:T(8,128)(2,1)S(1)}, bf16[128,2048]{1,0:T(8,128)(2,1)}, u32[]{:S(2)}) copy-start(bf16[128,2048]{1,0:T(8,128)(2,1)} %refs_4_.3) | copy-start | bytes 1572868
  30.4 32.6 %copy-start.9 = (f32[2048]{0:T(1024)S(1)}, f32[2048]{0:T(1024)}, u32[]{:S(2)}) copy-start(f32[2048]{0:T(1024)} %param.19) | copy-start | bytes 24580
  30.4 29.1 %collective-permute-start.3 = (bf16[128,2048]{1,0:T(8,128)(2,1)S(1)}, bf16[128,2048]{1,0:T(8,128)(2,1)S(1)}, u32[]{:S(2)}, u32[]{:S(2)}) collective-permute-start(bf16[128,2048]{1,0:T(8,128)(2,1)S(1)} %get-tuple-element.42), channel_id=1, source_target_pairs={{4,0},{8,12},{5,1},{9,13},{6,2},{10,14},{7,3},{11,15},{20,16},{24,... | collective-permute-start | bytes 1572872 | tf_op jit(solution)/shard_map/ppermute | solution.py:707
  35.6 5.7 %collective-permute-start.7 = (bf16[64,2304]{1,0:T(8,128)(2,1)S(1)}, bf16[64,2304]{1,0:T(8,128)(2,1)S(1)}, u32[]{:S(2)}, u32[]{:S(2)}) collective-permute-start(bf16[64,2304]{1,0:T(8,128)(2,1)S(1)} %get-tuple-element.50.own_ref), channel_id=1, source_target_pairs={{4,8},{8,4},{5,9},{9,5},{6,10},{10,6},{7,11},{11,7},{20,24},{24,20... | collective-permute-start | bytes 884744 | tf_op jit(solution)/shard_map/ppermute | solution.py:707
  36.3 1.2 %collective-permute-start.5 = (f32[32,64]{1,0:T(8,128)S(1)}, f32[32,64]{1,0:T(8,128)S(1)}, u32[]{:S(2)}, u32[]{:S(2)}) collective-permute-start(f32[32,64]{1,0:T(8,128)S(1)} %get-tuple-element.49), channel_id=1, source_target_pairs={{0,1},{1,0},{2,3},{3,2},{4,5},{5,4},{6,7},{7,6},{8,9},{9,8},{10,11... | collective-permute-start | bytes 24584 | tf_op jit(solution)/shard_map/ppermute | solution.py:809
  37.5 3.7 %collective-permute-start.6 = (f32[32,64]{1,0:T(8,128)S(1)}, f32[32,64]{1,0:T(8,128)S(1)}, u32[]{:S(2)}, u32[]{:S(2)}) collective-permute-start(f32[32,64]{1,0:T(8,128)S(1)} %add.9), channel_id=1, source_target_pairs={{0,2},{1,3},{2,0},{3,1},{4,6},{5,7},{6,4},{7,5},{8,10},{9,11},{10,... | collective-permute-start | bytes 24584 | tf_op jit(solution)/shard_map/ppermute | solution.py:809
  59.6 12.6 %collective-permute-start.8 = (bf16[64,2304]{1,0:T(8,128)(2,1)S(1)}, bf16[64,2304]{1,0:T(8,128)(2,1)S(1)}, u32[]{:S(2)}, u32[]{:S(2)}) collective-permute-start(bf16[64,2304]{1,0:T(8,128)(2,1)S(1)} %total.1.own_ref), channel_id=1, source_target_pairs={{4,0},{8,12},{5,1},{9,13},{6,2},{10,14},{7,3},{11,15},{20,16},{24,... | collective-permute-start | bytes 884744 | tf_op jit(solution)/shard_map/ppermute | solution.py:707
  60.9 0.7 collective-permute-start.9
  61.6 10.6 %collective-permute-start.10 = (f32[32,64]{1,0:T(8,128)S(1)}, f32[32,64]{1,0:T(8,128)S(1)}, u32[]{:S(2)}, u32[]{:S(2)}) collective-permute-start(f32[32,64]{1,0:T(8,128)S(1)} %add.11.first_ref), channel_id=1, source_target_pairs={{4,0},{8,12},{5,1},{9,13},{6,2},{10,14},{7,3},{11,15},{20,16},{24,... | collective-permute-start | bytes 24584 | tf_op jit(solution)/shard_map/ppermute | solution.py:707

commit v12 on v11

--- a/solution.py
+++ b/solution.py
@@ -744,9 +744,7 @@
         ],
         limit=60,
     )(rank, feats[:rows], first_weight, pair, other, second_weight, rate_row, front, back, featt, bias)
-    edge, _ = lax.optimization_barrier((edge, send))
-    far = move(edge, [(0, 2), (shards - 1, shards - 3)])
-
+    late_feats, _ = lax.optimization_barrier((jnp.asarray(feats), send))
     spec, trans, slope = call(
         functools.partial(filters_kernel, rows, shards, blocks, width), "filters", 8,
         [
@@ -755,9 +753,11 @@
         ],
         [vmem] * 5,
         scratch=[pltpu.VMEM((seq_len, 3 * hid_count), bf16)],
-    )(feats, first_weight, second_weight, rate_row, front)
-
-    send, _ = lax.optimization_barrier((send, slope))
+    )(late_feats, first_weight, second_weight, rate_row, front)
+
+    edge, _ = lax.optimization_barrier((edge, slope))
+    far = move(edge, [(0, 2), (shards - 1, shards - 3)])
+    send, _ = lax.optimization_barrier((send, pair_in))
     come = move(send, inward)
 
     conv, corr, ahead, sums, first = call(
@@ -802,7 +802,7 @@
         [anywhere, smem] + [vmem] * 13,
         scratch=[pltpu.VMEM((2 * rows, hid_count), f32)],
     )(late, rank, pair_in, far, second_weight, rate_row, front, back, trans, featt, slope, sums, first, bias, come)
-    pay_come = move(pay, across)
+    pay_come = move(pay, across + [(0, 0), (shards - 1, shards - 1)])
     group = lax.axis_size(("ch", "sub"))
     bit = 1
     while bit < group:
@@ -814,9 +814,9 @@
         [shape(*pay_shape, dtype=bf16)],
         [anywhere] * 2 + [vmem] * 2,
     )(part_come, first, pay, pay_come)
-    total_come = move(total, outward)
-    first = first + move(first, across)
-    first_come = move(first, outward)
+    total_come = move(total, inward + outward)
+    first = first + move(first, [(i, shards - 1 - i) for i in range(shards)])
+    first_come = move(first, inward + outward)
 
     grad_one, grad_two, grad_value = call(
         looped(

time: 73.4 us -> 67 us (0.913)
  waiting for transfers between devices: 36.3 us -> 28.3 us
  starting transfers between devices: 13.4 us -> 15.1 us
    ppermute x9, waiting for transfers between devices: 32.9 us -> 24.9 us  [move(): return lax.ppermute(array, 'ctx', pairs)]
    ppermute x9, starting transfers between devices: 11.9 us -> 13.5 us  [move(): return lax.ppermute(array, 'ctx', pairs)]
  transfers between devices with their start and end apart: 11 -> 11, of which waited for: 6 -> 7; matrix products, arithmetic and copies ran while one was open for 0% -> 0% of each run, Pallas kernels for 25% -> 28%
where the time goes in v12:
time: 67 us; the launch traced here: 66.7 us
  waiting for transfers between devices  28.3 us (42%)
  Pallas kernels  22.2 us (33%)
  starting transfers between devices  15.1 us (23%)
  between operations  0.97 us (1%)
    ppermute x9, waiting for transfers between devices, move(): return lax.ppermute(array, 'ctx', pairs)  24.9 us
    ppermute x9, starting transfers between devices, move(): return lax.ppermute(array, 'ctx', pairs)  13.5 us
    pallas_call x1, Pallas kernels, few_shards_body(): call(functools.partial(filters_kernel, rows, shards, blocks, width), 'fil...  6.52 us
    pallas_call x1, Pallas kernels, few_shards_body(): call(only(False, shards, 0, functools.partial(own_kernel, rows, shards, c...  6.08 us
    pallas_call x1, Pallas kernels, few_shards_body(): call(functools.partial(near_kernel, rows, shards, blocks, width), 'near_b...  3.8 us
    ppermute x2, waiting for transfers between devices, few_shards_body(): lax.ppermute(first, ('ch', 'sub'), [(i, i ^ bit) for i in range(group)])  3.41 us
    pallas_call x1, Pallas kernels, few_shards_body(): pl.pallas_call(products_kernel, grid=(rows // row_step,), in_specs=[smem]...  2.79 us
    pallas_call x1, Pallas kernels, few_shards_body(): call(looped(functools.partial(gates_kernel, shards), (None,) + (ROWS,) *...  2.08 us
  transfers between devices with their start and end apart: 11, of which 7 were waited for; matrix products, arithmetic and copies ran while one was open for 0% of the time, Pallas kernels for 28%

profile of v12, /device:TPU:0, one launch (start us, length us, event | category | flops | bytes accessed | tf_op | source)
XLA Modules:
  0.0 66.7 jit_solution(2294342398494010696)
XLA Ops:
  0.6 2.8 %products.1 = (bf16[128,2048]{1,0:T(8,128)(2,1)}, bf16[128,2048]{1,0:T(8,128)(2,1)}, bf16[128,2048]{1,0:T(8,128)(2,1)}, f32[1,2048]{1,0:T(1,128)}) custom-call(s32[1]{0:T(128)} %bitcast.rank_ref.refs_0_.refs_1_, bf16[128,2048]{1,0:T(8,128)(2,1)} %refs_1_.2, bf16[128,2048]{1,0:T(8,128)(2,1)} %refs_2_.3, bf16[128,2048]{1,0:T(8,128)(2,1)} %refs_3_.2, ...), custom_call_target="tpu_custom_call" | custom-call | tf_op jit(solution)/shard_map/products/pallas_call | solution.py:718
  3.4 0.0 copy-start.4
  3.4 0.0 copy-start.5
  3.4 0.0 copy-start.8
  3.5 0.0 copy-start.13
  3.5 0.0 copy-start.14
  3.5 3.1 %collective-permute-start = (bf16[128,2048]{1,0:T(8,128)(2,1)}, bf16[128,2048]{1,0:T(8,128)(2,1)S(1)}, u32[]{:S(2)}, u32[]{:S(2)}) collective-permute-start(bf16[128,2048]{1,0:T(8,128)(2,1)} %get-tuple-element.31.refs_3_.pair_ref), channel_id=1, source_target_pairs={{0,4},{12,8},{4,0},{8,12},{1,5},{13,9},{5,1},{9,13},{2,6},{14,10},... | collective-permute-start | bytes 1572872 | tf_op jit(solution)/shard_map/ppermute | solution.py:707
  6.6 0.7 %collective-permute-start.1 = (bf16[128,2048]{1,0:T(8,128)(2,1)}, bf16[128,2048]{1,0:T(8,128)(2,1)S(1)}, u32[]{:S(2)}, u32[]{:S(2)}) collective-permute-start(bf16[128,2048]{1,0:T(8,128)(2,1)} %get-tuple-element.32.refs_4_.other_ref), channel_id=1, source_target_pairs={{4,8},{8,4},{5,9},{9,5},{6,10},{10,6},{7,11},{11,7},{20,24},{24,20... | collective-permute-start | bytes 1572872 | tf_op jit(solution)/shard_map/ppermute | solution.py:707
  7.3 6.1 %own_pair.1 = bf16[64,2304]{1,0:T(8,128)(2,1)} custom-call(s32[1]{0:T(128)} %bitcast.rank_ref.refs_0_.refs_1_, f32[128,32]{1,0:T(8,128)} %constant.15.clone.refs_1_, f32[32,64]{1,0:T(8,128)} %first_ref.1, bf16[128,2048]{1,0:T(8,128)(2,1)} %get-tuple-element.31.refs_3_.pair_ref, bf16[128,2048]{1,0:T(8,128)(2,1)} %get-tuple-element.32.refs_4_.other_ref, ...), custom_call_target="tpu_custom_call" | custom-call | flops 2147483648 | bytes 262144 | tf_op jit(solution)/shard_map/own_pair/pallas_call | solution.py:735
  13.4 0.0 copy-done.4
  13.4 0.0 copy-done.5
  13.4 0.0 copy-done.8
  13.4 0.0 copy-done.13
  13.4 0.0 copy-done.14
  13.4 0.0 copy-start.15
  13.4 0.0 copy-start.16
  13.4 0.0 copy-start.6
  13.4 0.0 copy-start.7
  13.5 0.0 copy-start.11
  13.5 0.0 copy-start.12
  13.5 6.5 %filters.1 = (bf16[4,256,2048]{2,1,0:T(8,128)(2,1)S(1)}, bf16[128,512]{1,0:T(8,128)(2,1)S(1)}, f32[512,64]{1,0:T(8,128)S(1)}) custom-call(f32[512,32]{1,0:T(8,128)S(1)} %copy-done.14, f32[32,64]{1,0:T(8,128)S(1)} %copy-done.13, f32[64,2048]{1,0:T(8,128)S(1)} %copy-done.4, f32[1,2048]{1,0:T(1,128)S(1)} %bitcast.5, bf16[256,256]{1,0:T(8,128)(2,1)S(1)} %copy-done.5), custom_call_target="tpu_custom_call" | custom-call | flops 2147483648 | bytes 262144 | tf_op jit(solution)/shard_map/filters/pallas_call | solution.py:748
  20.0 0.0 copy-done.15
  20.0 1.3 %collective-permute-start.2 = (bf16[128,2048]{1,0:T(8,128)(2,1)S(1)}, bf16[128,2048]{1,0:T(8,128)(2,1)S(1)}, u32[]{:S(2)}, u32[]{:S(2)}) collective-permute-start(bf16[128,2048]{1,0:T(8,128)(2,1)S(1)} %copy-done.15), channel_id=1, source_target_pairs={{0,8},{12,4},{1,9},{13,5},{2,10},{14,6},{3,11},{15,7},{16,24},{28,... | collective-permute-start | bytes 1572872 | tf_op jit(solution)/shard_map/ppermute | solution.py:707
  21.3 0.0 collective-permute-done.pair_in_ref.refs_2_
  21.4 0.0 copy-done.16
  21.4 1.3 %collective-permute-start.4 = (bf16[64,2304]{1,0:T(8,128)(2,1)S(1)}, bf16[64,2304]{1,0:T(8,128)(2,1)S(1)}, u32[]{:S(2)}, u32[]{:S(2)}) collective-permute-start(bf16[64,2304]{1,0:T(8,128)(2,1)S(1)} %copy-done.16), channel_id=1, source_target_pairs={{0,4},{12,8},{1,5},{13,9},{2,6},{14,10},{3,7},{15,11},{16,20},{28,... | collective-permute-start | bytes 884744 | tf_op jit(solution)/shard_map/ppermute | solution.py:707
  22.7 0.0 collective-permute-done.1.middle_in_ref
  22.7 0.0 copy-done.6
  22.7 0.0 copy-done.7
  22.7 0.0 copy-done.11
  22.7 0.0 copy-done.12
  22.7 3.8 %near_blocks.1 = (f32[128,2048]{1,0:T(8,128)S(1)}, f32[128,2048]{1,0:T(8,128)S(1)}, f32[128,2048]{1,0:T(8,128)S(1)}, f32[64,2048]{1,0:T(8,128)S(1)}, f32[32,64]{1,0:T(8,128)S(1)}) custom-call(s32[1]{0:T(128)} %bitcast.rank_ref.refs_0_.refs_1_, bf16[128,2048]{1,0:T(8,128)(2,1)S(1)} %copy-done.11, bf16[128,2048]{1,0:T(8,128)(2,1)S(1)} %copy-done.12, ...), custom_call_target="tpu_custom_call" | custom-call | flops 5368709120 | bytes 262144 | tf_op jit(solution)/shard_map/near_blocks/pallas_call | solution.py:763
  26.5 0.0 copy-start.10
  26.5 7.1 %collective-permute-done.2.refs_1_.refs_3_ = bf16[128,2048]{1,0:T(8,128)(2,1)S(1)} collective-permute-done((bf16[128,2048]{1,0:T(8,128)(2,1)S(1)}, bf16[128,2048]{1,0:T(8,128)(2,1)S(1)}, u32[]{:S(2)}, u32[]{:S(2)}) %collective-permute-start.2) | collective-permute-done | bytes 524320 | tf_op jit(solution)/shard_map/ppermute | solution.py:707
  33.6 0.0 copy-start
  33.6 0.0 copy-start.1
  33.6 0.0 copy-start.2
  33.6 0.0 copy-start.3
  33.6 0.0 copy-start.9
  33.7 1.4 %collective-permute-start.3 = (bf16[128,2048]{1,0:T(8,128)(2,1)S(1)}, bf16[128,2048]{1,0:T(8,128)(2,1)S(1)}, u32[]{:S(2)}, u32[]{:S(2)}) collective-permute-start(bf16[128,2048]{1,0:T(8,128)(2,1)S(1)} %get-tuple-element.44), channel_id=1, source_target_pairs={{4,0},{8,12},{5,1},{9,13},{6,2},{10,14},{7,3},{11,15},{20,16},{24,... | collective-permute-start | bytes 1572872 | tf_op jit(solution)/shard_map/ppermute | solution.py:707
  35.1 3.7 %collective-permute-done.4.refs_14_ = bf16[64,2304]{1,0:T(8,128)(2,1)S(1)} collective-permute-done((bf16[64,2304]{1,0:T(8,128)(2,1)S(1)}, bf16[64,2304]{1,0:T(8,128)(2,1)S(1)}, u32[]{:S(2)}, u32[]{:S(2)}) %collective-permute-start.4) | collective-permute-done | bytes 294944 | tf_op jit(solution)/shard_map/ppermute | solution.py:707
  38.8 0.0 copy-done.10
  38.8 0.7 %collective-permute-start.7 = (bf16[64,2304]{1,0:T(8,128)(2,1)S(1)}, bf16[64,2304]{1,0:T(8,128)(2,1)S(1)}, u32[]{:S(2)}, u32[]{:S(2)}) collective-permute-start(bf16[64,2304]{1,0:T(8,128)(2,1)S(1)} %get-tuple-element.52.own_ref), channel_id=1, source_target_pairs={{4,8},{8,4},{0,0},{12,12},{5,9},{9,5},{1,1},{13,13},{6,10},{10,6},... | collective-permute-start | bytes 884744 | tf_op jit(solution)/shard_map/ppermute | solution.py:707
  39.5 0.1 collective-permute-start.5
  39.5 1.2 %collective-permute-done.5 = f32[32,64]{1,0:T(8,128)S(1)} collective-permute-done((f32[32,64]{1,0:T(8,128)S(1)}, f32[32,64]{1,0:T(8,128)S(1)}, u32[]{:S(2)}, u32[]{:S(2)}) %collective-permute-start.5) | collective-permute-done | bytes 8224 | tf_op jit(solution)/shard_map/ppermute | solution.py:809
  40.7 1.5 %collective-permute-start.6 = (f32[32,64]{1,0:T(8,128)S(1)}, f32[32,64]{1,0:T(8,128)S(1)}, u32[]{:S(2)}, u32[]{:S(2)}) collective-permute-start(f32[32,64]{1,0:T(8,128)S(1)} %add.9), channel_id=1, source_target_pairs={{0,2},{1,3},{2,0},{3,1},{4,6},{5,7},{6,4},{7,5},{8,10},{9,11},{10,... | collective-permute-start | bytes 24584 | tf_op jit(solution)/shard_map/ppermute | solution.py:809
  42.2 2.2 %collective-permute-done.6 = f32[32,64]{1,0:T(8,128)S(1)} collective-permute-done((f32[32,64]{1,0:T(8,128)S(1)}, f32[32,64]{1,0:T(8,128)S(1)}, u32[]{:S(2)}, u32[]{:S(2)}) %collective-permute-start.6) | collective-permute-done | bytes 8224 | tf_op jit(solution)/shard_map/ppermute | solution.py:809
  44.5 6.9 %collective-permute-done.3.refs_9_.part_ref = bf16[128,2048]{1,0:T(8,128)(2,1)S(1)} collective-permute-done((bf16[128,2048]{1,0:T(8,128)(2,1)S(1)}, bf16[128,2048]{1,0:T(8,128)(2,1)S(1)}, u32[]{:S(2)}, u32[]{:S(2)}) %collective-permute-start.3) | collective-permute-done | bytes 524320 | tf_op jit(solution)/shard_map/ppermute | solution.py:707
  51.4 0.0 collective-permute-done.7.come_ref
  51.4 0.1 total.1.own_ref
  51.5 2.4 %collective-permute-start.8 = (bf16[64,2304]{1,0:T(8,128)(2,1)S(1)}, bf16[64,2304]{1,0:T(8,128)(2,1)S(1)}, u32[]{:S(2)}, u32[]{:S(2)}) collective-permute-start(bf16[64,2304]{1,0:T(8,128)(2,1)S(1)} %total.1.own_ref), channel_id=1, source_target_pairs={{0,4},{12,8},{4,0},{8,12},{1,5},{13,9},{5,1},{9,13},{2,6},{14,10},... | collective-permute-start | bytes 884744 | tf_op jit(solution)/shard_map/ppermute | solution.py:707
  53.9 2.6 %collective-permute-start.9 = (f32[32,64]{1,0:T(8,128)S(1)}, f32[32,64]{1,0:T(8,128)S(1)}, u32[]{:S(2)}, u32[]{:S(2)}) collective-permute-start(f32[32,64]{1,0:T(8,128)S(1)} %add.10.first_ref), channel_id=1, source_target_pairs={{0,12},{4,8},{8,4},{12,0},{1,13},{5,9},{9,5},{13,1},{2,14},{6,10},... | collective-permute-start | bytes 24584 | tf_op jit(solution)/shard_map/ppermute | solution.py:707
  56.5 5.6 %collective-permute-done.9 = f32[32,64]{1,0:T(8,128)S(1)} collective-permute-done((f32[32,64]{1,0:T(8,128)S(1)}, f32[32,64]{1,0:T(8,128)S(1)}, u32[]{:S(2)}, u32[]{:S(2)}) %collective-permute-start.9) | collective-permute-done | bytes 8224 | tf_op jit(solution)/shard_map/ppermute | solution.py:707
  62.1 0.0 collective-permute-start.10
  62.1 0.0 copy-done
  62.1 0.0 copy-done.1
  62.1 0.0 copy-done.2
  62.2 0.0 copy-done.3
  62.2 0.0 copy-done.9
  62.2 2.1 %gates.1 = (bf16[128,2048]{1,0:T(8,128)(2,1)}, bf16[128,2048]{1,0:T(8,128)(2,1)}, bf16[128,2048]{1,0:T(8,128)(2,1)}) custom-call(s32[1]{0:T(128)} %bitcast.rank_ref.refs_0_.refs_1_, bf16[128,2048]{1,0:T(8,128)(2,1)S(1)} %copy-done, bf16[128,2048]{1,0:T(8,128)(2,1)S(1)} %copy-done.1, bf16[128,2048]{1,0:T(8,128)(2,1)S(1)} %copy-done.2, ...), custom_call_target="tpu_custom_call" | custom-call | bytes 262144 | tf_op jit(solution)/shard_map/gates/pallas_call | solution.py:821
  64.3 1.6 %collective-permute-done.10.first_come_ref = f32[32,64]{1,0:T(8,128)S(1)} collective-permute-done((f32[32,64]{1,0:T(8,128)S(1)}, f32[32,64]{1,0:T(8,128)S(1)}, u32[]{:S(2)}, u32[]{:S(2)}) %collective-permute-start.10) | collective-permute-done | bytes 8224 | tf_op jit(solution)/shard_map/ppermute | solution.py:707
  65.9 0.0 collective-permute-done.8.come_ref
  65.9 0.9 %finish.1 = (f32[64,2048]{1,0:T(8,128)}, f32[32,64]{1,0:T(8,128)}, f32[1,2048]{1,0:T(1,128)}) custom-call(s32[1]{0:T(128)} %bitcast.rank_ref.refs_0_.refs_1_, bf16[64,2304]{1,0:T(8,128)(2,1)S(1)} %total.1.own_ref, bf16[64,2304]{1,0:T(8,128)(2,1)S(1)} %collective-permute-done.8.come_ref, f32[32,64]{1,0:T(8,128)S(1)} %add.11.first_ref, ...), custom_call_target="tpu_custom_call" | custom-call | bytes 262144 | tf_op jit(solution)/shard_map/finish/pallas_call | solution.py:831
  (5 shorter events, 0.0 us)
Async XLA Ops:
  3.4 9.9 %copy-start.4 = (f32[64,2048]{1,0:T(8,128)S(1)}, f32[64,2048]{1,0:T(8,128)}, u32[]{:S(2)}) copy-start(f32[64,2048]{1,0:T(8,128)} %refs_4_.4) | copy-start | bytes 1572868
  3.4 9.9 %copy-start.5 = (bf16[256,256]{1,0:T(8,128)(2,1)S(1)}, bf16[256,256]{1,0:T(8,128)(2,1)}, u32[]{:S(2)}) copy-start(bf16[256,256]{1,0:T(8,128)(2,1)} %constant.16.clone.refs_7_.front_ref.refs_3_.refs_6_) | copy-start | bytes 393220
  3.4 9.9 %copy-start.8 = (f32[2048]{0:T(1024)S(1)}, f32[2048]{0:T(1024)}, u32[]{:S(2)}) copy-start(f32[2048]{0:T(1024)} %param.20) | copy-start | bytes 24580
  3.5 9.9 %copy-start.13 = (f32[32,64]{1,0:T(8,128)S(1)}, f32[32,64]{1,0:T(8,128)}, u32[]{:S(2)}) copy-start(f32[32,64]{1,0:T(8,128)} %first_ref.1) | copy-start | bytes 24580
  3.5 9.9 %copy-start.14 = (f32[512,32]{1,0:T(8,128)S(1)}, f32[512,32]{1,0:T(8,128)}, u32[]{:S(2)}) copy-start(f32[512,32]{1,0:T(8,128)} %constant.19.clone.feats_ref) | copy-start | bytes 196612
  3.5 17.9 %collective-permute-start = (bf16[128,2048]{1,0:T(8,128)(2,1)}, bf16[128,2048]{1,0:T(8,128)(2,1)S(1)}, u32[]{:S(2)}, u32[]{:S(2)}) collective-permute-start(bf16[128,2048]{1,0:T(8,128)(2,1)} %get-tuple-element.31.refs_3_.pair_ref), channel_id=1, source_target_pairs={{0,4},{12,8},{4,0},{8,12},{1,5},{13,9},{5,1},{9,13},{2,6},{14,10},... | collective-permute-start | bytes 1572872 | tf_op jit(solution)/shard_map/ppermute | solution.py:707
  6.6 16.1 %collective-permute-start.1 = (bf16[128,2048]{1,0:T(8,128)(2,1)}, bf16[128,2048]{1,0:T(8,128)(2,1)S(1)}, u32[]{:S(2)}, u32[]{:S(2)}) collective-permute-start(bf16[128,2048]{1,0:T(8,128)(2,1)} %get-tuple-element.32.refs_4_.other_ref), channel_id=1, source_target_pairs={{4,8},{8,4},{5,9},{9,5},{6,10},{10,6},{7,11},{11,7},{20,24},{24,20... | collective-permute-start | bytes 1572872 | tf_op jit(solution)/shard_map/ppermute | solution.py:707
  13.4 6.6 %copy-start.15 = (bf16[128,2048]{1,0:T(8,128)(2,1)S(1)}, bf16[128,2048]{1,0:T(8,128)(2,1)}, u32[]{:S(2)}) copy-start(bf16[128,2048]{1,0:T(8,128)(2,1)} %get-tuple-element.41) | copy-start | bytes 1572868
  13.4 7.9 %copy-start.16 = (bf16[64,2304]{1,0:T(8,128)(2,1)S(1)}, bf16[64,2304]{1,0:T(8,128)(2,1)}, u32[]{:S(2)}) copy-start(bf16[64,2304]{1,0:T(8,128)(2,1)} %own_pair.1) | copy-start | bytes 884740
  13.4 9.3 %copy-start.6 = (bf16[256,256]{1,0:T(8,128)(2,1)S(1)}, bf16[256,256]{1,0:T(8,128)(2,1)}, u32[]{:S(2)}) copy-start(bf16[256,256]{1,0:T(8,128)(2,1)} %constant.17.clone.refs_8_.back_ref.refs_4_.refs_7_) | copy-start | bytes 393220
  13.4 9.3 %copy-start.7 = (f32[32,512]{1,0:T(8,128)S(1)}, f32[32,512]{1,0:T(8,128)}, u32[]{:S(2)}) copy-start(f32[32,512]{1,0:T(8,128)} %constant.18.clone.refs_9_.featt_ref) | copy-start | bytes 196612
  13.5 9.3 %copy-start.11 = (bf16[128,2048]{1,0:T(8,128)(2,1)S(1)}, bf16[128,2048]{1,0:T(8,128)(2,1)}, u32[]{:S(2)}) copy-start(bf16[128,2048]{1,0:T(8,128)(2,1)} %get-tuple-element.31.refs_3_.pair_ref) | copy-start | bytes 1572868
  13.5 9.3 %copy-start.12 = (bf16[128,2048]{1,0:T(8,128)(2,1)S(1)}, bf16[128,2048]{1,0:T(8,128)(2,1)}, u32[]{:S(2)}) copy-start(bf16[128,2048]{1,0:T(8,128)(2,1)} %get-tuple-element.32.refs_4_.other_ref) | copy-start | bytes 1572868
  20.0 13.6 %collective-permute-start.2 = (bf16[128,2048]{1,0:T(8,128)(2,1)S(1)}, bf16[128,2048]{1,0:T(8,128)(2,1)S(1)}, u32[]{:S(2)}, u32[]{:S(2)}) collective-permute-start(bf16[128,2048]{1,0:T(8,128)(2,1)S(1)} %copy-done.15), channel_id=1, source_target_pairs={{0,8},{12,4},{1,9},{13,5},{2,10},{14,6},{3,11},{15,7},{16,24},{28,... | collective-permute-start | bytes 1572872 | tf_op jit(solution)/shard_map/ppermute | solution.py:707
  21.4 17.4 %collective-permute-start.4 = (bf16[64,2304]{1,0:T(8,128)(2,1)S(1)}, bf16[64,2304]{1,0:T(8,128)(2,1)S(1)}, u32[]{:S(2)}, u32[]{:S(2)}) collective-permute-start(bf16[64,2304]{1,0:T(8,128)(2,1)S(1)} %copy-done.16), channel_id=1, source_target_pairs={{0,4},{12,8},{1,5},{13,9},{2,6},{14,10},{3,7},{15,11},{16,20},{28,... | collective-permute-start | bytes 884744 | tf_op jit(solution)/shard_map/ppermute | solution.py:707
  26.5 12.2 %copy-start.10 = (f32[1,2048]{1,0:T(1,128)S(1)}, f32[1,2048]{1,0:T(1,128)}, u32[]{:S(2)}) copy-start(f32[1,2048]{1,0:T(1,128)} %get-tuple-element.33.refs_10_.refs_13_) | copy-start | bytes 24580
  33.6 28.5 %copy-start = (bf16[128,2048]{1,0:T(8,128)(2,1)S(1)}, bf16[128,2048]{1,0:T(8,128)(2,1)}, u32[]{:S(2)}) copy-start(bf16[128,2048]{1,0:T(8,128)(2,1)} %refs_1_.2) | copy-start | bytes 1572868
  33.6 28.5 %copy-start.1 = (bf16[128,2048]{1,0:T(8,128)(2,1)S(1)}, bf16[128,2048]{1,0:T(8,128)(2,1)}, u32[]{:S(2)}) copy-start(bf16[128,2048]{1,0:T(8,128)(2,1)} %refs_2_.3) | copy-start | bytes 1572868
  33.6 28.5 %copy-start.2 = (bf16[128,2048]{1,0:T(8,128)(2,1)S(1)}, bf16[128,2048]{1,0:T(8,128)(2,1)}, u32[]{:S(2)}) copy-start(bf16[128,2048]{1,0:T(8,128)(2,1)} %refs_3_.2) | copy-start | bytes 1572868
  33.6 28.5 %copy-start.3 = (bf16[128,2048]{1,0:T(8,128)(2,1)S(1)}, bf16[128,2048]{1,0:T(8,128)(2,1)}, u32[]{:S(2)}) copy-start(bf16[128,2048]{1,0:T(8,128)(2,1)} %refs_4_.3) | copy-start | bytes 1572868
  33.6 28.5 %copy-start.9 = (f32[2048]{0:T(1024)S(1)}, f32[2048]{0:T(1024)}, u32[]{:S(2)}) copy-start(f32[2048]{0:T(1024)} %param.19) | copy-start | bytes 24580
  33.7 17.7 %collective-permute-start.3 = (bf16[128,2048]{1,0:T(8,128)(2,1)S(1)}, bf16[128,2048]{1,0:T(8,128)(2,1)S(1)}, u32[]{:S(2)}, u32[]{:S(2)}) collective-permute-start(bf16[128,2048]{1,0:T(8,128)(2,1)S(1)} %get-tuple-element.44), channel_id=1, source_target_pairs={{4,0},{8,12},{5,1},{9,13},{6,2},{10,14},{7,3},{11,15},{20,16},{24,... | collective-permute-start | bytes 1572872 | tf_op jit(solution)/shard_map/ppermute | solution.py:707
  38.8 12.6 %collective-permute-start.7 = (bf16[64,2304]{1,0:T(8,128)(2,1)S(1)}, bf16[64,2304]{1,0:T(8,128)(2,1)S(1)}, u32[]{:S(2)}, u32[]{:S(2)}) collective-permute-start(bf16[64,2304]{1,0:T(8,128)(2,1)S(1)} %get-tuple-element.52.own_ref), channel_id=1, source_target_pairs={{4,8},{8,4},{0,0},{12,12},{5,9},{9,5},{1,1},{13,13},{6,10},{10,6},... | collective-permute-start | bytes 884744 | tf_op jit(solution)/shard_map/ppermute | solution.py:707
  39.5 1.2 %collective-permute-start.5 = (f32[32,64]{1,0:T(8,128)S(1)}, f32[32,64]{1,0:T(8,128)S(1)}, u32[]{:S(2)}, u32[]{:S(2)}) collective-permute-start(f32[32,64]{1,0:T(8,128)S(1)} %get-tuple-element.51), channel_id=1, source_target_pairs={{0,1},{1,0},{2,3},{3,2},{4,5},{5,4},{6,7},{7,6},{8,9},{9,8},{10,11... | collective-permute-start | bytes 24584 | tf_op jit(solution)/shard_map/ppermute | solution.py:809
  40.7 3.7 %collective-permute-start.6 = (f32[32,64]{1,0:T(8,128)S(1)}, f32[32,64]{1,0:T(8,128)S(1)}, u32[]{:S(2)}, u32[]{:S(2)}) collective-permute-start(f32[32,64]{1,0:T(8,128)S(1)} %add.9), channel_id=1, source_target_pairs={{0,2},{1,3},{2,0},{3,1},{4,6},{5,7},{6,4},{7,5},{8,10},{9,11},{10,... | collective-permute-start | bytes 24584 | tf_op jit(solution)/shard_map/ppermute | solution.py:809
  51.5 14.4 %collective-permute-start.8 = (bf16[64,2304]{1,0:T(8,128)(2,1)S(1)}, bf16[64,2304]{1,0:T(8,128)(2,1)S(1)}, u32[]{:S(2)}, u32[]{:S(2)}) collective-permute-start(bf16[64,2304]{1,0:T(8,128)(2,1)S(1)} %total.1.own_ref), channel_id=1, source_target_pairs={{0,4},{12,8},{4,0},{8,12},{1,5},{13,9},{5,1},{9,13},{2,6},{14,10},... | collective-permute-start | bytes 884744 | tf_op jit(solution)/shard_map/ppermute | solution.py:707
  53.9 8.2 %collective-permute-start.9 = (f32[32,64]{1,0:T(8,128)S(1)}, f32[32,64]{1,0:T(8,128)S(1)}, u32[]{:S(2)}, u32[]{:S(2)}) collective-permute-start(f32[32,64]{1,0:T(8,128)S(1)} %add.10.first_ref), channel_id=1, source_target_pairs={{0,12},{4,8},{8,4},{12,0},{1,13},{5,9},{9,5},{13,1},{2,14},{6,10},... | collective-permute-start | bytes 24584 | tf_op jit(solution)/shard_map/ppermute | solution.py:707
  62.1 3.7 %collective-permute-start.10 = (f32[32,64]{1,0:T(8,128)S(1)}, f32[32,64]{1,0:T(8,128)S(1)}, u32[]{:S(2)}, u32[]{:S(2)}) collective-permute-start(f32[32,64]{1,0:T(8,128)S(1)} %add.11.first_ref), channel_id=1, source_target_pairs={{0,4},{12,8},{4,0},{8,12},{1,5},{13,9},{5,1},{9,13},{2,6},{14,10},... | collective-permute-start | bytes 24584 | tf_op jit(solution)/shard_map/ppermute | solution.py:707

commit v13 on v12

--- a/solution.py
+++ b/solution.py
@@ -171,7 +171,7 @@
 
 
 STEP = 16
-SIDE = 256
+SIDE = 128
 
 
 def halves(array):
@@ -421,17 +421,17 @@
 def put_side(pay_ref, channels, bias, first=None):
     half = pay_ref.shape[0] // 2
     pay_ref[:, channels:] = jnp.zeros((2 * half, SIDE), bf16)
-    for start, part in zip((0, 128), split(bias)):
-        pay_ref[: bias.shape[0], channels + start : channels + start + 128] = part
+    for start, part in zip((0, half // 2), split(bias)):
+        pay_ref[start : start + bias.shape[0], channels:] = part
     if first is not None:
-        for start, part in zip((0, 128), split(first)):
-            pay_ref[half:, channels + start : channels + start + first.shape[1]] = part
+        pay_ref[half:, channels:] = jnp.concatenate(split(first), axis=1)
 
 
 def get_side(pay, channels, lanes, hid_count):
     half = pay.shape[0] // 2
-    side = pay[:, channels : channels + 128].astype(f32) + pay[:, channels + 128 :].astype(f32)
-    return side[:lanes], side[half:, :hid_count]
+    side = pay[:, channels:].astype(f32)
+    low = side[half:]
+    return side[:lanes] + side[half // 2 : half // 2 + lanes], low[:, :hid_count] + low[:, hid_count:]
 
 
 def near_kernel(
@@ -709,6 +709,7 @@
     inward = [(0, 1), (shards - 1, shards - 2)]
     outward = [(1, 0), (shards - 2, shards - 1)]
     across = [(1, 2), (2, 1)]
+    alone = [(0, 0), (shards - 1, shards - 1)]
     pay_shape = (hid_count, channels + SIDE)
     block_bf16 = shape(rows, channels, dtype=bf16)
     block_f32 = shape(rows, channels)
@@ -744,6 +745,7 @@
         ],
         limit=60,
     )(rank, feats[:rows], first_weight, pair, other, second_weight, rate_row, front, back, featt, bias)
+    come = move(send, inward)
     late_feats, _ = lax.optimization_barrier((jnp.asarray(feats), send))
     spec, trans, slope = call(
         functools.partial(filters_kernel, rows, shards, blocks, width), "filters", 8,
@@ -757,9 +759,6 @@
 
     edge, _ = lax.optimization_barrier((edge, slope))
     far = move(edge, [(0, 2), (shards - 1, shards - 3)])
-    send, _ = lax.optimization_barrier((send, pair_in))
-    come = move(send, inward)
-
     conv, corr, ahead, sums, first = call(
         functools.partial(near_kernel, rows, shards, blocks, width), "near_blocks", 20,
         [block_f32] * 3 + [shape(hid_count, channels), shape(feat_count, hid_count)],
@@ -802,7 +801,7 @@
         [anywhere, smem] + [vmem] * 13,
         scratch=[pltpu.VMEM((2 * rows, hid_count), f32)],
     )(late, rank, pair_in, far, second_weight, rate_row, front, back, trans, featt, slope, sums, first, bias, come)
-    pay_come = move(pay, across + [(0, 0), (shards - 1, shards - 1)])
+    pay_come = move(pay, across + alone)
     group = lax.axis_size(("ch", "sub"))
     bit = 1
     while bit < group:
@@ -815,7 +814,7 @@
         [anywhere] * 2 + [vmem] * 2,
     )(part_come, first, pay, pay_come)
     total_come = move(total, inward + outward)
-    first = first + move(first, [(i, shards - 1 - i) for i in range(shards)])
+    first = first + move(first, across + alone)
     first_come = move(first, inward + outward)
 
     grad_one, grad_two, grad_value = call(

time: 67 us -> 62.4 us (0.931)
  waiting for transfers between devices: 28.3 us -> 21.1 us
  starting transfers between devices: 15.1 us -> 17.7 us
    ppermute x9, waiting for transfers between devices: 24.9 us -> 17.7 us  [move(): return lax.ppermute(array, 'ctx', pairs)]
    ppermute x9, starting transfers between devices: 13.5 us -> 16.2 us  [move(): return lax.ppermute(array, 'ctx', pairs)]
  transfers between devices with their start and end apart: 11 -> 11, of which waited for: 7 -> 5; matrix products, arithmetic and copies ran while one was open for 0% -> 0% of each run, Pallas kernels for 28% -> 30%
where the time goes in v13:
time: 62.4 us; the launch traced here: 62.2 us
  Pallas kernels  22.2 us (36%)
  waiting for transfers between devices  21.1 us (34%)
  starting transfers between devices  17.7 us (28%)
  between operations  0.96 us (2%)
    ppermute x9, waiting for transfers between devices, move(): return lax.ppermute(array, 'ctx', pairs)  17.7 us
    ppermute x9, starting transfers between devices, move(): return lax.ppermute(array, 'ctx', pairs)  16.2 us
    pallas_call x1, Pallas kernels, few_shards_body(): call(functools.partial(filters_kernel, rows, shards, blocks, width), 'fil...  6.5 us
    pallas_call x1, Pallas kernels, few_shards_body(): call(only(False, shards, 0, functools.partial(own_kernel, rows, shards, c...  6.15 us
    pallas_call x1, Pallas kernels, few_shards_body(): call(functools.partial(near_kernel, rows, shards, blocks, width), 'near_b...  3.8 us
    ppermute x2, waiting for transfers between devices, few_shards_body(): lax.ppermute(first, ('ch', 'sub'), [(i, i ^ bit) for i in range(group)])  3.41 us
    pallas_call x1, Pallas kernels, few_shards_body(): pl.pallas_call(products_kernel, grid=(rows // row_step,), in_specs=[smem]...  2.79 us
    pallas_call x1, Pallas kernels, few_shards_body(): call(looped(functools.partial(gates_kernel, shards), (None,) + (ROWS,) *...  2.08 us
  transfers between devices with their start and end apart: 11, of which 5 were waited for; matrix products, arithmetic and copies ran while one was open for 0% of the time, Pallas kernels for 30%

profile of v13, /device:TPU:0, one launch (start us, length us, event | category | flops | bytes accessed | tf_op | source)
XLA Modules:
  0.0 62.2 jit_solution(11101351261743564944)
XLA Ops:
  0.6 2.8 %products.1 = (bf16[128,2048]{1,0:T(8,128)(2,1)}, bf16[128,2048]{1,0:T(8,128)(2,1)}, bf16[128,2048]{1,0:T(8,128)(2,1)}, f32[1,2048]{1,0:T(1,128)}) custom-call(s32[1]{0:T(128)} %bitcast.rank_ref.refs_0_.refs_1_, bf16[128,2048]{1,0:T(8,128)(2,1)} %refs_1_.2, bf16[128,2048]{1,0:T(8,128)(2,1)} %refs_2_.3, bf16[128,2048]{1,0:T(8,128)(2,1)} %refs_3_.2, ...), custom_call_target="tpu_custom_call" | custom-call | tf_op jit(solution)/shard_map/products/pallas_call | solution.py:719
  3.4 0.0 copy-start.4
  3.4 0.0 copy-start.5
  3.4 0.0 copy-start.8
  3.5 0.0 copy-start.13
  3.5 0.0 copy-start.14
  3.5 3.1 %collective-permute-start = (bf16[128,2048]{1,0:T(8,128)(2,1)}, bf16[128,2048]{1,0:T(8,128)(2,1)S(1)}, u32[]{:S(2)}, u32[]{:S(2)}) collective-permute-start(bf16[128,2048]{1,0:T(8,128)(2,1)} %get-tuple-element.30.refs_3_.pair_ref), channel_id=1, source_target_pairs={{0,4},{12,8},{4,0},{8,12},{1,5},{13,9},{5,1},{9,13},{2,6},{14,10},... | collective-permute-start | bytes 1572872 | tf_op jit(solution)/shard_map/ppermute | solution.py:707
  6.6 0.7 %collective-permute-start.1 = (bf16[128,2048]{1,0:T(8,128)(2,1)}, bf16[128,2048]{1,0:T(8,128)(2,1)S(1)}, u32[]{:S(2)}, u32[]{:S(2)}) collective-permute-start(bf16[128,2048]{1,0:T(8,128)(2,1)} %get-tuple-element.31.refs_4_.other_ref), channel_id=1, source_target_pairs={{4,8},{8,4},{5,9},{9,5},{6,10},{10,6},{7,11},{11,7},{20,24},{24,20... | collective-permute-start | bytes 1572872 | tf_op jit(solution)/shard_map/ppermute | solution.py:707
  7.3 6.1 %own_pair.1 = bf16[64,2176]{1,0:T(8,128)(2,1)} custom-call(s32[1]{0:T(128)} %bitcast.rank_ref.refs_0_.refs_1_, f32[128,32]{1,0:T(8,128)} %constant.15.clone.refs_1_, f32[32,64]{1,0:T(8,128)} %first_ref.1, bf16[128,2048]{1,0:T(8,128)(2,1)} %get-tuple-element.30.refs_3_.pair_ref, bf16[128,2048]{1,0:T(8,128)(2,1)} %get-tuple-element.31.refs_4_.other_ref, ...), custom_call_target="tpu_custom_call" | custom-call | flops 2147483648 | bytes 262144 | tf_op jit(solution)/shard_map/own_pair/pallas_call | solution.py:736
  13.4 0.0 copy-done.4
  13.4 0.0 copy-done.5
  13.4 0.0 copy-done.8
  13.4 0.0 copy-done.13
  13.5 0.0 copy-done.14
  13.5 0.0 copy-start.15
  13.5 0.0 copy-start.16
  13.5 0.0 copy-start.6
  13.5 0.0 copy-start.7
  13.5 0.0 copy-start.11
  13.5 0.0 copy-start.12
  13.5 6.5 %filters.1 = (bf16[4,256,2048]{2,1,0:T(8,128)(2,1)S(1)}, bf16[128,512]{1,0:T(8,128)(2,1)S(1)}, f32[512,64]{1,0:T(8,128)S(1)}) custom-call(f32[512,32]{1,0:T(8,128)S(1)} %copy-done.14, f32[32,64]{1,0:T(8,128)S(1)} %copy-done.13, f32[64,2048]{1,0:T(8,128)S(1)} %copy-done.4, f32[1,2048]{1,0:T(1,128)S(1)} %bitcast.5, bf16[256,256]{1,0:T(8,128)(2,1)S(1)} %copy-done.5), custom_call_target="tpu_custom_call" | custom-call | flops 2147483648 | bytes 262144 | tf_op jit(solution)/shard_map/filters/pallas_call | solution.py:750
  20.0 0.0 copy-done.15
  20.1 1.3 %collective-permute-start.2 = (bf16[128,2048]{1,0:T(8,128)(2,1)S(1)}, bf16[128,2048]{1,0:T(8,128)(2,1)S(1)}, u32[]{:S(2)}, u32[]{:S(2)}) collective-permute-start(bf16[128,2048]{1,0:T(8,128)(2,1)S(1)} %copy-done.15), channel_id=1, source_target_pairs={{0,8},{12,4},{1,9},{13,5},{2,10},{14,6},{3,11},{15,7},{16,24},{28,... | collective-permute-start | bytes 1572872 | tf_op jit(solution)/shard_map/ppermute | solution.py:707
  21.4 0.0 copy-done.16
  21.4 1.3 %collective-permute-start.4 = (bf16[64,2176]{1,0:T(8,128)(2,1)S(1)}, bf16[64,2176]{1,0:T(8,128)(2,1)S(1)}, u32[]{:S(2)}, u32[]{:S(2)}) collective-permute-start(bf16[64,2176]{1,0:T(8,128)(2,1)S(1)} %copy-done.16), channel_id=1, source_target_pairs={{0,4},{12,8},{1,5},{13,9},{2,6},{14,10},{3,7},{15,11},{16,20},{28,... | collective-permute-start | bytes 835592 | tf_op jit(solution)/shard_map/ppermute | solution.py:707
  22.7 0.0 collective-permute-done.pair_in_ref.refs_2_
  22.7 0.0 collective-permute-done.1.middle_in_ref
  22.7 0.0 copy-done.6
  22.7 0.0 copy-done.7
  22.8 0.0 copy-done.11
  22.8 0.0 copy-done.12
  22.8 3.8 %near_blocks.1 = (f32[128,2048]{1,0:T(8,128)S(1)}, f32[128,2048]{1,0:T(8,128)S(1)}, f32[128,2048]{1,0:T(8,128)S(1)}, f32[64,2048]{1,0:T(8,128)S(1)}, f32[32,64]{1,0:T(8,128)S(1)}) custom-call(s32[1]{0:T(128)} %bitcast.rank_ref.refs_0_.refs_1_, bf16[128,2048]{1,0:T(8,128)(2,1)S(1)} %copy-done.11, bf16[128,2048]{1,0:T(8,128)(2,1)S(1)} %copy-done.12, ...), custom_call_target="tpu_custom_call" | custom-call | flops 5368709120 | bytes 262144 | tf_op jit(solution)/shard_map/near_blocks/pallas_call | solution.py:762
  26.6 0.0 copy-start.10
  26.6 7.1 %collective-permute-done.2.refs_1_.refs_3_ = bf16[128,2048]{1,0:T(8,128)(2,1)S(1)} collective-permute-done((bf16[128,2048]{1,0:T(8,128)(2,1)S(1)}, bf16[128,2048]{1,0:T(8,128)(2,1)S(1)}, u32[]{:S(2)}, u32[]{:S(2)}) %collective-permute-start.2) | collective-permute-done | bytes 524320 | tf_op jit(solution)/shard_map/ppermute | solution.py:707
  33.7 0.0 copy-start
  33.7 0.0 copy-start.1
  33.7 0.0 copy-start.2
  33.7 0.0 copy-start.3
  33.7 0.0 copy-start.9
  33.7 1.4 %collective-permute-start.3 = (bf16[128,2048]{1,0:T(8,128)(2,1)S(1)}, bf16[128,2048]{1,0:T(8,128)(2,1)S(1)}, u32[]{:S(2)}, u32[]{:S(2)}) collective-permute-start(bf16[128,2048]{1,0:T(8,128)(2,1)S(1)} %get-tuple-element.43), channel_id=1, source_target_pairs={{4,0},{8,12},{5,1},{9,13},{6,2},{10,14},{7,3},{11,15},{20,16},{24,... | collective-permute-start | bytes 1572872 | tf_op jit(solution)/shard_map/ppermute | solution.py:707
  35.1 3.4 %collective-permute-done.4.refs_14_ = bf16[64,2176]{1,0:T(8,128)(2,1)S(1)} collective-permute-done((bf16[64,2176]{1,0:T(8,128)(2,1)S(1)}, bf16[64,2176]{1,0:T(8,128)(2,1)S(1)}, u32[]{:S(2)}, u32[]{:S(2)}) %collective-permute-start.4) | collective-permute-done | bytes 278560 | tf_op jit(solution)/shard_map/ppermute | solution.py:707
  38.5 0.0 copy-done.10
  38.5 0.7 %collective-permute-start.7 = (bf16[64,2176]{1,0:T(8,128)(2,1)S(1)}, bf16[64,2176]{1,0:T(8,128)(2,1)S(1)}, u32[]{:S(2)}, u32[]{:S(2)}) collective-permute-start(bf16[64,2176]{1,0:T(8,128)(2,1)S(1)} %get-tuple-element.50.own_ref), channel_id=1, source_target_pairs={{4,8},{8,4},{0,0},{12,12},{5,9},{9,5},{1,1},{13,13},{6,10},{10,6},... | collective-permute-start | bytes 835592 | tf_op jit(solution)/shard_map/ppermute | solution.py:707
  39.2 0.1 collective-permute-start.5
  39.3 1.2 %collective-permute-done.5 = f32[32,64]{1,0:T(8,128)S(1)} collective-permute-done((f32[32,64]{1,0:T(8,128)S(1)}, f32[32,64]{1,0:T(8,128)S(1)}, u32[]{:S(2)}, u32[]{:S(2)}) %collective-permute-start.5) | collective-permute-done | bytes 8224 | tf_op jit(solution)/shard_map/ppermute | solution.py:808
  40.4 1.5 %collective-permute-start.6 = (f32[32,64]{1,0:T(8,128)S(1)}, f32[32,64]{1,0:T(8,128)S(1)}, u32[]{:S(2)}, u32[]{:S(2)}) collective-permute-start(f32[32,64]{1,0:T(8,128)S(1)} %add.9), channel_id=1, source_target_pairs={{0,2},{1,3},{2,0},{3,1},{4,6},{5,7},{6,4},{7,5},{8,10},{9,11},{10,... | collective-permute-start | bytes 24584 | tf_op jit(solution)/shard_map/ppermute | solution.py:808
  41.9 2.2 %collective-permute-done.6 = f32[32,64]{1,0:T(8,128)S(1)} collective-permute-done((f32[32,64]{1,0:T(8,128)S(1)}, f32[32,64]{1,0:T(8,128)S(1)}, u32[]{:S(2)}, u32[]{:S(2)}) %collective-permute-start.6) | collective-permute-done | bytes 8224 | tf_op jit(solution)/shard_map/ppermute | solution.py:808
  44.2 0.0 collective-permute-done.7.come_ref
  44.2 7.2 %collective-permute-done.3.refs_9_.part_ref = bf16[128,2048]{1,0:T(8,128)(2,1)S(1)} collective-permute-done((bf16[128,2048]{1,0:T(8,128)(2,1)S(1)}, bf16[128,2048]{1,0:T(8,128)(2,1)S(1)}, u32[]{:S(2)}, u32[]{:S(2)}) %collective-permute-start.3) | collective-permute-done | bytes 524320 | tf_op jit(solution)/shard_map/ppermute | solution.py:707
  51.4 0.1 total.1.own_ref
  51.5 1.7 %collective-permute-start.8 = (bf16[64,2176]{1,0:T(8,128)(2,1)S(1)}, bf16[64,2176]{1,0:T(8,128)(2,1)S(1)}, u32[]{:S(2)}, u32[]{:S(2)}) collective-permute-start(bf16[64,2176]{1,0:T(8,128)(2,1)S(1)} %total.1.own_ref), channel_id=1, source_target_pairs={{0,4},{12,8},{4,0},{8,12},{1,5},{13,9},{5,1},{9,13},{2,6},{14,10},... | collective-permute-start | bytes 835592 | tf_op jit(solution)/shard_map/ppermute | solution.py:707
  53.2 0.7 %collective-permute-start.9 = (f32[32,64]{1,0:T(8,128)S(1)}, f32[32,64]{1,0:T(8,128)S(1)}, u32[]{:S(2)}, u32[]{:S(2)}) collective-permute-start(f32[32,64]{1,0:T(8,128)S(1)} %add.10.first_ref), channel_id=1, source_target_pairs={{4,8},{8,4},{0,0},{12,12},{5,9},{9,5},{1,1},{13,13},{6,10},{10,6},... | collective-permute-start | bytes 24584 | tf_op jit(solution)/shard_map/ppermute | solution.py:707
  53.8 0.0 collective-permute-done.9
  53.9 5.3 %collective-permute-start.10 = (f32[32,64]{1,0:T(8,128)S(1)}, f32[32,64]{1,0:T(8,128)S(1)}, u32[]{:S(2)}, u32[]{:S(2)}) collective-permute-start(f32[32,64]{1,0:T(8,128)S(1)} %add.11.first_ref), channel_id=1, source_target_pairs={{0,4},{12,8},{4,0},{8,12},{1,5},{13,9},{5,1},{9,13},{2,6},{14,10},... | collective-permute-start | bytes 24584 | tf_op jit(solution)/shard_map/ppermute | solution.py:707
  59.2 0.0 copy-done
  59.2 0.0 copy-done.1
  59.2 0.0 copy-done.2
  59.2 0.0 copy-done.3
  59.2 0.0 copy-done.9
  59.2 2.1 %gates.1 = (bf16[128,2048]{1,0:T(8,128)(2,1)}, bf16[128,2048]{1,0:T(8,128)(2,1)}, bf16[128,2048]{1,0:T(8,128)(2,1)}) custom-call(s32[1]{0:T(128)} %bitcast.rank_ref.refs_0_.refs_1_, bf16[128,2048]{1,0:T(8,128)(2,1)S(1)} %copy-done, bf16[128,2048]{1,0:T(8,128)(2,1)S(1)} %copy-done.1, bf16[128,2048]{1,0:T(8,128)(2,1)S(1)} %copy-done.2, ...), custom_call_target="tpu_custom_call" | custom-call | bytes 262144 | tf_op jit(solution)/shard_map/gates/pallas_call | solution.py:820
  61.3 0.0 collective-permute-done.10.first_come_ref
  61.3 0.0 collective-permute-done.8.come_ref
  61.3 0.9 %finish.1 = (f32[64,2048]{1,0:T(8,128)}, f32[32,64]{1,0:T(8,128)}, f32[1,2048]{1,0:T(1,128)}) custom-call(s32[1]{0:T(128)} %bitcast.rank_ref.refs_0_.refs_1_, bf16[64,2176]{1,0:T(8,128)(2,1)S(1)} %total.1.own_ref, bf16[64,2176]{1,0:T(8,128)(2,1)S(1)} %collective-permute-done.8.come_ref, f32[32,64]{1,0:T(8,128)S(1)} %add.11.first_ref, ...), custom_call_target="tpu_custom_call" | custom-call | bytes 262144 | tf_op jit(solution)/shard_map/finish/pallas_call | solution.py:830
  (5 shorter events, 0.0 us)
Async XLA Ops:
  3.4 10.0 %copy-start.4 = (f32[64,2048]{1,0:T(8,128)S(1)}, f32[64,2048]{1,0:T(8,128)}, u32[]{:S(2)}) copy-start(f32[64,2048]{1,0:T(8,128)} %refs_4_.4) | copy-start | bytes 1572868
  3.4 10.0 %copy-start.5 = (bf16[256,256]{1,0:T(8,128)(2,1)S(1)}, bf16[256,256]{1,0:T(8,128)(2,1)}, u32[]{:S(2)}) copy-start(bf16[256,256]{1,0:T(8,128)(2,1)} %constant.16.clone.refs_7_.front_ref.refs_3_.refs_6_) | copy-start | bytes 393220
  3.4 10.0 %copy-start.8 = (f32[2048]{0:T(1024)S(1)}, f32[2048]{0:T(1024)}, u32[]{:S(2)}) copy-start(f32[2048]{0:T(1024)} %param.20) | copy-start | bytes 24580
  3.5 10.0 %copy-start.13 = (f32[32,64]{1,0:T(8,128)S(1)}, f32[32,64]{1,0:T(8,128)}, u32[]{:S(2)}) copy-start(f32[32,64]{1,0:T(8,128)} %first_ref.1) | copy-start | bytes 24580
  3.5 10.0 %copy-start.14 = (f32[512,32]{1,0:T(8,128)S(1)}, f32[512,32]{1,0:T(8,128)}, u32[]{:S(2)}) copy-start(f32[512,32]{1,0:T(8,128)} %constant.19.clone.feats_ref) | copy-start | bytes 196612
  3.5 19.2 %collective-permute-start = (bf16[128,2048]{1,0:T(8,128)(2,1)}, bf16[128,2048]{1,0:T(8,128)(2,1)S(1)}, u32[]{:S(2)}, u32[]{:S(2)}) collective-permute-start(bf16[128,2048]{1,0:T(8,128)(2,1)} %get-tuple-element.30.refs_3_.pair_ref), channel_id=1, source_target_pairs={{0,4},{12,8},{4,0},{8,12},{1,5},{13,9},{5,1},{9,13},{2,6},{14,10},... | collective-permute-start | bytes 1572872 | tf_op jit(solution)/shard_map/ppermute | solution.py:707
  6.6 16.2 %collective-permute-start.1 = (bf16[128,2048]{1,0:T(8,128)(2,1)}, bf16[128,2048]{1,0:T(8,128)(2,1)S(1)}, u32[]{:S(2)}, u32[]{:S(2)}) collective-permute-start(bf16[128,2048]{1,0:T(8,128)(2,1)} %get-tuple-element.31.refs_4_.other_ref), channel_id=1, source_target_pairs={{4,8},{8,4},{5,9},{9,5},{6,10},{10,6},{7,11},{11,7},{20,24},{24,20... | collective-permute-start | bytes 1572872 | tf_op jit(solution)/shard_map/ppermute | solution.py:707
  13.5 6.6 %copy-start.15 = (bf16[128,2048]{1,0:T(8,128)(2,1)S(1)}, bf16[128,2048]{1,0:T(8,128)(2,1)}, u32[]{:S(2)}) copy-start(bf16[128,2048]{1,0:T(8,128)(2,1)} %get-tuple-element.40) | copy-start | bytes 1572868
  13.5 7.9 %copy-start.16 = (bf16[64,2176]{1,0:T(8,128)(2,1)S(1)}, bf16[64,2176]{1,0:T(8,128)(2,1)}, u32[]{:S(2)}) copy-start(bf16[64,2176]{1,0:T(8,128)(2,1)} %own_pair.1) | copy-start | bytes 835588
  13.5 9.2 %copy-start.6 = (bf16[256,256]{1,0:T(8,128)(2,1)S(1)}, bf16[256,256]{1,0:T(8,128)(2,1)}, u32[]{:S(2)}) copy-start(bf16[256,256]{1,0:T(8,128)(2,1)} %constant.17.clone.refs_8_.back_ref.refs_4_.refs_7_) | copy-start | bytes 393220
  13.5 9.2 %copy-start.7 = (f32[32,512]{1,0:T(8,128)S(1)}, f32[32,512]{1,0:T(8,128)}, u32[]{:S(2)}) copy-start(f32[32,512]{1,0:T(8,128)} %constant.18.clone.refs_9_.featt_ref) | copy-start | bytes 196612
  13.5 9.2 %copy-start.11 = (bf16[128,2048]{1,0:T(8,128)(2,1)S(1)}, bf16[128,2048]{1,0:T(8,128)(2,1)}, u32[]{:S(2)}) copy-start(bf16[128,2048]{1,0:T(8,128)(2,1)} %get-tuple-element.30.refs_3_.pair_ref) | copy-start | bytes 1572868
  13.5 9.2 %copy-start.12 = (bf16[128,2048]{1,0:T(8,128)(2,1)S(1)}, bf16[128,2048]{1,0:T(8,128)(2,1)}, u32[]{:S(2)}) copy-start(bf16[128,2048]{1,0:T(8,128)(2,1)} %get-tuple-element.31.refs_4_.other_ref) | copy-start | bytes 1572868
  20.1 13.6 %collective-permute-start.2 = (bf16[128,2048]{1,0:T(8,128)(2,1)S(1)}, bf16[128,2048]{1,0:T(8,128)(2,1)S(1)}, u32[]{:S(2)}, u32[]{:S(2)}) collective-permute-start(bf16[128,2048]{1,0:T(8,128)(2,1)S(1)} %copy-done.15), channel_id=1, source_target_pairs={{0,8},{12,4},{1,9},{13,5},{2,10},{14,6},{3,11},{15,7},{16,24},{28,... | collective-permute-start | bytes 1572872 | tf_op jit(solution)/shard_map/ppermute | solution.py:707
  21.4 17.1 %collective-permute-start.4 = (bf16[64,2176]{1,0:T(8,128)(2,1)S(1)}, bf16[64,2176]{1,0:T(8,128)(2,1)S(1)}, u32[]{:S(2)}, u32[]{:S(2)}) collective-permute-start(bf16[64,2176]{1,0:T(8,128)(2,1)S(1)} %copy-done.16), channel_id=1, source_target_pairs={{0,4},{12,8},{1,5},{13,9},{2,6},{14,10},{3,7},{15,11},{16,20},{28,... | collective-permute-start | bytes 835592 | tf_op jit(solution)/shard_map/ppermute | solution.py:707
  26.6 11.9 %copy-start.10 = (f32[1,2048]{1,0:T(1,128)S(1)}, f32[1,2048]{1,0:T(1,128)}, u32[]{:S(2)}) copy-start(f32[1,2048]{1,0:T(1,128)} %get-tuple-element.32.refs_10_.refs_13_) | copy-start | bytes 24580
  33.7 25.5 %copy-start = (bf16[128,2048]{1,0:T(8,128)(2,1)S(1)}, bf16[128,2048]{1,0:T(8,128)(2,1)}, u32[]{:S(2)}) copy-start(bf16[128,2048]{1,0:T(8,128)(2,1)} %refs_1_.2) | copy-start | bytes 1572868
  33.7 25.5 %copy-start.1 = (bf16[128,2048]{1,0:T(8,128)(2,1)S(1)}, bf16[128,2048]{1,0:T(8,128)(2,1)}, u32[]{:S(2)}) copy-start(bf16[128,2048]{1,0:T(8,128)(2,1)} %refs_2_.3) | copy-start | bytes 1572868
  33.7 25.5 %copy-start.2 = (bf16[128,2048]{1,0:T(8,128)(2,1)S(1)}, bf16[128,2048]{1,0:T(8,128)(2,1)}, u32[]{:S(2)}) copy-start(bf16[128,2048]{1,0:T(8,128)(2,1)} %refs_3_.2) | copy-start | bytes 1572868
  33.7 25.5 %copy-start.3 = (bf16[128,2048]{1,0:T(8,128)(2,1)S(1)}, bf16[128,2048]{1,0:T(8,128)(2,1)}, u32[]{:S(2)}) copy-start(bf16[128,2048]{1,0:T(8,128)(2,1)} %refs_4_.3) | copy-start | bytes 1572868
  33.7 25.5 %copy-start.9 = (f32[2048]{0:T(1024)S(1)}, f32[2048]{0:T(1024)}, u32[]{:S(2)}) copy-start(f32[2048]{0:T(1024)} %param.19) | copy-start | bytes 24580
  33.7 17.7 %collective-permute-start.3 = (bf16[128,2048]{1,0:T(8,128)(2,1)S(1)}, bf16[128,2048]{1,0:T(8,128)(2,1)S(1)}, u32[]{:S(2)}, u32[]{:S(2)}) collective-permute-start(bf16[128,2048]{1,0:T(8,128)(2,1)S(1)} %get-tuple-element.43), channel_id=1, source_target_pairs={{4,0},{8,12},{5,1},{9,13},{6,2},{10,14},{7,3},{11,15},{20,16},{24,... | collective-permute-start | bytes 1572872 | tf_op jit(solution)/shard_map/ppermute | solution.py:707
  38.5 5.7 %collective-permute-start.7 = (bf16[64,2176]{1,0:T(8,128)(2,1)S(1)}, bf16[64,2176]{1,0:T(8,128)(2,1)S(1)}, u32[]{:S(2)}, u32[]{:S(2)}) collective-permute-start(bf16[64,2176]{1,0:T(8,128)(2,1)S(1)} %get-tuple-element.50.own_ref), channel_id=1, source_target_pairs={{4,8},{8,4},{0,0},{12,12},{5,9},{9,5},{1,1},{13,13},{6,10},{10,6},... | collective-permute-start | bytes 835592 | tf_op jit(solution)/shard_map/ppermute | solution.py:707
  39.2 1.2 %collective-permute-start.5 = (f32[32,64]{1,0:T(8,128)S(1)}, f32[32,64]{1,0:T(8,128)S(1)}, u32[]{:S(2)}, u32[]{:S(2)}) collective-permute-start(f32[32,64]{1,0:T(8,128)S(1)} %get-tuple-element.49), channel_id=1, source_target_pairs={{0,1},{1,0},{2,3},{3,2},{4,5},{5,4},{6,7},{7,6},{8,9},{9,8},{10,11... | collective-permute-start | bytes 24584 | tf_op jit(solution)/shard_map/ppermute | solution.py:808
  40.4 3.7 %collective-permute-start.6 = (f32[32,64]{1,0:T(8,128)S(1)}, f32[32,64]{1,0:T(8,128)S(1)}, u32[]{:S(2)}, u32[]{:S(2)}) collective-permute-start(f32[32,64]{1,0:T(8,128)S(1)} %add.9), channel_id=1, source_target_pairs={{0,2},{1,3},{2,0},{3,1},{4,6},{5,7},{6,4},{7,5},{8,10},{9,11},{10,... | collective-permute-start | bytes 24584 | tf_op jit(solution)/shard_map/ppermute | solution.py:808
  51.5 9.8 %collective-permute-start.8 = (bf16[64,2176]{1,0:T(8,128)(2,1)S(1)}, bf16[64,2176]{1,0:T(8,128)(2,1)S(1)}, u32[]{:S(2)}, u32[]{:S(2)}) collective-permute-start(bf16[64,2176]{1,0:T(8,128)(2,1)S(1)} %total.1.own_ref), channel_id=1, source_target_pairs={{0,4},{12,8},{4,0},{8,12},{1,5},{13,9},{5,1},{9,13},{2,6},{14,10},... | collective-permute-start | bytes 835592 | tf_op jit(solution)/shard_map/ppermute | solution.py:707
  53.2 0.7 %collective-permute-start.9 = (f32[32,64]{1,0:T(8,128)S(1)}, f32[32,64]{1,0:T(8,128)S(1)}, u32[]{:S(2)}, u32[]{:S(2)}) collective-permute-start(f32[32,64]{1,0:T(8,128)S(1)} %add.10.first_ref), channel_id=1, source_target_pairs={{4,8},{8,4},{0,0},{12,12},{5,9},{9,5},{1,1},{13,13},{6,10},{10,6},... | collective-permute-start | bytes 24584 | tf_op jit(solution)/shard_map/ppermute | solution.py:707
  53.9 7.4 %collective-permute-start.10 = (f32[32,64]{1,0:T(8,128)S(1)}, f32[32,64]{1,0:T(8,128)S(1)}, u32[]{:S(2)}, u32[]{:S(2)}) collective-permute-start(f32[32,64]{1,0:T(8,128)S(1)} %add.11.first_ref), channel_id=1, source_target_pairs={{0,4},{12,8},{4,0},{8,12},{1,5},{13,9},{5,1},{9,13},{2,6},{14,10},... | collective-permute-start | bytes 24584 | tf_op jit(solution)/shard_map/ppermute | solution.py:707

commit v14 on v13

--- a/solution.py
+++ b/solution.py
@@ -545,14 +545,19 @@
     return run
 
 
-def far_kernel(rows, block, blocks, rank_ref, far_ref, spec_ref, front_ref, back_ref, ahead_ref, part_ref, late_ref):
+def far_kernel(rows, block, blocks, rank_ref, far_ref, spec_ref, front_ref, back_ref, ahead_ref, part_ref):
     side = jnp.where(rank_ref[0] == 2, 1.0, -1.0).astype(f32)
     far = forward(front_ref, far_ref[...])
-    far = (far[:rows], far[rows:])
-    w2, w3 = ((spec_ref[i, :rows, :].astype(f32), spec_ref[i, rows:, :].astype(f32) * side) for i in range(2))
-    ahead = jnp.concatenate(times(w3, far), axis=0).astype(bf16)
+    w3 = (spec_ref[0, :rows, :].astype(f32), spec_ref[0, rows:, :].astype(f32) * side)
+    ahead = jnp.concatenate(times(w3, (far[:rows], far[rows:])), axis=0).astype(bf16)
     part_ref[...] = (ahead_ref[...] + backward(back_ref, ahead)).astype(bf16)
-    late = jnp.concatenate(times(w2, far), axis=0).astype(bf16)
+
+
+def late_kernel(rows, block, blocks, rank_ref, far_ref, spec_ref, front_ref, back_ref, late_ref):
+    side = jnp.where(rank_ref[0] == 2, 1.0, -1.0).astype(f32)
+    far = forward(front_ref, far_ref[...])
+    w2 = (spec_ref[0, :rows, :].astype(f32), spec_ref[0, rows:, :].astype(f32) * side)
+    late = jnp.concatenate(times(w2, (far[:rows], far[rows:])), axis=0).astype(bf16)
     late_ref[...] = backward(back_ref, late)
 
 
@@ -609,31 +614,46 @@
         total_ref[...] = first
 
 
-def total_kernel(channels, hid_count, part_ref, first_ref, own_ref, come_ref, pay_ref):
-    del part_ref, first_ref
+def total_kernel(channels, hid_count, part_ref, first_ref, late_ref, own_ref, come_ref, pay_ref):
+    del part_ref, first_ref, late_ref
     lanes = channels // 128
     pay_ref[:, :channels] = (own_ref[:, :channels].astype(f32) + come_ref[:, :channels].astype(f32)).astype(bf16)
     own, come = (get_side(ref[...], channels, lanes, hid_count)[0] for ref in (own_ref, come_ref))
     put_side(pay_ref, channels, own + come)
 
 
-def gates_kernel(
-    shards, block, blocks, rank_ref, one_ref, two_ref, val_ref, out_ref, skip_ref, conv_ref, corr_ref, late_ref, part_ref,
+def gates_kernel(inner, shards, blocks, width, before, *refs):
+    refs = refs[before:]
+    inputs, outs, held, sems = refs[:10], refs[10:13], refs[13:16], refs[16]
+
+    def leaving(block, i):
+        cols = pl.ds(pl.multiple_of(block * width, width), width)
+        return pltpu.make_async_copy(held[i].at[:, cols], outs[i].at[:, cols], sems.at[block, i])
+
+    def strip(block, blocks, *views):
+        gates_strip(inner, shards, *views)
+        for i in range(3):
+            leaving(block, i).start()
+
+    looped(strip, (None,) + (ROWS,) * 12, blocks, width)(*inputs, *held)
+    for block in range(blocks):
+        for i in range(3):
+            leaving(block, i).wait()
+
+
+def gates_strip(
+    inner, shards, rank_ref, one_ref, two_ref, val_ref, out_ref, skip_ref, conv_ref, corr_ref, late_ref, part_ref,
     grad_one_ref, grad_two_ref, grad_value_ref,
 ):
-    rank = rank_ref[0]
-
-    def on(wanted, value):
-        return jnp.where(rank == wanted, value, jnp.zeros_like(value))
-
-    part = part_ref[...].astype(f32)
-    late = late_ref[...]
+    late = late_ref[...] if inner else part_ref[...].astype(f32)
+    upper = rank_ref[0] >= shards // 2
+    zero = jnp.zeros_like(late)
     one = one_ref[...].astype(f32)
     val = val_ref[...].astype(f32)
     out = out_ref[...].astype(f32)
     skip = skip_ref[...]
-    conv = conv_ref[...] + on(2, late) + on(shards - 1, part)
-    corr = corr_ref[...] + on(1, late) + on(0, part)
+    conv = conv_ref[...] + jnp.where(upper, late, zero)
+    corr = corr_ref[...] + jnp.where(upper, zero, late)
     grad_two_ref[...] = (out * (conv + skip * (one * val))).astype(bf16)
     mid = corr + skip * (out * two_ref[...].astype(f32))
     grad_one_ref[...] = (mid * val).astype(bf16)
@@ -772,19 +792,32 @@
         ],
     )(rank, pair, other, pair_in, middle_in, spec, second_weight, rate_row, front, back, trans, featt, slope)
 
-    part, late = call(
+    (part,) = call(
         only(
             True, shards, 0,
             looped(
                 functools.partial(far_kernel, rows),
-                (None, ROWS, (slice(2, 4), slice(None)), None, None, ROWS, ROWS, ROWS),
+                (None, ROWS, (slice(3, 4), slice(None)), None, None, ROWS, ROWS),
                 blocks, width,
             ),
         ),
         "far_block", 1,
-        [block_bf16, block_f32],
+        [block_bf16],
         [smem] + [vmem] * 5,
     )(rank, far, spec, front, back, ahead)
+    (late,) = call(
+        only(
+            True, shards, 0,
+            looped(
+                functools.partial(late_kernel, rows),
+                (None, ROWS, (slice(2, 3), slice(None)), None, None, ROWS),
+                blocks, width,
+            ),
+        ),
+        "late_block", 1,
+        [block_f32],
+        [smem] + [vmem] * 4,
+    )(rank, far, spec, front, back)
     part_come = move(part, outward)
 
     pay, first = call(
@@ -800,7 +833,7 @@
         [shape(*pay_shape, dtype=bf16), shape(feat_count, hid_count)],
         [anywhere, smem] + [vmem] * 13,
         scratch=[pltpu.VMEM((2 * rows, hid_count), f32)],
-    )(late, rank, pair_in, far, second_weight, rate_row, front, back, trans, featt, slope, sums, first, bias, come)
+    )(part, rank, pair_in, far, second_weight, rate_row, front, back, trans, featt, slope, sums, first, bias, come)
     pay_come = move(pay, across + alone)
     group = lax.axis_size(("ch", "sub"))
     bit = 1
@@ -811,20 +844,29 @@
     (total,) = call(
         functools.partial(total_kernel, channels, hid_count), "total", 0,
         [shape(*pay_shape, dtype=bf16)],
-        [anywhere] * 2 + [vmem] * 2,
-    )(part_come, first, pay, pay_come)
+        [anywhere] * 3 + [vmem] * 2,
+    )(part_come, first, late, pay, pay_come)
     total_come = move(total, inward + outward)
+
+    def gates(inner, *before):
+        return call(
+            only(
+                inner, shards, len(before),
+                functools.partial(gates_kernel, inner, shards, blocks, width, len(before)),
+            ),
+            "gates", 0,
+            [block_bf16] * 3,
+            [anywhere] * len(before) + [smem] + [vmem] * 9,
+            out_specs=[anywhere] * 3,
+            scratch=[pltpu.VMEM((rows, channels), bf16)] * 3 + [pltpu.SemaphoreType.DMA((blocks, 3))],
+            aliases={i: i for i in range(3)} if inner else {},
+        )(*before, rank, x_one, x_two, values, grad_out, skip_row, conv, corr, late, part_come)
+
+    grads = gates(False, total)
+    first, _ = lax.optimization_barrier((first, grads[0]))
     first = first + move(first, across + alone)
     first_come = move(first, inward + outward)
-
-    grad_one, grad_two, grad_value = call(
-        looped(
-            functools.partial(gates_kernel, shards), (None,) + (ROWS,) * 12, blocks, width
-        ),
-        "gates", 0,
-        [block_bf16] * 3,
-        [smem] + [vmem] * 9,
-    )(rank, x_one, x_two, values, grad_out, skip_row, conv, corr, late, part_come)
+    grad_one, grad_two, grad_value = gates(True, *grads)
 
     outs = [shape(hid_count, channels), shape(feat_count, hid_count), shape(1, channels)]
     grad_second, grad_first, grad_bias = call(

time: 62.4 us -> 61.8 us (level)
  starting transfers between devices: 17.7 us -> 16.7 us
  waiting for transfers between devices: 21.1 us -> 21.9 us
    ppermute x9, starting transfers between devices: 16.2 us -> 15 us  [move(): return lax.ppermute(array, 'ctx', pairs)]
    ppermute x9, waiting for transfers between devices: 17.7 us -> 18.5 us  [move(): return lax.ppermute(array, 'ctx', pairs)]
    pallas_call x1 -> x3, Pallas kernels: 2.08 us -> 1.75 us  [the longest x2 1.75 us: gates(): call(only(inner, shards, len(before), functools.partial(gates_kernel, inn...]
  transfers between devices with their start and end apart: 11 -> 11, of which waited for: 5 -> 6; matrix products, arithmetic and copies ran while one was open for 0% -> 0% of each run, Pallas kernels for 30% -> 30%
where the time goes in v14:
time: 61.8 us; the launch traced here: 61.6 us
  Pallas kernels  21.9 us (35%)
  waiting for transfers between devices  21.9 us (35%)
  starting transfers between devices  16.7 us (27%)
  between operations  1 us (2%)
    ppermute x9, waiting for transfers between devices, move(): return lax.ppermute(array, 'ctx', pairs)  18.5 us
    ppermute x9, starting transfers between devices, move(): return lax.ppermute(array, 'ctx', pairs)  15 us
    pallas_call x1, Pallas kernels, few_shards_body(): call(functools.partial(filters_kernel, rows, shards, blocks, width), 'fil...  6.5 us
    pallas_call x1, Pallas kernels, few_shards_body(): call(only(False, shards, 0, functools.partial(own_kernel, rows, shards, c...  6.15 us
    pallas_call x1, Pallas kernels, few_shards_body(): call(functools.partial(near_kernel, rows, shards, blocks, width), 'near_b...  3.82 us
    ppermute x2, waiting for transfers between devices, few_shards_body(): lax.ppermute(first, ('ch', 'sub'), [(i, i ^ bit) for i in range(group)])  3.41 us
    pallas_call x1, Pallas kernels, few_shards_body(): pl.pallas_call(products_kernel, grid=(rows // row_step,), in_specs=[smem]...  2.79 us
    pallas_call x2, Pallas kernels, gates(): call(only(inner, shards, len(before), functools.partial(gates_kernel, inn...  1.75 us
  transfers between devices with their start and end apart: 11, of which 6 were waited for; matrix products, arithmetic and copies ran while one was open for 0% of the time, Pallas kernels for 30%

profile of v14, /device:TPU:0, one launch (start us, length us, event | category | flops | bytes accessed | tf_op | source)
XLA Modules:
  0.0 61.6 jit_solution(4708017835965795548)
XLA Ops:
  0.6 2.8 %products.1 = (bf16[128,2048]{1,0:T(8,128)(2,1)}, bf16[128,2048]{1,0:T(8,128)(2,1)}, bf16[128,2048]{1,0:T(8,128)(2,1)}, f32[1,2048]{1,0:T(1,128)}) custom-call(s32[1]{0:T(128)} %bitcast.rank_ref.refs_0_.refs_1_.refs_3_, bf16[128,2048]{1,0:T(8,128)(2,1)} %refs_4_.7, bf16[128,2048]{1,0:T(8,128)(2,1)} %refs_5_.5, bf16[128,2048]{1,0:T(8,128)(2,1)} %refs_6_.2, ...), custom_call_target="tpu_custom_call" | custom-call | tf_op jit(solution)/shard_map/products/pallas_call | solution.py:739
  3.4 0.0 copy-start.4
  3.4 0.0 copy-start.6
  3.4 0.0 copy-start.9
  3.5 0.0 copy-start.13
  3.5 0.0 copy-start.14
  3.5 3.1 %collective-permute-start.1 = (bf16[128,2048]{1,0:T(8,128)(2,1)}, bf16[128,2048]{1,0:T(8,128)(2,1)S(1)}, u32[]{:S(2)}, u32[]{:S(2)}) collective-permute-start(bf16[128,2048]{1,0:T(8,128)(2,1)} %get-tuple-element.33.refs_3_.pair_ref), channel_id=1, source_target_pairs={{0,4},{12,8},{4,0},{8,12},{1,5},{13,9},{5,1},{9,13},{2,6},{14,10},... | collective-permute-start | bytes 1572872 | tf_op jit(solution)/shard_map/ppermute | solution.py:727
  6.6 0.7 %collective-permute-start.2 = (bf16[128,2048]{1,0:T(8,128)(2,1)}, bf16[128,2048]{1,0:T(8,128)(2,1)S(1)}, u32[]{:S(2)}, u32[]{:S(2)}) collective-permute-start(bf16[128,2048]{1,0:T(8,128)(2,1)} %get-tuple-element.34.refs_4_.other_ref), channel_id=1, source_target_pairs={{4,8},{8,4},{5,9},{9,5},{6,10},{10,6},{7,11},{11,7},{20,24},{24,20... | collective-permute-start | bytes 1572872 | tf_op jit(solution)/shard_map/ppermute | solution.py:727
  7.3 6.1 %own_pair.1 = bf16[64,2176]{1,0:T(8,128)(2,1)} custom-call(s32[1]{0:T(128)} %bitcast.rank_ref.refs_0_.refs_1_.refs_3_, f32[128,32]{1,0:T(8,128)} %constant.15.clone.refs_1_, f32[32,64]{1,0:T(8,128)} %first_ref.1, bf16[128,2048]{1,0:T(8,128)(2,1)} %get-tuple-element.33.refs_3_.pair_ref, bf16[128,2048]{1,0:T(8,128)(2,1)} %get-tuple-element.34.refs_4_.other_ref, ...), custom_call_target="tpu_custom_call" | custom-call | flops 2147483648 | bytes 262144 | tf_op jit(solution)/shard_map/own_pair/pallas_call | solution.py:756
  13.4 0.0 copy-done.4
  13.4 0.0 copy-done.6
  13.4 0.0 copy-done.9
  13.4 0.0 copy-done.13
  13.5 0.0 copy-done.14
  13.5 0.0 copy-start.15
  13.5 0.0 copy-start.16
  13.5 0.0 copy-start.5
  13.5 0.0 copy-start.7
  13.5 0.0 copy-start.11
  13.5 0.0 copy-start.12
  13.5 6.5 %filters.1 = (bf16[4,256,2048]{2,1,0:T(8,128)(2,1)S(1)}, bf16[128,512]{1,0:T(8,128)(2,1)S(1)}, f32[512,64]{1,0:T(8,128)S(1)}) custom-call(f32[512,32]{1,0:T(8,128)S(1)} %copy-done.14, f32[32,64]{1,0:T(8,128)S(1)} %copy-done.13, f32[64,2048]{1,0:T(8,128)S(1)} %copy-done.6, f32[1,2048]{1,0:T(1,128)S(1)} %bitcast.7, bf16[256,256]{1,0:T(8,128)(2,1)S(1)} %copy-done.4), custom_call_target="tpu_custom_call" | custom-call | flops 2147483648 | bytes 262144 | tf_op jit(solution)/shard_map/filters/pallas_call | solution.py:770
  20.0 0.0 copy-done.15
  20.1 1.3 %collective-permute-start = (bf16[128,2048]{1,0:T(8,128)(2,1)S(1)}, bf16[128,2048]{1,0:T(8,128)(2,1)S(1)}, u32[]{:S(2)}, u32[]{:S(2)}) collective-permute-start(bf16[128,2048]{1,0:T(8,128)(2,1)S(1)} %copy-done.15), channel_id=1, source_target_pairs={{0,8},{12,4},{1,9},{13,5},{2,10},{14,6},{3,11},{15,7},{16,24},{28,... | collective-permute-start | bytes 1572872 | tf_op jit(solution)/shard_map/ppermute | solution.py:727
  21.4 0.0 copy-done.16
  21.4 1.3 %collective-permute-start.4 = (bf16[64,2176]{1,0:T(8,128)(2,1)S(1)}, bf16[64,2176]{1,0:T(8,128)(2,1)S(1)}, u32[]{:S(2)}, u32[]{:S(2)}) collective-permute-start(bf16[64,2176]{1,0:T(8,128)(2,1)S(1)} %copy-done.16), channel_id=1, source_target_pairs={{0,4},{12,8},{1,5},{13,9},{2,6},{14,10},{3,7},{15,11},{16,20},{28,... | collective-permute-start | bytes 835592 | tf_op jit(solution)/shard_map/ppermute | solution.py:727
  22.7 0.0 collective-permute-done.1.pair_in_ref.refs_2_
  22.7 0.0 collective-permute-done.2.middle_in_ref
  22.7 0.0 copy-done.5
  22.7 0.0 copy-done.7
  22.8 0.0 copy-done.11
  22.8 0.0 copy-done.12
  22.8 3.8 %near_blocks.1 = (f32[128,2048]{1,0:T(8,128)S(1)}, f32[128,2048]{1,0:T(8,128)S(1)}, f32[128,2048]{1,0:T(8,128)S(1)}, f32[64,2048]{1,0:T(8,128)S(1)}, f32[32,64]{1,0:T(8,128)S(1)}) custom-call(s32[1]{0:T(128)} %bitcast.rank_ref.refs_0_.refs_1_.refs_3_, bf16[128,2048]{1,0:T(8,128)(2,1)S(1)} %copy-done.11, bf16[128,2048]{1,0:T(8,128)(2,1)S(1)} %copy-done.12, ...), custom_call_target="tpu_custom_call" | custom-call | flops 5368709120 | bytes 262144 | tf_op jit(solution)/shard_map/near_blocks/pallas_call | solution.py:782
  26.6 0.0 copy-start.10
  26.6 7.1 %collective-permute-done.refs_1_.refs_3_ = bf16[128,2048]{1,0:T(8,128)(2,1)S(1)} collective-permute-done((bf16[128,2048]{1,0:T(8,128)(2,1)S(1)}, bf16[128,2048]{1,0:T(8,128)(2,1)S(1)}, u32[]{:S(2)}, u32[]{:S(2)}) %collective-permute-start) | collective-permute-done | bytes 524320 | tf_op jit(solution)/shard_map/ppermute | solution.py:727
  33.7 1.3 %collective-permute-start.3 = (bf16[128,2048]{1,0:T(8,128)(2,1)S(1)}, bf16[128,2048]{1,0:T(8,128)(2,1)S(1)}, u32[]{:S(2)}, u32[]{:S(2)}) collective-permute-start(bf16[128,2048]{1,0:T(8,128)(2,1)S(1)} %far_block.1.refs_0_), channel_id=1, source_target_pairs={{4,0},{8,12},{5,1},{9,13},{6,2},{10,14},{7,3},{11,15},{20,16},{24,... | collective-permute-start | bytes 1572872 | tf_op jit(solution)/shard_map/ppermute | solution.py:727
  35.0 3.5 %collective-permute-done.4.refs_14_ = bf16[64,2176]{1,0:T(8,128)(2,1)S(1)} collective-permute-done((bf16[64,2176]{1,0:T(8,128)(2,1)S(1)}, bf16[64,2176]{1,0:T(8,128)(2,1)S(1)}, u32[]{:S(2)}, u32[]{:S(2)}) %collective-permute-start.4) | collective-permute-done | bytes 278560 | tf_op jit(solution)/shard_map/ppermute | solution.py:727
  38.5 0.0 copy-done.10
  38.5 0.7 %collective-permute-start.7 = (bf16[64,2176]{1,0:T(8,128)(2,1)S(1)}, bf16[64,2176]{1,0:T(8,128)(2,1)S(1)}, u32[]{:S(2)}, u32[]{:S(2)}) collective-permute-start(bf16[64,2176]{1,0:T(8,128)(2,1)S(1)} %get-tuple-element.45.own_ref), channel_id=1, source_target_pairs={{4,8},{8,4},{0,0},{12,12},{5,9},{9,5},{1,1},{13,13},{6,10},{10,6},... | collective-permute-start | bytes 835592 | tf_op jit(solution)/shard_map/ppermute | solution.py:727
  39.2 0.1 collective-permute-start.5
  39.3 1.2 %collective-permute-done.5 = f32[32,64]{1,0:T(8,128)S(1)} collective-permute-done((f32[32,64]{1,0:T(8,128)S(1)}, f32[32,64]{1,0:T(8,128)S(1)}, u32[]{:S(2)}, u32[]{:S(2)}) %collective-permute-start.5) | collective-permute-done | bytes 8224 | tf_op jit(solution)/shard_map/ppermute | solution.py:841
  40.4 0.0 copy-start
  40.4 0.0 copy-start.1
  40.4 0.0 copy-start.2
  40.5 0.0 copy-start.3
  40.5 0.0 copy-start.8
  40.5 1.6 %collective-permute-start.6 = (f32[32,64]{1,0:T(8,128)S(1)}, f32[32,64]{1,0:T(8,128)S(1)}, u32[]{:S(2)}, u32[]{:S(2)}) collective-permute-start(f32[32,64]{1,0:T(8,128)S(1)} %add.9), channel_id=1, source_target_pairs={{0,2},{1,3},{2,0},{3,1},{4,6},{5,7},{6,4},{7,5},{8,10},{9,11},{10,... | collective-permute-start | bytes 24584 | tf_op jit(solution)/shard_map/ppermute | solution.py:841
  42.0 2.2 %collective-permute-done.6 = f32[32,64]{1,0:T(8,128)S(1)} collective-permute-done((f32[32,64]{1,0:T(8,128)S(1)}, f32[32,64]{1,0:T(8,128)S(1)}, u32[]{:S(2)}, u32[]{:S(2)}) %collective-permute-start.6) | collective-permute-done | bytes 8224 | tf_op jit(solution)/shard_map/ppermute | solution.py:841
  44.3 0.0 collective-permute-done.7.come_ref
  44.3 6.3 %collective-permute-done.3.part_ref.refs_10_.refs_12_ = bf16[128,2048]{1,0:T(8,128)(2,1)S(1)} collective-permute-done((bf16[128,2048]{1,0:T(8,128)(2,1)S(1)}, bf16[128,2048]{1,0:T(8,128)(2,1)S(1)}, u32[]{:S(2)}, u32[]{:S(2)}) %collective-permute-start.3) | collective-permute-done | bytes 524320 | tf_op jit(solution)/shard_map/ppermute | solution.py:727
  50.5 0.1 total.1.refs_0_.own_ref
  50.6 2.6 %collective-permute-start.8 = (bf16[64,2176]{1,0:T(8,128)(2,1)S(1)}, bf16[64,2176]{1,0:T(8,128)(2,1)S(1)}, u32[]{:S(2)}, u32[]{:S(2)}) collective-permute-start(bf16[64,2176]{1,0:T(8,128)(2,1)S(1)} %total.1.refs_0_.own_ref), channel_id=1, source_target_pairs={{0,4},{12,8},{4,0},{8,12},{1,5},{13,9},{5,1},{9,13},{2,6},{14,10},... | collective-permute-start | bytes 835592 | tf_op jit(solution)/shard_map/ppermute | solution.py:727
  53.2 0.0 copy-done
  53.2 0.0 copy-done.1
  53.2 0.0 copy-done.2
  53.2 0.0 copy-done.3
  53.2 0.0 copy-done.8
  53.2 1.6 %gates.2 = (bf16[128,2048]{1,0:T(8,128)(2,1)}, bf16[128,2048]{1,0:T(8,128)(2,1)}, bf16[128,2048]{1,0:T(8,128)(2,1)}) custom-call(bf16[64,2176]{1,0:T(8,128)(2,1)S(1)} %total.1.refs_0_.own_ref, s32[1]{0:T(128)} %bitcast.rank_ref.refs_0_.refs_1_.refs_3_, bf16[128,2048]{1,0:T(8,128)(2,1)S(1)} %copy-done, bf16[128,2048]{1,0:T(8,128)(2,1)S(1)} %copy-done.1, ...), custom_call_target="tpu_custom_call" | custom-call | bytes 262144 | tf_op jit(solution)/shard_map/gates/pallas_call | solution.py:852
  54.8 0.7 %collective-permute-start.9 = (f32[32,64]{1,0:T(8,128)S(1)}, f32[32,64]{1,0:T(8,128)S(1)}, u32[]{:S(2)}, u32[]{:S(2)}) collective-permute-start(f32[32,64]{1,0:T(8,128)S(1)} %add.10.first_ref), channel_id=1, source_target_pairs={{4,8},{8,4},{0,0},{12,12},{5,9},{9,5},{1,1},{13,13},{6,10},{10,6},... | collective-permute-start | bytes 24584 | tf_op jit(solution)/shard_map/ppermute | solution.py:727
  55.5 0.0 collective-permute-done.9
  55.5 3.5 %collective-permute-start.10 = (f32[32,64]{1,0:T(8,128)S(1)}, f32[32,64]{1,0:T(8,128)S(1)}, u32[]{:S(2)}, u32[]{:S(2)}) collective-permute-start(f32[32,64]{1,0:T(8,128)S(1)} %add.11.first_ref), channel_id=1, source_target_pairs={{0,4},{12,8},{4,0},{8,12},{1,5},{13,9},{5,1},{9,13},{2,6},{14,10},... | collective-permute-start | bytes 24584 | tf_op jit(solution)/shard_map/ppermute | solution.py:727
  59.0 0.1 gates.3
  59.1 1.6 %collective-permute-done.10.first_come_ref = f32[32,64]{1,0:T(8,128)S(1)} collective-permute-done((f32[32,64]{1,0:T(8,128)S(1)}, f32[32,64]{1,0:T(8,128)S(1)}, u32[]{:S(2)}, u32[]{:S(2)}) %collective-permute-start.10) | collective-permute-done | bytes 8224 | tf_op jit(solution)/shard_map/ppermute | solution.py:727
  60.7 0.0 collective-permute-done.8.come_ref
  60.7 0.9 %finish.1 = (f32[64,2048]{1,0:T(8,128)}, f32[32,64]{1,0:T(8,128)}, f32[1,2048]{1,0:T(1,128)}) custom-call(s32[1]{0:T(128)} %bitcast.rank_ref.refs_0_.refs_1_.refs_3_, bf16[64,2176]{1,0:T(8,128)(2,1)S(1)} %total.1.refs_0_.own_ref, bf16[64,2176]{1,0:T(8,128)(2,1)S(1)} %collective-permute-done.8.come_ref, f32[32,64]{1,0:T(8,128)S(1)} %add.11.first_ref, ...), custom_call_target="tpu_custom_call" | custom-call | bytes 262144 | tf_op jit(solution)/shard_map/finish/pallas_call | solution.py:872
  (6 shorter events, 0.0 us)
Async XLA Ops:
  3.4 10.0 %copy-start.4 = (bf16[256,256]{1,0:T(8,128)(2,1)S(1)}, bf16[256,256]{1,0:T(8,128)(2,1)}, u32[]{:S(2)}) copy-start(bf16[256,256]{1,0:T(8,128)(2,1)} %constant.16.clone.refs_7_.front_ref.refs_3_.refs_6_) | copy-start | bytes 393220
  3.4 10.0 %copy-start.6 = (f32[64,2048]{1,0:T(8,128)S(1)}, f32[64,2048]{1,0:T(8,128)}, u32[]{:S(2)}) copy-start(f32[64,2048]{1,0:T(8,128)} %refs_4_.5) | copy-start | bytes 1572868
  3.4 10.0 %copy-start.9 = (f32[2048]{0:T(1024)S(1)}, f32[2048]{0:T(1024)}, u32[]{:S(2)}) copy-start(f32[2048]{0:T(1024)} %param.20) | copy-start | bytes 24580
  3.5 10.0 %copy-start.13 = (f32[32,64]{1,0:T(8,128)S(1)}, f32[32,64]{1,0:T(8,128)}, u32[]{:S(2)}) copy-start(f32[32,64]{1,0:T(8,128)} %first_ref.1) | copy-start | bytes 24580
  3.5 10.0 %copy-start.14 = (f32[512,32]{1,0:T(8,128)S(1)}, f32[512,32]{1,0:T(8,128)}, u32[]{:S(2)}) copy-start(f32[512,32]{1,0:T(8,128)} %constant.19.clone.feats_ref) | copy-start | bytes 196612
  3.5 19.2 %collective-permute-start.1 = (bf16[128,2048]{1,0:T(8,128)(2,1)}, bf16[128,2048]{1,0:T(8,128)(2,1)S(1)}, u32[]{:S(2)}, u32[]{:S(2)}) collective-permute-start(bf16[128,2048]{1,0:T(8,128)(2,1)} %get-tuple-element.33.refs_3_.pair_ref), channel_id=1, source_target_pairs={{0,4},{12,8},{4,0},{8,12},{1,5},{13,9},{5,1},{9,13},{2,6},{14,10},... | collective-permute-start | bytes 1572872 | tf_op jit(solution)/shard_map/ppermute | solution.py:727
  6.6 16.2 %collective-permute-start.2 = (bf16[128,2048]{1,0:T(8,128)(2,1)}, bf16[128,2048]{1,0:T(8,128)(2,1)S(1)}, u32[]{:S(2)}, u32[]{:S(2)}) collective-permute-start(bf16[128,2048]{1,0:T(8,128)(2,1)} %get-tuple-element.34.refs_4_.other_ref), channel_id=1, source_target_pairs={{4,8},{8,4},{5,9},{9,5},{6,10},{10,6},{7,11},{11,7},{20,24},{24,20... | collective-permute-start | bytes 1572872 | tf_op jit(solution)/shard_map/ppermute | solution.py:727
  13.5 6.6 %copy-start.15 = (bf16[128,2048]{1,0:T(8,128)(2,1)S(1)}, bf16[128,2048]{1,0:T(8,128)(2,1)}, u32[]{:S(2)}) copy-start(bf16[128,2048]{1,0:T(8,128)(2,1)} %get-tuple-element.38) | copy-start | bytes 1572868
  13.5 7.9 %copy-start.16 = (bf16[64,2176]{1,0:T(8,128)(2,1)S(1)}, bf16[64,2176]{1,0:T(8,128)(2,1)}, u32[]{:S(2)}) copy-start(bf16[64,2176]{1,0:T(8,128)(2,1)} %own_pair.1) | copy-start | bytes 835588
  13.5 9.2 %copy-start.5 = (bf16[256,256]{1,0:T(8,128)(2,1)S(1)}, bf16[256,256]{1,0:T(8,128)(2,1)}, u32[]{:S(2)}) copy-start(bf16[256,256]{1,0:T(8,128)(2,1)} %constant.17.clone.refs_8_.back_ref.refs_4_.refs_7_) | copy-start | bytes 393220
  13.5 9.2 %copy-start.7 = (f32[32,512]{1,0:T(8,128)S(1)}, f32[32,512]{1,0:T(8,128)}, u32[]{:S(2)}) copy-start(f32[32,512]{1,0:T(8,128)} %constant.18.clone.refs_9_.featt_ref) | copy-start | bytes 196612
  13.5 9.2 %copy-start.11 = (bf16[128,2048]{1,0:T(8,128)(2,1)S(1)}, bf16[128,2048]{1,0:T(8,128)(2,1)}, u32[]{:S(2)}) copy-start(bf16[128,2048]{1,0:T(8,128)(2,1)} %get-tuple-element.33.refs_3_.pair_ref) | copy-start | bytes 1572868
  13.5 9.2 %copy-start.12 = (bf16[128,2048]{1,0:T(8,128)(2,1)S(1)}, bf16[128,2048]{1,0:T(8,128)(2,1)}, u32[]{:S(2)}) copy-start(bf16[128,2048]{1,0:T(8,128)(2,1)} %get-tuple-element.34.refs_4_.other_ref) | copy-start | bytes 1572868
  20.1 13.6 %collective-permute-start = (bf16[128,2048]{1,0:T(8,128)(2,1)S(1)}, bf16[128,2048]{1,0:T(8,128)(2,1)S(1)}, u32[]{:S(2)}, u32[]{:S(2)}) collective-permute-start(bf16[128,2048]{1,0:T(8,128)(2,1)S(1)} %copy-done.15), channel_id=1, source_target_pairs={{0,8},{12,4},{1,9},{13,5},{2,10},{14,6},{3,11},{15,7},{16,24},{28,... | collective-permute-start | bytes 1572872 | tf_op jit(solution)/shard_map/ppermute | solution.py:727
  21.4 17.1 %collective-permute-start.4 = (bf16[64,2176]{1,0:T(8,128)(2,1)S(1)}, bf16[64,2176]{1,0:T(8,128)(2,1)S(1)}, u32[]{:S(2)}, u32[]{:S(2)}) collective-permute-start(bf16[64,2176]{1,0:T(8,128)(2,1)S(1)} %copy-done.16), channel_id=1, source_target_pairs={{0,4},{12,8},{1,5},{13,9},{2,6},{14,10},{3,7},{15,11},{16,20},{28,... | collective-permute-start | bytes 835592 | tf_op jit(solution)/shard_map/ppermute | solution.py:727
  26.6 11.9 %copy-start.10 = (f32[1,2048]{1,0:T(1,128)S(1)}, f32[1,2048]{1,0:T(1,128)}, u32[]{:S(2)}) copy-start(f32[1,2048]{1,0:T(1,128)} %get-tuple-element.35.refs_10_.refs_13_) | copy-start | bytes 24580
  33.7 16.9 %collective-permute-start.3 = (bf16[128,2048]{1,0:T(8,128)(2,1)S(1)}, bf16[128,2048]{1,0:T(8,128)(2,1)S(1)}, u32[]{:S(2)}, u32[]{:S(2)}) collective-permute-start(bf16[128,2048]{1,0:T(8,128)(2,1)S(1)} %far_block.1.refs_0_), channel_id=1, source_target_pairs={{4,0},{8,12},{5,1},{9,13},{6,2},{10,14},{7,3},{11,15},{20,16},{24,... | collective-permute-start | bytes 1572872 | tf_op jit(solution)/shard_map/ppermute | solution.py:727
  38.5 5.8 %collective-permute-start.7 = (bf16[64,2176]{1,0:T(8,128)(2,1)S(1)}, bf16[64,2176]{1,0:T(8,128)(2,1)S(1)}, u32[]{:S(2)}, u32[]{:S(2)}) collective-permute-start(bf16[64,2176]{1,0:T(8,128)(2,1)S(1)} %get-tuple-element.45.own_ref), channel_id=1, source_target_pairs={{4,8},{8,4},{0,0},{12,12},{5,9},{9,5},{1,1},{13,13},{6,10},{10,6},... | collective-permute-start | bytes 835592 | tf_op jit(solution)/shard_map/ppermute | solution.py:727
  39.2 1.2 %collective-permute-start.5 = (f32[32,64]{1,0:T(8,128)S(1)}, f32[32,64]{1,0:T(8,128)S(1)}, u32[]{:S(2)}, u32[]{:S(2)}) collective-permute-start(f32[32,64]{1,0:T(8,128)S(1)} %get-tuple-element.44), channel_id=1, source_target_pairs={{0,1},{1,0},{2,3},{3,2},{4,5},{5,4},{6,7},{7,6},{8,9},{9,8},{10,11... | collective-permute-start | bytes 24584 | tf_op jit(solution)/shard_map/ppermute | solution.py:841
  40.4 12.7 %copy-start = (bf16[128,2048]{1,0:T(8,128)(2,1)S(1)}, bf16[128,2048]{1,0:T(8,128)(2,1)}, u32[]{:S(2)}) copy-start(bf16[128,2048]{1,0:T(8,128)(2,1)} %refs_4_.7) | copy-start | bytes 1572868
  40.4 12.7 %copy-start.1 = (bf16[128,2048]{1,0:T(8,128)(2,1)S(1)}, bf16[128,2048]{1,0:T(8,128)(2,1)}, u32[]{:S(2)}) copy-start(bf16[128,2048]{1,0:T(8,128)(2,1)} %refs_5_.5) | copy-start | bytes 1572868
  40.4 12.7 %copy-start.2 = (bf16[128,2048]{1,0:T(8,128)(2,1)S(1)}, bf16[128,2048]{1,0:T(8,128)(2,1)}, u32[]{:S(2)}) copy-start(bf16[128,2048]{1,0:T(8,128)(2,1)} %refs_6_.2) | copy-start | bytes 1572868
  40.5 12.7 %copy-start.3 = (bf16[128,2048]{1,0:T(8,128)(2,1)S(1)}, bf16[128,2048]{1,0:T(8,128)(2,1)}, u32[]{:S(2)}) copy-start(bf16[128,2048]{1,0:T(8,128)(2,1)} %refs_7_.3) | copy-start | bytes 1572868
  40.5 12.7 %copy-start.8 = (f32[2048]{0:T(1024)S(1)}, f32[2048]{0:T(1024)}, u32[]{:S(2)}) copy-start(f32[2048]{0:T(1024)} %param.19) | copy-start | bytes 24580
  40.5 3.8 %collective-permute-start.6 = (f32[32,64]{1,0:T(8,128)S(1)}, f32[32,64]{1,0:T(8,128)S(1)}, u32[]{:S(2)}, u32[]{:S(2)}) collective-permute-start(f32[32,64]{1,0:T(8,128)S(1)} %add.9), channel_id=1, source_target_pairs={{0,2},{1,3},{2,0},{3,1},{4,6},{5,7},{6,4},{7,5},{8,10},{9,11},{10,... | collective-permute-start | bytes 24584 | tf_op jit(solution)/shard_map/ppermute | solution.py:841
  50.6 10.1 %collective-permute-start.8 = (bf16[64,2176]{1,0:T(8,128)(2,1)S(1)}, bf16[64,2176]{1,0:T(8,128)(2,1)S(1)}, u32[]{:S(2)}, u32[]{:S(2)}) collective-permute-start(bf16[64,2176]{1,0:T(8,128)(2,1)S(1)} %total.1.refs_0_.own_ref), channel_id=1, source_target_pairs={{0,4},{12,8},{4,0},{8,12},{1,5},{13,9},{5,1},{9,13},{2,6},{14,10},... | collective-permute-start | bytes 835592 | tf_op jit(solution)/shard_map/ppermute | solution.py:727
  54.8 0.7 %collective-permute-start.9 = (f32[32,64]{1,0:T(8,128)S(1)}, f32[32,64]{1,0:T(8,128)S(1)}, u32[]{:S(2)}, u32[]{:S(2)}) collective-permute-start(f32[32,64]{1,0:T(8,128)S(1)} %add.10.first_ref), channel_id=1, source_target_pairs={{4,8},{8,4},{0,0},{12,12},{5,9},{9,5},{1,1},{13,13},{6,10},{10,6},... | collective-permute-start | bytes 24584 | tf_op jit(solution)/shard_map/ppermute | solution.py:727
  55.5 5.2 %collective-permute-start.10 = (f32[32,64]{1,0:T(8,128)S(1)}, f32[32,64]{1,0:T(8,128)S(1)}, u32[]{:S(2)}, u32[]{:S(2)}) collective-permute-start(f32[32,64]{1,0:T(8,128)S(1)} %add.11.first_ref), channel_id=1, source_target_pairs={{0,4},{12,8},{4,0},{8,12},{1,5},{13,9},{5,1},{9,13},{2,6},{14,10},... | collective-permute-start | bytes 24584 | tf_op jit(solution)/shard_map/ppermute | solution.py:727

commit v15 on v14

--- a/solution.py
+++ b/solution.py
@@ -437,7 +437,7 @@
 def near_kernel(
     rows, shards, blocks, width, rank_ref, pair_ref, other_ref, pair_in_ref, middle_in_ref, spec_ref, weight_ref,
     rate_ref, front_ref, back_ref, trans_ref, featt_ref, slope_ref, conv_ref, corr_ref, ahead_ref, sums_ref, first_ref,
-    fields, fast, high_ref, low_ref, acc_ref,
+    near_ref, fields, fast, high_ref, low_ref, acc_ref,
 ):
     rank = rank_ref[0]
     inner = jnp.logical_and(rank > 0, rank < shards - 1)
@@ -456,8 +456,8 @@
     def _():
         acc_ref[...] = jnp.zeros_like(acc_ref)
         looped(
-            functools.partial(inner_strip, rows, shards), kinds + (None, None, None) + (ROWS,) * 4, blocks, width
-        )(*common, trans_ref, weight_ref, rate_ref, ahead_ref, sums_ref, high_ref, low_ref, acc_ref)
+            functools.partial(inner_strip, rows, shards), kinds + (None,) * 3 + (ROWS,) * 5, blocks, width
+        )(*common, trans_ref, weight_ref, rate_ref, ahead_ref, sums_ref, near_ref, high_ref, low_ref, acc_ref)
         first_ref[...] = exact_dot(
             featt_ref[:, : count * rows], acc_ref[...] * slope_ref[: count * rows, :]
         )
@@ -490,8 +490,8 @@
 
 def inner_strip(
     rows, shards, block, blocks, rank_ref, front_ref, back_ref, pair_ref, other_ref, pair_in_ref, middle_in_ref,
-    spec_ref, conv_ref, corr_ref, fields, fast, trans_ref, weight_ref, rate_ref, ahead_ref, sums_ref, high_ref, low_ref,
-    acc_ref,
+    spec_ref, conv_ref, corr_ref, fields, fast, trans_ref, weight_ref, rate_ref, ahead_ref, sums_ref, near_ref, high_ref,
+    low_ref, acc_ref,
 ):
     lower = rank_ref[0] == 1
     upper = jnp.where(lower, 0.0, 1.0).astype(f32)
@@ -513,6 +513,7 @@
         for index, value in enumerate(values):
             fast[index, re, :] = value[0].astype(bf16)
             fast[index, im, :] = value[1].astype(bf16)
+        near_ref[re, :], near_ref[im, :] = choose(lower, x1, c1)
         zero = conj_times(x0, c0)
         one = plus(conj_times(x1, c0), scaled(conj_times(x0, c1), upper))
         two = conj_times(x1, c1)
@@ -545,24 +546,26 @@
     return run
 
 
-def far_kernel(rows, block, blocks, rank_ref, far_ref, spec_ref, front_ref, back_ref, ahead_ref, part_ref):
+def far_kernel(
+    rows, block, blocks, rank_ref, far_ref, spec_ref, front_ref, back_ref, ahead_ref, part_ref, far_spec_ref
+):
     side = jnp.where(rank_ref[0] == 2, 1.0, -1.0).astype(f32)
     far = forward(front_ref, far_ref[...])
+    far_spec_ref[...] = far
     w3 = (spec_ref[0, :rows, :].astype(f32), spec_ref[0, rows:, :].astype(f32) * side)
     ahead = jnp.concatenate(times(w3, (far[:rows], far[rows:])), axis=0).astype(bf16)
     part_ref[...] = (ahead_ref[...] + backward(back_ref, ahead)).astype(bf16)
 
 
-def late_kernel(rows, block, blocks, rank_ref, far_ref, spec_ref, front_ref, back_ref, late_ref):
+def late_kernel(rows, block, blocks, rank_ref, far_ref, spec_ref, back_ref, late_ref):
     side = jnp.where(rank_ref[0] == 2, 1.0, -1.0).astype(f32)
-    far = forward(front_ref, far_ref[...])
     w2 = (spec_ref[0, :rows, :].astype(f32), spec_ref[0, rows:, :].astype(f32) * side)
-    late = jnp.concatenate(times(w2, (far[:rows], far[rows:])), axis=0).astype(bf16)
+    late = jnp.concatenate(times(w2, (far_ref[:rows, :], far_ref[rows:, :])), axis=0).astype(bf16)
     late_ref[...] = backward(back_ref, late)
 
 
 def last_kernel(
-    rows, shards, channels, block, blocks, after_ref, rank_ref, near_ref, far_ref, weight_ref, rate_ref, front_ref, back_ref,
+    rows, shards, channels, block, blocks, after_ref, rank_ref, near_ref, far_ref, weight_ref, rate_ref, back_ref,
     trans_ref, featt_ref, slope_ref, sums_ref, first_ref, bias_ref, in_ref, pay_ref, total_ref, acc_ref,
 ):
     del after_ref
@@ -579,9 +582,7 @@
     @pl.when(mine)
     def _():
         sign = jnp.where(lower, 1.0, -1.0).astype(f32)
-        near = forward(front_ref, near_ref[...])
-        far = forward(front_ref, far_ref[...])
-        three = conj_times((near[:rows], near[rows:]), (far[:rows], far[rows:]))
+        three = conj_times((near_ref[:rows, :], near_ref[rows:, :]), (far_ref[:rows, :], far_ref[rows:, :]))
         three = (three[0], three[1] * sign)
         half = rows // 2
         two = jnp.concatenate([three[1][:half], -three[1][half:], -three[0][:half], three[0][half:]], axis=0)
@@ -694,6 +695,8 @@
     double = 2 * rows
     width = min(512, channels)
     blocks = channels // width
+    wide = 2 * width if blocks % 4 == 0 else width
+    few = channels // wide
     rank = lax.axis_index("ctx").astype(jnp.int32).reshape(1)
     front, back = block_tables(rows)
     feats = feature_table(seq_len)
@@ -779,9 +782,10 @@
 
     edge, _ = lax.optimization_barrier((edge, slope))
     far = move(edge, [(0, 2), (shards - 1, shards - 3)])
-    conv, corr, ahead, sums, first = call(
+    conv, corr, ahead, sums, first, near_spec = call(
         functools.partial(near_kernel, rows, shards, blocks, width), "near_blocks", 20,
-        [block_f32] * 3 + [shape(hid_count, channels), shape(feat_count, hid_count)],
+        [block_f32] * 3
+        + [shape(hid_count, channels), shape(feat_count, hid_count), shape(double, channels)],
         [smem] + [vmem] * 12,
         scratch=[
             pltpu.VMEM((4, double, width), f32),
@@ -792,17 +796,17 @@
         ],
     )(rank, pair, other, pair_in, middle_in, spec, second_weight, rate_row, front, back, trans, featt, slope)
 
-    (part,) = call(
+    part, far_spec = call(
         only(
             True, shards, 0,
             looped(
                 functools.partial(far_kernel, rows),
-                (None, ROWS, (slice(3, 4), slice(None)), None, None, ROWS, ROWS),
-                blocks, width,
+                (None, ROWS, (slice(3, 4), slice(None)), None, None, ROWS, ROWS, ROWS),
+                few, wide,
             ),
         ),
         "far_block", 1,
-        [block_bf16],
+        [block_bf16, shape(double, channels)],
         [smem] + [vmem] * 5,
     )(rank, far, spec, front, back, ahead)
     (late,) = call(
@@ -810,14 +814,14 @@
             True, shards, 0,
             looped(
                 functools.partial(late_kernel, rows),
-                (None, ROWS, (slice(2, 3), slice(None)), None, None, ROWS),
-                blocks, width,
+                (None, ROWS, (slice(2, 3), slice(None)), None, ROWS),
+                few, wide,
             ),
         ),
         "late_block", 1,
         [block_f32],
-        [smem] + [vmem] * 4,
-    )(rank, far, spec, front, back)
+        [smem] + [vmem] * 3,
+    )(rank, far_spec, spec, back)
     part_come = move(part, outward)
 
     pay, first = call(
@@ -825,15 +829,15 @@
             True, shards, 1,
             looped(
                 functools.partial(last_kernel, rows, shards, channels),
-                (None, None, ROWS, ROWS, ROWS, ROWS, None, None, None, None, None, ROWS),
-                blocks, width,
+                (None, None, ROWS, ROWS, ROWS, ROWS, None, None, None, None, ROWS),
+                few, wide,
             ),
         ),
         "last_pair", 1,
         [shape(*pay_shape, dtype=bf16), shape(feat_count, hid_count)],
-        [anywhere, smem] + [vmem] * 13,
+        [anywhere, smem] + [vmem] * 12,
         scratch=[pltpu.VMEM((2 * rows, hid_count), f32)],
-    )(part, rank, pair_in, far, second_weight, rate_row, front, back, trans, featt, slope, sums, first, bias, come)
+    )(part, rank, near_spec, far_spec, second_weight, rate_row, back, trans, featt, slope, sums, first, bias, come)
     pay_come = move(pay, across + alone)
     group = lax.axis_size(("ch", "sub"))
     bit = 1

time: 61.8 us -> 61.1 us (0.989)
  waiting for transfers between devices: 21.9 us -> 20.9 us
    ppermute x9, waiting for transfers between devices: 18.5 us -> 17.5 us  [move(): return lax.ppermute(array, 'ctx', pairs)]
where the time goes in v15:
time: 61.1 us; the launch traced here: 60.8 us
  Pallas kernels  22 us (36%)
  waiting for transfers between devices  20.9 us (34%)
  starting transfers between devices  16.9 us (28%)
  between operations  0.98 us (2%)
    ppermute x9, waiting for transfers between devices, move(): return lax.ppermute(array, 'ctx', pairs)  17.5 us
    ppermute x9, starting transfers between devices, move(): return lax.ppermute(array, 'ctx', pairs)  15.3 us
    pallas_call x1, Pallas kernels, few_shards_body(): call(functools.partial(filters_kernel, rows, shards, blocks, width), 'fil...  6.51 us
    pallas_call x1, Pallas kernels, few_shards_body(): call(only(False, shards, 0, functools.partial(own_kernel, rows, shards, c...  6.2 us
    pallas_call x1, Pallas kernels, few_shards_body(): call(functools.partial(near_kernel, rows, shards, blocks, width), 'near_b...  3.82 us
    ppermute x2, waiting for transfers between devices, few_shards_body(): lax.ppermute(first, ('ch', 'sub'), [(i, i ^ bit) for i in range(group)])  3.38 us
    pallas_call x1, Pallas kernels, few_shards_body(): pl.pallas_call(products_kernel, grid=(rows // row_step,), in_specs=[smem]...  2.79 us
    pallas_call x2, Pallas kernels, gates(): call(only(inner, shards, len(before), functools.partial(gates_kernel, inn...  1.74 us
  transfers between devices with their start and end apart: 11, of which 6 were waited for; matrix products, arithmetic and copies ran while one was open for 0% of the time, Pallas kernels for 30%

profile of v15, /device:TPU:0, one launch (start us, length us, event | category | flops | bytes accessed | tf_op | source)
XLA Modules:
  0.0 60.8 jit_solution(12587791753535802288)
XLA Ops:
  0.6 2.8 %products.1 = (bf16[128,2048]{1,0:T(8,128)(2,1)}, bf16[128,2048]{1,0:T(8,128)(2,1)}, bf16[128,2048]{1,0:T(8,128)(2,1)}, f32[1,2048]{1,0:T(1,128)}) custom-call(s32[1]{0:T(128)} %bitcast.rank_ref.refs_0_.refs_1_.refs_3_, bf16[128,2048]{1,0:T(8,128)(2,1)} %refs_4_.6, bf16[128,2048]{1,0:T(8,128)(2,1)} %refs_5_.5, bf16[128,2048]{1,0:T(8,128)(2,1)} %refs_6_.2, ...), custom_call_target="tpu_custom_call" | custom-call | tf_op jit(solution)/shard_map/products/pallas_call | solution.py:742
  3.4 3.1 %collective-permute-start.1 = (bf16[128,2048]{1,0:T(8,128)(2,1)}, bf16[128,2048]{1,0:T(8,128)(2,1)S(1)}, u32[]{:S(2)}, u32[]{:S(2)}) collective-permute-start(bf16[128,2048]{1,0:T(8,128)(2,1)} %get-tuple-element.36.refs_3_.pair_ref), channel_id=1, source_target_pairs={{0,4},{12,8},{4,0},{8,12},{1,5},{13,9},{5,1},{9,13},{2,6},{14,10},... | collective-permute-start | bytes 1572872 | tf_op jit(solution)/shard_map/ppermute | solution.py:730
  6.5 0.7 %collective-permute-start.2 = (bf16[128,2048]{1,0:T(8,128)(2,1)}, bf16[128,2048]{1,0:T(8,128)(2,1)S(1)}, u32[]{:S(2)}, u32[]{:S(2)}) collective-permute-start(bf16[128,2048]{1,0:T(8,128)(2,1)} %get-tuple-element.37.refs_4_.other_ref), channel_id=1, source_target_pairs={{4,8},{8,4},{5,9},{9,5},{6,10},{10,6},{7,11},{11,7},{20,24},{24,20... | collective-permute-start | bytes 1572872 | tf_op jit(solution)/shard_map/ppermute | solution.py:730
  7.2 0.0 copy-start.5
  7.2 0.0 copy-start.6
  7.2 0.0 copy-start.9
  7.2 0.0 copy-start.13
  7.2 0.0 copy-start.14
  7.3 6.2 %own_pair.1 = bf16[64,2176]{1,0:T(8,128)(2,1)} custom-call(s32[1]{0:T(128)} %bitcast.rank_ref.refs_0_.refs_1_.refs_3_, f32[128,32]{1,0:T(8,128)} %constant.15.clone.refs_1_, f32[32,64]{1,0:T(8,128)} %first_ref.1, bf16[128,2048]{1,0:T(8,128)(2,1)} %get-tuple-element.36.refs_3_.pair_ref, bf16[128,2048]{1,0:T(8,128)(2,1)} %get-tuple-element.37.refs_4_.other_ref, ...), custom_call_target="tpu_custom_call" | custom-call | flops 2147483648 | bytes 262144 | tf_op jit(solution)/shard_map/own_pair/pallas_call | solution.py:759
  13.5 0.0 copy-done.5
  13.5 0.0 copy-done.6
  13.5 0.0 copy-done.9
  13.5 0.0 copy-done.13
  13.5 0.0 copy-done.14
  13.5 0.0 copy-start.15
  13.5 0.0 copy-start.16
  13.5 0.0 copy-start.4
  13.6 0.0 copy-start.7
  13.6 0.0 copy-start.11
  13.6 0.0 copy-start.12
  13.6 6.5 %filters.1 = (bf16[4,256,2048]{2,1,0:T(8,128)(2,1)S(1)}, bf16[128,512]{1,0:T(8,128)(2,1)S(1)}, f32[512,64]{1,0:T(8,128)S(1)}) custom-call(f32[512,32]{1,0:T(8,128)S(1)} %copy-done.14, f32[32,64]{1,0:T(8,128)S(1)} %copy-done.13, f32[64,2048]{1,0:T(8,128)S(1)} %copy-done.5, f32[1,2048]{1,0:T(1,128)S(1)} %bitcast.7, bf16[256,256]{1,0:T(8,128)(2,1)S(1)} %copy-done.6), custom_call_target="tpu_custom_call" | custom-call | flops 2147483648 | bytes 262144 | tf_op jit(solution)/shard_map/filters/pallas_call | solution.py:773
  20.1 0.0 copy-done.15
  20.1 1.3 %collective-permute-start = (bf16[128,2048]{1,0:T(8,128)(2,1)S(1)}, bf16[128,2048]{1,0:T(8,128)(2,1)S(1)}, u32[]{:S(2)}, u32[]{:S(2)}) collective-permute-start(bf16[128,2048]{1,0:T(8,128)(2,1)S(1)} %copy-done.15), channel_id=1, source_target_pairs={{0,8},{12,4},{1,9},{13,5},{2,10},{14,6},{3,11},{15,7},{16,24},{28,... | collective-permute-start | bytes 1572872 | tf_op jit(solution)/shard_map/ppermute | solution.py:730
  21.4 0.0 copy-done.16
  21.5 1.3 %collective-permute-start.4 = (bf16[64,2176]{1,0:T(8,128)(2,1)S(1)}, bf16[64,2176]{1,0:T(8,128)(2,1)S(1)}, u32[]{:S(2)}, u32[]{:S(2)}) collective-permute-start(bf16[64,2176]{1,0:T(8,128)(2,1)S(1)} %copy-done.16), channel_id=1, source_target_pairs={{0,4},{12,8},{1,5},{13,9},{2,6},{14,10},{3,7},{15,11},{16,20},{28,... | collective-permute-start | bytes 835592 | tf_op jit(solution)/shard_map/ppermute | solution.py:730
  22.8 0.0 collective-permute-done.1.pair_in_ref
  22.8 0.0 collective-permute-done.2.middle_in_ref
  22.8 0.0 copy-done.4
  22.8 0.0 copy-done.7
  22.8 0.0 copy-done.11
  22.8 0.0 copy-done.12
  22.8 3.8 %near_blocks.1 = (f32[128,2048]{1,0:T(8,128)S(1)}, f32[128,2048]{1,0:T(8,128)S(1)}, f32[128,2048]{1,0:T(8,128)S(1)}, f32[64,2048]{1,0:T(8,128)S(1)}, f32[32,64]{1,0:T(8,128)S(1)}, /*index=5*/f32[256,2048]{1,0:T(8,128)S(1)}) custom-call(s32[1]{0:T(128)} %bitcast.rank_ref.refs_0_.refs_1_.refs_3_, bf16[128,2048]{1,0:T(8,128)(2,1)S(1)} %copy-done.11, ...), custom_call_target="tpu_custom_call" | custom-call | flops 5368709120 | bytes 262144 | tf_op jit(solution)/shard_map/near_blocks/pallas_call | solution.py:785
  26.7 7.1 %collective-permute-done.refs_1_ = bf16[128,2048]{1,0:T(8,128)(2,1)S(1)} collective-permute-done((bf16[128,2048]{1,0:T(8,128)(2,1)S(1)}, bf16[128,2048]{1,0:T(8,128)(2,1)S(1)}, u32[]{:S(2)}, u32[]{:S(2)}) %collective-permute-start) | collective-permute-done | bytes 524320 | tf_op jit(solution)/shard_map/ppermute | solution.py:730
  33.7 0.0 copy-start.10
  33.7 1.4 %collective-permute-start.3 = (bf16[128,2048]{1,0:T(8,128)(2,1)S(1)}, bf16[128,2048]{1,0:T(8,128)(2,1)S(1)}, u32[]{:S(2)}, u32[]{:S(2)}) collective-permute-start(bf16[128,2048]{1,0:T(8,128)(2,1)S(1)} %get-tuple-element.45.refs_0_), channel_id=1, source_target_pairs={{4,0},{8,12},{5,1},{9,13},{6,2},{10,14},{7,3},{11,15},{20,16},{24,... | collective-permute-start | bytes 1572872 | tf_op jit(solution)/shard_map/ppermute | solution.py:730
  35.1 3.4 %collective-permute-done.4.refs_13_ = bf16[64,2176]{1,0:T(8,128)(2,1)S(1)} collective-permute-done((bf16[64,2176]{1,0:T(8,128)(2,1)S(1)}, bf16[64,2176]{1,0:T(8,128)(2,1)S(1)}, u32[]{:S(2)}, u32[]{:S(2)}) %collective-permute-start.4) | collective-permute-done | bytes 278560 | tf_op jit(solution)/shard_map/ppermute | solution.py:730
  38.5 0.0 copy-done.10
  38.5 0.7 %collective-permute-start.7 = (bf16[64,2176]{1,0:T(8,128)(2,1)S(1)}, bf16[64,2176]{1,0:T(8,128)(2,1)S(1)}, u32[]{:S(2)}, u32[]{:S(2)}) collective-permute-start(bf16[64,2176]{1,0:T(8,128)(2,1)S(1)} %get-tuple-element.51.own_ref), channel_id=1, source_target_pairs={{4,8},{8,4},{0,0},{12,12},{5,9},{9,5},{1,1},{13,13},{6,10},{10,6},... | collective-permute-start | bytes 835592 | tf_op jit(solution)/shard_map/ppermute | solution.py:730
  39.2 0.1 collective-permute-start.5
  39.3 1.2 %collective-permute-done.5 = f32[32,64]{1,0:T(8,128)S(1)} collective-permute-done((f32[32,64]{1,0:T(8,128)S(1)}, f32[32,64]{1,0:T(8,128)S(1)}, u32[]{:S(2)}, u32[]{:S(2)}) %collective-permute-start.5) | collective-permute-done | bytes 8224 | tf_op jit(solution)/shard_map/ppermute | solution.py:845
  40.5 1.5 %collective-permute-start.6 = (f32[32,64]{1,0:T(8,128)S(1)}, f32[32,64]{1,0:T(8,128)S(1)}, u32[]{:S(2)}, u32[]{:S(2)}) collective-permute-start(f32[32,64]{1,0:T(8,128)S(1)} %add.9), channel_id=1, source_target_pairs={{0,2},{1,3},{2,0},{3,1},{4,6},{5,7},{6,4},{7,5},{8,10},{9,11},{10,... | collective-permute-start | bytes 24584 | tf_op jit(solution)/shard_map/ppermute | solution.py:845
  42.0 0.0 copy-start
  42.0 0.0 copy-start.1
  42.0 0.0 copy-start.2
  42.0 0.0 copy-start.3
  42.0 0.0 copy-start.8
  42.0 2.2 %collective-permute-done.6 = f32[32,64]{1,0:T(8,128)S(1)} collective-permute-done((f32[32,64]{1,0:T(8,128)S(1)}, f32[32,64]{1,0:T(8,128)S(1)}, u32[]{:S(2)}, u32[]{:S(2)}) %collective-permute-start.6) | collective-permute-done | bytes 8224 | tf_op jit(solution)/shard_map/ppermute | solution.py:845
  44.2 0.0 collective-permute-done.7.come_ref
  44.2 5.4 %collective-permute-done.3.part_ref.refs_10_.refs_12_ = bf16[128,2048]{1,0:T(8,128)(2,1)S(1)} collective-permute-done((bf16[128,2048]{1,0:T(8,128)(2,1)S(1)}, bf16[128,2048]{1,0:T(8,128)(2,1)S(1)}, u32[]{:S(2)}, u32[]{:S(2)}) %collective-permute-start.3) | collective-permute-done | bytes 524320 | tf_op jit(solution)/shard_map/ppermute | solution.py:730
  49.6 0.1 total.1.refs_0_.own_ref
  49.7 2.7 %collective-permute-start.8 = (bf16[64,2176]{1,0:T(8,128)(2,1)S(1)}, bf16[64,2176]{1,0:T(8,128)(2,1)S(1)}, u32[]{:S(2)}, u32[]{:S(2)}) collective-permute-start(bf16[64,2176]{1,0:T(8,128)(2,1)S(1)} %total.1.refs_0_.own_ref), channel_id=1, source_target_pairs={{0,4},{12,8},{4,0},{8,12},{1,5},{13,9},{5,1},{9,13},{2,6},{14,10},... | collective-permute-start | bytes 835592 | tf_op jit(solution)/shard_map/ppermute | solution.py:730
  52.4 0.0 copy-done
  52.4 0.0 copy-done.1
  52.4 0.0 copy-done.2
  52.4 0.0 copy-done.3
  52.4 0.0 copy-done.8
  52.4 1.6 %gates.2 = (bf16[128,2048]{1,0:T(8,128)(2,1)}, bf16[128,2048]{1,0:T(8,128)(2,1)}, bf16[128,2048]{1,0:T(8,128)(2,1)}) custom-call(bf16[64,2176]{1,0:T(8,128)(2,1)S(1)} %total.1.refs_0_.own_ref, s32[1]{0:T(128)} %bitcast.rank_ref.refs_0_.refs_1_.refs_3_, bf16[128,2048]{1,0:T(8,128)(2,1)S(1)} %copy-done, bf16[128,2048]{1,0:T(8,128)(2,1)S(1)} %copy-done.1, ...), custom_call_target="tpu_custom_call" | custom-call | bytes 262144 | tf_op jit(solution)/shard_map/gates/pallas_call | solution.py:856
  54.1 0.7 %collective-permute-start.9 = (f32[32,64]{1,0:T(8,128)S(1)}, f32[32,64]{1,0:T(8,128)S(1)}, u32[]{:S(2)}, u32[]{:S(2)}) collective-permute-start(f32[32,64]{1,0:T(8,128)S(1)} %add.10.first_ref), channel_id=1, source_target_pairs={{4,8},{8,4},{0,0},{12,12},{5,9},{9,5},{1,1},{13,13},{6,10},{10,6},... | collective-permute-start | bytes 24584 | tf_op jit(solution)/shard_map/ppermute | solution.py:730
  54.7 0.0 collective-permute-done.9
  54.8 3.5 %collective-permute-start.10 = (f32[32,64]{1,0:T(8,128)S(1)}, f32[32,64]{1,0:T(8,128)S(1)}, u32[]{:S(2)}, u32[]{:S(2)}) collective-permute-start(f32[32,64]{1,0:T(8,128)S(1)} %add.11.first_ref), channel_id=1, source_target_pairs={{0,4},{12,8},{4,0},{8,12},{1,5},{13,9},{5,1},{9,13},{2,6},{14,10},... | collective-permute-start | bytes 24584 | tf_op jit(solution)/shard_map/ppermute | solution.py:730
  58.2 0.1 gates.3
  58.4 1.6 %collective-permute-done.10.first_come_ref = f32[32,64]{1,0:T(8,128)S(1)} collective-permute-done((f32[32,64]{1,0:T(8,128)S(1)}, f32[32,64]{1,0:T(8,128)S(1)}, u32[]{:S(2)}, u32[]{:S(2)}) %collective-permute-start.10) | collective-permute-done | bytes 8224 | tf_op jit(solution)/shard_map/ppermute | solution.py:730
  60.0 0.0 collective-permute-done.8.come_ref
  60.0 0.9 %finish.1 = (f32[64,2048]{1,0:T(8,128)}, f32[32,64]{1,0:T(8,128)}, f32[1,2048]{1,0:T(1,128)}) custom-call(s32[1]{0:T(128)} %bitcast.rank_ref.refs_0_.refs_1_.refs_3_, bf16[64,2176]{1,0:T(8,128)(2,1)S(1)} %total.1.refs_0_.own_ref, bf16[64,2176]{1,0:T(8,128)(2,1)S(1)} %collective-permute-done.8.come_ref, f32[32,64]{1,0:T(8,128)S(1)} %add.11.first_ref, ...), custom_call_target="tpu_custom_call" | custom-call | bytes 262144 | tf_op jit(solution)/shard_map/finish/pallas_call | solution.py:876
  (6 shorter events, 0.0 us)
Async XLA Ops:
  3.4 19.3 %collective-permute-start.1 = (bf16[128,2048]{1,0:T(8,128)(2,1)}, bf16[128,2048]{1,0:T(8,128)(2,1)S(1)}, u32[]{:S(2)}, u32[]{:S(2)}) collective-permute-start(bf16[128,2048]{1,0:T(8,128)(2,1)} %get-tuple-element.36.refs_3_.pair_ref), channel_id=1, source_target_pairs={{0,4},{12,8},{4,0},{8,12},{1,5},{13,9},{5,1},{9,13},{2,6},{14,10},... | collective-permute-start | bytes 1572872 | tf_op jit(solution)/shard_map/ppermute | solution.py:730
  6.5 16.3 %collective-permute-start.2 = (bf16[128,2048]{1,0:T(8,128)(2,1)}, bf16[128,2048]{1,0:T(8,128)(2,1)S(1)}, u32[]{:S(2)}, u32[]{:S(2)}) collective-permute-start(bf16[128,2048]{1,0:T(8,128)(2,1)} %get-tuple-element.37.refs_4_.other_ref), channel_id=1, source_target_pairs={{4,8},{8,4},{5,9},{9,5},{6,10},{10,6},{7,11},{11,7},{20,24},{24,20... | collective-permute-start | bytes 1572872 | tf_op jit(solution)/shard_map/ppermute | solution.py:730
  7.2 6.3 %copy-start.5 = (f32[64,2048]{1,0:T(8,128)S(1)}, f32[64,2048]{1,0:T(8,128)}, u32[]{:S(2)}) copy-start(f32[64,2048]{1,0:T(8,128)} %refs_4_.4) | copy-start | bytes 1572868
  7.2 6.3 %copy-start.6 = (bf16[256,256]{1,0:T(8,128)(2,1)S(1)}, bf16[256,256]{1,0:T(8,128)(2,1)}, u32[]{:S(2)}) copy-start(bf16[256,256]{1,0:T(8,128)(2,1)} %constant.16.clone.refs_7_.front_ref.refs_3_) | copy-start | bytes 393220
  7.2 6.3 %copy-start.9 = (f32[2048]{0:T(1024)S(1)}, f32[2048]{0:T(1024)}, u32[]{:S(2)}) copy-start(f32[2048]{0:T(1024)} %param.20) | copy-start | bytes 24580
  7.2 6.3 %copy-start.13 = (f32[32,64]{1,0:T(8,128)S(1)}, f32[32,64]{1,0:T(8,128)}, u32[]{:S(2)}) copy-start(f32[32,64]{1,0:T(8,128)} %first_ref.1) | copy-start | bytes 24580
  7.2 6.3 %copy-start.14 = (f32[512,32]{1,0:T(8,128)S(1)}, f32[512,32]{1,0:T(8,128)}, u32[]{:S(2)}) copy-start(f32[512,32]{1,0:T(8,128)} %constant.19.clone.feats_ref) | copy-start | bytes 196612
  13.5 6.6 %copy-start.15 = (bf16[128,2048]{1,0:T(8,128)(2,1)S(1)}, bf16[128,2048]{1,0:T(8,128)(2,1)}, u32[]{:S(2)}) copy-start(bf16[128,2048]{1,0:T(8,128)(2,1)} %get-tuple-element.41) | copy-start | bytes 1572868
  13.5 7.9 %copy-start.16 = (bf16[64,2176]{1,0:T(8,128)(2,1)S(1)}, bf16[64,2176]{1,0:T(8,128)(2,1)}, u32[]{:S(2)}) copy-start(bf16[64,2176]{1,0:T(8,128)(2,1)} %own_pair.1) | copy-start | bytes 835588
  13.5 9.3 %copy-start.4 = (bf16[256,256]{1,0:T(8,128)(2,1)S(1)}, bf16[256,256]{1,0:T(8,128)(2,1)}, u32[]{:S(2)}) copy-start(bf16[256,256]{1,0:T(8,128)(2,1)} %constant.17.clone.refs_8_.back_ref.refs_4_.refs_6_.refs_3_) | copy-start | bytes 393220
  13.6 9.2 %copy-start.7 = (f32[32,512]{1,0:T(8,128)S(1)}, f32[32,512]{1,0:T(8,128)}, u32[]{:S(2)}) copy-start(f32[32,512]{1,0:T(8,128)} %constant.18.clone.refs_9_.featt_ref.refs_8_) | copy-start | bytes 196612
  13.6 9.2 %copy-start.11 = (bf16[128,2048]{1,0:T(8,128)(2,1)S(1)}, bf16[128,2048]{1,0:T(8,128)(2,1)}, u32[]{:S(2)}) copy-start(bf16[128,2048]{1,0:T(8,128)(2,1)} %get-tuple-element.36.refs_3_.pair_ref) | copy-start | bytes 1572868
  13.6 9.2 %copy-start.12 = (bf16[128,2048]{1,0:T(8,128)(2,1)S(1)}, bf16[128,2048]{1,0:T(8,128)(2,1)}, u32[]{:S(2)}) copy-start(bf16[128,2048]{1,0:T(8,128)(2,1)} %get-tuple-element.37.refs_4_.other_ref) | copy-start | bytes 1572868
  20.1 13.6 %collective-permute-start = (bf16[128,2048]{1,0:T(8,128)(2,1)S(1)}, bf16[128,2048]{1,0:T(8,128)(2,1)S(1)}, u32[]{:S(2)}, u32[]{:S(2)}) collective-permute-start(bf16[128,2048]{1,0:T(8,128)(2,1)S(1)} %copy-done.15), channel_id=1, source_target_pairs={{0,8},{12,4},{1,9},{13,5},{2,10},{14,6},{3,11},{15,7},{16,24},{28,... | collective-permute-start | bytes 1572872 | tf_op jit(solution)/shard_map/ppermute | solution.py:730
  21.5 17.1 %collective-permute-start.4 = (bf16[64,2176]{1,0:T(8,128)(2,1)S(1)}, bf16[64,2176]{1,0:T(8,128)(2,1)S(1)}, u32[]{:S(2)}, u32[]{:S(2)}) collective-permute-start(bf16[64,2176]{1,0:T(8,128)(2,1)S(1)} %copy-done.16), channel_id=1, source_target_pairs={{0,4},{12,8},{1,5},{13,9},{2,6},{14,10},{3,7},{15,11},{16,20},{28,... | collective-permute-start | bytes 835592 | tf_op jit(solution)/shard_map/ppermute | solution.py:730
  33.7 4.8 %copy-start.10 = (f32[1,2048]{1,0:T(1,128)S(1)}, f32[1,2048]{1,0:T(1,128)}, u32[]{:S(2)}) copy-start(f32[1,2048]{1,0:T(1,128)} %get-tuple-element.38.refs_10_.refs_12_) | copy-start | bytes 24580
  33.7 15.9 %collective-permute-start.3 = (bf16[128,2048]{1,0:T(8,128)(2,1)S(1)}, bf16[128,2048]{1,0:T(8,128)(2,1)S(1)}, u32[]{:S(2)}, u32[]{:S(2)}) collective-permute-start(bf16[128,2048]{1,0:T(8,128)(2,1)S(1)} %get-tuple-element.45.refs_0_), channel_id=1, source_target_pairs={{4,0},{8,12},{5,1},{9,13},{6,2},{10,14},{7,3},{11,15},{20,16},{24,... | collective-permute-start | bytes 1572872 | tf_op jit(solution)/shard_map/ppermute | solution.py:730
  38.5 5.7 %collective-permute-start.7 = (bf16[64,2176]{1,0:T(8,128)(2,1)S(1)}, bf16[64,2176]{1,0:T(8,128)(2,1)S(1)}, u32[]{:S(2)}, u32[]{:S(2)}) collective-permute-start(bf16[64,2176]{1,0:T(8,128)(2,1)S(1)} %get-tuple-element.51.own_ref), channel_id=1, source_target_pairs={{4,8},{8,4},{0,0},{12,12},{5,9},{9,5},{1,1},{13,13},{6,10},{10,6},... | collective-permute-start | bytes 835592 | tf_op jit(solution)/shard_map/ppermute | solution.py:730
  39.2 1.2 %collective-permute-start.5 = (f32[32,64]{1,0:T(8,128)S(1)}, f32[32,64]{1,0:T(8,128)S(1)}, u32[]{:S(2)}, u32[]{:S(2)}) collective-permute-start(f32[32,64]{1,0:T(8,128)S(1)} %get-tuple-element.50), channel_id=1, source_target_pairs={{0,1},{1,0},{2,3},{3,2},{4,5},{5,4},{6,7},{7,6},{8,9},{9,8},{10,11... | collective-permute-start | bytes 24584 | tf_op jit(solution)/shard_map/ppermute | solution.py:845
  40.5 3.7 %collective-permute-start.6 = (f32[32,64]{1,0:T(8,128)S(1)}, f32[32,64]{1,0:T(8,128)S(1)}, u32[]{:S(2)}, u32[]{:S(2)}) collective-permute-start(f32[32,64]{1,0:T(8,128)S(1)} %add.9), channel_id=1, source_target_pairs={{0,2},{1,3},{2,0},{3,1},{4,6},{5,7},{6,4},{7,5},{8,10},{9,11},{10,... | collective-permute-start | bytes 24584 | tf_op jit(solution)/shard_map/ppermute | solution.py:845
  42.0 10.4 %copy-start = (bf16[128,2048]{1,0:T(8,128)(2,1)S(1)}, bf16[128,2048]{1,0:T(8,128)(2,1)}, u32[]{:S(2)}) copy-start(bf16[128,2048]{1,0:T(8,128)(2,1)} %refs_4_.6) | copy-start | bytes 1572868
  42.0 10.4 %copy-start.1 = (bf16[128,2048]{1,0:T(8,128)(2,1)S(1)}, bf16[128,2048]{1,0:T(8,128)(2,1)}, u32[]{:S(2)}) copy-start(bf16[128,2048]{1,0:T(8,128)(2,1)} %refs_5_.5) | copy-start | bytes 1572868
  42.0 10.4 %copy-start.2 = (bf16[128,2048]{1,0:T(8,128)(2,1)S(1)}, bf16[128,2048]{1,0:T(8,128)(2,1)}, u32[]{:S(2)}) copy-start(bf16[128,2048]{1,0:T(8,128)(2,1)} %refs_6_.2) | copy-start | bytes 1572868
  42.0 10.4 %copy-start.3 = (bf16[128,2048]{1,0:T(8,128)(2,1)S(1)}, bf16[128,2048]{1,0:T(8,128)(2,1)}, u32[]{:S(2)}) copy-start(bf16[128,2048]{1,0:T(8,128)(2,1)} %refs_7_.2) | copy-start | bytes 1572868
  42.0 10.4 %copy-start.8 = (f32[2048]{0:T(1024)S(1)}, f32[2048]{0:T(1024)}, u32[]{:S(2)}) copy-start(f32[2048]{0:T(1024)} %param.19) | copy-start | bytes 24580
  49.7 10.2 %collective-permute-start.8 = (bf16[64,2176]{1,0:T(8,128)(2,1)S(1)}, bf16[64,2176]{1,0:T(8,128)(2,1)S(1)}, u32[]{:S(2)}, u32[]{:S(2)}) collective-permute-start(bf16[64,2176]{1,0:T(8,128)(2,1)S(1)} %total.1.refs_0_.own_ref), channel_id=1, source_target_pairs={{0,4},{12,8},{4,0},{8,12},{1,5},{13,9},{5,1},{9,13},{2,6},{14,10},... | collective-permute-start | bytes 835592 | tf_op jit(solution)/shard_map/ppermute | solution.py:730
  54.1 0.7 %collective-permute-start.9 = (f32[32,64]{1,0:T(8,128)S(1)}, f32[32,64]{1,0:T(8,128)S(1)}, u32[]{:S(2)}, u32[]{:S(2)}) collective-permute-start(f32[32,64]{1,0:T(8,128)S(1)} %add.10.first_ref), channel_id=1, source_target_pairs={{4,8},{8,4},{0,0},{12,12},{5,9},{9,5},{1,1},{13,13},{6,10},{10,6},... | collective-permute-start | bytes 24584 | tf_op jit(solution)/shard_map/ppermute | solution.py:730
  54.8 5.2 %collective-permute-start.10 = (f32[32,64]{1,0:T(8,128)S(1)}, f32[32,64]{1,0:T(8,128)S(1)}, u32[]{:S(2)}, u32[]{:S(2)}) collective-permute-start(f32[32,64]{1,0:T(8,128)S(1)} %add.11.first_ref), channel_id=1, source_target_pairs={{0,4},{12,8},{4,0},{8,12},{1,5},{13,9},{5,1},{9,13},{2,6},{14,10},... | collective-permute-start | bytes 24584 | tf_op jit(solution)/shard_map/ppermute | solution.py:730

commit v16 on v15

--- a/solution.py
+++ b/solution.py
@@ -782,6 +782,8 @@
 
     edge, _ = lax.optimization_barrier((edge, slope))
     far = move(edge, [(0, 2), (shards - 1, shards - 3)])
+    pair_in, come = lax.optimization_barrier((pair_in, come))
+
     conv, corr, ahead, sums, first, near_spec = call(
         functools.partial(near_kernel, rows, shards, blocks, width), "near_blocks", 20,
         [block_f32] * 3

time: 61.1 us -> 63.1 us (1.033)
  waiting for transfers between devices: 20.9 us -> 23.4 us
    ppermute x9, waiting for transfers between devices: 17.5 us -> 20 us  [move(): return lax.ppermute(array, 'ctx', pairs)]
  transfers between devices with their start and end apart: 11 -> 11, of which waited for: 6 -> 6; matrix products, arithmetic and copies ran while one was open for 0% -> 0% of each run, Pallas kernels for 30% -> 29%
where the time goes in v16:
time: 63.1 us; the launch traced here: 62.8 us
  waiting for transfers between devices  23.4 us (37%)
  Pallas kernels  22 us (35%)
  starting transfers between devices  16.4 us (26%)
  between operations  0.96 us (2%)
    ppermute x9, waiting for transfers between devices, move(): return lax.ppermute(array, 'ctx', pairs)  20 us
    ppermute x9, starting transfers between devices, move(): return lax.ppermute(array, 'ctx', pairs)  14.8 us
    pallas_call x1, Pallas kernels, few_shards_body(): call(functools.partial(filters_kernel, rows, shards, blocks, width), 'fil...  6.52 us
    pallas_call x1, Pallas kernels, few_shards_body(): call(only(False, shards, 0, functools.partial(own_kernel, rows, shards, c...  6.2 us
    pallas_call x1, Pallas kernels, few_shards_body(): call(functools.partial(near_kernel, rows, shards, blocks, width), 'near_b...  3.82 us
    ppermute x2, waiting for transfers between devices, few_shards_body(): lax.ppermute(first, ('ch', 'sub'), [(i, i ^ bit) for i in range(group)])  3.39 us
    pallas_call x1, Pallas kernels, few_shards_body(): pl.pallas_call(products_kernel, grid=(rows // row_step,), in_specs=[smem]...  2.79 us
    pallas_call x2, Pallas kernels, gates(): call(only(inner, shards, len(before), functools.partial(gates_kernel, inn...  1.74 us
  transfers between devices with their start and end apart: 11, of which 6 were waited for; matrix products, arithmetic and copies ran while one was open for 0% of the time, Pallas kernels for 29%

profile of v16, /device:TPU:0, one launch (start us, length us, event | category | flops | bytes accessed | tf_op | source)
XLA Modules:
  0.0 62.8 jit_solution(6741642741356276474)
XLA Ops:
  0.6 2.8 %products.1 = (bf16[128,2048]{1,0:T(8,128)(2,1)}, bf16[128,2048]{1,0:T(8,128)(2,1)}, bf16[128,2048]{1,0:T(8,128)(2,1)}, f32[1,2048]{1,0:T(1,128)}) custom-call(s32[1]{0:T(128)} %bitcast.rank_ref.refs_0_.refs_1_.refs_3_, bf16[128,2048]{1,0:T(8,128)(2,1)} %refs_4_.6, bf16[128,2048]{1,0:T(8,128)(2,1)} %refs_5_.5, bf16[128,2048]{1,0:T(8,128)(2,1)} %refs_6_.2, ...), custom_call_target="tpu_custom_call" | custom-call | tf_op jit(solution)/shard_map/products/pallas_call | solution.py:742
  3.4 3.1 %collective-permute-start.1 = (bf16[128,2048]{1,0:T(8,128)(2,1)}, bf16[128,2048]{1,0:T(8,128)(2,1)S(1)}, u32[]{:S(2)}, u32[]{:S(2)}) collective-permute-start(bf16[128,2048]{1,0:T(8,128)(2,1)} %get-tuple-element.38.refs_3_.pair_ref), channel_id=1, source_target_pairs={{0,4},{12,8},{4,0},{8,12},{1,5},{13,9},{5,1},{9,13},{2,6},{14,10},... | collective-permute-start | bytes 1572872 | tf_op jit(solution)/shard_map/ppermute | solution.py:730
  6.5 0.7 %collective-permute-start.3 = (bf16[128,2048]{1,0:T(8,128)(2,1)}, bf16[128,2048]{1,0:T(8,128)(2,1)S(1)}, u32[]{:S(2)}, u32[]{:S(2)}) collective-permute-start(bf16[128,2048]{1,0:T(8,128)(2,1)} %get-tuple-element.39.refs_4_.other_ref), channel_id=1, source_target_pairs={{4,8},{8,4},{5,9},{9,5},{6,10},{10,6},{7,11},{11,7},{20,24},{24,20... | collective-permute-start | bytes 1572872 | tf_op jit(solution)/shard_map/ppermute | solution.py:730
  7.2 0.0 copy-start.5
  7.2 0.0 copy-start.6
  7.2 0.0 copy-start.9
  7.2 0.0 copy-start.13
  7.2 0.0 copy-start.14
  7.3 6.2 %own_pair.1 = bf16[64,2176]{1,0:T(8,128)(2,1)} custom-call(s32[1]{0:T(128)} %bitcast.rank_ref.refs_0_.refs_1_.refs_3_, f32[128,32]{1,0:T(8,128)} %constant.15.clone.refs_1_, f32[32,64]{1,0:T(8,128)} %first_ref.1, bf16[128,2048]{1,0:T(8,128)(2,1)} %get-tuple-element.38.refs_3_.pair_ref, bf16[128,2048]{1,0:T(8,128)(2,1)} %get-tuple-element.39.refs_4_.other_ref, ...), custom_call_target="tpu_custom_call" | custom-call | flops 2147483648 | bytes 262144 | tf_op jit(solution)/shard_map/own_pair/pallas_call | solution.py:759
  13.5 0.0 copy-start.15
  13.5 0.0 copy-start.4
  13.5 0.0 copy-start.7
  13.5 0.0 copy-start.11
  13.5 0.0 copy-start.12
  13.5 1.4 %collective-permute-start.2 = (bf16[64,2176]{1,0:T(8,128)(2,1)}, bf16[64,2176]{1,0:T(8,128)(2,1)S(1)}, u32[]{:S(2)}, u32[]{:S(2)}) collective-permute-start(bf16[64,2176]{1,0:T(8,128)(2,1)} %own_pair.1), channel_id=1, source_target_pairs={{0,4},{12,8},{1,5},{13,9},{2,6},{14,10},{3,7},{15,11},{16,20},{28,... | collective-permute-start | bytes 835592 | tf_op jit(solution)/shard_map/ppermute | solution.py:730
  15.0 0.0 copy-done.5
  15.0 0.0 copy-done.6
  15.0 0.0 copy-done.9
  15.0 0.0 copy-done.13
  15.0 0.0 copy-done.14
  15.0 6.5 %filters.1 = (bf16[4,256,2048]{2,1,0:T(8,128)(2,1)S(1)}, bf16[128,512]{1,0:T(8,128)(2,1)S(1)}, f32[512,64]{1,0:T(8,128)S(1)}) custom-call(f32[512,32]{1,0:T(8,128)S(1)} %copy-done.14, f32[32,64]{1,0:T(8,128)S(1)} %copy-done.13, f32[64,2048]{1,0:T(8,128)S(1)} %copy-done.5, f32[1,2048]{1,0:T(1,128)S(1)} %bitcast.7, bf16[256,256]{1,0:T(8,128)(2,1)S(1)} %copy-done.6), custom_call_target="tpu_custom_call" | custom-call | flops 2147483648 | bytes 262144 | tf_op jit(solution)/shard_map/filters/pallas_call | solution.py:773
  21.6 0.0 copy-done.15
  21.6 1.3 %collective-permute-start = (bf16[128,2048]{1,0:T(8,128)(2,1)S(1)}, bf16[128,2048]{1,0:T(8,128)(2,1)S(1)}, u32[]{:S(2)}, u32[]{:S(2)}) collective-permute-start(bf16[128,2048]{1,0:T(8,128)(2,1)S(1)} %copy-done.15), channel_id=1, source_target_pairs={{0,8},{12,4},{1,9},{13,5},{2,10},{14,6},{3,11},{15,7},{16,24},{28,... | collective-permute-start | bytes 1572872 | tf_op jit(solution)/shard_map/ppermute | solution.py:730
  22.9 2.1 %collective-permute-done.2.refs_13_ = bf16[64,2176]{1,0:T(8,128)(2,1)S(1)} collective-permute-done((bf16[64,2176]{1,0:T(8,128)(2,1)}, bf16[64,2176]{1,0:T(8,128)(2,1)S(1)}, u32[]{:S(2)}, u32[]{:S(2)}) %collective-permute-start.2) | collective-permute-done | bytes 278560 | tf_op jit(solution)/shard_map/ppermute | solution.py:730
  25.0 0.0 collective-permute-done.1.pair_in_ref
  25.0 0.0 collective-permute-done.3.middle_in_ref
  25.0 0.0 copy-done.4
  25.0 0.0 copy-done.7
  25.0 0.0 copy-done.11
  25.0 0.0 copy-done.12
  25.0 3.8 %near_blocks.1 = (f32[128,2048]{1,0:T(8,128)S(1)}, f32[128,2048]{1,0:T(8,128)S(1)}, f32[128,2048]{1,0:T(8,128)S(1)}, f32[64,2048]{1,0:T(8,128)S(1)}, f32[32,64]{1,0:T(8,128)S(1)}, /*index=5*/f32[256,2048]{1,0:T(8,128)S(1)}) custom-call(s32[1]{0:T(128)} %bitcast.rank_ref.refs_0_.refs_1_.refs_3_, bf16[128,2048]{1,0:T(8,128)(2,1)S(1)} %copy-done.11, ...), custom_call_target="tpu_custom_call" | custom-call | flops 5368709120 | bytes 262144 | tf_op jit(solution)/shard_map/near_blocks/pallas_call | solution.py:787
  28.9 6.2 %collective-permute-done.refs_1_ = bf16[128,2048]{1,0:T(8,128)(2,1)S(1)} collective-permute-done((bf16[128,2048]{1,0:T(8,128)(2,1)S(1)}, bf16[128,2048]{1,0:T(8,128)(2,1)S(1)}, u32[]{:S(2)}, u32[]{:S(2)}) %collective-permute-start) | collective-permute-done | bytes 524320 | tf_op jit(solution)/shard_map/ppermute | solution.py:730
  35.1 0.0 copy-start.10
  35.1 1.4 %collective-permute-start.4 = (bf16[128,2048]{1,0:T(8,128)(2,1)S(1)}, bf16[128,2048]{1,0:T(8,128)(2,1)S(1)}, u32[]{:S(2)}, u32[]{:S(2)}) collective-permute-start(bf16[128,2048]{1,0:T(8,128)(2,1)S(1)} %get-tuple-element.48.refs_0_), channel_id=1, source_target_pairs={{4,0},{8,12},{5,1},{9,13},{6,2},{10,14},{7,3},{11,15},{20,16},{24,... | collective-permute-start | bytes 1572872 | tf_op jit(solution)/shard_map/ppermute | solution.py:730
  36.5 0.0 copy-done.10
  36.6 0.7 %collective-permute-start.7 = (bf16[64,2176]{1,0:T(8,128)(2,1)S(1)}, bf16[64,2176]{1,0:T(8,128)(2,1)S(1)}, u32[]{:S(2)}, u32[]{:S(2)}) collective-permute-start(bf16[64,2176]{1,0:T(8,128)(2,1)S(1)} %get-tuple-element.55.own_ref), channel_id=1, source_target_pairs={{4,8},{8,4},{0,0},{12,12},{5,9},{9,5},{1,1},{13,13},{6,10},{10,6},... | collective-permute-start | bytes 835592 | tf_op jit(solution)/shard_map/ppermute | solution.py:730
  37.2 0.1 collective-permute-start.5
  37.3 1.2 %collective-permute-done.5 = f32[32,64]{1,0:T(8,128)S(1)} collective-permute-done((f32[32,64]{1,0:T(8,128)S(1)}, f32[32,64]{1,0:T(8,128)S(1)}, u32[]{:S(2)}, u32[]{:S(2)}) %collective-permute-start.5) | collective-permute-done | bytes 8224 | tf_op jit(solution)/shard_map/ppermute | solution.py:847
  38.5 1.5 %collective-permute-start.6 = (f32[32,64]{1,0:T(8,128)S(1)}, f32[32,64]{1,0:T(8,128)S(1)}, u32[]{:S(2)}, u32[]{:S(2)}) collective-permute-start(f32[32,64]{1,0:T(8,128)S(1)} %add.9), channel_id=1, source_target_pairs={{0,2},{1,3},{2,0},{3,1},{4,6},{5,7},{6,4},{7,5},{8,10},{9,11},{10,... | collective-permute-start | bytes 24584 | tf_op jit(solution)/shard_map/ppermute | solution.py:847
  40.0 0.0 copy-start
  40.0 0.0 copy-start.1
  40.0 0.0 copy-start.2
  40.0 0.0 copy-start.3
  40.0 0.0 copy-start.8
  40.0 2.2 %collective-permute-done.6 = f32[32,64]{1,0:T(8,128)S(1)} collective-permute-done((f32[32,64]{1,0:T(8,128)S(1)}, f32[32,64]{1,0:T(8,128)S(1)}, u32[]{:S(2)}, u32[]{:S(2)}) %collective-permute-start.6) | collective-permute-done | bytes 8224 | tf_op jit(solution)/shard_map/ppermute | solution.py:847
  42.2 0.0 collective-permute-done.7.come_ref
  42.3 10.0 %collective-permute-done.4.part_ref.refs_10_.refs_12_ = bf16[128,2048]{1,0:T(8,128)(2,1)S(1)} collective-permute-done((bf16[128,2048]{1,0:T(8,128)(2,1)S(1)}, bf16[128,2048]{1,0:T(8,128)(2,1)S(1)}, u32[]{:S(2)}, u32[]{:S(2)}) %collective-permute-start.4) | collective-permute-done | bytes 524320 | tf_op jit(solution)/shard_map/ppermute | solution.py:730
  52.3 0.1 total.1.refs_0_.own_ref
  52.4 0.3 collective-permute-start.8
  52.7 0.0 copy-done
  52.7 0.0 copy-done.1
  52.7 0.0 copy-done.2
  52.7 0.0 copy-done.3
  52.7 0.0 copy-done.8
  52.7 1.6 %gates.2 = (bf16[128,2048]{1,0:T(8,128)(2,1)}, bf16[128,2048]{1,0:T(8,128)(2,1)}, bf16[128,2048]{1,0:T(8,128)(2,1)}) custom-call(bf16[64,2176]{1,0:T(8,128)(2,1)S(1)} %total.1.refs_0_.own_ref, s32[1]{0:T(128)} %bitcast.rank_ref.refs_0_.refs_1_.refs_3_, bf16[128,2048]{1,0:T(8,128)(2,1)S(1)} %copy-done, bf16[128,2048]{1,0:T(8,128)(2,1)S(1)} %copy-done.1, ...), custom_call_target="tpu_custom_call" | custom-call | bytes 262144 | tf_op jit(solution)/shard_map/gates/pallas_call | solution.py:858
  54.4 0.7 %collective-permute-start.9 = (f32[32,64]{1,0:T(8,128)S(1)}, f32[32,64]{1,0:T(8,128)S(1)}, u32[]{:S(2)}, u32[]{:S(2)}) collective-permute-start(f32[32,64]{1,0:T(8,128)S(1)} %add.10.first_ref), channel_id=1, source_target_pairs={{4,8},{8,4},{0,0},{12,12},{5,9},{9,5},{1,1},{13,13},{6,10},{10,6},... | collective-permute-start | bytes 24584 | tf_op jit(solution)/shard_map/ppermute | solution.py:730
  55.1 0.0 collective-permute-done.9
  55.1 5.2 %collective-permute-start.10 = (f32[32,64]{1,0:T(8,128)S(1)}, f32[32,64]{1,0:T(8,128)S(1)}, u32[]{:S(2)}, u32[]{:S(2)}) collective-permute-start(f32[32,64]{1,0:T(8,128)S(1)} %add.11.first_ref), channel_id=1, source_target_pairs={{0,4},{12,8},{4,0},{8,12},{1,5},{13,9},{5,1},{9,13},{2,6},{14,10},... | collective-permute-start | bytes 24584 | tf_op jit(solution)/shard_map/ppermute | solution.py:730
  60.3 0.1 gates.3
  60.4 1.6 %collective-permute-done.10.first_come_ref = f32[32,64]{1,0:T(8,128)S(1)} collective-permute-done((f32[32,64]{1,0:T(8,128)S(1)}, f32[32,64]{1,0:T(8,128)S(1)}, u32[]{:S(2)}, u32[]{:S(2)}) %collective-permute-start.10) | collective-permute-done | bytes 8224 | tf_op jit(solution)/shard_map/ppermute | solution.py:730
  62.0 0.0 collective-permute-done.8.come_ref
  62.0 0.9 %finish.1 = (f32[64,2048]{1,0:T(8,128)}, f32[32,64]{1,0:T(8,128)}, f32[1,2048]{1,0:T(1,128)}) custom-call(s32[1]{0:T(128)} %bitcast.rank_ref.refs_0_.refs_1_.refs_3_, bf16[64,2176]{1,0:T(8,128)(2,1)S(1)} %total.1.refs_0_.own_ref, bf16[64,2176]{1,0:T(8,128)(2,1)S(1)} %collective-permute-done.8.come_ref, f32[32,64]{1,0:T(8,128)S(1)} %add.11.first_ref, ...), custom_call_target="tpu_custom_call" | custom-call | bytes 262144 | tf_op jit(solution)/shard_map/finish/pallas_call | solution.py:878
  (6 shorter events, 0.0 us)
Async XLA Ops:
  3.4 21.6 %collective-permute-start.1 = (bf16[128,2048]{1,0:T(8,128)(2,1)}, bf16[128,2048]{1,0:T(8,128)(2,1)S(1)}, u32[]{:S(2)}, u32[]{:S(2)}) collective-permute-start(bf16[128,2048]{1,0:T(8,128)(2,1)} %get-tuple-element.38.refs_3_.pair_ref), channel_id=1, source_target_pairs={{0,4},{12,8},{4,0},{8,12},{1,5},{13,9},{5,1},{9,13},{2,6},{14,10},... | collective-permute-start | bytes 1572872 | tf_op jit(solution)/shard_map/ppermute | solution.py:730
  6.5 18.5 %collective-permute-start.3 = (bf16[128,2048]{1,0:T(8,128)(2,1)}, bf16[128,2048]{1,0:T(8,128)(2,1)S(1)}, u32[]{:S(2)}, u32[]{:S(2)}) collective-permute-start(bf16[128,2048]{1,0:T(8,128)(2,1)} %get-tuple-element.39.refs_4_.other_ref), channel_id=1, source_target_pairs={{4,8},{8,4},{5,9},{9,5},{6,10},{10,6},{7,11},{11,7},{20,24},{24,20... | collective-permute-start | bytes 1572872 | tf_op jit(solution)/shard_map/ppermute | solution.py:730
  7.2 7.8 %copy-start.5 = (f32[64,2048]{1,0:T(8,128)S(1)}, f32[64,2048]{1,0:T(8,128)}, u32[]{:S(2)}) copy-start(f32[64,2048]{1,0:T(8,128)} %refs_4_.4) | copy-start | bytes 1572868
  7.2 7.8 %copy-start.6 = (bf16[256,256]{1,0:T(8,128)(2,1)S(1)}, bf16[256,256]{1,0:T(8,128)(2,1)}, u32[]{:S(2)}) copy-start(bf16[256,256]{1,0:T(8,128)(2,1)} %constant.16.clone.refs_7_.front_ref.refs_3_) | copy-start | bytes 393220
  7.2 7.8 %copy-start.9 = (f32[2048]{0:T(1024)S(1)}, f32[2048]{0:T(1024)}, u32[]{:S(2)}) copy-start(f32[2048]{0:T(1024)} %param.20) | copy-start | bytes 24580
  7.2 7.8 %copy-start.13 = (f32[32,64]{1,0:T(8,128)S(1)}, f32[32,64]{1,0:T(8,128)}, u32[]{:S(2)}) copy-start(f32[32,64]{1,0:T(8,128)} %first_ref.1) | copy-start | bytes 24580
  7.2 7.8 %copy-start.14 = (f32[512,32]{1,0:T(8,128)S(1)}, f32[512,32]{1,0:T(8,128)}, u32[]{:S(2)}) copy-start(f32[512,32]{1,0:T(8,128)} %constant.19.clone.feats_ref) | copy-start | bytes 196612
  13.5 8.1 %copy-start.15 = (bf16[128,2048]{1,0:T(8,128)(2,1)S(1)}, bf16[128,2048]{1,0:T(8,128)(2,1)}, u32[]{:S(2)}) copy-start(bf16[128,2048]{1,0:T(8,128)(2,1)} %get-tuple-element.43) | copy-start | bytes 1572868
  13.5 11.5 %copy-start.4 = (bf16[256,256]{1,0:T(8,128)(2,1)S(1)}, bf16[256,256]{1,0:T(8,128)(2,1)}, u32[]{:S(2)}) copy-start(bf16[256,256]{1,0:T(8,128)(2,1)} %constant.17.clone.refs_8_.back_ref.refs_4_.refs_6_.refs_3_) | copy-start | bytes 393220
  13.5 11.5 %copy-start.7 = (f32[32,512]{1,0:T(8,128)S(1)}, f32[32,512]{1,0:T(8,128)}, u32[]{:S(2)}) copy-start(f32[32,512]{1,0:T(8,128)} %constant.18.clone.refs_9_.featt_ref.refs_8_) | copy-start | bytes 196612
  13.5 11.5 %copy-start.11 = (bf16[128,2048]{1,0:T(8,128)(2,1)S(1)}, bf16[128,2048]{1,0:T(8,128)(2,1)}, u32[]{:S(2)}) copy-start(bf16[128,2048]{1,0:T(8,128)(2,1)} %get-tuple-element.38.refs_3_.pair_ref) | copy-start | bytes 1572868
  13.5 11.5 %copy-start.12 = (bf16[128,2048]{1,0:T(8,128)(2,1)S(1)}, bf16[128,2048]{1,0:T(8,128)(2,1)}, u32[]{:S(2)}) copy-start(bf16[128,2048]{1,0:T(8,128)(2,1)} %get-tuple-element.39.refs_4_.other_ref) | copy-start | bytes 1572868
  13.5 11.5 %collective-permute-start.2 = (bf16[64,2176]{1,0:T(8,128)(2,1)}, bf16[64,2176]{1,0:T(8,128)(2,1)S(1)}, u32[]{:S(2)}, u32[]{:S(2)}) collective-permute-start(bf16[64,2176]{1,0:T(8,128)(2,1)} %own_pair.1), channel_id=1, source_target_pairs={{0,4},{12,8},{1,5},{13,9},{2,6},{14,10},{3,7},{15,11},{16,20},{28,... | collective-permute-start | bytes 835592 | tf_op jit(solution)/shard_map/ppermute | solution.py:730
  21.6 13.5 %collective-permute-start = (bf16[128,2048]{1,0:T(8,128)(2,1)S(1)}, bf16[128,2048]{1,0:T(8,128)(2,1)S(1)}, u32[]{:S(2)}, u32[]{:S(2)}) collective-permute-start(bf16[128,2048]{1,0:T(8,128)(2,1)S(1)} %copy-done.15), channel_id=1, source_target_pairs={{0,8},{12,4},{1,9},{13,5},{2,10},{14,6},{3,11},{15,7},{16,24},{28,... | collective-permute-start | bytes 1572872 | tf_op jit(solution)/shard_map/ppermute | solution.py:730
  35.1 1.4 %copy-start.10 = (f32[1,2048]{1,0:T(1,128)S(1)}, f32[1,2048]{1,0:T(1,128)}, u32[]{:S(2)}) copy-start(f32[1,2048]{1,0:T(1,128)} %get-tuple-element.40.refs_10_.refs_12_) | copy-start | bytes 24580
  35.1 17.2 %collective-permute-start.4 = (bf16[128,2048]{1,0:T(8,128)(2,1)S(1)}, bf16[128,2048]{1,0:T(8,128)(2,1)S(1)}, u32[]{:S(2)}, u32[]{:S(2)}) collective-permute-start(bf16[128,2048]{1,0:T(8,128)(2,1)S(1)} %get-tuple-element.48.refs_0_), channel_id=1, source_target_pairs={{4,0},{8,12},{5,1},{9,13},{6,2},{10,14},{7,3},{11,15},{20,16},{24,... | collective-permute-start | bytes 1572872 | tf_op jit(solution)/shard_map/ppermute | solution.py:730
  36.6 5.7 %collective-permute-start.7 = (bf16[64,2176]{1,0:T(8,128)(2,1)S(1)}, bf16[64,2176]{1,0:T(8,128)(2,1)S(1)}, u32[]{:S(2)}, u32[]{:S(2)}) collective-permute-start(bf16[64,2176]{1,0:T(8,128)(2,1)S(1)} %get-tuple-element.55.own_ref), channel_id=1, source_target_pairs={{4,8},{8,4},{0,0},{12,12},{5,9},{9,5},{1,1},{13,13},{6,10},{10,6},... | collective-permute-start | bytes 835592 | tf_op jit(solution)/shard_map/ppermute | solution.py:730
  37.2 1.2 %collective-permute-start.5 = (f32[32,64]{1,0:T(8,128)S(1)}, f32[32,64]{1,0:T(8,128)S(1)}, u32[]{:S(2)}, u32[]{:S(2)}) collective-permute-start(f32[32,64]{1,0:T(8,128)S(1)} %get-tuple-element.54), channel_id=1, source_target_pairs={{0,1},{1,0},{2,3},{3,2},{4,5},{5,4},{6,7},{7,6},{8,9},{9,8},{10,11... | collective-permute-start | bytes 24584 | tf_op jit(solution)/shard_map/ppermute | solution.py:847
  38.5 3.7 %collective-permute-start.6 = (f32[32,64]{1,0:T(8,128)S(1)}, f32[32,64]{1,0:T(8,128)S(1)}, u32[]{:S(2)}, u32[]{:S(2)}) collective-permute-start(f32[32,64]{1,0:T(8,128)S(1)} %add.9), channel_id=1, source_target_pairs={{0,2},{1,3},{2,0},{3,1},{4,6},{5,7},{6,4},{7,5},{8,10},{9,11},{10,... | collective-permute-start | bytes 24584 | tf_op jit(solution)/shard_map/ppermute | solution.py:847
  40.0 12.7 %copy-start = (bf16[128,2048]{1,0:T(8,128)(2,1)S(1)}, bf16[128,2048]{1,0:T(8,128)(2,1)}, u32[]{:S(2)}) copy-start(bf16[128,2048]{1,0:T(8,128)(2,1)} %refs_4_.6) | copy-start | bytes 1572868
  40.0 12.7 %copy-start.1 = (bf16[128,2048]{1,0:T(8,128)(2,1)S(1)}, bf16[128,2048]{1,0:T(8,128)(2,1)}, u32[]{:S(2)}) copy-start(bf16[128,2048]{1,0:T(8,128)(2,1)} %refs_5_.5) | copy-start | bytes 1572868
  40.0 12.7 %copy-start.2 = (bf16[128,2048]{1,0:T(8,128)(2,1)S(1)}, bf16[128,2048]{1,0:T(8,128)(2,1)}, u32[]{:S(2)}) copy-start(bf16[128,2048]{1,0:T(8,128)(2,1)} %refs_6_.2) | copy-start | bytes 1572868
  40.0 12.7 %copy-start.3 = (bf16[128,2048]{1,0:T(8,128)(2,1)S(1)}, bf16[128,2048]{1,0:T(8,128)(2,1)}, u32[]{:S(2)}) copy-start(bf16[128,2048]{1,0:T(8,128)(2,1)} %refs_7_.2) | copy-start | bytes 1572868
  40.0 12.7 %copy-start.8 = (f32[2048]{0:T(1024)S(1)}, f32[2048]{0:T(1024)}, u32[]{:S(2)}) copy-start(f32[2048]{0:T(1024)} %param.19) | copy-start | bytes 24580
  52.4 9.6 %collective-permute-start.8 = (bf16[64,2176]{1,0:T(8,128)(2,1)S(1)}, bf16[64,2176]{1,0:T(8,128)(2,1)S(1)}, u32[]{:S(2)}, u32[]{:S(2)}) collective-permute-start(bf16[64,2176]{1,0:T(8,128)(2,1)S(1)} %total.1.refs_0_.own_ref), channel_id=1, source_target_pairs={{0,4},{12,8},{4,0},{8,12},{1,5},{13,9},{5,1},{9,13},{2,6},{14,10},... | collective-permute-start | bytes 835592 | tf_op jit(solution)/shard_map/ppermute | solution.py:730
  54.4 0.7 %collective-permute-start.9 = (f32[32,64]{1,0:T(8,128)S(1)}, f32[32,64]{1,0:T(8,128)S(1)}, u32[]{:S(2)}, u32[]{:S(2)}) collective-permute-start(f32[32,64]{1,0:T(8,128)S(1)} %add.10.first_ref), channel_id=1, source_target_pairs={{4,8},{8,4},{0,0},{12,12},{5,9},{9,5},{1,1},{13,13},{6,10},{10,6},... | collective-permute-start | bytes 24584 | tf_op jit(solution)/shard_map/ppermute | solution.py:730
  55.1 6.9 %collective-permute-start.10 = (f32[32,64]{1,0:T(8,128)S(1)}, f32[32,64]{1,0:T(8,128)S(1)}, u32[]{:S(2)}, u32[]{:S(2)}) collective-permute-start(f32[32,64]{1,0:T(8,128)S(1)} %add.11.first_ref), channel_id=1, source_target_pairs={{0,4},{12,8},{4,0},{8,12},{1,5},{13,9},{5,1},{9,13},{2,6},{14,10},... | collective-permute-start | bytes 24584 | tf_op jit(solution)/shard_map/ppermute | solution.py:730

commit v17 on v15

--- a/solution.py
+++ b/solution.py
@@ -840,10 +840,15 @@
     )(part, rank, near_spec, far_spec, second_weight, rate_row, back, trans, featt, slope, sums, first, bias, come)
     pay_come = move(pay, across + alone)
     group = lax.axis_size(("ch", "sub"))
-    bit = 1
-    while bit < group:
-        first = first + lax.ppermute(first, ("ch", "sub"), [(i, i ^ bit) for i in range(group)])
-        bit *= 2
+
+    def swapped(array, bits):
+        for bit in bits:
+            array = array + lax.ppermute(array, ("ch", "sub"), [(i, i ^ bit) for i in range(group)])
+        return array
+
+    bits = [1 << i for i in range(group.bit_length() - 1)]
+    first = swapped(first, bits[:1])
+    first = first + move(first, across + alone)
 
     (total,) = call(
         functools.partial(total_kernel, channels, hid_count), "total", 0,
@@ -868,7 +873,7 @@
 
     grads = gates(False, total)
     first, _ = lax.optimization_barrier((first, grads[0]))
-    first = first + move(first, across + alone)
+    first = swapped(first, bits[1:])
     first_come = move(first, inward + outward)
     grad_one, grad_two, grad_value = gates(True, *grads)
 

time: 61.1 us -> 63.7 us (1.043)
  waiting for transfers between devices: 20.9 us -> 25.9 us
  starting transfers between devices: 16.9 us -> 14.4 us
    ppermute x9, waiting for transfers between devices: 17.5 us -> 22.5 us  [move(): return lax.ppermute(array, 'ctx', pairs)]
    ppermute x9, starting transfers between devices: 15.3 us -> 12.8 us  [move(): return lax.ppermute(array, 'ctx', pairs)]
  transfers between devices with their start and end apart: 11 -> 11, of which waited for: 6 -> 6; matrix products, arithmetic and copies ran while one was open for 0% -> 0% of each run, Pallas kernels for 30% -> 29%
where the time goes in v17:
time: 63.7 us; the launch traced here: 63.5 us
  waiting for transfers between devices  25.9 us (41%)
  Pallas kernels  22 us (35%)
  starting transfers between devices  14.4 us (23%)
  between operations  1.02 us (2%)
    ppermute x9, waiting for transfers between devices, move(): return lax.ppermute(array, 'ctx', pairs)  22.5 us
    ppermute x9, starting transfers between devices, move(): return lax.ppermute(array, 'ctx', pairs)  12.8 us
    pallas_call x1, Pallas kernels, few_shards_body(): call(functools.partial(filters_kernel, rows, shards, blocks, width), 'fil...  6.51 us
    pallas_call x1, Pallas kernels, few_shards_body(): call(only(False, shards, 0, functools.partial(own_kernel, rows, shards, c...  6.2 us
    pallas_call x1, Pallas kernels, few_shards_body(): call(functools.partial(near_kernel, rows, shards, blocks, width), 'near_b...  3.82 us
    ppermute x2, waiting for transfers between devices, swapped(): lax.ppermute(array, ('ch', 'sub'), [(i, i ^ bit) for i in range(group)])  3.4 us
    pallas_call x1, Pallas kernels, few_shards_body(): pl.pallas_call(products_kernel, grid=(rows // row_step,), in_specs=[smem]...  2.79 us
    pallas_call x2, Pallas kernels, gates(): call(only(inner, shards, len(before), functools.partial(gates_kernel, inn...  1.76 us
  transfers between devices with their start and end apart: 11, of which 6 were waited for; matrix products, arithmetic and copies ran while one was open for 0% of the time, Pallas kernels for 29%

profile of v17, /device:TPU:0, one launch (start us, length us, event | category | flops | bytes accessed | tf_op | source)
XLA Modules:
  0.0 63.5 jit_solution(7442719827912846023)
XLA Ops:
  0.6 2.8 %products.1 = (bf16[128,2048]{1,0:T(8,128)(2,1)}, bf16[128,2048]{1,0:T(8,128)(2,1)}, bf16[128,2048]{1,0:T(8,128)(2,1)}, f32[1,2048]{1,0:T(1,128)}) custom-call(s32[1]{0:T(128)} %bitcast.rank_ref.refs_0_.refs_1_.refs_3_, bf16[128,2048]{1,0:T(8,128)(2,1)} %refs_4_.6, bf16[128,2048]{1,0:T(8,128)(2,1)} %refs_5_.5, bf16[128,2048]{1,0:T(8,128)(2,1)} %refs_6_.2, ...), custom_call_target="tpu_custom_call" | custom-call | tf_op jit(solution)/shard_map/products/pallas_call | solution.py:742
  3.4 3.1 %collective-permute-start.1 = (bf16[128,2048]{1,0:T(8,128)(2,1)}, bf16[128,2048]{1,0:T(8,128)(2,1)S(1)}, u32[]{:S(2)}, u32[]{:S(2)}) collective-permute-start(bf16[128,2048]{1,0:T(8,128)(2,1)} %get-tuple-element.36.refs_3_.pair_ref), channel_id=1, source_target_pairs={{0,4},{12,8},{4,0},{8,12},{1,5},{13,9},{5,1},{9,13},{2,6},{14,10},... | collective-permute-start | bytes 1572872 | tf_op jit(solution)/shard_map/ppermute | solution.py:730
  6.5 0.7 %collective-permute-start.2 = (bf16[128,2048]{1,0:T(8,128)(2,1)}, bf16[128,2048]{1,0:T(8,128)(2,1)S(1)}, u32[]{:S(2)}, u32[]{:S(2)}) collective-permute-start(bf16[128,2048]{1,0:T(8,128)(2,1)} %get-tuple-element.37.refs_4_.other_ref), channel_id=1, source_target_pairs={{4,8},{8,4},{5,9},{9,5},{6,10},{10,6},{7,11},{11,7},{20,24},{24,20... | collective-permute-start | bytes 1572872 | tf_op jit(solution)/shard_map/ppermute | solution.py:730
  7.2 0.0 copy-start.5
  7.2 0.0 copy-start.6
  7.2 0.0 copy-start.9
  7.2 0.0 copy-start.13
  7.2 0.0 copy-start.14
  7.3 6.2 %own_pair.1 = bf16[64,2176]{1,0:T(8,128)(2,1)} custom-call(s32[1]{0:T(128)} %bitcast.rank_ref.refs_0_.refs_1_.refs_3_, f32[128,32]{1,0:T(8,128)} %constant.15.clone.refs_1_, f32[32,64]{1,0:T(8,128)} %first_ref.1, bf16[128,2048]{1,0:T(8,128)(2,1)} %get-tuple-element.36.refs_3_.pair_ref, bf16[128,2048]{1,0:T(8,128)(2,1)} %get-tuple-element.37.refs_4_.other_ref, ...), custom_call_target="tpu_custom_call" | custom-call | flops 2147483648 | bytes 262144 | tf_op jit(solution)/shard_map/own_pair/pallas_call | solution.py:759
  13.5 0.0 copy-done.5
  13.5 0.0 copy-done.6
  13.5 0.0 copy-done.9
  13.5 0.0 copy-done.13
  13.5 0.0 copy-done.14
  13.5 0.0 copy-start.15
  13.5 0.0 copy-start.16
  13.5 0.0 copy-start.4
  13.6 0.0 copy-start.7
  13.6 0.0 copy-start.11
  13.6 0.0 copy-start.12
  13.6 6.5 %filters.1 = (bf16[4,256,2048]{2,1,0:T(8,128)(2,1)S(1)}, bf16[128,512]{1,0:T(8,128)(2,1)S(1)}, f32[512,64]{1,0:T(8,128)S(1)}) custom-call(f32[512,32]{1,0:T(8,128)S(1)} %copy-done.14, f32[32,64]{1,0:T(8,128)S(1)} %copy-done.13, f32[64,2048]{1,0:T(8,128)S(1)} %copy-done.5, f32[1,2048]{1,0:T(1,128)S(1)} %bitcast.7, bf16[256,256]{1,0:T(8,128)(2,1)S(1)} %copy-done.6), custom_call_target="tpu_custom_call" | custom-call | flops 2147483648 | bytes 262144 | tf_op jit(solution)/shard_map/filters/pallas_call | solution.py:773
  20.1 0.0 copy-done.15
  20.1 1.3 %collective-permute-start = (bf16[128,2048]{1,0:T(8,128)(2,1)S(1)}, bf16[128,2048]{1,0:T(8,128)(2,1)S(1)}, u32[]{:S(2)}, u32[]{:S(2)}) collective-permute-start(bf16[128,2048]{1,0:T(8,128)(2,1)S(1)} %copy-done.15), channel_id=1, source_target_pairs={{0,8},{12,4},{1,9},{13,5},{2,10},{14,6},{3,11},{15,7},{16,24},{28,... | collective-permute-start | bytes 1572872 | tf_op jit(solution)/shard_map/ppermute | solution.py:730
  21.4 0.0 copy-done.16
  21.5 1.3 %collective-permute-start.4 = (bf16[64,2176]{1,0:T(8,128)(2,1)S(1)}, bf16[64,2176]{1,0:T(8,128)(2,1)S(1)}, u32[]{:S(2)}, u32[]{:S(2)}) collective-permute-start(bf16[64,2176]{1,0:T(8,128)(2,1)S(1)} %copy-done.16), channel_id=1, source_target_pairs={{0,4},{12,8},{1,5},{13,9},{2,6},{14,10},{3,7},{15,11},{16,20},{28,... | collective-permute-start | bytes 835592 | tf_op jit(solution)/shard_map/ppermute | solution.py:730
  22.8 0.0 collective-permute-done.1.pair_in_ref
  22.8 0.0 collective-permute-done.2.middle_in_ref
  22.8 0.0 copy-done.4
  22.8 0.0 copy-done.7
  22.8 0.0 copy-done.11
  22.8 0.0 copy-done.12
  22.8 3.8 %near_blocks.1 = (f32[128,2048]{1,0:T(8,128)S(1)}, f32[128,2048]{1,0:T(8,128)S(1)}, f32[128,2048]{1,0:T(8,128)S(1)}, f32[64,2048]{1,0:T(8,128)S(1)}, f32[32,64]{1,0:T(8,128)S(1)}, /*index=5*/f32[256,2048]{1,0:T(8,128)S(1)}) custom-call(s32[1]{0:T(128)} %bitcast.rank_ref.refs_0_.refs_1_.refs_3_, bf16[128,2048]{1,0:T(8,128)(2,1)S(1)} %copy-done.11, ...), custom_call_target="tpu_custom_call" | custom-call | flops 5368709120 | bytes 262144 | tf_op jit(solution)/shard_map/near_blocks/pallas_call | solution.py:785
  26.7 7.1 %collective-permute-done.refs_1_ = bf16[128,2048]{1,0:T(8,128)(2,1)S(1)} collective-permute-done((bf16[128,2048]{1,0:T(8,128)(2,1)S(1)}, bf16[128,2048]{1,0:T(8,128)(2,1)S(1)}, u32[]{:S(2)}, u32[]{:S(2)}) %collective-permute-start) | collective-permute-done | bytes 524320 | tf_op jit(solution)/shard_map/ppermute | solution.py:730
  33.7 0.0 copy-start.10
  33.7 1.4 %collective-permute-start.3 = (bf16[128,2048]{1,0:T(8,128)(2,1)S(1)}, bf16[128,2048]{1,0:T(8,128)(2,1)S(1)}, u32[]{:S(2)}, u32[]{:S(2)}) collective-permute-start(bf16[128,2048]{1,0:T(8,128)(2,1)S(1)} %get-tuple-element.45.refs_0_), channel_id=1, source_target_pairs={{4,0},{8,12},{5,1},{9,13},{6,2},{10,14},{7,3},{11,15},{20,16},{24,... | collective-permute-start | bytes 1572872 | tf_op jit(solution)/shard_map/ppermute | solution.py:730
  35.1 3.4 %collective-permute-done.4.refs_13_ = bf16[64,2176]{1,0:T(8,128)(2,1)S(1)} collective-permute-done((bf16[64,2176]{1,0:T(8,128)(2,1)S(1)}, bf16[64,2176]{1,0:T(8,128)(2,1)S(1)}, u32[]{:S(2)}, u32[]{:S(2)}) %collective-permute-start.4) | collective-permute-done | bytes 278560 | tf_op jit(solution)/shard_map/ppermute | solution.py:730
  38.5 0.0 copy-done.10
  38.5 0.7 %collective-permute-start.7 = (bf16[64,2176]{1,0:T(8,128)(2,1)S(1)}, bf16[64,2176]{1,0:T(8,128)(2,1)S(1)}, u32[]{:S(2)}, u32[]{:S(2)}) collective-permute-start(bf16[64,2176]{1,0:T(8,128)(2,1)S(1)} %get-tuple-element.51.own_ref), channel_id=1, source_target_pairs={{4,8},{8,4},{0,0},{12,12},{5,9},{9,5},{1,1},{13,13},{6,10},{10,6},... | collective-permute-start | bytes 835592 | tf_op jit(solution)/shard_map/ppermute | solution.py:730
  39.2 0.1 collective-permute-start.5
  39.3 1.2 %collective-permute-done.5 = f32[32,64]{1,0:T(8,128)S(1)} collective-permute-done((f32[32,64]{1,0:T(8,128)S(1)}, f32[32,64]{1,0:T(8,128)S(1)}, u32[]{:S(2)}, u32[]{:S(2)}) %collective-permute-start.5) | collective-permute-done | bytes 8224 | tf_op jit(solution)/shard_map/ppermute | solution.py:846
  40.5 0.7 %collective-permute-start.6 = (f32[32,64]{1,0:T(8,128)S(1)}, f32[32,64]{1,0:T(8,128)S(1)}, u32[]{:S(2)}, u32[]{:S(2)}) collective-permute-start(f32[32,64]{1,0:T(8,128)S(1)} %add.9), channel_id=1, source_target_pairs={{4,8},{8,4},{0,0},{12,12},{5,9},{9,5},{1,1},{13,13},{6,10},{10,6},... | collective-permute-start | bytes 24584 | tf_op jit(solution)/shard_map/ppermute | solution.py:730
  41.2 0.0 copy-start
  41.2 0.0 copy-start.1
  41.2 0.0 copy-start.2
  41.2 0.0 copy-start.3
  41.2 0.0 copy-start.8
  41.2 0.0 collective-permute-done.6
  41.2 0.0 collective-permute-done.7.come_ref
  41.2 8.4 %collective-permute-done.3.part_ref.refs_10_.refs_12_ = bf16[128,2048]{1,0:T(8,128)(2,1)S(1)} collective-permute-done((bf16[128,2048]{1,0:T(8,128)(2,1)S(1)}, bf16[128,2048]{1,0:T(8,128)(2,1)S(1)}, u32[]{:S(2)}, u32[]{:S(2)}) %collective-permute-start.3) | collective-permute-done | bytes 524320 | tf_op jit(solution)/shard_map/ppermute | solution.py:730
  49.6 0.1 total.1.refs_0_.own_ref
  49.7 3.7 %collective-permute-start.8 = (bf16[64,2176]{1,0:T(8,128)(2,1)S(1)}, bf16[64,2176]{1,0:T(8,128)(2,1)S(1)}, u32[]{:S(2)}, u32[]{:S(2)}) collective-permute-start(bf16[64,2176]{1,0:T(8,128)(2,1)S(1)} %total.1.refs_0_.own_ref), channel_id=1, source_target_pairs={{0,4},{12,8},{4,0},{8,12},{1,5},{13,9},{5,1},{9,13},{2,6},{14,10},... | collective-permute-start | bytes 835592 | tf_op jit(solution)/shard_map/ppermute | solution.py:730
  53.4 0.0 copy-done
  53.4 0.0 copy-done.1
  53.4 0.0 copy-done.2
  53.4 0.0 copy-done.3
  53.4 0.0 copy-done.8
  53.4 1.6 %gates.2 = (bf16[128,2048]{1,0:T(8,128)(2,1)}, bf16[128,2048]{1,0:T(8,128)(2,1)}, bf16[128,2048]{1,0:T(8,128)(2,1)}) custom-call(bf16[64,2176]{1,0:T(8,128)(2,1)S(1)} %total.1.refs_0_.own_ref, s32[1]{0:T(128)} %bitcast.rank_ref.refs_0_.refs_1_.refs_3_, bf16[128,2048]{1,0:T(8,128)(2,1)S(1)} %copy-done, bf16[128,2048]{1,0:T(8,128)(2,1)S(1)} %copy-done.1, ...), custom_call_target="tpu_custom_call" | custom-call | bytes 262144 | tf_op jit(solution)/shard_map/gates/pallas_call | solution.py:861
  55.0 1.6 %collective-permute-start.9 = (f32[32,64]{1,0:T(8,128)S(1)}, f32[32,64]{1,0:T(8,128)S(1)}, u32[]{:S(2)}, u32[]{:S(2)}) collective-permute-start(f32[32,64]{1,0:T(8,128)S(1)} %add.10.first_ref), channel_id=1, source_target_pairs={{0,2},{1,3},{2,0},{3,1},{4,6},{5,7},{6,4},{7,5},{8,10},{9,11},{10,... | collective-permute-start | bytes 24584 | tf_op jit(solution)/shard_map/ppermute | solution.py:846
  56.6 2.2 %collective-permute-done.9 = f32[32,64]{1,0:T(8,128)S(1)} collective-permute-done((f32[32,64]{1,0:T(8,128)S(1)}, f32[32,64]{1,0:T(8,128)S(1)}, u32[]{:S(2)}, u32[]{:S(2)}) %collective-permute-start.9) | collective-permute-done | bytes 8224 | tf_op jit(solution)/shard_map/ppermute | solution.py:846
  58.9 0.0 collective-permute-start.10
  58.9 0.1 gates.3
  59.0 3.6 %collective-permute-done.10.first_come_ref = f32[32,64]{1,0:T(8,128)S(1)} collective-permute-done((f32[32,64]{1,0:T(8,128)S(1)}, f32[32,64]{1,0:T(8,128)S(1)}, u32[]{:S(2)}, u32[]{:S(2)}) %collective-permute-start.10) | collective-permute-done | bytes 8224 | tf_op jit(solution)/shard_map/ppermute | solution.py:730
  62.6 0.0 collective-permute-done.8.come_ref
  62.6 0.9 %finish.1 = (f32[64,2048]{1,0:T(8,128)}, f32[32,64]{1,0:T(8,128)}, f32[1,2048]{1,0:T(1,128)}) custom-call(s32[1]{0:T(128)} %bitcast.rank_ref.refs_0_.refs_1_.refs_3_, bf16[64,2176]{1,0:T(8,128)(2,1)S(1)} %total.1.refs_0_.own_ref, bf16[64,2176]{1,0:T(8,128)(2,1)S(1)} %collective-permute-done.8.come_ref, f32[32,64]{1,0:T(8,128)S(1)} %add.11.first_ref, ...), custom_call_target="tpu_custom_call" | custom-call | bytes 262144 | tf_op jit(solution)/shard_map/finish/pallas_call | solution.py:881
  (6 shorter events, 0.0 us)
Async XLA Ops:
  3.4 19.3 %collective-permute-start.1 = (bf16[128,2048]{1,0:T(8,128)(2,1)}, bf16[128,2048]{1,0:T(8,128)(2,1)S(1)}, u32[]{:S(2)}, u32[]{:S(2)}) collective-permute-start(bf16[128,2048]{1,0:T(8,128)(2,1)} %get-tuple-element.36.refs_3_.pair_ref), channel_id=1, source_target_pairs={{0,4},{12,8},{4,0},{8,12},{1,5},{13,9},{5,1},{9,13},{2,6},{14,10},... | collective-permute-start | bytes 1572872 | tf_op jit(solution)/shard_map/ppermute | solution.py:730
  6.5 16.3 %collective-permute-start.2 = (bf16[128,2048]{1,0:T(8,128)(2,1)}, bf16[128,2048]{1,0:T(8,128)(2,1)S(1)}, u32[]{:S(2)}, u32[]{:S(2)}) collective-permute-start(bf16[128,2048]{1,0:T(8,128)(2,1)} %get-tuple-element.37.refs_4_.other_ref), channel_id=1, source_target_pairs={{4,8},{8,4},{5,9},{9,5},{6,10},{10,6},{7,11},{11,7},{20,24},{24,20... | collective-permute-start | bytes 1572872 | tf_op jit(solution)/shard_map/ppermute | solution.py:730
  7.2 6.3 %copy-start.5 = (f32[64,2048]{1,0:T(8,128)S(1)}, f32[64,2048]{1,0:T(8,128)}, u32[]{:S(2)}) copy-start(f32[64,2048]{1,0:T(8,128)} %refs_4_.4) | copy-start | bytes 1572868
  7.2 6.3 %copy-start.6 = (bf16[256,256]{1,0:T(8,128)(2,1)S(1)}, bf16[256,256]{1,0:T(8,128)(2,1)}, u32[]{:S(2)}) copy-start(bf16[256,256]{1,0:T(8,128)(2,1)} %constant.16.clone.refs_7_.front_ref.refs_3_) | copy-start | bytes 393220
  7.2 6.3 %copy-start.9 = (f32[2048]{0:T(1024)S(1)}, f32[2048]{0:T(1024)}, u32[]{:S(2)}) copy-start(f32[2048]{0:T(1024)} %param.20) | copy-start | bytes 24580
  7.2 6.3 %copy-start.13 = (f32[32,64]{1,0:T(8,128)S(1)}, f32[32,64]{1,0:T(8,128)}, u32[]{:S(2)}) copy-start(f32[32,64]{1,0:T(8,128)} %first_ref.1) | copy-start | bytes 24580
  7.2 6.3 %copy-start.14 = (f32[512,32]{1,0:T(8,128)S(1)}, f32[512,32]{1,0:T(8,128)}, u32[]{:S(2)}) copy-start(f32[512,32]{1,0:T(8,128)} %constant.19.clone.feats_ref) | copy-start | bytes 196612
  13.5 6.6 %copy-start.15 = (bf16[128,2048]{1,0:T(8,128)(2,1)S(1)}, bf16[128,2048]{1,0:T(8,128)(2,1)}, u32[]{:S(2)}) copy-start(bf16[128,2048]{1,0:T(8,128)(2,1)} %get-tuple-element.41) | copy-start | bytes 1572868
  13.5 7.9 %copy-start.16 = (bf16[64,2176]{1,0:T(8,128)(2,1)S(1)}, bf16[64,2176]{1,0:T(8,128)(2,1)}, u32[]{:S(2)}) copy-start(bf16[64,2176]{1,0:T(8,128)(2,1)} %own_pair.1) | copy-start | bytes 835588
  13.5 9.3 %copy-start.4 = (bf16[256,256]{1,0:T(8,128)(2,1)S(1)}, bf16[256,256]{1,0:T(8,128)(2,1)}, u32[]{:S(2)}) copy-start(bf16[256,256]{1,0:T(8,128)(2,1)} %constant.17.clone.refs_8_.back_ref.refs_4_.refs_6_.refs_3_) | copy-start | bytes 393220
  13.6 9.2 %copy-start.7 = (f32[32,512]{1,0:T(8,128)S(1)}, f32[32,512]{1,0:T(8,128)}, u32[]{:S(2)}) copy-start(f32[32,512]{1,0:T(8,128)} %constant.18.clone.refs_9_.featt_ref.refs_8_) | copy-start | bytes 196612
  13.6 9.2 %copy-start.11 = (bf16[128,2048]{1,0:T(8,128)(2,1)S(1)}, bf16[128,2048]{1,0:T(8,128)(2,1)}, u32[]{:S(2)}) copy-start(bf16[128,2048]{1,0:T(8,128)(2,1)} %get-tuple-element.36.refs_3_.pair_ref) | copy-start | bytes 1572868
  13.6 9.2 %copy-start.12 = (bf16[128,2048]{1,0:T(8,128)(2,1)S(1)}, bf16[128,2048]{1,0:T(8,128)(2,1)}, u32[]{:S(2)}) copy-start(bf16[128,2048]{1,0:T(8,128)(2,1)} %get-tuple-element.37.refs_4_.other_ref) | copy-start | bytes 1572868
  20.1 13.6 %collective-permute-start = (bf16[128,2048]{1,0:T(8,128)(2,1)S(1)}, bf16[128,2048]{1,0:T(8,128)(2,1)S(1)}, u32[]{:S(2)}, u32[]{:S(2)}) collective-permute-start(bf16[128,2048]{1,0:T(8,128)(2,1)S(1)} %copy-done.15), channel_id=1, source_target_pairs={{0,8},{12,4},{1,9},{13,5},{2,10},{14,6},{3,11},{15,7},{16,24},{28,... | collective-permute-start | bytes 1572872 | tf_op jit(solution)/shard_map/ppermute | solution.py:730
  21.5 17.1 %collective-permute-start.4 = (bf16[64,2176]{1,0:T(8,128)(2,1)S(1)}, bf16[64,2176]{1,0:T(8,128)(2,1)S(1)}, u32[]{:S(2)}, u32[]{:S(2)}) collective-permute-start(bf16[64,2176]{1,0:T(8,128)(2,1)S(1)} %copy-done.16), channel_id=1, source_target_pairs={{0,4},{12,8},{1,5},{13,9},{2,6},{14,10},{3,7},{15,11},{16,20},{28,... | collective-permute-start | bytes 835592 | tf_op jit(solution)/shard_map/ppermute | solution.py:730
  33.7 4.8 %copy-start.10 = (f32[1,2048]{1,0:T(1,128)S(1)}, f32[1,2048]{1,0:T(1,128)}, u32[]{:S(2)}) copy-start(f32[1,2048]{1,0:T(1,128)} %get-tuple-element.38.refs_10_.refs_12_) | copy-start | bytes 24580
  33.7 15.9 %collective-permute-start.3 = (bf16[128,2048]{1,0:T(8,128)(2,1)S(1)}, bf16[128,2048]{1,0:T(8,128)(2,1)S(1)}, u32[]{:S(2)}, u32[]{:S(2)}) collective-permute-start(bf16[128,2048]{1,0:T(8,128)(2,1)S(1)} %get-tuple-element.45.refs_0_), channel_id=1, source_target_pairs={{4,0},{8,12},{5,1},{9,13},{6,2},{10,14},{7,3},{11,15},{20,16},{24,... | collective-permute-start | bytes 1572872 | tf_op jit(solution)/shard_map/ppermute | solution.py:730
  38.5 2.7 %collective-permute-start.7 = (bf16[64,2176]{1,0:T(8,128)(2,1)S(1)}, bf16[64,2176]{1,0:T(8,128)(2,1)S(1)}, u32[]{:S(2)}, u32[]{:S(2)}) collective-permute-start(bf16[64,2176]{1,0:T(8,128)(2,1)S(1)} %get-tuple-element.51.own_ref), channel_id=1, source_target_pairs={{4,8},{8,4},{0,0},{12,12},{5,9},{9,5},{1,1},{13,13},{6,10},{10,6},... | collective-permute-start | bytes 835592 | tf_op jit(solution)/shard_map/ppermute | solution.py:730
  39.2 1.2 %collective-permute-start.5 = (f32[32,64]{1,0:T(8,128)S(1)}, f32[32,64]{1,0:T(8,128)S(1)}, u32[]{:S(2)}, u32[]{:S(2)}) collective-permute-start(f32[32,64]{1,0:T(8,128)S(1)} %get-tuple-element.50), channel_id=1, source_target_pairs={{0,1},{1,0},{2,3},{3,2},{4,5},{5,4},{6,7},{7,6},{8,9},{9,8},{10,11... | collective-permute-start | bytes 24584 | tf_op jit(solution)/shard_map/ppermute | solution.py:846
  40.5 0.7 %collective-permute-start.6 = (f32[32,64]{1,0:T(8,128)S(1)}, f32[32,64]{1,0:T(8,128)S(1)}, u32[]{:S(2)}, u32[]{:S(2)}) collective-permute-start(f32[32,64]{1,0:T(8,128)S(1)} %add.9), channel_id=1, source_target_pairs={{4,8},{8,4},{0,0},{12,12},{5,9},{9,5},{1,1},{13,13},{6,10},{10,6},... | collective-permute-start | bytes 24584 | tf_op jit(solution)/shard_map/ppermute | solution.py:730
  41.2 12.2 %copy-start = (bf16[128,2048]{1,0:T(8,128)(2,1)S(1)}, bf16[128,2048]{1,0:T(8,128)(2,1)}, u32[]{:S(2)}) copy-start(bf16[128,2048]{1,0:T(8,128)(2,1)} %refs_4_.6) | copy-start | bytes 1572868
  41.2 12.2 %copy-start.1 = (bf16[128,2048]{1,0:T(8,128)(2,1)S(1)}, bf16[128,2048]{1,0:T(8,128)(2,1)}, u32[]{:S(2)}) copy-start(bf16[128,2048]{1,0:T(8,128)(2,1)} %refs_5_.5) | copy-start | bytes 1572868
  41.2 12.2 %copy-start.2 = (bf16[128,2048]{1,0:T(8,128)(2,1)S(1)}, bf16[128,2048]{1,0:T(8,128)(2,1)}, u32[]{:S(2)}) copy-start(bf16[128,2048]{1,0:T(8,128)(2,1)} %refs_6_.2) | copy-start | bytes 1572868
  41.2 12.2 %copy-start.3 = (bf16[128,2048]{1,0:T(8,128)(2,1)S(1)}, bf16[128,2048]{1,0:T(8,128)(2,1)}, u32[]{:S(2)}) copy-start(bf16[128,2048]{1,0:T(8,128)(2,1)} %refs_7_.2) | copy-start | bytes 1572868
  41.2 12.2 %copy-start.8 = (f32[2048]{0:T(1024)S(1)}, f32[2048]{0:T(1024)}, u32[]{:S(2)}) copy-start(f32[2048]{0:T(1024)} %param.19) | copy-start | bytes 24580
  49.7 12.9 %collective-permute-start.8 = (bf16[64,2176]{1,0:T(8,128)(2,1)S(1)}, bf16[64,2176]{1,0:T(8,128)(2,1)S(1)}, u32[]{:S(2)}, u32[]{:S(2)}) collective-permute-start(bf16[64,2176]{1,0:T(8,128)(2,1)S(1)} %total.1.refs_0_.own_ref), channel_id=1, source_target_pairs={{0,4},{12,8},{4,0},{8,12},{1,5},{13,9},{5,1},{9,13},{2,6},{14,10},... | collective-permute-start | bytes 835592 | tf_op jit(solution)/shard_map/ppermute | solution.py:730
  55.0 3.8 %collective-permute-start.9 = (f32[32,64]{1,0:T(8,128)S(1)}, f32[32,64]{1,0:T(8,128)S(1)}, u32[]{:S(2)}, u32[]{:S(2)}) collective-permute-start(f32[32,64]{1,0:T(8,128)S(1)} %add.10.first_ref), channel_id=1, source_target_pairs={{0,2},{1,3},{2,0},{3,1},{4,6},{5,7},{6,4},{7,5},{8,10},{9,11},{10,... | collective-permute-start | bytes 24584 | tf_op jit(solution)/shard_map/ppermute | solution.py:846
  58.9 3.7 %collective-permute-start.10 = (f32[32,64]{1,0:T(8,128)S(1)}, f32[32,64]{1,0:T(8,128)S(1)}, u32[]{:S(2)}, u32[]{:S(2)}) collective-permute-start(f32[32,64]{1,0:T(8,128)S(1)} %add.11.first_ref), channel_id=1, source_target_pairs={{0,4},{12,8},{4,0},{8,12},{1,5},{13,9},{5,1},{9,13},{2,6},{14,10},... | collective-permute-start | bytes 24584 | tf_op jit(solution)/shard_map/ppermute | solution.py:730

commit v18 on v17

--- a/solution.py
+++ b/solution.py
@@ -872,7 +872,6 @@
         )(*before, rank, x_one, x_two, values, grad_out, skip_row, conv, corr, late, part_come)
 
     grads = gates(False, total)
-    first, _ = lax.optimization_barrier((first, grads[0]))
     first = swapped(first, bits[1:])
     first_come = move(first, inward + outward)
     grad_one, grad_two, grad_value = gates(True, *grads)

time: 63.7 us -> 62 us (0.973)
  waiting for transfers between devices: 25.9 us -> 24.1 us
    ppermute x9, waiting for transfers between devices: 22.5 us -> 20.7 us  [move(): return lax.ppermute(array, 'ctx', pairs)]
  transfers between devices with their start and end apart: 11 -> 11, of which waited for: 6 -> 6; matrix products, arithmetic and copies ran while one was open for 0% -> 0% of each run, Pallas kernels for 29% -> 30%
where the time goes in v18:
time: 62 us; the launch traced here: 61.7 us
  waiting for transfers between devices  24.1 us (39%)
  Pallas kernels  22 us (35%)
  starting transfers between devices  14.4 us (23%)
  between operations  1.02 us (2%)
    ppermute x9, waiting for transfers between devices, move(): return lax.ppermute(array, 'ctx', pairs)  20.7 us
    ppermute x9, starting transfers between devices, move(): return lax.ppermute(array, 'ctx', pairs)  12.9 us
    pallas_call x1, Pallas kernels, few_shards_body(): call(functools.partial(filters_kernel, rows, shards, blocks, width), 'fil...  6.51 us
    pallas_call x1, Pallas kernels, few_shards_body(): call(only(False, shards, 0, functools.partial(own_kernel, rows, shards, c...  6.2 us
    pallas_call x1, Pallas kernels, few_shards_body(): call(functools.partial(near_kernel, rows, shards, blocks, width), 'near_b...  3.82 us
    ppermute x2, waiting for transfers between devices, swapped(): lax.ppermute(array, ('ch', 'sub'), [(i, i ^ bit) for i in range(group)])  3.4 us
    pallas_call x1, Pallas kernels, few_shards_body(): pl.pallas_call(products_kernel, grid=(rows // row_step,), in_specs=[smem]...  2.79 us
    pallas_call x2, Pallas kernels, gates(): call(only(inner, shards, len(before), functools.partial(gates_kernel, inn...  1.76 us
  transfers between devices with their start and end apart: 11, of which 6 were waited for; matrix products, arithmetic and copies ran while one was open for 0% of the time, Pallas kernels for 30%

profile of v18, /device:TPU:0, one launch (start us, length us, event | category | flops | bytes accessed | tf_op | source)
XLA Modules:
  0.0 61.7 jit_solution(8693961035596765462)
XLA Ops:
  0.6 2.8 %products.1 = (bf16[128,2048]{1,0:T(8,128)(2,1)}, bf16[128,2048]{1,0:T(8,128)(2,1)}, bf16[128,2048]{1,0:T(8,128)(2,1)}, f32[1,2048]{1,0:T(1,128)}) custom-call(s32[1]{0:T(128)} %bitcast.rank_ref.refs_0_.refs_1_.refs_3_, bf16[128,2048]{1,0:T(8,128)(2,1)} %refs_4_.6, bf16[128,2048]{1,0:T(8,128)(2,1)} %refs_5_.5, bf16[128,2048]{1,0:T(8,128)(2,1)} %refs_6_.2, ...), custom_call_target="tpu_custom_call" | custom-call | tf_op jit(solution)/shard_map/products/pallas_call | solution.py:742
  3.4 3.1 %collective-permute-start.1 = (bf16[128,2048]{1,0:T(8,128)(2,1)}, bf16[128,2048]{1,0:T(8,128)(2,1)S(1)}, u32[]{:S(2)}, u32[]{:S(2)}) collective-permute-start(bf16[128,2048]{1,0:T(8,128)(2,1)} %get-tuple-element.35.refs_3_.pair_ref), channel_id=1, source_target_pairs={{0,4},{12,8},{4,0},{8,12},{1,5},{13,9},{5,1},{9,13},{2,6},{14,10},... | collective-permute-start | bytes 1572872 | tf_op jit(solution)/shard_map/ppermute | solution.py:730
  6.5 0.7 %collective-permute-start.2 = (bf16[128,2048]{1,0:T(8,128)(2,1)}, bf16[128,2048]{1,0:T(8,128)(2,1)S(1)}, u32[]{:S(2)}, u32[]{:S(2)}) collective-permute-start(bf16[128,2048]{1,0:T(8,128)(2,1)} %get-tuple-element.36.refs_4_.other_ref), channel_id=1, source_target_pairs={{4,8},{8,4},{5,9},{9,5},{6,10},{10,6},{7,11},{11,7},{20,24},{24,20... | collective-permute-start | bytes 1572872 | tf_op jit(solution)/shard_map/ppermute | solution.py:730
  7.2 0.0 copy-start.5
  7.2 0.0 copy-start.6
  7.2 0.0 copy-start.9
  7.2 0.0 copy-start.13
  7.2 0.0 copy-start.14
  7.3 6.2 %own_pair.1 = bf16[64,2176]{1,0:T(8,128)(2,1)} custom-call(s32[1]{0:T(128)} %bitcast.rank_ref.refs_0_.refs_1_.refs_3_, f32[128,32]{1,0:T(8,128)} %constant.15.clone.refs_1_, f32[32,64]{1,0:T(8,128)} %first_ref.1, bf16[128,2048]{1,0:T(8,128)(2,1)} %get-tuple-element.35.refs_3_.pair_ref, bf16[128,2048]{1,0:T(8,128)(2,1)} %get-tuple-element.36.refs_4_.other_ref, ...), custom_call_target="tpu_custom_call" | custom-call | flops 2147483648 | bytes 262144 | tf_op jit(solution)/shard_map/own_pair/pallas_call | solution.py:759
  13.5 0.0 copy-done.5
  13.5 0.0 copy-done.6
  13.5 0.0 copy-done.9
  13.5 0.0 copy-done.13
  13.5 0.0 copy-done.14
  13.5 0.0 copy-start.15
  13.5 0.0 copy-start.16
  13.5 0.0 copy-start.4
  13.6 0.0 copy-start.7
  13.6 0.0 copy-start.11
  13.6 0.0 copy-start.12
  13.6 6.5 %filters.1 = (bf16[4,256,2048]{2,1,0:T(8,128)(2,1)S(1)}, bf16[128,512]{1,0:T(8,128)(2,1)S(1)}, f32[512,64]{1,0:T(8,128)S(1)}) custom-call(f32[512,32]{1,0:T(8,128)S(1)} %copy-done.14, f32[32,64]{1,0:T(8,128)S(1)} %copy-done.13, f32[64,2048]{1,0:T(8,128)S(1)} %copy-done.5, f32[1,2048]{1,0:T(1,128)S(1)} %bitcast.7, bf16[256,256]{1,0:T(8,128)(2,1)S(1)} %copy-done.6), custom_call_target="tpu_custom_call" | custom-call | flops 2147483648 | bytes 262144 | tf_op jit(solution)/shard_map/filters/pallas_call | solution.py:773
  20.1 0.0 copy-done.15
  20.1 1.3 %collective-permute-start = (bf16[128,2048]{1,0:T(8,128)(2,1)S(1)}, bf16[128,2048]{1,0:T(8,128)(2,1)S(1)}, u32[]{:S(2)}, u32[]{:S(2)}) collective-permute-start(bf16[128,2048]{1,0:T(8,128)(2,1)S(1)} %copy-done.15), channel_id=1, source_target_pairs={{0,8},{12,4},{1,9},{13,5},{2,10},{14,6},{3,11},{15,7},{16,24},{28,... | collective-permute-start | bytes 1572872 | tf_op jit(solution)/shard_map/ppermute | solution.py:730
  21.4 0.0 copy-done.16
  21.5 1.3 %collective-permute-start.4 = (bf16[64,2176]{1,0:T(8,128)(2,1)S(1)}, bf16[64,2176]{1,0:T(8,128)(2,1)S(1)}, u32[]{:S(2)}, u32[]{:S(2)}) collective-permute-start(bf16[64,2176]{1,0:T(8,128)(2,1)S(1)} %copy-done.16), channel_id=1, source_target_pairs={{0,4},{12,8},{1,5},{13,9},{2,6},{14,10},{3,7},{15,11},{16,20},{28,... | collective-permute-start | bytes 835592 | tf_op jit(solution)/shard_map/ppermute | solution.py:730
  22.8 0.0 collective-permute-done.1.pair_in_ref
  22.8 0.0 collective-permute-done.2.middle_in_ref
  22.8 0.0 copy-done.4
  22.8 0.0 copy-done.7
  22.8 0.0 copy-done.11
  22.8 0.0 copy-done.12
  22.8 3.8 %near_blocks.1 = (f32[128,2048]{1,0:T(8,128)S(1)}, f32[128,2048]{1,0:T(8,128)S(1)}, f32[128,2048]{1,0:T(8,128)S(1)}, f32[64,2048]{1,0:T(8,128)S(1)}, f32[32,64]{1,0:T(8,128)S(1)}, /*index=5*/f32[256,2048]{1,0:T(8,128)S(1)}) custom-call(s32[1]{0:T(128)} %bitcast.rank_ref.refs_0_.refs_1_.refs_3_, bf16[128,2048]{1,0:T(8,128)(2,1)S(1)} %copy-done.11, ...), custom_call_target="tpu_custom_call" | custom-call | flops 5368709120 | bytes 262144 | tf_op jit(solution)/shard_map/near_blocks/pallas_call | solution.py:785
  26.7 7.1 %collective-permute-done.refs_1_ = bf16[128,2048]{1,0:T(8,128)(2,1)S(1)} collective-permute-done((bf16[128,2048]{1,0:T(8,128)(2,1)S(1)}, bf16[128,2048]{1,0:T(8,128)(2,1)S(1)}, u32[]{:S(2)}, u32[]{:S(2)}) %collective-permute-start) | collective-permute-done | bytes 524320 | tf_op jit(solution)/shard_map/ppermute | solution.py:730
  33.7 0.0 copy-start.10
  33.7 1.4 %collective-permute-start.3 = (bf16[128,2048]{1,0:T(8,128)(2,1)S(1)}, bf16[128,2048]{1,0:T(8,128)(2,1)S(1)}, u32[]{:S(2)}, u32[]{:S(2)}) collective-permute-start(bf16[128,2048]{1,0:T(8,128)(2,1)S(1)} %get-tuple-element.44.refs_0_), channel_id=1, source_target_pairs={{4,0},{8,12},{5,1},{9,13},{6,2},{10,14},{7,3},{11,15},{20,16},{24,... | collective-permute-start | bytes 1572872 | tf_op jit(solution)/shard_map/ppermute | solution.py:730
  35.1 3.4 %collective-permute-done.4.refs_13_ = bf16[64,2176]{1,0:T(8,128)(2,1)S(1)} collective-permute-done((bf16[64,2176]{1,0:T(8,128)(2,1)S(1)}, bf16[64,2176]{1,0:T(8,128)(2,1)S(1)}, u32[]{:S(2)}, u32[]{:S(2)}) %collective-permute-start.4) | collective-permute-done | bytes 278560 | tf_op jit(solution)/shard_map/ppermute | solution.py:730
  38.5 0.0 copy-done.10
  38.5 0.7 %collective-permute-start.7 = (bf16[64,2176]{1,0:T(8,128)(2,1)S(1)}, bf16[64,2176]{1,0:T(8,128)(2,1)S(1)}, u32[]{:S(2)}, u32[]{:S(2)}) collective-permute-start(bf16[64,2176]{1,0:T(8,128)(2,1)S(1)} %get-tuple-element.50.own_ref), channel_id=1, source_target_pairs={{4,8},{8,4},{0,0},{12,12},{5,9},{9,5},{1,1},{13,13},{6,10},{10,6},... | collective-permute-start | bytes 835592 | tf_op jit(solution)/shard_map/ppermute | solution.py:730
  39.2 0.1 collective-permute-start.5
  39.3 1.2 %collective-permute-done.5 = f32[32,64]{1,0:T(8,128)S(1)} collective-permute-done((f32[32,64]{1,0:T(8,128)S(1)}, f32[32,64]{1,0:T(8,128)S(1)}, u32[]{:S(2)}, u32[]{:S(2)}) %collective-permute-start.5) | collective-permute-done | bytes 8224 | tf_op jit(solution)/shard_map/ppermute | solution.py:846
  40.5 0.7 %collective-permute-start.6 = (f32[32,64]{1,0:T(8,128)S(1)}, f32[32,64]{1,0:T(8,128)S(1)}, u32[]{:S(2)}, u32[]{:S(2)}) collective-permute-start(f32[32,64]{1,0:T(8,128)S(1)} %add.9), channel_id=1, source_target_pairs={{4,8},{8,4},{0,0},{12,12},{5,9},{9,5},{1,1},{13,13},{6,10},{10,6},... | collective-permute-start | bytes 24584 | tf_op jit(solution)/shard_map/ppermute | solution.py:730
  41.2 0.0 copy-start
  41.2 0.0 copy-start.1
  41.2 0.0 copy-start.2
  41.2 0.0 copy-start.3
  41.2 0.0 copy-start.8
  41.2 0.0 collective-permute-done.6
  41.2 0.0 collective-permute-done.7.come_ref
  41.2 8.4 %collective-permute-done.3.part_ref.refs_10_.refs_12_ = bf16[128,2048]{1,0:T(8,128)(2,1)S(1)} collective-permute-done((bf16[128,2048]{1,0:T(8,128)(2,1)S(1)}, bf16[128,2048]{1,0:T(8,128)(2,1)S(1)}, u32[]{:S(2)}, u32[]{:S(2)}) %collective-permute-start.3) | collective-permute-done | bytes 524320 | tf_op jit(solution)/shard_map/ppermute | solution.py:730
  49.6 0.1 total.1.refs_0_.own_ref
  49.7 3.7 %collective-permute-start.8 = (bf16[64,2176]{1,0:T(8,128)(2,1)S(1)}, bf16[64,2176]{1,0:T(8,128)(2,1)S(1)}, u32[]{:S(2)}, u32[]{:S(2)}) collective-permute-start(bf16[64,2176]{1,0:T(8,128)(2,1)S(1)} %total.1.refs_0_.own_ref), channel_id=1, source_target_pairs={{0,4},{12,8},{4,0},{8,12},{1,5},{13,9},{5,1},{9,13},{2,6},{14,10},... | collective-permute-start | bytes 835592 | tf_op jit(solution)/shard_map/ppermute | solution.py:730
  53.4 1.5 %collective-permute-start.9 = (f32[32,64]{1,0:T(8,128)S(1)}, f32[32,64]{1,0:T(8,128)S(1)}, u32[]{:S(2)}, u32[]{:S(2)}) collective-permute-start(f32[32,64]{1,0:T(8,128)S(1)} %add.10.first_ref), channel_id=1, source_target_pairs={{0,2},{1,3},{2,0},{3,1},{4,6},{5,7},{6,4},{7,5},{8,10},{9,11},{10,... | collective-permute-start | bytes 24584 | tf_op jit(solution)/shard_map/ppermute | solution.py:846
  54.9 2.2 %collective-permute-done.9 = f32[32,64]{1,0:T(8,128)S(1)} collective-permute-done((f32[32,64]{1,0:T(8,128)S(1)}, f32[32,64]{1,0:T(8,128)S(1)}, u32[]{:S(2)}, u32[]{:S(2)}) %collective-permute-start.9) | collective-permute-done | bytes 8224 | tf_op jit(solution)/shard_map/ppermute | solution.py:846
  57.1 0.1 collective-permute-start.10
  57.2 0.0 copy-done
  57.2 0.0 copy-done.1
  57.2 0.0 copy-done.2
  57.2 0.0 copy-done.3
  57.2 0.0 copy-done.8
  57.2 1.6 %gates.2 = (bf16[128,2048]{1,0:T(8,128)(2,1)}, bf16[128,2048]{1,0:T(8,128)(2,1)}, bf16[128,2048]{1,0:T(8,128)(2,1)}) custom-call(bf16[64,2176]{1,0:T(8,128)(2,1)S(1)} %total.1.refs_0_.own_ref, s32[1]{0:T(128)} %bitcast.rank_ref.refs_0_.refs_1_.refs_3_, bf16[128,2048]{1,0:T(8,128)(2,1)S(1)} %copy-done, bf16[128,2048]{1,0:T(8,128)(2,1)S(1)} %copy-done.1, ...), custom_call_target="tpu_custom_call" | custom-call | bytes 262144 | tf_op jit(solution)/shard_map/gates/pallas_call | solution.py:861
  58.9 0.1 gates.3
  59.0 1.9 %collective-permute-done.10.first_come_ref = f32[32,64]{1,0:T(8,128)S(1)} collective-permute-done((f32[32,64]{1,0:T(8,128)S(1)}, f32[32,64]{1,0:T(8,128)S(1)}, u32[]{:S(2)}, u32[]{:S(2)}) %collective-permute-start.10) | collective-permute-done | bytes 8224 | tf_op jit(solution)/shard_map/ppermute | solution.py:730
  60.9 0.0 collective-permute-done.8.come_ref
  60.9 0.9 %finish.1 = (f32[64,2048]{1,0:T(8,128)}, f32[32,64]{1,0:T(8,128)}, f32[1,2048]{1,0:T(1,128)}) custom-call(s32[1]{0:T(128)} %bitcast.rank_ref.refs_0_.refs_1_.refs_3_, bf16[64,2176]{1,0:T(8,128)(2,1)S(1)} %total.1.refs_0_.own_ref, bf16[64,2176]{1,0:T(8,128)(2,1)S(1)} %collective-permute-done.8.come_ref, f32[32,64]{1,0:T(8,128)S(1)} %add.11.first_ref, ...), custom_call_target="tpu_custom_call" | custom-call | bytes 262144 | tf_op jit(solution)/shard_map/finish/pallas_call | solution.py:880
  (6 shorter events, 0.0 us)
Async XLA Ops:
  3.4 19.3 %collective-permute-start.1 = (bf16[128,2048]{1,0:T(8,128)(2,1)}, bf16[128,2048]{1,0:T(8,128)(2,1)S(1)}, u32[]{:S(2)}, u32[]{:S(2)}) collective-permute-start(bf16[128,2048]{1,0:T(8,128)(2,1)} %get-tuple-element.35.refs_3_.pair_ref), channel_id=1, source_target_pairs={{0,4},{12,8},{4,0},{8,12},{1,5},{13,9},{5,1},{9,13},{2,6},{14,10},... | collective-permute-start | bytes 1572872 | tf_op jit(solution)/shard_map/ppermute | solution.py:730
  6.5 16.3 %collective-permute-start.2 = (bf16[128,2048]{1,0:T(8,128)(2,1)}, bf16[128,2048]{1,0:T(8,128)(2,1)S(1)}, u32[]{:S(2)}, u32[]{:S(2)}) collective-permute-start(bf16[128,2048]{1,0:T(8,128)(2,1)} %get-tuple-element.36.refs_4_.other_ref), channel_id=1, source_target_pairs={{4,8},{8,4},{5,9},{9,5},{6,10},{10,6},{7,11},{11,7},{20,24},{24,20... | collective-permute-start | bytes 1572872 | tf_op jit(solution)/shard_map/ppermute | solution.py:730
  7.2 6.3 %copy-start.5 = (f32[64,2048]{1,0:T(8,128)S(1)}, f32[64,2048]{1,0:T(8,128)}, u32[]{:S(2)}) copy-start(f32[64,2048]{1,0:T(8,128)} %refs_4_.4) | copy-start | bytes 1572868
  7.2 6.3 %copy-start.6 = (bf16[256,256]{1,0:T(8,128)(2,1)S(1)}, bf16[256,256]{1,0:T(8,128)(2,1)}, u32[]{:S(2)}) copy-start(bf16[256,256]{1,0:T(8,128)(2,1)} %constant.16.clone.refs_7_.front_ref.refs_3_) | copy-start | bytes 393220
  7.2 6.3 %copy-start.9 = (f32[2048]{0:T(1024)S(1)}, f32[2048]{0:T(1024)}, u32[]{:S(2)}) copy-start(f32[2048]{0:T(1024)} %param.20) | copy-start | bytes 24580
  7.2 6.3 %copy-start.13 = (f32[32,64]{1,0:T(8,128)S(1)}, f32[32,64]{1,0:T(8,128)}, u32[]{:S(2)}) copy-start(f32[32,64]{1,0:T(8,128)} %first_ref.1) | copy-start | bytes 24580
  7.2 6.3 %copy-start.14 = (f32[512,32]{1,0:T(8,128)S(1)}, f32[512,32]{1,0:T(8,128)}, u32[]{:S(2)}) copy-start(f32[512,32]{1,0:T(8,128)} %constant.19.clone.feats_ref) | copy-start | bytes 196612
  13.5 6.6 %copy-start.15 = (bf16[128,2048]{1,0:T(8,128)(2,1)S(1)}, bf16[128,2048]{1,0:T(8,128)(2,1)}, u32[]{:S(2)}) copy-start(bf16[128,2048]{1,0:T(8,128)(2,1)} %get-tuple-element.40) | copy-start | bytes 1572868
  13.5 7.9 %copy-start.16 = (bf16[64,2176]{1,0:T(8,128)(2,1)S(1)}, bf16[64,2176]{1,0:T(8,128)(2,1)}, u32[]{:S(2)}) copy-start(bf16[64,2176]{1,0:T(8,128)(2,1)} %own_pair.1) | copy-start | bytes 835588
  13.5 9.3 %copy-start.4 = (bf16[256,256]{1,0:T(8,128)(2,1)S(1)}, bf16[256,256]{1,0:T(8,128)(2,1)}, u32[]{:S(2)}) copy-start(bf16[256,256]{1,0:T(8,128)(2,1)} %constant.17.clone.refs_8_.back_ref.refs_4_.refs_6_.refs_3_) | copy-start | bytes 393220
  13.6 9.2 %copy-start.7 = (f32[32,512]{1,0:T(8,128)S(1)}, f32[32,512]{1,0:T(8,128)}, u32[]{:S(2)}) copy-start(f32[32,512]{1,0:T(8,128)} %constant.18.clone.refs_9_.featt_ref.refs_8_) | copy-start | bytes 196612
  13.6 9.2 %copy-start.11 = (bf16[128,2048]{1,0:T(8,128)(2,1)S(1)}, bf16[128,2048]{1,0:T(8,128)(2,1)}, u32[]{:S(2)}) copy-start(bf16[128,2048]{1,0:T(8,128)(2,1)} %get-tuple-element.35.refs_3_.pair_ref) | copy-start | bytes 1572868
  13.6 9.2 %copy-start.12 = (bf16[128,2048]{1,0:T(8,128)(2,1)S(1)}, bf16[128,2048]{1,0:T(8,128)(2,1)}, u32[]{:S(2)}) copy-start(bf16[128,2048]{1,0:T(8,128)(2,1)} %get-tuple-element.36.refs_4_.other_ref) | copy-start | bytes 1572868
  20.1 13.6 %collective-permute-start = (bf16[128,2048]{1,0:T(8,128)(2,1)S(1)}, bf16[128,2048]{1,0:T(8,128)(2,1)S(1)}, u32[]{:S(2)}, u32[]{:S(2)}) collective-permute-start(bf16[128,2048]{1,0:T(8,128)(2,1)S(1)} %copy-done.15), channel_id=1, source_target_pairs={{0,8},{12,4},{1,9},{13,5},{2,10},{14,6},{3,11},{15,7},{16,24},{28,... | collective-permute-start | bytes 1572872 | tf_op jit(solution)/shard_map/ppermute | solution.py:730
  21.5 17.1 %collective-permute-start.4 = (bf16[64,2176]{1,0:T(8,128)(2,1)S(1)}, bf16[64,2176]{1,0:T(8,128)(2,1)S(1)}, u32[]{:S(2)}, u32[]{:S(2)}) collective-permute-start(bf16[64,2176]{1,0:T(8,128)(2,1)S(1)} %copy-done.16), channel_id=1, source_target_pairs={{0,4},{12,8},{1,5},{13,9},{2,6},{14,10},{3,7},{15,11},{16,20},{28,... | collective-permute-start | bytes 835592 | tf_op jit(solution)/shard_map/ppermute | solution.py:730
  33.7 4.8 %copy-start.10 = (f32[1,2048]{1,0:T(1,128)S(1)}, f32[1,2048]{1,0:T(1,128)}, u32[]{:S(2)}) copy-start(f32[1,2048]{1,0:T(1,128)} %get-tuple-element.37.refs_10_.refs_12_) | copy-start | bytes 24580
  33.7 15.9 %collective-permute-start.3 = (bf16[128,2048]{1,0:T(8,128)(2,1)S(1)}, bf16[128,2048]{1,0:T(8,128)(2,1)S(1)}, u32[]{:S(2)}, u32[]{:S(2)}) collective-permute-start(bf16[128,2048]{1,0:T(8,128)(2,1)S(1)} %get-tuple-element.44.refs_0_), channel_id=1, source_target_pairs={{4,0},{8,12},{5,1},{9,13},{6,2},{10,14},{7,3},{11,15},{20,16},{24,... | collective-permute-start | bytes 1572872 | tf_op jit(solution)/shard_map/ppermute | solution.py:730
  38.5 2.7 %collective-permute-start.7 = (bf16[64,2176]{1,0:T(8,128)(2,1)S(1)}, bf16[64,2176]{1,0:T(8,128)(2,1)S(1)}, u32[]{:S(2)}, u32[]{:S(2)}) collective-permute-start(bf16[64,2176]{1,0:T(8,128)(2,1)S(1)} %get-tuple-element.50.own_ref), channel_id=1, source_target_pairs={{4,8},{8,4},{0,0},{12,12},{5,9},{9,5},{1,1},{13,13},{6,10},{10,6},... | collective-permute-start | bytes 835592 | tf_op jit(solution)/shard_map/ppermute | solution.py:730
  39.2 1.2 %collective-permute-start.5 = (f32[32,64]{1,0:T(8,128)S(1)}, f32[32,64]{1,0:T(8,128)S(1)}, u32[]{:S(2)}, u32[]{:S(2)}) collective-permute-start(f32[32,64]{1,0:T(8,128)S(1)} %get-tuple-element.49), channel_id=1, source_target_pairs={{0,1},{1,0},{2,3},{3,2},{4,5},{5,4},{6,7},{7,6},{8,9},{9,8},{10,11... | collective-permute-start | bytes 24584 | tf_op jit(solution)/shard_map/ppermute | solution.py:846
  40.5 0.7 %collective-permute-start.6 = (f32[32,64]{1,0:T(8,128)S(1)}, f32[32,64]{1,0:T(8,128)S(1)}, u32[]{:S(2)}, u32[]{:S(2)}) collective-permute-start(f32[32,64]{1,0:T(8,128)S(1)} %add.9), channel_id=1, source_target_pairs={{4,8},{8,4},{0,0},{12,12},{5,9},{9,5},{1,1},{13,13},{6,10},{10,6},... | collective-permute-start | bytes 24584 | tf_op jit(solution)/shard_map/ppermute | solution.py:730
  41.2 16.1 %copy-start = (bf16[128,2048]{1,0:T(8,128)(2,1)S(1)}, bf16[128,2048]{1,0:T(8,128)(2,1)}, u32[]{:S(2)}) copy-start(bf16[128,2048]{1,0:T(8,128)(2,1)} %refs_4_.6) | copy-start | bytes 1572868
  41.2 16.0 %copy-start.1 = (bf16[128,2048]{1,0:T(8,128)(2,1)S(1)}, bf16[128,2048]{1,0:T(8,128)(2,1)}, u32[]{:S(2)}) copy-start(bf16[128,2048]{1,0:T(8,128)(2,1)} %refs_5_.5) | copy-start | bytes 1572868
  41.2 16.0 %copy-start.2 = (bf16[128,2048]{1,0:T(8,128)(2,1)S(1)}, bf16[128,2048]{1,0:T(8,128)(2,1)}, u32[]{:S(2)}) copy-start(bf16[128,2048]{1,0:T(8,128)(2,1)} %refs_6_.2) | copy-start | bytes 1572868
  41.2 16.0 %copy-start.3 = (bf16[128,2048]{1,0:T(8,128)(2,1)S(1)}, bf16[128,2048]{1,0:T(8,128)(2,1)}, u32[]{:S(2)}) copy-start(bf16[128,2048]{1,0:T(8,128)(2,1)} %refs_7_.2) | copy-start | bytes 1572868
  41.2 16.0 %copy-start.8 = (f32[2048]{0:T(1024)S(1)}, f32[2048]{0:T(1024)}, u32[]{:S(2)}) copy-start(f32[2048]{0:T(1024)} %param.19) | copy-start | bytes 24580
  49.7 11.2 %collective-permute-start.8 = (bf16[64,2176]{1,0:T(8,128)(2,1)S(1)}, bf16[64,2176]{1,0:T(8,128)(2,1)S(1)}, u32[]{:S(2)}, u32[]{:S(2)}) collective-permute-start(bf16[64,2176]{1,0:T(8,128)(2,1)S(1)} %total.1.refs_0_.own_ref), channel_id=1, source_target_pairs={{0,4},{12,8},{4,0},{8,12},{1,5},{13,9},{5,1},{9,13},{2,6},{14,10},... | collective-permute-start | bytes 835592 | tf_op jit(solution)/shard_map/ppermute | solution.py:730
  53.4 3.7 %collective-permute-start.9 = (f32[32,64]{1,0:T(8,128)S(1)}, f32[32,64]{1,0:T(8,128)S(1)}, u32[]{:S(2)}, u32[]{:S(2)}) collective-permute-start(f32[32,64]{1,0:T(8,128)S(1)} %add.10.first_ref), channel_id=1, source_target_pairs={{0,2},{1,3},{2,0},{3,1},{4,6},{5,7},{6,4},{7,5},{8,10},{9,11},{10,... | collective-permute-start | bytes 24584 | tf_op jit(solution)/shard_map/ppermute | solution.py:846
  57.1 3.7 %collective-permute-start.10 = (f32[32,64]{1,0:T(8,128)S(1)}, f32[32,64]{1,0:T(8,128)S(1)}, u32[]{:S(2)}, u32[]{:S(2)}) collective-permute-start(f32[32,64]{1,0:T(8,128)S(1)} %add.11.first_ref), channel_id=1, source_target_pairs={{0,4},{12,8},{4,0},{8,12},{1,5},{13,9},{5,1},{9,13},{2,6},{14,10},... | collective-permute-start | bytes 24584 | tf_op jit(solution)/shard_map/ppermute | solution.py:730

commit v19 on v18

--- a/solution.py
+++ b/solution.py
@@ -843,7 +843,11 @@
 
     def swapped(array, bits):
         for bit in bits:
-            array = array + lax.ppermute(array, ("ch", "sub"), [(i, i ^ bit) for i in range(group)])
+            pairs = [
+                (c * group + i, c * group + (i ^ bit if 0 < c < shards - 1 else i))
+                for c in range(shards) for i in range(group)
+            ]
+            array = array + lax.ppermute(array, ("ctx", "ch", "sub"), pairs)
         return array
 
     bits = [1 << i for i in range(group.bit_length() - 1)]

time: 62 us -> 63.9 us (1.031)
  starting transfers between devices: 14.4 us -> 20.9 us
  waiting for transfers between devices: 24.1 us -> 19.4 us
    ppermute x9, starting transfers between devices: 12.9 us -> 19.6 us  [move(): return lax.ppermute(array, 'ctx', pairs)]
    ppermute x2, waiting for transfers between devices: 3.4 us -> 0.01 us  [swapped(): array = array + lax.ppermute(array, ('ctx', 'ch', 'sub'), pairs)]
    ppermute x9, waiting for transfers between devices: 20.7 us -> 19.4 us  [move(): return lax.ppermute(array, 'ctx', pairs)]
  transfers between devices with their start and end apart: 11 -> 11, of which waited for: 6 -> 3; matrix products, arithmetic and copies ran while one was open for 0% -> 0% of each run, Pallas kernels for 30% -> 29%
where the time goes in v19:
time: 63.9 us; the launch traced here: 63.5 us
  Pallas kernels  22 us (34%)
  starting transfers between devices  20.9 us (33%)
  waiting for transfers between devices  19.4 us (30%)
  between operations  1.07 us (2%)
    ppermute x9, starting transfers between devices, move(): return lax.ppermute(array, 'ctx', pairs)  19.6 us
    ppermute x9, waiting for transfers between devices, move(): return lax.ppermute(array, 'ctx', pairs)  19.4 us
    pallas_call x1, Pallas kernels, few_shards_body(): call(functools.partial(filters_kernel, rows, shards, blocks, width), 'fil...  6.51 us
    pallas_call x1, Pallas kernels, few_shards_body(): call(only(False, shards, 0, functools.partial(own_kernel, rows, shards, c...  6.2 us
    pallas_call x1, Pallas kernels, few_shards_body(): call(functools.partial(near_kernel, rows, shards, blocks, width), 'near_b...  3.82 us
    pallas_call x1, Pallas kernels, few_shards_body(): pl.pallas_call(products_kernel, grid=(rows // row_step,), in_specs=[smem]...  2.79 us
    pallas_call x2, Pallas kernels, gates(): call(only(inner, shards, len(before), functools.partial(gates_kernel, inn...  1.76 us
    ppermute x2, starting transfers between devices, swapped(): array = array + lax.ppermute(array, ('ctx', 'ch', 'sub'), pairs)  1.31 us
  transfers between devices with their start and end apart: 11, of which 3 were waited for; matrix products, arithmetic and copies ran while one was open for 0% of the time, Pallas kernels for 29%

profile of v19, /device:TPU:0, one launch (start us, length us, event | category | flops | bytes accessed | tf_op | source)
XLA Modules:
  0.0 63.5 jit_solution(1256063885846601406)
XLA Ops:
  0.6 2.8 %products.1 = (bf16[128,2048]{1,0:T(8,128)(2,1)}, bf16[128,2048]{1,0:T(8,128)(2,1)}, bf16[128,2048]{1,0:T(8,128)(2,1)}, f32[1,2048]{1,0:T(1,128)}) custom-call(s32[1]{0:T(128)} %bitcast.rank_ref.refs_0_.refs_1_.refs_3_, bf16[128,2048]{1,0:T(8,128)(2,1)} %refs_4_.6, bf16[128,2048]{1,0:T(8,128)(2,1)} %refs_5_.5, bf16[128,2048]{1,0:T(8,128)(2,1)} %refs_6_.2, ...), custom_call_target="tpu_custom_call" | custom-call | tf_op jit(solution)/shard_map/products/pallas_call | solution.py:742
  3.4 3.1 %collective-permute-start.1 = (bf16[128,2048]{1,0:T(8,128)(2,1)}, bf16[128,2048]{1,0:T(8,128)(2,1)S(1)}, u32[]{:S(2)}, u32[]{:S(2)}) collective-permute-start(bf16[128,2048]{1,0:T(8,128)(2,1)} %get-tuple-element.35.refs_3_.pair_ref), channel_id=1, source_target_pairs={{0,4},{12,8},{4,0},{8,12},{1,5},{13,9},{5,1},{9,13},{2,6},{14,10},... | collective-permute-start | bytes 1572872 | tf_op jit(solution)/shard_map/ppermute | solution.py:730
  6.5 0.7 %collective-permute-start.2 = (bf16[128,2048]{1,0:T(8,128)(2,1)}, bf16[128,2048]{1,0:T(8,128)(2,1)S(1)}, u32[]{:S(2)}, u32[]{:S(2)}) collective-permute-start(bf16[128,2048]{1,0:T(8,128)(2,1)} %get-tuple-element.36.refs_4_.other_ref), channel_id=1, source_target_pairs={{4,8},{8,4},{5,9},{9,5},{6,10},{10,6},{7,11},{11,7},{20,24},{24,20... | collective-permute-start | bytes 1572872 | tf_op jit(solution)/shard_map/ppermute | solution.py:730
  7.2 0.0 copy-start.5
  7.2 0.0 copy-start.6
  7.2 0.0 copy-start.9
  7.2 0.0 copy-start.13
  7.2 0.0 copy-start.14
  7.3 6.2 %own_pair.1 = bf16[64,2176]{1,0:T(8,128)(2,1)} custom-call(s32[1]{0:T(128)} %bitcast.rank_ref.refs_0_.refs_1_.refs_3_, f32[128,32]{1,0:T(8,128)} %constant.15.clone.refs_1_, f32[32,64]{1,0:T(8,128)} %first_ref.1, bf16[128,2048]{1,0:T(8,128)(2,1)} %get-tuple-element.35.refs_3_.pair_ref, bf16[128,2048]{1,0:T(8,128)(2,1)} %get-tuple-element.36.refs_4_.other_ref, ...), custom_call_target="tpu_custom_call" | custom-call | flops 2147483648 | bytes 262144 | tf_op jit(solution)/shard_map/own_pair/pallas_call | solution.py:759
  13.5 0.0 copy-done.5
  13.5 0.0 copy-done.6
  13.5 0.0 copy-done.9
  13.5 0.0 copy-done.13
  13.5 0.0 copy-done.14
  13.5 0.0 copy-start.15
  13.5 0.0 copy-start.16
  13.5 0.0 copy-start.4
  13.6 0.0 copy-start.7
  13.6 0.0 copy-start.11
  13.6 0.0 copy-start.12
  13.6 6.5 %filters.1 = (bf16[4,256,2048]{2,1,0:T(8,128)(2,1)S(1)}, bf16[128,512]{1,0:T(8,128)(2,1)S(1)}, f32[512,64]{1,0:T(8,128)S(1)}) custom-call(f32[512,32]{1,0:T(8,128)S(1)} %copy-done.14, f32[32,64]{1,0:T(8,128)S(1)} %copy-done.13, f32[64,2048]{1,0:T(8,128)S(1)} %copy-done.5, f32[1,2048]{1,0:T(1,128)S(1)} %bitcast.7, bf16[256,256]{1,0:T(8,128)(2,1)S(1)} %copy-done.6), custom_call_target="tpu_custom_call" | custom-call | flops 2147483648 | bytes 262144 | tf_op jit(solution)/shard_map/filters/pallas_call | solution.py:773
  20.1 0.0 copy-done.15
  20.1 1.3 %collective-permute-start = (bf16[128,2048]{1,0:T(8,128)(2,1)S(1)}, bf16[128,2048]{1,0:T(8,128)(2,1)S(1)}, u32[]{:S(2)}, u32[]{:S(2)}) collective-permute-start(bf16[128,2048]{1,0:T(8,128)(2,1)S(1)} %copy-done.15), channel_id=1, source_target_pairs={{0,8},{12,4},{1,9},{13,5},{2,10},{14,6},{3,11},{15,7},{16,24},{28,... | collective-permute-start | bytes 1572872 | tf_op jit(solution)/shard_map/ppermute | solution.py:730
  21.4 0.0 copy-done.16
  21.5 1.3 %collective-permute-start.4 = (bf16[64,2176]{1,0:T(8,128)(2,1)S(1)}, bf16[64,2176]{1,0:T(8,128)(2,1)S(1)}, u32[]{:S(2)}, u32[]{:S(2)}) collective-permute-start(bf16[64,2176]{1,0:T(8,128)(2,1)S(1)} %copy-done.16), channel_id=1, source_target_pairs={{0,4},{12,8},{1,5},{13,9},{2,6},{14,10},{3,7},{15,11},{16,20},{28,... | collective-permute-start | bytes 835592 | tf_op jit(solution)/shard_map/ppermute | solution.py:730
  22.8 0.0 collective-permute-done.1.pair_in_ref
  22.8 0.0 collective-permute-done.2.middle_in_ref
  22.8 0.0 copy-done.4
  22.8 0.0 copy-done.7
  22.8 0.0 copy-done.11
  22.8 0.0 copy-done.12
  22.8 3.8 %near_blocks.1 = (f32[128,2048]{1,0:T(8,128)S(1)}, f32[128,2048]{1,0:T(8,128)S(1)}, f32[128,2048]{1,0:T(8,128)S(1)}, f32[64,2048]{1,0:T(8,128)S(1)}, f32[32,64]{1,0:T(8,128)S(1)}, /*index=5*/f32[256,2048]{1,0:T(8,128)S(1)}) custom-call(s32[1]{0:T(128)} %bitcast.rank_ref.refs_0_.refs_1_.refs_3_, bf16[128,2048]{1,0:T(8,128)(2,1)S(1)} %copy-done.11, ...), custom_call_target="tpu_custom_call" | custom-call | flops 5368709120 | bytes 262144 | tf_op jit(solution)/shard_map/near_blocks/pallas_call | solution.py:785
  26.7 7.1 %collective-permute-done.refs_1_ = bf16[128,2048]{1,0:T(8,128)(2,1)S(1)} collective-permute-done((bf16[128,2048]{1,0:T(8,128)(2,1)S(1)}, bf16[128,2048]{1,0:T(8,128)(2,1)S(1)}, u32[]{:S(2)}, u32[]{:S(2)}) %collective-permute-start) | collective-permute-done | bytes 524320 | tf_op jit(solution)/shard_map/ppermute | solution.py:730
  33.7 0.0 copy-start.10
  33.7 1.4 %collective-permute-start.3 = (bf16[128,2048]{1,0:T(8,128)(2,1)S(1)}, bf16[128,2048]{1,0:T(8,128)(2,1)S(1)}, u32[]{:S(2)}, u32[]{:S(2)}) collective-permute-start(bf16[128,2048]{1,0:T(8,128)(2,1)S(1)} %get-tuple-element.44.refs_0_), channel_id=1, source_target_pairs={{4,0},{8,12},{5,1},{9,13},{6,2},{10,14},{7,3},{11,15},{20,16},{24,... | collective-permute-start | bytes 1572872 | tf_op jit(solution)/shard_map/ppermute | solution.py:730
  35.1 3.4 %collective-permute-done.4.refs_13_ = bf16[64,2176]{1,0:T(8,128)(2,1)S(1)} collective-permute-done((bf16[64,2176]{1,0:T(8,128)(2,1)S(1)}, bf16[64,2176]{1,0:T(8,128)(2,1)S(1)}, u32[]{:S(2)}, u32[]{:S(2)}) %collective-permute-start.4) | collective-permute-done | bytes 278560 | tf_op jit(solution)/shard_map/ppermute | solution.py:730
  38.5 0.0 copy-done.10
  38.5 0.7 %collective-permute-start.7 = (bf16[64,2176]{1,0:T(8,128)(2,1)S(1)}, bf16[64,2176]{1,0:T(8,128)(2,1)S(1)}, u32[]{:S(2)}, u32[]{:S(2)}) collective-permute-start(bf16[64,2176]{1,0:T(8,128)(2,1)S(1)} %get-tuple-element.50.own_ref), channel_id=1, source_target_pairs={{4,8},{8,4},{0,0},{12,12},{5,9},{9,5},{1,1},{13,13},{6,10},{10,6},... | collective-permute-start | bytes 835592 | tf_op jit(solution)/shard_map/ppermute | solution.py:730
  39.2 0.7 %collective-permute-start.5 = (f32[32,64]{1,0:T(8,128)S(1)}, f32[32,64]{1,0:T(8,128)S(1)}, u32[]{:S(2)}, u32[]{:S(2)}) collective-permute-start(f32[32,64]{1,0:T(8,128)S(1)} %get-tuple-element.49), channel_id=1, source_target_pairs={{0,0},{1,1},{2,2},{3,3},{4,5},{5,4},{6,7},{7,6},{8,9},{9,8},{10,11... | collective-permute-start | bytes 24584 | tf_op jit(solution)/shard_map/ppermute | solution.py:850
  39.9 0.0 collective-permute-done.5
  39.9 0.7 %collective-permute-start.6 = (f32[32,64]{1,0:T(8,128)S(1)}, f32[32,64]{1,0:T(8,128)S(1)}, u32[]{:S(2)}, u32[]{:S(2)}) collective-permute-start(f32[32,64]{1,0:T(8,128)S(1)} %add.9), channel_id=1, source_target_pairs={{4,8},{8,4},{0,0},{12,12},{5,9},{9,5},{1,1},{13,13},{6,10},{10,6},... | collective-permute-start | bytes 24584 | tf_op jit(solution)/shard_map/ppermute | solution.py:730
  40.6 0.0 copy-start
  40.6 0.0 copy-start.1
  40.6 0.0 copy-start.2
  40.6 0.0 copy-start.3
  40.6 0.0 copy-start.8
  40.7 0.0 collective-permute-done.6
  40.7 0.0 collective-permute-done.7.come_ref
  40.7 8.9 %collective-permute-done.3.part_ref.refs_10_.refs_12_ = bf16[128,2048]{1,0:T(8,128)(2,1)S(1)} collective-permute-done((bf16[128,2048]{1,0:T(8,128)(2,1)S(1)}, bf16[128,2048]{1,0:T(8,128)(2,1)S(1)}, u32[]{:S(2)}, u32[]{:S(2)}) %collective-permute-start.3) | collective-permute-done | bytes 524320 | tf_op jit(solution)/shard_map/ppermute | solution.py:730
  49.6 0.1 total.1.refs_0_.own_ref
  49.7 5.5 %collective-permute-start.8 = (bf16[64,2176]{1,0:T(8,128)(2,1)S(1)}, bf16[64,2176]{1,0:T(8,128)(2,1)S(1)}, u32[]{:S(2)}, u32[]{:S(2)}) collective-permute-start(bf16[64,2176]{1,0:T(8,128)(2,1)S(1)} %total.1.refs_0_.own_ref), channel_id=1, source_target_pairs={{0,4},{12,8},{4,0},{8,12},{1,5},{13,9},{5,1},{9,13},{2,6},{14,10},... | collective-permute-start | bytes 835592 | tf_op jit(solution)/shard_map/ppermute | solution.py:730
  55.2 0.7 %collective-permute-start.9 = (f32[32,64]{1,0:T(8,128)S(1)}, f32[32,64]{1,0:T(8,128)S(1)}, u32[]{:S(2)}, u32[]{:S(2)}) collective-permute-start(f32[32,64]{1,0:T(8,128)S(1)} %add.10.first_ref), channel_id=1, source_target_pairs={{0,0},{1,1},{2,2},{3,3},{4,6},{5,7},{6,4},{7,5},{8,10},{9,11},{10,... | collective-permute-start | bytes 24584 | tf_op jit(solution)/shard_map/ppermute | solution.py:850
  55.9 0.0 collective-permute-done.9
  55.9 5.0 %collective-permute-start.10 = (f32[32,64]{1,0:T(8,128)S(1)}, f32[32,64]{1,0:T(8,128)S(1)}, u32[]{:S(2)}, u32[]{:S(2)}) collective-permute-start(f32[32,64]{1,0:T(8,128)S(1)} %add.11.first_ref), channel_id=1, source_target_pairs={{0,4},{12,8},{4,0},{8,12},{1,5},{13,9},{5,1},{9,13},{2,6},{14,10},... | collective-permute-start | bytes 24584 | tf_op jit(solution)/shard_map/ppermute | solution.py:730
  60.9 0.0 copy-done
  60.9 0.0 copy-done.1
  60.9 0.0 copy-done.2
  60.9 0.0 copy-done.3
  60.9 0.0 copy-done.8
  60.9 1.6 %gates.2 = (bf16[128,2048]{1,0:T(8,128)(2,1)}, bf16[128,2048]{1,0:T(8,128)(2,1)}, bf16[128,2048]{1,0:T(8,128)(2,1)}) custom-call(bf16[64,2176]{1,0:T(8,128)(2,1)S(1)} %total.1.refs_0_.own_ref, s32[1]{0:T(128)} %bitcast.rank_ref.refs_0_.refs_1_.refs_3_, bf16[128,2048]{1,0:T(8,128)(2,1)S(1)} %copy-done, bf16[128,2048]{1,0:T(8,128)(2,1)S(1)} %copy-done.1, ...), custom_call_target="tpu_custom_call" | custom-call | bytes 262144 | tf_op jit(solution)/shard_map/gates/pallas_call | solution.py:865
  62.5 0.1 gates.3
  62.7 0.0 collective-permute-done.10.first_come_ref
  62.7 0.0 collective-permute-done.8.come_ref
  62.7 0.9 %finish.1 = (f32[64,2048]{1,0:T(8,128)}, f32[32,64]{1,0:T(8,128)}, f32[1,2048]{1,0:T(1,128)}) custom-call(s32[1]{0:T(128)} %bitcast.rank_ref.refs_0_.refs_1_.refs_3_, bf16[64,2176]{1,0:T(8,128)(2,1)S(1)} %total.1.refs_0_.own_ref, bf16[64,2176]{1,0:T(8,128)(2,1)S(1)} %collective-permute-done.8.come_ref, f32[32,64]{1,0:T(8,128)S(1)} %add.11.first_ref, ...), custom_call_target="tpu_custom_call" | custom-call | bytes 262144 | tf_op jit(solution)/shard_map/finish/pallas_call | solution.py:884
  (6 shorter events, 0.0 us)
Async XLA Ops:
  3.4 19.3 %collective-permute-start.1 = (bf16[128,2048]{1,0:T(8,128)(2,1)}, bf16[128,2048]{1,0:T(8,128)(2,1)S(1)}, u32[]{:S(2)}, u32[]{:S(2)}) collective-permute-start(bf16[128,2048]{1,0:T(8,128)(2,1)} %get-tuple-element.35.refs_3_.pair_ref), channel_id=1, source_target_pairs={{0,4},{12,8},{4,0},{8,12},{1,5},{13,9},{5,1},{9,13},{2,6},{14,10},... | collective-permute-start | bytes 1572872 | tf_op jit(solution)/shard_map/ppermute | solution.py:730
  6.5 16.3 %collective-permute-start.2 = (bf16[128,2048]{1,0:T(8,128)(2,1)}, bf16[128,2048]{1,0:T(8,128)(2,1)S(1)}, u32[]{:S(2)}, u32[]{:S(2)}) collective-permute-start(bf16[128,2048]{1,0:T(8,128)(2,1)} %get-tuple-element.36.refs_4_.other_ref), channel_id=1, source_target_pairs={{4,8},{8,4},{5,9},{9,5},{6,10},{10,6},{7,11},{11,7},{20,24},{24,20... | collective-permute-start | bytes 1572872 | tf_op jit(solution)/shard_map/ppermute | solution.py:730
  7.2 6.3 %copy-start.5 = (f32[64,2048]{1,0:T(8,128)S(1)}, f32[64,2048]{1,0:T(8,128)}, u32[]{:S(2)}) copy-start(f32[64,2048]{1,0:T(8,128)} %refs_4_.4) | copy-start | bytes 1572868
  7.2 6.3 %copy-start.6 = (bf16[256,256]{1,0:T(8,128)(2,1)S(1)}, bf16[256,256]{1,0:T(8,128)(2,1)}, u32[]{:S(2)}) copy-start(bf16[256,256]{1,0:T(8,128)(2,1)} %constant.16.clone.refs_7_.front_ref.refs_3_) | copy-start | bytes 393220
  7.2 6.3 %copy-start.9 = (f32[2048]{0:T(1024)S(1)}, f32[2048]{0:T(1024)}, u32[]{:S(2)}) copy-start(f32[2048]{0:T(1024)} %param.20) | copy-start | bytes 24580
  7.2 6.3 %copy-start.13 = (f32[32,64]{1,0:T(8,128)S(1)}, f32[32,64]{1,0:T(8,128)}, u32[]{:S(2)}) copy-start(f32[32,64]{1,0:T(8,128)} %first_ref.1) | copy-start | bytes 24580
  7.2 6.3 %copy-start.14 = (f32[512,32]{1,0:T(8,128)S(1)}, f32[512,32]{1,0:T(8,128)}, u32[]{:S(2)}) copy-start(f32[512,32]{1,0:T(8,128)} %constant.19.clone.feats_ref) | copy-start | bytes 196612
  13.5 6.6 %copy-start.15 = (bf16[128,2048]{1,0:T(8,128)(2,1)S(1)}, bf16[128,2048]{1,0:T(8,128)(2,1)}, u32[]{:S(2)}) copy-start(bf16[128,2048]{1,0:T(8,128)(2,1)} %get-tuple-element.40) | copy-start | bytes 1572868
  13.5 7.9 %copy-start.16 = (bf16[64,2176]{1,0:T(8,128)(2,1)S(1)}, bf16[64,2176]{1,0:T(8,128)(2,1)}, u32[]{:S(2)}) copy-start(bf16[64,2176]{1,0:T(8,128)(2,1)} %own_pair.1) | copy-start | bytes 835588
  13.5 9.3 %copy-start.4 = (bf16[256,256]{1,0:T(8,128)(2,1)S(1)}, bf16[256,256]{1,0:T(8,128)(2,1)}, u32[]{:S(2)}) copy-start(bf16[256,256]{1,0:T(8,128)(2,1)} %constant.17.clone.refs_8_.back_ref.refs_4_.refs_6_.refs_3_) | copy-start | bytes 393220
  13.6 9.2 %copy-start.7 = (f32[32,512]{1,0:T(8,128)S(1)}, f32[32,512]{1,0:T(8,128)}, u32[]{:S(2)}) copy-start(f32[32,512]{1,0:T(8,128)} %constant.18.clone.refs_9_.featt_ref.refs_8_) | copy-start | bytes 196612
  13.6 9.2 %copy-start.11 = (bf16[128,2048]{1,0:T(8,128)(2,1)S(1)}, bf16[128,2048]{1,0:T(8,128)(2,1)}, u32[]{:S(2)}) copy-start(bf16[128,2048]{1,0:T(8,128)(2,1)} %get-tuple-element.35.refs_3_.pair_ref) | copy-start | bytes 1572868
  13.6 9.2 %copy-start.12 = (bf16[128,2048]{1,0:T(8,128)(2,1)S(1)}, bf16[128,2048]{1,0:T(8,128)(2,1)}, u32[]{:S(2)}) copy-start(bf16[128,2048]{1,0:T(8,128)(2,1)} %get-tuple-element.36.refs_4_.other_ref) | copy-start | bytes 1572868
  20.1 13.6 %collective-permute-start = (bf16[128,2048]{1,0:T(8,128)(2,1)S(1)}, bf16[128,2048]{1,0:T(8,128)(2,1)S(1)}, u32[]{:S(2)}, u32[]{:S(2)}) collective-permute-start(bf16[128,2048]{1,0:T(8,128)(2,1)S(1)} %copy-done.15), channel_id=1, source_target_pairs={{0,8},{12,4},{1,9},{13,5},{2,10},{14,6},{3,11},{15,7},{16,24},{28,... | collective-permute-start | bytes 1572872 | tf_op jit(solution)/shard_map/ppermute | solution.py:730
  21.5 17.1 %collective-permute-start.4 = (bf16[64,2176]{1,0:T(8,128)(2,1)S(1)}, bf16[64,2176]{1,0:T(8,128)(2,1)S(1)}, u32[]{:S(2)}, u32[]{:S(2)}) collective-permute-start(bf16[64,2176]{1,0:T(8,128)(2,1)S(1)} %copy-done.16), channel_id=1, source_target_pairs={{0,4},{12,8},{1,5},{13,9},{2,6},{14,10},{3,7},{15,11},{16,20},{28,... | collective-permute-start | bytes 835592 | tf_op jit(solution)/shard_map/ppermute | solution.py:730
  33.7 4.8 %copy-start.10 = (f32[1,2048]{1,0:T(1,128)S(1)}, f32[1,2048]{1,0:T(1,128)}, u32[]{:S(2)}) copy-start(f32[1,2048]{1,0:T(1,128)} %get-tuple-element.37.refs_10_.refs_12_) | copy-start | bytes 24580
  33.7 15.9 %collective-permute-start.3 = (bf16[128,2048]{1,0:T(8,128)(2,1)S(1)}, bf16[128,2048]{1,0:T(8,128)(2,1)S(1)}, u32[]{:S(2)}, u32[]{:S(2)}) collective-permute-start(bf16[128,2048]{1,0:T(8,128)(2,1)S(1)} %get-tuple-element.44.refs_0_), channel_id=1, source_target_pairs={{4,0},{8,12},{5,1},{9,13},{6,2},{10,14},{7,3},{11,15},{20,16},{24,... | collective-permute-start | bytes 1572872 | tf_op jit(solution)/shard_map/ppermute | solution.py:730
  38.5 2.1 %collective-permute-start.7 = (bf16[64,2176]{1,0:T(8,128)(2,1)S(1)}, bf16[64,2176]{1,0:T(8,128)(2,1)S(1)}, u32[]{:S(2)}, u32[]{:S(2)}) collective-permute-start(bf16[64,2176]{1,0:T(8,128)(2,1)S(1)} %get-tuple-element.50.own_ref), channel_id=1, source_target_pairs={{4,8},{8,4},{0,0},{12,12},{5,9},{9,5},{1,1},{13,13},{6,10},{10,6},... | collective-permute-start | bytes 835592 | tf_op jit(solution)/shard_map/ppermute | solution.py:730
  39.2 0.7 %collective-permute-start.5 = (f32[32,64]{1,0:T(8,128)S(1)}, f32[32,64]{1,0:T(8,128)S(1)}, u32[]{:S(2)}, u32[]{:S(2)}) collective-permute-start(f32[32,64]{1,0:T(8,128)S(1)} %get-tuple-element.49), channel_id=1, source_target_pairs={{0,0},{1,1},{2,2},{3,3},{4,5},{5,4},{6,7},{7,6},{8,9},{9,8},{10,11... | collective-permute-start | bytes 24584 | tf_op jit(solution)/shard_map/ppermute | solution.py:850
  39.9 0.8 %collective-permute-start.6 = (f32[32,64]{1,0:T(8,128)S(1)}, f32[32,64]{1,0:T(8,128)S(1)}, u32[]{:S(2)}, u32[]{:S(2)}) collective-permute-start(f32[32,64]{1,0:T(8,128)S(1)} %add.9), channel_id=1, source_target_pairs={{4,8},{8,4},{0,0},{12,12},{5,9},{9,5},{1,1},{13,13},{6,10},{10,6},... | collective-permute-start | bytes 24584 | tf_op jit(solution)/shard_map/ppermute | solution.py:730
  40.6 20.3 %copy-start = (bf16[128,2048]{1,0:T(8,128)(2,1)S(1)}, bf16[128,2048]{1,0:T(8,128)(2,1)}, u32[]{:S(2)}) copy-start(bf16[128,2048]{1,0:T(8,128)(2,1)} %refs_4_.6) | copy-start | bytes 1572868
  40.6 20.2 %copy-start.1 = (bf16[128,2048]{1,0:T(8,128)(2,1)S(1)}, bf16[128,2048]{1,0:T(8,128)(2,1)}, u32[]{:S(2)}) copy-start(bf16[128,2048]{1,0:T(8,128)(2,1)} %refs_5_.5) | copy-start | bytes 1572868
  40.6 20.2 %copy-start.2 = (bf16[128,2048]{1,0:T(8,128)(2,1)S(1)}, bf16[128,2048]{1,0:T(8,128)(2,1)}, u32[]{:S(2)}) copy-start(bf16[128,2048]{1,0:T(8,128)(2,1)} %refs_6_.2) | copy-start | bytes 1572868
  40.6 20.2 %copy-start.3 = (bf16[128,2048]{1,0:T(8,128)(2,1)S(1)}, bf16[128,2048]{1,0:T(8,128)(2,1)}, u32[]{:S(2)}) copy-start(bf16[128,2048]{1,0:T(8,128)(2,1)} %refs_7_.2) | copy-start | bytes 1572868
  40.6 20.2 %copy-start.8 = (f32[2048]{0:T(1024)S(1)}, f32[2048]{0:T(1024)}, u32[]{:S(2)}) copy-start(f32[2048]{0:T(1024)} %param.19) | copy-start | bytes 24580
  49.7 13.0 %collective-permute-start.8 = (bf16[64,2176]{1,0:T(8,128)(2,1)S(1)}, bf16[64,2176]{1,0:T(8,128)(2,1)S(1)}, u32[]{:S(2)}, u32[]{:S(2)}) collective-permute-start(bf16[64,2176]{1,0:T(8,128)(2,1)S(1)} %total.1.refs_0_.own_ref), channel_id=1, source_target_pairs={{0,4},{12,8},{4,0},{8,12},{1,5},{13,9},{5,1},{9,13},{2,6},{14,10},... | collective-permute-start | bytes 835592 | tf_op jit(solution)/shard_map/ppermute | solution.py:730
  55.2 0.7 %collective-permute-start.9 = (f32[32,64]{1,0:T(8,128)S(1)}, f32[32,64]{1,0:T(8,128)S(1)}, u32[]{:S(2)}, u32[]{:S(2)}) collective-permute-start(f32[32,64]{1,0:T(8,128)S(1)} %add.10.first_ref), channel_id=1, source_target_pairs={{0,0},{1,1},{2,2},{3,3},{4,6},{5,7},{6,4},{7,5},{8,10},{9,11},{10,... | collective-permute-start | bytes 24584 | tf_op jit(solution)/shard_map/ppermute | solution.py:850
  55.9 6.8 %collective-permute-start.10 = (f32[32,64]{1,0:T(8,128)S(1)}, f32[32,64]{1,0:T(8,128)S(1)}, u32[]{:S(2)}, u32[]{:S(2)}) collective-permute-start(f32[32,64]{1,0:T(8,128)S(1)} %add.11.first_ref), channel_id=1, source_target_pairs={{0,4},{12,8},{4,0},{8,12},{1,5},{13,9},{5,1},{9,13},{2,6},{14,10},... | collective-permute-start | bytes 24584 | tf_op jit(solution)/shard_map/ppermute | solution.py:730

commit v20 on v15

--- a/solution.py
+++ b/solution.py
@@ -757,7 +757,7 @@
         shape(feat_count, seq_len), shape(1, channels), shape(*pay_shape, dtype=bf16),
     ]
     (send,) = call(
-        only(False, shards, 0, functools.partial(own_kernel, rows, shards, channels, blocks, width)), "own_pair", 8,
+        only(False, shards, 0, functools.partial(own_kernel, rows, shards, channels, few, wide)), "own_pair", 8,
         [shape(*pay_shape, dtype=bf16)],
         [smem] + [anywhere] * 10,
         out_specs=[anywhere],

time: 61.1 us -> 66.2 us (1.083)
  waiting for transfers between devices: 20.9 us -> 24.6 us
  starting transfers between devices: 16.9 us -> 19.3 us
  Pallas kernels: 22 us -> 20.9 us
    ppermute x9, waiting for transfers between devices: 17.5 us -> 21.2 us  [move(): return lax.ppermute(array, 'ctx', pairs)]
    ppermute x9, starting transfers between devices: 15.3 us -> 17.8 us  [move(): return lax.ppermute(array, 'ctx', pairs)]
    pallas_call x1, Pallas kernels: 6.2 us -> 5.09 us  [few_shards_body(): call(only(False, shards, 0, functools.partial(own_kernel, rows, shards, c...]
  transfers between devices with their start and end apart: 11 -> 11, of which waited for: 6 -> 6; matrix products, arithmetic and copies ran while one was open for 0% -> 0% of each run, Pallas kernels for 30% -> 26%
where the time goes in v20:
time: 66.2 us; the launch traced here: 65.9 us
  waiting for transfers between devices  24.6 us (37%)
  Pallas kernels  20.9 us (32%)
  starting transfers between devices  19.3 us (29%)
  between operations  0.98 us (1%)
    ppermute x9, waiting for transfers between devices, move(): return lax.ppermute(array, 'ctx', pairs)  21.2 us
    ppermute x9, starting transfers between devices, move(): return lax.ppermute(array, 'ctx', pairs)  17.8 us
    pallas_call x1, Pallas kernels, few_shards_body(): call(functools.partial(filters_kernel, rows, shards, blocks, width), 'fil...  6.51 us
    pallas_call x1, Pallas kernels, few_shards_body(): call(only(False, shards, 0, functools.partial(own_kernel, rows, shards, c...  5.09 us
    pallas_call x1, Pallas kernels, few_shards_body(): call(functools.partial(near_kernel, rows, shards, blocks, width), 'near_b...  3.82 us
    ppermute x2, waiting for transfers between devices, few_shards_body(): lax.ppermute(first, ('ch', 'sub'), [(i, i ^ bit) for i in range(group)])  3.39 us
    pallas_call x1, Pallas kernels, few_shards_body(): pl.pallas_call(products_kernel, grid=(rows // row_step,), in_specs=[smem]...  2.79 us
    pallas_call x2, Pallas kernels, gates(): call(only(inner, shards, len(before), functools.partial(gates_kernel, inn...  1.74 us
  transfers between devices with their start and end apart: 11, of which 6 were waited for; matrix products, arithmetic and copies ran while one was open for 0% of the time, Pallas kernels for 26%

profile of v20, /device:TPU:0, one launch (start us, length us, event | category | flops | bytes accessed | tf_op | source)
XLA Modules:
  0.0 65.9 jit_solution(2000231610323823712)
XLA Ops:
  0.6 2.8 %products.1 = (bf16[128,2048]{1,0:T(8,128)(2,1)}, bf16[128,2048]{1,0:T(8,128)(2,1)}, bf16[128,2048]{1,0:T(8,128)(2,1)}, f32[1,2048]{1,0:T(1,128)}) custom-call(s32[1]{0:T(128)} %bitcast.rank_ref.refs_0_.refs_1_.refs_3_, bf16[128,2048]{1,0:T(8,128)(2,1)} %refs_4_.6, bf16[128,2048]{1,0:T(8,128)(2,1)} %refs_5_.5, bf16[128,2048]{1,0:T(8,128)(2,1)} %refs_6_.2, ...), custom_call_target="tpu_custom_call" | custom-call | tf_op jit(solution)/shard_map/products/pallas_call | solution.py:742
  3.4 3.1 %collective-permute-start.1 = (bf16[128,2048]{1,0:T(8,128)(2,1)}, bf16[128,2048]{1,0:T(8,128)(2,1)S(1)}, u32[]{:S(2)}, u32[]{:S(2)}) collective-permute-start(bf16[128,2048]{1,0:T(8,128)(2,1)} %get-tuple-element.36.refs_3_.pair_ref), channel_id=1, source_target_pairs={{0,4},{12,8},{4,0},{8,12},{1,5},{13,9},{5,1},{9,13},{2,6},{14,10},... | collective-permute-start | bytes 1572872 | tf_op jit(solution)/shard_map/ppermute | solution.py:730
  6.5 0.7 %collective-permute-start.2 = (bf16[128,2048]{1,0:T(8,128)(2,1)}, bf16[128,2048]{1,0:T(8,128)(2,1)S(1)}, u32[]{:S(2)}, u32[]{:S(2)}) collective-permute-start(bf16[128,2048]{1,0:T(8,128)(2,1)} %get-tuple-element.37.refs_4_.other_ref), channel_id=1, source_target_pairs={{4,8},{8,4},{5,9},{9,5},{6,10},{10,6},{7,11},{11,7},{20,24},{24,20... | collective-permute-start | bytes 1572872 | tf_op jit(solution)/shard_map/ppermute | solution.py:730
  7.2 0.0 copy-start.5
  7.2 0.0 copy-start.6
  7.2 0.0 copy-start.9
  7.2 0.0 copy-start.13
  7.2 0.0 copy-start.14
  7.3 5.1 %own_pair.1 = bf16[64,2176]{1,0:T(8,128)(2,1)} custom-call(s32[1]{0:T(128)} %bitcast.rank_ref.refs_0_.refs_1_.refs_3_, f32[128,32]{1,0:T(8,128)} %constant.15.clone.refs_1_, f32[32,64]{1,0:T(8,128)} %first_ref.1, bf16[128,2048]{1,0:T(8,128)(2,1)} %get-tuple-element.36.refs_3_.pair_ref, bf16[128,2048]{1,0:T(8,128)(2,1)} %get-tuple-element.37.refs_4_.other_ref, ...), custom_call_target="tpu_custom_call" | custom-call | flops 2147483648 | bytes 262144 | tf_op jit(solution)/shard_map/own_pair/pallas_call | solution.py:759
  12.4 0.0 copy-done.5
  12.4 0.0 copy-done.6
  12.4 0.0 copy-done.9
  12.4 0.0 copy-done.13
  12.4 0.0 copy-done.14
  12.4 0.0 copy-start.15
  12.4 0.0 copy-start.16
  12.4 0.0 copy-start.4
  12.4 0.0 copy-start.7
  12.5 0.0 copy-start.11
  12.5 0.0 copy-start.12
  12.5 6.5 %filters.1 = (bf16[4,256,2048]{2,1,0:T(8,128)(2,1)S(1)}, bf16[128,512]{1,0:T(8,128)(2,1)S(1)}, f32[512,64]{1,0:T(8,128)S(1)}) custom-call(f32[512,32]{1,0:T(8,128)S(1)} %copy-done.14, f32[32,64]{1,0:T(8,128)S(1)} %copy-done.13, f32[64,2048]{1,0:T(8,128)S(1)} %copy-done.5, f32[1,2048]{1,0:T(1,128)S(1)} %bitcast.7, bf16[256,256]{1,0:T(8,128)(2,1)S(1)} %copy-done.6), custom_call_target="tpu_custom_call" | custom-call | flops 2147483648 | bytes 262144 | tf_op jit(solution)/shard_map/filters/pallas_call | solution.py:773
  19.0 0.0 copy-done.15
  19.0 1.7 %collective-permute-start = (bf16[128,2048]{1,0:T(8,128)(2,1)S(1)}, bf16[128,2048]{1,0:T(8,128)(2,1)S(1)}, u32[]{:S(2)}, u32[]{:S(2)}) collective-permute-start(bf16[128,2048]{1,0:T(8,128)(2,1)S(1)} %copy-done.15), channel_id=1, source_target_pairs={{0,8},{12,4},{1,9},{13,5},{2,10},{14,6},{3,11},{15,7},{16,24},{28,... | collective-permute-start | bytes 1572872 | tf_op jit(solution)/shard_map/ppermute | solution.py:730
  20.7 0.0 copy-done.16
  20.7 1.8 %collective-permute-start.4 = (bf16[64,2176]{1,0:T(8,128)(2,1)S(1)}, bf16[64,2176]{1,0:T(8,128)(2,1)S(1)}, u32[]{:S(2)}, u32[]{:S(2)}) collective-permute-start(bf16[64,2176]{1,0:T(8,128)(2,1)S(1)} %copy-done.16), channel_id=1, source_target_pairs={{0,4},{12,8},{1,5},{13,9},{2,6},{14,10},{3,7},{15,11},{16,20},{28,... | collective-permute-start | bytes 835592 | tf_op jit(solution)/shard_map/ppermute | solution.py:730
  22.5 0.0 collective-permute-done.1.pair_in_ref
  22.6 0.0 collective-permute-done.2.middle_in_ref
  22.6 0.0 copy-done.4
  22.6 0.0 copy-done.7
  22.6 0.0 copy-done.11
  22.6 0.0 copy-done.12
  22.6 3.8 %near_blocks.1 = (f32[128,2048]{1,0:T(8,128)S(1)}, f32[128,2048]{1,0:T(8,128)S(1)}, f32[128,2048]{1,0:T(8,128)S(1)}, f32[64,2048]{1,0:T(8,128)S(1)}, f32[32,64]{1,0:T(8,128)S(1)}, /*index=5*/f32[256,2048]{1,0:T(8,128)S(1)}) custom-call(s32[1]{0:T(128)} %bitcast.rank_ref.refs_0_.refs_1_.refs_3_, bf16[128,2048]{1,0:T(8,128)(2,1)S(1)} %copy-done.11, ...), custom_call_target="tpu_custom_call" | custom-call | flops 5368709120 | bytes 262144 | tf_op jit(solution)/shard_map/near_blocks/pallas_call | solution.py:785
  26.4 6.6 %collective-permute-done.refs_1_ = bf16[128,2048]{1,0:T(8,128)(2,1)S(1)} collective-permute-done((bf16[128,2048]{1,0:T(8,128)(2,1)S(1)}, bf16[128,2048]{1,0:T(8,128)(2,1)S(1)}, u32[]{:S(2)}, u32[]{:S(2)}) %collective-permute-start) | collective-permute-done | bytes 524320 | tf_op jit(solution)/shard_map/ppermute | solution.py:730
  33.1 0.0 copy-start.10
  33.1 1.4 %collective-permute-start.3 = (bf16[128,2048]{1,0:T(8,128)(2,1)S(1)}, bf16[128,2048]{1,0:T(8,128)(2,1)S(1)}, u32[]{:S(2)}, u32[]{:S(2)}) collective-permute-start(bf16[128,2048]{1,0:T(8,128)(2,1)S(1)} %get-tuple-element.45.refs_0_), channel_id=1, source_target_pairs={{4,0},{8,12},{5,1},{9,13},{6,2},{10,14},{7,3},{11,15},{20,16},{24,... | collective-permute-start | bytes 1572872 | tf_op jit(solution)/shard_map/ppermute | solution.py:730
  34.5 3.1 %collective-permute-done.4.refs_13_ = bf16[64,2176]{1,0:T(8,128)(2,1)S(1)} collective-permute-done((bf16[64,2176]{1,0:T(8,128)(2,1)S(1)}, bf16[64,2176]{1,0:T(8,128)(2,1)S(1)}, u32[]{:S(2)}, u32[]{:S(2)}) %collective-permute-start.4) | collective-permute-done | bytes 278560 | tf_op jit(solution)/shard_map/ppermute | solution.py:730
  37.6 0.0 copy-done.10
  37.6 0.7 %collective-permute-start.7 = (bf16[64,2176]{1,0:T(8,128)(2,1)S(1)}, bf16[64,2176]{1,0:T(8,128)(2,1)S(1)}, u32[]{:S(2)}, u32[]{:S(2)}) collective-permute-start(bf16[64,2176]{1,0:T(8,128)(2,1)S(1)} %get-tuple-element.51.own_ref), channel_id=1, source_target_pairs={{4,8},{8,4},{0,0},{12,12},{5,9},{9,5},{1,1},{13,13},{6,10},{10,6},... | collective-permute-start | bytes 835592 | tf_op jit(solution)/shard_map/ppermute | solution.py:730
  38.3 0.1 collective-permute-start.5
  38.4 1.2 %collective-permute-done.5 = f32[32,64]{1,0:T(8,128)S(1)} collective-permute-done((f32[32,64]{1,0:T(8,128)S(1)}, f32[32,64]{1,0:T(8,128)S(1)}, u32[]{:S(2)}, u32[]{:S(2)}) %collective-permute-start.5) | collective-permute-done | bytes 8224 | tf_op jit(solution)/shard_map/ppermute | solution.py:845
  39.5 1.5 %collective-permute-start.6 = (f32[32,64]{1,0:T(8,128)S(1)}, f32[32,64]{1,0:T(8,128)S(1)}, u32[]{:S(2)}, u32[]{:S(2)}) collective-permute-start(f32[32,64]{1,0:T(8,128)S(1)} %add.9), channel_id=1, source_target_pairs={{0,2},{1,3},{2,0},{3,1},{4,6},{5,7},{6,4},{7,5},{8,10},{9,11},{10,... | collective-permute-start | bytes 24584 | tf_op jit(solution)/shard_map/ppermute | solution.py:845
  41.0 0.0 copy-start
  41.0 0.0 copy-start.1
  41.0 0.0 copy-start.2
  41.0 0.0 copy-start.3
  41.0 0.0 copy-start.8
  41.0 2.2 %collective-permute-done.6 = f32[32,64]{1,0:T(8,128)S(1)} collective-permute-done((f32[32,64]{1,0:T(8,128)S(1)}, f32[32,64]{1,0:T(8,128)S(1)}, u32[]{:S(2)}, u32[]{:S(2)}) %collective-permute-start.6) | collective-permute-done | bytes 8224 | tf_op jit(solution)/shard_map/ppermute | solution.py:845
  43.3 0.0 collective-permute-done.7.come_ref
  43.3 9.8 %collective-permute-done.3.part_ref.refs_10_.refs_12_ = bf16[128,2048]{1,0:T(8,128)(2,1)S(1)} collective-permute-done((bf16[128,2048]{1,0:T(8,128)(2,1)S(1)}, bf16[128,2048]{1,0:T(8,128)(2,1)S(1)}, u32[]{:S(2)}, u32[]{:S(2)}) %collective-permute-start.3) | collective-permute-done | bytes 524320 | tf_op jit(solution)/shard_map/ppermute | solution.py:730
  53.1 0.1 total.1.refs_0_.own_ref
  53.2 4.3 %collective-permute-start.8 = (bf16[64,2176]{1,0:T(8,128)(2,1)S(1)}, bf16[64,2176]{1,0:T(8,128)(2,1)S(1)}, u32[]{:S(2)}, u32[]{:S(2)}) collective-permute-start(bf16[64,2176]{1,0:T(8,128)(2,1)S(1)} %total.1.refs_0_.own_ref), channel_id=1, source_target_pairs={{0,4},{12,8},{4,0},{8,12},{1,5},{13,9},{5,1},{9,13},{2,6},{14,10},... | collective-permute-start | bytes 835592 | tf_op jit(solution)/shard_map/ppermute | solution.py:730
  57.5 0.0 copy-done
  57.5 0.0 copy-done.1
  57.5 0.0 copy-done.2
  57.5 0.0 copy-done.3
  57.5 0.0 copy-done.8
  57.5 1.6 %gates.2 = (bf16[128,2048]{1,0:T(8,128)(2,1)}, bf16[128,2048]{1,0:T(8,128)(2,1)}, bf16[128,2048]{1,0:T(8,128)(2,1)}) custom-call(bf16[64,2176]{1,0:T(8,128)(2,1)S(1)} %total.1.refs_0_.own_ref, s32[1]{0:T(128)} %bitcast.rank_ref.refs_0_.refs_1_.refs_3_, bf16[128,2048]{1,0:T(8,128)(2,1)S(1)} %copy-done, bf16[128,2048]{1,0:T(8,128)(2,1)S(1)} %copy-done.1, ...), custom_call_target="tpu_custom_call" | custom-call | bytes 262144 | tf_op jit(solution)/shard_map/gates/pallas_call | solution.py:856
  59.1 0.7 %collective-permute-start.9 = (f32[32,64]{1,0:T(8,128)S(1)}, f32[32,64]{1,0:T(8,128)S(1)}, u32[]{:S(2)}, u32[]{:S(2)}) collective-permute-start(f32[32,64]{1,0:T(8,128)S(1)} %add.10.first_ref), channel_id=1, source_target_pairs={{4,8},{8,4},{0,0},{12,12},{5,9},{9,5},{1,1},{13,13},{6,10},{10,6},... | collective-permute-start | bytes 24584 | tf_op jit(solution)/shard_map/ppermute | solution.py:730
  59.8 0.0 collective-permute-done.9
  59.8 3.5 %collective-permute-start.10 = (f32[32,64]{1,0:T(8,128)S(1)}, f32[32,64]{1,0:T(8,128)S(1)}, u32[]{:S(2)}, u32[]{:S(2)}) collective-permute-start(f32[32,64]{1,0:T(8,128)S(1)} %add.11.first_ref), channel_id=1, source_target_pairs={{0,4},{12,8},{4,0},{8,12},{1,5},{13,9},{5,1},{9,13},{2,6},{14,10},... | collective-permute-start | bytes 24584 | tf_op jit(solution)/shard_map/ppermute | solution.py:730
  63.3 0.1 gates.3
  63.4 1.6 %collective-permute-done.10.first_come_ref = f32[32,64]{1,0:T(8,128)S(1)} collective-permute-done((f32[32,64]{1,0:T(8,128)S(1)}, f32[32,64]{1,0:T(8,128)S(1)}, u32[]{:S(2)}, u32[]{:S(2)}) %collective-permute-start.10) | collective-permute-done | bytes 8224 | tf_op jit(solution)/shard_map/ppermute | solution.py:730
  65.0 0.0 collective-permute-done.8.come_ref
  65.0 0.9 %finish.1 = (f32[64,2048]{1,0:T(8,128)}, f32[32,64]{1,0:T(8,128)}, f32[1,2048]{1,0:T(1,128)}) custom-call(s32[1]{0:T(128)} %bitcast.rank_ref.refs_0_.refs_1_.refs_3_, bf16[64,2176]{1,0:T(8,128)(2,1)S(1)} %total.1.refs_0_.own_ref, bf16[64,2176]{1,0:T(8,128)(2,1)S(1)} %collective-permute-done.8.come_ref, f32[32,64]{1,0:T(8,128)S(1)} %add.11.first_ref, ...), custom_call_target="tpu_custom_call" | custom-call | bytes 262144 | tf_op jit(solution)/shard_map/finish/pallas_call | solution.py:876
  (6 shorter events, 0.0 us)
Async XLA Ops:
  3.4 19.1 %collective-permute-start.1 = (bf16[128,2048]{1,0:T(8,128)(2,1)}, bf16[128,2048]{1,0:T(8,128)(2,1)S(1)}, u32[]{:S(2)}, u32[]{:S(2)}) collective-permute-start(bf16[128,2048]{1,0:T(8,128)(2,1)} %get-tuple-element.36.refs_3_.pair_ref), channel_id=1, source_target_pairs={{0,4},{12,8},{4,0},{8,12},{1,5},{13,9},{5,1},{9,13},{2,6},{14,10},... | collective-permute-start | bytes 1572872 | tf_op jit(solution)/shard_map/ppermute | solution.py:730
  6.5 16.1 %collective-permute-start.2 = (bf16[128,2048]{1,0:T(8,128)(2,1)}, bf16[128,2048]{1,0:T(8,128)(2,1)S(1)}, u32[]{:S(2)}, u32[]{:S(2)}) collective-permute-start(bf16[128,2048]{1,0:T(8,128)(2,1)} %get-tuple-element.37.refs_4_.other_ref), channel_id=1, source_target_pairs={{4,8},{8,4},{5,9},{9,5},{6,10},{10,6},{7,11},{11,7},{20,24},{24,20... | collective-permute-start | bytes 1572872 | tf_op jit(solution)/shard_map/ppermute | solution.py:730
  7.2 5.2 %copy-start.5 = (f32[64,2048]{1,0:T(8,128)S(1)}, f32[64,2048]{1,0:T(8,128)}, u32[]{:S(2)}) copy-start(f32[64,2048]{1,0:T(8,128)} %refs_4_.4) | copy-start | bytes 1572868
  7.2 5.2 %copy-start.6 = (bf16[256,256]{1,0:T(8,128)(2,1)S(1)}, bf16[256,256]{1,0:T(8,128)(2,1)}, u32[]{:S(2)}) copy-start(bf16[256,256]{1,0:T(8,128)(2,1)} %constant.16.clone.refs_7_.front_ref.refs_3_) | copy-start | bytes 393220
  7.2 5.2 %copy-start.9 = (f32[2048]{0:T(1024)S(1)}, f32[2048]{0:T(1024)}, u32[]{:S(2)}) copy-start(f32[2048]{0:T(1024)} %param.20) | copy-start | bytes 24580
  7.2 5.2 %copy-start.13 = (f32[32,64]{1,0:T(8,128)S(1)}, f32[32,64]{1,0:T(8,128)}, u32[]{:S(2)}) copy-start(f32[32,64]{1,0:T(8,128)} %first_ref.1) | copy-start | bytes 24580
  7.2 5.2 %copy-start.14 = (f32[512,32]{1,0:T(8,128)S(1)}, f32[512,32]{1,0:T(8,128)}, u32[]{:S(2)}) copy-start(f32[512,32]{1,0:T(8,128)} %constant.19.clone.feats_ref) | copy-start | bytes 196612
  12.4 6.6 %copy-start.15 = (bf16[128,2048]{1,0:T(8,128)(2,1)S(1)}, bf16[128,2048]{1,0:T(8,128)(2,1)}, u32[]{:S(2)}) copy-start(bf16[128,2048]{1,0:T(8,128)(2,1)} %get-tuple-element.41) | copy-start | bytes 1572868
  12.4 8.3 %copy-start.16 = (bf16[64,2176]{1,0:T(8,128)(2,1)S(1)}, bf16[64,2176]{1,0:T(8,128)(2,1)}, u32[]{:S(2)}) copy-start(bf16[64,2176]{1,0:T(8,128)(2,1)} %own_pair.1) | copy-start | bytes 835588
  12.4 10.1 %copy-start.4 = (bf16[256,256]{1,0:T(8,128)(2,1)S(1)}, bf16[256,256]{1,0:T(8,128)(2,1)}, u32[]{:S(2)}) copy-start(bf16[256,256]{1,0:T(8,128)(2,1)} %constant.17.clone.refs_8_.back_ref.refs_4_.refs_6_.refs_3_) | copy-start | bytes 393220
  12.4 10.1 %copy-start.7 = (f32[32,512]{1,0:T(8,128)S(1)}, f32[32,512]{1,0:T(8,128)}, u32[]{:S(2)}) copy-start(f32[32,512]{1,0:T(8,128)} %constant.18.clone.refs_9_.featt_ref.refs_8_) | copy-start | bytes 196612
  12.5 10.1 %copy-start.11 = (bf16[128,2048]{1,0:T(8,128)(2,1)S(1)}, bf16[128,2048]{1,0:T(8,128)(2,1)}, u32[]{:S(2)}) copy-start(bf16[128,2048]{1,0:T(8,128)(2,1)} %get-tuple-element.36.refs_3_.pair_ref) | copy-start | bytes 1572868
  12.5 10.1 %copy-start.12 = (bf16[128,2048]{1,0:T(8,128)(2,1)S(1)}, bf16[128,2048]{1,0:T(8,128)(2,1)}, u32[]{:S(2)}) copy-start(bf16[128,2048]{1,0:T(8,128)(2,1)} %get-tuple-element.37.refs_4_.other_ref) | copy-start | bytes 1572868
  19.0 14.0 %collective-permute-start = (bf16[128,2048]{1,0:T(8,128)(2,1)S(1)}, bf16[128,2048]{1,0:T(8,128)(2,1)S(1)}, u32[]{:S(2)}, u32[]{:S(2)}) collective-permute-start(bf16[128,2048]{1,0:T(8,128)(2,1)S(1)} %copy-done.15), channel_id=1, source_target_pairs={{0,8},{12,4},{1,9},{13,5},{2,10},{14,6},{3,11},{15,7},{16,24},{28,... | collective-permute-start | bytes 1572872 | tf_op jit(solution)/shard_map/ppermute | solution.py:730
  20.7 16.9 %collective-permute-start.4 = (bf16[64,2176]{1,0:T(8,128)(2,1)S(1)}, bf16[64,2176]{1,0:T(8,128)(2,1)S(1)}, u32[]{:S(2)}, u32[]{:S(2)}) collective-permute-start(bf16[64,2176]{1,0:T(8,128)(2,1)S(1)} %copy-done.16), channel_id=1, source_target_pairs={{0,4},{12,8},{1,5},{13,9},{2,6},{14,10},{3,7},{15,11},{16,20},{28,... | collective-permute-start | bytes 835592 | tf_op jit(solution)/shard_map/ppermute | solution.py:730
  33.1 4.5 %copy-start.10 = (f32[1,2048]{1,0:T(1,128)S(1)}, f32[1,2048]{1,0:T(1,128)}, u32[]{:S(2)}) copy-start(f32[1,2048]{1,0:T(1,128)} %get-tuple-element.38.refs_10_.refs_12_) | copy-start | bytes 24580
  33.1 20.1 %collective-permute-start.3 = (bf16[128,2048]{1,0:T(8,128)(2,1)S(1)}, bf16[128,2048]{1,0:T(8,128)(2,1)S(1)}, u32[]{:S(2)}, u32[]{:S(2)}) collective-permute-start(bf16[128,2048]{1,0:T(8,128)(2,1)S(1)} %get-tuple-element.45.refs_0_), channel_id=1, source_target_pairs={{4,0},{8,12},{5,1},{9,13},{6,2},{10,14},{7,3},{11,15},{20,16},{24,... | collective-permute-start | bytes 1572872 | tf_op jit(solution)/shard_map/ppermute | solution.py:730
  37.6 5.7 %collective-permute-start.7 = (bf16[64,2176]{1,0:T(8,128)(2,1)S(1)}, bf16[64,2176]{1,0:T(8,128)(2,1)S(1)}, u32[]{:S(2)}, u32[]{:S(2)}) collective-permute-start(bf16[64,2176]{1,0:T(8,128)(2,1)S(1)} %get-tuple-element.51.own_ref), channel_id=1, source_target_pairs={{4,8},{8,4},{0,0},{12,12},{5,9},{9,5},{1,1},{13,13},{6,10},{10,6},... | collective-permute-start | bytes 835592 | tf_op jit(solution)/shard_map/ppermute | solution.py:730
  38.3 1.2 %collective-permute-start.5 = (f32[32,64]{1,0:T(8,128)S(1)}, f32[32,64]{1,0:T(8,128)S(1)}, u32[]{:S(2)}, u32[]{:S(2)}) collective-permute-start(f32[32,64]{1,0:T(8,128)S(1)} %get-tuple-element.50), channel_id=1, source_target_pairs={{0,1},{1,0},{2,3},{3,2},{4,5},{5,4},{6,7},{7,6},{8,9},{9,8},{10,11... | collective-permute-start | bytes 24584 | tf_op jit(solution)/shard_map/ppermute | solution.py:845
  39.5 3.7 %collective-permute-start.6 = (f32[32,64]{1,0:T(8,128)S(1)}, f32[32,64]{1,0:T(8,128)S(1)}, u32[]{:S(2)}, u32[]{:S(2)}) collective-permute-start(f32[32,64]{1,0:T(8,128)S(1)} %add.9), channel_id=1, source_target_pairs={{0,2},{1,3},{2,0},{3,1},{4,6},{5,7},{6,4},{7,5},{8,10},{9,11},{10,... | collective-permute-start | bytes 24584 | tf_op jit(solution)/shard_map/ppermute | solution.py:845
  41.0 16.5 %copy-start = (bf16[128,2048]{1,0:T(8,128)(2,1)S(1)}, bf16[128,2048]{1,0:T(8,128)(2,1)}, u32[]{:S(2)}) copy-start(bf16[128,2048]{1,0:T(8,128)(2,1)} %refs_4_.6) | copy-start | bytes 1572868
  41.0 16.5 %copy-start.1 = (bf16[128,2048]{1,0:T(8,128)(2,1)S(1)}, bf16[128,2048]{1,0:T(8,128)(2,1)}, u32[]{:S(2)}) copy-start(bf16[128,2048]{1,0:T(8,128)(2,1)} %refs_5_.5) | copy-start | bytes 1572868
  41.0 16.5 %copy-start.2 = (bf16[128,2048]{1,0:T(8,128)(2,1)S(1)}, bf16[128,2048]{1,0:T(8,128)(2,1)}, u32[]{:S(2)}) copy-start(bf16[128,2048]{1,0:T(8,128)(2,1)} %refs_6_.2) | copy-start | bytes 1572868
  41.0 16.5 %copy-start.3 = (bf16[128,2048]{1,0:T(8,128)(2,1)S(1)}, bf16[128,2048]{1,0:T(8,128)(2,1)}, u32[]{:S(2)}) copy-start(bf16[128,2048]{1,0:T(8,128)(2,1)} %refs_7_.2) | copy-start | bytes 1572868
  41.0 16.5 %copy-start.8 = (f32[2048]{0:T(1024)S(1)}, f32[2048]{0:T(1024)}, u32[]{:S(2)}) copy-start(f32[2048]{0:T(1024)} %param.19) | copy-start | bytes 24580
  53.2 11.8 %collective-permute-start.8 = (bf16[64,2176]{1,0:T(8,128)(2,1)S(1)}, bf16[64,2176]{1,0:T(8,128)(2,1)S(1)}, u32[]{:S(2)}, u32[]{:S(2)}) collective-permute-start(bf16[64,2176]{1,0:T(8,128)(2,1)S(1)} %total.1.refs_0_.own_ref), channel_id=1, source_target_pairs={{0,4},{12,8},{4,0},{8,12},{1,5},{13,9},{5,1},{9,13},{2,6},{14,10},... | collective-permute-start | bytes 835592 | tf_op jit(solution)/shard_map/ppermute | solution.py:730
  59.1 0.7 %collective-permute-start.9 = (f32[32,64]{1,0:T(8,128)S(1)}, f32[32,64]{1,0:T(8,128)S(1)}, u32[]{:S(2)}, u32[]{:S(2)}) collective-permute-start(f32[32,64]{1,0:T(8,128)S(1)} %add.10.first_ref), channel_id=1, source_target_pairs={{4,8},{8,4},{0,0},{12,12},{5,9},{9,5},{1,1},{13,13},{6,10},{10,6},... | collective-permute-start | bytes 24584 | tf_op jit(solution)/shard_map/ppermute | solution.py:730
  59.8 5.2 %collective-permute-start.10 = (f32[32,64]{1,0:T(8,128)S(1)}, f32[32,64]{1,0:T(8,128)S(1)}, u32[]{:S(2)}, u32[]{:S(2)}) collective-permute-start(f32[32,64]{1,0:T(8,128)S(1)} %add.11.first_ref), channel_id=1, source_target_pairs={{0,4},{12,8},{4,0},{8,12},{1,5},{13,9},{5,1},{9,13},{2,6},{14,10},... | collective-permute-start | bytes 24584 | tf_op jit(solution)/shard_map/ppermute | solution.py:730
